TPU v7x, 32 devices: a whole 2x2x4 slice. The times are simulated.
32 devices in a mesh: grp: 2 (over y), seq: 4 (over z), head: 2 (over x), sub: 2 (over core).
Axes of the slice: x: 2, y: 2, z: 4, core: 2. Of those that a mesh axis runs over, the one named last changes fastest.
Arguments:
- tokens_in: bfloat16 [16384, 1024], P(('grp', 'seq', 'sub')), parts along dimension 0, may hold values from -16 to 16
- w_query: bfloat16 [1024, 1024], P(None, 'head'), may hold values from -0.1875 to 0.1875
- w_value: bfloat16 [1024, 1024], P(None, 'head'), may hold values from -0.1875 to 0.1875
- cotangent: bfloat16 [16384, 1024], P(('grp', 'seq', 'sub'), 'head'), parts along dimension 0, may hold values from -6 to 6
- assignment: int32 [16384, 1], P(('grp', 'seq', 'sub')), parts along dimension 0, may hold values from 0 to 63; in each aligned block of 1024 rows (0 to 1023, 1024 to 2047, ...) at most 32 rows name the same one
Outputs:
- grad_input: bfloat16 [16384, 1024], P(('grp', 'seq', 'sub'), 'head'), parts along dimension 0
- grad_wq: float32 [2048, 1024], P(('grp', 'seq', 'sub'), 'head'), parts along dimension 0
- grad_wv: float32 [2048, 1024], P(('grp', 'seq', 'sub'), 'head'), parts along dimension 0
- centroid_grad: float32 [128, 1024], P('grp', 'head'), parts along dimension 0
There are 2 independent parts, one for each index of `grp`. A program takes and returns all parts, laid end to end along the dimension named above; an argument that names none is the same for every part. Nothing has to cross between parts.
Inputs may be any that keep to these rules, and one draw needn't show every extreme that they name: `assignment`: in each device's aligned block of 1024 rows no cluster holds more than 32 tokens, and some cluster holds exactly 32.
All inputs are finite; a program needn't handle non-finite values.
Results may differ from a plain program's by a relative error of at most 0.018.
The roundings to bfloat16 on the way count: a program that leaves them out, or rounds other values in their place, can miss the bound.
Values may be sent and summed in bfloat16 or wider, within the bound.
No kernel may reach another device: no remote copies, remote signals or barrier semaphores. Data moves between devices by JAX's collectives and lax.ppermute only.
A program may use at most 64 MiB of HBM per device.

v0:
```python
import jax
import jax.numpy as jnp
from jax import lax
from jax.sharding import PartitionSpec as P

HD = 64
CLUSTERS = 64
BLOCK_ROWS = 128


def block_backward(queries, values, cotangent):
    score_scale = 0.5 * HD ** (-0.5)
    scores = (
        jnp.einsum("bihd,bjhd->bhij", queries, queries, preferred_element_type=jnp.float32)
        * score_scale
    )
    length = queries.shape[1]
    lower = jnp.tril(jnp.ones((length, length), dtype=bool))
    scores = jnp.where(lower, scores, -jnp.inf)
    highest = jnp.max(scores, axis=-1, keepdims=True)
    raised = jnp.exp(scores - highest)
    probs = raised / jnp.sum(raised, axis=-1, keepdims=True)
    probs_half = probs.astype(jnp.bfloat16)
    output = jnp.einsum("bhij,bjhd->bihd", probs_half, values, preferred_element_type=jnp.float32)
    grad_probs = jnp.einsum(
        "bihd,bjhd->bhij", cotangent, values, preferred_element_type=jnp.float32
    )
    row_dot = jnp.transpose(jnp.sum(cotangent.astype(jnp.float32) * output, axis=-1), (0, 2, 1))[
        ..., None
    ]
    grad_scores = (probs * (grad_probs - row_dot)).astype(jnp.bfloat16)
    grad_query = score_scale * (
        jnp.einsum("bhij,bjhd->bihd", grad_scores, queries, preferred_element_type=jnp.float32)
        + jnp.einsum("bhij,bihd->bjhd", grad_scores, queries, preferred_element_type=jnp.float32)
    )
    grad_value = jnp.einsum(
        "bhij,bihd->bjhd", probs_half, cotangent, preferred_element_type=jnp.float32
    )
    return (grad_query.astype(jnp.bfloat16), grad_value.astype(jnp.bfloat16))


def on_device(tokens_in, w_query, w_value, cotangent, assignment):
    owners = lax.axis_size(("seq", "sub"))
    width_dev = cotangent.shape[1]
    heads_dev = width_dev // HD
    tok_rows = tokens_in.shape[0]
    per_slot = 2 * tok_rows // CLUSTERS
    owned = CLUSTERS // owners
    capacity = (per_slot * owners + BLOCK_ROWS - 1) // BLOCK_ROWS * BLOCK_ROWS
    queries = jnp.dot(tokens_in, w_query, preferred_element_type=jnp.float32).astype(jnp.bfloat16)
    values = jnp.dot(tokens_in, w_value, preferred_element_type=jnp.float32).astype(jnp.bfloat16)
    cluster = assignment[:, 0]
    onehot = (cluster[:, None] == jnp.arange(CLUSTERS, dtype=jnp.int32)[None, :]).astype(jnp.int32)
    running = jnp.cumsum(onehot, axis=0)
    ranking = jnp.sum(running * onehot, axis=1) - 1
    slots = cluster * per_slot + ranking
    counts = jnp.sum(onehot, axis=0)

    def pack(rows):
        filled = jnp.zeros((CLUSTERS * per_slot, width_dev), jnp.bfloat16).at[slots].set(rows)
        return filled.reshape(owners, owned * per_slot, width_dev)

    send_query = pack(queries)
    send_value = pack(values)
    send_cotan = pack(cotangent)
    send_counts = counts.reshape(owners, owned).astype(jnp.bfloat16)
    got_query, got_value, got_cotan, got_counts = (
        lax.all_to_all(send_query, ("seq", "sub"), split_axis=0, concat_axis=0, tiled=True),
        lax.all_to_all(send_value, ("seq", "sub"), split_axis=0, concat_axis=0, tiled=True),
        lax.all_to_all(send_cotan, ("seq", "sub"), split_axis=0, concat_axis=0, tiled=True),
        lax.all_to_all(send_counts, ("seq", "sub"), split_axis=0, concat_axis=0, tiled=True),
    )
    arrived = got_counts.astype(jnp.int32)
    before = jnp.cumsum(arrived, axis=0) - arrived
    within = jnp.arange(per_slot, dtype=jnp.int32)
    index_rows = (
        jnp.arange(owned, dtype=jnp.int32)[None, :, None] * capacity
        + before[:, :, None]
        + within[None, None, :]
    )
    index_rows = jnp.where(
        within[None, None, :] < arrived[:, :, None], index_rows, owned * capacity
    ).reshape(-1)
    block_shape = (owned, capacity // BLOCK_ROWS, BLOCK_ROWS, heads_dev, HD)

    def unpack(rows):
        compact = jnp.zeros((owned * capacity, width_dev), jnp.bfloat16)
        compact = compact.at[index_rows].set(rows.reshape(-1, width_dev), mode="drop")
        return compact.reshape(block_shape)

    def per_cluster(items):
        return block_backward(items[0], items[1], items[2])

    grad_q_blocks, grad_v_blocks = lax.map(
        per_cluster, (unpack(got_query), unpack(got_value), unpack(got_cotan))
    )
    compact_q = grad_q_blocks.reshape(owned * capacity, width_dev)
    compact_v = grad_v_blocks.reshape(owned * capacity, width_dev)
    safe_rows = jnp.minimum(index_rows, owned * capacity - 1)
    back_query = compact_q[safe_rows].reshape(owners, owned * per_slot, width_dev)
    back_value = compact_v[safe_rows].reshape(owners, owned * per_slot, width_dev)
    home_query, home_value = (
        lax.all_to_all(back_query, ("seq", "sub"), split_axis=0, concat_axis=0, tiled=True),
        lax.all_to_all(back_value, ("seq", "sub"), split_axis=0, concat_axis=0, tiled=True),
    )
    grad_q = home_query.reshape(CLUSTERS * per_slot, width_dev)[slots]
    grad_v = home_value.reshape(CLUSTERS * per_slot, width_dev)[slots]
    partial_sum = jnp.dot(grad_q, w_query.T, preferred_element_type=jnp.float32)
    partial_sum = partial_sum + jnp.dot(grad_v, w_value.T, preferred_element_type=jnp.float32)
    grad_input = lax.psum_scatter(
        partial_sum.astype(jnp.bfloat16), "head", scatter_dimension=1, tiled=True
    )
    contract = (((0,), (0,)), ((), ()))
    columns = tokens_in
    grad_wq = lax.psum_scatter(
        lax.dot_general(columns, grad_q, contract, preferred_element_type=jnp.float32).astype(
            jnp.bfloat16
        ),
        ("seq", "sub"),
        scatter_dimension=0,
        tiled=True,
    ).astype(jnp.float32)
    columns = tokens_in
    grad_wv = lax.psum_scatter(
        lax.dot_general(columns, grad_v, contract, preferred_element_type=jnp.float32).astype(
            jnp.bfloat16
        ),
        ("seq", "sub"),
        scatter_dimension=0,
        tiled=True,
    ).astype(jnp.float32)
    factor = (CLUSTERS / (tok_rows * owners)) ** 0.5
    local_sums = lax.dot_general(
        onehot.astype(jnp.bfloat16), grad_q, contract, preferred_element_type=jnp.float32
    )
    centroid_grad = (
        lax.psum(local_sums.astype(jnp.bfloat16), ("seq", "sub")).astype(jnp.float32) * factor
    )
    return (grad_input, grad_wq, grad_wv, centroid_grad)


def solution(mesh):
    return jax.shard_map(
        on_device,
        mesh=mesh,
        in_specs=(
            P(("grp", "seq", "sub"), None),
            P(None, "head"),
            P(None, "head"),
            P(("grp", "seq", "sub"), "head"),
            P(("grp", "seq", "sub"), None),
        ),
        out_specs=(
            P(("grp", "seq", "sub"), "head"),
            P(("grp", "seq", "sub"), "head"),
            P(("grp", "seq", "sub"), "head"),
            P("grp", "head"),
        ),
        check_vma=False,
    )
```

profile of v0, /device:TPU:0, one launch (start us, length us, event | category | flops | bytes accessed | tf_op | source)
XLA Modules:
  0.0 644.2 jit_solution(12790563853105592934)
XLA Ops:
  8.1 18.0 %reduce-window.6 = s32[64,8,128]{2,1,0:T(8,128)S(1)} reduce-window(s32[64,8,128]{2,1,0:T(8,128)S(1)} %fusion.71, s32[]{:T(128)} %copy.95), window={size=1x1x128 pad=0_0x0_0x127_0}, to_apply=%region_2.3 | reduce-window | flops 8323072 | bytes 524292 | tf_op jit(solution)/shard_map/reduce-window
  27.5 6.3 all-to-all-start
  33.8 3.4 convolution_convert_fusion.4
  37.3 7.1 %scatter_custom_fusion = bf16[2048,512]{1,0:T(8,128)(2,1)} fusion(s32[1024]{0:T(1024)S(1)} %bitcast.160, bf16[1024,512]{1,0:T(8,128)(2,1)} %convolution_convert_fusion.4, bf16[]{:T(256)} %constant.21.clone.1), kind=kCustom, calls=%fused_computation.75 | custom fusion | bytes 2097664 | tf_op jit(solution)/shard_map/scatter | solution.py:60
  44.4 5.2 all-to-all-start.1
  51.9 7.2 %scatter_custom_fusion.4 = bf16[2048,512]{1,0:T(8,128)(2,1)} fusion(s32[1024]{0:T(1024)S(1)} %bitcast.161, bf16[1024,512]{1,0:T(8,128)(2,1)} %convolution_convert_fusion.3, bf16[]{:T(256)} %constant.21.clone.1), kind=kCustom, calls=%fused_computation.67 | custom fusion | bytes 2097664 | tf_op jit(solution)/shard_map/scatter | solution.py:60
  59.1 39.8 %all-to-all-done.1 = bf16[8,256,512]{2,1,0:T(8,128)(2,1)} async-done(((bf16[8,256,512]{2,1,0:T(8,128)(2,1)}), bf16[8,256,512]{2,1,0:T(8,128)(2,1)}, u32[]{:S(2)}, u32[]{:S(2)}) %all-to-all-start.1) | async-done | bytes 2097184 | tf_op jit(solution)/shard_map/all_to_all | solution.py:68
  98.8 4.5 all-to-all-start.3
  103.4 7.2 %scatter_custom_fusion.2 = bf16[2048,512]{1,0:T(8,128)(2,1)} fusion(s32[1024]{0:T(1024)S(1)} %bitcast.162, bf16[1024,512]{1,0:T(8,128)(2,1)} %param.10, bf16[]{:T(256)} %constant.21.clone.1), kind=kCustom, calls=%fused_computation.71 | custom fusion | bytes 2097664 | tf_op jit(solution)/shard_map/scatter | solution.py:60
  110.5 41.9 %all-to-all-done.3 = bf16[8,256,512]{2,1,0:T(8,128)(2,1)} async-done(((bf16[8,256,512]{2,1,0:T(8,128)(2,1)}), bf16[8,256,512]{2,1,0:T(8,128)(2,1)}, u32[]{:S(2)}, u32[]{:S(2)}) %all-to-all-start.3) | async-done | bytes 2097184 | tf_op jit(solution)/shard_map/all_to_all | solution.py:69
  152.4 4.3 all-to-all-start.2
  157.1 11.5 %scatter_custom_fusion.1 = bf16[2048,512]{1,0:T(8,128)(2,1)} fusion(s32[2048]{0:T(1024)S(1)} %bitcast.165, bf16[2048,512]{1,0:T(8,128)(2,1)} %bitcast.19, bf16[]{:T(256)} %constant.21.clone.1), kind=kCustom, calls=%fused_computation.73 | custom fusion | bytes 2097664 | tf_op jit(solution)/shard_map/scatter | solution.py:88
  168.6 11.6 %scatter_custom_fusion.5 = bf16[2048,512]{1,0:T(8,128)(2,1)} fusion(s32[2048]{0:T(1024)S(1)} %bitcast.166, bf16[2048,512]{1,0:T(8,128)(2,1)} %bitcast.23, bf16[]{:T(256)} %constant.21.clone.1), kind=kCustom, calls=%fused_computation.65 | custom fusion | bytes 2097664 | tf_op jit(solution)/shard_map/scatter | solution.py:88
  180.2 25.6 %all-to-all-done.2 = bf16[8,256,512]{2,1,0:T(8,128)(2,1)} async-done(((bf16[8,256,512]{2,1,0:T(8,128)(2,1)}), bf16[8,256,512]{2,1,0:T(8,128)(2,1)}, u32[]{:S(2)}, u32[]{:S(2)}) %all-to-all-start.2) | async-done | bytes 2097184 | tf_op jit(solution)/shard_map/all_to_all | solution.py:70
  205.8 11.5 %scatter_custom_fusion.3 = bf16[2048,512]{1,0:T(8,128)(2,1)} fusion(s32[2048]{0:T(1024)S(1)} %bitcast.167, bf16[2048,512]{1,0:T(8,128)(2,1)} %bitcast.21, bf16[]{:T(256)} %constant.21.clone.1), kind=kCustom, calls=%fused_computation.69 | custom fusion | bytes 2097664 | tf_op jit(solution)/shard_map/scatter | solution.py:88
  217.3 6.2 reshape.318
  223.5 5.1 copy.50
  228.6 6.2 reshape.319
  234.8 5.1 copy.51
  239.9 6.2 reshape.317
  246.1 5.1 copy.49
  251.1 97.3 %while.12 = (s32[]{:T(128)}, bf16[8,2,128,8,64]{2,4,3,1,0:T(8,128)(2,1)}, bf16[8,2,128,8,64]{2,4,3,1,0:T(8,128)(2,1)}, bf16[8,2,128,8,64]{2,4,3,1,0:T(8,128)(2,1...) while((s32[]{:T(128)}, ...), condition=%wide.region_15.16_spmd, body=%wide.region_11.15_spmd.sunk | while | flops 274090368 | bytes 7984221 | solution.py:94
  260.7 2.6 fusion.129
  285.0 2.6 fusion.129
  297.2 2.6 fusion.129
  309.4 2.6 fusion.129
  321.5 2.6 fusion.129
  333.7 2.6 fusion.129
  345.8 2.6 fusion.129
  348.4 5.0 copy.70
  353.4 6.5 %reshape.321 = bf16[2048,512]{1,0:T(8,128)(2,1)} reshape(bf16[8,2,128,8,64]{4,3,2,1,0:T(8,128)(2,1)} %copy.70) | data formatting | bytes 4194304 | tf_op jit(solution)/shard_map/reshape | solution.py:98
  359.9 11.1 %gather_fusion.2 = bf16[2048,512]{1,0:T(8,128)(2,1)} fusion(bf16[2048,512]{1,0:T(8,128)(2,1)} %reshape.321, s32[2048]{0:T(1024)S(1)} %broadcast_clamp_fusion), kind=kCustom, calls=%fused_computation.2 | custom fusion | bytes 4202496 | tf_op jit(solution)/shard_map/gather | solution.py:101
  371.0 4.6 all-to-all-start.5
  375.6 5.0 copy.69
  380.6 6.5 %reshape.320 = bf16[2048,512]{1,0:T(8,128)(2,1)} reshape(bf16[8,2,128,8,64]{4,3,2,1,0:T(8,128)(2,1)} %copy.69) | data formatting | bytes 4194304 | tf_op jit(solution)/shard_map/reshape | solution.py:97
  387.1 11.1 %gather_fusion = bf16[2048,512]{1,0:T(8,128)(2,1)} fusion(bf16[2048,512]{1,0:T(8,128)(2,1)} %reshape.320, s32[2048]{0:T(1024)S(1)} %broadcast_clamp_fusion), kind=kCustom, calls=%fused_computation | custom fusion | bytes 4202496 | tf_op jit(solution)/shard_map/gather | solution.py:100
  398.2 26.5 %all-to-all-done.5 = bf16[8,256,512]{2,1,0:T(8,128)(2,1)} async-done(((bf16[8,256,512]{2,1,0:T(8,128)(2,1)}), bf16[8,256,512]{2,1,0:T(8,128)(2,1)}, u32[]{:S(2)}, u32[]{:S(2)}) %all-to-all-start.5) | async-done | bytes 2097184 | tf_op jit(solution)/shard_map/all_to_all | solution.py:104
  424.6 4.3 all-to-all-start.4
  429.0 7.0 %gather_fusion.3 = bf16[1024,512]{1,0:T(8,128)(2,1)} fusion(bf16[2048,512]{1,0:T(8,128)(2,1)} %bitcast.28, s32[1024]{0:T(1024)S(1)} %broadcast_clamp_fusion.1), kind=kCustom, calls=%fused_computation.3 | custom fusion | bytes 2101248 | tf_op jit(solution)/shard_map/gather | solution.py:107
  436.0 42.0 %all-to-all-done.4 = bf16[8,256,512]{2,1,0:T(8,128)(2,1)} async-done(((bf16[8,256,512]{2,1,0:T(8,128)(2,1)}), bf16[8,256,512]{2,1,0:T(8,128)(2,1)}, u32[]{:S(2)}, u32[]{:S(2)}) %all-to-all-start.4) | async-done | bytes 2097184 | tf_op jit(solution)/shard_map/all_to_all | solution.py:103
  478.0 5.8 gather_fusion.1
  484.9 3.5 fusion.56
  495.4 2.7 fusion.76
  498.1 2.6 add_convert_fusion
  500.8 36.8 %all-reduce.2.cloned.1.call-done = bf16[64,512]{1,0:T(8,128)(2,1)} async-done(((bf16[64,512]{1,0:T(8,128)(2,1)}), bf16[64,512]{1,0:T(8,128)(2,1)}) %all-reduce.2.cloned.1.call-update) | async-done | bytes 65552 | tf_op jit(solution)/shard_map/psum | solution.py:137
  539.0 32.1 %reduce-scatter.12.cloned.1.call-done = bf16[128,512]{1,0:T(8,128)(2,1)} async-done(((bf16[1024,512]{1,0:T(8,128)(2,1)}), bf16[128,512]{1,0:T(8,128)(2,1)}) %reduce-scatter.12.cloned.1.call-update) | async-done | bytes 131088
  572.9 31.2 %reduce-scatter.10.cloned.1.call-done = bf16[128,512]{1,0:T(8,128)(2,1)} async-done(((bf16[1024,512]{1,0:T(8,128)(2,1)}), bf16[128,512]{1,0:T(8,128)(2,1)}) %reduce-scatter.10.cloned.1.call-update) | async-done | bytes 131088
  606.0 31.2 %reduce-scatter.8.cloned.1.call-done = bf16[1024,512]{1,0:T(8,128)(2,1)} async-done(((bf16[1024,1024]{1,0:T(8,128)(2,1)}), bf16[1024,512]{1,0:T(8,128)(2,1)}) %reduce-scatter.8.cloned.1.call-update) | async-done | bytes 1048592 | tf_op jit(solution)/shard_map/reduce_scatter | solution.py:110
  (101 shorter events, 96.9 us)
Async XLA Ops:
  7.2 26.6 %copy-start = (bf16[1024,1024]{1,0:T(8,128)(2,1)S(1)}, bf16[1024,1024]{1,0:T(8,128)(2,1)}, u32[]{:S(2)}) copy-start(bf16[1024,1024]{1,0:T(8,128)(2,1)} %param.7) | copy-start | bytes 6291460
  7.2 19.4 %copy-start.4 = (s32[1024,1]{0,1:T(1,128)S(1)}, s32[1024,1]{0,1:T(1,128)}, u32[]{:S(2)}) copy-start(s32[1024,1]{0,1:T(1,128)} %param.11) | copy-start | bytes 12292
  27.5 16.9 %all-to-all-start = ((bf16[8,1,8]{2,1,0:T(2,128)(2,1)}), bf16[8,1,8]{2,1,0:T(2,128)(2,1)S(1)}, u32[]{:S(2)}, u32[]{:S(2)}) async-start(bf16[8,1,8]{2,1,0:T(2,128)(2,1)} %convert_element_type.113), calls=%async_computation | async-start | bytes 8192 | tf_op jit(solution)/shard_map/all_to_all | solution.py:71
  44.4 5.2 copy-start.2
  44.4 54.4 %all-to-all-start.1 = ((bf16[8,256,512]{2,1,0:T(8,128)(2,1)}), bf16[8,256,512]{2,1,0:T(8,128)(2,1)}, u32[]{:S(2)}, u32[]{:S(2)}) async-start(bf16[8,256,512]{2,1,0:T(8,128)(2,1)} %bitcast.152), calls=%async_computation.1 | async-start | bytes 4194304 | tf_op jit(solution)/shard_map/all_to_all | solution.py:68
  98.8 53.6 %all-to-all-start.3 = ((bf16[8,256,512]{2,1,0:T(8,128)(2,1)}), bf16[8,256,512]{2,1,0:T(8,128)(2,1)}, u32[]{:S(2)}, u32[]{:S(2)}) async-start(bf16[8,256,512]{2,1,0:T(8,128)(2,1)} %bitcast.153), calls=%async_computation.3 | async-start | bytes 4194304 | tf_op jit(solution)/shard_map/all_to_all | solution.py:69
  152.4 53.4 %all-to-all-start.2 = ((bf16[8,256,512]{2,1,0:T(8,128)(2,1)}), bf16[8,256,512]{2,1,0:T(8,128)(2,1)}, u32[]{:S(2)}, u32[]{:S(2)}) async-start(bf16[8,256,512]{2,1,0:T(8,128)(2,1)} %bitcast.151), calls=%async_computation.2 | async-start | bytes 4194304 | tf_op jit(solution)/shard_map/all_to_all | solution.py:70
  371.0 53.7 %all-to-all-start.5 = ((bf16[8,256,512]{2,1,0:T(8,128)(2,1)}), bf16[8,256,512]{2,1,0:T(8,128)(2,1)}, u32[]{:S(2)}, u32[]{:S(2)}) async-start(bf16[8,256,512]{2,1,0:T(8,128)(2,1)} %bitcast.150), calls=%async_computation.5 | async-start | bytes 4194304 | tf_op jit(solution)/shard_map/all_to_all | solution.py:104
  424.6 53.4 %all-to-all-start.4 = ((bf16[8,256,512]{2,1,0:T(8,128)(2,1)}), bf16[8,256,512]{2,1,0:T(8,128)(2,1)}, u32[]{:S(2)}, u32[]{:S(2)}) async-start(bf16[8,256,512]{2,1,0:T(8,128)(2,1)} %bitcast.149), calls=%async_computation.4 | async-start | bytes 4194304 | tf_op jit(solution)/shard_map/all_to_all | solution.py:103
  429.0 108.5 %all-reduce.2.cloned.1.call-start = ((), (), s32[]{:S(2)}) async-start(), calls=%async_computation.10 | async-start | bytes 131072 | tf_op jit(solution)/shard_map/psum | solution.py:137
  484.9 86.2 %reduce-scatter.12.cloned.1.call-start = ((), (), s32[]{:S(2)}) async-start(), calls=%async_computation.12 | async-start | bytes 1179648
  490.7 113.5 %reduce-scatter.10.cloned.1.call-start = ((), (), s32[]{:S(2)}) async-start(), calls=%async_computation.11 | async-start | bytes 1179648
  495.3 141.9 %reduce-scatter.8.cloned.1.call-start = ((), (), s32[]{:S(2)}) async-start(), calls=%async_computation.9 | async-start | bytes 3145728 | tf_op jit(solution)/shard_map/reduce_scatter | solution.py:110
  495.4 2.7 copy-start.1
  495.4 2.7 copy-start.3
Sparse Core Ops, SparseCore 0:
  485.0 52.4 all-reduce.1
  539.9 31.1 reduce-scatter.11
  573.5 30.6 reduce-scatter.9
  606.9 30.2 reduce-scatter.7
where the time goes:
time: 654 us; the launch traced here: 644 us
  waiting for transfers between devices  307 us (47%)
  local copies, waits for them, and re-layouts  157 us (24%)
  matrix products  115 us (18%)
  starting transfers between devices  29.5 us (5%)
  other arithmetic  21 us (3%)
  between operations  14.5 us (2%)
    unnamed x6, waiting for transfers between devices  63.4 us
    all_to_all x1, waiting for transfers between devices, on_device(): lax.all_to_all(back_query, ('seq', 'sub'), split_axis=0, concat_axis=0, t...  42 us
    all_to_all x1, waiting for transfers between devices, on_device(): lax.all_to_all(send_value, ('seq', 'sub'), split_axis=0, concat_axis=0, t...  41.9 us
    all_to_all x1, waiting for transfers between devices, on_device(): lax.all_to_all(send_query, ('seq', 'sub'), split_axis=0, concat_axis=0, t...  39.8 us
    psum x1, waiting for transfers between devices, on_device(): lax.psum(local_sums.astype(jnp.bfloat16), ('seq', 'sub'))  36.8 us
    scatter x3, local copies, waits for them, and re-layouts, unpack(): compact.at[index_rows].set(rows.reshape(-1, width_dev), mode='drop')  34.7 us
    reduce_scatter x1, waiting for transfers between devices, on_device(): lax.psum_scatter(partial_sum.astype(jnp.bfloat16), 'head', scatter_dimens...  31.2 us
    all_to_all x1, waiting for transfers between devices, on_device(): lax.all_to_all(back_value, ('seq', 'sub'), split_axis=0, concat_axis=0, t...  26.5 us
  transfers between devices with their start and end apart: 10, of which 9 were waited for; matrix products, arithmetic and copies ran while one was open for 16% of the time, Pallas kernels for 0%

commit v1 on v0

v1 whole, which is shorter than its diff:
```python
import functools

import jax
import jax.numpy as jnp
from jax import lax
from jax.experimental import pallas as pl
from jax.experimental.pallas import tpu as pltpu
from jax.sharding import PartitionSpec as P

HD = 64
CLUSTERS = 64
BLOCK_ROWS = 128
LANES = 128
SCALE = 0.5 * HD ** (-0.5)
F32 = jnp.float32
BF16 = jnp.bfloat16
VMEM_LIMIT = 56 * 1024 * 1024
OWNERS = ("seq", "sub")


def iota(shape, dim):
    return lax.broadcasted_iota(jnp.int32, shape, dim)


def low_half(shape):
    return iota(shape, 1) < HD


def swap_halves(tile):
    return pltpu.roll(tile, HD, 1)


def dot(a, b):
    return jnp.dot(a, b, preferred_element_type=F32)


def dot_nt(a, b):
    return lax.dot_general(a, b, (((1,), (1,)), ((), ())), preferred_element_type=F32)


def ones_where(condition):
    return jnp.where(condition, 1.0, 0.0).astype(BF16)


def project_query_kernel(
    groups, rows, assign_ref, tokens_ref, weight_ref, cotan_ref, out_ref, slot_ref, counts_ref, mixed_ref
):
    toks = tokens_ref.shape[0]
    per_group = CLUSTERS // groups
    heads = weight_ref.shape[1] // HD
    member = iota((CLUSTERS, toks), 0) == assign_ref[...]
    member_f = jnp.where(member, 1.0, 0.0)
    member_b = member_f.astype(BF16)
    upto = ones_where(iota((toks, toks), 0) <= iota((toks, toks), 1))
    running = dot(member_b, upto)
    counts = jnp.broadcast_to(jnp.sum(member_f, axis=1, keepdims=True), (CLUSTERS, LANES))
    here, other = iota((CLUSTERS, CLUSTERS), 0), iota((CLUSTERS, CLUSTERS), 1)
    group_of = lambda index: lax.div(index, jnp.int32(per_group))
    earlier = ones_where((other < here) & (group_of(other) == group_of(here)))
    base = dot(earlier, counts.astype(BF16))[:, :1]
    base = base + (group_of(iota((CLUSTERS, 1), 0)) * rows).astype(F32)
    slot = jnp.sum(member_f * (running - 1.0 + base), axis=0, keepdims=True).astype(jnp.int32)
    slot_ref[...] = slot
    counts_ref[...] = dot_nt(jnp.ones((8, toks), BF16), member_b).astype(jnp.int32)

    step = min(256, toks)

    @pl.loop(0, toks // step)
    def _(i):
        where = pl.ds(pl.multiple_of(i * step, step), step)
        query = dot(tokens_ref[where, :], weight_ref[...])
        cotan = cotan_ref[where, :].astype(F32)
        low = low_half((step, LANES))
        for pair in range(heads // 2):
            q_tile = query[:, pair * LANES : (pair + 1) * LANES]
            c_tile = cotan[:, pair * LANES : (pair + 1) * LANES]
            even = jnp.where(low, q_tile, swap_halves(c_tile)).astype(BF16)
            odd = jnp.where(low, swap_halves(q_tile), c_tile).astype(BF16)
            mixed_ref[where, 2 * pair * LANES : (2 * pair + 1) * LANES] = even
            mixed_ref[where, (2 * pair + 1) * LANES : (2 * pair + 2) * LANES] = odd

    part = min(256, rows)
    pieces = rows // part

    @pl.loop(0, groups * pieces)
    def _(i):
        group, piece = lax.div(i, jnp.int32(pieces)), lax.rem(i, jnp.int32(pieces))
        first = pl.multiple_of(piece * part, part)
        pick = ones_where(iota((part, toks), 0) + i * part == slot_ref[...])
        sorted_rows = dot(pick, mixed_ref[...]).astype(BF16)
        for head in range(heads):
            out_ref[group * heads + head, pl.ds(first, part), :] = sorted_rows[
                :, head * LANES : (head + 1) * LANES
            ]


def project_value_kernel(groups, rows, slot_ref, tokens_ref, weight_ref, out_ref, value_ref):
    toks = tokens_ref.shape[0]
    heads = weight_ref.shape[1] // HD
    step = min(256, toks)

    @pl.loop(0, toks // step)
    def _(i):
        where = pl.ds(pl.multiple_of(i * step, step), step)
        value_ref[where, :] = dot(tokens_ref[where, :], weight_ref[...]).astype(BF16)

    half = rows // 2
    part = min(256, half)
    pieces = half // part

    @pl.loop(0, groups * pieces)
    def _(i):
        group, piece = lax.div(i, jnp.int32(pieces)), lax.rem(i, jnp.int32(pieces))
        first = pl.multiple_of(piece * part, part)
        index = iota((part, toks), 0) + group * rows + first
        upper = dot(ones_where(index == slot_ref[...]), value_ref[...])
        lower = dot(ones_where(index + half == slot_ref[...]), value_ref[...])
        low = low_half((part, LANES))
        for pair in range(heads // 2):
            up = upper[:, pair * LANES : (pair + 1) * LANES]
            down = lower[:, pair * LANES : (pair + 1) * LANES]
            even = jnp.where(low, up, swap_halves(down)).astype(BF16)
            odd = jnp.where(low, swap_halves(up), down).astype(BF16)
            out_ref[group * heads + 2 * pair, pl.ds(first, part), :] = even
            out_ref[group * heads + 2 * pair + 1, pl.ds(first, part), :] = odd


def sort_tokens_kernel(slot_ref, tokens_ref, out_ref):
    toks = tokens_ref.shape[0]
    slots = out_ref.shape[1]
    turned = tokens_ref[...].T
    part = min(256, slots)

    for i in range(slots // part):
        pick = ones_where(iota((part, toks), 0) + i * part == slot_ref[...])
        out_ref[:, i * part : (i + 1) * part] = dot_nt(turned, pick).astype(BF16)


def softmax_turned(mixed, query):
    scores = dot_nt(query, mixed) * SCALE
    shape = scores.shape
    seen = iota(shape, 0) <= iota(shape, 1)
    scores = jnp.where(seen, scores, -jnp.inf)
    raised = jnp.exp(scores - jnp.max(scores, axis=0, keepdims=True))
    return raised * (1.0 / jnp.sum(raised, axis=0, keepdims=True))


def for_each_cluster(counts_ref, first_ref, place_ref, owners, per_group, slot_rows, body):
    for source in range(owners):
        place_ref[source] = 0

    @pl.loop(0, per_group)
    def _(cluster):
        runs = []
        total = 0
        for source in range(owners):
            count = counts_ref[source * 8, first_ref[0] + cluster]
            start = place_ref[source]
            runs.append((source, start, total))
            place_ref[source] = start + count
            total = total + count
        body(cluster, runs, total)


def value_grad_kernel(
    per_group, slot_rows, first_ref, counts_ref, mixed_ref, out_ref, place_ref, wide_ref, block_ref, grad_ref, home_ref
):
    owners, rows, _ = mixed_ref.shape
    capacity = block_ref.shape[0] - slot_rows
    for source in range(owners):
        wide_ref[source, :rows, :] = mixed_ref[source].astype(F32)
        wide_ref[source, rows:, :] = jnp.zeros((slot_rows, LANES), F32)

    def body(cluster, runs, total):
        for source, start, before in runs:
            block_ref[pl.ds(before, slot_rows), :] = wide_ref[source, pl.ds(start, slot_rows), :]
        low = low_half((BLOCK_ROWS, LANES))
        for first in range(0, capacity, BLOCK_ROWS):
            filled = iota((BLOCK_ROWS, LANES), 0) + first < total
            mixed = jnp.where(filled, block_ref[first : first + BLOCK_ROWS, :], 0.0)
            query = jnp.where(low, mixed, 0.0).astype(BF16)
            mixed = mixed.astype(BF16)
            probs_half = softmax_turned(mixed, query).astype(BF16)
            grad_ref[first : first + BLOCK_ROWS, :] = dot(probs_half, mixed)
        for source, start, before in runs:
            home_ref[source, pl.ds(start, slot_rows), :] = grad_ref[pl.ds(before, slot_rows), :]

    for_each_cluster(counts_ref, first_ref, place_ref, owners, per_group, slot_rows, body)
    half = rows // 2
    for source in range(owners):
        up, down = home_ref[source, :half, :], home_ref[source, half:rows, :]
        out_ref[source] = jnp.where(low_half((half, LANES)), swap_halves(up), down).astype(BF16)


def query_grad_kernel(
    per_group,
    slot_rows,
    first_ref,
    counts_ref,
    mixed_ref,
    value_in_ref,
    out_ref,
    sums_ref,
    place_ref,
    wide_ref,
    value_ref,
    block_ref,
    value_block_ref,
    grad_ref,
    home_ref,
):
    owners, rows, _ = mixed_ref.shape
    half = rows // 2
    capacity = block_ref.shape[0] - slot_rows
    for source in range(owners):
        wide_ref[source, :rows, :] = mixed_ref[source].astype(F32)
        wide_ref[source, rows:, :] = jnp.zeros((slot_rows, LANES), F32)
        value = value_in_ref[source].astype(F32)
        value_ref[source, :half, :] = swap_halves(value)
        value_ref[source, half:rows, :] = value
        value_ref[source, rows:, :] = jnp.zeros((slot_rows, LANES), F32)

    def body(cluster, runs, total):
        for source, start, before in runs:
            block_ref[pl.ds(before, slot_rows), :] = wide_ref[source, pl.ds(start, slot_rows), :]
            value_block_ref[pl.ds(before, slot_rows), :] = value_ref[source, pl.ds(start, slot_rows), :]
        low = low_half((BLOCK_ROWS, LANES))
        sums = jnp.zeros((1, LANES), F32)
        for first in range(0, capacity, BLOCK_ROWS):
            filled = iota((BLOCK_ROWS, LANES), 0) + first < total
            mixed = jnp.where(filled, block_ref[first : first + BLOCK_ROWS, :], 0.0)
            value = jnp.where(filled, value_block_ref[first : first + BLOCK_ROWS, :], 0.0).astype(BF16)
            query = jnp.where(low, mixed, 0.0).astype(BF16)
            cotan = jnp.where(low, 0.0, mixed).astype(BF16)
            probs = softmax_turned(mixed.astype(BF16), query)
            grad_probs = dot_nt(value, cotan)
            probs_half = probs.astype(BF16).astype(F32)
            row_dot = jnp.sum(probs_half * grad_probs, axis=0, keepdims=True)
            grad_scores = (probs * (grad_probs - row_dot)).astype(BF16).astype(F32)
            both = (grad_scores + grad_scores.T).astype(BF16)
            grad = (dot(both, query) * SCALE).astype(BF16).astype(F32)
            grad_ref[first : first + BLOCK_ROWS, :] = grad
            sums = sums + jnp.sum(grad, axis=0, keepdims=True)
        sums_ref[pl.ds(cluster, 1), :] = sums
        for source, start, before in runs:
            home_ref[source, pl.ds(start, slot_rows), :] = grad_ref[pl.ds(before, slot_rows), :]

    for_each_cluster(counts_ref, first_ref, place_ref, owners, per_group, slot_rows, body)
    for source in range(owners):
        up, down = home_ref[source, :half, :], home_ref[source, half:rows, :]
        out_ref[source] = jnp.where(low_half((half, LANES)), up, swap_halves(down)).astype(BF16)


def unfold(home_ref, out_ref, heads):
    owners, half, _ = home_ref.shape
    low = low_half((half, LANES))
    for group in range(owners // heads):
        first = group * 2 * half
        for pair in range(heads // 2):
            even = home_ref[group * heads + 2 * pair].astype(F32)
            odd = home_ref[group * heads + 2 * pair + 1].astype(F32)
            columns = slice(pair * LANES, (pair + 1) * LANES)
            out_ref[first : first + half, columns] = jnp.where(low, even, swap_halves(odd)).astype(BF16)
            out_ref[first + half : first + 2 * half, columns] = jnp.where(
                low, swap_halves(even), odd
            ).astype(BF16)


def weight_grad_kernel(heads, home_ref, turned_ref, out_ref, rows_ref):
    unfold(home_ref, rows_ref, heads)
    width = turned_ref.shape[0]
    step = min(256, width)

    @pl.loop(0, width // step)
    def _(i):
        where = pl.ds(pl.multiple_of(i * step, step), step)
        out_ref[where, :] = dot(turned_ref[where, :], rows_ref[...]).astype(BF16)


def input_grad_kernel(
    heads, me_ref, query_home_ref, value_rows_ref, w_query_ref, w_value_ref, turned_ref, *rest
):
    out_refs, weight_out_ref, rows_ref = rest[:-2], rest[-2], rest[-1]
    unfold(query_home_ref, rows_ref, heads)
    parts = len(out_refs)
    slots = rows_ref.shape[0]
    columns = w_query_ref.shape[0] // parts
    step = min(256, slots)
    for ahead, out_ref in enumerate(out_refs):
        dest = lax.rem(me_ref[0] + ahead, jnp.int32(parts))
        mine = pl.ds(pl.multiple_of(dest * columns, columns), columns)

        @pl.loop(0, slots // step)
        def _(i):
            where = pl.ds(pl.multiple_of(i * step, step), step)
            total = dot_nt(rows_ref[where, :], w_query_ref[mine, :])
            total = total + dot_nt(value_rows_ref[where, :], w_value_ref[mine, :])
            out_ref[where, :] = total.astype(BF16)

    width = turned_ref.shape[0]
    step_w = min(256, width)

    @pl.loop(0, width // step_w)
    def _(i):
        where = pl.ds(pl.multiple_of(i * step_w, step_w), step_w)
        weight_out_ref[where, :] = dot(turned_ref[where, :], rows_ref[...]).astype(BF16)


def unsort_kernel(slot_ref, *refs):
    part_refs, out_ref, total_ref = refs[:-2], refs[-2], refs[-1]
    total = part_refs[0][...].astype(F32)
    for part_ref in part_refs[1:]:
        total = total + part_ref[...].astype(F32)
    total_ref[...] = total.astype(BF16)
    toks = out_ref.shape[0]
    slots = total_ref.shape[0]
    step = min(256, toks)

    @pl.loop(0, toks // step)
    def _(i):
        where = pl.ds(pl.multiple_of(i * step, step), step)
        pick = ones_where(iota((step, slots), 1) == slot_ref[where, :])
        out_ref[where, :] = dot(pick, total_ref[...]).astype(BF16)


def call(kernel, outs, inputs, smem=(), scratch=(), flops=0, name=None):
    specs = [
        pl.BlockSpec(memory_space=pltpu.SMEM if i in smem else pltpu.VMEM) for i in range(len(inputs))
    ]
    moved = sum(x.size * x.dtype.itemsize for x in inputs) + sum(
        x.size * x.dtype.itemsize for x in jax.tree.leaves(outs)
    )
    return pl.pallas_call(
        kernel,
        out_shape=outs,
        in_specs=specs,
        out_specs=jax.tree.map(lambda _: pl.BlockSpec(memory_space=pltpu.VMEM), outs),
        scratch_shapes=list(scratch),
        compiler_params=pltpu.CompilerParams(vmem_limit_bytes=VMEM_LIMIT),
        cost_estimate=pl.CostEstimate(flops=flops, bytes_accessed=moved, transcendentals=0),
        name=name,
    )(*inputs)


def exchange(rows):
    return lax.all_to_all(rows, OWNERS, split_axis=0, concat_axis=0, tiled=True)


def on_device(tokens_in, w_query, w_value, cotangent, assignment):
    owners = lax.axis_size(OWNERS)
    parts = lax.axis_size("head")
    toks, width = tokens_in.shape
    width_dev = cotangent.shape[1]
    heads = width_dev // HD
    slot_rows = 2 * toks // CLUSTERS
    assert owners % heads == 0 and heads % 2 == 0
    groups = owners // heads
    per_group = CLUSTERS // groups
    rows = toks if groups == 1 else per_group * slot_rows
    half = rows // 2
    slots = groups * rows
    capacity = (slot_rows * owners + BLOCK_ROWS - 1) // BLOCK_ROWS * BLOCK_ROWS
    shape = jax.ShapeDtypeStruct

    assign_row = assignment.reshape(1, toks)
    send_mixed, slot_row, counts = call(
        functools.partial(project_query_kernel, groups, rows),
        (
            shape((owners, rows, LANES), BF16),
            shape((1, toks), jnp.int32),
            shape((8, CLUSTERS), jnp.int32),
        ),
        (assign_row, tokens_in, w_query, cotangent),
        scratch=[pltpu.VMEM((toks, 2 * width_dev), BF16)],
        flops=2 * toks * width * width_dev + 4 * slots * toks * width_dev,
        name="project_query",
    )
    got_mixed = exchange(send_mixed)
    all_counts = lax.all_gather(counts, OWNERS, axis=0, tiled=True)
    send_value = call(
        functools.partial(project_value_kernel, groups, rows),
        shape((owners, half, LANES), BF16),
        (slot_row, tokens_in, w_value),
        scratch=[pltpu.VMEM((toks, width_dev), BF16)],
        flops=2 * toks * width * width_dev + 2 * slots * toks * width_dev,
        name="project_value",
    )
    got_value = exchange(send_value)
    turned = call(
        sort_tokens_kernel,
        shape((width, slots), BF16),
        (slot_row, tokens_in),
        flops=2 * slots * toks * width,
        name="sort_tokens",
    )
    owner = lax.axis_index(OWNERS)
    first = (lax.div(owner, jnp.int32(heads)) * per_group).astype(jnp.int32).reshape(1)
    blocks = per_group * capacity // BLOCK_ROWS
    block_flops = 2 * BLOCK_ROWS * BLOCK_ROWS * LANES
    tall = pltpu.VMEM((owners, rows + slot_rows, LANES), F32)
    block = pltpu.VMEM((capacity + slot_rows, LANES), F32)
    place = pltpu.SMEM((owners,), jnp.int32)
    back_value = call(
        functools.partial(value_grad_kernel, per_group, slot_rows),
        shape((owners, half, LANES), BF16),
        (first, all_counts, got_mixed),
        smem=(0, 1),
        scratch=[place, tall, block, block, tall],
        flops=8 * blocks * block_flops,
        name="value_grad",
    )
    home_value = exchange(back_value)
    back_query, sums = call(
        functools.partial(query_grad_kernel, per_group, slot_rows),
        (shape((owners, half, LANES), BF16), shape((per_group, LANES), F32)),
        (first, all_counts, got_mixed, got_value),
        smem=(0, 1),
        scratch=[place, tall, tall, block, block, block, tall],
        flops=12 * blocks * block_flops,
        name="query_grad",
    )
    home_query = exchange(back_query)
    weight_flops = 2 * slots * width * width_dev
    partial_wv, value_rows = call(
        functools.partial(weight_grad_kernel, heads),
        (shape((width, width_dev), BF16), shape((slots, width_dev), BF16)),
        (home_value, turned),
        flops=weight_flops,
        name="weight_grad",
    )
    grad_wv = lax.psum_scatter(partial_wv, OWNERS, scatter_dimension=0, tiled=True).astype(F32)
    me = lax.axis_index("head").astype(jnp.int32).reshape(1)
    *partials, partial_wq = call(
        functools.partial(input_grad_kernel, heads),
        tuple([shape((slots, width // parts), BF16)] * parts + [shape((width, width_dev), BF16)]),
        (me, home_query, value_rows, w_query, w_value, turned),
        smem=(0,),
        scratch=[pltpu.VMEM((slots, width_dev), BF16)],
        flops=3 * weight_flops,
        name="input_grad",
    )
    arrived = [partials[0]]
    for ahead in range(1, parts):
        arrived.append(
            lax.ppermute(partials[ahead], "head", [(i, (i + ahead) % parts) for i in range(parts)])
        )
    grad_wq = lax.psum_scatter(partial_wq, OWNERS, scatter_dimension=0, tiled=True).astype(F32)
    grad_input = call(
        unsort_kernel,
        shape((toks, width // parts), BF16),
        (slot_row.reshape(toks, 1), *arrived),
        scratch=[pltpu.VMEM((slots, width // parts), BF16)],
        flops=2 * slots * toks * width // parts,
        name="unsort",
    )
    factor = (CLUSTERS / (toks * owners)) ** 0.5
    gathered = lax.all_gather(sums[:, :HD].astype(BF16), OWNERS, axis=0, tiled=False)
    gathered = gathered.reshape(groups, heads, per_group, HD).transpose(0, 2, 1, 3)
    centroid_grad = gathered.reshape(CLUSTERS, width_dev).astype(F32) * factor
    return (grad_input, grad_wq, grad_wv, centroid_grad)


def solution(mesh):
    return jax.shard_map(
        on_device,
        mesh=mesh,
        in_specs=(
            P(("grp", "seq", "sub"), None),
            P(None, "head"),
            P(None, "head"),
            P(("grp", "seq", "sub"), "head"),
            P(("grp", "seq", "sub"), None),
        ),
        out_specs=(
            P(("grp", "seq", "sub"), "head"),
            P(("grp", "seq", "sub"), "head"),
            P(("grp", "seq", "sub"), "head"),
            P("grp", "head"),
        ),
        check_vma=False,
    )
```

time: 654 us -> 322 us (0.49); the launches traced: 644 us -> 322 us
  waiting for transfers between devices: 307 us -> 97.9 us
  local copies, waits for them, and re-layouts: 157 us -> 4.39 us
  Pallas kernels: 0 us -> 134 us
  matrix products: 115 us -> 0 us
  blocking collectives: 0 us -> 47.6 us
  other arithmetic: 21 us -> 3.29 us
  starting transfers between devices: 29.5 us -> 20.4 us
    pallas_call x0 -> x8, Pallas kernels: none -> 134 us  [call(): pl.pallas_call(kernel, out_shape=outs, in_specs=specs, out_specs=jax.tree...]
    all_to_all x6 -> x4, waiting for transfers between devices: 176 us -> 59 us  [exchange(): return lax.all_to_all(rows, OWNERS, split_axis=0, concat_axis=0, tiled=True)]
    dot_general x47 -> x0, matrix products: 94.6 us -> none  [the longest x8 20.8 us: block_backward(): jnp.einsum('bhij,bihd->bjhd', probs_half, cotangent, preferred_element_ty...]
    unnamed x6 -> x2, waiting for transfers between devices: 63.4 us -> 0.71 us
    scatter x6 -> x0, local copies, waits for them, and re-layouts: 56.1 us -> none  [the longest x3 34.7 us: unpack(): compact.at[index_rows].set(rows.reshape(-1, width_dev), mode='drop')]
    all_gather x0 -> x2, blocking collectives: none -> 47.6 us  [the longest x1 33.4 us: on_device(): all_counts = lax.all_gather(counts, OWNERS, axis=0, tiled=True)]
    reshape x7 -> x1, local copies, waits for them, and re-layouts: 41.5 us -> 1.02 us  [on_device(): slot_row.reshape(toks, 1)]
    psum x1 -> x0, waiting for transfers between devices: 36.8 us -> none  [on_device(): lax.psum(local_sums.astype(jnp.bfloat16), ('seq', 'sub'))]
  transfers between devices with their start and end apart: 10 -> 7, of which waited for: 9 -> 5; matrix products, arithmetic and copies ran while one was open for 16% -> 1% of each run, Pallas kernels for 0% -> 36%
where the time goes in v1:
time: 322 us
  Pallas kernels  134 us (42%)
  waiting for transfers between devices  97.9 us (30%)
  blocking collectives  47.6 us (15%)
  starting transfers between devices  20.4 us (6%)
  between operations  14.1 us (4%)
  local copies, waits for them, and re-layouts  4.39 us (1%)
  other arithmetic  3.29 us (1%)
    pallas_call x8, Pallas kernels, call(): pl.pallas_call(kernel, out_shape=outs, in_specs=specs, out_specs=jax.tree...  134 us
    all_to_all x4, waiting for transfers between devices, exchange(): return lax.all_to_all(rows, OWNERS, split_axis=0, concat_axis=0, tiled=True)  59 us
    all_gather x1, blocking collectives, on_device(): all_counts = lax.all_gather(counts, OWNERS, axis=0, tiled=True)  33.4 us
    reduce_scatter x1, waiting for transfers between devices, on_device(): lax.psum_scatter(partial_wv, OWNERS, scatter_dimension=0, tiled=True)  31 us
    all_to_all x4, starting transfers between devices, exchange(): return lax.all_to_all(rows, OWNERS, split_axis=0, concat_axis=0, tiled=True)  18.8 us
    all_gather x1, blocking collectives, on_device(): lax.all_gather(sums[:, :HD].astype(BF16), OWNERS, axis=0, tiled=False)  14.2 us
    ppermute x1, waiting for transfers between devices, on_device(): lax.ppermute(partials[ahead], 'head', [(i, (i + ahead) % parts) for i in...  7.05 us
  transfers between devices with their start and end apart: 7, of which 5 were waited for; matrix products, arithmetic and copies ran while one was open for 1% of the time, Pallas kernels for 36%

profile of v1, /device:TPU:0, one launch (start us, length us, event | category | flops | bytes accessed | tf_op | source)
XLA Modules:
  0.0 321.9 jit_solution(5996155914155995915)
XLA Ops:
  7.2 9.0 %project_query.1 = (bf16[8,1024,128]{2,1,0:T(8,128)(2,1)}, s32[1,1024]{1,0:T(1,128)}, s32[8,64]{1,0:T(8,128)}) custom-call(s32[1,1024]{1,0:T(1,128)} %bitcast.11, bf16[1024,1024]{1,0:T(8,128)(2,1)} %tokens_ref.5, bf16[1024,512]{1,0:T(8,128)(2,1)} %w_query_ref.1, bf16[1024,512]{1,0:T(8,128)(2,1)} %cotan_ref.1), custom_call_target="tpu_custom_call" | custom-call | flops 3221225472 | bytes 6301696 | tf_op jit(solution)/shard_map/project_query/pallas_call | solution.py:333
  16.1 6.3 %all-to-all-start = ((bf16[8,1024,128]{2,1,0:T(8,128)(2,1)}), bf16[8,1024,128]{2,1,0:T(8,128)(2,1)S(1)}, u32[]{:S(2)}, u32[]{:S(2)}) async-start(bf16[8,1024,128]{2,1,0:T(8,128)(2,1)} %get-tuple-element.16), calls=%async_computation | async-start | bytes 4194304 | tf_op jit(solution)/shard_map/all_to_all | solution.py:346
  22.5 6.2 %project_value.1 = bf16[8,512,128]{2,1,0:T(8,128)(2,1)} custom-call(s32[1,1024]{1,0:T(1,128)} %get-tuple-element.14.slot_ref, bf16[1024,1024]{1,0:T(8,128)(2,1)} %tokens_ref.5, bf16[1024,512]{1,0:T(8,128)(2,1)} %w_value_ref.1), custom_call_target="tpu_custom_call" | custom-call | flops 2147483648 | bytes 4198400 | tf_op jit(solution)/shard_map/project_value/pallas_call | solution.py:333
  28.7 0.0 copy-start.6
  28.7 42.9 %all-to-all-done.mixed_ref = bf16[8,1024,128]{2,1,0:T(8,128)(2,1)S(1)} async-done(((bf16[8,1024,128]{2,1,0:T(8,128)(2,1)}), bf16[8,1024,128]{2,1,0:T(8,128)(2,1)S(1)}, u32[]{:S(2)}, u32[]{:S(2)}) %all-to-all-start) | async-done | bytes 2097184 | tf_op jit(solution)/shard_map/all_to_all | solution.py:346
  71.5 0.0 copy-start
  71.5 3.6 %all-to-all-start.1 = ((bf16[8,512,128]{2,1,0:T(8,128)(2,1)}), bf16[8,512,128]{2,1,0:T(8,128)(2,1)S(1)}, u32[]{:S(2)}, u32[]{:S(2)}) async-start(bf16[8,512,128]{2,1,0:T(8,128)(2,1)} %project_value.1), calls=%async_computation.1 | async-start | bytes 2097152 | tf_op jit(solution)/shard_map/all_to_all | solution.py:346
  75.1 0.0 copy-done.6
  75.1 33.4 %all_gather.9.counts_ref = s32[64,64]{1,0:T(8,128)} all-gather(s32[8,64]{1,0:T(8,128)S(1)} %copy-done.6), channel_id=1, replica_groups=mesh['grp'=2,'seq'=4,'head'=2,'sub'=2] {'seq','sub'}, dimensions={0}, use_global_device_ids=true | all-gather | bytes 18432 | tf_op jit(solution)/shard_map/all_gather | solution.py:379
  108.5 0.0 copy-done
  108.6 40.9 %value_grad.1 = bf16[8,512,128]{2,1,0:T(8,128)(2,1)} custom-call(s32[1]{0:T(128)} %bitcast.3.first_ref, s32[64,64]{1,0:T(8,128)} %all_gather.9.counts_ref, bf16[8,1024,128]{2,1,0:T(8,128)(2,1)} %copy-done), custom_call_target="tpu_custom_call" | custom-call | flops 4294967296 | bytes 3162116 | tf_op jit(solution)/shard_map/value_grad/pallas_call | solution.py:333
  149.4 0.0 all-to-all-done.1.value_in_ref
  149.4 0.0 copy-start.1
  149.4 3.9 %all-to-all-start.3 = ((bf16[8,512,128]{2,1,0:T(8,128)(2,1)}), bf16[8,512,128]{2,1,0:T(8,128)(2,1)S(1)}, u32[]{:S(2)}, u32[]{:S(2)}) async-start(bf16[8,512,128]{2,1,0:T(8,128)(2,1)} %value_grad.1), calls=%async_computation.3 | async-start | bytes 2097152 | tf_op jit(solution)/shard_map/all_to_all | solution.py:346
  153.3 0.0 copy-done.1
  153.3 52.7 %query_grad.1 = (bf16[8,512,128]{2,1,0:T(8,128)(2,1)}, f32[64,128]{1,0:T(8,128)}) custom-call(s32[1]{0:T(128)} %bitcast.3.first_ref, s32[64,64]{1,0:T(8,128)} %all_gather.9.counts_ref, bf16[8,1024,128]{2,1,0:T(8,128)(2,1)} %copy-done, bf16[8,512,128]{2,1,0:T(8,128)(2,1)} %copy-done.1), custom_call_target="tpu_custom_call" | custom-call | flops 6442450944 | bytes 4243460 | tf_op jit(solution)/shard_map/query_grad/pallas_call | solution.py:333
  206.0 0.0 all-to-all-done.3.home_ref
  206.0 0.0 copy-start.2
  206.0 5.1 %all-to-all-start.2 = ((bf16[8,512,128]{2,1,0:T(8,128)(2,1)}), bf16[8,512,128]{2,1,0:T(8,128)(2,1)S(1)}, u32[]{:S(2)}, u32[]{:S(2)}) async-start(bf16[8,512,128]{2,1,0:T(8,128)(2,1)} %get-tuple-element.17), calls=%async_computation.2 | async-start | bytes 2097152 | tf_op jit(solution)/shard_map/all_to_all | solution.py:346
  211.1 0.0 reduce-scatter.3.cloned.1.call-start
  211.2 5.3 %sort_tokens.1.turned_ref = bf16[1024,1024]{1,0:T(8,128)(2,1)} custom-call(s32[1,1024]{1,0:T(1,128)} %get-tuple-element.14.slot_ref, bf16[1024,1024]{1,0:T(8,128)(2,1)} %tokens_ref.5), custom_call_target="tpu_custom_call" | custom-call | flops 2147483648 | bytes 4198400 | tf_op jit(solution)/shard_map/sort_tokens/pallas_call | solution.py:333
  216.5 0.0 copy-done.2
  216.5 5.1 %weight_grad.1 = (bf16[1024,512]{1,0:T(8,128)(2,1)}, bf16[1024,512]{1,0:T(8,128)(2,1)}) custom-call(bf16[8,512,128]{2,1,0:T(8,128)(2,1)} %copy-done.2, bf16[1024,1024]{1,0:T(8,128)(2,1)} %sort_tokens.1.turned_ref), custom_call_target="tpu_custom_call" | custom-call | flops 1073741824 | bytes 5242880 | tf_op jit(solution)/shard_map/weight_grad/pallas_call | solution.py:333
  221.5 16.2 %all-to-all-done.2.query_home_ref = bf16[8,512,128]{2,1,0:T(8,128)(2,1)S(1)} async-done(((bf16[8,512,128]{2,1,0:T(8,128)(2,1)}), bf16[8,512,128]{2,1,0:T(8,128)(2,1)S(1)}, u32[]{:S(2)}, u32[]{:S(2)}) %all-to-all-start.2) | async-done | bytes 1048608 | tf_op jit(solution)/shard_map/all_to_all | solution.py:346
  237.7 0.0 copy-start.3
  237.7 1.0 copy-done.3
  238.7 10.1 %input_grad.1 = (bf16[1024,512]{1,0:T(8,128)(2,1)}, bf16[1024,512]{1,0:T(8,128)(2,1)}, bf16[1024,512]{1,0:T(8,128)(2,1)}) custom-call(s32[1]{0:T(128)} %bitcast.2.me_ref, bf16[8,512,128]{2,1,0:T(8,128)(2,1)} %copy-done.3, bf16[1024,512]{1,0:T(8,128)(2,1)} %get-tuple-element.18.value_rows_ref, bf16[1024,512]{1,0:T(8,128)(2,1)} %w_query_ref.1, ...), custom_call_target="tpu_custom_call" | custom-call | flops 3221225472 | bytes 9437188 | tf_op jit(solution)/shard_map/input_grad/pallas_call | solution.py:333
  248.8 0.0 copy-start.7
  248.8 0.0 copy-start.5
  248.8 0.0 copy-start.4
  248.8 0.0 reduce-scatter.3.cloned.1.call-update
  248.8 0.0 reduce-scatter.5.cloned.1.call-start
  248.8 0.7 reduce-scatter.5.cloned.1.call-update
  249.5 0.4 copy-done.7
  250.0 1.5 collective-permute-start
  251.5 0.0 copy-done.5
  251.5 1.0 copy.10.slot_ref
  252.5 0.0 copy-done.4
  252.5 14.2 %all-gather = bf16[512,64]{1,0:T(8,128)(2,1)S(1)} all-gather(bf16[64,64]{1,0:T(8,128)(2,1)S(1)} %slice.7), channel_id=2, replica_groups=mesh['grp'=2,'seq'=4,'head'=2,'sub'=2] {'seq','sub'}, dimensions={0}, use_global_device_ids=true | all-gather | bytes 73728 | tf_op jit(solution)/shard_map/all_gather | solution.py:457
  266.7 0.2 copy.11
  266.9 0.8 mul.27
  267.6 7.0 %collective-permute-done.refs_1_ = bf16[1024,512]{1,0:T(8,128)(2,1)S(1)} collective-permute-done((bf16[1024,512]{1,0:T(8,128)(2,1)S(1)}, bf16[1024,512]{1,0:T(8,128)(2,1)S(1)}, u32[]{:S(2)}, u32[]{:S(2)}) %collective-permute-start) | collective-permute-done | bytes 1048608 | tf_op jit(solution)/shard_map/ppermute | solution.py:445
  274.7 1.0 copy-done.8
  275.7 5.0 %unsort.1 = bf16[1024,512]{1,0:T(8,128)(2,1)} custom-call(s32[1024,1]{1,0:T(8,128)} %copy.10.slot_ref, bf16[1024,512]{1,0:T(8,128)(2,1)} %get-tuple-element.19.refs_0_, bf16[1024,512]{1,0:T(8,128)(2,1)} %copy-done.8), custom_call_target="tpu_custom_call" | custom-call | flops 1073741824 | bytes 3149824 | tf_op jit(solution)/shard_map/unsort/pallas_call | solution.py:333
  280.7 0.1 reduce-scatter.3.cloned.1.call-done
  280.8 1.6 convert_element_type.13
  282.4 31.0 %reduce-scatter.5.cloned.1.call-done = bf16[128,512]{1,0:T(8,128)(2,1)} async-done(((bf16[1024,512]{1,0:T(8,128)(2,1)}), bf16[128,512]{1,0:T(8,128)(2,1)}) %reduce-scatter.5.cloned.1.call-update) | async-done | bytes 131088 | tf_op jit(solution)/shard_map/reduce_scatter | solution.py:431
  313.4 1.6 convert_element_type.14
  (3 shorter events, 0.0 us)
Async XLA Ops:
  16.1 55.4 %all-to-all-start = ((bf16[8,1024,128]{2,1,0:T(8,128)(2,1)}), bf16[8,1024,128]{2,1,0:T(8,128)(2,1)S(1)}, u32[]{:S(2)}, u32[]{:S(2)}) async-start(bf16[8,1024,128]{2,1,0:T(8,128)(2,1)} %get-tuple-element.16), calls=%async_computation | async-start | bytes 4194304 | tf_op jit(solution)/shard_map/all_to_all | solution.py:346
  28.7 46.4 %copy-start.6 = (s32[8,64]{1,0:T(8,128)S(1)}, s32[8,64]{1,0:T(8,128)}, u32[]{:S(2)}) copy-start(s32[8,64]{1,0:T(8,128)} %get-tuple-element.15) | copy-start | bytes 6148
  71.5 37.0 %copy-start = (bf16[8,1024,128]{2,1,0:T(8,128)(2,1)}, bf16[8,1024,128]{2,1,0:T(8,128)(2,1)S(1)}, u32[]{:S(2)}) copy-start(bf16[8,1024,128]{2,1,0:T(8,128)(2,1)S(1)} %all-to-all-done.mixed_ref) | copy-start | bytes 6291460
  71.5 77.9 %all-to-all-start.1 = ((bf16[8,512,128]{2,1,0:T(8,128)(2,1)}), bf16[8,512,128]{2,1,0:T(8,128)(2,1)S(1)}, u32[]{:S(2)}, u32[]{:S(2)}) async-start(bf16[8,512,128]{2,1,0:T(8,128)(2,1)} %project_value.1), calls=%async_computation.1 | async-start | bytes 2097152 | tf_op jit(solution)/shard_map/all_to_all | solution.py:346
  149.4 3.9 %copy-start.1 = (bf16[8,512,128]{2,1,0:T(8,128)(2,1)}, bf16[8,512,128]{2,1,0:T(8,128)(2,1)S(1)}, u32[]{:S(2)}) copy-start(bf16[8,512,128]{2,1,0:T(8,128)(2,1)S(1)} %all-to-all-done.1.value_in_ref) | copy-start | bytes 3145732
  149.4 56.6 %all-to-all-start.3 = ((bf16[8,512,128]{2,1,0:T(8,128)(2,1)}), bf16[8,512,128]{2,1,0:T(8,128)(2,1)S(1)}, u32[]{:S(2)}, u32[]{:S(2)}) async-start(bf16[8,512,128]{2,1,0:T(8,128)(2,1)} %value_grad.1), calls=%async_computation.3 | async-start | bytes 2097152 | tf_op jit(solution)/shard_map/all_to_all | solution.py:346
  206.0 10.5 %copy-start.2 = (bf16[8,512,128]{2,1,0:T(8,128)(2,1)}, bf16[8,512,128]{2,1,0:T(8,128)(2,1)S(1)}, u32[]{:S(2)}) copy-start(bf16[8,512,128]{2,1,0:T(8,128)(2,1)S(1)} %all-to-all-done.3.home_ref) | copy-start | bytes 3145732
  206.0 31.7 %all-to-all-start.2 = ((bf16[8,512,128]{2,1,0:T(8,128)(2,1)}), bf16[8,512,128]{2,1,0:T(8,128)(2,1)S(1)}, u32[]{:S(2)}, u32[]{:S(2)}) async-start(bf16[8,512,128]{2,1,0:T(8,128)(2,1)} %get-tuple-element.17), calls=%async_computation.2 | async-start | bytes 2097152 | tf_op jit(solution)/shard_map/all_to_all | solution.py:346
  211.1 69.7 %reduce-scatter.3.cloned.1.call-start = ((), (), s32[]{:S(2)}) async-start(), calls=%async_computation.6 | async-start | bytes 1179648 | tf_op jit(solution)/shard_map/reduce_scatter | solution.py:447
  237.7 1.0 copy-start.3
  248.8 1.2 copy-start.7
  248.8 2.7 copy-start.5
  248.8 3.7 %copy-start.4 = (f32[64,128]{1,0:T(8,128)S(1)}, f32[64,128]{1,0:T(8,128)}, u32[]{:S(2)}) copy-start(f32[64,128]{1,0:T(8,128)} %get-tuple-element.23) | copy-start | bytes 98308
  248.8 64.6 %reduce-scatter.5.cloned.1.call-start = ((), (), s32[]{:S(2)}) async-start(), calls=%async_computation.7 | async-start | bytes 1179648 | tf_op jit(solution)/shard_map/reduce_scatter | solution.py:431
  250.0 24.7 %collective-permute-start = (bf16[1024,512]{1,0:T(8,128)(2,1)S(1)}, bf16[1024,512]{1,0:T(8,128)(2,1)S(1)}, u32[]{:S(2)}, u32[]{:S(2)}) collective-permute-start(bf16[1024,512]{1,0:T(8,128)(2,1)S(1)} %copy-done.7), channel_id=1, source_target_pairs={{0,2},{2,0},{1,3},{3,1},{4,6},{6,4},{5,7},{7,5},{8,10},{10,8},{9,1... | collective-permute-start | bytes 3145736 | tf_op jit(solution)/shard_map/ppermute | solution.py:445
  274.7 1.0 copy-start.8
Sparse Core Ops, SparseCore 0:
  248.9 31.8 reduce-scatter.2
  283.1 30.2 reduce-scatter.4

commit v2 on v1

v2 whole, which is shorter than its diff:
```python
import functools

import jax
import jax.numpy as jnp
from jax import lax
from jax.experimental import pallas as pl
from jax.experimental.pallas import tpu as pltpu
from jax.sharding import PartitionSpec as P

HD = 64
CLUSTERS = 64
BLOCK_ROWS = 128
LANES = 128
UNROLL = 4
COUNT_ROWS = 16
SCALE = 0.5 * HD ** (-0.5)
F32 = jnp.float32
BF16 = jnp.bfloat16
VMEM_LIMIT = 56 * 1024 * 1024
OWNERS = ("seq", "sub")


def iota(shape, dim):
    return lax.broadcasted_iota(jnp.int32, shape, dim)


def low_half(shape):
    return iota(shape, 1) < HD


def swap_halves(tile):
    return pltpu.roll(tile, HD, 1)


def dot(a, b):
    return jnp.dot(a, b, preferred_element_type=F32)


def dot_nt(a, b):
    return lax.dot_general(a, b, (((1,), (1,)), ((), ())), preferred_element_type=F32)


def ones_where(condition):
    return jnp.where(condition, 1.0, 0.0).astype(BF16)


def project_query_kernel(
    groups, rows, assign_ref, tokens_ref, weight_ref, cotan_ref, out_ref, slot_ref, mixed_ref
):
    toks = tokens_ref.shape[0]
    per_group = CLUSTERS // groups
    heads = weight_ref.shape[1] // HD
    member = iota((CLUSTERS, toks), 0) == assign_ref[...]
    member_f = jnp.where(member, 1.0, 0.0)
    member_b = member_f.astype(BF16)
    upto = ones_where(iota((toks, toks), 0) <= iota((toks, toks), 1))
    running = dot(member_b, upto)
    counts = jnp.broadcast_to(jnp.sum(member_f, axis=1, keepdims=True), (CLUSTERS, LANES))
    here, other = iota((CLUSTERS, CLUSTERS), 0), iota((CLUSTERS, CLUSTERS), 1)
    group_of = lambda index: lax.div(index, jnp.int32(per_group))
    earlier = ones_where((other < here) & (group_of(other) == group_of(here)))
    base = dot(earlier, counts.astype(BF16))[:, :1]
    base = base + (group_of(iota((CLUSTERS, 1), 0)) * rows).astype(F32)
    slot = jnp.sum(member_f * (running - 1.0 + base), axis=0, keepdims=True).astype(jnp.int32)
    slot_ref[...] = slot
    spread = jnp.concatenate([member_b, jnp.zeros((LANES - CLUSTERS, toks), BF16)], axis=0)
    tallies = dot_nt(jnp.ones((COUNT_ROWS, toks), BF16), spread).astype(BF16)
    for owner in range(out_ref.shape[0]):
        out_ref[owner, rows:, :] = tallies

    step = min(256, toks)

    @pl.loop(0, toks // step)
    def _(i):
        where = pl.ds(pl.multiple_of(i * step, step), step)
        query = dot(tokens_ref[where, :], weight_ref[...])
        cotan = cotan_ref[where, :].astype(F32)
        low = low_half((step, LANES))
        for pair in range(heads // 2):
            q_tile = query[:, pair * LANES : (pair + 1) * LANES]
            c_tile = cotan[:, pair * LANES : (pair + 1) * LANES]
            even = jnp.where(low, q_tile, swap_halves(c_tile)).astype(BF16)
            odd = jnp.where(low, swap_halves(q_tile), c_tile).astype(BF16)
            mixed_ref[where, 2 * pair * LANES : (2 * pair + 1) * LANES] = even
            mixed_ref[where, (2 * pair + 1) * LANES : (2 * pair + 2) * LANES] = odd

    part = min(256, rows)
    pieces = rows // part

    @pl.loop(0, groups * pieces)
    def _(i):
        group, piece = lax.div(i, jnp.int32(pieces)), lax.rem(i, jnp.int32(pieces))
        first = pl.multiple_of(piece * part, part)
        pick = ones_where(iota((part, toks), 0) + i * part == slot_ref[...])
        sorted_rows = dot(pick, mixed_ref[...]).astype(BF16)
        for head in range(heads):
            out_ref[group * heads + head, pl.ds(first, part), :] = sorted_rows[
                :, head * LANES : (head + 1) * LANES
            ]


def project_value_kernel(groups, rows, slot_ref, tokens_ref, weight_ref, out_ref, value_ref):
    toks = tokens_ref.shape[0]
    heads = weight_ref.shape[1] // HD
    step = min(256, toks)

    @pl.loop(0, toks // step)
    def _(i):
        where = pl.ds(pl.multiple_of(i * step, step), step)
        value_ref[where, :] = dot(tokens_ref[where, :], weight_ref[...]).astype(BF16)

    half = rows // 2
    part = min(256, half)
    pieces = half // part

    @pl.loop(0, groups * pieces)
    def _(i):
        group, piece = lax.div(i, jnp.int32(pieces)), lax.rem(i, jnp.int32(pieces))
        first = pl.multiple_of(piece * part, part)
        index = iota((part, toks), 0) + group * rows + first
        upper = dot(ones_where(index == slot_ref[...]), value_ref[...])
        lower = dot(ones_where(index + half == slot_ref[...]), value_ref[...])
        low = low_half((part, LANES))
        for pair in range(heads // 2):
            up = upper[:, pair * LANES : (pair + 1) * LANES]
            down = lower[:, pair * LANES : (pair + 1) * LANES]
            even = jnp.where(low, up, swap_halves(down)).astype(BF16)
            odd = jnp.where(low, swap_halves(up), down).astype(BF16)
            out_ref[group * heads + 2 * pair, pl.ds(first, part), :] = even
            out_ref[group * heads + 2 * pair + 1, pl.ds(first, part), :] = odd


def sort_tokens_kernel(slot_ref, tokens_ref, out_ref):
    toks = tokens_ref.shape[0]
    slots = out_ref.shape[1]
    turned = tokens_ref[...].T
    part = min(256, slots)

    for i in range(slots // part):
        pick = ones_where(iota((part, toks), 0) + i * part == slot_ref[...])
        out_ref[:, i * part : (i + 1) * part] = dot_nt(turned, pick).astype(BF16)


def softmax_turned(mixed):
    query = jnp.where(low_half(mixed.shape), mixed.astype(F32) * SCALE, 0.0).astype(BF16)
    scores = dot_nt(query, mixed)
    shape = scores.shape
    seen = iota(shape, 0) <= iota(shape, 1)
    scores = jnp.where(seen, scores, -jnp.inf)
    raised = jnp.exp(scores - jnp.max(scores, axis=0, keepdims=True))
    return raised * (1.0 / jnp.sum(raised, axis=0, keepdims=True))


def load_counts(mixed_ref, rows, wide_counts_ref, counts_ref):
    for source in range(mixed_ref.shape[0]):
        tail = mixed_ref[source, rows:, :].astype(F32).astype(jnp.int32)
        wide_counts_ref[source : source + 1, :] = tail[:1, :]
    pltpu.sync_copy(wide_counts_ref, counts_ref)


def for_each_cluster(counts_ref, first_ref, place_ref, owners, per_group, body):
    for source in range(owners):
        place_ref[source] = 0

    def step(cluster, block):
        runs = []
        total = 0
        base = block * BLOCK_ROWS
        for source in range(owners):
            count = counts_ref[source, first_ref[0] + cluster]
            start = place_ref[source]
            runs.append((source, start, base + total))
            place_ref[source] = start + count
            total = total + count
        body(cluster, block, runs, base + total)
        return block + lax.shift_right_logical(total + (BLOCK_ROWS - 1), jnp.int32(7))

    return lax.fori_loop(0, per_group, step, jnp.int32(0))


def for_each_block(blocks, body):
    def step(i, carry):
        for ahead in range(UNROLL):
            body(i * UNROLL + ahead)
        return carry

    lax.fori_loop(0, lax.div(blocks + (UNROLL - 1), jnp.int32(UNROLL)), step, 0)


def block_rows(block):
    return pl.ds(pl.multiple_of(block * BLOCK_ROWS, BLOCK_ROWS), BLOCK_ROWS)


def value_grad_kernel(
    per_group,
    slot_rows,
    first_ref,
    mixed_ref,
    out_ref,
    dense_ref,
    wide_counts_ref,
    counts_ref,
    place_ref,
    wide_ref,
    block_ref,
):
    owners = mixed_ref.shape[0]
    rows = 2 * out_ref.shape[1]
    load_counts(mixed_ref, rows, wide_counts_ref, counts_ref)
    for source in range(owners):
        wide_ref[source, :rows, :] = mixed_ref[source, :rows, :].astype(F32)
        wide_ref[source, rows:, :] = jnp.zeros((slot_rows, LANES), F32)

    def gather(cluster, block, runs, end):
        for source, start, row in runs:
            block_ref[pl.ds(row, slot_rows), :] = wide_ref[source, pl.ds(start, slot_rows), :]
        block_ref[pl.ds(end, BLOCK_ROWS), :] = jnp.zeros((BLOCK_ROWS, LANES), F32)

    blocks = for_each_cluster(counts_ref, first_ref, place_ref, owners, per_group, gather)
    spare = pl.ds(pl.multiple_of(blocks * BLOCK_ROWS, BLOCK_ROWS), UNROLL * BLOCK_ROWS)
    block_ref[spare, :] = jnp.zeros((UNROLL * BLOCK_ROWS, LANES), F32)

    def one_block(block):
        where = block_rows(block)
        mixed = block_ref[where, :].astype(BF16)
        dense_ref[where, :] = mixed
        probs_half = softmax_turned(mixed).astype(BF16)
        block_ref[where, :] = dot(probs_half, mixed)

    for_each_block(blocks, one_block)

    def scatter(cluster, block, runs, end):
        for source, start, row in runs:
            wide_ref[source, pl.ds(start, slot_rows), :] = block_ref[pl.ds(row, slot_rows), :]

    for_each_cluster(counts_ref, first_ref, place_ref, owners, per_group, scatter)
    half = rows // 2
    for source in range(owners):
        up, down = wide_ref[source, :half, :], wide_ref[source, half:rows, :]
        out_ref[source] = jnp.where(low_half((half, LANES)), swap_halves(up), down).astype(BF16)


def query_grad_kernel(
    per_group,
    slot_rows,
    first_ref,
    counts_in_ref,
    dense_ref,
    value_in_ref,
    out_ref,
    wide_counts_ref,
    counts_ref,
    place_ref,
    wide_ref,
    block_ref,
    sums_ref,
    centroid_ref,
):
    owners, half, _ = value_in_ref.shape
    rows = 2 * half
    load_counts(counts_in_ref, 0, wide_counts_ref, counts_ref)
    for source in range(owners):
        value = value_in_ref[source].astype(F32)
        wide_ref[source, :half, :] = swap_halves(value)
        wide_ref[source, half:rows, :] = value
        wide_ref[source, rows:, :] = jnp.zeros((slot_rows, LANES), F32)

    def gather(cluster, block, runs, end):
        for source, start, row in runs:
            block_ref[pl.ds(row, slot_rows), :] = wide_ref[source, pl.ds(start, slot_rows), :]
        block_ref[pl.ds(end, BLOCK_ROWS), :] = jnp.zeros((BLOCK_ROWS, LANES), F32)

    blocks = for_each_cluster(counts_ref, first_ref, place_ref, owners, per_group, gather)
    spare = pl.ds(pl.multiple_of(blocks * BLOCK_ROWS, BLOCK_ROWS), UNROLL * BLOCK_ROWS)
    block_ref[spare, :] = jnp.zeros((UNROLL * BLOCK_ROWS, LANES), F32)

    def one_block(block):
        where = block_rows(block)
        mixed = dense_ref[where, :]
        value = block_ref[where, :].astype(BF16)
        low = low_half((BLOCK_ROWS, LANES))
        cotan = jnp.where(low, jnp.zeros_like(mixed), mixed)
        probs = softmax_turned(mixed)
        grad_probs = dot_nt(value, cotan)
        probs_half = probs.astype(BF16).astype(F32)
        row_dot = jnp.sum(probs_half * grad_probs, axis=0, keepdims=True)
        grad_scores = (probs * (grad_probs - row_dot)).astype(BF16).astype(F32)
        both = (grad_scores + grad_scores.T).astype(BF16)
        grad = (dot(both, mixed) * SCALE).astype(BF16).astype(F32)
        block_ref[where, :] = grad
        sums_ref[pl.ds(block, 1), :] = jnp.sum(grad, axis=0, keepdims=True)

    for_each_block(blocks, one_block)

    most = owners * slot_rows // BLOCK_ROWS if owners * slot_rows >= BLOCK_ROWS else 1

    def scatter(cluster, block, runs, end):
        total = jnp.zeros((1, LANES), F32)
        for ahead in range(most):
            here = block + ahead
            total = total + jnp.where(here * BLOCK_ROWS < end, sums_ref[pl.ds(here, 1), :], 0.0)
        centroid_ref[pl.ds(cluster, 1), :] = total
        for source, start, row in runs:
            wide_ref[source, pl.ds(start, slot_rows), :] = block_ref[pl.ds(row, slot_rows), :]

    for_each_cluster(counts_ref, first_ref, place_ref, owners, per_group, scatter)
    extra = out_ref.shape[1] - half
    centroid = jnp.where(
        low_half((extra, LANES)), centroid_ref[:extra, :], swap_halves(centroid_ref[extra:, :])
    ).astype(BF16)
    for source in range(owners):
        up, down = wide_ref[source, :half, :], wide_ref[source, half:rows, :]
        out_ref[source, :half, :] = jnp.where(low_half((half, LANES)), up, swap_halves(down)).astype(BF16)
        out_ref[source, half:, :] = centroid


def unfold(home_ref, out_ref, heads, start, half, finish):
    low = low_half((half, LANES))
    for group in range(home_ref.shape[0] // heads):
        first = group * 2 * half
        for pair in range(heads // 2):
            even = home_ref[group * heads + 2 * pair, start : start + half, :].astype(F32)
            odd = home_ref[group * heads + 2 * pair + 1, start : start + half, :].astype(F32)
            columns = slice(pair * LANES, (pair + 1) * LANES)
            out_ref[first : first + half, columns] = finish(jnp.where(low, even, swap_halves(odd)))
            out_ref[first + half : first + 2 * half, columns] = finish(
                jnp.where(low, swap_halves(even), odd)
            )


def to_half(x):
    return x.astype(BF16)


def unfold_kernel(heads, home_ref, out_ref):
    unfold(home_ref, out_ref, heads, 0, home_ref.shape[1], to_half)


def weight_grad_kernel(me_ref, turned_ref, rows_ref, *out_refs):
    subs = len(out_refs)
    seqs, piece, _ = out_refs[0].shape
    for ahead, out_ref in enumerate(out_refs):
        sub = lax.rem(me_ref[0] + ahead, jnp.int32(subs))

        @pl.loop(0, seqs)
        def _(seq):
            where = pl.ds(pl.multiple_of((seq * subs + sub) * piece, piece), piece)
            out_ref[seq] = dot(turned_ref[where, :], rows_ref[...]).astype(BF16)


def fold_subs_kernel(me_ref, *refs):
    seqs = refs[0].shape[0]
    terms, out_refs = refs[:-seqs], refs[-seqs:]
    for ahead, out_ref in enumerate(out_refs):
        seq = lax.rem(me_ref[0] + ahead, jnp.int32(seqs))
        total = terms[0][seq].astype(F32)
        for term in terms[1:]:
            total = total + term[seq].astype(F32)
        out_ref[...] = total.astype(BF16)


def sum_kernel(*refs):
    total = refs[0][...].astype(F32)
    for ref in refs[1:-1]:
        total = total + ref[...].astype(F32)
    refs[-1][...] = total


def input_grad_kernel(
    heads, factor, me_ref, query_home_ref, value_rows_ref, w_query_ref, w_value_ref, *rest
):
    out_refs, rows_ref, centroid_ref = rest[:-2], rest[-2], rest[-1]
    parts = len(out_refs)
    slots = rows_ref.shape[0]
    half = slots * heads // query_home_ref.shape[0] // 2
    unfold(query_home_ref, rows_ref, heads, 0, half, to_half)
    extra = query_home_ref.shape[1] - half
    unfold(query_home_ref, centroid_ref, heads, half, extra, lambda x: x * factor)
    columns = w_query_ref.shape[0] // parts
    step = min(256, slots)
    for ahead, out_ref in enumerate(out_refs):
        dest = lax.rem(me_ref[0] + ahead, jnp.int32(parts))
        mine = pl.ds(pl.multiple_of(dest * columns, columns), columns)

        @pl.loop(0, slots // step)
        def _(i):
            where = pl.ds(pl.multiple_of(i * step, step), step)
            total = dot_nt(rows_ref[where, :], w_query_ref[mine, :])
            total = total + dot_nt(value_rows_ref[where, :], w_value_ref[mine, :])
            out_ref[where, :] = total.astype(BF16)


def unsort_kernel(slot_ref, *refs):
    part_refs, out_ref, total_ref = refs[:-2], refs[-2], refs[-1]
    total = part_refs[0][...].astype(F32)
    for part_ref in part_refs[1:]:
        total = total + part_ref[...].astype(F32)
    total_ref[...] = total.astype(BF16)
    toks = out_ref.shape[0]
    slots = total_ref.shape[0]
    step = min(256, toks)

    @pl.loop(0, toks // step)
    def _(i):
        where = pl.ds(pl.multiple_of(i * step, step), step)
        pick = ones_where(iota((step, slots), 1) == slot_ref[where, :])
        out_ref[where, :] = dot(pick, total_ref[...]).astype(BF16)


def call(kernel, outs, inputs, smem=(), scratch=(), flops=0, name=None):
    specs = [
        pl.BlockSpec(memory_space=pltpu.SMEM if i in smem else pltpu.VMEM) for i in range(len(inputs))
    ]
    moved = sum(x.size * x.dtype.itemsize for x in inputs) + sum(
        x.size * x.dtype.itemsize for x in jax.tree.leaves(outs)
    )
    return pl.pallas_call(
        kernel,
        out_shape=outs,
        in_specs=specs,
        out_specs=jax.tree.map(lambda _: pl.BlockSpec(memory_space=pltpu.VMEM), outs),
        scratch_shapes=list(scratch),
        compiler_params=pltpu.CompilerParams(vmem_limit_bytes=VMEM_LIMIT),
        cost_estimate=pl.CostEstimate(flops=flops, bytes_accessed=moved, transcendentals=0),
        name=name,
    )(*inputs)


def exchange(rows):
    return lax.all_to_all(rows, OWNERS, split_axis=0, concat_axis=0, tiled=True)


def pass_round(parts, axis):
    size = len(parts)
    return [parts[0]] + [
        lax.ppermute(parts[ahead], axis, [(i, (i + ahead) % size) for i in range(size)])
        for ahead in range(1, size)
    ]


def index_of(axis):
    return lax.axis_index(axis).astype(jnp.int32).reshape(1)


def weight_grad(turned, rows, name):
    seqs, subs = lax.axis_size("seq"), lax.axis_size("sub")
    width, slots = turned.shape
    columns = rows.shape[1]
    piece = width // (seqs * subs)
    shape = jax.ShapeDtypeStruct
    by_sub = call(
        weight_grad_kernel,
        (shape((seqs, piece, columns), BF16),) * subs,
        (index_of("sub"), turned, rows),
        smem=(0,),
        flops=2 * slots * width * columns,
        name=name,
    )
    by_seq = call(
        fold_subs_kernel,
        (shape((piece, columns), BF16),) * seqs,
        (index_of("seq"), *pass_round(by_sub, "sub")),
        smem=(0,),
        name=name + "_subs",
    )
    return call(
        sum_kernel, shape((piece, columns), F32), tuple(pass_round(by_seq, "seq")), name=name + "_sum"
    )


def on_device(tokens_in, w_query, w_value, cotangent, assignment):
    owners = lax.axis_size(OWNERS)
    parts = lax.axis_size("head")
    toks, width = tokens_in.shape
    width_dev = cotangent.shape[1]
    heads = width_dev // HD
    slot_rows = 2 * toks // CLUSTERS
    assert owners % heads == 0 and heads % 2 == 0
    groups = owners // heads
    per_group = CLUSTERS // groups
    rows = toks if groups == 1 else per_group * slot_rows
    half = rows // 2
    slots = groups * rows
    capacity = (slot_rows * owners + BLOCK_ROWS - 1) // BLOCK_ROWS * BLOCK_ROWS
    extra = max(per_group // 2, 16)
    shape = jax.ShapeDtypeStruct

    assign_row = assignment.reshape(1, toks)
    send_mixed, slot_row = call(
        functools.partial(project_query_kernel, groups, rows),
        (shape((owners, rows + COUNT_ROWS, LANES), BF16), shape((1, toks), jnp.int32)),
        (assign_row, tokens_in, w_query, cotangent),
        scratch=[pltpu.VMEM((toks, 2 * width_dev), BF16)],
        flops=2 * toks * width * width_dev + 4 * slots * toks * width_dev,
        name="project_query",
    )
    got_mixed = exchange(send_mixed)
    send_value = call(
        functools.partial(project_value_kernel, groups, rows),
        shape((owners, half, LANES), BF16),
        (slot_row, tokens_in, w_value),
        scratch=[pltpu.VMEM((toks, width_dev), BF16)],
        flops=2 * toks * width * width_dev + 2 * slots * toks * width_dev,
        name="project_value",
    )
    got_value = exchange(send_value)
    turned = call(
        sort_tokens_kernel,
        shape((width, slots), BF16),
        (slot_row, tokens_in),
        flops=2 * slots * toks * width,
        name="sort_tokens",
    )
    owner = lax.axis_index(OWNERS)
    first = (lax.div(owner, jnp.int32(heads)) * per_group).astype(jnp.int32).reshape(1)
    blocks = per_group * capacity // BLOCK_ROWS
    dense_rows = blocks * BLOCK_ROWS
    block_flops = 2 * BLOCK_ROWS * BLOCK_ROWS * LANES
    common = [
        pltpu.VMEM((owners, LANES), jnp.int32),
        pltpu.SMEM((owners, LANES), jnp.int32),
        pltpu.SMEM((owners,), jnp.int32),
        pltpu.VMEM((owners, rows + slot_rows, LANES), F32),
        pltpu.VMEM((dense_rows + UNROLL * BLOCK_ROWS, LANES), F32),
    ]
    back_value, dense = call(
        functools.partial(value_grad_kernel, per_group, slot_rows),
        (shape((owners, half, LANES), BF16), shape((dense_rows, LANES), BF16)),
        (first, got_mixed),
        smem=(0,),
        scratch=common,
        flops=4 * blocks * block_flops,
        name="value_grad",
    )
    home_value = exchange(back_value)
    back_query = call(
        functools.partial(query_grad_kernel, per_group, slot_rows),
        shape((owners, half + extra, LANES), BF16),
        (first, got_mixed[:, rows:, :], dense, got_value),
        smem=(0,),
        scratch=common + [pltpu.VMEM((blocks + 8, LANES), F32), pltpu.VMEM((2 * extra, LANES), F32)],
        flops=6 * blocks * block_flops,
        name="query_grad",
    )
    home_query = exchange(back_query)
    weight_flops = 2 * slots * width * width_dev
    value_rows = call(
        functools.partial(unfold_kernel, heads), shape((slots, width_dev), BF16), (home_value,), name="unfold"
    )
    grad_wv = weight_grad(turned, value_rows, "value_weight")
    *partials, query_rows, centroid_grad = call(
        functools.partial(input_grad_kernel, heads, (CLUSTERS / (toks * owners)) ** 0.5),
        (shape((slots, width // parts), BF16),) * parts
        + (shape((slots, width_dev), BF16), shape((groups * 2 * extra, width_dev), F32)),
        (index_of("head"), home_query, value_rows, w_query, w_value),
        smem=(0,),
        flops=2 * weight_flops,
        name="input_grad",
    )
    arrived = pass_round(partials, "head")
    grad_wq = weight_grad(turned, query_rows, "query_weight")
    grad_input = call(
        unsort_kernel,
        shape((toks, width // parts), BF16),
        (slot_row.reshape(toks, 1), *arrived),
        scratch=[pltpu.VMEM((slots, width // parts), BF16)],
        flops=2 * slots * toks * width // parts,
        name="unsort",
    )
    if groups > 1:
        centroid_grad = centroid_grad.reshape(groups, 2 * extra, width_dev)[:, :per_group]
        centroid_grad = centroid_grad.reshape(CLUSTERS, width_dev)
    return (grad_input, grad_wq, grad_wv, centroid_grad)


def solution(mesh):
    return jax.shard_map(
        on_device,
        mesh=mesh,
        in_specs=(
            P(("grp", "seq", "sub"), None),
            P(None, "head"),
            P(None, "head"),
            P(("grp", "seq", "sub"), "head"),
            P(("grp", "seq", "sub"), None),
        ),
        out_specs=(
            P(("grp", "seq", "sub"), "head"),
            P(("grp", "seq", "sub"), "head"),
            P(("grp", "seq", "sub"), "head"),
            P("grp", "head"),
        ),
        check_vma=False,
    )
```

time: 322 us -> 239 us (0.74)
  blocking collectives: 47.6 us -> 0 us
  waiting for transfers between devices: 97.9 us -> 77.3 us
  between operations: 14.1 us -> 0.7 us
  Pallas kernels: 134 us -> 121 us
  starting transfers between devices: 20.4 us -> 31.7 us
  other arithmetic: 3.29 us -> 0 us
    all_gather x2 -> x0, blocking collectives: 47.6 us -> none  [the longest x1 33.4 us: on_device(): all_counts = lax.all_gather(counts, OWNERS, axis=0, tiled=True)]
    reduce_scatter x2 -> x0, waiting for transfers between devices: 31.1 us -> none  [the longest x1 31 us: on_device(): lax.psum_scatter(partial_wv, OWNERS, scatter_dimension=0, tiled=True)]
    pallas_call x8 -> x14, Pallas kernels: 134 us -> 121 us  [call(): pl.pallas_call(kernel, out_shape=outs, in_specs=specs, out_specs=jax.tree...]
    ppermute x1 -> x9, starting transfers between devices: 1.49 us -> 11.7 us  [pass_round(): lax.ppermute(parts[ahead], axis, [(i, (i + ahead) % size) for i in range(...]
    all_to_all x4, waiting for transfers between devices: 59 us -> 69 us  [exchange(): return lax.all_to_all(rows, OWNERS, split_axis=0, concat_axis=0, tiled=True)]
    convert_element_type x2 -> x0, other arithmetic: 3.26 us -> none  [the longest x1 1.63 us: on_device(): lax.psum_scatter(partial_wq, OWNERS, scatter_dimension=0, tiled=True)]
    ppermute x1 -> x9, waiting for transfers between devices: 7.05 us -> 8.3 us  [pass_round(): lax.ppermute(parts[ahead], axis, [(i, (i + ahead) % size) for i in range(...]
  transfers between devices with their start and end apart: 7 -> 13, of which waited for: 5 -> 5; matrix products, arithmetic and copies ran while one was open for 1% -> 1% of each run, Pallas kernels for 36% -> 42%
where the time goes in v2:
time: 239 us; the launch traced here: 238 us
  Pallas kernels  121 us (51%)
  waiting for transfers between devices  77.3 us (32%)
  starting transfers between devices  31.7 us (13%)
  local copies, waits for them, and re-layouts  7.34 us (3%)
    pallas_call x14, Pallas kernels, call(): pl.pallas_call(kernel, out_shape=outs, in_specs=specs, out_specs=jax.tree...  121 us
    all_to_all x4, waiting for transfers between devices, exchange(): return lax.all_to_all(rows, OWNERS, split_axis=0, concat_axis=0, tiled=True)  69 us
    all_to_all x4, starting transfers between devices, exchange(): return lax.all_to_all(rows, OWNERS, split_axis=0, concat_axis=0, tiled=True)  20 us
    ppermute x9, starting transfers between devices, pass_round(): lax.ppermute(parts[ahead], axis, [(i, (i + ahead) % size) for i in range(...  11.7 us
    ppermute x9, waiting for transfers between devices, pass_round(): lax.ppermute(parts[ahead], axis, [(i, (i + ahead) % size) for i in range(...  8.3 us
    unnamed x28, local copies, waits for them, and re-layouts  4.94 us
  transfers between devices with their start and end apart: 13, of which 5 were waited for; matrix products, arithmetic and copies ran while one was open for 1% of the time, Pallas kernels for 42%

profile of v2, /device:TPU:0, one launch (start us, length us, event | category | flops | bytes accessed | tf_op | source)
XLA Modules:
  0.0 238.3 jit_solution(9009038539716244827)
XLA Ops:
  0.6 9.0 %project_query.1 = (bf16[8,1040,128]{2,1,0:T(8,128)(2,1)}, s32[1,1024]{1,0:T(1,128)}) custom-call(s32[1,1024]{1,0:T(1,128)} %bitcast.7, bf16[1024,1024]{1,0:T(8,128)(2,1)} %tokens_ref.5, bf16[1024,512]{1,0:T(8,128)(2,1)} %w_query_ref.1, bf16[1024,512]{1,0:T(8,128)(2,1)} %cotan_ref.1), custom_call_target="tpu_custom_call" | custom-call | flops 3221225472 | bytes 6332416 | tf_op jit(solution)/shard_map/project_query/pallas_call | solution.py:417
  9.7 6.3 %all-to-all-start = ((bf16[8,1040,128]{2,1,0:T(8,128)(2,1)}), bf16[8,1040,128]{2,1,0:T(8,128)(2,1)S(1)}, u32[]{:S(2)}, u32[]{:S(2)}) async-start(bf16[8,1040,128]{2,1,0:T(8,128)(2,1)} %get-tuple-element.25), calls=%async_computation | async-start | bytes 4259840 | tf_op jit(solution)/shard_map/all_to_all | solution.py:430
  16.0 6.2 %project_value.1 = bf16[8,512,128]{2,1,0:T(8,128)(2,1)} custom-call(s32[1,1024]{1,0:T(1,128)} %get-tuple-element.24.slot_ref, bf16[1024,1024]{1,0:T(8,128)(2,1)} %tokens_ref.5, bf16[1024,512]{1,0:T(8,128)(2,1)} %w_value_ref.1), custom_call_target="tpu_custom_call" | custom-call | flops 2147483648 | bytes 4198400 | tf_op jit(solution)/shard_map/project_value/pallas_call | solution.py:417
  22.2 43.6 %all-to-all-done.mixed_ref = bf16[8,1040,128]{2,1,0:T(8,128)(2,1)S(1)} async-done(((bf16[8,1040,128]{2,1,0:T(8,128)(2,1)}), bf16[8,1040,128]{2,1,0:T(8,128)(2,1)S(1)}, u32[]{:S(2)}, u32[]{:S(2)}) %all-to-all-start) | async-done | bytes 2129952 | tf_op jit(solution)/shard_map/all_to_all | solution.py:430
  65.7 3.6 %all-to-all-start.1 = ((bf16[8,512,128]{2,1,0:T(8,128)(2,1)}), bf16[8,512,128]{2,1,0:T(8,128)(2,1)S(1)}, u32[]{:S(2)}, u32[]{:S(2)}) async-start(bf16[8,512,128]{2,1,0:T(8,128)(2,1)} %project_value.1), calls=%async_computation.1 | async-start | bytes 2097152 | tf_op jit(solution)/shard_map/all_to_all | solution.py:430
  69.3 30.7 %value_grad.1 = (bf16[8,512,128]{2,1,0:T(8,128)(2,1)}, bf16[16384,128]{1,0:T(8,128)(2,1)}) custom-call(s32[1]{0:T(128)} %bitcast.3.first_ref, bf16[8,1040,128]{2,1,0:T(8,128)(2,1)} %copy-done.1), custom_call_target="tpu_custom_call" | custom-call | flops 2147483648 | bytes 7372804 | tf_op jit(solution)/shard_map/value_grad/pallas_call | solution.py:417
  100.0 0.0 all-to-all-done.1.value_in_ref
  100.0 5.0 %all-to-all-start.3 = ((bf16[8,512,128]{2,1,0:T(8,128)(2,1)}), bf16[8,512,128]{2,1,0:T(8,128)(2,1)S(1)}, u32[]{:S(2)}, u32[]{:S(2)}) async-start(bf16[8,512,128]{2,1,0:T(8,128)(2,1)} %get-tuple-element.27), calls=%async_computation.3 | async-start | bytes 2097152 | tf_op jit(solution)/shard_map/all_to_all | solution.py:430
  105.0 1.4 slice.4.counts_in_ref
  106.4 36.5 %query_grad.1 = bf16[8,544,128]{2,1,0:T(8,128)(2,1)} custom-call(s32[1]{0:T(128)} %bitcast.3.first_ref, bf16[8,16,128]{2,1,0:T(8,128)(2,1)} %slice.4.counts_in_ref, bf16[16384,128]{1,0:T(8,128)(2,1)} %get-tuple-element.26.dense_ref, bf16[8,512,128]{2,1,0:T(8,128)(2,1)} %copy-done.3), custom_call_target="tpu_custom_call" | custom-call | flops 3221225472 | bytes 6389764 | tf_op jit(solution)/shard_map/query_grad/pallas_call | solution.py:417
  142.9 0.0 all-to-all-done.3.home_ref
  142.9 5.1 %all-to-all-start.2 = ((bf16[8,544,128]{2,1,0:T(8,128)(2,1)}), bf16[8,544,128]{2,1,0:T(8,128)(2,1)S(1)}, u32[]{:S(2)}, u32[]{:S(2)}) async-start(bf16[8,544,128]{2,1,0:T(8,128)(2,1)} %query_grad.1), calls=%async_computation.2 | async-start | bytes 2228224 | tf_op jit(solution)/shard_map/all_to_all | solution.py:430
  148.0 2.6 %unfold.1.value_rows_ref.rows_ref = bf16[1024,512]{1,0:T(8,128)(2,1)} custom-call(bf16[8,512,128]{2,1,0:T(8,128)(2,1)} %copy-done), custom_call_target="tpu_custom_call" | custom-call | bytes 2097152 | tf_op jit(solution)/shard_map/unfold/pallas_call | solution.py:417
  150.7 25.4 %all-to-all-done.2.query_home_ref = bf16[8,544,128]{2,1,0:T(8,128)(2,1)S(1)} async-done(((bf16[8,544,128]{2,1,0:T(8,128)(2,1)}), bf16[8,544,128]{2,1,0:T(8,128)(2,1)S(1)}, u32[]{:S(2)}, u32[]{:S(2)}) %all-to-all-start.2) | async-done | bytes 1114144 | tf_op jit(solution)/shard_map/all_to_all | solution.py:430
  176.0 1.0 copy-done.2
  177.0 7.8 %input_grad.1 = (bf16[1024,512]{1,0:T(8,128)(2,1)}, bf16[1024,512]{1,0:T(8,128)(2,1)}, bf16[1024,512]{1,0:T(8,128)(2,1)}, f32[64,512]{1,0:T(8,128)}) custom-call(s32[1]{0:T(128)} %bitcast.2.me_ref, bf16[8,544,128]{2,1,0:T(8,128)(2,1)} %copy-done.2, bf16[1024,512]{1,0:T(8,128)(2,1)} %unfold.1.value_rows_ref.rows_ref, bf16[1024,512]{1,0:T(8,128)(2,1)} %w_query_ref.1, ...), custom_call_target="tpu_custom_call" | custom-call | flops 2147483648 | bytes 7536644 | tf_op jit(solution)/shard_map/input_grad/pallas_call | solution.py:417
  184.8 1.5 collective-permute-start
  186.3 5.3 %sort_tokens.1.turned_ref = bf16[1024,1024]{1,0:T(8,128)(2,1)} custom-call(s32[1,1024]{1,0:T(1,128)} %get-tuple-element.24.slot_ref, bf16[1024,1024]{1,0:T(8,128)(2,1)} %tokens_ref.5), custom_call_target="tpu_custom_call" | custom-call | flops 2147483648 | bytes 4198400 | tf_op jit(solution)/shard_map/sort_tokens/pallas_call | solution.py:417
  191.6 5.2 %value_weight.1 = (bf16[4,128,512]{2,1,0:T(8,128)(2,1)}, bf16[4,128,512]{2,1,0:T(8,128)(2,1)}) custom-call(s32[1]{0:T(128)} %bitcast.5.me_ref, bf16[1024,1024]{1,0:T(8,128)(2,1)} %sort_tokens.1.turned_ref, bf16[1024,512]{1,0:T(8,128)(2,1)} %unfold.1.value_rows_ref.rows_ref), custom_call_target="tpu_custom_call" | custom-call | flops 1073741824 | bytes 4194308 | tf_op jit(solution)/shard_map/value_weight/pallas_call | solution.py:417
  196.8 0.0 collective-permute-start.5
  196.8 5.2 %query_weight.1 = (bf16[4,128,512]{2,1,0:T(8,128)(2,1)}, bf16[4,128,512]{2,1,0:T(8,128)(2,1)}) custom-call(s32[1]{0:T(128)} %bitcast.5.me_ref, bf16[1024,1024]{1,0:T(8,128)(2,1)} %sort_tokens.1.turned_ref, bf16[1024,512]{1,0:T(8,128)(2,1)} %get-tuple-element.30.rows_ref), custom_call_target="tpu_custom_call" | custom-call | flops 1073741824 | bytes 4194308 | tf_op jit(solution)/shard_map/query_weight/pallas_call | solution.py:417
  202.0 0.5 collective-permute-start.1
  202.5 0.0 collective-permute-done.5.refs_1_
  202.5 0.8 copy-done.5
  203.3 2.0 value_weight_subs.1
  205.3 0.0 collective-permute-start.6
  205.3 1.8 collective-permute-start.7
  207.2 2.0 collective-permute-start.8
  209.2 0.0 collective-permute-done.1.refs_1_
  209.2 0.8 copy-done.4
  210.0 2.0 query_weight_subs.1
  212.0 0.6 collective-permute-start.2
  212.6 1.3 collective-permute-done.6.refs_1_
  213.8 0.3 collective-permute-start.3
  214.1 5.3 %collective-permute-done.7.refs_2_ = bf16[128,512]{1,0:T(8,128)(2,1)S(1)} collective-permute-done((bf16[128,512]{1,0:T(8,128)(2,1)}, bf16[128,512]{1,0:T(8,128)(2,1)S(1)}, u32[]{:S(2)}, u32[]{:S(2)}) %collective-permute-start.7) | collective-permute-done | bytes 131104 | tf_op jit(solution)/shard_map/ppermute | solution.py:436
  219.4 5.0 %collective-permute-start.4 = (bf16[128,512]{1,0:T(8,128)(2,1)}, bf16[128,512]{1,0:T(8,128)(2,1)S(1)}, u32[]{:S(2)}, u32[]{:S(2)}) collective-permute-start(bf16[128,512]{1,0:T(8,128)(2,1)} %get-tuple-element.36), channel_id=1, source_target_pairs={{0,12},{4,0},{8,4},{12,8},{1,13},{5,1},{9,5},{13,9},{2,14},{6,2},{... | collective-permute-start | bytes 393224 | tf_op jit(solution)/shard_map/ppermute | solution.py:436
  224.5 1.0 copy.9.slot_ref
  225.5 0.0 collective-permute-done.8.refs_3_
  225.5 0.6 copy-done.8
  226.1 1.9 value_weight_sum.1
  228.0 0.0 collective-permute-done.2.refs_1_
  228.0 1.7 collective-permute-done.3.refs_2_
  229.7 0.0 collective-permute-done.4.refs_3_
  229.7 0.6 copy-done.10
  230.3 0.1 copy-done.11
  230.4 1.9 query_weight_sum.1
  232.3 1.0 copy-done.13
  233.2 5.0 %unsort.1 = bf16[1024,512]{1,0:T(8,128)(2,1)} custom-call(s32[1024,1]{1,0:T(8,128)} %copy.9.slot_ref, bf16[1024,512]{1,0:T(8,128)(2,1)} %get-tuple-element.28.refs_0_, bf16[1024,512]{1,0:T(8,128)(2,1)} %copy-done.13), custom_call_target="tpu_custom_call" | custom-call | flops 1073741824 | bytes 3149824 | tf_op jit(solution)/shard_map/unsort/pallas_call | solution.py:417
  (22 shorter events, 0.0 us)
Async XLA Ops:
  9.7 56.1 %all-to-all-start = ((bf16[8,1040,128]{2,1,0:T(8,128)(2,1)}), bf16[8,1040,128]{2,1,0:T(8,128)(2,1)S(1)}, u32[]{:S(2)}, u32[]{:S(2)}) async-start(bf16[8,1040,128]{2,1,0:T(8,128)(2,1)} %get-tuple-element.25), calls=%async_computation | async-start | bytes 4259840 | tf_op jit(solution)/shard_map/all_to_all | solution.py:430
  65.7 3.6 %copy-start.1 = (bf16[8,1040,128]{2,1,0:T(8,128)(2,1)}, bf16[8,1040,128]{2,1,0:T(8,128)(2,1)S(1)}, u32[]{:S(2)}) copy-start(bf16[8,1040,128]{2,1,0:T(8,128)(2,1)S(1)} %all-to-all-done.mixed_ref) | copy-start | bytes 6389764
  65.7 34.3 %all-to-all-start.1 = ((bf16[8,512,128]{2,1,0:T(8,128)(2,1)}), bf16[8,512,128]{2,1,0:T(8,128)(2,1)S(1)}, u32[]{:S(2)}, u32[]{:S(2)}) async-start(bf16[8,512,128]{2,1,0:T(8,128)(2,1)} %project_value.1), calls=%async_computation.1 | async-start | bytes 2097152 | tf_op jit(solution)/shard_map/all_to_all | solution.py:430
  100.0 6.4 %copy-start.3 = (bf16[8,512,128]{2,1,0:T(8,128)(2,1)}, bf16[8,512,128]{2,1,0:T(8,128)(2,1)S(1)}, u32[]{:S(2)}) copy-start(bf16[8,512,128]{2,1,0:T(8,128)(2,1)S(1)} %all-to-all-done.1.value_in_ref) | copy-start | bytes 3145732
  100.0 42.9 %all-to-all-start.3 = ((bf16[8,512,128]{2,1,0:T(8,128)(2,1)}), bf16[8,512,128]{2,1,0:T(8,128)(2,1)S(1)}, u32[]{:S(2)}, u32[]{:S(2)}) async-start(bf16[8,512,128]{2,1,0:T(8,128)(2,1)} %get-tuple-element.27), calls=%async_computation.3 | async-start | bytes 2097152 | tf_op jit(solution)/shard_map/all_to_all | solution.py:430
  142.9 5.1 %copy-start = (bf16[8,512,128]{2,1,0:T(8,128)(2,1)}, bf16[8,512,128]{2,1,0:T(8,128)(2,1)S(1)}, u32[]{:S(2)}) copy-start(bf16[8,512,128]{2,1,0:T(8,128)(2,1)S(1)} %all-to-all-done.3.home_ref) | copy-start | bytes 3145732
  142.9 33.1 %all-to-all-start.2 = ((bf16[8,544,128]{2,1,0:T(8,128)(2,1)}), bf16[8,544,128]{2,1,0:T(8,128)(2,1)S(1)}, u32[]{:S(2)}, u32[]{:S(2)}) async-start(bf16[8,544,128]{2,1,0:T(8,128)(2,1)} %query_grad.1), calls=%async_computation.2 | async-start | bytes 2228224 | tf_op jit(solution)/shard_map/all_to_all | solution.py:430
  176.0 1.0 copy-start.2
  184.8 47.5 %collective-permute-start = (bf16[1024,512]{1,0:T(8,128)(2,1)}, bf16[1024,512]{1,0:T(8,128)(2,1)S(1)}, u32[]{:S(2)}, u32[]{:S(2)}) collective-permute-start(bf16[1024,512]{1,0:T(8,128)(2,1)} %get-tuple-element.29), channel_id=1, source_target_pairs={{0,2},{2,0},{1,3},{3,1},{4,6},{6,4},{5,7},{7,5},{8,10},{10,8},{9,1... | collective-permute-start | bytes 3145736 | tf_op jit(solution)/shard_map/ppermute | solution.py:436
  196.8 5.7 %collective-permute-start.5 = (bf16[4,128,512]{2,1,0:T(8,128)(2,1)}, bf16[4,128,512]{2,1,0:T(8,128)(2,1)S(1)}, u32[]{:S(2)}, u32[]{:S(2)}) collective-permute-start(bf16[4,128,512]{2,1,0:T(8,128)(2,1)} %get-tuple-element.38), channel_id=1, source_target_pairs={{0,1},{1,0},{2,3},{3,2},{4,5},{5,4},{6,7},{7,6},{8,9},{9,8},{10,11... | collective-permute-start | bytes 1572872 | tf_op jit(solution)/shard_map/ppermute | solution.py:436
  196.8 27.7 %copy-start.12 = (s32[1,1024]{1,0:T(1,128)S(1)}, s32[1,1024]{1,0:T(1,128)}, u32[]{:S(2)}) copy-start(s32[1,1024]{1,0:T(1,128)} %get-tuple-element.24.slot_ref) | copy-start | bytes 12292
  202.0 7.2 %collective-permute-start.1 = (bf16[4,128,512]{2,1,0:T(8,128)(2,1)}, bf16[4,128,512]{2,1,0:T(8,128)(2,1)S(1)}, u32[]{:S(2)}, u32[]{:S(2)}) collective-permute-start(bf16[4,128,512]{2,1,0:T(8,128)(2,1)} %get-tuple-element.32), channel_id=1, source_target_pairs={{0,1},{1,0},{2,3},{3,2},{4,5},{5,4},{6,7},{7,6},{8,9},{9,8},{10,11... | collective-permute-start | bytes 1572872 | tf_op jit(solution)/shard_map/ppermute | solution.py:436
  202.5 0.8 copy-start.5
  205.3 8.5 %collective-permute-start.6 = (bf16[128,512]{1,0:T(8,128)(2,1)}, bf16[128,512]{1,0:T(8,128)(2,1)S(1)}, u32[]{:S(2)}, u32[]{:S(2)}) collective-permute-start(bf16[128,512]{1,0:T(8,128)(2,1)} %get-tuple-element.40), channel_id=1, source_target_pairs={{0,4},{4,8},{8,12},{12,0},{1,5},{5,9},{9,13},{13,1},{2,6},{6,10},{... | collective-permute-start | bytes 393224 | tf_op jit(solution)/shard_map/ppermute | solution.py:436
  205.3 14.1 %collective-permute-start.7 = (bf16[128,512]{1,0:T(8,128)(2,1)}, bf16[128,512]{1,0:T(8,128)(2,1)S(1)}, u32[]{:S(2)}, u32[]{:S(2)}) collective-permute-start(bf16[128,512]{1,0:T(8,128)(2,1)} %get-tuple-element.41), channel_id=1, source_target_pairs={{0,8},{4,12},{8,0},{12,4},{1,9},{5,13},{9,1},{13,5},{2,10},{6,14},... | collective-permute-start | bytes 393224 | tf_op jit(solution)/shard_map/ppermute | solution.py:436
  207.2 18.3 %collective-permute-start.8 = (bf16[128,512]{1,0:T(8,128)(2,1)}, bf16[128,512]{1,0:T(8,128)(2,1)S(1)}, u32[]{:S(2)}, u32[]{:S(2)}) collective-permute-start(bf16[128,512]{1,0:T(8,128)(2,1)} %get-tuple-element.42), channel_id=1, source_target_pairs={{0,12},{4,0},{8,4},{12,8},{1,13},{5,1},{9,5},{13,9},{2,14},{6,2},{... | collective-permute-start | bytes 393224 | tf_op jit(solution)/shard_map/ppermute | solution.py:436
  209.2 0.8 copy-start.4
  212.0 16.0 %collective-permute-start.2 = (bf16[128,512]{1,0:T(8,128)(2,1)}, bf16[128,512]{1,0:T(8,128)(2,1)S(1)}, u32[]{:S(2)}, u32[]{:S(2)}) collective-permute-start(bf16[128,512]{1,0:T(8,128)(2,1)} %get-tuple-element.34), channel_id=1, source_target_pairs={{0,4},{4,8},{8,12},{12,0},{1,5},{5,9},{9,13},{13,1},{2,6},{6,10},{... | collective-permute-start | bytes 393224 | tf_op jit(solution)/shard_map/ppermute | solution.py:436
  213.8 11.6 %copy-start.6 = (bf16[128,512]{1,0:T(8,128)(2,1)}, bf16[128,512]{1,0:T(8,128)(2,1)S(1)}, u32[]{:S(2)}) copy-start(bf16[128,512]{1,0:T(8,128)(2,1)S(1)} %collective-permute-done.6.refs_1_) | copy-start | bytes 393220
  213.8 15.8 %collective-permute-start.3 = (bf16[128,512]{1,0:T(8,128)(2,1)}, bf16[128,512]{1,0:T(8,128)(2,1)S(1)}, u32[]{:S(2)}, u32[]{:S(2)}) collective-permute-start(bf16[128,512]{1,0:T(8,128)(2,1)} %get-tuple-element.35), channel_id=1, source_target_pairs={{0,8},{4,12},{8,0},{12,4},{1,9},{5,13},{9,1},{13,5},{2,10},{6,14},... | collective-permute-start | bytes 393224 | tf_op jit(solution)/shard_map/ppermute | solution.py:436
  219.4 6.1 %copy-start.7 = (bf16[128,512]{1,0:T(8,128)(2,1)}, bf16[128,512]{1,0:T(8,128)(2,1)S(1)}, u32[]{:S(2)}) copy-start(bf16[128,512]{1,0:T(8,128)(2,1)S(1)} %collective-permute-done.7.refs_2_) | copy-start | bytes 393220
  219.4 10.3 %collective-permute-start.4 = (bf16[128,512]{1,0:T(8,128)(2,1)}, bf16[128,512]{1,0:T(8,128)(2,1)S(1)}, u32[]{:S(2)}, u32[]{:S(2)}) collective-permute-start(bf16[128,512]{1,0:T(8,128)(2,1)} %get-tuple-element.36), channel_id=1, source_target_pairs={{0,12},{4,0},{8,4},{12,8},{1,13},{5,1},{9,5},{13,9},{2,14},{6,2},{... | collective-permute-start | bytes 393224 | tf_op jit(solution)/shard_map/ppermute | solution.py:436
  225.5 0.7 copy-start.8
  228.0 1.7 copy-start.9
  229.7 0.7 copy-start.10
  229.7 0.7 copy-start.11
  232.3 1.0 copy-start.13

commit v3 on v2

v3 whole, which is shorter than its diff:
```python
import functools

import jax
import jax.numpy as jnp
from jax import lax
from jax.experimental import pallas as pl
from jax.experimental.pallas import tpu as pltpu
from jax.sharding import PartitionSpec as P

HD = 64
CLUSTERS = 64
BLOCK_ROWS = 128
LANES = 128
UNROLL = 4
COUNT_ROWS = 16
SCALE = 0.5 * HD ** (-0.5)
F32 = jnp.float32
BF16 = jnp.bfloat16
VMEM_LIMIT = 56 * 1024 * 1024
OWNERS = ("seq", "sub")
GROUP_ROWS = UNROLL * BLOCK_ROWS
LEAD = 2


def iota(shape, dim):
    return lax.broadcasted_iota(jnp.int32, shape, dim)


def low_half(shape):
    return iota(shape, 1) < HD


def swap_halves(tile):
    return pltpu.roll(tile, HD, 1)


def dot(a, b):
    return jnp.dot(a, b, preferred_element_type=F32)


def dot_nt(a, b):
    return lax.dot_general(a, b, (((1,), (1,)), ((), ())), preferred_element_type=F32)


def ones_where(condition):
    return jnp.where(condition, 1.0, 0.0).astype(BF16)


def owner_of(me_ref, ahead, sizes):
    seq = lax.rem(me_ref[0] + ahead[0], jnp.int32(sizes[0]))
    sub = lax.rem(me_ref[1] + ahead[1], jnp.int32(sizes[1]))
    return seq * sizes[1] + sub


def source_of(me_ref, ahead, sizes):
    return owner_of(me_ref, ((sizes[0] - ahead[0]) % sizes[0], (sizes[1] - ahead[1]) % sizes[1]), sizes)


def steps_of(sizes):
    return [(seq, sub) for seq in range(sizes[0]) for sub in range(sizes[1])]


def hand_out(by_owner_ref, out_refs, me_ref, sizes):
    for ahead, out_ref in zip(steps_of(sizes), out_refs):
        out_ref[...] = by_owner_ref[owner_of(me_ref, ahead, sizes)]


def project_query_kernel(sizes, groups, rows, me_ref, assign_ref, tokens_ref, weight_ref, cotan_ref, *rest):
    out_refs, (slot_ref, mixed_ref, sorted_ref) = rest[:-3], rest[-3:]
    toks = tokens_ref.shape[0]
    per_group = CLUSTERS // groups
    heads = weight_ref.shape[1] // HD
    member = iota((CLUSTERS, toks), 0) == assign_ref[...]
    member_f = jnp.where(member, 1.0, 0.0)
    member_b = member_f.astype(BF16)
    upto = ones_where(iota((toks, toks), 0) <= iota((toks, toks), 1))
    running = dot(member_b, upto)
    counts = jnp.broadcast_to(jnp.sum(member_f, axis=1, keepdims=True), (CLUSTERS, LANES))
    here, other = iota((CLUSTERS, CLUSTERS), 0), iota((CLUSTERS, CLUSTERS), 1)
    group_of = lambda index: lax.div(index, jnp.int32(per_group))
    earlier = ones_where((other < here) & (group_of(other) == group_of(here)))
    base = dot(earlier, counts.astype(BF16))[:, :1]
    base = base + (group_of(iota((CLUSTERS, 1), 0)) * rows).astype(F32)
    slot = jnp.sum(member_f * (running - 1.0 + base), axis=0, keepdims=True).astype(jnp.int32)
    slot_ref[...] = slot
    spread = jnp.concatenate([member_b, jnp.zeros((LANES - CLUSTERS, toks), BF16)], axis=0)
    tallies = dot_nt(jnp.ones((COUNT_ROWS, toks), BF16), spread).astype(BF16)
    for owner in range(sorted_ref.shape[0]):
        sorted_ref[owner, rows:, :] = tallies

    step = min(512, toks)

    @pl.loop(0, toks // step)
    def _(i):
        where = pl.ds(pl.multiple_of(i * step, step), step)
        query = dot(tokens_ref[where, :], weight_ref[...])
        cotan = cotan_ref[where, :].astype(F32)
        low = low_half((step, LANES))
        for pair in range(heads // 2):
            q_tile = query[:, pair * LANES : (pair + 1) * LANES]
            c_tile = cotan[:, pair * LANES : (pair + 1) * LANES]
            even = jnp.where(low, q_tile, swap_halves(c_tile)).astype(BF16)
            odd = jnp.where(low, swap_halves(q_tile), c_tile).astype(BF16)
            mixed_ref[where, 2 * pair * LANES : (2 * pair + 1) * LANES] = even
            mixed_ref[where, (2 * pair + 1) * LANES : (2 * pair + 2) * LANES] = odd

    part = min(512, rows)
    pieces = rows // part

    @pl.loop(0, groups * pieces)
    def _(i):
        group, piece = lax.div(i, jnp.int32(pieces)), lax.rem(i, jnp.int32(pieces))
        first = pl.multiple_of(piece * part, part)
        pick = ones_where(iota((part, toks), 0) + i * part == slot_ref[...])
        sorted_rows = dot(pick, mixed_ref[...]).astype(BF16)
        for head in range(heads):
            sorted_ref[group * heads + head, pl.ds(first, part), :] = sorted_rows[
                :, head * LANES : (head + 1) * LANES
            ]

    hand_out(sorted_ref, out_refs, me_ref, sizes)


def project_value_kernel(
    sizes, groups, rows, parts, me_ref, slot_ref, tokens_ref, w_value_ref, w_query_ref, *rest
):
    owners = sizes[0] * sizes[1]
    out_refs, weight_refs, (turned_ref, value_ref, sorted_ref) = (
        rest[:owners],
        rest[owners : owners + parts],
        rest[owners + parts :],
    )
    toks = tokens_ref.shape[0]
    heads = w_value_ref.shape[1] // HD
    step = min(512, toks)

    @pl.loop(0, toks // step)
    def _(i):
        where = pl.ds(pl.multiple_of(i * step, step), step)
        value_ref[where, :] = dot(tokens_ref[where, :], w_value_ref[...]).astype(BF16)

    half = rows // 2
    part = min(256, half)
    pieces = half // part

    @pl.loop(0, groups * pieces)
    def _(i):
        group, piece = lax.div(i, jnp.int32(pieces)), lax.rem(i, jnp.int32(pieces))
        first = pl.multiple_of(piece * part, part)
        index = iota((part, toks), 0) + group * rows + first
        upper = dot(ones_where(index == slot_ref[...]), value_ref[...])
        lower = dot(ones_where(index + half == slot_ref[...]), value_ref[...])
        low = low_half((part, LANES))
        for pair in range(heads // 2):
            up = upper[:, pair * LANES : (pair + 1) * LANES]
            down = lower[:, pair * LANES : (pair + 1) * LANES]
            even = jnp.where(low, up, swap_halves(down)).astype(BF16)
            odd = jnp.where(low, swap_halves(up), down).astype(BF16)
            sorted_ref[group * heads + 2 * pair, pl.ds(first, part), :] = even
            sorted_ref[group * heads + 2 * pair + 1, pl.ds(first, part), :] = odd

    hand_out(sorted_ref, out_refs, me_ref, sizes)
    columns = w_query_ref.shape[0] // parts
    for ahead, weight_out_ref in enumerate(weight_refs):
        dest = lax.rem(me_ref[2] + ahead, jnp.int32(parts))
        mine = pl.ds(pl.multiple_of(dest * columns, columns), columns)
        weight_out_ref[0] = w_query_ref[mine, :]
        weight_out_ref[1] = w_value_ref[mine, :]
    turned = tokens_ref[...].T
    slots = turned_ref.shape[1]
    part = min(256, slots)
    for i in range(slots // part):
        pick = ones_where(iota((part, toks), 0) + i * part == slot_ref[...])
        turned_ref[:, i * part : (i + 1) * part] = dot_nt(turned, pick).astype(BF16)


def score(mixed):
    query = jnp.where(low_half(mixed.shape), mixed.astype(F32) * SCALE, 0.0).astype(BF16)
    return dot_nt(query, mixed)


def softmax_turned(scores):
    shape = scores.shape
    seen = iota(shape, 0) <= iota(shape, 1)
    scores = jnp.where(seen, scores, -jnp.inf)
    raised = jnp.exp(scores - jnp.max(scores, axis=0, keepdims=True))
    return raised * (1.0 / jnp.sum(raised, axis=0, keepdims=True))


def for_each_cluster(counts_ref, me_ref, place_ref, owners, per_group, body):
    for source in range(owners):
        place_ref[source] = 0

    def step(cluster, block):
        runs = []
        total = 0
        base = block * BLOCK_ROWS
        for source in range(owners):
            count = counts_ref[source, me_ref[3] + cluster]
            start = place_ref[source]
            runs.append((source, start, base + total))
            place_ref[source] = start + count
            total = total + count
        body(cluster, block, runs, base + total)
        return block + lax.shift_right_logical(total + (BLOCK_ROWS - 1), jnp.int32(7))

    return lax.fori_loop(0, per_group, step, jnp.int32(LEAD * UNROLL))


def gather_blocks(counts_ref, me_ref, place_ref, owners, per_group, slot_rows, wide_ref, block_ref):
    def body(cluster, block, runs, end):
        for source, start, row in runs:
            block_ref[pl.ds(row, slot_rows), :] = wide_ref[source, pl.ds(start, slot_rows), :]
        block_ref[pl.ds(end, BLOCK_ROWS), :] = jnp.zeros((BLOCK_ROWS, LANES), F32)

    blocks = for_each_cluster(counts_ref, me_ref, place_ref, owners, per_group, body)
    spare = pl.ds(pl.multiple_of(blocks * BLOCK_ROWS, BLOCK_ROWS), GROUP_ROWS)
    block_ref[spare, :] = jnp.zeros((GROUP_ROWS, LANES), F32)
    return blocks


def for_each_group(blocks, stages):
    first, second, third = stages
    groups = lax.div(blocks + (UNROLL - 1), jnp.int32(UNROLL))

    def step(i, carry):
        for slot in range(2):
            group = LEAD + 2 * i + slot
            third(group - 2, slot)
            second(group - 1, 1 - slot)
            first(group, slot)
        return carry

    lax.fori_loop(0, lax.shift_right_logical(groups + 1, jnp.int32(1)), step, 0)


def block_rows(group, ahead):
    return pl.ds(pl.multiple_of((group * UNROLL + ahead) * BLOCK_ROWS, BLOCK_ROWS), BLOCK_ROWS)


def tile_rows(ahead):
    return slice(ahead * BLOCK_ROWS, (ahead + 1) * BLOCK_ROWS)


def value_grad_kernel(sizes, per_group, slot_rows, me_ref, *refs):
    owners = sizes[0] * sizes[1]
    mixed_refs, out_refs, rest = refs[:owners], refs[owners : 2 * owners], refs[2 * owners :]
    dense_ref, counts_out_ref, counts_ref, place_ref, wide_ref, block_ref, home_ref = rest[:7]
    score_refs, probs_refs = rest[7:9], rest[9:11]
    half = out_refs[0].shape[0]
    rows = 2 * half
    for ahead, mixed_ref in zip(steps_of(sizes), mixed_refs):
        source = source_of(me_ref, ahead, sizes)
        tail = mixed_ref[rows:, :].astype(F32).astype(jnp.int32)
        counts_out_ref[pl.ds(source, 1), :] = tail[:1, :]
        wide_ref[source, :rows, :] = mixed_ref[:rows, :].astype(F32)
        wide_ref[source, rows:, :] = jnp.zeros((slot_rows, LANES), F32)
    pltpu.sync_copy(counts_out_ref, counts_ref)
    blocks = gather_blocks(counts_ref, me_ref, place_ref, owners, per_group, slot_rows, wide_ref, block_ref)

    def first(group, slot):
        for ahead in range(UNROLL):
            where = block_rows(group, ahead)
            mixed = block_ref[where, :].astype(BF16)
            dense_ref[where, :] = mixed
            score_refs[slot][tile_rows(ahead), :] = score(mixed)

    def second(group, slot):
        for ahead in range(UNROLL):
            tile = tile_rows(ahead)
            probs_refs[slot][tile, :] = softmax_turned(score_refs[slot][tile, :]).astype(BF16)

    def third(group, slot):
        for ahead in range(UNROLL):
            where = block_rows(group, ahead)
            block_ref[where, :] = dot(probs_refs[slot][tile_rows(ahead), :], dense_ref[where, :])

    for_each_group(blocks, (first, second, third))

    def scatter(cluster, block, runs, end):
        for source, start, row in runs:
            wide_ref[source, pl.ds(start, slot_rows), :] = block_ref[pl.ds(row, slot_rows), :]

    for_each_cluster(counts_ref, me_ref, place_ref, owners, per_group, scatter)
    for ahead, out_ref in zip(steps_of(sizes), out_refs):
        source = owner_of(me_ref, ahead, sizes)
        up, down = wide_ref[source, :half, :], wide_ref[source, half:rows, :]
        out_ref[...] = jnp.where(low_half((half, LANES)), swap_halves(up), down).astype(BF16)


def query_grad_kernel(sizes, per_group, slot_rows, me_ref, counts_ref, dense_ref, *refs):
    owners = sizes[0] * sizes[1]
    value_refs, out_refs, rest = refs[:owners], refs[owners : 2 * owners], refs[2 * owners :]
    place_ref, wide_ref, block_ref, sums_ref, centroid_ref = rest[:5]
    score_refs, grad_probs_refs, both_refs = rest[5:7], rest[7:9], rest[9:11]
    half = value_refs[0].shape[0]
    rows = 2 * half
    for ahead, value_ref in zip(steps_of(sizes), value_refs):
        source = source_of(me_ref, ahead, sizes)
        value = value_ref[...].astype(F32)
        wide_ref[source, :half, :] = swap_halves(value)
        wide_ref[source, half:rows, :] = value
        wide_ref[source, rows:, :] = jnp.zeros((slot_rows, LANES), F32)
    blocks = gather_blocks(counts_ref, me_ref, place_ref, owners, per_group, slot_rows, wide_ref, block_ref)

    def first(group, slot):
        for ahead in range(UNROLL):
            where, tile = block_rows(group, ahead), tile_rows(ahead)
            mixed = dense_ref[where, :]
            value = block_ref[where, :].astype(BF16)
            cotan = jnp.where(low_half(mixed.shape), jnp.zeros_like(mixed), mixed)
            score_refs[slot][tile, :] = score(mixed)
            grad_probs_refs[slot][tile, :] = dot_nt(value, cotan)

    def second(group, slot):
        for ahead in range(UNROLL):
            tile = tile_rows(ahead)
            probs = softmax_turned(score_refs[slot][tile, :])
            grad_probs = grad_probs_refs[slot][tile, :]
            probs_half = probs.astype(BF16).astype(F32)
            row_dot = jnp.sum(probs_half * grad_probs, axis=0, keepdims=True)
            grad_scores = (probs * (grad_probs - row_dot)).astype(BF16).astype(F32)
            both_refs[slot][tile, :] = (grad_scores + grad_scores.T).astype(BF16)

    def third(group, slot):
        for ahead in range(UNROLL):
            where = block_rows(group, ahead)
            grad = dot(both_refs[slot][tile_rows(ahead), :], dense_ref[where, :]) * SCALE
            grad = grad.astype(BF16).astype(F32)
            block_ref[where, :] = grad
            sums_ref[pl.ds(group * UNROLL + ahead, 1), :] = jnp.sum(grad, axis=0, keepdims=True)

    for_each_group(blocks, (first, second, third))
    most = (owners * slot_rows + BLOCK_ROWS - 1) // BLOCK_ROWS

    def scatter(cluster, block, runs, end):
        total = jnp.zeros((1, LANES), F32)
        for ahead in range(most):
            here = block + ahead
            total = total + jnp.where(here * BLOCK_ROWS < end, sums_ref[pl.ds(here, 1), :], 0.0)
        centroid_ref[pl.ds(cluster, 1), :] = total
        for source, start, row in runs:
            wide_ref[source, pl.ds(start, slot_rows), :] = block_ref[pl.ds(row, slot_rows), :]

    for_each_cluster(counts_ref, me_ref, place_ref, owners, per_group, scatter)
    extra = out_refs[0].shape[0] - half
    centroid = jnp.where(
        low_half((extra, LANES)), centroid_ref[:extra, :], swap_halves(centroid_ref[extra:, :])
    ).astype(BF16)
    for ahead, out_ref in zip(steps_of(sizes), out_refs):
        source = owner_of(me_ref, ahead, sizes)
        up, down = wide_ref[source, :half, :], wide_ref[source, half:rows, :]
        out_ref[:half, :] = jnp.where(low_half((half, LANES)), up, swap_halves(down)).astype(BF16)
        out_ref[half:, :] = centroid


def unfold(home_ref, out_ref, heads, start, half, finish):
    low = low_half((half, LANES))
    for group in range(home_ref.shape[0] // heads):
        first = group * 2 * half
        for pair in range(heads // 2):
            even = home_ref[group * heads + 2 * pair, start : start + half, :].astype(F32)
            odd = home_ref[group * heads + 2 * pair + 1, start : start + half, :].astype(F32)
            columns = slice(pair * LANES, (pair + 1) * LANES)
            out_ref[first : first + half, columns] = finish(jnp.where(low, even, swap_halves(odd)))
            out_ref[first + half : first + 2 * half, columns] = finish(
                jnp.where(low, swap_halves(even), odd)
            )


def to_half(x):
    return x.astype(BF16)


def weight_grad_kernel(sizes, heads, factor, me_ref, turned_ref, *refs):
    owners = sizes[0] * sizes[1]
    home_refs, rows_ref, sub_refs, rest = (
        refs[:owners],
        refs[owners],
        refs[owners + 1 : owners + 1 + sizes[1]],
        refs[owners + 1 + sizes[1] :],
    )
    home_ref, whole_ref = rest[-2:]
    for ahead, part_ref in zip(steps_of(sizes), home_refs):
        home_ref[source_of(me_ref, ahead, sizes)] = part_ref[...]
    slots = rows_ref.shape[0]
    half = slots * heads // owners // 2
    unfold(home_ref, rows_ref, heads, 0, half, to_half)
    if factor is not None:
        unfold(home_ref, rest[0], heads, half, home_ref.shape[1] - half, lambda x: x * factor)
    width = turned_ref.shape[0]
    step = min(512, width)

    @pl.loop(0, width // step)
    def _(i):
        where = pl.ds(pl.multiple_of(i * step, step), step)
        whole_ref[where, :] = dot(turned_ref[where, :], rows_ref[...]).astype(BF16)

    piece = width // owners
    for ahead, sub_ref in enumerate(sub_refs):
        sub = lax.rem(me_ref[1] + ahead, jnp.int32(sizes[1]))
        for seq in range(sizes[0]):
            first = pl.multiple_of((seq * sizes[1] + sub) * piece, piece)
            sub_ref[seq] = whole_ref[pl.ds(first, piece), :]


def fold_subs_kernel(me_ref, *refs):
    seqs = refs[0].shape[0]
    terms, out_refs = refs[:-seqs], refs[-seqs:]
    for ahead, out_ref in enumerate(out_refs):
        seq = lax.rem(me_ref[0] + ahead, jnp.int32(seqs))
        total = terms[0][seq].astype(F32)
        for term in terms[1:]:
            total = total + term[seq].astype(F32)
        out_ref[...] = total.astype(BF16)


def sum_kernel(*refs):
    total = refs[0][...].astype(F32)
    for ref in refs[1:-1]:
        total = total + ref[...].astype(F32)
    refs[-1][...] = total


def input_grad_kernel(sizes, heads, parts, me_ref, slot_ref, *refs):
    value_refs, weight_refs, query_refs = refs[:parts], refs[parts : 2 * parts], refs[2 * parts : -5]
    out_ref, home_ref, rows_ref, sum_ref, total_ref = refs[-5:]
    owners = sizes[0] * sizes[1]
    slots = rows_ref.shape[0]
    step = min(512, slots)
    each = (len(query_refs) - 1) // max(parts - 1, 1)
    for group in range(parts):
        if group == 0:
            source_ref = query_refs[0]
        else:
            pieces = query_refs[1 + (group - 1) * each : 1 + group * each]
            for index, ahead in enumerate(steps_of(sizes)):
                piece = pieces[index][...] if each > 1 else pieces[0][index]
                home_ref[source_of(me_ref, ahead, sizes)] = piece
            unfold(home_ref, rows_ref, heads, 0, slots * heads // owners // 2, to_half)
            source_ref = rows_ref

        @pl.loop(0, slots // step)
        def _(i):
            where = pl.ds(pl.multiple_of(i * step, step), step)
            total = dot_nt(source_ref[where, :], weight_refs[group][0])
            total = total + dot_nt(value_refs[group][where, :], weight_refs[group][1])
            total = total.astype(BF16).astype(F32)
            if group > 0:
                total = sum_ref[where, :] + total
            if group == parts - 1:
                total_ref[where, :] = total.astype(BF16)
            else:
                sum_ref[where, :] = total

    toks = out_ref.shape[0]
    step_t = min(512, toks)

    @pl.loop(0, toks // step_t)
    def _(i):
        where = pl.ds(pl.multiple_of(i * step_t, step_t), step_t)
        pick = ones_where(iota((step_t, slots), 1) == slot_ref[where, :])
        out_ref[where, :] = dot(pick, total_ref[...]).astype(BF16)


def call(kernel, outs, inputs, smem=(0,), scratch=(), flops=0, name=None):
    specs = [
        pl.BlockSpec(memory_space=pltpu.SMEM if i in smem else pltpu.VMEM) for i in range(len(inputs))
    ]
    moved = sum(x.size * x.dtype.itemsize for x in inputs) + sum(
        x.size * x.dtype.itemsize for x in jax.tree.leaves(outs)
    )
    return pl.pallas_call(
        kernel,
        out_shape=outs,
        in_specs=specs,
        out_specs=jax.tree.map(lambda _: pl.BlockSpec(memory_space=pltpu.VMEM), outs),
        scratch_shapes=list(scratch),
        compiler_params=pltpu.CompilerParams(vmem_limit_bytes=VMEM_LIMIT),
        cost_estimate=pl.CostEstimate(flops=flops, bytes_accessed=moved, transcendentals=0),
        name=name,
    )(*inputs)


def exchange(parts, sizes):
    out = []
    for ahead, part in zip(steps_of(sizes), parts):
        moves = [
            (
                seq * sizes[1] + sub,
                (seq + ahead[0]) % sizes[0] * sizes[1] + (sub + ahead[1]) % sizes[1],
            )
            for seq, sub in steps_of(sizes)
        ]
        out.append(part if ahead == (0, 0) else lax.ppermute(part, OWNERS, moves))
    return out


def shift(part, axis, ahead):
    size = lax.axis_size(axis)
    return lax.ppermute(part, axis, [(i, (i + ahead) % size) for i in range(size)])


def pass_round(parts, axis):
    return [parts[0]] + [shift(parts[ahead], axis, ahead) for ahead in range(1, len(parts))]


def reduce_weight(me, by_sub, name):
    seqs, piece, columns = by_sub[0].shape
    shape = jax.ShapeDtypeStruct
    by_seq = call(
        fold_subs_kernel,
        (shape((piece, columns), BF16),) * seqs,
        (me, *pass_round(by_sub, "sub")),
        name=name + "_subs",
    )
    return call(
        sum_kernel,
        shape((piece, columns), F32),
        tuple(pass_round(by_seq, "seq")),
        smem=(),
        name=name + "_sum",
    )


def on_device(tokens_in, w_query, w_value, cotangent, assignment):
    sizes = (lax.axis_size("seq"), lax.axis_size("sub"))
    owners = sizes[0] * sizes[1]
    parts = lax.axis_size("head")
    toks, width = tokens_in.shape
    width_dev = cotangent.shape[1]
    heads = width_dev // HD
    slot_rows = 2 * toks // CLUSTERS
    assert owners % heads == 0 and heads % 2 == 0
    groups = owners // heads
    per_group = CLUSTERS // groups
    rows = toks if groups == 1 else per_group * slot_rows
    half = rows // 2
    slots = groups * rows
    columns = width // parts
    capacity = (slot_rows * owners + BLOCK_ROWS - 1) // BLOCK_ROWS * BLOCK_ROWS
    extra = max(per_group // 2, 16)
    shape = jax.ShapeDtypeStruct
    seq, sub = lax.axis_index("seq"), lax.axis_index("sub")
    first = lax.div(seq * sizes[1] + sub, jnp.int32(heads)) * per_group
    me = jnp.stack([seq, sub, lax.axis_index("head"), first]).astype(jnp.int32)

    def several(count, *dims):
        return (shape(dims, BF16),) * count

    *send_mixed, slot_row = call(
        functools.partial(project_query_kernel, sizes, groups, rows),
        several(owners, rows + COUNT_ROWS, LANES) + (shape((1, toks), jnp.int32),),
        (me, assignment.reshape(1, toks), tokens_in, w_query, cotangent),
        scratch=[pltpu.VMEM((toks, 2 * width_dev), BF16), pltpu.VMEM((owners, rows + COUNT_ROWS, LANES), BF16)],
        flops=2 * toks * width * width_dev + 4 * slots * toks * width_dev,
        name="project_query",
    )
    got_mixed = exchange(send_mixed, sizes)
    sent = call(
        functools.partial(project_value_kernel, sizes, groups, rows, parts),
        several(owners, half, LANES) + several(parts, 2, columns, width_dev) + several(1, width, slots),
        (me, slot_row, tokens_in, w_value, w_query),
        scratch=[pltpu.VMEM((toks, width_dev), BF16), pltpu.VMEM((owners, half, LANES), BF16)],
        flops=2 * toks * width * width_dev + 2 * slots * toks * (width_dev + width),
        name="project_value",
    )
    got_value = exchange(sent[:owners], sizes)
    weights = pass_round(sent[owners:-1], "head")
    turned = sent[-1]
    blocks = per_group * capacity // BLOCK_ROWS
    held = blocks + (LEAD + 4) * UNROLL
    block_flops = 2 * BLOCK_ROWS * BLOCK_ROWS * LANES
    tall = pltpu.VMEM((owners, rows + slot_rows, LANES), F32)
    dense_rows = pltpu.VMEM((held * BLOCK_ROWS, LANES), F32)
    group_f32 = pltpu.VMEM((GROUP_ROWS, BLOCK_ROWS), F32)
    group_b16 = pltpu.VMEM((GROUP_ROWS, BLOCK_ROWS), BF16)
    place = pltpu.SMEM((owners,), jnp.int32)
    *back_value, dense, counts = call(
        functools.partial(value_grad_kernel, sizes, per_group, slot_rows),
        several(owners, half, LANES)
        + several(1, held * BLOCK_ROWS, LANES)
        + (shape((owners, LANES), jnp.int32),),
        (me, *got_mixed),
        scratch=[pltpu.SMEM((owners, LANES), jnp.int32), place, tall, dense_rows, tall]
        + [group_f32] * 2
        + [group_b16] * 2,
        flops=4 * blocks * block_flops,
        name="value_grad",
    )
    home_value = exchange(back_value, sizes)
    back_query = call(
        functools.partial(query_grad_kernel, sizes, per_group, slot_rows),
        several(owners, half + extra, LANES),
        (me, counts, dense, *got_value),
        smem=(0, 1),
        scratch=[place, tall, dense_rows, pltpu.VMEM((held, LANES), F32), pltpu.VMEM((2 * extra, LANES), F32)]
        + [group_f32] * 4
        + [group_b16] * 2,
        flops=6 * blocks * block_flops,
        name="query_grad",
    )
    home_query = exchange(back_query, sizes)
    weight_flops = 2 * slots * width * width_dev
    weight_outs = several(1, slots, width_dev) + several(sizes[1], sizes[0], width // owners, width_dev)
    value_rows, *value_weight = call(
        functools.partial(weight_grad_kernel, sizes, heads, None),
        weight_outs,
        (me, turned, *home_value),
        scratch=[pltpu.VMEM((owners, half, LANES), BF16), pltpu.VMEM((width, width_dev), BF16)],
        flops=weight_flops,
        name="value_weight",
    )
    all_value_rows = pass_round([value_rows] * parts, "head")
    grad_wv = reduce_weight(me, value_weight, "value_weight")
    if parts == 2:
        others = [shift(piece, "head", 1) for piece in home_query]
    else:
        stacked = jnp.stack(home_query)
        others = [shift(stacked, "head", ahead) for ahead in range(1, parts)]
    query_rows, *query_weight, centroid_grad = call(
        functools.partial(weight_grad_kernel, sizes, heads, (CLUSTERS / (toks * owners)) ** 0.5),
        weight_outs + (shape((groups * 2 * extra, width_dev), F32),),
        (me, turned, *home_query),
        scratch=[pltpu.VMEM((owners, half + extra, LANES), BF16), pltpu.VMEM((width, width_dev), BF16)],
        flops=weight_flops,
        name="query_weight",
    )
    grad_wq = reduce_weight(me, query_weight, "query_weight")
    grad_input = call(
        functools.partial(input_grad_kernel, sizes, heads, parts),
        shape((toks, columns), BF16),
        (me, slot_row.reshape(toks, 1), *all_value_rows, *weights, query_rows, *others),
        scratch=[
            pltpu.VMEM((owners, half + extra, LANES), BF16),
            pltpu.VMEM((slots, width_dev), BF16),
            pltpu.VMEM((slots, columns), F32),
            pltpu.VMEM((slots, columns), BF16),
        ],
        flops=2 * weight_flops + 2 * slots * toks * columns,
        name="input_grad",
    )
    if groups > 1:
        centroid_grad = centroid_grad.reshape(groups, 2 * extra, width_dev)[:, :per_group]
        centroid_grad = centroid_grad.reshape(CLUSTERS, width_dev)
    return (grad_input, grad_wq, grad_wv, centroid_grad)


def solution(mesh):
    return jax.shard_map(
        on_device,
        mesh=mesh,
        in_specs=(
            P(("grp", "seq", "sub"), None),
            P(None, "head"),
            P(None, "head"),
            P(("grp", "seq", "sub"), "head"),
            P(("grp", "seq", "sub"), None),
        ),
        out_specs=(
            P(("grp", "seq", "sub"), "head"),
            P(("grp", "seq", "sub"), "head"),
            P(("grp", "seq", "sub"), "head"),
            P("grp", "head"),
        ),
        check_vma=False,
    )
```

time: 239 us -> 241 us (level)
  Pallas kernels: 121 us -> 76.2 us
  starting transfers between devices: 31.7 us -> 74.8 us
  waiting for transfers between devices: 77.3 us -> 83.1 us
  local copies, waits for them, and re-layouts: 7.34 us -> 4.4 us
    ppermute x9 -> x46, waiting for transfers between devices: 8.3 us -> 83.1 us  [the longest x18 55.6 us: shift(): lax.ppermute(part, axis, [(i, (i + ahead) % size) for i in range(size)])]
    all_to_all x4 -> x0, waiting for transfers between devices: 69 us -> none  [exchange(): return lax.all_to_all(rows, OWNERS, split_axis=0, concat_axis=0, tiled=True)]
    ppermute x9 -> x46, starting transfers between devices: 11.7 us -> 74.8 us  [the longest x28 49.2 us: exchange(): out.append(part if ahead == (0, 0) else lax.ppermute(part, OWNERS, moves))]
    pallas_call x14 -> x11, Pallas kernels: 121 us -> 76.2 us  [call(): pl.pallas_call(kernel, out_shape=outs, in_specs=specs, out_specs=jax.tree...]
    all_to_all x4 -> x0, starting transfers between devices: 20 us -> none  [exchange(): return lax.all_to_all(rows, OWNERS, split_axis=0, concat_axis=0, tiled=True)]
    unnamed x28 -> x100, local copies, waits for them, and re-layouts: 4.94 us -> 3.37 us
  transfers between devices with their start and end apart: 13 -> 46, of which waited for: 5 -> 14; matrix products, arithmetic and copies ran while one was open for 1% -> 0% of each run, Pallas kernels for 42% -> 25%
where the time goes in v3:
time: 241 us; the launch traced here: 240 us
  waiting for transfers between devices  83.1 us (34%)
  Pallas kernels  76.2 us (32%)
  starting transfers between devices  74.8 us (31%)
  local copies, waits for them, and re-layouts  4.4 us (2%)
    pallas_call x11, Pallas kernels, call(): pl.pallas_call(kernel, out_shape=outs, in_specs=specs, out_specs=jax.tree...  76.2 us
    ppermute x18, waiting for transfers between devices, shift(): lax.ppermute(part, axis, [(i, (i + ahead) % size) for i in range(size)])  55.6 us
    ppermute x28, starting transfers between devices, exchange(): out.append(part if ahead == (0, 0) else lax.ppermute(part, OWNERS, moves))  49.2 us
    ppermute x28, waiting for transfers between devices, exchange(): out.append(part if ahead == (0, 0) else lax.ppermute(part, OWNERS, moves))  27.5 us
    ppermute x18, starting transfers between devices, shift(): lax.ppermute(part, axis, [(i, (i + ahead) % size) for i in range(size)])  25.6 us
  transfers between devices with their start and end apart: 46, of which 14 were waited for; matrix products, arithmetic and copies ran while one was open for 0% of the time, Pallas kernels for 25%

profile of v3, /device:TPU:0, one launch (start us, length us, event | category | flops | bytes accessed | tf_op | source)
XLA Modules:
  0.0 240.2 jit_solution(13283387260858252151)
XLA Ops:
  1.3 8.4 %project_query.1 = (bf16[1040,128]{1,0:T(8,128)(2,1)}, bf16[1040,128]{1,0:T(8,128)(2,1)}, bf16[1040,128]{1,0:T(8,128)(2,1)}, bf16[1040,128]{1,0:T(8,128)(2,1)}, ...) custom-call(s32[4]{0:T(128)} %pad_add_fusion.me_ref, ...), custom_call_target="tpu_custom_call" | custom-call | flops 3221225472 | bytes 6332432 | tf_op jit(solution)/shard_map/project_query/pallas_call | solution.py:473
  10.1 2.6 %collective-permute-start.1 = (bf16[1040,128]{1,0:T(8,128)(2,1)}, bf16[1040,128]{1,0:T(8,128)(2,1)S(1)}, u32[]{:S(2)}, u32[]{:S(2)}) collective-permute-start(bf16[1040,128]{1,0:T(8,128)(2,1)} %get-tuple-element.61), channel_id=1, source_target_pairs={{0,4},{1,5},{4,8},{5,9},{8,12},{9,13},{12,0},{13,1},{2,6},{3,7},{6... | collective-permute-start | bytes 798728 | tf_op jit(solution)/shard_map/ppermute | solution.py:495
  12.8 1.4 collective-permute-start.2
  14.1 1.3 collective-permute-start.3
  16.7 2.2 collective-permute-start.5
  19.0 3.5 %collective-permute-done.1.refs_2_ = bf16[1040,128]{1,0:T(8,128)(2,1)S(1)} collective-permute-done((bf16[1040,128]{1,0:T(8,128)(2,1)}, bf16[1040,128]{1,0:T(8,128)(2,1)S(1)}, u32[]{:S(2)}, u32[]{:S(2)}) %collective-permute-start.1) | collective-permute-done | bytes 266272 | tf_op jit(solution)/shard_map/ppermute | solution.py:495
  23.0 9.9 %project_value.1 = (bf16[512,128]{1,0:T(8,128)(2,1)}, bf16[512,128]{1,0:T(8,128)(2,1)}, bf16[512,128]{1,0:T(8,128)(2,1)}, bf16[512,128]{1,0:T(8,128)(2,1)}, bf16...) custom-call(s32[4]{0:T(128)} %pad_add_fusion.me_ref, ...), custom_call_target="tpu_custom_call" | custom-call | flops 4294967296 | bytes 9441296 | tf_op jit(solution)/shard_map/project_value/pallas_call | solution.py:473
  33.0 1.4 collective-permute-start.16
  34.4 10.6 %collective-permute-done.3.refs_4_ = bf16[1040,128]{1,0:T(8,128)(2,1)S(1)} collective-permute-done((bf16[1040,128]{1,0:T(8,128)(2,1)}, bf16[1040,128]{1,0:T(8,128)(2,1)S(1)}, u32[]{:S(2)}, u32[]{:S(2)}) %collective-permute-start.3) | collective-permute-done | bytes 266272 | tf_op jit(solution)/shard_map/ppermute | solution.py:495
  44.9 10.7 %collective-permute-start.17 = (bf16[512,128]{1,0:T(8,128)(2,1)}, bf16[512,128]{1,0:T(8,128)(2,1)S(1)}, u32[]{:S(2)}, u32[]{:S(2)}) collective-permute-start(bf16[512,128]{1,0:T(8,128)(2,1)} %get-tuple-element.82), channel_id=1, source_target_pairs={{0,4},{1,5},{4,8},{5,9},{8,12},{9,13},{12,0},{13,1},{2,6},{3,7},{6... | collective-permute-start | bytes 393224 | tf_op jit(solution)/shard_map/ppermute | solution.py:495
  55.6 4.6 %collective-permute-start.18 = (bf16[512,128]{1,0:T(8,128)(2,1)}, bf16[512,128]{1,0:T(8,128)(2,1)S(1)}, u32[]{:S(2)}, u32[]{:S(2)}) collective-permute-start(bf16[512,128]{1,0:T(8,128)(2,1)} %get-tuple-element.83), channel_id=1, source_target_pairs={{0,5},{1,4},{4,9},{5,8},{8,13},{9,12},{12,1},{13,0},{2,7},{3,6},{6... | collective-permute-start | bytes 393224 | tf_op jit(solution)/shard_map/ppermute | solution.py:495
  60.2 3.9 %collective-permute-start.19 = (bf16[512,128]{1,0:T(8,128)(2,1)}, bf16[512,128]{1,0:T(8,128)(2,1)S(1)}, u32[]{:S(2)}, u32[]{:S(2)}) collective-permute-start(bf16[512,128]{1,0:T(8,128)(2,1)} %get-tuple-element.84), channel_id=1, source_target_pairs={{0,8},{1,9},{4,12},{5,13},{8,0},{9,1},{12,4},{13,5},{2,10},{3,11},... | collective-permute-start | bytes 393224 | tf_op jit(solution)/shard_map/ppermute | solution.py:495
  64.8 14.4 %value_grad.1 = (bf16[512,128]{1,0:T(8,128)(2,1)}, bf16[512,128]{1,0:T(8,128)(2,1)}, bf16[512,128]{1,0:T(8,128)(2,1)}, bf16[512,128]{1,0:T(8,128)(2,1)}, bf16[51...) custom-call(s32[4]{0:T(128)} %pad_add_fusion.me_ref, ...), custom_call_target="tpu_custom_call" | custom-call | flops 2147483648 | bytes 8163344 | tf_op jit(solution)/shard_map/value_grad/pallas_call | solution.py:473
  79.2 2.8 %collective-permute-start.21 = (bf16[512,128]{1,0:T(8,128)(2,1)S(1)}, bf16[512,128]{1,0:T(8,128)(2,1)S(1)}, u32[]{:S(2)}, u32[]{:S(2)}) collective-permute-start(bf16[512,128]{1,0:T(8,128)(2,1)S(1)} %copy-done.43), channel_id=1, source_target_pairs={{0,12},{1,13},{4,0},{5,1},{8,4},{9,5},{12,8},{13,9},{2,14},{3,15},... | collective-permute-start | bytes 393224 | tf_op jit(solution)/shard_map/ppermute | solution.py:495
  82.5 1.7 collective-permute-start.8
  84.2 1.7 collective-permute-done.21.refs_6_
  87.1 1.6 collective-permute-done.22.refs_7_
  89.6 2.5 %collective-permute-start.12 = (bf16[512,128]{1,0:T(8,128)(2,1)}, bf16[512,128]{1,0:T(8,128)(2,1)S(1)}, u32[]{:S(2)}, u32[]{:S(2)}) collective-permute-start(bf16[512,128]{1,0:T(8,128)(2,1)} %get-tuple-element.73), channel_id=1, source_target_pairs={{0,12},{1,13},{4,0},{5,1},{8,4},{9,5},{12,8},{13,9},{2,14},{3,15},... | collective-permute-start | bytes 393224 | tf_op jit(solution)/shard_map/ppermute | solution.py:495
  92.2 2.0 collective-permute-start.13
  94.3 17.0 %query_grad.1 = (bf16[544,128]{1,0:T(8,128)(2,1)}, bf16[544,128]{1,0:T(8,128)(2,1)}, bf16[544,128]{1,0:T(8,128)(2,1)}, bf16[544,128]{1,0:T(8,128)(2,1)}, bf16[54...) custom-call(s32[4]{0:T(128)} %pad_add_fusion.me_ref, ...), custom_call_target="tpu_custom_call" | custom-call | flops 3221225472 | bytes 7147536 | tf_op jit(solution)/shard_map/query_grad/pallas_call | solution.py:473
  112.8 3.6 %collective-permute-start.26 = (bf16[544,128]{1,0:T(8,128)(2,1)}, bf16[544,128]{1,0:T(8,128)(2,1)S(1)}, u32[]{:S(2)}, u32[]{:S(2)}) collective-permute-start(bf16[544,128]{1,0:T(8,128)(2,1)} %get-tuple-element.92), channel_id=1, source_target_pairs={{0,8},{1,9},{4,12},{5,13},{8,0},{9,1},{12,4},{13,5},{2,10},{3,11},... | collective-permute-start | bytes 417800 | tf_op jit(solution)/shard_map/ppermute | solution.py:495
  116.8 2.1 collective-permute-start.28
  118.9 2.4 %collective-permute-done.24.refs_2_ = bf16[544,128]{1,0:T(8,128)(2,1)S(1)} collective-permute-done((bf16[544,128]{1,0:T(8,128)(2,1)}, bf16[544,128]{1,0:T(8,128)(2,1)S(1)}, u32[]{:S(2)}, u32[]{:S(2)}) %collective-permute-start.24) | collective-permute-done | bytes 139296 | tf_op jit(solution)/shard_map/ppermute | solution.py:495
  121.4 4.9 %value_weight.1 = (bf16[1024,512]{1,0:T(8,128)(2,1)}, bf16[4,128,512]{2,1,0:T(8,128)(2,1)}, bf16[4,128,512]{2,1,0:T(8,128)(2,1)}) custom-call(s32[4]{0:T(128)} %pad_add_fusion.me_ref, bf16[1024,1024]{1,0:T(8,128)(2,1)} %get-tuple-element.58.turned_ref, bf16[512,128]{1,0:T(8,128)(2,1)} %get-tuple-element.67.refs_0_, bf16[512,128]{1,0:T(8,128)(2,1)} %copy-done.35, ...), custom_call_target="tpu_custom_call" | custom-call | flops 1073741824 | bytes 5242896 | tf_op jit(solution)/shard_map/value_weight/pallas_call | solution.py:473
  126.3 5.9 %collective-permute-done.26.refs_4_ = bf16[544,128]{1,0:T(8,128)(2,1)S(1)} collective-permute-done((bf16[544,128]{1,0:T(8,128)(2,1)}, bf16[544,128]{1,0:T(8,128)(2,1)S(1)}, u32[]{:S(2)}, u32[]{:S(2)}) %collective-permute-start.26) | collective-permute-done | bytes 139296 | tf_op jit(solution)/shard_map/ppermute | solution.py:495
  132.2 1.5 collective-permute-start.15
  133.7 1.5 collective-permute-done.27.refs_5_
  135.2 1.5 collective-permute-start.14
  138.0 4.9 %query_weight.1 = (bf16[1024,512]{1,0:T(8,128)(2,1)}, bf16[4,128,512]{2,1,0:T(8,128)(2,1)}, bf16[4,128,512]{2,1,0:T(8,128)(2,1)}, f32[64,512]{1,0:T(8,128)}) custom-call(s32[4]{0:T(128)} %pad_add_fusion.me_ref, bf16[1024,1024]{1,0:T(8,128)(2,1)} %get-tuple-element.58.turned_ref, bf16[544,128]{1,0:T(8,128)(2,1)} %get-tuple-element.88.refs_0_, ...), custom_call_target="tpu_custom_call" | custom-call | flops 1073741824 | bytes 5439504 | tf_op jit(solution)/shard_map/query_weight/pallas_call | solution.py:473
  143.0 39.8 %collective-permute-done.30.refs_5_ = bf16[544,128]{1,0:T(8,128)(2,1)S(1)} collective-permute-done((bf16[544,128]{1,0:T(8,128)(2,1)S(1)}, bf16[544,128]{1,0:T(8,128)(2,1)S(1)}, u32[]{:S(2)}, u32[]{:S(2)}) %collective-permute-start.30) | collective-permute-done | bytes 139296 | tf_op jit(solution)/shard_map/ppermute | solution.py:501
  182.9 1.5 collective-permute-start.31
  184.3 3.8 %collective-permute-done.31.refs_6_ = bf16[544,128]{1,0:T(8,128)(2,1)S(1)} collective-permute-done((bf16[544,128]{1,0:T(8,128)(2,1)}, bf16[544,128]{1,0:T(8,128)(2,1)S(1)}, u32[]{:S(2)}, u32[]{:S(2)}) %collective-permute-start.31) | collective-permute-done | bytes 139296 | tf_op jit(solution)/shard_map/ppermute | solution.py:501
  188.1 1.5 collective-permute-start.32
  189.6 3.9 %collective-permute-done.32.refs_7_ = bf16[544,128]{1,0:T(8,128)(2,1)S(1)} collective-permute-done((bf16[544,128]{1,0:T(8,128)(2,1)}, bf16[544,128]{1,0:T(8,128)(2,1)S(1)}, u32[]{:S(2)}, u32[]{:S(2)}) %collective-permute-start.32) | collective-permute-done | bytes 139296 | tf_op jit(solution)/shard_map/ppermute | solution.py:501
  193.6 1.5 collective-permute-start.33
  195.9 2.1 value_weight_subs.1
  198.8 3.8 %collective-permute-start.43 = (bf16[128,512]{1,0:T(8,128)(2,1)}, bf16[128,512]{1,0:T(8,128)(2,1)S(1)}, u32[]{:S(2)}, u32[]{:S(2)}) collective-permute-start(bf16[128,512]{1,0:T(8,128)(2,1)} %get-tuple-element.106), channel_id=1, source_target_pairs={{0,4},{4,8},{8,12},{12,0},{1,5},{5,9},{9,13},{13,1},{2,6},{6,10},{... | collective-permute-start | bytes 393224 | tf_op jit(solution)/shard_map/ppermute | solution.py:501
  203.3 3.3 %collective-permute-start.44 = (bf16[128,512]{1,0:T(8,128)(2,1)}, bf16[128,512]{1,0:T(8,128)(2,1)S(1)}, u32[]{:S(2)}, u32[]{:S(2)}) collective-permute-start(bf16[128,512]{1,0:T(8,128)(2,1)} %get-tuple-element.107), channel_id=1, source_target_pairs={{0,8},{4,12},{8,0},{12,4},{1,9},{5,13},{9,1},{13,5},{2,10},{6,14},... | collective-permute-start | bytes 393224 | tf_op jit(solution)/shard_map/ppermute | solution.py:501
  207.5 2.0 query_weight_subs.1
  209.6 1.3 collective-permute-start.39
  210.9 4.9 %collective-permute-done.44.refs_2_ = bf16[128,512]{1,0:T(8,128)(2,1)S(1)} collective-permute-done((bf16[128,512]{1,0:T(8,128)(2,1)}, bf16[128,512]{1,0:T(8,128)(2,1)S(1)}, u32[]{:S(2)}, u32[]{:S(2)}) %collective-permute-start.44) | collective-permute-done | bytes 131104 | tf_op jit(solution)/shard_map/ppermute | solution.py:501
  215.9 3.8 %collective-permute-start.41 = (bf16[128,512]{1,0:T(8,128)(2,1)}, bf16[128,512]{1,0:T(8,128)(2,1)S(1)}, u32[]{:S(2)}, u32[]{:S(2)}) collective-permute-start(bf16[128,512]{1,0:T(8,128)(2,1)} %get-tuple-element.102), channel_id=1, source_target_pairs={{0,12},{4,0},{8,4},{12,8},{1,13},{5,1},{9,5},{13,9},{2,14},{6,2},{... | collective-permute-start | bytes 393224 | tf_op jit(solution)/shard_map/ppermute | solution.py:501
  219.7 1.5 collective-permute-start.35
  221.3 2.2 collective-permute-done.40.refs_2_
  223.5 1.5 collective-permute-start.36
  226.6 1.9 value_weight_sum.1
  228.5 1.9 query_weight_sum.1
  231.4 8.9 %input_grad.1 = bf16[1024,512]{1,0:T(8,128)(2,1)} custom-call(s32[4]{0:T(128)} %pad_add_fusion.me_ref, s32[1024,1]{1,0:T(8,128)} %copy.9.slot_ref, bf16[1024,512]{1,0:T(8,128)(2,1)} %get-tuple-element.75.refs_0_, bf16[1024,512]{1,0:T(8,128)(2,1)} %collective-permute-done.14.refs_1_, bf16[2,512,512]{2,1,0:T(8,128)(2,1)} %get-tuple-element.76.refs_2_, ...), custom_call_target="tpu_custom_call" | custom-call | flops 3221225472 | bytes 7409680 | tf_op jit(solution)/shard_map/input_grad/pallas_call | solution.py:473
  (157 shorter events, 15.7 us)
Async XLA Ops:
  9.7 7.0 %collective-permute-start = (bf16[1040,128]{1,0:T(8,128)(2,1)}, bf16[1040,128]{1,0:T(8,128)(2,1)S(1)}, u32[]{:S(2)}, u32[]{:S(2)}) collective-permute-start(bf16[1040,128]{1,0:T(8,128)(2,1)} %get-tuple-element.60), channel_id=1, source_target_pairs={{0,1},{1,0},{4,5},{5,4},{8,9},{9,8},{12,13},{13,12},{2,3},{3,2},{6... | collective-permute-start | bytes 798728 | tf_op jit(solution)/shard_map/ppermute | solution.py:495
  10.1 12.3 %collective-permute-start.1 = (bf16[1040,128]{1,0:T(8,128)(2,1)}, bf16[1040,128]{1,0:T(8,128)(2,1)S(1)}, u32[]{:S(2)}, u32[]{:S(2)}) collective-permute-start(bf16[1040,128]{1,0:T(8,128)(2,1)} %get-tuple-element.61), channel_id=1, source_target_pairs={{0,4},{1,5},{4,8},{5,9},{8,12},{9,13},{12,0},{13,1},{2,6},{3,7},{6... | collective-permute-start | bytes 798728 | tf_op jit(solution)/shard_map/ppermute | solution.py:495
  12.8 20.2 %collective-permute-start.2 = (bf16[1040,128]{1,0:T(8,128)(2,1)}, bf16[1040,128]{1,0:T(8,128)(2,1)S(1)}, u32[]{:S(2)}, u32[]{:S(2)}) collective-permute-start(bf16[1040,128]{1,0:T(8,128)(2,1)} %get-tuple-element.62), channel_id=1, source_target_pairs={{0,5},{1,4},{4,9},{5,8},{8,13},{9,12},{12,1},{13,0},{2,7},{3,6},{6... | collective-permute-start | bytes 798728 | tf_op jit(solution)/shard_map/ppermute | solution.py:495
  14.1 30.8 %collective-permute-start.3 = (bf16[1040,128]{1,0:T(8,128)(2,1)}, bf16[1040,128]{1,0:T(8,128)(2,1)S(1)}, u32[]{:S(2)}, u32[]{:S(2)}) collective-permute-start(bf16[1040,128]{1,0:T(8,128)(2,1)} %get-tuple-element.63), channel_id=1, source_target_pairs={{0,8},{1,9},{4,12},{5,13},{8,0},{9,1},{12,4},{13,5},{2,10},{3,11},... | collective-permute-start | bytes 798728 | tf_op jit(solution)/shard_map/ppermute | solution.py:495
  15.5 40.2 %collective-permute-start.4 = (bf16[1040,128]{1,0:T(8,128)(2,1)}, bf16[1040,128]{1,0:T(8,128)(2,1)S(1)}, u32[]{:S(2)}, u32[]{:S(2)}) collective-permute-start(bf16[1040,128]{1,0:T(8,128)(2,1)} %get-tuple-element.64), channel_id=1, source_target_pairs={{0,9},{1,8},{4,13},{5,12},{8,1},{9,0},{12,5},{13,4},{2,11},{3,10},... | collective-permute-start | bytes 798728 | tf_op jit(solution)/shard_map/ppermute | solution.py:495
  16.7 43.5 %collective-permute-start.5 = (bf16[1040,128]{1,0:T(8,128)(2,1)}, bf16[1040,128]{1,0:T(8,128)(2,1)S(1)}, u32[]{:S(2)}, u32[]{:S(2)}) collective-permute-start(bf16[1040,128]{1,0:T(8,128)(2,1)} %get-tuple-element.65), channel_id=1, source_target_pairs={{0,12},{1,13},{4,0},{5,1},{8,4},{9,5},{12,8},{13,9},{2,14},{3,15},... | collective-permute-start | bytes 798728 | tf_op jit(solution)/shard_map/ppermute | solution.py:495
  22.5 41.6 %collective-permute-start.6 = (bf16[1040,128]{1,0:T(8,128)(2,1)}, bf16[1040,128]{1,0:T(8,128)(2,1)S(1)}, u32[]{:S(2)}, u32[]{:S(2)}) collective-permute-start(bf16[1040,128]{1,0:T(8,128)(2,1)} %get-tuple-element.66), channel_id=1, source_target_pairs={{0,13},{1,12},{4,1},{5,0},{8,5},{9,4},{12,9},{13,8},{2,15},{3,14},... | collective-permute-start | bytes 798728 | tf_op jit(solution)/shard_map/ppermute | solution.py:495
  33.0 46.2 %collective-permute-start.16 = (bf16[512,128]{1,0:T(8,128)(2,1)}, bf16[512,128]{1,0:T(8,128)(2,1)S(1)}, u32[]{:S(2)}, u32[]{:S(2)}) collective-permute-start(bf16[512,128]{1,0:T(8,128)(2,1)} %get-tuple-element.81), channel_id=1, source_target_pairs={{0,1},{1,0},{4,5},{5,4},{8,9},{9,8},{12,13},{13,12},{2,3},{3,2},{6... | collective-permute-start | bytes 393224 | tf_op jit(solution)/shard_map/ppermute | solution.py:495
  44.9 37.1 %collective-permute-start.17 = (bf16[512,128]{1,0:T(8,128)(2,1)}, bf16[512,128]{1,0:T(8,128)(2,1)S(1)}, u32[]{:S(2)}, u32[]{:S(2)}) collective-permute-start(bf16[512,128]{1,0:T(8,128)(2,1)} %get-tuple-element.82), channel_id=1, source_target_pairs={{0,4},{1,5},{4,8},{5,9},{8,12},{9,13},{12,0},{13,1},{2,6},{3,7},{6... | collective-permute-start | bytes 393224 | tf_op jit(solution)/shard_map/ppermute | solution.py:495
  55.6 26.9 %collective-permute-start.18 = (bf16[512,128]{1,0:T(8,128)(2,1)}, bf16[512,128]{1,0:T(8,128)(2,1)S(1)}, u32[]{:S(2)}, u32[]{:S(2)}) collective-permute-start(bf16[512,128]{1,0:T(8,128)(2,1)} %get-tuple-element.83), channel_id=1, source_target_pairs={{0,5},{1,4},{4,9},{5,8},{8,13},{9,12},{12,1},{13,0},{2,7},{3,6},{6... | collective-permute-start | bytes 393224 | tf_op jit(solution)/shard_map/ppermute | solution.py:495
  60.2 22.3 %collective-permute-start.19 = (bf16[512,128]{1,0:T(8,128)(2,1)}, bf16[512,128]{1,0:T(8,128)(2,1)S(1)}, u32[]{:S(2)}, u32[]{:S(2)}) collective-permute-start(bf16[512,128]{1,0:T(8,128)(2,1)} %get-tuple-element.84), channel_id=1, source_target_pairs={{0,8},{1,9},{4,12},{5,13},{8,0},{9,1},{12,4},{13,5},{2,10},{3,11},... | collective-permute-start | bytes 393224 | tf_op jit(solution)/shard_map/ppermute | solution.py:495
  64.1 20.1 %collective-permute-start.20 = (bf16[512,128]{1,0:T(8,128)(2,1)}, bf16[512,128]{1,0:T(8,128)(2,1)S(1)}, u32[]{:S(2)}, u32[]{:S(2)}) collective-permute-start(bf16[512,128]{1,0:T(8,128)(2,1)} %get-tuple-element.85), channel_id=1, source_target_pairs={{0,9},{1,8},{4,13},{5,12},{8,1},{9,0},{12,5},{13,4},{2,11},{3,10},... | collective-permute-start | bytes 393224 | tf_op jit(solution)/shard_map/ppermute | solution.py:495
  79.2 6.7 %collective-permute-start.21 = (bf16[512,128]{1,0:T(8,128)(2,1)S(1)}, bf16[512,128]{1,0:T(8,128)(2,1)S(1)}, u32[]{:S(2)}, u32[]{:S(2)}) collective-permute-start(bf16[512,128]{1,0:T(8,128)(2,1)S(1)} %copy-done.43), channel_id=1, source_target_pairs={{0,12},{1,13},{4,0},{5,1},{8,4},{9,5},{12,8},{13,9},{2,14},{3,15},... | collective-permute-start | bytes 393224 | tf_op jit(solution)/shard_map/ppermute | solution.py:495
  82.0 6.7 %collective-permute-start.22 = (bf16[512,128]{1,0:T(8,128)(2,1)S(1)}, bf16[512,128]{1,0:T(8,128)(2,1)S(1)}, u32[]{:S(2)}, u32[]{:S(2)}) collective-permute-start(bf16[512,128]{1,0:T(8,128)(2,1)S(1)} %copy-done.40), channel_id=1, source_target_pairs={{0,13},{1,12},{4,1},{5,0},{8,5},{9,4},{12,9},{13,8},{2,15},{3,14},... | collective-permute-start | bytes 393224 | tf_op jit(solution)/shard_map/ppermute | solution.py:495
  82.5 7.1 %collective-permute-start.7 = (bf16[512,128]{1,0:T(8,128)(2,1)}, bf16[512,128]{1,0:T(8,128)(2,1)S(1)}, u32[]{:S(2)}, u32[]{:S(2)}) collective-permute-start(bf16[512,128]{1,0:T(8,128)(2,1)} %get-tuple-element.68), channel_id=1, source_target_pairs={{0,1},{1,0},{4,5},{5,4},{8,9},{9,8},{12,13},{13,12},{2,3},{3,2},{6... | collective-permute-start | bytes 393224 | tf_op jit(solution)/shard_map/ppermute | solution.py:495
  82.5 9.7 %collective-permute-start.8 = (bf16[512,128]{1,0:T(8,128)(2,1)}, bf16[512,128]{1,0:T(8,128)(2,1)S(1)}, u32[]{:S(2)}, u32[]{:S(2)}) collective-permute-start(bf16[512,128]{1,0:T(8,128)(2,1)} %get-tuple-element.69), channel_id=1, source_target_pairs={{0,4},{1,5},{4,8},{5,9},{8,12},{9,13},{12,0},{13,1},{2,6},{3,7},{6... | collective-permute-start | bytes 393224 | tf_op jit(solution)/shard_map/ppermute | solution.py:495
  84.2 27.2 %collective-permute-start.9 = (bf16[512,128]{1,0:T(8,128)(2,1)}, bf16[512,128]{1,0:T(8,128)(2,1)S(1)}, u32[]{:S(2)}, u32[]{:S(2)}) collective-permute-start(bf16[512,128]{1,0:T(8,128)(2,1)} %get-tuple-element.70), channel_id=1, source_target_pairs={{0,5},{1,4},{4,9},{5,8},{8,13},{9,12},{12,1},{13,0},{2,7},{3,6},{6... | collective-permute-start | bytes 393224 | tf_op jit(solution)/shard_map/ppermute | solution.py:495
  85.9 26.6 %collective-permute-start.10 = (bf16[512,128]{1,0:T(8,128)(2,1)}, bf16[512,128]{1,0:T(8,128)(2,1)S(1)}, u32[]{:S(2)}, u32[]{:S(2)}) collective-permute-start(bf16[512,128]{1,0:T(8,128)(2,1)} %get-tuple-element.71), channel_id=1, source_target_pairs={{0,8},{1,9},{4,12},{5,13},{8,0},{9,1},{12,4},{13,5},{2,10},{3,11},... | collective-permute-start | bytes 393224 | tf_op jit(solution)/shard_map/ppermute | solution.py:495
  88.7 23.8 %collective-permute-start.11 = (bf16[512,128]{1,0:T(8,128)(2,1)}, bf16[512,128]{1,0:T(8,128)(2,1)S(1)}, u32[]{:S(2)}, u32[]{:S(2)}) collective-permute-start(bf16[512,128]{1,0:T(8,128)(2,1)} %get-tuple-element.72), channel_id=1, source_target_pairs={{0,9},{1,8},{4,13},{5,12},{8,1},{9,0},{12,5},{13,4},{2,11},{3,10},... | collective-permute-start | bytes 393224 | tf_op jit(solution)/shard_map/ppermute | solution.py:495
  89.6 23.2 %collective-permute-start.12 = (bf16[512,128]{1,0:T(8,128)(2,1)}, bf16[512,128]{1,0:T(8,128)(2,1)S(1)}, u32[]{:S(2)}, u32[]{:S(2)}) collective-permute-start(bf16[512,128]{1,0:T(8,128)(2,1)} %get-tuple-element.73), channel_id=1, source_target_pairs={{0,12},{1,13},{4,0},{5,1},{8,4},{9,5},{12,8},{13,9},{2,14},{3,15},... | collective-permute-start | bytes 393224 | tf_op jit(solution)/shard_map/ppermute | solution.py:495
  92.2 24.1 %collective-permute-start.13 = (bf16[512,128]{1,0:T(8,128)(2,1)}, bf16[512,128]{1,0:T(8,128)(2,1)S(1)}, u32[]{:S(2)}, u32[]{:S(2)}) collective-permute-start(bf16[512,128]{1,0:T(8,128)(2,1)} %get-tuple-element.74), channel_id=1, source_target_pairs={{0,13},{1,12},{4,1},{5,0},{8,5},{9,4},{12,9},{13,8},{2,15},{3,14},... | collective-permute-start | bytes 393224 | tf_op jit(solution)/shard_map/ppermute | solution.py:495
  111.4 5.4 %collective-permute-start.23 = (bf16[544,128]{1,0:T(8,128)(2,1)}, bf16[544,128]{1,0:T(8,128)(2,1)S(1)}, u32[]{:S(2)}, u32[]{:S(2)}) collective-permute-start(bf16[544,128]{1,0:T(8,128)(2,1)} %get-tuple-element.89), channel_id=1, source_target_pairs={{0,1},{1,0},{4,5},{5,4},{8,9},{9,8},{12,13},{13,12},{2,3},{3,2},{6... | collective-permute-start | bytes 417800 | tf_op jit(solution)/shard_map/ppermute | solution.py:495
  112.6 8.7 %collective-permute-start.24 = (bf16[544,128]{1,0:T(8,128)(2,1)}, bf16[544,128]{1,0:T(8,128)(2,1)S(1)}, u32[]{:S(2)}, u32[]{:S(2)}) collective-permute-start(bf16[544,128]{1,0:T(8,128)(2,1)} %get-tuple-element.90), channel_id=1, source_target_pairs={{0,4},{1,5},{4,8},{5,9},{8,12},{9,13},{12,0},{13,1},{2,6},{3,7},{6... | collective-permute-start | bytes 417800 | tf_op jit(solution)/shard_map/ppermute | solution.py:495
  112.6 13.6 %collective-permute-start.25 = (bf16[544,128]{1,0:T(8,128)(2,1)}, bf16[544,128]{1,0:T(8,128)(2,1)S(1)}, u32[]{:S(2)}, u32[]{:S(2)}) collective-permute-start(bf16[544,128]{1,0:T(8,128)(2,1)} %get-tuple-element.91), channel_id=1, source_target_pairs={{0,5},{1,4},{4,9},{5,8},{8,13},{9,12},{12,1},{13,0},{2,7},{3,6},{6... | collective-permute-start | bytes 417800 | tf_op jit(solution)/shard_map/ppermute | solution.py:495
  112.8 19.4 %collective-permute-start.26 = (bf16[544,128]{1,0:T(8,128)(2,1)}, bf16[544,128]{1,0:T(8,128)(2,1)S(1)}, u32[]{:S(2)}, u32[]{:S(2)}) collective-permute-start(bf16[544,128]{1,0:T(8,128)(2,1)} %get-tuple-element.92), channel_id=1, source_target_pairs={{0,8},{1,9},{4,12},{5,13},{8,0},{9,1},{12,4},{13,5},{2,10},{3,11},... | collective-permute-start | bytes 417800 | tf_op jit(solution)/shard_map/ppermute | solution.py:495
  116.4 18.8 %collective-permute-start.27 = (bf16[544,128]{1,0:T(8,128)(2,1)}, bf16[544,128]{1,0:T(8,128)(2,1)S(1)}, u32[]{:S(2)}, u32[]{:S(2)}) collective-permute-start(bf16[544,128]{1,0:T(8,128)(2,1)} %get-tuple-element.93), channel_id=1, source_target_pairs={{0,9},{1,8},{4,13},{5,12},{8,1},{9,0},{12,5},{13,4},{2,11},{3,10},... | collective-permute-start | bytes 417800 | tf_op jit(solution)/shard_map/ppermute | solution.py:495
  116.8 19.9 %collective-permute-start.28 = (bf16[544,128]{1,0:T(8,128)(2,1)}, bf16[544,128]{1,0:T(8,128)(2,1)S(1)}, u32[]{:S(2)}, u32[]{:S(2)}) collective-permute-start(bf16[544,128]{1,0:T(8,128)(2,1)} %get-tuple-element.94), channel_id=1, source_target_pairs={{0,12},{1,13},{4,0},{5,1},{8,4},{9,5},{12,8},{13,9},{2,14},{3,15},... | collective-permute-start | bytes 417800 | tf_op jit(solution)/shard_map/ppermute | solution.py:495
  121.3 16.0 %collective-permute-start.29 = (bf16[544,128]{1,0:T(8,128)(2,1)}, bf16[544,128]{1,0:T(8,128)(2,1)S(1)}, u32[]{:S(2)}, u32[]{:S(2)}) collective-permute-start(bf16[544,128]{1,0:T(8,128)(2,1)} %get-tuple-element.95), channel_id=1, source_target_pairs={{0,13},{1,12},{4,1},{5,0},{8,5},{9,4},{12,9},{13,8},{2,15},{3,14},... | collective-permute-start | bytes 417800 | tf_op jit(solution)/shard_map/ppermute | solution.py:495
  126.2 68.8 %collective-permute-start.42 = (bf16[4,128,512]{2,1,0:T(8,128)(2,1)}, bf16[4,128,512]{2,1,0:T(8,128)(2,1)S(1)}, u32[]{:S(2)}, u32[]{:S(2)}) collective-permute-start(bf16[4,128,512]{2,1,0:T(8,128)(2,1)} %get-tuple-element.104), channel_id=1, source_target_pairs={{0,1},{1,0},{2,3},{3,2},{4,5},{5,4},{6,7},{7,6},{8,9},{9,8},{10,11... | collective-permute-start | bytes 1572872 | tf_op jit(solution)/shard_map/ppermute | solution.py:501
  132.2 98.1 %collective-permute-start.15 = (bf16[2,512,512]{2,1,0:T(8,128)(2,1)S(1)}, bf16[2,512,512]{2,1,0:T(8,128)(2,1)S(1)}, u32[]{:S(2)}, u32[]{:S(2)}) collective-permute-start(bf16[2,512,512]{2,1,0:T(8,128)(2,1)S(1)} %copy-done.9), channel_id=1, source_target_pairs={{0,2},{2,0},{1,3},{3,1},{4,6},{6,4},{5,7},{7,5},{8,10},{10,8},{9,1... | collective-permute-start | bytes 3145736 | tf_op jit(solution)/shard_map/ppermute | solution.py:501
  135.2 95.2 %collective-permute-start.14 = (bf16[1024,512]{1,0:T(8,128)(2,1)}, bf16[1024,512]{1,0:T(8,128)(2,1)}, u32[]{:S(2)}, u32[]{:S(2)}) collective-permute-start(bf16[1024,512]{1,0:T(8,128)(2,1)} %get-tuple-element.75.refs_0_), channel_id=1, source_target_pairs={{0,2},{2,0},{1,3},{3,1},{4,6},{6,4},{5,7},{7,5},{8,10},{10,8},{9,1... | collective-permute-start | bytes 3145736 | tf_op jit(solution)/shard_map/ppermute | solution.py:501
  136.7 88.9 %copy-start.8 = (s32[1,1024]{1,0:T(1,128)S(1)}, s32[1,1024]{1,0:T(1,128)}, u32[]{:S(2)}) copy-start(s32[1,1024]{1,0:T(1,128)} %get-tuple-element.57.slot_ref) | copy-start | bytes 12292
  136.7 46.1 %collective-permute-start.30 = (bf16[544,128]{1,0:T(8,128)(2,1)S(1)}, bf16[544,128]{1,0:T(8,128)(2,1)S(1)}, u32[]{:S(2)}, u32[]{:S(2)}) collective-permute-start(bf16[544,128]{1,0:T(8,128)(2,1)S(1)} %copy-done.31), channel_id=1, source_target_pairs={{0,2},{2,0},{1,3},{3,1},{4,6},{6,4},{5,7},{7,5},{8,10},{10,8},{9,1... | collective-permute-start | bytes 417800 | tf_op jit(solution)/shard_map/ppermute | solution.py:501
  142.9 82.0 %copy-start.23 = (bf16[544,128]{1,0:T(8,128)(2,1)S(1)}, bf16[544,128]{1,0:T(8,128)(2,1)}, u32[]{:S(2)}) copy-start(bf16[544,128]{1,0:T(8,128)(2,1)} %copy-done.22) | copy-start | bytes 417796
  142.9 63.6 %collective-permute-start.38 = (bf16[4,128,512]{2,1,0:T(8,128)(2,1)}, bf16[4,128,512]{2,1,0:T(8,128)(2,1)S(1)}, u32[]{:S(2)}, u32[]{:S(2)}) collective-permute-start(bf16[4,128,512]{2,1,0:T(8,128)(2,1)} %get-tuple-element.98), channel_id=1, source_target_pairs={{0,1},{1,0},{2,3},{3,2},{4,5},{5,4},{6,7},{7,6},{8,9},{9,8},{10,11... | collective-permute-start | bytes 1572872 | tf_op jit(solution)/shard_map/ppermute | solution.py:501
  182.9 5.3 %collective-permute-start.31 = (bf16[544,128]{1,0:T(8,128)(2,1)}, bf16[544,128]{1,0:T(8,128)(2,1)S(1)}, u32[]{:S(2)}, u32[]{:S(2)}) collective-permute-start(bf16[544,128]{1,0:T(8,128)(2,1)} %copy-done.32), channel_id=1, source_target_pairs={{0,2},{2,0},{1,3},{3,1},{4,6},{6,4},{5,7},{7,5},{8,10},{10,8},{9,1... | collective-permute-start | bytes 417800 | tf_op jit(solution)/shard_map/ppermute | solution.py:501
  188.1 5.4 %collective-permute-start.32 = (bf16[544,128]{1,0:T(8,128)(2,1)}, bf16[544,128]{1,0:T(8,128)(2,1)S(1)}, u32[]{:S(2)}, u32[]{:S(2)}) collective-permute-start(bf16[544,128]{1,0:T(8,128)(2,1)} %copy-done.33), channel_id=1, source_target_pairs={{0,2},{2,0},{1,3},{3,1},{4,6},{6,4},{5,7},{7,5},{8,10},{10,8},{9,1... | collective-permute-start | bytes 417800 | tf_op jit(solution)/shard_map/ppermute | solution.py:501
  193.6 5.3 %collective-permute-start.33 = (bf16[544,128]{1,0:T(8,128)(2,1)}, bf16[544,128]{1,0:T(8,128)(2,1)S(1)}, u32[]{:S(2)}, u32[]{:S(2)}) collective-permute-start(bf16[544,128]{1,0:T(8,128)(2,1)} %copy-done.28), channel_id=1, source_target_pairs={{0,2},{2,0},{1,3},{3,1},{4,6},{6,4},{5,7},{7,5},{8,10},{10,8},{9,1... | collective-permute-start | bytes 417800 | tf_op jit(solution)/shard_map/ppermute | solution.py:501
  195.1 7.6 %collective-permute-start.34 = (bf16[544,128]{1,0:T(8,128)(2,1)}, bf16[544,128]{1,0:T(8,128)(2,1)S(1)}, u32[]{:S(2)}, u32[]{:S(2)}) collective-permute-start(bf16[544,128]{1,0:T(8,128)(2,1)} %copy-done.29), channel_id=1, source_target_pairs={{0,2},{2,0},{1,3},{3,1},{4,6},{6,4},{5,7},{7,5},{8,10},{10,8},{9,1... | collective-permute-start | bytes 417800 | tf_op jit(solution)/shard_map/ppermute | solution.py:501
  198.8 10.8 %collective-permute-start.43 = (bf16[128,512]{1,0:T(8,128)(2,1)}, bf16[128,512]{1,0:T(8,128)(2,1)S(1)}, u32[]{:S(2)}, u32[]{:S(2)}) collective-permute-start(bf16[128,512]{1,0:T(8,128)(2,1)} %get-tuple-element.106), channel_id=1, source_target_pairs={{0,4},{4,8},{8,12},{12,0},{1,5},{5,9},{9,13},{13,1},{2,6},{6,10},{... | collective-permute-start | bytes 393224 | tf_op jit(solution)/shard_map/ppermute | solution.py:501
  203.3 12.6 %collective-permute-start.44 = (bf16[128,512]{1,0:T(8,128)(2,1)}, bf16[128,512]{1,0:T(8,128)(2,1)S(1)}, u32[]{:S(2)}, u32[]{:S(2)}) collective-permute-start(bf16[128,512]{1,0:T(8,128)(2,1)} %get-tuple-element.107), channel_id=1, source_target_pairs={{0,8},{4,12},{8,0},{12,4},{1,9},{5,13},{9,1},{13,5},{2,10},{6,14},... | collective-permute-start | bytes 393224 | tf_op jit(solution)/shard_map/ppermute | solution.py:501
  206.6 9.3 %collective-permute-start.45 = (bf16[128,512]{1,0:T(8,128)(2,1)}, bf16[128,512]{1,0:T(8,128)(2,1)S(1)}, u32[]{:S(2)}, u32[]{:S(2)}) collective-permute-start(bf16[128,512]{1,0:T(8,128)(2,1)} %get-tuple-element.108), channel_id=1, source_target_pairs={{0,12},{4,0},{8,4},{12,8},{1,13},{5,1},{9,5},{13,9},{2,14},{6,2},{... | collective-permute-start | bytes 393224 | tf_op jit(solution)/shard_map/ppermute | solution.py:501
  209.6 10.1 %collective-permute-start.39 = (bf16[128,512]{1,0:T(8,128)(2,1)}, bf16[128,512]{1,0:T(8,128)(2,1)S(1)}, u32[]{:S(2)}, u32[]{:S(2)}) collective-permute-start(bf16[128,512]{1,0:T(8,128)(2,1)} %get-tuple-element.100), channel_id=1, source_target_pairs={{0,4},{4,8},{8,12},{12,0},{1,5},{5,9},{9,13},{13,1},{2,6},{6,10},{... | collective-permute-start | bytes 393224 | tf_op jit(solution)/shard_map/ppermute | solution.py:501
  215.9 7.6 %collective-permute-start.40 = (bf16[128,512]{1,0:T(8,128)(2,1)}, bf16[128,512]{1,0:T(8,128)(2,1)S(1)}, u32[]{:S(2)}, u32[]{:S(2)}) collective-permute-start(bf16[128,512]{1,0:T(8,128)(2,1)} %get-tuple-element.101), channel_id=1, source_target_pairs={{0,8},{4,12},{8,0},{12,4},{1,9},{5,13},{9,1},{13,5},{2,10},{6,14},... | collective-permute-start | bytes 393224 | tf_op jit(solution)/shard_map/ppermute | solution.py:501
  215.9 9.1 %collective-permute-start.41 = (bf16[128,512]{1,0:T(8,128)(2,1)}, bf16[128,512]{1,0:T(8,128)(2,1)S(1)}, u32[]{:S(2)}, u32[]{:S(2)}) collective-permute-start(bf16[128,512]{1,0:T(8,128)(2,1)} %get-tuple-element.102), channel_id=1, source_target_pairs={{0,12},{4,0},{8,4},{12,8},{1,13},{5,1},{9,5},{13,9},{2,14},{6,2},{... | collective-permute-start | bytes 393224 | tf_op jit(solution)/shard_map/ppermute | solution.py:501
  219.7 10.6 %collective-permute-start.35 = (bf16[544,128]{1,0:T(8,128)(2,1)S(1)}, bf16[544,128]{1,0:T(8,128)(2,1)}, u32[]{:S(2)}, u32[]{:S(2)}) collective-permute-start(bf16[544,128]{1,0:T(8,128)(2,1)S(1)} %copy-done.19), channel_id=1, source_target_pairs={{0,2},{2,0},{1,3},{3,1},{4,6},{6,4},{5,7},{7,5},{8,10},{10,8},{9,1... | collective-permute-start | bytes 417800 | tf_op jit(solution)/shard_map/ppermute | solution.py:501
  223.5 6.9 %collective-permute-start.36 = (bf16[544,128]{1,0:T(8,128)(2,1)S(1)}, bf16[544,128]{1,0:T(8,128)(2,1)}, u32[]{:S(2)}, u32[]{:S(2)}) collective-permute-start(bf16[544,128]{1,0:T(8,128)(2,1)S(1)} %copy-done.21), channel_id=1, source_target_pairs={{0,2},{2,0},{1,3},{3,1},{4,6},{6,4},{5,7},{7,5},{8,10},{10,8},{9,1... | collective-permute-start | bytes 417800 | tf_op jit(solution)/shard_map/ppermute | solution.py:501
  225.0 5.4 %collective-permute-start.37 = (bf16[544,128]{1,0:T(8,128)(2,1)S(1)}, bf16[544,128]{1,0:T(8,128)(2,1)}, u32[]{:S(2)}, u32[]{:S(2)}) collective-permute-start(bf16[544,128]{1,0:T(8,128)(2,1)S(1)} %copy-done.23), channel_id=1, source_target_pairs={{0,2},{2,0},{1,3},{3,1},{4,6},{6,4},{5,7},{7,5},{8,10},{10,8},{9,1... | collective-permute-start | bytes 417800 | tf_op jit(solution)/shard_map/ppermute | solution.py:501
  (48 other events, 741.2 us)

commit v4 on v3

--- a/solution.py
+++ b/solution.py
@@ -16,7 +16,6 @@
 SCALE = 0.5 * HD ** (-0.5)
 F32 = jnp.float32
 BF16 = jnp.bfloat16
-VMEM_LIMIT = 56 * 1024 * 1024
 OWNERS = ("seq", "sub")
 GROUP_ROWS = UNROLL * BLOCK_ROWS
 LEAD = 2
@@ -121,23 +120,16 @@
     hand_out(sorted_ref, out_refs, me_ref, sizes)
 
 
-def project_value_kernel(
-    sizes, groups, rows, parts, me_ref, slot_ref, tokens_ref, w_value_ref, w_query_ref, *rest
-):
-    owners = sizes[0] * sizes[1]
-    out_refs, weight_refs, (turned_ref, value_ref, sorted_ref) = (
-        rest[:owners],
-        rest[owners : owners + parts],
-        rest[owners + parts :],
-    )
+def project_value_kernel(sizes, groups, rows, me_ref, slot_ref, tokens_ref, weight_ref, *rest):
+    out_refs, (turned_ref, unsort_ref, value_ref, sorted_ref) = rest[:-4], rest[-4:]
     toks = tokens_ref.shape[0]
-    heads = w_value_ref.shape[1] // HD
+    heads = weight_ref.shape[1] // HD
     step = min(512, toks)
 
     @pl.loop(0, toks // step)
     def _(i):
         where = pl.ds(pl.multiple_of(i * step, step), step)
-        value_ref[where, :] = dot(tokens_ref[where, :], w_value_ref[...]).astype(BF16)
+        value_ref[where, :] = dot(tokens_ref[where, :], weight_ref[...]).astype(BF16)
 
     half = rows // 2
     part = min(256, half)
@@ -160,18 +152,12 @@
             sorted_ref[group * heads + 2 * pair + 1, pl.ds(first, part), :] = odd
 
     hand_out(sorted_ref, out_refs, me_ref, sizes)
-    columns = w_query_ref.shape[0] // parts
-    for ahead, weight_out_ref in enumerate(weight_refs):
-        dest = lax.rem(me_ref[2] + ahead, jnp.int32(parts))
-        mine = pl.ds(pl.multiple_of(dest * columns, columns), columns)
-        weight_out_ref[0] = w_query_ref[mine, :]
-        weight_out_ref[1] = w_value_ref[mine, :]
-    turned = tokens_ref[...].T
-    slots = turned_ref.shape[1]
+    turned_ref[...] = tokens_ref[...].T
+    slots = unsort_ref.shape[1]
     part = min(256, slots)
     for i in range(slots // part):
         pick = ones_where(iota((part, toks), 0) + i * part == slot_ref[...])
-        turned_ref[:, i * part : (i + 1) * part] = dot_nt(turned, pick).astype(BF16)
+        unsort_ref[:, i * part : (i + 1) * part] = pick.T
 
 
 def score(mixed):
@@ -372,22 +358,21 @@
     return x.astype(BF16)
 
 
-def weight_grad_kernel(sizes, heads, factor, me_ref, turned_ref, *refs):
-    owners = sizes[0] * sizes[1]
-    home_refs, rows_ref, sub_refs, rest = (
-        refs[:owners],
-        refs[owners],
-        refs[owners + 1 : owners + 1 + sizes[1]],
-        refs[owners + 1 + sizes[1] :],
-    )
-    home_ref, whole_ref = rest[-2:]
-    for ahead, part_ref in zip(steps_of(sizes), home_refs):
+def bring_home(sizes, heads, me_ref, part_refs, unsort_ref, home_ref, sorted_ref, rows_ref):
+    for ahead, part_ref in zip(steps_of(sizes), part_refs):
         home_ref[source_of(me_ref, ahead, sizes)] = part_ref[...]
-    slots = rows_ref.shape[0]
-    half = slots * heads // owners // 2
-    unfold(home_ref, rows_ref, heads, 0, half, to_half)
-    if factor is not None:
-        unfold(home_ref, rest[0], heads, half, home_ref.shape[1] - half, lambda x: x * factor)
+    half = sorted_ref.shape[0] * heads // (sizes[0] * sizes[1]) // 2
+    unfold(home_ref, sorted_ref, heads, 0, half, to_half)
+    toks = rows_ref.shape[0]
+    step = min(512, toks)
+
+    @pl.loop(0, toks // step)
+    def _(i):
+        where = pl.ds(pl.multiple_of(i * step, step), step)
+        rows_ref[where, :] = dot(unsort_ref[where, :], sorted_ref[...]).astype(BF16)
+
+
+def weight_partial(sizes, me_ref, turned_ref, rows_ref, whole_ref, sub_refs):
     width = turned_ref.shape[0]
     step = min(512, width)
 
@@ -396,12 +381,49 @@
         where = pl.ds(pl.multiple_of(i * step, step), step)
         whole_ref[where, :] = dot(turned_ref[where, :], rows_ref[...]).astype(BF16)
 
-    piece = width // owners
+    piece = width // (sizes[0] * sizes[1])
     for ahead, sub_ref in enumerate(sub_refs):
         sub = lax.rem(me_ref[1] + ahead, jnp.int32(sizes[1]))
         for seq in range(sizes[0]):
             first = pl.multiple_of((seq * sizes[1] + sub) * piece, piece)
             sub_ref[seq] = whole_ref[pl.ds(first, piece), :]
+
+
+def value_home_kernel(sizes, heads, me_ref, turned_ref, unsort_ref, *refs):
+    part_refs, rows_ref, sub_refs = refs[: -4 - sizes[1]], refs[-4 - sizes[1]], refs[-3 - sizes[1] : -3]
+    home_ref, sorted_ref, whole_ref = refs[-3:]
+    bring_home(sizes, heads, me_ref, part_refs, unsort_ref, home_ref, sorted_ref, rows_ref)
+    weight_partial(sizes, me_ref, turned_ref, rows_ref, whole_ref, sub_refs)
+
+
+def query_home_kernel(
+    sizes, heads, factor, parts, me_ref, unsort_ref, value_rows_ref, w_query_ref, w_value_ref, *refs
+):
+    part_refs, out_refs, (rows_ref, centroid_ref, home_ref, sorted_ref) = (
+        refs[: -4 - parts],
+        refs[-4 - parts : -4],
+        refs[-4:],
+    )
+    bring_home(sizes, heads, me_ref, part_refs, unsort_ref, home_ref, sorted_ref, rows_ref)
+    half = sorted_ref.shape[0] * heads // (sizes[0] * sizes[1]) // 2
+    unfold(home_ref, centroid_ref, heads, half, home_ref.shape[1] - half, lambda x: x * factor)
+    toks = rows_ref.shape[0]
+    columns = w_query_ref.shape[0] // parts
+    step = min(512, toks)
+    for ahead, out_ref in enumerate(out_refs):
+        dest = lax.rem(me_ref[2] + ahead, jnp.int32(parts))
+        mine = pl.ds(pl.multiple_of(dest * columns, columns), columns)
+
+        @pl.loop(0, toks // step)
+        def _(i):
+            where = pl.ds(pl.multiple_of(i * step, step), step)
+            total = dot_nt(rows_ref[where, :], w_query_ref[mine, :])
+            total = total + dot_nt(value_rows_ref[where, :], w_value_ref[mine, :])
+            out_ref[where, :] = total.astype(BF16)
+
+
+def query_weight_kernel(sizes, me_ref, turned_ref, rows_ref, *refs):
+    weight_partial(sizes, me_ref, turned_ref, rows_ref, refs[-1], refs[:-1])
 
 
 def fold_subs_kernel(me_ref, *refs):
@@ -419,51 +441,10 @@
     total = refs[0][...].astype(F32)
     for ref in refs[1:-1]:
         total = total + ref[...].astype(F32)
-    refs[-1][...] = total
-
-
-def input_grad_kernel(sizes, heads, parts, me_ref, slot_ref, *refs):
-    value_refs, weight_refs, query_refs = refs[:parts], refs[parts : 2 * parts], refs[2 * parts : -5]
-    out_ref, home_ref, rows_ref, sum_ref, total_ref = refs[-5:]
-    owners = sizes[0] * sizes[1]
-    slots = rows_ref.shape[0]
-    step = min(512, slots)
-    each = (len(query_refs) - 1) // max(parts - 1, 1)
-    for group in range(parts):
-        if group == 0:
-            source_ref = query_refs[0]
-        else:
-            pieces = query_refs[1 + (group - 1) * each : 1 + group * each]
-            for index, ahead in enumerate(steps_of(sizes)):
-                piece = pieces[index][...] if each > 1 else pieces[0][index]
-                home_ref[source_of(me_ref, ahead, sizes)] = piece
-            unfold(home_ref, rows_ref, heads, 0, slots * heads // owners // 2, to_half)
-            source_ref = rows_ref
-
-        @pl.loop(0, slots // step)
-        def _(i):
-            where = pl.ds(pl.multiple_of(i * step, step), step)
-            total = dot_nt(source_ref[where, :], weight_refs[group][0])
-            total = total + dot_nt(value_refs[group][where, :], weight_refs[group][1])
-            total = total.astype(BF16).astype(F32)
-            if group > 0:
-                total = sum_ref[where, :] + total
-            if group == parts - 1:
-                total_ref[where, :] = total.astype(BF16)
-            else:
-                sum_ref[where, :] = total
-
-    toks = out_ref.shape[0]
-    step_t = min(512, toks)
-
-    @pl.loop(0, toks // step_t)
-    def _(i):
-        where = pl.ds(pl.multiple_of(i * step_t, step_t), step_t)
-        pick = ones_where(iota((step_t, slots), 1) == slot_ref[where, :])
-        out_ref[where, :] = dot(pick, total_ref[...]).astype(BF16)
-
-
-def call(kernel, outs, inputs, smem=(0,), scratch=(), flops=0, name=None):
+    refs[-1][...] = total.astype(refs[-1].dtype)
+
+
+def call(kernel, outs, inputs, smem=(0,), scratch=(), flops=0, vmem=24, name=None):
     specs = [
         pl.BlockSpec(memory_space=pltpu.SMEM if i in smem else pltpu.VMEM) for i in range(len(inputs))
     ]
@@ -476,7 +457,7 @@
         in_specs=specs,
         out_specs=jax.tree.map(lambda _: pl.BlockSpec(memory_space=pltpu.VMEM), outs),
         scratch_shapes=list(scratch),
-        compiler_params=pltpu.CompilerParams(vmem_limit_bytes=VMEM_LIMIT),
+        compiler_params=pltpu.CompilerParams(vmem_limit_bytes=vmem * 2**20),
         cost_estimate=pl.CostEstimate(flops=flops, bytes_accessed=moved, transcendentals=0),
         name=name,
     )(*inputs)
@@ -505,22 +486,18 @@
     return [parts[0]] + [shift(parts[ahead], axis, ahead) for ahead in range(1, len(parts))]
 
 
-def reduce_weight(me, by_sub, name):
+def fold_subs(me, by_sub, name):
     seqs, piece, columns = by_sub[0].shape
-    shape = jax.ShapeDtypeStruct
-    by_seq = call(
+    return call(
         fold_subs_kernel,
-        (shape((piece, columns), BF16),) * seqs,
+        (jax.ShapeDtypeStruct((piece, columns), BF16),) * seqs,
         (me, *pass_round(by_sub, "sub")),
-        name=name + "_subs",
-    )
-    return call(
-        sum_kernel,
-        shape((piece, columns), F32),
-        tuple(pass_round(by_seq, "seq")),
-        smem=(),
-        name=name + "_sum",
-    )
+        name=name,
+    )
+
+
+def add_up(terms, dtype, name):
+    return call(sum_kernel, jax.ShapeDtypeStruct(terms[0].shape, dtype), tuple(terms), smem=(), name=name)
 
 
 def on_device(tokens_in, w_query, w_value, cotangent, assignment):
@@ -557,17 +534,15 @@
         name="project_query",
     )
     got_mixed = exchange(send_mixed, sizes)
-    sent = call(
-        functools.partial(project_value_kernel, sizes, groups, rows, parts),
-        several(owners, half, LANES) + several(parts, 2, columns, width_dev) + several(1, width, slots),
-        (me, slot_row, tokens_in, w_value, w_query),
+    *send_value, turned, unsort = call(
+        functools.partial(project_value_kernel, sizes, groups, rows),
+        several(owners, half, LANES) + several(1, width, toks) + several(1, toks, slots),
+        (me, slot_row, tokens_in, w_value),
         scratch=[pltpu.VMEM((toks, width_dev), BF16), pltpu.VMEM((owners, half, LANES), BF16)],
-        flops=2 * toks * width * width_dev + 2 * slots * toks * (width_dev + width),
+        flops=2 * toks * width * width_dev + 2 * slots * toks * width_dev,
         name="project_value",
     )
-    got_value = exchange(sent[:owners], sizes)
-    weights = pass_round(sent[owners:-1], "head")
-    turned = sent[-1]
+    got_value = exchange(send_value, sizes)
     blocks = per_group * capacity // BLOCK_ROWS
     held = blocks + (LEAD + 4) * UNROLL
     block_flops = 2 * BLOCK_ROWS * BLOCK_ROWS * LANES
@@ -586,6 +561,7 @@
         + [group_f32] * 2
         + [group_b16] * 2,
         flops=4 * blocks * block_flops,
+        vmem=48,
         name="value_grad",
     )
     home_value = exchange(back_value, sizes)
@@ -598,48 +574,49 @@
         + [group_f32] * 4
         + [group_b16] * 2,
         flops=6 * blocks * block_flops,
+        vmem=48,
         name="query_grad",
     )
     home_query = exchange(back_query, sizes)
-    weight_flops = 2 * slots * width * width_dev
-    weight_outs = several(1, slots, width_dev) + several(sizes[1], sizes[0], width // owners, width_dev)
+    weight_flops = 2 * toks * width * width_dev
+    home_flops = 2 * slots * toks * width_dev
+    sub_shapes = several(sizes[1], sizes[0], width // owners, width_dev)
+    whole = pltpu.VMEM((width, width_dev), BF16)
+    sorted_rows = pltpu.VMEM((slots, width_dev), BF16)
     value_rows, *value_weight = call(
-        functools.partial(weight_grad_kernel, sizes, heads, None),
-        weight_outs,
-        (me, turned, *home_value),
-        scratch=[pltpu.VMEM((owners, half, LANES), BF16), pltpu.VMEM((width, width_dev), BF16)],
-        flops=weight_flops,
-        name="value_weight",
-    )
-    all_value_rows = pass_round([value_rows] * parts, "head")
-    grad_wv = reduce_weight(me, value_weight, "value_weight")
-    if parts == 2:
-        others = [shift(piece, "head", 1) for piece in home_query]
-    else:
-        stacked = jnp.stack(home_query)
-        others = [shift(stacked, "head", ahead) for ahead in range(1, parts)]
-    query_rows, *query_weight, centroid_grad = call(
-        functools.partial(weight_grad_kernel, sizes, heads, (CLUSTERS / (toks * owners)) ** 0.5),
-        weight_outs + (shape((groups * 2 * extra, width_dev), F32),),
-        (me, turned, *home_query),
-        scratch=[pltpu.VMEM((owners, half + extra, LANES), BF16), pltpu.VMEM((width, width_dev), BF16)],
+        functools.partial(value_home_kernel, sizes, heads),
+        several(1, toks, width_dev) + sub_shapes,
+        (me, turned, unsort, *home_value),
+        scratch=[pltpu.VMEM((owners, half, LANES), BF16), sorted_rows, whole],
+        flops=weight_flops + home_flops,
+        name="value_home",
+    )
+    value_weight = fold_subs(me, value_weight, "value_subs")
+    *partials, query_rows, centroid_grad = call(
+        functools.partial(query_home_kernel, sizes, heads, (CLUSTERS / (toks * owners)) ** 0.5, parts),
+        several(parts, toks, columns)
+        + several(1, toks, width_dev)
+        + (shape((groups * 2 * extra, width_dev), F32),),
+        (me, unsort, value_rows, w_query, w_value, *home_query),
+        scratch=[pltpu.VMEM((owners, half + extra, LANES), BF16), sorted_rows],
+        flops=2 * weight_flops + home_flops,
+        name="query_home",
+    )
+    arrived = pass_round(partials, "head")
+    value_weight, _ = lax.optimization_barrier((value_weight, home_query))
+    value_weight = pass_round(value_weight, "seq")
+    query_weight = call(
+        functools.partial(query_weight_kernel, sizes),
+        sub_shapes,
+        (me, turned, query_rows),
+        scratch=[whole],
         flops=weight_flops,
         name="query_weight",
     )
-    grad_wq = reduce_weight(me, query_weight, "query_weight")
-    grad_input = call(
-        functools.partial(input_grad_kernel, sizes, heads, parts),
-        shape((toks, columns), BF16),
-        (me, slot_row.reshape(toks, 1), *all_value_rows, *weights, query_rows, *others),
-        scratch=[
-            pltpu.VMEM((owners, half + extra, LANES), BF16),
-            pltpu.VMEM((slots, width_dev), BF16),
-            pltpu.VMEM((slots, columns), F32),
-            pltpu.VMEM((slots, columns), BF16),
-        ],
-        flops=2 * weight_flops + 2 * slots * toks * columns,
-        name="input_grad",
-    )
+    query_weight = pass_round(fold_subs(me, query_weight, "query_subs"), "seq")
+    grad_wv = add_up(value_weight, F32, "value_sum")
+    grad_wq = add_up(query_weight, F32, "query_sum")
+    grad_input = add_up(arrived, BF16, "input_sum")
     if groups > 1:
         centroid_grad = centroid_grad.reshape(groups, 2 * extra, width_dev)[:, :per_group]
         centroid_grad = centroid_grad.reshape(CLUSTERS, width_dev)

time: 241 us -> 183 us (0.76)
  waiting for transfers between devices: 83.1 us -> 52.2 us
  Pallas kernels: 76.2 us -> 54.5 us
  starting transfers between devices: 74.8 us -> 68.9 us
    ppermute x18 -> x9, waiting for transfers between devices: 55.6 us -> 7.96 us  [shift(): lax.ppermute(part, axis, [(i, (i + ahead) % size) for i in range(size)])]
    pallas_call x11 -> x12, Pallas kernels: 76.2 us -> 54.5 us  [call(): pl.pallas_call(kernel, out_shape=outs, in_specs=specs, out_specs=jax.tree...]
    ppermute x28, waiting for transfers between devices: 27.5 us -> 44.2 us  [exchange(): out.append(part if ahead == (0, 0) else lax.ppermute(part, OWNERS, moves))]
    ppermute x18 -> x9, starting transfers between devices: 25.6 us -> 19.3 us  [shift(): lax.ppermute(part, axis, [(i, (i + ahead) % size) for i in range(size)])]
  transfers between devices with their start and end apart: 46 -> 37, of which waited for: 14 -> 10; matrix products, arithmetic and copies ran while one was open for 0% -> 0% of each run, Pallas kernels for 25% -> 23%
where the time goes in v4:
time: 183 us; the launch traced here: 181 us
  starting transfers between devices  68.9 us (38%)
  Pallas kernels  54.5 us (30%)
  waiting for transfers between devices  52.2 us (29%)
  local copies, waits for them, and re-layouts  4.74 us (3%)
    pallas_call x12, Pallas kernels, call(): pl.pallas_call(kernel, out_shape=outs, in_specs=specs, out_specs=jax.tree...  54.5 us
    ppermute x28, starting transfers between devices, exchange(): out.append(part if ahead == (0, 0) else lax.ppermute(part, OWNERS, moves))  49.6 us
    ppermute x28, waiting for transfers between devices, exchange(): out.append(part if ahead == (0, 0) else lax.ppermute(part, OWNERS, moves))  44.2 us
    ppermute x9, starting transfers between devices, shift(): lax.ppermute(part, axis, [(i, (i + ahead) % size) for i in range(size)])  19.3 us
    ppermute x9, waiting for transfers between devices, shift(): lax.ppermute(part, axis, [(i, (i + ahead) % size) for i in range(size)])  7.96 us
    unnamed x14, local copies, waits for them, and re-layouts  4.74 us
  transfers between devices with their start and end apart: 37, of which 10 were waited for; matrix products, arithmetic and copies ran while one was open for 0% of the time, Pallas kernels for 23%

profile of v4, /device:TPU:0, one launch (start us, length us, event | category | flops | bytes accessed | tf_op | source)
XLA Modules:
  0.0 181.2 jit_solution(14986483361449872788)
XLA Ops:
  0.7 1.6 copy-done
  2.3 1.2 copy-done.2
  3.5 1.2 copy-done.3
  4.8 0.7 copy-done.6
  5.5 5.4 %project_query.1 = (bf16[1040,128]{1,0:T(8,128)(2,1)S(1)}, bf16[1040,128]{1,0:T(8,128)(2,1)S(1)}, bf16[1040,128]{1,0:T(8,128)(2,1)S(1)}, bf16[1040,128]{1,0:T(8,...) custom-call(s32[4]{0:T(128)S(1)} %pad_add_fusion.me_ref, ...), custom_call_target="tpu_custom_call" | custom-call | flops 3221225472 | bytes 6332432 | tf_op jit(solution)/shard_map/project_query/pallas_call | solution.py:454
  11.4 2.6 %collective-permute-start.1 = (bf16[1040,128]{1,0:T(8,128)(2,1)S(1)}, bf16[1040,128]{1,0:T(8,128)(2,1)S(1)}, u32[]{:S(2)}, u32[]{:S(2)}) collective-permute-start(bf16[1040,128]{1,0:T(8,128)(2,1)S(1)} %get-tuple-element.67), channel_id=1, source_target_pairs={{0,4},{1,5},{4,8},{5,9},{8,12},{9,13},{12,0},{13,1},{2,6},{3,7},{6... | collective-permute-start | bytes 798728 | tf_op jit(solution)/shard_map/ppermute | solution.py:476
  14.0 4.8 %project_value.1 = (bf16[512,128]{1,0:T(8,128)(2,1)S(1)}, bf16[512,128]{1,0:T(8,128)(2,1)S(1)}, bf16[512,128]{1,0:T(8,128)(2,1)S(1)}, bf16[512,128]{1,0:T(8,128)...) custom-call(s32[4]{0:T(128)S(1)} %pad_add_fusion.me_ref, ...), custom_call_target="tpu_custom_call" | custom-call | flops 2147483648 | bytes 8392720 | tf_op jit(solution)/shard_map/project_value/pallas_call | solution.py:454
  19.0 1.6 collective-permute-start.15
  20.6 1.2 collective-permute-start.2
  21.9 1.2 collective-permute-start.3
  23.1 4.1 %collective-permute-done.15.refs_2_ = bf16[512,128]{1,0:T(8,128)(2,1)S(1)} collective-permute-done((bf16[512,128]{1,0:T(8,128)(2,1)S(1)}, bf16[512,128]{1,0:T(8,128)(2,1)S(1)}, u32[]{:S(2)}, u32[]{:S(2)}) %collective-permute-start.15) | collective-permute-done | bytes 131104 | tf_op jit(solution)/shard_map/ppermute | solution.py:476
  27.3 0.8 collective-permute-start.5
  28.0 3.1 %collective-permute-start.6 = (bf16[1040,128]{1,0:T(8,128)(2,1)S(1)}, bf16[1040,128]{1,0:T(8,128)(2,1)S(1)}, u32[]{:S(2)}, u32[]{:S(2)}) collective-permute-start(bf16[1040,128]{1,0:T(8,128)(2,1)S(1)} %get-tuple-element.72), channel_id=1, source_target_pairs={{0,13},{1,12},{4,1},{5,0},{8,5},{9,4},{12,9},{13,8},{2,15},{3,14},... | collective-permute-start | bytes 798728 | tf_op jit(solution)/shard_map/ppermute | solution.py:476
  31.1 0.8 collective-permute-done.2.refs_3_
  32.1 17.4 %collective-permute-done.3.refs_4_ = bf16[1040,128]{1,0:T(8,128)(2,1)S(1)} collective-permute-done((bf16[1040,128]{1,0:T(8,128)(2,1)S(1)}, bf16[1040,128]{1,0:T(8,128)(2,1)S(1)}, u32[]{:S(2)}, u32[]{:S(2)}) %collective-permute-start.3) | collective-permute-done | bytes 266272 | tf_op jit(solution)/shard_map/ppermute | solution.py:476
  49.5 6.1 %collective-permute-done.4.refs_5_ = bf16[1040,128]{1,0:T(8,128)(2,1)S(1)} collective-permute-done((bf16[1040,128]{1,0:T(8,128)(2,1)S(1)}, bf16[1040,128]{1,0:T(8,128)(2,1)S(1)}, u32[]{:S(2)}, u32[]{:S(2)}) %collective-permute-start.4) | collective-permute-done | bytes 266272 | tf_op jit(solution)/shard_map/ppermute | solution.py:476
  55.5 1.3 collective-permute-start.18
  56.8 16.5 %collective-permute-start.19 = (bf16[512,128]{1,0:T(8,128)(2,1)S(1)}, bf16[512,128]{1,0:T(8,128)(2,1)S(1)}, u32[]{:S(2)}, u32[]{:S(2)}) collective-permute-start(bf16[512,128]{1,0:T(8,128)(2,1)S(1)} %get-tuple-element.90), channel_id=1, source_target_pairs={{0,12},{1,13},{4,0},{5,1},{8,4},{9,5},{12,8},{13,9},{2,14},{3,15},... | collective-permute-start | bytes 393224 | tf_op jit(solution)/shard_map/ppermute | solution.py:476
  73.3 0.7 collective-permute-start.20
  74.0 13.1 %value_grad.1 = (bf16[512,128]{1,0:T(8,128)(2,1)S(1)}, bf16[512,128]{1,0:T(8,128)(2,1)S(1)}, bf16[512,128]{1,0:T(8,128)(2,1)S(1)}, bf16[512,128]{1,0:T(8,128)(2,...) custom-call(s32[4]{0:T(128)S(1)} %pad_add_fusion.me_ref, ...), custom_call_target="tpu_custom_call" | custom-call | flops 2147483648 | bytes 8163344 | tf_op jit(solution)/shard_map/value_grad/pallas_call | solution.py:454
  87.1 1.7 collective-permute-start.8
  89.4 1.9 %collective-permute-start.10 = (bf16[512,128]{1,0:T(8,128)(2,1)S(1)}, bf16[512,128]{1,0:T(8,128)(2,1)S(1)}, u32[]{:S(2)}, u32[]{:S(2)}) collective-permute-start(bf16[512,128]{1,0:T(8,128)(2,1)S(1)} %get-tuple-element.77), channel_id=1, source_target_pairs={{0,8},{1,9},{4,12},{5,13},{8,0},{9,1},{12,4},{13,5},{2,10},{3,11},... | collective-permute-start | bytes 393224 | tf_op jit(solution)/shard_map/ppermute | solution.py:476
  91.3 15.8 %query_grad.1 = (bf16[544,128]{1,0:T(8,128)(2,1)S(1)}, bf16[544,128]{1,0:T(8,128)(2,1)S(1)}, bf16[544,128]{1,0:T(8,128)(2,1)S(1)}, bf16[544,128]{1,0:T(8,128)(2,...) custom-call(s32[4]{0:T(128)S(1)} %pad_add_fusion.me_ref, ...), custom_call_target="tpu_custom_call" | custom-call | flops 3221225472 | bytes 7147536 | tf_op jit(solution)/shard_map/query_grad/pallas_call | solution.py:454
  107.2 1.7 collective-permute-start.22
  108.9 0.8 collective-permute-start.11
  109.7 1.6 collective-permute-start.12
  111.4 1.3 collective-permute-start.13
  112.7 8.0 %collective-permute-done.11.refs_5_ = bf16[512,128]{1,0:T(8,128)(2,1)S(1)} collective-permute-done((bf16[512,128]{1,0:T(8,128)(2,1)S(1)}, bf16[512,128]{1,0:T(8,128)(2,1)S(1)}, u32[]{:S(2)}, u32[]{:S(2)}) %collective-permute-start.11) | collective-permute-done | bytes 131104 | tf_op jit(solution)/shard_map/ppermute | solution.py:476
  120.7 2.6 %collective-permute-start.23 = (bf16[544,128]{1,0:T(8,128)(2,1)S(1)}, bf16[544,128]{1,0:T(8,128)(2,1)S(1)}, u32[]{:S(2)}, u32[]{:S(2)}) collective-permute-start(bf16[544,128]{1,0:T(8,128)(2,1)S(1)} %get-tuple-element.95), channel_id=1, source_target_pairs={{0,5},{1,4},{4,9},{5,8},{8,13},{9,12},{12,1},{13,0},{2,7},{3,6},{6... | collective-permute-start | bytes 417800 | tf_op jit(solution)/shard_map/ppermute | solution.py:476
  123.4 3.4 %collective-permute-start.24 = (bf16[544,128]{1,0:T(8,128)(2,1)S(1)}, bf16[544,128]{1,0:T(8,128)(2,1)S(1)}, u32[]{:S(2)}, u32[]{:S(2)}) collective-permute-start(bf16[544,128]{1,0:T(8,128)(2,1)S(1)} %get-tuple-element.96), channel_id=1, source_target_pairs={{0,8},{1,9},{4,12},{5,13},{8,0},{9,1},{12,4},{13,5},{2,10},{3,11},... | collective-permute-start | bytes 417800 | tf_op jit(solution)/shard_map/ppermute | solution.py:476
  126.8 2.1 %collective-permute-start.26 = (bf16[544,128]{1,0:T(8,128)(2,1)S(1)}, bf16[544,128]{1,0:T(8,128)(2,1)S(1)}, u32[]{:S(2)}, u32[]{:S(2)}) collective-permute-start(bf16[544,128]{1,0:T(8,128)(2,1)S(1)} %get-tuple-element.98), channel_id=1, source_target_pairs={{0,12},{1,13},{4,0},{5,1},{8,4},{9,5},{12,8},{13,9},{2,14},{3,15},... | collective-permute-start | bytes 417800 | tf_op jit(solution)/shard_map/ppermute | solution.py:476
  128.9 1.7 collective-permute-start.27
  130.6 3.9 %value_home.1 = (bf16[1024,512]{1,0:T(8,128)(2,1)S(1)}, bf16[4,128,512]{2,1,0:T(8,128)(2,1)S(1)}, bf16[4,128,512]{2,1,0:T(8,128)(2,1)S(1)}) custom-call(s32[4]{0:T(128)S(1)} %pad_add_fusion.me_ref, bf16[1024,1024]{1,0:T(8,128)(2,1)S(1)} %get-tuple-element.64.turned_ref, bf16[1024,1024]{1,0:T(8,128)(2,1)S(1)} %get-tuple-element.63.unsort_ref, ...), custom_call_target="tpu_custom_call" | custom-call | flops 2147483648 | bytes 7340048 | tf_op jit(solution)/shard_map/value_home/pallas_call | solution.py:454
  134.6 4.8 %collective-permute-done.24.refs_4_ = bf16[544,128]{1,0:T(8,128)(2,1)S(1)} collective-permute-done((bf16[544,128]{1,0:T(8,128)(2,1)S(1)}, bf16[544,128]{1,0:T(8,128)(2,1)S(1)}, u32[]{:S(2)}, u32[]{:S(2)}) %collective-permute-start.24) | collective-permute-done | bytes 139296 | tf_op jit(solution)/shard_map/ppermute | solution.py:476
  139.4 2.9 %collective-permute-done.25.refs_5_ = bf16[544,128]{1,0:T(8,128)(2,1)S(1)} collective-permute-done((bf16[544,128]{1,0:T(8,128)(2,1)S(1)}, bf16[544,128]{1,0:T(8,128)(2,1)S(1)}, u32[]{:S(2)}, u32[]{:S(2)}) %collective-permute-start.25) | collective-permute-done | bytes 139296 | tf_op jit(solution)/shard_map/ppermute | solution.py:476
  142.3 5.5 %query_home.1 = (bf16[1024,512]{1,0:T(8,128)(2,1)S(1)}, bf16[1024,512]{1,0:T(8,128)(2,1)S(1)}, bf16[1024,512]{1,0:T(8,128)(2,1)S(1)}, f32[64,512]{1,0:T(8,128)}) custom-call(s32[4]{0:T(128)S(1)} %pad_add_fusion.me_ref, bf16[1024,1024]{1,0:T(8,128)(2,1)S(1)} %get-tuple-element.63.unsort_ref, bf16[1024,512]{1,0:T(8,128)(2,1)S(1)} %get-tuple-element.81.value_rows_ref, ...), custom_call_target="tpu_custom_call" | custom-call | flops 3221225472 | bytes 9633808 | tf_op jit(solution)/shard_map/query_home/pallas_call | solution.py:454
  147.8 1.6 collective-permute-start.28
  149.4 2.0 %query_weight.1 = (bf16[4,128,512]{2,1,0:T(8,128)(2,1)S(1)}, bf16[4,128,512]{2,1,0:T(8,128)(2,1)S(1)}) custom-call(s32[4]{0:T(128)S(1)} %pad_add_fusion.me_ref, bf16[1024,1024]{1,0:T(8,128)(2,1)S(1)} %get-tuple-element.64.turned_ref, bf16[1024,512]{1,0:T(8,128)(2,1)S(1)} %get-tuple-element.102.rows_ref), custom_call_target="tpu_custom_call" | custom-call | flops 1073741824 | bytes 4194320 | tf_op jit(solution)/shard_map/query_weight/pallas_call | solution.py:454
  152.7 6.6 %collective-permute-start.34 = (bf16[128,512]{1,0:T(8,128)(2,1)S(1)}, bf16[128,512]{1,0:T(8,128)(2,1)S(1)}, u32[]{:S(2)}, u32[]{:S(2)}) collective-permute-start(bf16[128,512]{1,0:T(8,128)(2,1)S(1)} %get-tuple-element.116), channel_id=1, source_target_pairs={{0,4},{4,8},{8,12},{12,0},{1,5},{5,9},{9,13},{13,1},{2,6},{6,10},{... | collective-permute-start | bytes 393224 | tf_op jit(solution)/shard_map/ppermute | solution.py:482
  159.2 2.4 %collective-permute-start.36 = (bf16[128,512]{1,0:T(8,128)(2,1)S(1)}, bf16[128,512]{1,0:T(8,128)(2,1)S(1)}, u32[]{:S(2)}, u32[]{:S(2)}) collective-permute-start(bf16[128,512]{1,0:T(8,128)(2,1)S(1)} %get-tuple-element.118), channel_id=1, source_target_pairs={{0,12},{4,0},{8,4},{12,8},{1,13},{5,1},{9,5},{13,9},{2,14},{6,2},{... | collective-permute-start | bytes 393224 | tf_op jit(solution)/shard_map/ppermute | solution.py:482
  162.4 0.7 collective-permute-done.34.refs_1_
  163.1 2.3 %collective-permute-start.31 = (bf16[128,512]{1,0:T(8,128)(2,1)S(1)}, bf16[128,512]{1,0:T(8,128)(2,1)S(1)}, u32[]{:S(2)}, u32[]{:S(2)}) collective-permute-start(bf16[128,512]{1,0:T(8,128)(2,1)S(1)} %get-tuple-element.107), channel_id=1, source_target_pairs={{0,8},{4,12},{8,0},{12,4},{1,9},{5,13},{9,1},{13,5},{2,10},{6,14},... | collective-permute-start | bytes 393224 | tf_op jit(solution)/shard_map/ppermute | solution.py:482
  165.3 3.6 %collective-permute-done.35.refs_2_ = bf16[128,512]{1,0:T(8,128)(2,1)S(1)} collective-permute-done((bf16[128,512]{1,0:T(8,128)(2,1)S(1)}, bf16[128,512]{1,0:T(8,128)(2,1)S(1)}, u32[]{:S(2)}, u32[]{:S(2)}) %collective-permute-start.35) | collective-permute-done | bytes 131104 | tf_op jit(solution)/shard_map/ppermute | solution.py:482
  168.9 5.8 %collective-permute-start.32 = (bf16[128,512]{1,0:T(8,128)(2,1)S(1)}, bf16[128,512]{1,0:T(8,128)(2,1)S(1)}, u32[]{:S(2)}, u32[]{:S(2)}) collective-permute-start(bf16[128,512]{1,0:T(8,128)(2,1)S(1)} %get-tuple-element.108), channel_id=1, source_target_pairs={{0,12},{4,0},{8,4},{12,8},{1,13},{5,1},{9,5},{13,9},{2,14},{6,2},{... | collective-permute-start | bytes 393224 | tf_op jit(solution)/shard_map/ppermute | solution.py:482
  174.7 0.8 value_sum.1
  175.5 3.7 %collective-permute-done.31.refs_2_ = bf16[128,512]{1,0:T(8,128)(2,1)S(1)} collective-permute-done((bf16[128,512]{1,0:T(8,128)(2,1)S(1)}, bf16[128,512]{1,0:T(8,128)(2,1)S(1)}, u32[]{:S(2)}, u32[]{:S(2)}) %collective-permute-start.31) | collective-permute-done | bytes 131104 | tf_op jit(solution)/shard_map/ppermute | solution.py:482
  179.2 0.8 query_sum.1
  180.0 1.2 input_sum.1
  (53 shorter events, 3.9 us)
Async XLA Ops:
  0.7 1.6 copy-start
  2.3 1.2 copy-start.2
  3.5 1.2 copy-start.3
  4.8 0.7 copy-start.6
  5.4 8.5 %copy-start.1 = (bf16[1024,1024]{1,0:T(8,128)(2,1)S(1)}, bf16[1024,1024]{1,0:T(8,128)(2,1)}, u32[]{:S(2)}) copy-start(bf16[1024,1024]{1,0:T(8,128)(2,1)} %tokens_ref.3) | copy-start | bytes 6291460
  5.4 8.5 %copy-start.5 = (bf16[1024,512]{1,0:T(8,128)(2,1)S(1)}, bf16[1024,512]{1,0:T(8,128)(2,1)}, u32[]{:S(2)}) copy-start(bf16[1024,512]{1,0:T(8,128)(2,1)} %w_value_ref.1) | copy-start | bytes 3145732
  10.8 16.4 %collective-permute-start = (bf16[1040,128]{1,0:T(8,128)(2,1)S(1)}, bf16[1040,128]{1,0:T(8,128)(2,1)S(1)}, u32[]{:S(2)}, u32[]{:S(2)}) collective-permute-start(bf16[1040,128]{1,0:T(8,128)(2,1)S(1)} %get-tuple-element.66), channel_id=1, source_target_pairs={{0,1},{1,0},{4,5},{5,4},{8,9},{9,8},{12,13},{13,12},{2,3},{3,2},{6... | collective-permute-start | bytes 798728 | tf_op jit(solution)/shard_map/ppermute | solution.py:476
  11.4 16.7 %collective-permute-start.1 = (bf16[1040,128]{1,0:T(8,128)(2,1)S(1)}, bf16[1040,128]{1,0:T(8,128)(2,1)S(1)}, u32[]{:S(2)}, u32[]{:S(2)}) collective-permute-start(bf16[1040,128]{1,0:T(8,128)(2,1)S(1)} %get-tuple-element.67), channel_id=1, source_target_pairs={{0,4},{1,5},{4,8},{5,9},{8,12},{9,13},{12,0},{13,1},{2,6},{3,7},{6... | collective-permute-start | bytes 798728 | tf_op jit(solution)/shard_map/ppermute | solution.py:476
  18.8 3.1 %collective-permute-start.14 = (bf16[512,128]{1,0:T(8,128)(2,1)S(1)}, bf16[512,128]{1,0:T(8,128)(2,1)S(1)}, u32[]{:S(2)}, u32[]{:S(2)}) collective-permute-start(bf16[512,128]{1,0:T(8,128)(2,1)S(1)} %get-tuple-element.85), channel_id=1, source_target_pairs={{0,1},{1,0},{4,5},{5,4},{8,9},{9,8},{12,13},{13,12},{2,3},{3,2},{6... | collective-permute-start | bytes 393224 | tf_op jit(solution)/shard_map/ppermute | solution.py:476
  19.0 8.2 %collective-permute-start.15 = (bf16[512,128]{1,0:T(8,128)(2,1)S(1)}, bf16[512,128]{1,0:T(8,128)(2,1)S(1)}, u32[]{:S(2)}, u32[]{:S(2)}) collective-permute-start(bf16[512,128]{1,0:T(8,128)(2,1)S(1)} %get-tuple-element.86), channel_id=1, source_target_pairs={{0,4},{1,5},{4,8},{5,9},{8,12},{9,13},{12,0},{13,1},{2,6},{3,7},{6... | collective-permute-start | bytes 393224 | tf_op jit(solution)/shard_map/ppermute | solution.py:476
  20.6 11.3 %collective-permute-start.2 = (bf16[1040,128]{1,0:T(8,128)(2,1)S(1)}, bf16[1040,128]{1,0:T(8,128)(2,1)S(1)}, u32[]{:S(2)}, u32[]{:S(2)}) collective-permute-start(bf16[1040,128]{1,0:T(8,128)(2,1)S(1)} %get-tuple-element.68), channel_id=1, source_target_pairs={{0,5},{1,4},{4,9},{5,8},{8,13},{9,12},{12,1},{13,0},{2,7},{3,6},{6... | collective-permute-start | bytes 798728 | tf_op jit(solution)/shard_map/ppermute | solution.py:476
  21.9 27.6 %collective-permute-start.3 = (bf16[1040,128]{1,0:T(8,128)(2,1)S(1)}, bf16[1040,128]{1,0:T(8,128)(2,1)S(1)}, u32[]{:S(2)}, u32[]{:S(2)}) collective-permute-start(bf16[1040,128]{1,0:T(8,128)(2,1)S(1)} %get-tuple-element.69), channel_id=1, source_target_pairs={{0,8},{1,9},{4,12},{5,13},{8,0},{9,1},{12,4},{13,5},{2,10},{3,11},... | collective-permute-start | bytes 798728 | tf_op jit(solution)/shard_map/ppermute | solution.py:476
  27.3 28.3 %collective-permute-start.4 = (bf16[1040,128]{1,0:T(8,128)(2,1)S(1)}, bf16[1040,128]{1,0:T(8,128)(2,1)S(1)}, u32[]{:S(2)}, u32[]{:S(2)}) collective-permute-start(bf16[1040,128]{1,0:T(8,128)(2,1)S(1)} %get-tuple-element.70), channel_id=1, source_target_pairs={{0,9},{1,8},{4,13},{5,12},{8,1},{9,0},{12,5},{13,4},{2,11},{3,10},... | collective-permute-start | bytes 798728 | tf_op jit(solution)/shard_map/ppermute | solution.py:476
  27.3 29.6 %collective-permute-start.5 = (bf16[1040,128]{1,0:T(8,128)(2,1)S(1)}, bf16[1040,128]{1,0:T(8,128)(2,1)S(1)}, u32[]{:S(2)}, u32[]{:S(2)}) collective-permute-start(bf16[1040,128]{1,0:T(8,128)(2,1)S(1)} %get-tuple-element.71), channel_id=1, source_target_pairs={{0,12},{1,13},{4,0},{5,1},{8,4},{9,5},{12,8},{13,9},{2,14},{3,15},... | collective-permute-start | bytes 798728 | tf_op jit(solution)/shard_map/ppermute | solution.py:476
  28.0 45.3 %collective-permute-start.6 = (bf16[1040,128]{1,0:T(8,128)(2,1)S(1)}, bf16[1040,128]{1,0:T(8,128)(2,1)S(1)}, u32[]{:S(2)}, u32[]{:S(2)}) collective-permute-start(bf16[1040,128]{1,0:T(8,128)(2,1)S(1)} %get-tuple-element.72), channel_id=1, source_target_pairs={{0,13},{1,12},{4,1},{5,0},{8,5},{9,4},{12,9},{13,8},{2,15},{3,14},... | collective-permute-start | bytes 798728 | tf_op jit(solution)/shard_map/ppermute | solution.py:476
  31.9 55.1 %collective-permute-start.16 = (bf16[512,128]{1,0:T(8,128)(2,1)S(1)}, bf16[512,128]{1,0:T(8,128)(2,1)S(1)}, u32[]{:S(2)}, u32[]{:S(2)}) collective-permute-start(bf16[512,128]{1,0:T(8,128)(2,1)S(1)} %get-tuple-element.87), channel_id=1, source_target_pairs={{0,5},{1,4},{4,9},{5,8},{8,13},{9,12},{12,1},{13,0},{2,7},{3,6},{6... | collective-permute-start | bytes 393224 | tf_op jit(solution)/shard_map/ppermute | solution.py:476
  49.5 37.6 %collective-permute-start.17 = (bf16[512,128]{1,0:T(8,128)(2,1)S(1)}, bf16[512,128]{1,0:T(8,128)(2,1)S(1)}, u32[]{:S(2)}, u32[]{:S(2)}) collective-permute-start(bf16[512,128]{1,0:T(8,128)(2,1)S(1)} %get-tuple-element.88), channel_id=1, source_target_pairs={{0,8},{1,9},{4,12},{5,13},{8,0},{9,1},{12,4},{13,5},{2,10},{3,11},... | collective-permute-start | bytes 393224 | tf_op jit(solution)/shard_map/ppermute | solution.py:476
  55.5 33.2 %collective-permute-start.18 = (bf16[512,128]{1,0:T(8,128)(2,1)S(1)}, bf16[512,128]{1,0:T(8,128)(2,1)S(1)}, u32[]{:S(2)}, u32[]{:S(2)}) collective-permute-start(bf16[512,128]{1,0:T(8,128)(2,1)S(1)} %get-tuple-element.89), channel_id=1, source_target_pairs={{0,9},{1,8},{4,13},{5,12},{8,1},{9,0},{12,5},{13,4},{2,11},{3,10},... | collective-permute-start | bytes 393224 | tf_op jit(solution)/shard_map/ppermute | solution.py:476
  56.8 32.6 %collective-permute-start.19 = (bf16[512,128]{1,0:T(8,128)(2,1)S(1)}, bf16[512,128]{1,0:T(8,128)(2,1)S(1)}, u32[]{:S(2)}, u32[]{:S(2)}) collective-permute-start(bf16[512,128]{1,0:T(8,128)(2,1)S(1)} %get-tuple-element.90), channel_id=1, source_target_pairs={{0,12},{1,13},{4,0},{5,1},{8,4},{9,5},{12,8},{13,9},{2,14},{3,15},... | collective-permute-start | bytes 393224 | tf_op jit(solution)/shard_map/ppermute | solution.py:476
  73.3 18.0 %collective-permute-start.20 = (bf16[512,128]{1,0:T(8,128)(2,1)S(1)}, bf16[512,128]{1,0:T(8,128)(2,1)S(1)}, u32[]{:S(2)}, u32[]{:S(2)}) collective-permute-start(bf16[512,128]{1,0:T(8,128)(2,1)S(1)} %get-tuple-element.91), channel_id=1, source_target_pairs={{0,13},{1,12},{4,1},{5,0},{8,5},{9,4},{12,9},{13,8},{2,15},{3,14},... | collective-permute-start | bytes 393224 | tf_op jit(solution)/shard_map/ppermute | solution.py:476
  87.0 20.1 %collective-permute-start.7 = (bf16[512,128]{1,0:T(8,128)(2,1)S(1)}, bf16[512,128]{1,0:T(8,128)(2,1)S(1)}, u32[]{:S(2)}, u32[]{:S(2)}) collective-permute-start(bf16[512,128]{1,0:T(8,128)(2,1)S(1)} %get-tuple-element.74), channel_id=1, source_target_pairs={{0,1},{1,0},{4,5},{5,4},{8,9},{9,8},{12,13},{13,12},{2,3},{3,2},{6... | collective-permute-start | bytes 393224 | tf_op jit(solution)/shard_map/ppermute | solution.py:476
  87.1 21.8 %collective-permute-start.8 = (bf16[512,128]{1,0:T(8,128)(2,1)S(1)}, bf16[512,128]{1,0:T(8,128)(2,1)S(1)}, u32[]{:S(2)}, u32[]{:S(2)}) collective-permute-start(bf16[512,128]{1,0:T(8,128)(2,1)S(1)} %get-tuple-element.75), channel_id=1, source_target_pairs={{0,4},{1,5},{4,8},{5,9},{8,12},{9,13},{12,0},{13,1},{2,6},{3,7},{6... | collective-permute-start | bytes 393224 | tf_op jit(solution)/shard_map/ppermute | solution.py:476
  88.8 20.9 %collective-permute-start.9 = (bf16[512,128]{1,0:T(8,128)(2,1)S(1)}, bf16[512,128]{1,0:T(8,128)(2,1)S(1)}, u32[]{:S(2)}, u32[]{:S(2)}) collective-permute-start(bf16[512,128]{1,0:T(8,128)(2,1)S(1)} %get-tuple-element.76), channel_id=1, source_target_pairs={{0,5},{1,4},{4,9},{5,8},{8,13},{9,12},{12,1},{13,0},{2,7},{3,6},{6... | collective-permute-start | bytes 393224 | tf_op jit(solution)/shard_map/ppermute | solution.py:476
  89.4 22.0 %collective-permute-start.10 = (bf16[512,128]{1,0:T(8,128)(2,1)S(1)}, bf16[512,128]{1,0:T(8,128)(2,1)S(1)}, u32[]{:S(2)}, u32[]{:S(2)}) collective-permute-start(bf16[512,128]{1,0:T(8,128)(2,1)S(1)} %get-tuple-element.77), channel_id=1, source_target_pairs={{0,8},{1,9},{4,12},{5,13},{8,0},{9,1},{12,4},{13,5},{2,10},{3,11},... | collective-permute-start | bytes 393224 | tf_op jit(solution)/shard_map/ppermute | solution.py:476
  107.1 19.8 %collective-permute-start.21 = (bf16[544,128]{1,0:T(8,128)(2,1)S(1)}, bf16[544,128]{1,0:T(8,128)(2,1)S(1)}, u32[]{:S(2)}, u32[]{:S(2)}) collective-permute-start(bf16[544,128]{1,0:T(8,128)(2,1)S(1)} %get-tuple-element.93), channel_id=1, source_target_pairs={{0,1},{1,0},{4,5},{5,4},{8,9},{9,8},{12,13},{13,12},{2,3},{3,2},{6... | collective-permute-start | bytes 417800 | tf_op jit(solution)/shard_map/ppermute | solution.py:476
  107.2 21.7 %collective-permute-start.22 = (bf16[544,128]{1,0:T(8,128)(2,1)S(1)}, bf16[544,128]{1,0:T(8,128)(2,1)S(1)}, u32[]{:S(2)}, u32[]{:S(2)}) collective-permute-start(bf16[544,128]{1,0:T(8,128)(2,1)S(1)} %get-tuple-element.94), channel_id=1, source_target_pairs={{0,4},{1,5},{4,8},{5,9},{8,12},{9,13},{12,0},{13,1},{2,6},{3,7},{6... | collective-permute-start | bytes 417800 | tf_op jit(solution)/shard_map/ppermute | solution.py:476
  108.9 11.8 %collective-permute-start.11 = (bf16[512,128]{1,0:T(8,128)(2,1)S(1)}, bf16[512,128]{1,0:T(8,128)(2,1)S(1)}, u32[]{:S(2)}, u32[]{:S(2)}) collective-permute-start(bf16[512,128]{1,0:T(8,128)(2,1)S(1)} %get-tuple-element.78), channel_id=1, source_target_pairs={{0,9},{1,8},{4,13},{5,12},{8,1},{9,0},{12,5},{13,4},{2,11},{3,10},... | collective-permute-start | bytes 393224 | tf_op jit(solution)/shard_map/ppermute | solution.py:476
  109.7 13.6 %collective-permute-start.12 = (bf16[512,128]{1,0:T(8,128)(2,1)S(1)}, bf16[512,128]{1,0:T(8,128)(2,1)S(1)}, u32[]{:S(2)}, u32[]{:S(2)}) collective-permute-start(bf16[512,128]{1,0:T(8,128)(2,1)S(1)} %get-tuple-element.79), channel_id=1, source_target_pairs={{0,12},{1,13},{4,0},{5,1},{8,4},{9,5},{12,8},{13,9},{2,14},{3,15},... | collective-permute-start | bytes 393224 | tf_op jit(solution)/shard_map/ppermute | solution.py:476
  111.4 15.4 %collective-permute-start.13 = (bf16[512,128]{1,0:T(8,128)(2,1)S(1)}, bf16[512,128]{1,0:T(8,128)(2,1)S(1)}, u32[]{:S(2)}, u32[]{:S(2)}) collective-permute-start(bf16[512,128]{1,0:T(8,128)(2,1)S(1)} %get-tuple-element.80), channel_id=1, source_target_pairs={{0,13},{1,12},{4,1},{5,0},{8,5},{9,4},{12,9},{13,8},{2,15},{3,14},... | collective-permute-start | bytes 393224 | tf_op jit(solution)/shard_map/ppermute | solution.py:476
  120.7 13.8 %collective-permute-start.23 = (bf16[544,128]{1,0:T(8,128)(2,1)S(1)}, bf16[544,128]{1,0:T(8,128)(2,1)S(1)}, u32[]{:S(2)}, u32[]{:S(2)}) collective-permute-start(bf16[544,128]{1,0:T(8,128)(2,1)S(1)} %get-tuple-element.95), channel_id=1, source_target_pairs={{0,5},{1,4},{4,9},{5,8},{8,13},{9,12},{12,1},{13,0},{2,7},{3,6},{6... | collective-permute-start | bytes 417800 | tf_op jit(solution)/shard_map/ppermute | solution.py:476
  123.4 16.0 %collective-permute-start.24 = (bf16[544,128]{1,0:T(8,128)(2,1)S(1)}, bf16[544,128]{1,0:T(8,128)(2,1)S(1)}, u32[]{:S(2)}, u32[]{:S(2)}) collective-permute-start(bf16[544,128]{1,0:T(8,128)(2,1)S(1)} %get-tuple-element.96), channel_id=1, source_target_pairs={{0,8},{1,9},{4,12},{5,13},{8,0},{9,1},{12,4},{13,5},{2,10},{3,11},... | collective-permute-start | bytes 417800 | tf_op jit(solution)/shard_map/ppermute | solution.py:476
  126.8 15.5 %collective-permute-start.25 = (bf16[544,128]{1,0:T(8,128)(2,1)S(1)}, bf16[544,128]{1,0:T(8,128)(2,1)S(1)}, u32[]{:S(2)}, u32[]{:S(2)}) collective-permute-start(bf16[544,128]{1,0:T(8,128)(2,1)S(1)} %get-tuple-element.97), channel_id=1, source_target_pairs={{0,9},{1,8},{4,13},{5,12},{8,1},{9,0},{12,5},{13,4},{2,11},{3,10},... | collective-permute-start | bytes 417800 | tf_op jit(solution)/shard_map/ppermute | solution.py:476
  126.8 15.5 %collective-permute-start.26 = (bf16[544,128]{1,0:T(8,128)(2,1)S(1)}, bf16[544,128]{1,0:T(8,128)(2,1)S(1)}, u32[]{:S(2)}, u32[]{:S(2)}) collective-permute-start(bf16[544,128]{1,0:T(8,128)(2,1)S(1)} %get-tuple-element.98), channel_id=1, source_target_pairs={{0,12},{1,13},{4,0},{5,1},{8,4},{9,5},{12,8},{13,9},{2,14},{3,15},... | collective-permute-start | bytes 417800 | tf_op jit(solution)/shard_map/ppermute | solution.py:476
  128.9 13.4 %collective-permute-start.27 = (bf16[544,128]{1,0:T(8,128)(2,1)S(1)}, bf16[544,128]{1,0:T(8,128)(2,1)S(1)}, u32[]{:S(2)}, u32[]{:S(2)}) collective-permute-start(bf16[544,128]{1,0:T(8,128)(2,1)S(1)} %get-tuple-element.99), channel_id=1, source_target_pairs={{0,13},{1,12},{4,1},{5,0},{8,5},{9,4},{12,9},{13,8},{2,15},{3,14},... | collective-permute-start | bytes 417800 | tf_op jit(solution)/shard_map/ppermute | solution.py:476
  130.6 11.7 %copy-start.4 = (bf16[1024,512]{1,0:T(8,128)(2,1)S(1)}, bf16[1024,512]{1,0:T(8,128)(2,1)}, u32[]{:S(2)}) copy-start(bf16[1024,512]{1,0:T(8,128)(2,1)} %w_query_ref.1) | copy-start | bytes 3145732
  147.8 32.2 %collective-permute-start.28 = (bf16[1024,512]{1,0:T(8,128)(2,1)S(1)}, bf16[1024,512]{1,0:T(8,128)(2,1)S(1)}, u32[]{:S(2)}, u32[]{:S(2)}) collective-permute-start(bf16[1024,512]{1,0:T(8,128)(2,1)S(1)} %get-tuple-element.101), channel_id=1, source_target_pairs={{0,2},{2,0},{1,3},{3,1},{4,6},{6,4},{5,7},{7,5},{8,10},{10,8},{9,1... | collective-permute-start | bytes 3145736 | tf_op jit(solution)/shard_map/ppermute | solution.py:482
  149.4 2.6 %collective-permute-start.33 = (bf16[4,128,512]{2,1,0:T(8,128)(2,1)S(1)}, bf16[4,128,512]{2,1,0:T(8,128)(2,1)S(1)}, u32[]{:S(2)}, u32[]{:S(2)}) collective-permute-start(bf16[4,128,512]{2,1,0:T(8,128)(2,1)S(1)} %get-tuple-element.110), channel_id=1, source_target_pairs={{0,1},{1,0},{2,3},{3,2},{4,5},{5,4},{6,7},{7,6},{8,9},{9,8},{10,11... | collective-permute-start | bytes 1572872 | tf_op jit(solution)/shard_map/ppermute | solution.py:482
  151.4 10.3 %collective-permute-start.29 = (bf16[4,128,512]{2,1,0:T(8,128)(2,1)S(1)}, bf16[4,128,512]{2,1,0:T(8,128)(2,1)S(1)}, u32[]{:S(2)}, u32[]{:S(2)}) collective-permute-start(bf16[4,128,512]{2,1,0:T(8,128)(2,1)S(1)} %get-tuple-element.104), channel_id=1, source_target_pairs={{0,1},{1,0},{2,3},{3,2},{4,5},{5,4},{6,7},{7,6},{8,9},{9,8},{10,11... | collective-permute-start | bytes 1572872 | tf_op jit(solution)/shard_map/ppermute | solution.py:482
  152.7 10.4 %collective-permute-start.34 = (bf16[128,512]{1,0:T(8,128)(2,1)S(1)}, bf16[128,512]{1,0:T(8,128)(2,1)S(1)}, u32[]{:S(2)}, u32[]{:S(2)}) collective-permute-start(bf16[128,512]{1,0:T(8,128)(2,1)S(1)} %get-tuple-element.116), channel_id=1, source_target_pairs={{0,4},{4,8},{8,12},{12,0},{1,5},{5,9},{9,13},{13,1},{2,6},{6,10},{... | collective-permute-start | bytes 393224 | tf_op jit(solution)/shard_map/ppermute | solution.py:482
  159.2 9.7 %collective-permute-start.35 = (bf16[128,512]{1,0:T(8,128)(2,1)S(1)}, bf16[128,512]{1,0:T(8,128)(2,1)S(1)}, u32[]{:S(2)}, u32[]{:S(2)}) collective-permute-start(bf16[128,512]{1,0:T(8,128)(2,1)S(1)} %get-tuple-element.117), channel_id=1, source_target_pairs={{0,8},{4,12},{8,0},{12,4},{1,9},{5,13},{9,1},{13,5},{2,10},{6,14},... | collective-permute-start | bytes 393224 | tf_op jit(solution)/shard_map/ppermute | solution.py:482
  159.2 15.5 %collective-permute-start.36 = (bf16[128,512]{1,0:T(8,128)(2,1)S(1)}, bf16[128,512]{1,0:T(8,128)(2,1)S(1)}, u32[]{:S(2)}, u32[]{:S(2)}) collective-permute-start(bf16[128,512]{1,0:T(8,128)(2,1)S(1)} %get-tuple-element.118), channel_id=1, source_target_pairs={{0,12},{4,0},{8,4},{12,8},{1,13},{5,1},{9,5},{13,9},{2,14},{6,2},{... | collective-permute-start | bytes 393224 | tf_op jit(solution)/shard_map/ppermute | solution.py:482
  162.3 13.2 %collective-permute-start.30 = (bf16[128,512]{1,0:T(8,128)(2,1)S(1)}, bf16[128,512]{1,0:T(8,128)(2,1)S(1)}, u32[]{:S(2)}, u32[]{:S(2)}) collective-permute-start(bf16[128,512]{1,0:T(8,128)(2,1)S(1)} %get-tuple-element.106), channel_id=1, source_target_pairs={{0,4},{4,8},{8,12},{12,0},{1,5},{5,9},{9,13},{13,1},{2,6},{6,10},{... | collective-permute-start | bytes 393224 | tf_op jit(solution)/shard_map/ppermute | solution.py:482
  163.1 16.1 %collective-permute-start.31 = (bf16[128,512]{1,0:T(8,128)(2,1)S(1)}, bf16[128,512]{1,0:T(8,128)(2,1)S(1)}, u32[]{:S(2)}, u32[]{:S(2)}) collective-permute-start(bf16[128,512]{1,0:T(8,128)(2,1)S(1)} %get-tuple-element.107), channel_id=1, source_target_pairs={{0,8},{4,12},{8,0},{12,4},{1,9},{5,13},{9,1},{13,5},{2,10},{6,14},... | collective-permute-start | bytes 393224 | tf_op jit(solution)/shard_map/ppermute | solution.py:482
  168.9 10.3 %collective-permute-start.32 = (bf16[128,512]{1,0:T(8,128)(2,1)S(1)}, bf16[128,512]{1,0:T(8,128)(2,1)S(1)}, u32[]{:S(2)}, u32[]{:S(2)}) collective-permute-start(bf16[128,512]{1,0:T(8,128)(2,1)S(1)} %get-tuple-element.108), channel_id=1, source_target_pairs={{0,12},{4,0},{8,4},{12,8},{1,13},{5,1},{9,5},{13,9},{2,14},{6,2},{... | collective-permute-start | bytes 393224 | tf_op jit(solution)/shard_map/ppermute | solution.py:482

commit v5 on v4

--- a/solution.py
+++ b/solution.py
@@ -59,14 +59,41 @@
     return [(seq, sub) for seq in range(sizes[0]) for sub in range(sizes[1])]
 
 
-def hand_out(by_owner_ref, out_refs, me_ref, sizes):
-    for ahead, out_ref in zip(steps_of(sizes), out_refs):
-        out_ref[...] = by_owner_ref[owner_of(me_ref, ahead, sizes)]
-
-
-def project_query_kernel(sizes, groups, rows, me_ref, assign_ref, tokens_ref, weight_ref, cotan_ref, *rest):
-    out_refs, (slot_ref, mixed_ref, sorted_ref) = rest[:-3], rest[-3:]
+def arrivals(sizes, me_ref, refs):
+    seqs, subs = sizes
+    for ahead in steps_of(sizes):
+        if ahead[1] == 0:
+            piece = refs[ahead[0]][me_ref[1]]
+        else:
+            piece = refs[seqs + ahead[1] - 1][ahead[0]]
+        yield source_of(me_ref, ahead, sizes), piece
+
+
+def swap_kernel(sizes, me_ref, *refs):
+    for k, out_ref in enumerate(refs[sizes[0] :]):
+        sub = lax.rem(me_ref[1] + (k + 1), jnp.int32(sizes[1]))
+        for seq in range(sizes[0]):
+            out_ref[seq] = refs[seq][sub]
+
+
+def project_query_kernel(sizes, groups, rows, me_ref, assign_ref, tokens_hbm, weight_hbm, cotan_hbm, *rest):
+    out_refs, rest = rest[:-8], rest[-8:]
+    slot_ref, tokens_ref, weight_ref, cotan_ref, mixed_ref, sorted_ref, in_sems, out_sems = rest
     toks = tokens_ref.shape[0]
+    step = min(512, toks)
+    load_weight = pltpu.make_async_copy(weight_hbm, weight_ref, in_sems.at[0])
+    load_weight.start()
+
+    def load(i):
+        where = pl.ds(i * step, step)
+        return (
+            pltpu.make_async_copy(tokens_hbm.at[where, :], tokens_ref.at[where, :], in_sems.at[1 + 2 * i]),
+            pltpu.make_async_copy(cotan_hbm.at[where, :], cotan_ref.at[where, :], in_sems.at[2 + 2 * i]),
+        )
+
+    for i in range(toks // step):
+        for copy in load(i):
+            copy.start()
     per_group = CLUSTERS // groups
     heads = weight_ref.shape[1] // HD
     member = iota((CLUSTERS, toks), 0) == assign_ref[...]
@@ -87,11 +114,11 @@
     for owner in range(sorted_ref.shape[0]):
         sorted_ref[owner, rows:, :] = tallies
 
-    step = min(512, toks)
-
-    @pl.loop(0, toks // step)
-    def _(i):
-        where = pl.ds(pl.multiple_of(i * step, step), step)
+    load_weight.wait()
+    for i in range(toks // step):
+        for copy in load(i):
+            copy.wait()
+        where = slice(i * step, (i + 1) * step)
         query = dot(tokens_ref[where, :], weight_ref[...])
         cotan = cotan_ref[where, :].astype(F32)
         low = low_half((step, LANES))
@@ -117,7 +144,14 @@
                 :, head * LANES : (head + 1) * LANES
             ]
 
-    hand_out(sorted_ref, out_refs, me_ref, sizes)
+    copies = [
+        pltpu.make_async_copy(sorted_ref.at[owner_of(me_ref, ahead, sizes)], out_ref, out_sems.at[k])
+        for k, (ahead, out_ref) in enumerate(zip(steps_of(sizes), out_refs))
+    ]
+    for copy in copies:
+        copy.start()
+    for copy in copies:
+        copy.wait()
 
 
 def project_value_kernel(sizes, groups, rows, me_ref, slot_ref, tokens_ref, weight_ref, *rest):
@@ -151,7 +185,9 @@
             sorted_ref[group * heads + 2 * pair, pl.ds(first, part), :] = even
             sorted_ref[group * heads + 2 * pair + 1, pl.ds(first, part), :] = odd
 
-    hand_out(sorted_ref, out_refs, me_ref, sizes)
+    for ahead, out_ref in enumerate(out_refs):
+        for sub in range(sizes[1]):
+            out_ref[sub] = sorted_ref[owner_of(me_ref, (ahead, 0), sizes) - me_ref[1] + sub]
     turned_ref[...] = tokens_ref[...].T
     slots = unsort_ref.shape[1]
     part = min(256, slots)
@@ -230,10 +266,10 @@
 
 def value_grad_kernel(sizes, per_group, slot_rows, me_ref, *refs):
     owners = sizes[0] * sizes[1]
-    mixed_refs, out_refs, rest = refs[:owners], refs[owners : 2 * owners], refs[2 * owners :]
+    mixed_refs, out_refs, rest = refs[:owners], refs[owners : owners + sizes[0]], refs[owners + sizes[0] :]
     dense_ref, counts_out_ref, counts_ref, place_ref, wide_ref, block_ref, home_ref = rest[:7]
     score_refs, probs_refs = rest[7:9], rest[9:11]
-    half = out_refs[0].shape[0]
+    half = out_refs[0].shape[1]
     rows = 2 * half
     for ahead, mixed_ref in zip(steps_of(sizes), mixed_refs):
         source = source_of(me_ref, ahead, sizes)
@@ -268,22 +304,23 @@
             wide_ref[source, pl.ds(start, slot_rows), :] = block_ref[pl.ds(row, slot_rows), :]
 
     for_each_cluster(counts_ref, me_ref, place_ref, owners, per_group, scatter)
-    for ahead, out_ref in zip(steps_of(sizes), out_refs):
-        source = owner_of(me_ref, ahead, sizes)
-        up, down = wide_ref[source, :half, :], wide_ref[source, half:rows, :]
-        out_ref[...] = jnp.where(low_half((half, LANES)), swap_halves(up), down).astype(BF16)
+    for ahead, out_ref in enumerate(out_refs):
+        for sub in range(sizes[1]):
+            source = owner_of(me_ref, (ahead, 0), sizes) - me_ref[1] + sub
+            up, down = wide_ref[source, :half, :], wide_ref[source, half:rows, :]
+            out_ref[sub] = jnp.where(low_half((half, LANES)), swap_halves(up), down).astype(BF16)
 
 
 def query_grad_kernel(sizes, per_group, slot_rows, me_ref, counts_ref, dense_ref, *refs):
     owners = sizes[0] * sizes[1]
-    value_refs, out_refs, rest = refs[:owners], refs[owners : 2 * owners], refs[2 * owners :]
+    values = sizes[0] + sizes[1] - 1
+    value_refs, out_refs, rest = refs[:values], refs[values : values + owners], refs[values + owners :]
     place_ref, wide_ref, block_ref, sums_ref, centroid_ref = rest[:5]
     score_refs, grad_probs_refs, both_refs = rest[5:7], rest[7:9], rest[9:11]
-    half = value_refs[0].shape[0]
+    half = value_refs[0].shape[1]
     rows = 2 * half
-    for ahead, value_ref in zip(steps_of(sizes), value_refs):
-        source = source_of(me_ref, ahead, sizes)
-        value = value_ref[...].astype(F32)
+    for source, value in arrivals(sizes, me_ref, value_refs):
+        value = value.astype(F32)
         wide_ref[source, :half, :] = swap_halves(value)
         wide_ref[source, half:rows, :] = value
         wide_ref[source, rows:, :] = jnp.zeros((slot_rows, LANES), F32)
@@ -358,9 +395,9 @@
     return x.astype(BF16)
 
 
-def bring_home(sizes, heads, me_ref, part_refs, unsort_ref, home_ref, sorted_ref, rows_ref):
-    for ahead, part_ref in zip(steps_of(sizes), part_refs):
-        home_ref[source_of(me_ref, ahead, sizes)] = part_ref[...]
+def bring_home(sizes, heads, pieces, unsort_ref, home_ref, sorted_ref, rows_ref):
+    for source, piece in pieces:
+        home_ref[source] = piece
     half = sorted_ref.shape[0] * heads // (sizes[0] * sizes[1]) // 2
     unfold(home_ref, sorted_ref, heads, 0, half, to_half)
     toks = rows_ref.shape[0]
@@ -392,38 +429,50 @@
 def value_home_kernel(sizes, heads, me_ref, turned_ref, unsort_ref, *refs):
     part_refs, rows_ref, sub_refs = refs[: -4 - sizes[1]], refs[-4 - sizes[1]], refs[-3 - sizes[1] : -3]
     home_ref, sorted_ref, whole_ref = refs[-3:]
-    bring_home(sizes, heads, me_ref, part_refs, unsort_ref, home_ref, sorted_ref, rows_ref)
+    pieces = arrivals(sizes, me_ref, part_refs)
+    bring_home(sizes, heads, pieces, unsort_ref, home_ref, sorted_ref, rows_ref)
     weight_partial(sizes, me_ref, turned_ref, rows_ref, whole_ref, sub_refs)
+
+
+def input_partial(me_ref, ahead, parts, rows_ref, value_rows_ref, w_query_ref, w_value_ref, out_ref):
+    toks = rows_ref.shape[0]
+    columns = w_query_ref.shape[0] // parts
+    step = min(512, toks)
+    dest = lax.rem(me_ref[2] + ahead, jnp.int32(parts))
+    mine = pl.ds(pl.multiple_of(dest * columns, columns), columns)
+
+    @pl.loop(0, toks // step)
+    def _(i):
+        where = pl.ds(pl.multiple_of(i * step, step), step)
+        total = dot_nt(rows_ref[where, :], w_query_ref[mine, :])
+        total = total + dot_nt(value_rows_ref[where, :], w_value_ref[mine, :])
+        out_ref[where, :] = total.astype(BF16)
 
 
 def query_home_kernel(
     sizes, heads, factor, parts, me_ref, unsort_ref, value_rows_ref, w_query_ref, w_value_ref, *refs
 ):
     part_refs, out_refs, (rows_ref, centroid_ref, home_ref, sorted_ref) = (
-        refs[: -4 - parts],
-        refs[-4 - parts : -4],
+        refs[: -3 - parts],
+        refs[-3 - parts : -4],
         refs[-4:],
     )
-    bring_home(sizes, heads, me_ref, part_refs, unsort_ref, home_ref, sorted_ref, rows_ref)
+    pieces = [
+        (source_of(me_ref, ahead, sizes), part_ref[...]) for ahead, part_ref in zip(steps_of(sizes), part_refs)
+    ]
+    bring_home(sizes, heads, pieces, unsort_ref, home_ref, sorted_ref, rows_ref)
     half = sorted_ref.shape[0] * heads // (sizes[0] * sizes[1]) // 2
     unfold(home_ref, centroid_ref, heads, half, home_ref.shape[1] - half, lambda x: x * factor)
-    toks = rows_ref.shape[0]
-    columns = w_query_ref.shape[0] // parts
-    step = min(512, toks)
     for ahead, out_ref in enumerate(out_refs):
-        dest = lax.rem(me_ref[2] + ahead, jnp.int32(parts))
-        mine = pl.ds(pl.multiple_of(dest * columns, columns), columns)
-
-        @pl.loop(0, toks // step)
-        def _(i):
-            where = pl.ds(pl.multiple_of(i * step, step), step)
-            total = dot_nt(rows_ref[where, :], w_query_ref[mine, :])
-            total = total + dot_nt(value_rows_ref[where, :], w_value_ref[mine, :])
-            out_ref[where, :] = total.astype(BF16)
-
-
-def query_weight_kernel(sizes, me_ref, turned_ref, rows_ref, *refs):
-    weight_partial(sizes, me_ref, turned_ref, rows_ref, refs[-1], refs[:-1])
+        input_partial(me_ref, ahead + 1, parts, rows_ref, value_rows_ref, w_query_ref, w_value_ref, out_ref)
+
+
+def query_weight_kernel(
+    sizes, parts, me_ref, turned_ref, rows_ref, value_rows_ref, w_query_ref, w_value_ref, *refs
+):
+    sub_refs, out_ref, whole_ref = refs[:-2], refs[-2], refs[-1]
+    weight_partial(sizes, me_ref, turned_ref, rows_ref, whole_ref, sub_refs)
+    input_partial(me_ref, 0, parts, rows_ref, value_rows_ref, w_query_ref, w_value_ref, out_ref)
 
 
 def fold_subs_kernel(me_ref, *refs):
@@ -444,23 +493,29 @@
     refs[-1][...] = total.astype(refs[-1].dtype)
 
 
-def call(kernel, outs, inputs, smem=(0,), scratch=(), flops=0, vmem=24, name=None):
-    specs = [
-        pl.BlockSpec(memory_space=pltpu.SMEM if i in smem else pltpu.VMEM) for i in range(len(inputs))
-    ]
+def call(kernel, outs, inputs, smem=(0,), in_place=(), after=(), scratch=(), flops=0, vmem=24, name=None):
+    def body(*refs):
+        kernel(*refs[: len(inputs)], *refs[len(inputs) + len(after) :])
+
+    def space(i):
+        return pltpu.SMEM if i in smem else pl.ANY if i in in_place else pltpu.VMEM
+
+    specs = [pl.BlockSpec(memory_space=space(i)) for i in range(len(inputs))]
+    specs += [pl.BlockSpec(memory_space=pl.ANY)] * len(after)
     moved = sum(x.size * x.dtype.itemsize for x in inputs) + sum(
         x.size * x.dtype.itemsize for x in jax.tree.leaves(outs)
     )
+    out_space = lambda x: pl.ANY if in_place and x.dtype == BF16 else pltpu.VMEM
     return pl.pallas_call(
-        kernel,
+        body,
         out_shape=outs,
         in_specs=specs,
-        out_specs=jax.tree.map(lambda _: pl.BlockSpec(memory_space=pltpu.VMEM), outs),
+        out_specs=jax.tree.map(lambda x: pl.BlockSpec(memory_space=out_space(x)), outs),
         scratch_shapes=list(scratch),
         compiler_params=pltpu.CompilerParams(vmem_limit_bytes=vmem * 2**20),
         cost_estimate=pl.CostEstimate(flops=flops, bytes_accessed=moved, transcendentals=0),
         name=name,
-    )(*inputs)
+    )(*inputs, *after)
 
 
 def exchange(parts, sizes):
@@ -486,14 +541,26 @@
     return [parts[0]] + [shift(parts[ahead], axis, ahead) for ahead in range(1, len(parts))]
 
 
-def fold_subs(me, by_sub, name):
+def fold_subs(me, by_sub, name, after=()):
     seqs, piece, columns = by_sub[0].shape
     return call(
         fold_subs_kernel,
         (jax.ShapeDtypeStruct((piece, columns), BF16),) * seqs,
         (me, *pass_round(by_sub, "sub")),
+        after=after,
         name=name,
     )
+
+
+def exchange_by_chip(me, parts, sizes, name):
+    came = pass_round(parts, "seq")
+    swapped = call(
+        functools.partial(swap_kernel, sizes),
+        (jax.ShapeDtypeStruct((sizes[0], *parts[0].shape[1:]), BF16),) * (sizes[1] - 1),
+        (me, *came),
+        name=name,
+    )
+    return came + [shift(part, "sub", k + 1) for k, part in enumerate(swapped)]
 
 
 def add_up(terms, dtype, name):
@@ -529,20 +596,31 @@
         functools.partial(project_query_kernel, sizes, groups, rows),
         several(owners, rows + COUNT_ROWS, LANES) + (shape((1, toks), jnp.int32),),
         (me, assignment.reshape(1, toks), tokens_in, w_query, cotangent),
-        scratch=[pltpu.VMEM((toks, 2 * width_dev), BF16), pltpu.VMEM((owners, rows + COUNT_ROWS, LANES), BF16)],
+        in_place=(2, 3, 4),
+        scratch=[
+            pltpu.VMEM((toks, width), BF16),
+            pltpu.VMEM((width, width_dev), BF16),
+            pltpu.VMEM((toks, width_dev), BF16),
+            pltpu.VMEM((toks, 2 * width_dev), BF16),
+            pltpu.VMEM((owners, rows + COUNT_ROWS, LANES), BF16),
+            pltpu.SemaphoreType.DMA((1 + 2 * (toks // min(512, toks)),)),
+            pltpu.SemaphoreType.DMA((owners,)),
+        ],
+        vmem=60,
         flops=2 * toks * width * width_dev + 4 * slots * toks * width_dev,
         name="project_query",
     )
     got_mixed = exchange(send_mixed, sizes)
     *send_value, turned, unsort = call(
         functools.partial(project_value_kernel, sizes, groups, rows),
-        several(owners, half, LANES) + several(1, width, toks) + several(1, toks, slots),
+        several(sizes[0], sizes[1], half, LANES) + several(1, width, toks) + several(1, toks, slots),
         (me, slot_row, tokens_in, w_value),
         scratch=[pltpu.VMEM((toks, width_dev), BF16), pltpu.VMEM((owners, half, LANES), BF16)],
         flops=2 * toks * width * width_dev + 2 * slots * toks * width_dev,
         name="project_value",
     )
-    got_value = exchange(send_value, sizes)
+    send_value, _ = lax.optimization_barrier((send_value, got_mixed[1:4]))
+    got_value = exchange_by_chip(me, send_value, sizes, "swap_value")
     blocks = per_group * capacity // BLOCK_ROWS
     held = blocks + (LEAD + 4) * UNROLL
     block_flops = 2 * BLOCK_ROWS * BLOCK_ROWS * LANES
@@ -553,7 +631,7 @@
     place = pltpu.SMEM((owners,), jnp.int32)
     *back_value, dense, counts = call(
         functools.partial(value_grad_kernel, sizes, per_group, slot_rows),
-        several(owners, half, LANES)
+        several(sizes[0], sizes[1], half, LANES)
         + several(1, held * BLOCK_ROWS, LANES)
         + (shape((owners, LANES), jnp.int32),),
         (me, *got_mixed),
@@ -564,7 +642,7 @@
         vmem=48,
         name="value_grad",
     )
-    home_value = exchange(back_value, sizes)
+    home_value = exchange_by_chip(me, back_value, sizes, "swap_value_grad")
     back_query = call(
         functools.partial(query_grad_kernel, sizes, per_group, slot_rows),
         several(owners, half + extra, LANES),
@@ -594,29 +672,31 @@
     value_weight = fold_subs(me, value_weight, "value_subs")
     *partials, query_rows, centroid_grad = call(
         functools.partial(query_home_kernel, sizes, heads, (CLUSTERS / (toks * owners)) ** 0.5, parts),
-        several(parts, toks, columns)
+        several(parts - 1, toks, columns)
         + several(1, toks, width_dev)
         + (shape((groups * 2 * extra, width_dev), F32),),
         (me, unsort, value_rows, w_query, w_value, *home_query),
+        after=value_weight,
         scratch=[pltpu.VMEM((owners, half + extra, LANES), BF16), sorted_rows],
-        flops=2 * weight_flops + home_flops,
+        flops=weight_flops + home_flops,
         name="query_home",
     )
-    arrived = pass_round(partials, "head")
+    arrived = [shift(partial, "head", k + 1) for k, partial in enumerate(partials)]
     value_weight, _ = lax.optimization_barrier((value_weight, home_query))
     value_weight = pass_round(value_weight, "seq")
-    query_weight = call(
-        functools.partial(query_weight_kernel, sizes),
-        sub_shapes,
-        (me, turned, query_rows),
+    *query_weight, own = call(
+        functools.partial(query_weight_kernel, sizes, parts),
+        sub_shapes + several(1, toks, columns),
+        (me, turned, query_rows, value_rows, w_query, w_value),
+        after=value_weight[1:2],
         scratch=[whole],
-        flops=weight_flops,
+        flops=2 * weight_flops,
         name="query_weight",
     )
-    query_weight = pass_round(fold_subs(me, query_weight, "query_subs"), "seq")
+    query_weight = pass_round(fold_subs(me, query_weight, "query_subs", value_weight[2:]), "seq")
     grad_wv = add_up(value_weight, F32, "value_sum")
     grad_wq = add_up(query_weight, F32, "query_sum")
-    grad_input = add_up(arrived, BF16, "input_sum")
+    grad_input = add_up([own] + arrived, BF16, "input_sum")
     if groups > 1:
         centroid_grad = centroid_grad.reshape(groups, 2 * extra, width_dev)[:, :per_group]
         centroid_grad = centroid_grad.reshape(CLUSTERS, width_dev)

time: 183 us -> 221 us (1.21)
  waiting for transfers between devices: 52.2 us -> 97.3 us
  starting transfers between devices: 68.9 us -> 61 us
  Pallas kernels: 54.5 us -> 60.1 us
  local copies, waits for them, and re-layouts: 4.74 us -> 0.97 us
    ppermute x9 -> x17, waiting for transfers between devices: 7.96 us -> 51.4 us  [shift(): lax.ppermute(part, axis, [(i, (i + ahead) % size) for i in range(size)])]
    ppermute x28 -> x14, starting transfers between devices: 49.6 us -> 20.5 us  [exchange(): out.append(part if ahead == (0, 0) else lax.ppermute(part, OWNERS, moves))]
    ppermute x9 -> x17, starting transfers between devices: 19.3 us -> 40.6 us  [shift(): lax.ppermute(part, axis, [(i, (i + ahead) % size) for i in range(size)])]
    pallas_call x12 -> x14, Pallas kernels: 54.5 us -> 60.1 us  [call(): pl.pallas_call(body, out_shape=outs, in_specs=specs, out_specs=jax.tree.m...]
    unnamed x14 -> x12, local copies, waits for them, and re-layouts: 4.74 us -> 0.97 us
    ppermute x28 -> x14, waiting for transfers between devices: 44.2 us -> 45.9 us  [exchange(): out.append(part if ahead == (0, 0) else lax.ppermute(part, OWNERS, moves))]
  transfers between devices with their start and end apart: 37 -> 31, of which waited for: 10 -> 15; matrix products, arithmetic and copies ran while one was open for 0% -> 0% of each run, Pallas kernels for 23% -> 15%
where the time goes in v5:
time: 221 us
  waiting for transfers between devices  97.3 us (44%)
  starting transfers between devices  61 us (28%)
  Pallas kernels  60.1 us (27%)
    pallas_call x14, Pallas kernels, call(): pl.pallas_call(body, out_shape=outs, in_specs=specs, out_specs=jax.tree.m...  60.1 us
    ppermute x17, waiting for transfers between devices, shift(): lax.ppermute(part, axis, [(i, (i + ahead) % size) for i in range(size)])  51.4 us
    ppermute x14, waiting for transfers between devices, exchange(): out.append(part if ahead == (0, 0) else lax.ppermute(part, OWNERS, moves))  45.9 us
    ppermute x17, starting transfers between devices, shift(): lax.ppermute(part, axis, [(i, (i + ahead) % size) for i in range(size)])  40.6 us
    ppermute x14, starting transfers between devices, exchange(): out.append(part if ahead == (0, 0) else lax.ppermute(part, OWNERS, moves))  20.5 us
  transfers between devices with their start and end apart: 31, of which 15 were waited for; matrix products, arithmetic and copies ran while one was open for 0% of the time, Pallas kernels for 15%

profile of v5, /device:TPU:0, one launch (start us, length us, event | category | flops | bytes accessed | tf_op | source)
XLA Modules:
  0.0 220.9 jit_solution(11222506147953085744)
XLA Ops:
  1.3 8.6 %project_query.1 = (bf16[1040,128]{1,0:T(8,128)(2,1)}, bf16[1040,128]{1,0:T(8,128)(2,1)}, bf16[1040,128]{1,0:T(8,128)(2,1)}, bf16[1040,128]{1,0:T(8,128)(2,1)}, ...) custom-call(s32[4]{0:T(128)} %pad_add_fusion.refs_0_, ...), custom_call_target="tpu_custom_call" | custom-call | flops 3221225472 | bytes 6332432 | tf_op jit(solution)/shard_map/project_query/pallas_call | solution.py:509
  10.5 2.6 %collective-permute-start.1 = (bf16[1040,128]{1,0:T(8,128)(2,1)}, bf16[1040,128]{1,0:T(8,128)(2,1)S(1)}, u32[]{:S(2)}, u32[]{:S(2)}) collective-permute-start(bf16[1040,128]{1,0:T(8,128)(2,1)} %get-tuple-element.63), channel_id=1, source_target_pairs={{0,4},{1,5},{4,8},{5,9},{8,12},{9,13},{12,0},{13,1},{2,6},{3,7},{6... | collective-permute-start | bytes 798728 | tf_op jit(solution)/shard_map/ppermute | solution.py:531
  13.1 1.4 collective-permute-start.2
  14.5 1.3 collective-permute-start.3
  15.8 1.3 collective-permute-start.4
  17.1 2.2 %collective-permute-start.5 = (bf16[1040,128]{1,0:T(8,128)(2,1)}, bf16[1040,128]{1,0:T(8,128)(2,1)S(1)}, u32[]{:S(2)}, u32[]{:S(2)}) collective-permute-start(bf16[1040,128]{1,0:T(8,128)(2,1)} %get-tuple-element.67), channel_id=1, source_target_pairs={{0,12},{1,13},{4,0},{5,1},{8,4},{9,5},{12,8},{13,9},{2,14},{3,15},... | collective-permute-start | bytes 798728 | tf_op jit(solution)/shard_map/ppermute | solution.py:531
  19.3 3.5 %collective-permute-done.1.refs_3_ = bf16[1040,128]{1,0:T(8,128)(2,1)S(1)} collective-permute-done((bf16[1040,128]{1,0:T(8,128)(2,1)}, bf16[1040,128]{1,0:T(8,128)(2,1)S(1)}, u32[]{:S(2)}, u32[]{:S(2)}) %collective-permute-start.1) | collective-permute-done | bytes 266272 | tf_op jit(solution)/shard_map/ppermute | solution.py:531
  23.4 4.6 %collective-permute-done.2.refs_4_ = bf16[1040,128]{1,0:T(8,128)(2,1)S(1)} collective-permute-done((bf16[1040,128]{1,0:T(8,128)(2,1)}, bf16[1040,128]{1,0:T(8,128)(2,1)S(1)}, u32[]{:S(2)}, u32[]{:S(2)}) %collective-permute-start.2) | collective-permute-done | bytes 266272 | tf_op jit(solution)/shard_map/ppermute | solution.py:531
  28.0 17.3 %collective-permute-done.3.refs_5_ = bf16[1040,128]{1,0:T(8,128)(2,1)S(1)} collective-permute-done((bf16[1040,128]{1,0:T(8,128)(2,1)}, bf16[1040,128]{1,0:T(8,128)(2,1)S(1)}, u32[]{:S(2)}, u32[]{:S(2)}) %collective-permute-start.3) | collective-permute-done | bytes 266272 | tf_op jit(solution)/shard_map/ppermute | solution.py:531
  45.3 5.6 %collective-permute-done.4.refs_6_ = bf16[1040,128]{1,0:T(8,128)(2,1)S(1)} collective-permute-done((bf16[1040,128]{1,0:T(8,128)(2,1)}, bf16[1040,128]{1,0:T(8,128)(2,1)S(1)}, u32[]{:S(2)}, u32[]{:S(2)}) %collective-permute-start.4) | collective-permute-done | bytes 266272 | tf_op jit(solution)/shard_map/ppermute | solution.py:531
  50.9 0.9 copy-done.4
  51.9 13.5 %value_grad.1 = (bf16[2,512,128]{2,1,0:T(8,128)(2,1)S(1)}, bf16[2,512,128]{2,1,0:T(8,128)(2,1)S(1)}, bf16[2,512,128]{2,1,0:T(8,128)(2,1)S(1)}, bf16[2,512,128]{2...) custom-call(s32[4]{0:T(128)S(1)} %copy-done, bf16[1040,128]{1,0:T(8,128)(2,1)S(1)} %copy-done.4, ...), custom_call_target="tpu_custom_call" | custom-call | flops 2147483648 | bytes 8163344 | tf_op jit(solution)/shard_map/value_grad/pallas_call | solution.py:509
  65.3 12.0 %collective-permute-start.7 = (bf16[2,512,128]{2,1,0:T(8,128)(2,1)S(1)}, bf16[2,512,128]{2,1,0:T(8,128)(2,1)S(1)}, u32[]{:S(2)}, u32[]{:S(2)}) collective-permute-start(bf16[2,512,128]{2,1,0:T(8,128)(2,1)S(1)} %get-tuple-element.70), channel_id=1, source_target_pairs={{0,4},{4,8},{8,12},{12,0},{1,5},{5,9},{9,13},{13,1},{2,6},{6,10},{... | collective-permute-start | bytes 786440 | tf_op jit(solution)/shard_map/ppermute | solution.py:537
  77.3 1.2 collective-permute-start.8
  78.5 1.2 collective-permute-start.9
  79.7 5.5 %collective-permute-done.7.refs_2_.refs_4_ = bf16[2,512,128]{2,1,0:T(8,128)(2,1)S(1)} collective-permute-done((bf16[2,512,128]{2,1,0:T(8,128)(2,1)S(1)}, bf16[2,512,128]{2,1,0:T(8,128)(2,1)S(1)}, u32[]{:S(2)}, u32[]{:S(2)}) %collective-permute-start.7) | collective-permute-done | bytes 262176 | tf_op jit(solution)/shard_map/ppermute | solution.py:537
  85.1 10.9 %collective-permute-done.8.refs_3_.refs_5_ = bf16[2,512,128]{2,1,0:T(8,128)(2,1)S(1)} collective-permute-done((bf16[2,512,128]{2,1,0:T(8,128)(2,1)S(1)}, bf16[2,512,128]{2,1,0:T(8,128)(2,1)S(1)}, u32[]{:S(2)}, u32[]{:S(2)}) %collective-permute-start.8) | collective-permute-done | bytes 262176 | tf_op jit(solution)/shard_map/ppermute | solution.py:537
  96.7 4.8 %project_value.1 = (bf16[2,512,128]{2,1,0:T(8,128)(2,1)S(1)}, bf16[2,512,128]{2,1,0:T(8,128)(2,1)S(1)}, bf16[2,512,128]{2,1,0:T(8,128)(2,1)S(1)}, bf16[2,512,128...) custom-call(s32[4]{0:T(128)S(1)} %copy-done, s32[1,1024]{1,0:T(1,128)S(1)} %copy-done.5, ...), custom_call_target="tpu_custom_call" | custom-call | flops 2147483648 | bytes 8392720 | tf_op jit(solution)/shard_map/project_value/pallas_call | solution.py:509
  101.6 6.1 %collective-permute-start.11 = (bf16[2,512,128]{2,1,0:T(8,128)(2,1)S(1)}, bf16[2,512,128]{2,1,0:T(8,128)(2,1)S(1)}, u32[]{:S(2)}, u32[]{:S(2)}) collective-permute-start(bf16[2,512,128]{2,1,0:T(8,128)(2,1)S(1)} %get-tuple-element.81), channel_id=1, source_target_pairs={{0,4},{4,8},{8,12},{12,0},{1,5},{5,9},{9,13},{13,1},{2,6},{6,10},{... | collective-permute-start | bytes 786440 | tf_op jit(solution)/shard_map/ppermute | solution.py:537
  107.7 1.5 collective-permute-start.12
  109.2 0.9 collective-permute-start.13
  110.1 5.8 %collective-permute-done.11.refs_2_.refs_4_ = bf16[2,512,128]{2,1,0:T(8,128)(2,1)S(1)} collective-permute-done((bf16[2,512,128]{2,1,0:T(8,128)(2,1)S(1)}, bf16[2,512,128]{2,1,0:T(8,128)(2,1)S(1)}, u32[]{:S(2)}, u32[]{:S(2)}) %collective-permute-start.11) | collective-permute-done | bytes 262176 | tf_op jit(solution)/shard_map/ppermute | solution.py:537
  116.0 11.0 %collective-permute-done.12.refs_3_.refs_5_ = bf16[2,512,128]{2,1,0:T(8,128)(2,1)S(1)} collective-permute-done((bf16[2,512,128]{2,1,0:T(8,128)(2,1)S(1)}, bf16[2,512,128]{2,1,0:T(8,128)(2,1)S(1)}, u32[]{:S(2)}, u32[]{:S(2)}) %collective-permute-start.12) | collective-permute-done | bytes 262176 | tf_op jit(solution)/shard_map/ppermute | solution.py:537
  127.6 3.9 %value_home.1 = (bf16[1024,512]{1,0:T(8,128)(2,1)S(1)}, bf16[4,128,512]{2,1,0:T(8,128)(2,1)S(1)}, bf16[4,128,512]{2,1,0:T(8,128)(2,1)S(1)}) custom-call(s32[4]{0:T(128)S(1)} %copy-done, bf16[1024,1024]{1,0:T(8,128)(2,1)S(1)} %get-tuple-element.59.refs_1_, bf16[1024,1024]{1,0:T(8,128)(2,1)S(1)} %get-tuple-element.60.refs_2_.refs_1_, ...), custom_call_target="tpu_custom_call" | custom-call | flops 2147483648 | bytes 7864336 | tf_op jit(solution)/shard_map/value_home/pallas_call | solution.py:509
  132.1 16.5 %query_grad.1 = (bf16[544,128]{1,0:T(8,128)(2,1)S(1)}, bf16[544,128]{1,0:T(8,128)(2,1)S(1)}, bf16[544,128]{1,0:T(8,128)(2,1)S(1)}, bf16[544,128]{1,0:T(8,128)(2,...) custom-call(s32[4]{0:T(128)S(1)} %copy-done, ...), custom_call_target="tpu_custom_call" | custom-call | flops 3221225472 | bytes 7671824 | tf_op jit(solution)/shard_map/query_grad/pallas_call | solution.py:509
  148.7 6.1 %collective-permute-start.16 = (bf16[544,128]{1,0:T(8,128)(2,1)S(1)}, bf16[544,128]{1,0:T(8,128)(2,1)S(1)}, u32[]{:S(2)}, u32[]{:S(2)}) collective-permute-start(bf16[544,128]{1,0:T(8,128)(2,1)S(1)} %get-tuple-element.86), channel_id=1, source_target_pairs={{0,4},{1,5},{4,8},{5,9},{8,12},{9,13},{12,0},{13,1},{2,6},{3,7},{6... | collective-permute-start | bytes 417800 | tf_op jit(solution)/shard_map/ppermute | solution.py:531
  155.0 1.4 collective-permute-start.18
  156.3 1.0 collective-permute-start.19
  157.3 3.0 %collective-permute-done.16.refs_7_ = bf16[544,128]{1,0:T(8,128)(2,1)S(1)} collective-permute-done((bf16[544,128]{1,0:T(8,128)(2,1)S(1)}, bf16[544,128]{1,0:T(8,128)(2,1)S(1)}, u32[]{:S(2)}, u32[]{:S(2)}) %collective-permute-start.16) | collective-permute-done | bytes 139296 | tf_op jit(solution)/shard_map/ppermute | solution.py:531
  160.3 1.8 collective-permute-start.20
  162.8 9.1 %collective-permute-done.18.refs_9_ = bf16[544,128]{1,0:T(8,128)(2,1)S(1)} collective-permute-done((bf16[544,128]{1,0:T(8,128)(2,1)S(1)}, bf16[544,128]{1,0:T(8,128)(2,1)S(1)}, u32[]{:S(2)}, u32[]{:S(2)}) %collective-permute-start.18) | collective-permute-done | bytes 139296 | tf_op jit(solution)/shard_map/ppermute | solution.py:531
  172.0 2.8 %collective-permute-done.19.refs_10_ = bf16[544,128]{1,0:T(8,128)(2,1)S(1)} collective-permute-done((bf16[544,128]{1,0:T(8,128)(2,1)S(1)}, bf16[544,128]{1,0:T(8,128)(2,1)S(1)}, u32[]{:S(2)}, u32[]{:S(2)}) %collective-permute-start.19) | collective-permute-done | bytes 139296 | tf_op jit(solution)/shard_map/ppermute | solution.py:531
  174.8 4.0 %query_home.1 = (bf16[1024,512]{1,0:T(8,128)(2,1)S(1)}, bf16[1024,512]{1,0:T(8,128)(2,1)S(1)}, f32[64,512]{1,0:T(8,128)}) custom-call(s32[4]{0:T(128)S(1)} %copy-done, bf16[1024,1024]{1,0:T(8,128)(2,1)S(1)} %get-tuple-element.60.refs_2_.refs_1_, bf16[1024,512]{1,0:T(8,128)(2,1)S(1)} %get-tuple-element.73.refs_2_.refs_3_, bf16[1024,512]{1,0:T(8,128)(2,1)S(1)} %copy-done.2, ...), custom_call_target="tpu_custom_call" | custom-call | flops 2147483648 | bytes 8585232 | tf_op jit(solution)/shard_map/query_home/pallas_call | solution.py:509
  178.8 1.5 collective-permute-start.24
  180.3 6.5 %collective-permute-start.23 = (bf16[128,512]{1,0:T(8,128)(2,1)S(1)}, bf16[128,512]{1,0:T(8,128)(2,1)S(1)}, u32[]{:S(2)}, u32[]{:S(2)}) collective-permute-start(bf16[128,512]{1,0:T(8,128)(2,1)S(1)} %get-tuple-element.99.refs_14_), channel_id=1, source_target_pairs={{0,4},{4,8},{8,12},{12,0},{1,5},{5,9},{9,13},{13,1},{2,6},{6,10},{... | collective-permute-start | bytes 393224 | tf_op jit(solution)/shard_map/ppermute | solution.py:537
  186.8 4.3 %collective-permute-done.23.refs_6_.refs_1_ = bf16[128,512]{1,0:T(8,128)(2,1)S(1)} collective-permute-done((bf16[128,512]{1,0:T(8,128)(2,1)S(1)}, bf16[128,512]{1,0:T(8,128)(2,1)S(1)}, u32[]{:S(2)}, u32[]{:S(2)}) %collective-permute-start.23) | collective-permute-done | bytes 131104 | tf_op jit(solution)/shard_map/ppermute | solution.py:537
  191.2 3.5 %query_weight.1 = (bf16[4,128,512]{2,1,0:T(8,128)(2,1)S(1)}, bf16[4,128,512]{2,1,0:T(8,128)(2,1)S(1)}, bf16[1024,512]{1,0:T(8,128)(2,1)S(1)}) custom-call(s32[4]{0:T(128)S(1)} %copy-done, bf16[1024,1024]{1,0:T(8,128)(2,1)S(1)} %get-tuple-element.59.refs_1_, bf16[1024,512]{1,0:T(8,128)(2,1)S(1)} %get-tuple-element.98.refs_2_, ...), custom_call_target="tpu_custom_call" | custom-call | flops 2147483648 | bytes 8388624 | tf_op jit(solution)/shard_map/query_weight/pallas_call | solution.py:509
  194.8 0.7 collective-permute-start.26
  195.5 2.6 %collective-permute-start.27 = (bf16[128,512]{1,0:T(8,128)(2,1)S(1)}, bf16[128,512]{1,0:T(8,128)(2,1)S(1)}, u32[]{:S(2)}, u32[]{:S(2)}) collective-permute-start(bf16[128,512]{1,0:T(8,128)(2,1)S(1)} %get-tuple-element.105.refs_16_), channel_id=1, source_target_pairs={{0,12},{4,0},{8,4},{12,8},{1,13},{5,1},{9,5},{13,9},{2,14},{6,2},{... | collective-permute-start | bytes 393224 | tf_op jit(solution)/shard_map/ppermute | solution.py:537
  198.1 6.7 %collective-permute-done.26.refs_3_.refs_2_ = bf16[128,512]{1,0:T(8,128)(2,1)S(1)} collective-permute-done((bf16[128,512]{1,0:T(8,128)(2,1)S(1)}, bf16[128,512]{1,0:T(8,128)(2,1)S(1)}, u32[]{:S(2)}, u32[]{:S(2)}) %collective-permute-start.26) | collective-permute-done | bytes 131104 | tf_op jit(solution)/shard_map/ppermute | solution.py:537
  205.4 3.1 %collective-permute-start.28 = (bf16[128,512]{1,0:T(8,128)(2,1)S(1)}, bf16[128,512]{1,0:T(8,128)(2,1)S(1)}, u32[]{:S(2)}, u32[]{:S(2)}) collective-permute-start(bf16[128,512]{1,0:T(8,128)(2,1)S(1)} %get-tuple-element.107), channel_id=1, source_target_pairs={{0,4},{4,8},{8,12},{12,0},{1,5},{5,9},{9,13},{13,1},{2,6},{6,10},{... | collective-permute-start | bytes 393224 | tf_op jit(solution)/shard_map/ppermute | solution.py:537
  208.5 1.5 collective-permute-start.29
  210.0 0.9 collective-permute-start.30
  210.9 0.8 value_sum.1
  211.7 2.1 collective-permute-done.28.refs_1_
  213.8 5.0 %collective-permute-done.29.refs_2_ = bf16[128,512]{1,0:T(8,128)(2,1)S(1)} collective-permute-done((bf16[128,512]{1,0:T(8,128)(2,1)S(1)}, bf16[128,512]{1,0:T(8,128)(2,1)S(1)}, u32[]{:S(2)}, u32[]{:S(2)}) %collective-permute-start.29) | collective-permute-done | bytes 131104 | tf_op jit(solution)/shard_map/ppermute | solution.py:537
  218.9 0.8 query_sum.1
  219.7 1.2 input_sum.1
  (41 shorter events, 5.3 us)
Async XLA Ops:
  1.3 49.6 %copy-start = (s32[4]{0:T(128)S(1)}, s32[4]{0:T(128)}, u32[]{:S(2)}) copy-start(s32[4]{0:T(128)} %pad_add_fusion.refs_0_) | copy-start | bytes 52
  10.0 7.1 %collective-permute-start = (bf16[1040,128]{1,0:T(8,128)(2,1)}, bf16[1040,128]{1,0:T(8,128)(2,1)S(1)}, u32[]{:S(2)}, u32[]{:S(2)}) collective-permute-start(bf16[1040,128]{1,0:T(8,128)(2,1)} %get-tuple-element.62), channel_id=1, source_target_pairs={{0,1},{1,0},{4,5},{5,4},{8,9},{9,8},{12,13},{13,12},{2,3},{3,2},{6... | collective-permute-start | bytes 798728 | tf_op jit(solution)/shard_map/ppermute | solution.py:531
  10.5 12.3 %collective-permute-start.1 = (bf16[1040,128]{1,0:T(8,128)(2,1)}, bf16[1040,128]{1,0:T(8,128)(2,1)S(1)}, u32[]{:S(2)}, u32[]{:S(2)}) collective-permute-start(bf16[1040,128]{1,0:T(8,128)(2,1)} %get-tuple-element.63), channel_id=1, source_target_pairs={{0,4},{1,5},{4,8},{5,9},{8,12},{9,13},{12,0},{13,1},{2,6},{3,7},{6... | collective-permute-start | bytes 798728 | tf_op jit(solution)/shard_map/ppermute | solution.py:531
  13.1 14.9 %collective-permute-start.2 = (bf16[1040,128]{1,0:T(8,128)(2,1)}, bf16[1040,128]{1,0:T(8,128)(2,1)S(1)}, u32[]{:S(2)}, u32[]{:S(2)}) collective-permute-start(bf16[1040,128]{1,0:T(8,128)(2,1)} %get-tuple-element.64), channel_id=1, source_target_pairs={{0,5},{1,4},{4,9},{5,8},{8,13},{9,12},{12,1},{13,0},{2,7},{3,6},{6... | collective-permute-start | bytes 798728 | tf_op jit(solution)/shard_map/ppermute | solution.py:531
  14.5 30.8 %collective-permute-start.3 = (bf16[1040,128]{1,0:T(8,128)(2,1)}, bf16[1040,128]{1,0:T(8,128)(2,1)S(1)}, u32[]{:S(2)}, u32[]{:S(2)}) collective-permute-start(bf16[1040,128]{1,0:T(8,128)(2,1)} %get-tuple-element.65), channel_id=1, source_target_pairs={{0,8},{1,9},{4,12},{5,13},{8,0},{9,1},{12,4},{13,5},{2,10},{3,11},... | collective-permute-start | bytes 798728 | tf_op jit(solution)/shard_map/ppermute | solution.py:531
  15.8 35.1 %collective-permute-start.4 = (bf16[1040,128]{1,0:T(8,128)(2,1)}, bf16[1040,128]{1,0:T(8,128)(2,1)S(1)}, u32[]{:S(2)}, u32[]{:S(2)}) collective-permute-start(bf16[1040,128]{1,0:T(8,128)(2,1)} %get-tuple-element.66), channel_id=1, source_target_pairs={{0,9},{1,8},{4,13},{5,12},{8,1},{9,0},{12,5},{13,4},{2,11},{3,10},... | collective-permute-start | bytes 798728 | tf_op jit(solution)/shard_map/ppermute | solution.py:531
  17.1 33.8 %collective-permute-start.5 = (bf16[1040,128]{1,0:T(8,128)(2,1)}, bf16[1040,128]{1,0:T(8,128)(2,1)S(1)}, u32[]{:S(2)}, u32[]{:S(2)}) collective-permute-start(bf16[1040,128]{1,0:T(8,128)(2,1)} %get-tuple-element.67), channel_id=1, source_target_pairs={{0,12},{1,13},{4,0},{5,1},{8,4},{9,5},{12,8},{13,9},{2,14},{3,15},... | collective-permute-start | bytes 798728 | tf_op jit(solution)/shard_map/ppermute | solution.py:531
  22.8 28.1 %collective-permute-start.6 = (bf16[1040,128]{1,0:T(8,128)(2,1)}, bf16[1040,128]{1,0:T(8,128)(2,1)S(1)}, u32[]{:S(2)}, u32[]{:S(2)}) collective-permute-start(bf16[1040,128]{1,0:T(8,128)(2,1)} %get-tuple-element.68), channel_id=1, source_target_pairs={{0,13},{1,12},{4,1},{5,0},{8,5},{9,4},{12,9},{13,8},{2,15},{3,14},... | collective-permute-start | bytes 798728 | tf_op jit(solution)/shard_map/ppermute | solution.py:531
  50.9 1.0 copy-start.4
  51.9 44.9 %copy-start.1 = (bf16[1024,1024]{1,0:T(8,128)(2,1)S(1)}, bf16[1024,1024]{1,0:T(8,128)(2,1)}, u32[]{:S(2)}) copy-start(bf16[1024,1024]{1,0:T(8,128)(2,1)} %refs_2_.3) | copy-start | bytes 6291460
  51.9 44.9 %copy-start.3 = (bf16[1024,512]{1,0:T(8,128)(2,1)S(1)}, bf16[1024,512]{1,0:T(8,128)(2,1)}, u32[]{:S(2)}) copy-start(bf16[1024,512]{1,0:T(8,128)(2,1)} %refs_5_.1) | copy-start | bytes 3145732
  51.9 44.9 %copy-start.5 = (s32[1,1024]{1,0:T(1,128)S(1)}, s32[1,1024]{1,0:T(1,128)}, u32[]{:S(2)}) copy-start(s32[1,1024]{1,0:T(1,128)} %get-tuple-element.58.refs_1_) | copy-start | bytes 12292
  65.3 19.8 %collective-permute-start.7 = (bf16[2,512,128]{2,1,0:T(8,128)(2,1)S(1)}, bf16[2,512,128]{2,1,0:T(8,128)(2,1)S(1)}, u32[]{:S(2)}, u32[]{:S(2)}) collective-permute-start(bf16[2,512,128]{2,1,0:T(8,128)(2,1)S(1)} %get-tuple-element.70), channel_id=1, source_target_pairs={{0,4},{4,8},{8,12},{12,0},{1,5},{5,9},{9,13},{13,1},{2,6},{6,10},{... | collective-permute-start | bytes 786440 | tf_op jit(solution)/shard_map/ppermute | solution.py:537
  77.3 18.8 %collective-permute-start.8 = (bf16[2,512,128]{2,1,0:T(8,128)(2,1)S(1)}, bf16[2,512,128]{2,1,0:T(8,128)(2,1)S(1)}, u32[]{:S(2)}, u32[]{:S(2)}) collective-permute-start(bf16[2,512,128]{2,1,0:T(8,128)(2,1)S(1)} %get-tuple-element.71), channel_id=1, source_target_pairs={{0,8},{4,12},{8,0},{12,4},{1,9},{5,13},{9,1},{13,5},{2,10},{6,14},... | collective-permute-start | bytes 786440 | tf_op jit(solution)/shard_map/ppermute | solution.py:537
  78.5 17.6 %collective-permute-start.9 = (bf16[2,512,128]{2,1,0:T(8,128)(2,1)S(1)}, bf16[2,512,128]{2,1,0:T(8,128)(2,1)S(1)}, u32[]{:S(2)}, u32[]{:S(2)}) collective-permute-start(bf16[2,512,128]{2,1,0:T(8,128)(2,1)S(1)} %get-tuple-element.72), channel_id=1, source_target_pairs={{0,12},{4,0},{8,4},{12,8},{1,13},{5,1},{9,5},{13,9},{2,14},{6,2},{... | collective-permute-start | bytes 786440 | tf_op jit(solution)/shard_map/ppermute | solution.py:537
  96.6 31.0 %collective-permute-start.10 = (bf16[4,512,128]{2,1,0:T(8,128)(2,1)S(1)}, bf16[4,512,128]{2,1,0:T(8,128)(2,1)S(1)}, u32[]{:S(2)}, u32[]{:S(2)}) collective-permute-start(bf16[4,512,128]{2,1,0:T(8,128)(2,1)S(1)} %swap_value_grad.1), channel_id=1, source_target_pairs={{0,1},{1,0},{2,3},{3,2},{4,5},{5,4},{6,7},{7,6},{8,9},{9,8},{10,11... | collective-permute-start | bytes 1572872 | tf_op jit(solution)/shard_map/ppermute | solution.py:537
  101.6 14.4 %collective-permute-start.11 = (bf16[2,512,128]{2,1,0:T(8,128)(2,1)S(1)}, bf16[2,512,128]{2,1,0:T(8,128)(2,1)S(1)}, u32[]{:S(2)}, u32[]{:S(2)}) collective-permute-start(bf16[2,512,128]{2,1,0:T(8,128)(2,1)S(1)} %get-tuple-element.81), channel_id=1, source_target_pairs={{0,4},{4,8},{8,12},{12,0},{1,5},{5,9},{9,13},{13,1},{2,6},{6,10},{... | collective-permute-start | bytes 786440 | tf_op jit(solution)/shard_map/ppermute | solution.py:537
  107.7 19.3 %collective-permute-start.12 = (bf16[2,512,128]{2,1,0:T(8,128)(2,1)S(1)}, bf16[2,512,128]{2,1,0:T(8,128)(2,1)S(1)}, u32[]{:S(2)}, u32[]{:S(2)}) collective-permute-start(bf16[2,512,128]{2,1,0:T(8,128)(2,1)S(1)} %get-tuple-element.82), channel_id=1, source_target_pairs={{0,8},{4,12},{8,0},{12,4},{1,9},{5,13},{9,1},{13,5},{2,10},{6,14},... | collective-permute-start | bytes 786440 | tf_op jit(solution)/shard_map/ppermute | solution.py:537
  109.2 17.7 %collective-permute-start.13 = (bf16[2,512,128]{2,1,0:T(8,128)(2,1)S(1)}, bf16[2,512,128]{2,1,0:T(8,128)(2,1)S(1)}, u32[]{:S(2)}, u32[]{:S(2)}) collective-permute-start(bf16[2,512,128]{2,1,0:T(8,128)(2,1)S(1)} %get-tuple-element.83), channel_id=1, source_target_pairs={{0,12},{4,0},{8,4},{12,8},{1,13},{5,1},{9,5},{13,9},{2,14},{6,2},{... | collective-permute-start | bytes 786440 | tf_op jit(solution)/shard_map/ppermute | solution.py:537
  127.5 4.5 %collective-permute-start.14 = (bf16[4,512,128]{2,1,0:T(8,128)(2,1)S(1)}, bf16[4,512,128]{2,1,0:T(8,128)(2,1)S(1)}, u32[]{:S(2)}, u32[]{:S(2)}) collective-permute-start(bf16[4,512,128]{2,1,0:T(8,128)(2,1)S(1)} %swap_value.1), channel_id=1, source_target_pairs={{0,1},{1,0},{2,3},{3,2},{4,5},{5,4},{6,7},{7,6},{8,9},{9,8},{10,11... | collective-permute-start | bytes 1572872 | tf_op jit(solution)/shard_map/ppermute | solution.py:537
  131.5 30.6 %collective-permute-start.22 = (bf16[4,128,512]{2,1,0:T(8,128)(2,1)S(1)}, bf16[4,128,512]{2,1,0:T(8,128)(2,1)S(1)}, u32[]{:S(2)}, u32[]{:S(2)}) collective-permute-start(bf16[4,128,512]{2,1,0:T(8,128)(2,1)S(1)} %get-tuple-element.93), channel_id=1, source_target_pairs={{0,1},{1,0},{2,3},{3,2},{4,5},{5,4},{6,7},{7,6},{8,9},{9,8},{10,11... | collective-permute-start | bytes 1572872 | tf_op jit(solution)/shard_map/ppermute | solution.py:537
  132.1 42.7 %copy-start.2 = (bf16[1024,512]{1,0:T(8,128)(2,1)S(1)}, bf16[1024,512]{1,0:T(8,128)(2,1)}, u32[]{:S(2)}) copy-start(bf16[1024,512]{1,0:T(8,128)(2,1)} %refs_4_.5) | copy-start | bytes 3145732
  148.6 7.7 %collective-permute-start.15 = (bf16[544,128]{1,0:T(8,128)(2,1)S(1)}, bf16[544,128]{1,0:T(8,128)(2,1)S(1)}, u32[]{:S(2)}, u32[]{:S(2)}) collective-permute-start(bf16[544,128]{1,0:T(8,128)(2,1)S(1)} %get-tuple-element.85), channel_id=1, source_target_pairs={{0,1},{1,0},{4,5},{5,4},{8,9},{9,8},{12,13},{13,12},{2,3},{3,2},{6... | collective-permute-start | bytes 417800 | tf_op jit(solution)/shard_map/ppermute | solution.py:531
  148.7 11.6 %collective-permute-start.16 = (bf16[544,128]{1,0:T(8,128)(2,1)S(1)}, bf16[544,128]{1,0:T(8,128)(2,1)S(1)}, u32[]{:S(2)}, u32[]{:S(2)}) collective-permute-start(bf16[544,128]{1,0:T(8,128)(2,1)S(1)} %get-tuple-element.86), channel_id=1, source_target_pairs={{0,4},{1,5},{4,8},{5,9},{8,12},{9,13},{12,0},{13,1},{2,6},{3,7},{6... | collective-permute-start | bytes 417800 | tf_op jit(solution)/shard_map/ppermute | solution.py:531
  154.9 8.0 %collective-permute-start.17 = (bf16[544,128]{1,0:T(8,128)(2,1)S(1)}, bf16[544,128]{1,0:T(8,128)(2,1)S(1)}, u32[]{:S(2)}, u32[]{:S(2)}) collective-permute-start(bf16[544,128]{1,0:T(8,128)(2,1)S(1)} %get-tuple-element.87), channel_id=1, source_target_pairs={{0,5},{1,4},{4,9},{5,8},{8,13},{9,12},{12,1},{13,0},{2,7},{3,6},{6... | collective-permute-start | bytes 417800 | tf_op jit(solution)/shard_map/ppermute | solution.py:531
  155.0 17.0 %collective-permute-start.18 = (bf16[544,128]{1,0:T(8,128)(2,1)S(1)}, bf16[544,128]{1,0:T(8,128)(2,1)S(1)}, u32[]{:S(2)}, u32[]{:S(2)}) collective-permute-start(bf16[544,128]{1,0:T(8,128)(2,1)S(1)} %get-tuple-element.88), channel_id=1, source_target_pairs={{0,8},{1,9},{4,12},{5,13},{8,0},{9,1},{12,4},{13,5},{2,10},{3,11},... | collective-permute-start | bytes 417800 | tf_op jit(solution)/shard_map/ppermute | solution.py:531
  156.3 18.5 %collective-permute-start.19 = (bf16[544,128]{1,0:T(8,128)(2,1)S(1)}, bf16[544,128]{1,0:T(8,128)(2,1)S(1)}, u32[]{:S(2)}, u32[]{:S(2)}) collective-permute-start(bf16[544,128]{1,0:T(8,128)(2,1)S(1)} %get-tuple-element.89), channel_id=1, source_target_pairs={{0,9},{1,8},{4,13},{5,12},{8,1},{9,0},{12,5},{13,4},{2,11},{3,10},... | collective-permute-start | bytes 417800 | tf_op jit(solution)/shard_map/ppermute | solution.py:531
  160.3 14.5 %collective-permute-start.20 = (bf16[544,128]{1,0:T(8,128)(2,1)S(1)}, bf16[544,128]{1,0:T(8,128)(2,1)S(1)}, u32[]{:S(2)}, u32[]{:S(2)}) collective-permute-start(bf16[544,128]{1,0:T(8,128)(2,1)S(1)} %get-tuple-element.90), channel_id=1, source_target_pairs={{0,12},{1,13},{4,0},{5,1},{8,4},{9,5},{12,8},{13,9},{2,14},{3,15},... | collective-permute-start | bytes 417800 | tf_op jit(solution)/shard_map/ppermute | solution.py:531
  162.1 12.6 %collective-permute-start.21 = (bf16[544,128]{1,0:T(8,128)(2,1)S(1)}, bf16[544,128]{1,0:T(8,128)(2,1)S(1)}, u32[]{:S(2)}, u32[]{:S(2)}) collective-permute-start(bf16[544,128]{1,0:T(8,128)(2,1)S(1)} %get-tuple-element.91), channel_id=1, source_target_pairs={{0,13},{1,12},{4,1},{5,0},{8,5},{9,4},{12,9},{13,8},{2,15},{3,14},... | collective-permute-start | bytes 417800 | tf_op jit(solution)/shard_map/ppermute | solution.py:531
  178.8 40.9 %collective-permute-start.24 = (bf16[1024,512]{1,0:T(8,128)(2,1)S(1)}, bf16[1024,512]{1,0:T(8,128)(2,1)S(1)}, u32[]{:S(2)}, u32[]{:S(2)}) collective-permute-start(bf16[1024,512]{1,0:T(8,128)(2,1)S(1)} %get-tuple-element.101), channel_id=1, source_target_pairs={{0,2},{2,0},{1,3},{3,1},{4,6},{6,4},{5,7},{7,5},{8,10},{10,8},{9,1... | collective-permute-start | bytes 3145736 | tf_op jit(solution)/shard_map/ppermute | solution.py:537
  180.3 10.9 %collective-permute-start.23 = (bf16[128,512]{1,0:T(8,128)(2,1)S(1)}, bf16[128,512]{1,0:T(8,128)(2,1)S(1)}, u32[]{:S(2)}, u32[]{:S(2)}) collective-permute-start(bf16[128,512]{1,0:T(8,128)(2,1)S(1)} %get-tuple-element.99.refs_14_), channel_id=1, source_target_pairs={{0,4},{4,8},{8,12},{12,0},{1,5},{5,9},{9,13},{13,1},{2,6},{6,10},{... | collective-permute-start | bytes 393224 | tf_op jit(solution)/shard_map/ppermute | solution.py:537
  194.7 10.1 %collective-permute-start.25 = (bf16[4,128,512]{2,1,0:T(8,128)(2,1)S(1)}, bf16[4,128,512]{2,1,0:T(8,128)(2,1)S(1)}, u32[]{:S(2)}, u32[]{:S(2)}) collective-permute-start(bf16[4,128,512]{2,1,0:T(8,128)(2,1)S(1)} %get-tuple-element.103), channel_id=1, source_target_pairs={{0,1},{1,0},{2,3},{3,2},{4,5},{5,4},{6,7},{7,6},{8,9},{9,8},{10,11... | collective-permute-start | bytes 1572872 | tf_op jit(solution)/shard_map/ppermute | solution.py:537
  194.8 10.0 %collective-permute-start.26 = (bf16[128,512]{1,0:T(8,128)(2,1)S(1)}, bf16[128,512]{1,0:T(8,128)(2,1)S(1)}, u32[]{:S(2)}, u32[]{:S(2)}) collective-permute-start(bf16[128,512]{1,0:T(8,128)(2,1)S(1)} %get-tuple-element.104.refs_15_), channel_id=1, source_target_pairs={{0,8},{4,12},{8,0},{12,4},{1,9},{5,13},{9,1},{13,5},{2,10},{6,14},... | collective-permute-start | bytes 393224 | tf_op jit(solution)/shard_map/ppermute | solution.py:537
  195.5 9.3 %collective-permute-start.27 = (bf16[128,512]{1,0:T(8,128)(2,1)S(1)}, bf16[128,512]{1,0:T(8,128)(2,1)S(1)}, u32[]{:S(2)}, u32[]{:S(2)}) collective-permute-start(bf16[128,512]{1,0:T(8,128)(2,1)S(1)} %get-tuple-element.105.refs_16_), channel_id=1, source_target_pairs={{0,12},{4,0},{8,4},{12,8},{1,13},{5,1},{9,5},{13,9},{2,14},{6,2},{... | collective-permute-start | bytes 393224 | tf_op jit(solution)/shard_map/ppermute | solution.py:537
  205.4 8.4 %collective-permute-start.28 = (bf16[128,512]{1,0:T(8,128)(2,1)S(1)}, bf16[128,512]{1,0:T(8,128)(2,1)S(1)}, u32[]{:S(2)}, u32[]{:S(2)}) collective-permute-start(bf16[128,512]{1,0:T(8,128)(2,1)S(1)} %get-tuple-element.107), channel_id=1, source_target_pairs={{0,4},{4,8},{8,12},{12,0},{1,5},{5,9},{9,13},{13,1},{2,6},{6,10},{... | collective-permute-start | bytes 393224 | tf_op jit(solution)/shard_map/ppermute | solution.py:537
  208.5 10.4 %collective-permute-start.29 = (bf16[128,512]{1,0:T(8,128)(2,1)S(1)}, bf16[128,512]{1,0:T(8,128)(2,1)S(1)}, u32[]{:S(2)}, u32[]{:S(2)}) collective-permute-start(bf16[128,512]{1,0:T(8,128)(2,1)S(1)} %get-tuple-element.108), channel_id=1, source_target_pairs={{0,8},{4,12},{8,0},{12,4},{1,9},{5,13},{9,1},{13,5},{2,10},{6,14},... | collective-permute-start | bytes 393224 | tf_op jit(solution)/shard_map/ppermute | solution.py:537
  210.0 8.9 %collective-permute-start.30 = (bf16[128,512]{1,0:T(8,128)(2,1)S(1)}, bf16[128,512]{1,0:T(8,128)(2,1)S(1)}, u32[]{:S(2)}, u32[]{:S(2)}) collective-permute-start(bf16[128,512]{1,0:T(8,128)(2,1)S(1)} %get-tuple-element.109), channel_id=1, source_target_pairs={{0,12},{4,0},{8,4},{12,8},{1,13},{5,1},{9,5},{13,9},{2,14},{6,2},{... | collective-permute-start | bytes 393224 | tf_op jit(solution)/shard_map/ppermute | solution.py:537

commit v6 on v5

--- a/solution.py
+++ b/solution.py
@@ -81,19 +81,20 @@
     slot_ref, tokens_ref, weight_ref, cotan_ref, mixed_ref, sorted_ref, in_sems, out_sems = rest
     toks = tokens_ref.shape[0]
     step = min(512, toks)
-    load_weight = pltpu.make_async_copy(weight_hbm, weight_ref, in_sems.at[0])
-    load_weight.start()
-
-    def load(i):
-        where = pl.ds(i * step, step)
-        return (
-            pltpu.make_async_copy(tokens_hbm.at[where, :], tokens_ref.at[where, :], in_sems.at[1 + 2 * i]),
-            pltpu.make_async_copy(cotan_hbm.at[where, :], cotan_ref.at[where, :], in_sems.at[2 + 2 * i]),
-        )
-
-    for i in range(toks // step):
-        for copy in load(i):
-            copy.start()
+    fine = min(128, toks)
+
+    def load(kind, first, last):
+        source, target = ((weight_hbm, weight_ref), (tokens_hbm, tokens_ref), (cotan_hbm, cotan_ref))[kind]
+        return [
+            pltpu.make_async_copy(
+                source.at[pl.ds(row, fine), :], target.at[pl.ds(row, fine), :], in_sems.at[kind, row // fine]
+            )
+            for row in range(first, last, fine)
+        ]
+
+    width = weight_ref.shape[0]
+    for copy in load(0, 0, width) + load(1, 0, toks) + load(2, 0, toks):
+        copy.start()
     per_group = CLUSTERS // groups
     heads = weight_ref.shape[1] // HD
     member = iota((CLUSTERS, toks), 0) == assign_ref[...]
@@ -114,9 +115,10 @@
     for owner in range(sorted_ref.shape[0]):
         sorted_ref[owner, rows:, :] = tallies
 
-    load_weight.wait()
+    for copy in load(0, 0, width):
+        copy.wait()
     for i in range(toks // step):
-        for copy in load(i):
+        for copy in load(1, i * step, (i + 1) * step) + load(2, i * step, (i + 1) * step):
             copy.wait()
         where = slice(i * step, (i + 1) * step)
         query = dot(tokens_ref[where, :], weight_ref[...])
@@ -552,12 +554,13 @@
     )
 
 
-def exchange_by_chip(me, parts, sizes, name):
+def exchange_by_chip(me, parts, sizes, name, after=()):
     came = pass_round(parts, "seq")
     swapped = call(
         functools.partial(swap_kernel, sizes),
         (jax.ShapeDtypeStruct((sizes[0], *parts[0].shape[1:]), BF16),) * (sizes[1] - 1),
         (me, *came),
+        after=after,
         name=name,
     )
     return came + [shift(part, "sub", k + 1) for k, part in enumerate(swapped)]
@@ -603,7 +606,7 @@
             pltpu.VMEM((toks, width_dev), BF16),
             pltpu.VMEM((toks, 2 * width_dev), BF16),
             pltpu.VMEM((owners, rows + COUNT_ROWS, LANES), BF16),
-            pltpu.SemaphoreType.DMA((1 + 2 * (toks // min(512, toks)),)),
+            pltpu.SemaphoreType.DMA((3, max(toks, width) // min(128, toks))),
             pltpu.SemaphoreType.DMA((owners,)),
         ],
         vmem=60,
@@ -620,7 +623,6 @@
         name="project_value",
     )
     send_value, _ = lax.optimization_barrier((send_value, got_mixed[1:4]))
-    got_value = exchange_by_chip(me, send_value, sizes, "swap_value")
     blocks = per_group * capacity // BLOCK_ROWS
     held = blocks + (LEAD + 4) * UNROLL
     block_flops = 2 * BLOCK_ROWS * BLOCK_ROWS * LANES
@@ -635,6 +637,7 @@
         + several(1, held * BLOCK_ROWS, LANES)
         + (shape((owners, LANES), jnp.int32),),
         (me, *got_mixed),
+        after=[unsort],
         scratch=[pltpu.SMEM((owners, LANES), jnp.int32), place, tall, dense_rows, tall]
         + [group_f32] * 2
         + [group_b16] * 2,
@@ -642,7 +645,7 @@
         vmem=48,
         name="value_grad",
     )
-    home_value = exchange_by_chip(me, back_value, sizes, "swap_value_grad")
+    got_value = exchange_by_chip(me, send_value, sizes, "swap_value", [dense])
     back_query = call(
         functools.partial(query_grad_kernel, sizes, per_group, slot_rows),
         several(owners, half + extra, LANES),
@@ -656,6 +659,7 @@
         name="query_grad",
     )
     home_query = exchange(back_query, sizes)
+    home_value = exchange_by_chip(me, back_value, sizes, "swap_value_grad", home_query[1:3])
     weight_flops = 2 * toks * width * width_dev
     home_flops = 2 * slots * toks * width_dev
     sub_shapes = several(sizes[1], sizes[0], width // owners, width_dev)
@@ -665,6 +669,7 @@
         functools.partial(value_home_kernel, sizes, heads),
         several(1, toks, width_dev) + sub_shapes,
         (me, turned, unsort, *home_value),
+        after=home_query[3:5],
         scratch=[pltpu.VMEM((owners, half, LANES), BF16), sorted_rows, whole],
         flops=weight_flops + home_flops,
         name="value_home",
@@ -688,12 +693,11 @@
         functools.partial(query_weight_kernel, sizes, parts),
         sub_shapes + several(1, toks, columns),
         (me, turned, query_rows, value_rows, w_query, w_value),
-        after=value_weight[1:2],
         scratch=[whole],
         flops=2 * weight_flops,
         name="query_weight",
     )
-    query_weight = pass_round(fold_subs(me, query_weight, "query_subs", value_weight[2:]), "seq")
+    query_weight = pass_round(fold_subs(me, query_weight, "query_subs", value_weight[1:]), "seq")
     grad_wv = add_up(value_weight, F32, "value_sum")
     grad_wq = add_up(query_weight, F32, "query_sum")
     grad_input = add_up([own] + arrived, BF16, "input_sum")

time: 221 us -> 188 us (0.85)
  waiting for transfers between devices: 97.3 us -> 45 us
  starting transfers between devices: 61 us -> 77.1 us
    ppermute x17, waiting for transfers between devices: 51.4 us -> 15.6 us  [shift(): lax.ppermute(part, axis, [(i, (i + ahead) % size) for i in range(size)])]
    ppermute x17, starting transfers between devices: 40.6 us -> 60.3 us  [shift(): lax.ppermute(part, axis, [(i, (i + ahead) % size) for i in range(size)])]
    ppermute x14, waiting for transfers between devices: 45.9 us -> 29.4 us  [exchange(): out.append(part if ahead == (0, 0) else lax.ppermute(part, OWNERS, moves))]
    ppermute x14, starting transfers between devices: 20.5 us -> 16.8 us  [exchange(): out.append(part if ahead == (0, 0) else lax.ppermute(part, OWNERS, moves))]
  transfers between devices with their start and end apart: 31 -> 31, of which waited for: 15 -> 13; matrix products, arithmetic and copies ran while one was open for 0% -> 0% of each run, Pallas kernels for 15% -> 22%
where the time goes in v6:
time: 188 us
  starting transfers between devices  77.1 us (41%)
  Pallas kernels  60.7 us (32%)
  waiting for transfers between devices  45 us (24%)
  local copies, waits for them, and re-layouts  3.11 us (2%)
    pallas_call x14, Pallas kernels, call(): pl.pallas_call(body, out_shape=outs, in_specs=specs, out_specs=jax.tree.m...  60.7 us
    ppermute x17, starting transfers between devices, shift(): lax.ppermute(part, axis, [(i, (i + ahead) % size) for i in range(size)])  60.3 us
    ppermute x14, waiting for transfers between devices, exchange(): out.append(part if ahead == (0, 0) else lax.ppermute(part, OWNERS, moves))  29.4 us
    ppermute x14, starting transfers between devices, exchange(): out.append(part if ahead == (0, 0) else lax.ppermute(part, OWNERS, moves))  16.8 us
    ppermute x17, waiting for transfers between devices, shift(): lax.ppermute(part, axis, [(i, (i + ahead) % size) for i in range(size)])  15.6 us
  transfers between devices with their start and end apart: 31, of which 13 were waited for; matrix products, arithmetic and copies ran while one was open for 0% of the time, Pallas kernels for 22%

profile of v6, /device:TPU:0, one launch (start us, length us, event | category | flops | bytes accessed | tf_op | source)
XLA Modules:
  0.0 187.5 jit_solution(18138722202950890681)
XLA Ops:
  0.6 0.7 pad_add_fusion.refs_0_
  1.3 9.4 %project_query.1 = (bf16[1040,128]{1,0:T(8,128)(2,1)}, bf16[1040,128]{1,0:T(8,128)(2,1)}, bf16[1040,128]{1,0:T(8,128)(2,1)}, bf16[1040,128]{1,0:T(8,128)(2,1)}, ...) custom-call(s32[4]{0:T(128)} %pad_add_fusion.refs_0_, ...), custom_call_target="tpu_custom_call" | custom-call | flops 3221225472 | bytes 6332432 | tf_op jit(solution)/shard_map/project_query/pallas_call | solution.py:511
  11.2 2.6 %collective-permute-start.1 = (bf16[1040,128]{1,0:T(8,128)(2,1)}, bf16[1040,128]{1,0:T(8,128)(2,1)S(1)}, u32[]{:S(2)}, u32[]{:S(2)}) collective-permute-start(bf16[1040,128]{1,0:T(8,128)(2,1)} %get-tuple-element.63), channel_id=1, source_target_pairs={{0,4},{1,5},{4,8},{5,9},{8,12},{9,13},{12,0},{13,1},{2,6},{3,7},{6... | collective-permute-start | bytes 798728 | tf_op jit(solution)/shard_map/ppermute | solution.py:533
  13.8 1.3 collective-permute-start.2
  15.2 1.3 collective-permute-start.3
  16.5 1.3 collective-permute-start.4
  17.8 2.2 %collective-permute-start.5 = (bf16[1040,128]{1,0:T(8,128)(2,1)}, bf16[1040,128]{1,0:T(8,128)(2,1)S(1)}, u32[]{:S(2)}, u32[]{:S(2)}) collective-permute-start(bf16[1040,128]{1,0:T(8,128)(2,1)} %get-tuple-element.67), channel_id=1, source_target_pairs={{0,12},{1,13},{4,0},{5,1},{8,4},{9,5},{12,8},{13,9},{2,14},{3,15},... | collective-permute-start | bytes 798728 | tf_op jit(solution)/shard_map/ppermute | solution.py:533
  20.0 3.5 %collective-permute-done.1.refs_3_ = bf16[1040,128]{1,0:T(8,128)(2,1)S(1)} collective-permute-done((bf16[1040,128]{1,0:T(8,128)(2,1)}, bf16[1040,128]{1,0:T(8,128)(2,1)S(1)}, u32[]{:S(2)}, u32[]{:S(2)}) %collective-permute-start.1) | collective-permute-done | bytes 266272 | tf_op jit(solution)/shard_map/ppermute | solution.py:533
  23.5 0.6 collective-permute-start.6
  24.1 0.7 copy-done.6
  24.8 4.8 %project_value.1 = (bf16[2,512,128]{2,1,0:T(8,128)(2,1)S(1)}, bf16[2,512,128]{2,1,0:T(8,128)(2,1)S(1)}, bf16[2,512,128]{2,1,0:T(8,128)(2,1)S(1)}, bf16[2,512,128...) custom-call(s32[4]{0:T(128)S(1)} %copy-done.1, s32[1,1024]{1,0:T(1,128)S(1)} %copy-done.6, ...), custom_call_target="tpu_custom_call" | custom-call | flops 2147483648 | bytes 8392720 | tf_op jit(solution)/shard_map/project_value/pallas_call | solution.py:511
  29.6 20.9 %collective-permute-start.10 = (bf16[2,512,128]{2,1,0:T(8,128)(2,1)S(1)}, bf16[2,512,128]{2,1,0:T(8,128)(2,1)S(1)}, u32[]{:S(2)}, u32[]{:S(2)}) collective-permute-start(bf16[2,512,128]{2,1,0:T(8,128)(2,1)S(1)} %get-tuple-element.80), channel_id=1, source_target_pairs={{0,4},{4,8},{8,12},{12,0},{1,5},{5,9},{9,13},{13,1},{2,6},{6,10},{... | collective-permute-start | bytes 786440 | tf_op jit(solution)/shard_map/ppermute | solution.py:539
  50.5 1.2 collective-permute-done.4.refs_6_
  51.7 18.1 %collective-permute-start.12 = (bf16[2,512,128]{2,1,0:T(8,128)(2,1)S(1)}, bf16[2,512,128]{2,1,0:T(8,128)(2,1)S(1)}, u32[]{:S(2)}, u32[]{:S(2)}) collective-permute-start(bf16[2,512,128]{2,1,0:T(8,128)(2,1)S(1)} %get-tuple-element.82), channel_id=1, source_target_pairs={{0,12},{4,0},{8,4},{12,8},{1,13},{5,1},{9,5},{13,9},{2,14},{6,2},{... | collective-permute-start | bytes 786440 | tf_op jit(solution)/shard_map/ppermute | solution.py:539
  69.8 13.5 %value_grad.1 = (bf16[2,512,128]{2,1,0:T(8,128)(2,1)S(1)}, bf16[2,512,128]{2,1,0:T(8,128)(2,1)S(1)}, bf16[2,512,128]{2,1,0:T(8,128)(2,1)S(1)}, bf16[2,512,128]{2...) custom-call(s32[4]{0:T(128)S(1)} %copy-done.1, bf16[1040,128]{1,0:T(8,128)(2,1)S(1)} %copy-done.5, ...), custom_call_target="tpu_custom_call" | custom-call | flops 2147483648 | bytes 8163344 | tf_op jit(solution)/shard_map/value_grad/pallas_call | solution.py:511
  83.3 2.4 %copy-done = bf16[19456,128]{1,0:T(8,128)(2,1)S(1)} copy-done((bf16[19456,128]{1,0:T(8,128)(2,1)S(1)}, bf16[19456,128]{1,0:T(8,128)(2,1)}, u32[]{:S(2)}) %copy-start) | copy-done | bytes 4980760
  85.7 0.6 swap_value.1
  86.8 4.6 %collective-permute-start.7 = (bf16[2,512,128]{2,1,0:T(8,128)(2,1)S(1)}, bf16[2,512,128]{2,1,0:T(8,128)(2,1)S(1)}, u32[]{:S(2)}, u32[]{:S(2)}) collective-permute-start(bf16[2,512,128]{2,1,0:T(8,128)(2,1)S(1)} %get-tuple-element.70), channel_id=1, source_target_pairs={{0,4},{4,8},{8,12},{12,0},{1,5},{5,9},{9,13},{13,1},{2,6},{6,10},{... | collective-permute-start | bytes 786440 | tf_op jit(solution)/shard_map/ppermute | solution.py:539
  91.4 2.4 %collective-permute-start.9 = (bf16[2,512,128]{2,1,0:T(8,128)(2,1)S(1)}, bf16[2,512,128]{2,1,0:T(8,128)(2,1)S(1)}, u32[]{:S(2)}, u32[]{:S(2)}) collective-permute-start(bf16[2,512,128]{2,1,0:T(8,128)(2,1)S(1)} %get-tuple-element.72), channel_id=1, source_target_pairs={{0,12},{4,0},{8,4},{12,8},{1,13},{5,1},{9,5},{13,9},{2,14},{6,2},{... | collective-permute-start | bytes 786440 | tf_op jit(solution)/shard_map/ppermute | solution.py:539
  93.9 16.5 %query_grad.1 = (bf16[544,128]{1,0:T(8,128)(2,1)S(1)}, bf16[544,128]{1,0:T(8,128)(2,1)S(1)}, bf16[544,128]{1,0:T(8,128)(2,1)S(1)}, bf16[544,128]{1,0:T(8,128)(2,...) custom-call(s32[4]{0:T(128)S(1)} %copy-done.1, ...), custom_call_target="tpu_custom_call" | custom-call | flops 3221225472 | bytes 7671824 | tf_op jit(solution)/shard_map/query_grad/pallas_call | solution.py:511
  110.5 1.2 collective-permute-done.14.refs_5_.refs_6_
  111.7 6.5 %collective-permute-done.15.refs_6_.refs_7_ = bf16[544,128]{1,0:T(8,128)(2,1)S(1)} collective-permute-done((bf16[544,128]{1,0:T(8,128)(2,1)S(1)}, bf16[544,128]{1,0:T(8,128)(2,1)S(1)}, u32[]{:S(2)}, u32[]{:S(2)}) %collective-permute-start.15) | collective-permute-done | bytes 139296 | tf_op jit(solution)/shard_map/ppermute | solution.py:533
  118.3 0.6 swap_value_grad.1
  119.0 2.8 %collective-permute-start.18 = (bf16[544,128]{1,0:T(8,128)(2,1)S(1)}, bf16[544,128]{1,0:T(8,128)(2,1)S(1)}, u32[]{:S(2)}, u32[]{:S(2)}) collective-permute-start(bf16[544,128]{1,0:T(8,128)(2,1)S(1)} %get-tuple-element.86), channel_id=1, source_target_pairs={{0,8},{1,9},{4,12},{5,13},{8,0},{9,1},{12,4},{13,5},{2,10},{3,11},... | collective-permute-start | bytes 417800 | tf_op jit(solution)/shard_map/ppermute | solution.py:533
  121.8 4.4 %collective-permute-done.17.refs_8_ = bf16[544,128]{1,0:T(8,128)(2,1)S(1)} collective-permute-done((bf16[544,128]{1,0:T(8,128)(2,1)S(1)}, bf16[544,128]{1,0:T(8,128)(2,1)S(1)}, u32[]{:S(2)}, u32[]{:S(2)}) %collective-permute-start.17) | collective-permute-done | bytes 139296 | tf_op jit(solution)/shard_map/ppermute | solution.py:533
  126.3 5.6 %collective-permute-done.18.refs_9_ = bf16[544,128]{1,0:T(8,128)(2,1)S(1)} collective-permute-done((bf16[544,128]{1,0:T(8,128)(2,1)S(1)}, bf16[544,128]{1,0:T(8,128)(2,1)S(1)}, u32[]{:S(2)}, u32[]{:S(2)}) %collective-permute-start.18) | collective-permute-done | bytes 139296 | tf_op jit(solution)/shard_map/ppermute | solution.py:533
  131.9 3.9 %value_home.1 = (bf16[1024,512]{1,0:T(8,128)(2,1)S(1)}, bf16[4,128,512]{2,1,0:T(8,128)(2,1)S(1)}, bf16[4,128,512]{2,1,0:T(8,128)(2,1)S(1)}) custom-call(s32[4]{0:T(128)S(1)} %copy-done.1, bf16[1024,1024]{1,0:T(8,128)(2,1)S(1)} %get-tuple-element.59.refs_1_, bf16[1024,1024]{1,0:T(8,128)(2,1)S(1)} %get-tuple-element.60.refs_9_.refs_2_.refs_1_, ...), custom_call_target="tpu_custom_call" | custom-call | flops 2147483648 | bytes 7864336 | tf_op jit(solution)/shard_map/value_home/pallas_call | solution.py:511
  135.9 1.4 collective-permute-start.20
  137.3 2.4 %collective-permute-start.21 = (bf16[544,128]{1,0:T(8,128)(2,1)S(1)}, bf16[544,128]{1,0:T(8,128)(2,1)S(1)}, u32[]{:S(2)}, u32[]{:S(2)}) collective-permute-start(bf16[544,128]{1,0:T(8,128)(2,1)S(1)} %get-tuple-element.91), channel_id=1, source_target_pairs={{0,13},{1,12},{4,1},{5,0},{8,5},{9,4},{12,9},{13,8},{2,15},{3,14},... | collective-permute-start | bytes 417800 | tf_op jit(solution)/shard_map/ppermute | solution.py:533
  139.8 0.7 value_subs.1
  140.4 4.1 %collective-permute-done.19.refs_10_ = bf16[544,128]{1,0:T(8,128)(2,1)S(1)} collective-permute-done((bf16[544,128]{1,0:T(8,128)(2,1)S(1)}, bf16[544,128]{1,0:T(8,128)(2,1)S(1)}, u32[]{:S(2)}, u32[]{:S(2)}) %collective-permute-start.19) | collective-permute-done | bytes 139296 | tf_op jit(solution)/shard_map/ppermute | solution.py:533
  144.5 0.9 collective-permute-done.20.refs_11_
  145.5 1.9 collective-permute-done.21.refs_12_
  147.4 4.0 %query_home.1 = (bf16[1024,512]{1,0:T(8,128)(2,1)S(1)}, bf16[1024,512]{1,0:T(8,128)(2,1)S(1)}, f32[64,512]{1,0:T(8,128)}) custom-call(s32[4]{0:T(128)S(1)} %copy-done.1, bf16[1024,1024]{1,0:T(8,128)(2,1)S(1)} %get-tuple-element.60.refs_9_.refs_2_.refs_1_, bf16[1024,512]{1,0:T(8,128)(2,1)S(1)} %get-tuple-element.87.refs_2_.refs_3_, ...), custom_call_target="tpu_custom_call" | custom-call | flops 2147483648 | bytes 8585232 | tf_op jit(solution)/shard_map/query_home/pallas_call | solution.py:511
  151.3 1.6 collective-permute-start.23
  152.9 3.5 %query_weight.1 = (bf16[4,128,512]{2,1,0:T(8,128)(2,1)S(1)}, bf16[4,128,512]{2,1,0:T(8,128)(2,1)S(1)}, bf16[1024,512]{1,0:T(8,128)(2,1)S(1)}) custom-call(s32[4]{0:T(128)S(1)} %copy-done.1, bf16[1024,1024]{1,0:T(8,128)(2,1)S(1)} %get-tuple-element.59.refs_1_, bf16[1024,512]{1,0:T(8,128)(2,1)S(1)} %get-tuple-element.98.refs_2_, ...), custom_call_target="tpu_custom_call" | custom-call | flops 2147483648 | bytes 8388624 | tf_op jit(solution)/shard_map/query_weight/pallas_call | solution.py:511
  156.6 3.6 %collective-permute-start.25 = (bf16[128,512]{1,0:T(8,128)(2,1)S(1)}, bf16[128,512]{1,0:T(8,128)(2,1)S(1)}, u32[]{:S(2)}, u32[]{:S(2)}) collective-permute-start(bf16[128,512]{1,0:T(8,128)(2,1)S(1)} %get-tuple-element.103.refs_14_), channel_id=1, source_target_pairs={{0,4},{4,8},{8,12},{12,0},{1,5},{5,9},{9,13},{13,1},{2,6},{6,10},{... | collective-permute-start | bytes 393224 | tf_op jit(solution)/shard_map/ppermute | solution.py:539
  160.2 2.5 %collective-permute-start.26 = (bf16[128,512]{1,0:T(8,128)(2,1)S(1)}, bf16[128,512]{1,0:T(8,128)(2,1)S(1)}, u32[]{:S(2)}, u32[]{:S(2)}) collective-permute-start(bf16[128,512]{1,0:T(8,128)(2,1)S(1)} %get-tuple-element.104.refs_15_), channel_id=1, source_target_pairs={{0,8},{4,12},{8,0},{12,4},{1,9},{5,13},{9,1},{13,5},{2,10},{6,14},... | collective-permute-start | bytes 393224 | tf_op jit(solution)/shard_map/ppermute | solution.py:539
  162.7 3.9 %collective-permute-done.25.refs_3_.refs_1_ = bf16[128,512]{1,0:T(8,128)(2,1)S(1)} collective-permute-done((bf16[128,512]{1,0:T(8,128)(2,1)S(1)}, bf16[128,512]{1,0:T(8,128)(2,1)S(1)}, u32[]{:S(2)}, u32[]{:S(2)}) %collective-permute-start.25) | collective-permute-done | bytes 131104 | tf_op jit(solution)/shard_map/ppermute | solution.py:539
  166.6 5.3 %collective-permute-done.26.refs_4_.refs_2_ = bf16[128,512]{1,0:T(8,128)(2,1)S(1)} collective-permute-done((bf16[128,512]{1,0:T(8,128)(2,1)S(1)}, bf16[128,512]{1,0:T(8,128)(2,1)S(1)}, u32[]{:S(2)}, u32[]{:S(2)}) %collective-permute-start.26) | collective-permute-done | bytes 131104 | tf_op jit(solution)/shard_map/ppermute | solution.py:539
  171.9 0.7 query_subs.1
  172.6 3.4 %collective-permute-start.28 = (bf16[128,512]{1,0:T(8,128)(2,1)S(1)}, bf16[128,512]{1,0:T(8,128)(2,1)S(1)}, u32[]{:S(2)}, u32[]{:S(2)}) collective-permute-start(bf16[128,512]{1,0:T(8,128)(2,1)S(1)} %get-tuple-element.107), channel_id=1, source_target_pairs={{0,4},{4,8},{8,12},{12,0},{1,5},{5,9},{9,13},{13,1},{2,6},{6,10},{... | collective-permute-start | bytes 393224 | tf_op jit(solution)/shard_map/ppermute | solution.py:539
  176.4 2.0 %collective-permute-start.30 = (bf16[128,512]{1,0:T(8,128)(2,1)S(1)}, bf16[128,512]{1,0:T(8,128)(2,1)S(1)}, u32[]{:S(2)}, u32[]{:S(2)}) collective-permute-start(bf16[128,512]{1,0:T(8,128)(2,1)S(1)} %get-tuple-element.109), channel_id=1, source_target_pairs={{0,12},{4,0},{8,4},{12,8},{1,13},{5,1},{9,5},{13,9},{2,14},{6,2},{... | collective-permute-start | bytes 393224 | tf_op jit(solution)/shard_map/ppermute | solution.py:539
  178.4 0.8 value_sum.1
  179.2 1.6 collective-permute-done.28.refs_1_
  180.7 4.8 %collective-permute-done.29.refs_2_ = bf16[128,512]{1,0:T(8,128)(2,1)S(1)} collective-permute-done((bf16[128,512]{1,0:T(8,128)(2,1)S(1)}, bf16[128,512]{1,0:T(8,128)(2,1)S(1)}, u32[]{:S(2)}, u32[]{:S(2)}) %collective-permute-start.29) | collective-permute-done | bytes 131104 | tf_op jit(solution)/shard_map/ppermute | solution.py:539
  185.5 0.8 query_sum.1
  186.3 1.2 input_sum.1
  (43 shorter events, 2.1 us)
Async XLA Ops:
  1.3 22.8 %copy-start.1 = (s32[4]{0:T(128)S(1)}, s32[4]{0:T(128)}, u32[]{:S(2)}) copy-start(s32[4]{0:T(128)} %pad_add_fusion.refs_0_) | copy-start | bytes 52
  1.3 22.8 %copy-start.2 = (bf16[1024,1024]{1,0:T(8,128)(2,1)S(1)}, bf16[1024,1024]{1,0:T(8,128)(2,1)}, u32[]{:S(2)}) copy-start(bf16[1024,1024]{1,0:T(8,128)(2,1)} %refs_2_.3) | copy-start | bytes 6291460
  1.3 22.8 %copy-start.4 = (bf16[1024,512]{1,0:T(8,128)(2,1)S(1)}, bf16[1024,512]{1,0:T(8,128)(2,1)}, u32[]{:S(2)}) copy-start(bf16[1024,512]{1,0:T(8,128)(2,1)} %refs_5_.1) | copy-start | bytes 3145732
  10.7 7.1 %collective-permute-start = (bf16[1040,128]{1,0:T(8,128)(2,1)}, bf16[1040,128]{1,0:T(8,128)(2,1)S(1)}, u32[]{:S(2)}, u32[]{:S(2)}) collective-permute-start(bf16[1040,128]{1,0:T(8,128)(2,1)} %get-tuple-element.62), channel_id=1, source_target_pairs={{0,1},{1,0},{4,5},{5,4},{8,9},{9,8},{12,13},{13,12},{2,3},{3,2},{6... | collective-permute-start | bytes 798728 | tf_op jit(solution)/shard_map/ppermute | solution.py:533
  11.2 12.3 %collective-permute-start.1 = (bf16[1040,128]{1,0:T(8,128)(2,1)}, bf16[1040,128]{1,0:T(8,128)(2,1)S(1)}, u32[]{:S(2)}, u32[]{:S(2)}) collective-permute-start(bf16[1040,128]{1,0:T(8,128)(2,1)} %get-tuple-element.63), channel_id=1, source_target_pairs={{0,4},{1,5},{4,8},{5,9},{8,12},{9,13},{12,0},{13,1},{2,6},{3,7},{6... | collective-permute-start | bytes 798728 | tf_op jit(solution)/shard_map/ppermute | solution.py:533
  13.8 15.8 %collective-permute-start.2 = (bf16[1040,128]{1,0:T(8,128)(2,1)}, bf16[1040,128]{1,0:T(8,128)(2,1)S(1)}, u32[]{:S(2)}, u32[]{:S(2)}) collective-permute-start(bf16[1040,128]{1,0:T(8,128)(2,1)} %get-tuple-element.64), channel_id=1, source_target_pairs={{0,5},{1,4},{4,9},{5,8},{8,13},{9,12},{12,1},{13,0},{2,7},{3,6},{6... | collective-permute-start | bytes 798728 | tf_op jit(solution)/shard_map/ppermute | solution.py:533
  15.2 35.4 %collective-permute-start.3 = (bf16[1040,128]{1,0:T(8,128)(2,1)}, bf16[1040,128]{1,0:T(8,128)(2,1)S(1)}, u32[]{:S(2)}, u32[]{:S(2)}) collective-permute-start(bf16[1040,128]{1,0:T(8,128)(2,1)} %get-tuple-element.65), channel_id=1, source_target_pairs={{0,8},{1,9},{4,12},{5,13},{8,0},{9,1},{12,4},{13,5},{2,10},{3,11},... | collective-permute-start | bytes 798728 | tf_op jit(solution)/shard_map/ppermute | solution.py:533
  16.5 35.2 %collective-permute-start.4 = (bf16[1040,128]{1,0:T(8,128)(2,1)}, bf16[1040,128]{1,0:T(8,128)(2,1)S(1)}, u32[]{:S(2)}, u32[]{:S(2)}) collective-permute-start(bf16[1040,128]{1,0:T(8,128)(2,1)} %get-tuple-element.66), channel_id=1, source_target_pairs={{0,9},{1,8},{4,13},{5,12},{8,1},{9,0},{12,5},{13,4},{2,11},{3,10},... | collective-permute-start | bytes 798728 | tf_op jit(solution)/shard_map/ppermute | solution.py:533
  17.8 52.1 %collective-permute-start.5 = (bf16[1040,128]{1,0:T(8,128)(2,1)}, bf16[1040,128]{1,0:T(8,128)(2,1)S(1)}, u32[]{:S(2)}, u32[]{:S(2)}) collective-permute-start(bf16[1040,128]{1,0:T(8,128)(2,1)} %get-tuple-element.67), channel_id=1, source_target_pairs={{0,12},{1,13},{4,0},{5,1},{8,4},{9,5},{12,8},{13,9},{2,14},{3,15},... | collective-permute-start | bytes 798728 | tf_op jit(solution)/shard_map/ppermute | solution.py:533
  23.5 46.3 %collective-permute-start.6 = (bf16[1040,128]{1,0:T(8,128)(2,1)}, bf16[1040,128]{1,0:T(8,128)(2,1)S(1)}, u32[]{:S(2)}, u32[]{:S(2)}) collective-permute-start(bf16[1040,128]{1,0:T(8,128)(2,1)} %get-tuple-element.68), channel_id=1, source_target_pairs={{0,13},{1,12},{4,1},{5,0},{8,5},{9,4},{12,9},{13,8},{2,15},{3,14},... | collective-permute-start | bytes 798728 | tf_op jit(solution)/shard_map/ppermute | solution.py:533
  24.1 0.7 copy-start.6
  24.8 45.1 %copy-start.5 = (bf16[1040,128]{1,0:T(8,128)(2,1)S(1)}, bf16[1040,128]{1,0:T(8,128)(2,1)}, u32[]{:S(2)}) copy-start(bf16[1040,128]{1,0:T(8,128)(2,1)} %get-tuple-element.61.refs_1_) | copy-start | bytes 798724
  29.6 53.7 %collective-permute-start.10 = (bf16[2,512,128]{2,1,0:T(8,128)(2,1)S(1)}, bf16[2,512,128]{2,1,0:T(8,128)(2,1)S(1)}, u32[]{:S(2)}, u32[]{:S(2)}) collective-permute-start(bf16[2,512,128]{2,1,0:T(8,128)(2,1)S(1)} %get-tuple-element.80), channel_id=1, source_target_pairs={{0,4},{4,8},{8,12},{12,0},{1,5},{5,9},{9,13},{13,1},{2,6},{6,10},{... | collective-permute-start | bytes 786440 | tf_op jit(solution)/shard_map/ppermute | solution.py:539
  50.5 32.8 %collective-permute-start.11 = (bf16[2,512,128]{2,1,0:T(8,128)(2,1)S(1)}, bf16[2,512,128]{2,1,0:T(8,128)(2,1)S(1)}, u32[]{:S(2)}, u32[]{:S(2)}) collective-permute-start(bf16[2,512,128]{2,1,0:T(8,128)(2,1)S(1)} %get-tuple-element.81), channel_id=1, source_target_pairs={{0,8},{4,12},{8,0},{12,4},{1,9},{5,13},{9,1},{13,5},{2,10},{6,14},... | collective-permute-start | bytes 786440 | tf_op jit(solution)/shard_map/ppermute | solution.py:539
  51.7 31.6 %collective-permute-start.12 = (bf16[2,512,128]{2,1,0:T(8,128)(2,1)S(1)}, bf16[2,512,128]{2,1,0:T(8,128)(2,1)S(1)}, u32[]{:S(2)}, u32[]{:S(2)}) collective-permute-start(bf16[2,512,128]{2,1,0:T(8,128)(2,1)S(1)} %get-tuple-element.82), channel_id=1, source_target_pairs={{0,12},{4,0},{8,4},{12,8},{1,13},{5,1},{9,5},{13,9},{2,14},{6,2},{... | collective-permute-start | bytes 786440 | tf_op jit(solution)/shard_map/ppermute | solution.py:539
  83.3 2.4 %copy-start = (bf16[19456,128]{1,0:T(8,128)(2,1)S(1)}, bf16[19456,128]{1,0:T(8,128)(2,1)}, u32[]{:S(2)}) copy-start(bf16[19456,128]{1,0:T(8,128)(2,1)} %get-tuple-element.74.refs_5_.refs_2_) | copy-start | bytes 14942212
  86.3 7.5 %collective-permute-start.13 = (bf16[4,512,128]{2,1,0:T(8,128)(2,1)S(1)}, bf16[4,512,128]{2,1,0:T(8,128)(2,1)S(1)}, u32[]{:S(2)}, u32[]{:S(2)}) collective-permute-start(bf16[4,512,128]{2,1,0:T(8,128)(2,1)S(1)} %swap_value.1), channel_id=1, source_target_pairs={{0,1},{1,0},{2,3},{3,2},{4,5},{5,4},{6,7},{7,6},{8,9},{9,8},{10,11... | collective-permute-start | bytes 1572872 | tf_op jit(solution)/shard_map/ppermute | solution.py:539
  86.8 23.6 %collective-permute-start.7 = (bf16[2,512,128]{2,1,0:T(8,128)(2,1)S(1)}, bf16[2,512,128]{2,1,0:T(8,128)(2,1)S(1)}, u32[]{:S(2)}, u32[]{:S(2)}) collective-permute-start(bf16[2,512,128]{2,1,0:T(8,128)(2,1)S(1)} %get-tuple-element.70), channel_id=1, source_target_pairs={{0,4},{4,8},{8,12},{12,0},{1,5},{5,9},{9,13},{13,1},{2,6},{6,10},{... | collective-permute-start | bytes 786440 | tf_op jit(solution)/shard_map/ppermute | solution.py:539
  91.4 19.0 %collective-permute-start.8 = (bf16[2,512,128]{2,1,0:T(8,128)(2,1)S(1)}, bf16[2,512,128]{2,1,0:T(8,128)(2,1)S(1)}, u32[]{:S(2)}, u32[]{:S(2)}) collective-permute-start(bf16[2,512,128]{2,1,0:T(8,128)(2,1)S(1)} %get-tuple-element.71), channel_id=1, source_target_pairs={{0,8},{4,12},{8,0},{12,4},{1,9},{5,13},{9,1},{13,5},{2,10},{6,14},... | collective-permute-start | bytes 786440 | tf_op jit(solution)/shard_map/ppermute | solution.py:539
  91.4 19.0 %collective-permute-start.9 = (bf16[2,512,128]{2,1,0:T(8,128)(2,1)S(1)}, bf16[2,512,128]{2,1,0:T(8,128)(2,1)S(1)}, u32[]{:S(2)}, u32[]{:S(2)}) collective-permute-start(bf16[2,512,128]{2,1,0:T(8,128)(2,1)S(1)} %get-tuple-element.72), channel_id=1, source_target_pairs={{0,12},{4,0},{8,4},{12,8},{1,13},{5,1},{9,5},{13,9},{2,14},{6,2},{... | collective-permute-start | bytes 786440 | tf_op jit(solution)/shard_map/ppermute | solution.py:539
  110.3 1.4 collective-permute-start.14
  110.4 7.9 %collective-permute-start.15 = (bf16[544,128]{1,0:T(8,128)(2,1)S(1)}, bf16[544,128]{1,0:T(8,128)(2,1)S(1)}, u32[]{:S(2)}, u32[]{:S(2)}) collective-permute-start(bf16[544,128]{1,0:T(8,128)(2,1)S(1)} %get-tuple-element.84), channel_id=1, source_target_pairs={{0,4},{1,5},{4,8},{5,9},{8,12},{9,13},{12,0},{13,1},{2,6},{3,7},{6... | collective-permute-start | bytes 417800 | tf_op jit(solution)/shard_map/ppermute | solution.py:533
  118.9 13.0 %collective-permute-start.16 = (bf16[4,512,128]{2,1,0:T(8,128)(2,1)S(1)}, bf16[4,512,128]{2,1,0:T(8,128)(2,1)S(1)}, u32[]{:S(2)}, u32[]{:S(2)}) collective-permute-start(bf16[4,512,128]{2,1,0:T(8,128)(2,1)S(1)} %swap_value_grad.1), channel_id=1, source_target_pairs={{0,1},{1,0},{2,3},{3,2},{4,5},{5,4},{6,7},{7,6},{8,9},{9,8},{10,11... | collective-permute-start | bytes 1572872 | tf_op jit(solution)/shard_map/ppermute | solution.py:539
  118.9 7.4 %collective-permute-start.17 = (bf16[544,128]{1,0:T(8,128)(2,1)S(1)}, bf16[544,128]{1,0:T(8,128)(2,1)S(1)}, u32[]{:S(2)}, u32[]{:S(2)}) collective-permute-start(bf16[544,128]{1,0:T(8,128)(2,1)S(1)} %get-tuple-element.85), channel_id=1, source_target_pairs={{0,5},{1,4},{4,9},{5,8},{8,13},{9,12},{12,1},{13,0},{2,7},{3,6},{6... | collective-permute-start | bytes 417800 | tf_op jit(solution)/shard_map/ppermute | solution.py:533
  119.0 12.9 %collective-permute-start.18 = (bf16[544,128]{1,0:T(8,128)(2,1)S(1)}, bf16[544,128]{1,0:T(8,128)(2,1)S(1)}, u32[]{:S(2)}, u32[]{:S(2)}) collective-permute-start(bf16[544,128]{1,0:T(8,128)(2,1)S(1)} %get-tuple-element.86), channel_id=1, source_target_pairs={{0,8},{1,9},{4,12},{5,13},{8,0},{9,1},{12,4},{13,5},{2,10},{3,11},... | collective-permute-start | bytes 417800 | tf_op jit(solution)/shard_map/ppermute | solution.py:533
  131.9 15.5 %copy-start.3 = (bf16[1024,512]{1,0:T(8,128)(2,1)S(1)}, bf16[1024,512]{1,0:T(8,128)(2,1)}, u32[]{:S(2)}) copy-start(bf16[1024,512]{1,0:T(8,128)(2,1)} %refs_4_.5) | copy-start | bytes 3145732
  135.8 4.0 %collective-permute-start.22 = (bf16[4,128,512]{2,1,0:T(8,128)(2,1)S(1)}, bf16[4,128,512]{2,1,0:T(8,128)(2,1)S(1)}, u32[]{:S(2)}, u32[]{:S(2)}) collective-permute-start(bf16[4,128,512]{2,1,0:T(8,128)(2,1)S(1)} %get-tuple-element.93), channel_id=1, source_target_pairs={{0,1},{1,0},{2,3},{3,2},{4,5},{5,4},{6,7},{7,6},{8,9},{9,8},{10,11... | collective-permute-start | bytes 1572872 | tf_op jit(solution)/shard_map/ppermute | solution.py:539
  135.9 8.7 %collective-permute-start.19 = (bf16[544,128]{1,0:T(8,128)(2,1)S(1)}, bf16[544,128]{1,0:T(8,128)(2,1)S(1)}, u32[]{:S(2)}, u32[]{:S(2)}) collective-permute-start(bf16[544,128]{1,0:T(8,128)(2,1)S(1)} %get-tuple-element.89), channel_id=1, source_target_pairs={{0,9},{1,8},{4,13},{5,12},{8,1},{9,0},{12,5},{13,4},{2,11},{3,10},... | collective-permute-start | bytes 417800 | tf_op jit(solution)/shard_map/ppermute | solution.py:533
  135.9 9.5 %collective-permute-start.20 = (bf16[544,128]{1,0:T(8,128)(2,1)S(1)}, bf16[544,128]{1,0:T(8,128)(2,1)S(1)}, u32[]{:S(2)}, u32[]{:S(2)}) collective-permute-start(bf16[544,128]{1,0:T(8,128)(2,1)S(1)} %get-tuple-element.90), channel_id=1, source_target_pairs={{0,12},{1,13},{4,0},{5,1},{8,4},{9,5},{12,8},{13,9},{2,14},{3,15},... | collective-permute-start | bytes 417800 | tf_op jit(solution)/shard_map/ppermute | solution.py:533
  137.3 10.0 %collective-permute-start.21 = (bf16[544,128]{1,0:T(8,128)(2,1)S(1)}, bf16[544,128]{1,0:T(8,128)(2,1)S(1)}, u32[]{:S(2)}, u32[]{:S(2)}) collective-permute-start(bf16[544,128]{1,0:T(8,128)(2,1)S(1)} %get-tuple-element.91), channel_id=1, source_target_pairs={{0,13},{1,12},{4,1},{5,0},{8,5},{9,4},{12,9},{13,8},{2,15},{3,14},... | collective-permute-start | bytes 417800 | tf_op jit(solution)/shard_map/ppermute | solution.py:533
  151.3 35.0 %collective-permute-start.23 = (bf16[1024,512]{1,0:T(8,128)(2,1)S(1)}, bf16[1024,512]{1,0:T(8,128)(2,1)S(1)}, u32[]{:S(2)}, u32[]{:S(2)}) collective-permute-start(bf16[1024,512]{1,0:T(8,128)(2,1)S(1)} %get-tuple-element.100), channel_id=1, source_target_pairs={{0,2},{2,0},{1,3},{3,1},{4,6},{6,4},{5,7},{7,5},{8,10},{10,8},{9,1... | collective-permute-start | bytes 3145736 | tf_op jit(solution)/shard_map/ppermute | solution.py:539
  156.4 15.5 %collective-permute-start.24 = (bf16[4,128,512]{2,1,0:T(8,128)(2,1)S(1)}, bf16[4,128,512]{2,1,0:T(8,128)(2,1)S(1)}, u32[]{:S(2)}, u32[]{:S(2)}) collective-permute-start(bf16[4,128,512]{2,1,0:T(8,128)(2,1)S(1)} %get-tuple-element.102), channel_id=1, source_target_pairs={{0,1},{1,0},{2,3},{3,2},{4,5},{5,4},{6,7},{7,6},{8,9},{9,8},{10,11... | collective-permute-start | bytes 1572872 | tf_op jit(solution)/shard_map/ppermute | solution.py:539
  156.6 10.0 %collective-permute-start.25 = (bf16[128,512]{1,0:T(8,128)(2,1)S(1)}, bf16[128,512]{1,0:T(8,128)(2,1)S(1)}, u32[]{:S(2)}, u32[]{:S(2)}) collective-permute-start(bf16[128,512]{1,0:T(8,128)(2,1)S(1)} %get-tuple-element.103.refs_14_), channel_id=1, source_target_pairs={{0,4},{4,8},{8,12},{12,0},{1,5},{5,9},{9,13},{13,1},{2,6},{6,10},{... | collective-permute-start | bytes 393224 | tf_op jit(solution)/shard_map/ppermute | solution.py:539
  160.2 11.7 %collective-permute-start.26 = (bf16[128,512]{1,0:T(8,128)(2,1)S(1)}, bf16[128,512]{1,0:T(8,128)(2,1)S(1)}, u32[]{:S(2)}, u32[]{:S(2)}) collective-permute-start(bf16[128,512]{1,0:T(8,128)(2,1)S(1)} %get-tuple-element.104.refs_15_), channel_id=1, source_target_pairs={{0,8},{4,12},{8,0},{12,4},{1,9},{5,13},{9,1},{13,5},{2,10},{6,14},... | collective-permute-start | bytes 393224 | tf_op jit(solution)/shard_map/ppermute | solution.py:539
  162.7 9.2 %collective-permute-start.27 = (bf16[128,512]{1,0:T(8,128)(2,1)S(1)}, bf16[128,512]{1,0:T(8,128)(2,1)S(1)}, u32[]{:S(2)}, u32[]{:S(2)}) collective-permute-start(bf16[128,512]{1,0:T(8,128)(2,1)S(1)} %get-tuple-element.105.refs_16_), channel_id=1, source_target_pairs={{0,12},{4,0},{8,4},{12,8},{1,13},{5,1},{9,5},{13,9},{2,14},{6,2},{... | collective-permute-start | bytes 393224 | tf_op jit(solution)/shard_map/ppermute | solution.py:539
  172.6 8.1 %collective-permute-start.28 = (bf16[128,512]{1,0:T(8,128)(2,1)S(1)}, bf16[128,512]{1,0:T(8,128)(2,1)S(1)}, u32[]{:S(2)}, u32[]{:S(2)}) collective-permute-start(bf16[128,512]{1,0:T(8,128)(2,1)S(1)} %get-tuple-element.107), channel_id=1, source_target_pairs={{0,4},{4,8},{8,12},{12,0},{1,5},{5,9},{9,13},{13,1},{2,6},{6,10},{... | collective-permute-start | bytes 393224 | tf_op jit(solution)/shard_map/ppermute | solution.py:539
  175.9 9.6 %collective-permute-start.29 = (bf16[128,512]{1,0:T(8,128)(2,1)S(1)}, bf16[128,512]{1,0:T(8,128)(2,1)S(1)}, u32[]{:S(2)}, u32[]{:S(2)}) collective-permute-start(bf16[128,512]{1,0:T(8,128)(2,1)S(1)} %get-tuple-element.108), channel_id=1, source_target_pairs={{0,8},{4,12},{8,0},{12,4},{1,9},{5,13},{9,1},{13,5},{2,10},{6,14},... | collective-permute-start | bytes 393224 | tf_op jit(solution)/shard_map/ppermute | solution.py:539
  176.4 9.1 %collective-permute-start.30 = (bf16[128,512]{1,0:T(8,128)(2,1)S(1)}, bf16[128,512]{1,0:T(8,128)(2,1)S(1)}, u32[]{:S(2)}, u32[]{:S(2)}) collective-permute-start(bf16[128,512]{1,0:T(8,128)(2,1)S(1)} %get-tuple-element.109), channel_id=1, source_target_pairs={{0,12},{4,0},{8,4},{12,8},{1,13},{5,1},{9,5},{13,9},{2,14},{6,2},{... | collective-permute-start | bytes 393224 | tf_op jit(solution)/shard_map/ppermute | solution.py:539

commit v7 on v4

--- a/solution.py
+++ b/solution.py
@@ -59,69 +59,88 @@
     return [(seq, sub) for seq in range(sizes[0]) for sub in range(sizes[1])]
 
 
-def hand_out(by_owner_ref, out_refs, me_ref, sizes):
-    for ahead, out_ref in zip(steps_of(sizes), out_refs):
-        out_ref[...] = by_owner_ref[owner_of(me_ref, ahead, sizes)]
-
-
-def project_query_kernel(sizes, groups, rows, me_ref, assign_ref, tokens_ref, weight_ref, cotan_ref, *rest):
-    out_refs, (slot_ref, mixed_ref, sorted_ref) = rest[:-3], rest[-3:]
-    toks = tokens_ref.shape[0]
+def slots_of(assign, groups, rows):
+    toks = assign.shape[1]
     per_group = CLUSTERS // groups
-    heads = weight_ref.shape[1] // HD
-    member = iota((CLUSTERS, toks), 0) == assign_ref[...]
-    member_f = jnp.where(member, 1.0, 0.0)
-    member_b = member_f.astype(BF16)
-    upto = ones_where(iota((toks, toks), 0) <= iota((toks, toks), 1))
-    running = dot(member_b, upto)
-    counts = jnp.broadcast_to(jnp.sum(member_f, axis=1, keepdims=True), (CLUSTERS, LANES))
+    member = jnp.where(iota((CLUSTERS, toks), 0) == assign, 1.0, 0.0)
+    member_b = member.astype(BF16)
+    upto = ones_where(iota((LANES, LANES), 0) <= iota((LANES, LANES), 1))
+    counts = jnp.zeros((CLUSTERS, 1), F32)
+    running = []
+    for first in range(0, toks, LANES):
+        within = dot(member_b[:, first : first + LANES], upto)
+        running.append(within + counts)
+        counts = counts + within[:, LANES - 1 :]
+    running = jnp.concatenate(running, axis=1)
     here, other = iota((CLUSTERS, CLUSTERS), 0), iota((CLUSTERS, CLUSTERS), 1)
     group_of = lambda index: lax.div(index, jnp.int32(per_group))
     earlier = ones_where((other < here) & (group_of(other) == group_of(here)))
-    base = dot(earlier, counts.astype(BF16))[:, :1]
+    base = dot(earlier, jnp.broadcast_to(counts, (CLUSTERS, LANES)).astype(BF16))[:, :1]
     base = base + (group_of(iota((CLUSTERS, 1), 0)) * rows).astype(F32)
-    slot = jnp.sum(member_f * (running - 1.0 + base), axis=0, keepdims=True).astype(jnp.int32)
+    slot = jnp.sum(member * (running - 1.0 + base), axis=0, keepdims=True).astype(jnp.int32)
+    spread = jnp.concatenate([member_b, jnp.zeros((LANES - CLUSTERS, toks), BF16)], axis=0)
+    return slot, dot_nt(jnp.ones((COUNT_ROWS, toks), BF16), spread).astype(BF16)
+
+
+def project_query_kernel(sizes, groups, rows, me_ref, assign_ref, tokens_hbm, weight_hbm, cotan_hbm, *rest):
+    out_refs, rest = rest[:-10], rest[-10:]
+    slot_ref, tokens_ref, weight_ref, cotan_ref, query_ref, pick_ref, part_ref, sorted_ref, in_sems, out_sems = rest
+    toks, width = tokens_ref.shape
+    heads = weight_ref.shape[1] // HD
+    fine = min(256, toks, width)
+
+    def load(kind):
+        source, target = ((cotan_hbm, cotan_ref), (weight_hbm, weight_ref), (tokens_hbm, tokens_ref))[kind]
+        return [
+            pltpu.make_async_copy(
+                source.at[pl.ds(row, fine), :], target.at[pl.ds(row, fine), :], in_sems.at[kind, row // fine]
+            )
+            for row in range(0, source.shape[0], fine)
+        ]
+
+    for copy in load(0) + load(1) + load(2):
+        copy.start()
+    slot, tallies = slots_of(assign_ref[...], groups, rows)
     slot_ref[...] = slot
-    spread = jnp.concatenate([member_b, jnp.zeros((LANES - CLUSTERS, toks), BF16)], axis=0)
-    tallies = dot_nt(jnp.ones((COUNT_ROWS, toks), BF16), spread).astype(BF16)
     for owner in range(sorted_ref.shape[0]):
         sorted_ref[owner, rows:, :] = tallies
-
-    step = min(512, toks)
-
-    @pl.loop(0, toks // step)
-    def _(i):
-        where = pl.ds(pl.multiple_of(i * step, step), step)
-        query = dot(tokens_ref[where, :], weight_ref[...])
-        cotan = cotan_ref[where, :].astype(F32)
-        low = low_half((step, LANES))
+    slots = pick_ref.shape[0]
+    step = min(512, slots)
+    for first in range(0, slots, step):
+        pick_ref[first : first + step, :] = ones_where(iota((step, toks), 0) + first == slot)
+    for copy in load(0):
+        copy.wait()
+    for first in range(0, slots, step):
+        part_ref[first : first + step, :] = dot(pick_ref[first : first + step, :], cotan_ref[...])
+    for copy in load(1):
+        copy.wait()
+    tokens = load(2)
+    for index, first in enumerate(range(0, toks, fine)):
+        tokens[index].wait()
+        query_ref[first : first + fine, :] = dot(tokens_ref[first : first + fine, :], weight_ref[...]).astype(BF16)
+    part = min(512, rows)
+    low = low_half((part, LANES))
+    for first in range(0, slots, part):
+        group, start = first // rows, first % rows
+        query = dot(pick_ref[first : first + part, :], query_ref[...])
         for pair in range(heads // 2):
-            q_tile = query[:, pair * LANES : (pair + 1) * LANES]
-            c_tile = cotan[:, pair * LANES : (pair + 1) * LANES]
+            columns = slice(pair * LANES, (pair + 1) * LANES)
+            q_tile, c_tile = query[:, columns], part_ref[first : first + part, columns]
             even = jnp.where(low, q_tile, swap_halves(c_tile)).astype(BF16)
             odd = jnp.where(low, swap_halves(q_tile), c_tile).astype(BF16)
-            mixed_ref[where, 2 * pair * LANES : (2 * pair + 1) * LANES] = even
-            mixed_ref[where, (2 * pair + 1) * LANES : (2 * pair + 2) * LANES] = odd
-
-    part = min(512, rows)
-    pieces = rows // part
-
-    @pl.loop(0, groups * pieces)
-    def _(i):
-        group, piece = lax.div(i, jnp.int32(pieces)), lax.rem(i, jnp.int32(pieces))
-        first = pl.multiple_of(piece * part, part)
-        pick = ones_where(iota((part, toks), 0) + i * part == slot_ref[...])
-        sorted_rows = dot(pick, mixed_ref[...]).astype(BF16)
-        for head in range(heads):
-            sorted_ref[group * heads + head, pl.ds(first, part), :] = sorted_rows[
-                :, head * LANES : (head + 1) * LANES
-            ]
-
-    hand_out(sorted_ref, out_refs, me_ref, sizes)
-
-
-def project_value_kernel(sizes, groups, rows, me_ref, slot_ref, tokens_ref, weight_ref, *rest):
-    out_refs, (turned_ref, unsort_ref, value_ref, sorted_ref) = rest[:-4], rest[-4:]
+            sorted_ref[group * heads + 2 * pair, start : start + part, :] = even
+            sorted_ref[group * heads + 2 * pair + 1, start : start + part, :] = odd
+    copies = [
+        pltpu.make_async_copy(sorted_ref.at[owner_of(me_ref, ahead, sizes)], out_ref, out_sems.at[k])
+        for k, (ahead, out_ref) in enumerate(zip(steps_of(sizes), out_refs))
+    ]
+    for copy in copies:
+        copy.start()
+    for copy in copies:
+        copy.wait()
+
+
+def project_value_kernel(groups, rows, slot_ref, tokens_ref, weight_ref, sorted_ref, turned_ref, unsort_ref, value_ref):
     toks = tokens_ref.shape[0]
     heads = weight_ref.shape[1] // HD
     step = min(512, toks)
@@ -151,7 +170,6 @@
             sorted_ref[group * heads + 2 * pair, pl.ds(first, part), :] = even
             sorted_ref[group * heads + 2 * pair + 1, pl.ds(first, part), :] = odd
 
-    hand_out(sorted_ref, out_refs, me_ref, sizes)
     turned_ref[...] = tokens_ref[...].T
     slots = unsort_ref.shape[1]
     part = min(256, slots)
@@ -274,16 +292,15 @@
         out_ref[...] = jnp.where(low_half((half, LANES)), swap_halves(up), down).astype(BF16)
 
 
-def query_grad_kernel(sizes, per_group, slot_rows, me_ref, counts_ref, dense_ref, *refs):
-    owners = sizes[0] * sizes[1]
-    value_refs, out_refs, rest = refs[:owners], refs[owners : 2 * owners], refs[2 * owners :]
-    place_ref, wide_ref, block_ref, sums_ref, centroid_ref = rest[:5]
-    score_refs, grad_probs_refs, both_refs = rest[5:7], rest[7:9], rest[9:11]
-    half = value_refs[0].shape[0]
+def query_grad_kernel(
+    owners, per_group, slot_rows, me_ref, counts_ref, dense_ref, value_in_ref, out_ref, place_ref, wide_ref, block_ref, *rest
+):
+    sums_ref, centroid_ref = rest[:2]
+    score_refs, grad_probs_refs, both_refs = rest[2:4], rest[4:6], rest[6:8]
+    half = value_in_ref.shape[1]
     rows = 2 * half
-    for ahead, value_ref in zip(steps_of(sizes), value_refs):
-        source = source_of(me_ref, ahead, sizes)
-        value = value_ref[...].astype(F32)
+    for source in range(owners):
+        value = value_in_ref[source].astype(F32)
         wide_ref[source, :half, :] = swap_halves(value)
         wide_ref[source, half:rows, :] = value
         wide_ref[source, rows:, :] = jnp.zeros((slot_rows, LANES), F32)
@@ -329,15 +346,14 @@
             wide_ref[source, pl.ds(start, slot_rows), :] = block_ref[pl.ds(row, slot_rows), :]
 
     for_each_cluster(counts_ref, me_ref, place_ref, owners, per_group, scatter)
-    extra = out_refs[0].shape[0] - half
+    extra = out_ref.shape[1] - half
     centroid = jnp.where(
         low_half((extra, LANES)), centroid_ref[:extra, :], swap_halves(centroid_ref[extra:, :])
     ).astype(BF16)
-    for ahead, out_ref in zip(steps_of(sizes), out_refs):
-        source = owner_of(me_ref, ahead, sizes)
+    for source in range(owners):
         up, down = wide_ref[source, :half, :], wide_ref[source, half:rows, :]
-        out_ref[:half, :] = jnp.where(low_half((half, LANES)), up, swap_halves(down)).astype(BF16)
-        out_ref[half:, :] = centroid
+        out_ref[source, :half, :] = jnp.where(low_half((half, LANES)), up, swap_halves(down)).astype(BF16)
+        out_ref[source, half:, :] = centroid
 
 
 def unfold(home_ref, out_ref, heads, start, half, finish):
@@ -358,10 +374,8 @@
     return x.astype(BF16)
 
 
-def bring_home(sizes, heads, me_ref, part_refs, unsort_ref, home_ref, sorted_ref, rows_ref):
-    for ahead, part_ref in zip(steps_of(sizes), part_refs):
-        home_ref[source_of(me_ref, ahead, sizes)] = part_ref[...]
-    half = sorted_ref.shape[0] * heads // (sizes[0] * sizes[1]) // 2
+def bring_home(heads, home_ref, unsort_ref, sorted_ref, rows_ref):
+    half = sorted_ref.shape[0] * heads // home_ref.shape[0] // 2
     unfold(home_ref, sorted_ref, heads, 0, half, to_half)
     toks = rows_ref.shape[0]
     step = min(512, toks)
@@ -392,26 +406,26 @@
 def value_home_kernel(sizes, heads, me_ref, turned_ref, unsort_ref, *refs):
     part_refs, rows_ref, sub_refs = refs[: -4 - sizes[1]], refs[-4 - sizes[1]], refs[-3 - sizes[1] : -3]
     home_ref, sorted_ref, whole_ref = refs[-3:]
-    bring_home(sizes, heads, me_ref, part_refs, unsort_ref, home_ref, sorted_ref, rows_ref)
+    for ahead, part_ref in zip(steps_of(sizes), part_refs):
+        home_ref[source_of(me_ref, ahead, sizes)] = part_ref[...]
+    bring_home(heads, home_ref, unsort_ref, sorted_ref, rows_ref)
     weight_partial(sizes, me_ref, turned_ref, rows_ref, whole_ref, sub_refs)
 
 
-def query_home_kernel(
-    sizes, heads, factor, parts, me_ref, unsort_ref, value_rows_ref, w_query_ref, w_value_ref, *refs
-):
-    part_refs, out_refs, (rows_ref, centroid_ref, home_ref, sorted_ref) = (
-        refs[: -4 - parts],
-        refs[-4 - parts : -4],
-        refs[-4:],
-    )
-    bring_home(sizes, heads, me_ref, part_refs, unsort_ref, home_ref, sorted_ref, rows_ref)
+def query_home_kernel(sizes, heads, factor, me_ref, turned_ref, unsort_ref, home_ref, *refs):
+    sub_refs, (rows_ref, centroid_ref, sorted_ref, whole_ref) = refs[:-4], refs[-4:]
+    bring_home(heads, home_ref, unsort_ref, sorted_ref, rows_ref)
     half = sorted_ref.shape[0] * heads // (sizes[0] * sizes[1]) // 2
     unfold(home_ref, centroid_ref, heads, half, home_ref.shape[1] - half, lambda x: x * factor)
+    weight_partial(sizes, me_ref, turned_ref, rows_ref, whole_ref, sub_refs)
+
+
+def input_grad_kernel(first, parts, me_ref, rows_ref, value_rows_ref, w_query_ref, w_value_ref, *out_refs):
     toks = rows_ref.shape[0]
     columns = w_query_ref.shape[0] // parts
     step = min(512, toks)
-    for ahead, out_ref in enumerate(out_refs):
-        dest = lax.rem(me_ref[2] + ahead, jnp.int32(parts))
+    for k, out_ref in enumerate(out_refs):
+        dest = lax.rem(me_ref[2] + (first + k), jnp.int32(parts))
         mine = pl.ds(pl.multiple_of(dest * columns, columns), columns)
 
         @pl.loop(0, toks // step)
@@ -422,45 +436,52 @@
             out_ref[where, :] = total.astype(BF16)
 
 
-def query_weight_kernel(sizes, me_ref, turned_ref, rows_ref, *refs):
-    weight_partial(sizes, me_ref, turned_ref, rows_ref, refs[-1], refs[:-1])
-
-
 def fold_subs_kernel(me_ref, *refs):
     seqs = refs[0].shape[0]
     terms, out_refs = refs[:-seqs], refs[-seqs:]
+    each = len(terms) // 2
     for ahead, out_ref in enumerate(out_refs):
         seq = lax.rem(me_ref[0] + ahead, jnp.int32(seqs))
-        total = terms[0][seq].astype(F32)
+        for which in range(2):
+            total = terms[which * each][seq].astype(F32)
+            for term in terms[which * each + 1 : (which + 1) * each]:
+                total = total + term[seq].astype(F32)
+            out_ref[which] = total.astype(BF16)
+
+
+def sum_kernel(*refs):
+    outs = 2 if len(refs[0].shape) == 3 else 1
+    terms, out_refs = refs[:-outs], refs[-outs:]
+    for which, out_ref in enumerate(out_refs):
+        total = (terms[0][which] if outs == 2 else terms[0][...]).astype(F32)
         for term in terms[1:]:
-            total = total + term[seq].astype(F32)
-        out_ref[...] = total.astype(BF16)
-
-
-def sum_kernel(*refs):
-    total = refs[0][...].astype(F32)
-    for ref in refs[1:-1]:
-        total = total + ref[...].astype(F32)
-    refs[-1][...] = total.astype(refs[-1].dtype)
-
-
-def call(kernel, outs, inputs, smem=(0,), scratch=(), flops=0, vmem=24, name=None):
-    specs = [
-        pl.BlockSpec(memory_space=pltpu.SMEM if i in smem else pltpu.VMEM) for i in range(len(inputs))
-    ]
+            total = total + (term[which] if outs == 2 else term[...]).astype(F32)
+        out_ref[...] = total.astype(out_ref.dtype)
+
+
+def call(kernel, outs, inputs, smem=(0,), in_place=(), after=(), scratch=(), flops=0, vmem=24, name=None):
+    def body(*refs):
+        kernel(*refs[: len(inputs)], *refs[len(inputs) + len(after) :])
+
+    def space(i):
+        return pltpu.SMEM if i in smem else pl.ANY if i in in_place else pltpu.VMEM
+
+    specs = [pl.BlockSpec(memory_space=space(i)) for i in range(len(inputs))]
+    specs += [pl.BlockSpec(memory_space=pl.ANY)] * len(after)
     moved = sum(x.size * x.dtype.itemsize for x in inputs) + sum(
         x.size * x.dtype.itemsize for x in jax.tree.leaves(outs)
     )
+    out_space = lambda x: pl.ANY if in_place and x.dtype == BF16 else pltpu.VMEM
     return pl.pallas_call(
-        kernel,
+        body,
         out_shape=outs,
         in_specs=specs,
-        out_specs=jax.tree.map(lambda _: pl.BlockSpec(memory_space=pltpu.VMEM), outs),
+        out_specs=jax.tree.map(lambda x: pl.BlockSpec(memory_space=out_space(x)), outs),
         scratch_shapes=list(scratch),
         compiler_params=pltpu.CompilerParams(vmem_limit_bytes=vmem * 2**20),
         cost_estimate=pl.CostEstimate(flops=flops, bytes_accessed=moved, transcendentals=0),
         name=name,
-    )(*inputs)
+    )(*inputs, *after)
 
 
 def exchange(parts, sizes):
@@ -486,18 +507,8 @@
     return [parts[0]] + [shift(parts[ahead], axis, ahead) for ahead in range(1, len(parts))]
 
 
-def fold_subs(me, by_sub, name):
-    seqs, piece, columns = by_sub[0].shape
-    return call(
-        fold_subs_kernel,
-        (jax.ShapeDtypeStruct((piece, columns), BF16),) * seqs,
-        (me, *pass_round(by_sub, "sub")),
-        name=name,
-    )
-
-
-def add_up(terms, dtype, name):
-    return call(sum_kernel, jax.ShapeDtypeStruct(terms[0].shape, dtype), tuple(terms), smem=(), name=name)
+def all_to_all(rows):
+    return lax.all_to_all(rows, OWNERS, split_axis=0, concat_axis=0, tiled=True)
 
 
 def on_device(tokens_in, w_query, w_value, cotangent, assignment):
@@ -529,20 +540,33 @@
         functools.partial(project_query_kernel, sizes, groups, rows),
         several(owners, rows + COUNT_ROWS, LANES) + (shape((1, toks), jnp.int32),),
         (me, assignment.reshape(1, toks), tokens_in, w_query, cotangent),
-        scratch=[pltpu.VMEM((toks, 2 * width_dev), BF16), pltpu.VMEM((owners, rows + COUNT_ROWS, LANES), BF16)],
+        in_place=(2, 3, 4),
+        scratch=[
+            pltpu.VMEM((toks, width), BF16),
+            pltpu.VMEM((width, width_dev), BF16),
+            pltpu.VMEM((toks, width_dev), BF16),
+            pltpu.VMEM((toks, width_dev), BF16),
+            pltpu.VMEM((slots, toks), BF16),
+            pltpu.VMEM((slots, width_dev), F32),
+            pltpu.VMEM((owners, rows + COUNT_ROWS, LANES), BF16),
+            pltpu.SemaphoreType.DMA((3, max(toks, width) // min(256, toks, width))),
+            pltpu.SemaphoreType.DMA((owners,)),
+        ],
         flops=2 * toks * width * width_dev + 4 * slots * toks * width_dev,
+        vmem=60,
         name="project_query",
     )
     got_mixed = exchange(send_mixed, sizes)
-    *send_value, turned, unsort = call(
-        functools.partial(project_value_kernel, sizes, groups, rows),
-        several(owners, half, LANES) + several(1, width, toks) + several(1, toks, slots),
-        (me, slot_row, tokens_in, w_value),
-        scratch=[pltpu.VMEM((toks, width_dev), BF16), pltpu.VMEM((owners, half, LANES), BF16)],
+    send_value, turned, unsort = call(
+        functools.partial(project_value_kernel, groups, rows),
+        several(1, owners, half, LANES) + several(1, width, toks) + several(1, toks, slots),
+        (slot_row, tokens_in, w_value),
+        smem=(),
+        scratch=[pltpu.VMEM((toks, width_dev), BF16)],
         flops=2 * toks * width * width_dev + 2 * slots * toks * width_dev,
         name="project_value",
     )
-    got_value = exchange(send_value, sizes)
+    got_value = all_to_all(send_value)
     blocks = per_group * capacity // BLOCK_ROWS
     held = blocks + (LEAD + 4) * UNROLL
     block_flops = 2 * BLOCK_ROWS * BLOCK_ROWS * LANES
@@ -566,9 +590,9 @@
     )
     home_value = exchange(back_value, sizes)
     back_query = call(
-        functools.partial(query_grad_kernel, sizes, per_group, slot_rows),
-        several(owners, half + extra, LANES),
-        (me, counts, dense, *got_value),
+        functools.partial(query_grad_kernel, owners, per_group, slot_rows),
+        shape((owners, half + extra, LANES), BF16),
+        (me, counts, dense, got_value),
         smem=(0, 1),
         scratch=[place, tall, dense_rows, pltpu.VMEM((held, LANES), F32), pltpu.VMEM((2 * extra, LANES), F32)]
         + [group_f32] * 4
@@ -577,10 +601,11 @@
         vmem=48,
         name="query_grad",
     )
-    home_query = exchange(back_query, sizes)
+    home_query = all_to_all(back_query)
     weight_flops = 2 * toks * width * width_dev
     home_flops = 2 * slots * toks * width_dev
-    sub_shapes = several(sizes[1], sizes[0], width // owners, width_dev)
+    piece = width // owners
+    sub_shapes = several(sizes[1], sizes[0], piece, width_dev)
     whole = pltpu.VMEM((width, width_dev), BF16)
     sorted_rows = pltpu.VMEM((slots, width_dev), BF16)
     value_rows, *value_weight = call(
@@ -591,32 +616,48 @@
         flops=weight_flops + home_flops,
         name="value_home",
     )
-    value_weight = fold_subs(me, value_weight, "value_subs")
-    *partials, query_rows, centroid_grad = call(
-        functools.partial(query_home_kernel, sizes, heads, (CLUSTERS / (toks * owners)) ** 0.5, parts),
-        several(parts, toks, columns)
-        + several(1, toks, width_dev)
-        + (shape((groups * 2 * extra, width_dev), F32),),
-        (me, unsort, value_rows, w_query, w_value, *home_query),
-        scratch=[pltpu.VMEM((owners, half + extra, LANES), BF16), sorted_rows],
-        flops=2 * weight_flops + home_flops,
+    *query_weight, query_rows, centroid_grad = call(
+        functools.partial(query_home_kernel, sizes, heads, (CLUSTERS / (toks * owners)) ** 0.5),
+        sub_shapes + several(1, toks, width_dev) + (shape((groups * 2 * extra, width_dev), F32),),
+        (me, turned, unsort, home_query),
+        after=[value_rows],
+        scratch=[sorted_rows, whole],
+        flops=weight_flops + home_flops,
         name="query_home",
     )
-    arrived = pass_round(partials, "head")
-    value_weight, _ = lax.optimization_barrier((value_weight, home_query))
-    value_weight = pass_round(value_weight, "seq")
-    query_weight = call(
-        functools.partial(query_weight_kernel, sizes),
-        sub_shapes,
-        (me, turned, query_rows),
-        scratch=[whole],
-        flops=weight_flops,
-        name="query_weight",
-    )
-    query_weight = pass_round(fold_subs(me, query_weight, "query_subs"), "seq")
-    grad_wv = add_up(value_weight, F32, "value_sum")
-    grad_wq = add_up(query_weight, F32, "query_sum")
-    grad_input = add_up(arrived, BF16, "input_sum")
+    partials = call(
+        functools.partial(input_grad_kernel, 1, parts),
+        several(parts - 1, toks, columns),
+        (me, query_rows, value_rows, w_query, w_value),
+        flops=weight_flops * (parts - 1) * 2 // parts,
+        name="input_others",
+    )
+    arrived = [shift(partial, "head", k + 1) for k, partial in enumerate(partials)]
+    by_seq = call(
+        fold_subs_kernel,
+        several(sizes[0], 2, piece, width_dev),
+        (me, *pass_round(value_weight, "sub"), *pass_round(query_weight, "sub")),
+        after=partials,
+        name="weight_subs",
+    )
+    own = call(
+        functools.partial(input_grad_kernel, 0, parts),
+        several(1, toks, columns),
+        (me, query_rows, value_rows, w_query, w_value),
+        after=by_seq[:1],
+        flops=weight_flops * 2 // parts,
+        name="input_own",
+    )
+    grad_wv, grad_wq = call(
+        sum_kernel,
+        (shape((piece, width_dev), F32),) * 2,
+        tuple(pass_round(by_seq, "seq")),
+        smem=(),
+        name="weight_sum",
+    )
+    grad_input = call(
+        sum_kernel, shape((toks, columns), BF16), tuple(list(own) + arrived), smem=(), name="input_sum"
+    )
     if groups > 1:
         centroid_grad = centroid_grad.reshape(groups, 2 * extra, width_dev)[:, :per_group]
         centroid_grad = centroid_grad.reshape(CLUSTERS, width_dev)

time: 183 us -> 230 us (1.26); the launches traced: 181 us -> 226 us
  waiting for transfers between devices: 52.2 us -> 108 us
  starting transfers between devices: 68.9 us -> 45.2 us
  local copies, waits for them, and re-layouts: 4.74 us -> 12.4 us
  Pallas kernels: 54.5 us -> 58.7 us
    ppermute x28 -> x14, waiting for transfers between devices: 44.2 us -> 91.2 us  [exchange(): out.append(part if ahead == (0, 0) else lax.ppermute(part, OWNERS, moves))]
    ppermute x28 -> x14, starting transfers between devices: 49.6 us -> 16.8 us  [exchange(): out.append(part if ahead == (0, 0) else lax.ppermute(part, OWNERS, moves))]
    all_to_all x0 -> x2, starting transfers between devices: none -> 20.9 us  [all_to_all(): return lax.all_to_all(rows, OWNERS, split_axis=0, concat_axis=0, tiled=True)]
    ppermute x9 -> x6, starting transfers between devices: 19.3 us -> 7.56 us  [shift(): lax.ppermute(part, axis, [(i, (i + ahead) % size) for i in range(size)])]
    ppermute x9 -> x6, waiting for transfers between devices: 7.96 us -> 16.7 us  [shift(): lax.ppermute(part, axis, [(i, (i + ahead) % size) for i in range(size)])]
    unnamed x14 -> x40, local copies, waits for them, and re-layouts: 4.74 us -> 12.4 us
    pallas_call x12 -> x11, Pallas kernels: 54.5 us -> 58.7 us  [call(): pl.pallas_call(body, out_shape=outs, in_specs=specs, out_specs=jax.tree.m...]
  transfers between devices with their start and end apart: 37 -> 22, of which waited for: 10 -> 13; matrix products, arithmetic and copies ran while one was open for 0% -> 0% of each run, Pallas kernels for 23% -> 9%
where the time goes in v7:
time: 230 us; the launch traced here: 226 us
  waiting for transfers between devices  108 us (47%)
  Pallas kernels  58.7 us (26%)
  starting transfers between devices  45.2 us (20%)
  local copies, waits for them, and re-layouts  12.4 us (5%)
    ppermute x14, waiting for transfers between devices, exchange(): out.append(part if ahead == (0, 0) else lax.ppermute(part, OWNERS, moves))  91.2 us
    pallas_call x11, Pallas kernels, call(): pl.pallas_call(body, out_shape=outs, in_specs=specs, out_specs=jax.tree.m...  58.7 us
    all_to_all x2, starting transfers between devices, all_to_all(): return lax.all_to_all(rows, OWNERS, split_axis=0, concat_axis=0, tiled=True)  20.9 us
    ppermute x14, starting transfers between devices, exchange(): out.append(part if ahead == (0, 0) else lax.ppermute(part, OWNERS, moves))  16.8 us
    ppermute x6, waiting for transfers between devices, shift(): lax.ppermute(part, axis, [(i, (i + ahead) % size) for i in range(size)])  16.7 us
    unnamed x40, local copies, waits for them, and re-layouts  12.4 us
    ppermute x6, starting transfers between devices, shift(): lax.ppermute(part, axis, [(i, (i + ahead) % size) for i in range(size)])  7.56 us
  transfers between devices with their start and end apart: 22, of which 13 were waited for; matrix products, arithmetic and copies ran while one was open for 0% of the time, Pallas kernels for 9%

profile of v7, /device:TPU:0, one launch (start us, length us, event | category | flops | bytes accessed | tf_op | source)
XLA Modules:
  0.0 225.6 jit_solution(1179961907260937573)
XLA Ops:
  1.3 8.5 %project_query.1 = (bf16[1040,128]{1,0:T(8,128)(2,1)}, bf16[1040,128]{1,0:T(8,128)(2,1)}, bf16[1040,128]{1,0:T(8,128)(2,1)}, bf16[1040,128]{1,0:T(8,128)(2,1)}, ...) custom-call(s32[4]{0:T(128)} %pad_add_fusion.refs_0_, ...), custom_call_target="tpu_custom_call" | custom-call | flops 3221225472 | bytes 6332432 | tf_op jit(solution)/shard_map/project_query/pallas_call | solution.py:475
  10.6 5.1 %project_value.1 = (bf16[8,512,128]{2,1,0:T(8,128)(2,1)}, bf16[1024,1024]{1,0:T(8,128)(2,1)S(1)}, bf16[1024,1024]{1,0:T(8,128)(2,1)S(1)}) custom-call(s32[1,1024]{1,0:T(1,128)S(1)} %copy-done.15, bf16[1024,1024]{1,0:T(8,128)(2,1)S(1)} %copy-done.5, bf16[1024,512]{1,0:T(8,128)(2,1)S(1)} %copy-done.1), custom_call_target="tpu_custom_call" | custom-call | flops 2147483648 | bytes 8392704 | tf_op jit(solution)/shard_map/project_value/pallas_call | solution.py:475
  15.7 1.3 copy-done.8
  17.0 1.4 copy-done.11
  18.4 6.5 %all-to-all-start = ((bf16[8,512,128]{2,1,0:T(8,128)(2,1)}), bf16[8,512,128]{2,1,0:T(8,128)(2,1)S(1)}, u32[]{:S(2)}, u32[]{:S(2)}) async-start(bf16[8,512,128]{2,1,0:T(8,128)(2,1)} %get-tuple-element.52), calls=%async_computation | async-start | bytes 2097152 | tf_op jit(solution)/shard_map/all_to_all | solution.py:511
  25.4 1.7 collective-permute-start.1
  27.1 1.1 collective-permute-start.2
  28.2 1.2 collective-permute-start.3
  29.5 1.5 collective-permute-start.4
  30.9 2.4 %collective-permute-start.5 = (bf16[1040,128]{1,0:T(8,128)(2,1)S(1)}, bf16[1040,128]{1,0:T(8,128)(2,1)S(1)}, u32[]{:S(2)}, u32[]{:S(2)}) collective-permute-start(bf16[1040,128]{1,0:T(8,128)(2,1)S(1)} %copy-done.17), channel_id=1, source_target_pairs={{0,12},{1,13},{4,0},{5,1},{8,4},{9,5},{12,8},{13,9},{2,14},{3,15},... | collective-permute-start | bytes 798728 | tf_op jit(solution)/shard_map/ppermute | solution.py:497
  33.3 19.8 %collective-permute-done.1.refs_3_ = bf16[1040,128]{1,0:T(8,128)(2,1)S(1)} collective-permute-done((bf16[1040,128]{1,0:T(8,128)(2,1)}, bf16[1040,128]{1,0:T(8,128)(2,1)S(1)}, u32[]{:S(2)}, u32[]{:S(2)}) %collective-permute-start.1) | collective-permute-done | bytes 266272 | tf_op jit(solution)/shard_map/ppermute | solution.py:497
  53.1 4.8 %collective-permute-done.2.refs_4_ = bf16[1040,128]{1,0:T(8,128)(2,1)S(1)} collective-permute-done((bf16[1040,128]{1,0:T(8,128)(2,1)}, bf16[1040,128]{1,0:T(8,128)(2,1)S(1)}, u32[]{:S(2)}, u32[]{:S(2)}) %collective-permute-start.2) | collective-permute-done | bytes 266272 | tf_op jit(solution)/shard_map/ppermute | solution.py:497
  58.0 22.6 %collective-permute-done.3.refs_5_ = bf16[1040,128]{1,0:T(8,128)(2,1)S(1)} collective-permute-done((bf16[1040,128]{1,0:T(8,128)(2,1)S(1)}, bf16[1040,128]{1,0:T(8,128)(2,1)S(1)}, u32[]{:S(2)}, u32[]{:S(2)}) %collective-permute-start.3) | collective-permute-done | bytes 266272 | tf_op jit(solution)/shard_map/ppermute | solution.py:497
  80.5 4.8 %collective-permute-done.4.refs_6_ = bf16[1040,128]{1,0:T(8,128)(2,1)S(1)} collective-permute-done((bf16[1040,128]{1,0:T(8,128)(2,1)S(1)}, bf16[1040,128]{1,0:T(8,128)(2,1)S(1)}, u32[]{:S(2)}, u32[]{:S(2)}) %collective-permute-start.4) | collective-permute-done | bytes 266272 | tf_op jit(solution)/shard_map/ppermute | solution.py:497
  85.3 0.9 copy-done.14
  86.2 13.1 %value_grad.1 = (bf16[512,128]{1,0:T(8,128)(2,1)S(1)}, bf16[512,128]{1,0:T(8,128)(2,1)S(1)}, bf16[512,128]{1,0:T(8,128)(2,1)S(1)}, bf16[512,128]{1,0:T(8,128)(2,...) custom-call(s32[4]{0:T(128)S(1)} %copy-done.4, ...), custom_call_target="tpu_custom_call" | custom-call | flops 2147483648 | bytes 8163344 | tf_op jit(solution)/shard_map/value_grad/pallas_call | solution.py:475
  99.3 16.8 %query_grad.1 = bf16[8,544,128]{2,1,0:T(8,128)(2,1)} custom-call(s32[4]{0:T(128)S(1)} %copy-done.4, s32[8,128]{1,0:T(8,128)S(1)} %get-tuple-element.50.refs_1_, bf16[19456,128]{1,0:T(8,128)(2,1)} %get-tuple-element.51.refs_2_, bf16[8,512,128]{2,1,0:T(8,128)(2,1)S(1)} %all-to-all-done.refs_3_), custom_call_target="tpu_custom_call" | custom-call | flops 3221225472 | bytes 7147536 | tf_op jit(solution)/shard_map/query_grad/pallas_call | solution.py:475
  116.1 14.4 %all-to-all-start.1 = ((bf16[8,544,128]{2,1,0:T(8,128)(2,1)}), bf16[8,544,128]{2,1,0:T(8,128)(2,1)S(1)}, u32[]{:S(2)}, u32[]{:S(2)}) async-start(bf16[8,544,128]{2,1,0:T(8,128)(2,1)} %query_grad.1), calls=%async_computation.1 | async-start | bytes 2228224 | tf_op jit(solution)/shard_map/all_to_all | solution.py:511
  131.0 1.7 collective-permute-start.8
  132.7 1.1 collective-permute-start.9
  133.8 1.2 collective-permute-start.10
  135.1 1.5 collective-permute-start.11
  136.5 2.4 %collective-permute-start.12 = (bf16[512,128]{1,0:T(8,128)(2,1)S(1)}, bf16[512,128]{1,0:T(8,128)(2,1)S(1)}, u32[]{:S(2)}, u32[]{:S(2)}) collective-permute-start(bf16[512,128]{1,0:T(8,128)(2,1)S(1)} %get-tuple-element.59), channel_id=1, source_target_pairs={{0,12},{1,13},{4,0},{5,1},{8,4},{9,5},{12,8},{13,9},{2,14},{3,15},... | collective-permute-start | bytes 393224 | tf_op jit(solution)/shard_map/ppermute | solution.py:497
  138.9 18.0 %collective-permute-done.8.refs_5_ = bf16[512,128]{1,0:T(8,128)(2,1)S(1)} collective-permute-done((bf16[512,128]{1,0:T(8,128)(2,1)S(1)}, bf16[512,128]{1,0:T(8,128)(2,1)S(1)}, u32[]{:S(2)}, u32[]{:S(2)}) %collective-permute-start.8) | collective-permute-done | bytes 131104 | tf_op jit(solution)/shard_map/ppermute | solution.py:497
  156.9 1.9 collective-permute-done.9.refs_6_
  158.7 14.4 %collective-permute-done.10.refs_7_ = bf16[512,128]{1,0:T(8,128)(2,1)S(1)} collective-permute-done((bf16[512,128]{1,0:T(8,128)(2,1)S(1)}, bf16[512,128]{1,0:T(8,128)(2,1)S(1)}, u32[]{:S(2)}, u32[]{:S(2)}) %collective-permute-start.10) | collective-permute-done | bytes 131104 | tf_op jit(solution)/shard_map/ppermute | solution.py:497
  173.1 1.9 collective-permute-done.11.refs_8_
  175.0 3.1 %collective-permute-done.13.refs_10_ = bf16[512,128]{1,0:T(8,128)(2,1)S(1)} collective-permute-done((bf16[512,128]{1,0:T(8,128)(2,1)S(1)}, bf16[512,128]{1,0:T(8,128)(2,1)S(1)}, u32[]{:S(2)}, u32[]{:S(2)}) %collective-permute-start.13) | collective-permute-done | bytes 131104 | tf_op jit(solution)/shard_map/ppermute | solution.py:497
  178.1 1.6 copy-done.9
  179.7 1.6 copy-done.12
  181.3 3.9 %value_home.1 = (bf16[1024,512]{1,0:T(8,128)(2,1)S(1)}, bf16[4,128,512]{2,1,0:T(8,128)(2,1)S(1)}, bf16[4,128,512]{2,1,0:T(8,128)(2,1)S(1)}) custom-call(s32[4]{0:T(128)S(1)} %copy-done.4, bf16[1024,1024]{1,0:T(8,128)(2,1)S(1)} %copy-done.9, bf16[1024,1024]{1,0:T(8,128)(2,1)S(1)} %copy-done.12, bf16[512,128]{1,0:T(8,128)(2,1)S(1)} %get-tuple-element.53.refs_3_, ...), custom_call_target="tpu_custom_call" | custom-call | flops 2147483648 | bytes 7340048 | tf_op jit(solution)/shard_map/value_home/pallas_call | solution.py:475
  185.2 0.8 copy-done.2
  186.0 0.8 copy-done.6
  186.8 1.6 copy-done.10
  188.4 1.6 copy-done.13
  190.0 4.4 %query_home.1 = (bf16[4,128,512]{2,1,0:T(8,128)(2,1)S(1)}, bf16[4,128,512]{2,1,0:T(8,128)(2,1)S(1)}, bf16[1024,512]{1,0:T(8,128)(2,1)S(1)}, f32[64,512]{1,0:T(8,128)}) custom-call(s32[4]{0:T(128)S(1)} %copy-done.4, bf16[1024,1024]{1,0:T(8,128)(2,1)S(1)} %copy-done.10, bf16[1024,1024]{1,0:T(8,128)(2,1)S(1)} %copy-done.13, ...), custom_call_target="tpu_custom_call" | custom-call | flops 2147483648 | bytes 7536656 | tf_op jit(solution)/shard_map/query_home/pallas_call | solution.py:475
  194.4 2.0 input_others.1.refs_5_
  196.4 1.6 collective-permute-start.16
  198.5 1.4 collective-permute-done.14.refs_2_
  200.6 0.8 weight_subs.1
  201.4 3.1 %collective-permute-start.17 = (bf16[2,128,512]{2,1,0:T(8,128)(2,1)S(1)}, bf16[2,128,512]{2,1,0:T(8,128)(2,1)S(1)}, u32[]{:S(2)}, u32[]{:S(2)}) collective-permute-start(bf16[2,128,512]{2,1,0:T(8,128)(2,1)S(1)} %get-tuple-element.68), channel_id=1, source_target_pairs={{0,4},{4,8},{8,12},{12,0},{1,5},{5,9},{9,13},{13,1},{2,6},{6,10},{... | collective-permute-start | bytes 786440 | tf_op jit(solution)/shard_map/ppermute | solution.py:503
  204.5 1.6 collective-permute-start.18
  206.1 0.8 collective-permute-start.19
  206.9 2.0 input_own.1.refs_0_
  208.9 3.8 %collective-permute-done.17.refs_1_ = bf16[2,128,512]{2,1,0:T(8,128)(2,1)S(1)} collective-permute-done((bf16[2,128,512]{2,1,0:T(8,128)(2,1)S(1)}, bf16[2,128,512]{2,1,0:T(8,128)(2,1)S(1)}, u32[]{:S(2)}, u32[]{:S(2)}) %collective-permute-start.17) | collective-permute-done | bytes 262176 | tf_op jit(solution)/shard_map/ppermute | solution.py:503
  212.8 10.7 %collective-permute-done.18.refs_2_ = bf16[2,128,512]{2,1,0:T(8,128)(2,1)S(1)} collective-permute-done((bf16[2,128,512]{2,1,0:T(8,128)(2,1)S(1)}, bf16[2,128,512]{2,1,0:T(8,128)(2,1)S(1)}, u32[]{:S(2)}, u32[]{:S(2)}) %collective-permute-start.18) | collective-permute-done | bytes 262176 | tf_op jit(solution)/shard_map/ppermute | solution.py:503
  223.5 0.9 weight_sum.1
  224.4 1.2 input_sum.1
  (48 shorter events, 3.7 us)
Async XLA Ops:
  1.3 8.5 %copy-start.1 = (bf16[1024,512]{1,0:T(8,128)(2,1)S(1)}, bf16[1024,512]{1,0:T(8,128)(2,1)}, u32[]{:S(2)}) copy-start(bf16[1024,512]{1,0:T(8,128)(2,1)} %refs_4_.5) | copy-start | bytes 3145732
  1.3 8.5 %copy-start.5 = (bf16[1024,1024]{1,0:T(8,128)(2,1)S(1)}, bf16[1024,1024]{1,0:T(8,128)(2,1)}, u32[]{:S(2)}) copy-start(bf16[1024,1024]{1,0:T(8,128)(2,1)} %refs_1_.1) | copy-start | bytes 6291460
  9.9 0.7 copy-start.15
  15.7 1.3 copy-start.8
  17.0 1.4 copy-start.11
  18.4 9.8 %copy-start.19 = (bf16[1040,128]{1,0:T(8,128)(2,1)S(1)}, bf16[1040,128]{1,0:T(8,128)(2,1)}, u32[]{:S(2)}) copy-start(bf16[1040,128]{1,0:T(8,128)(2,1)} %get-tuple-element.46) | copy-start | bytes 798724
  18.4 11.0 %copy-start.18 = (bf16[1040,128]{1,0:T(8,128)(2,1)S(1)}, bf16[1040,128]{1,0:T(8,128)(2,1)}, u32[]{:S(2)}) copy-start(bf16[1040,128]{1,0:T(8,128)(2,1)} %get-tuple-element.47) | copy-start | bytes 798724
  18.4 12.5 %copy-start.17 = (bf16[1040,128]{1,0:T(8,128)(2,1)S(1)}, bf16[1040,128]{1,0:T(8,128)(2,1)}, u32[]{:S(2)}) copy-start(bf16[1040,128]{1,0:T(8,128)(2,1)} %get-tuple-element.48) | copy-start | bytes 798724
  18.4 34.7 %copy-start.16 = (bf16[1040,128]{1,0:T(8,128)(2,1)S(1)}, bf16[1040,128]{1,0:T(8,128)(2,1)}, u32[]{:S(2)}) copy-start(bf16[1040,128]{1,0:T(8,128)(2,1)} %get-tuple-element.49) | copy-start | bytes 798724
  18.4 66.8 %copy-start.4 = (s32[4]{0:T(128)S(1)}, s32[4]{0:T(128)}, u32[]{:S(2)}) copy-start(s32[4]{0:T(128)} %pad_add_fusion.refs_0_) | copy-start | bytes 52
  18.4 80.9 %all-to-all-start = ((bf16[8,512,128]{2,1,0:T(8,128)(2,1)}), bf16[8,512,128]{2,1,0:T(8,128)(2,1)S(1)}, u32[]{:S(2)}, u32[]{:S(2)}) async-start(bf16[8,512,128]{2,1,0:T(8,128)(2,1)} %get-tuple-element.52), calls=%async_computation | async-start | bytes 2097152 | tf_op jit(solution)/shard_map/all_to_all | solution.py:511
  24.9 6.0 %collective-permute-start = (bf16[1040,128]{1,0:T(8,128)(2,1)}, bf16[1040,128]{1,0:T(8,128)(2,1)S(1)}, u32[]{:S(2)}, u32[]{:S(2)}) collective-permute-start(bf16[1040,128]{1,0:T(8,128)(2,1)} %get-tuple-element.43), channel_id=1, source_target_pairs={{0,1},{1,0},{4,5},{5,4},{8,9},{9,8},{12,13},{13,12},{2,3},{3,2},{6... | collective-permute-start | bytes 798728 | tf_op jit(solution)/shard_map/ppermute | solution.py:497
  25.4 27.7 %collective-permute-start.1 = (bf16[1040,128]{1,0:T(8,128)(2,1)}, bf16[1040,128]{1,0:T(8,128)(2,1)S(1)}, u32[]{:S(2)}, u32[]{:S(2)}) collective-permute-start(bf16[1040,128]{1,0:T(8,128)(2,1)} %get-tuple-element.44), channel_id=1, source_target_pairs={{0,4},{1,5},{4,8},{5,9},{8,12},{9,13},{12,0},{13,1},{2,6},{3,7},{6... | collective-permute-start | bytes 798728 | tf_op jit(solution)/shard_map/ppermute | solution.py:497
  27.1 30.9 %collective-permute-start.2 = (bf16[1040,128]{1,0:T(8,128)(2,1)}, bf16[1040,128]{1,0:T(8,128)(2,1)S(1)}, u32[]{:S(2)}, u32[]{:S(2)}) collective-permute-start(bf16[1040,128]{1,0:T(8,128)(2,1)} %get-tuple-element.45), channel_id=1, source_target_pairs={{0,5},{1,4},{4,9},{5,8},{8,13},{9,12},{12,1},{13,0},{2,7},{3,6},{6... | collective-permute-start | bytes 798728 | tf_op jit(solution)/shard_map/ppermute | solution.py:497
  28.2 52.3 %collective-permute-start.3 = (bf16[1040,128]{1,0:T(8,128)(2,1)S(1)}, bf16[1040,128]{1,0:T(8,128)(2,1)S(1)}, u32[]{:S(2)}, u32[]{:S(2)}) collective-permute-start(bf16[1040,128]{1,0:T(8,128)(2,1)S(1)} %copy-done.19), channel_id=1, source_target_pairs={{0,8},{1,9},{4,12},{5,13},{8,0},{9,1},{12,4},{13,5},{2,10},{3,11},... | collective-permute-start | bytes 798728 | tf_op jit(solution)/shard_map/ppermute | solution.py:497
  29.5 55.8 %collective-permute-start.4 = (bf16[1040,128]{1,0:T(8,128)(2,1)S(1)}, bf16[1040,128]{1,0:T(8,128)(2,1)S(1)}, u32[]{:S(2)}, u32[]{:S(2)}) collective-permute-start(bf16[1040,128]{1,0:T(8,128)(2,1)S(1)} %copy-done.18), channel_id=1, source_target_pairs={{0,9},{1,8},{4,13},{5,12},{8,1},{9,0},{12,5},{13,4},{2,11},{3,10},... | collective-permute-start | bytes 798728 | tf_op jit(solution)/shard_map/ppermute | solution.py:497
  30.9 54.3 %collective-permute-start.5 = (bf16[1040,128]{1,0:T(8,128)(2,1)S(1)}, bf16[1040,128]{1,0:T(8,128)(2,1)S(1)}, u32[]{:S(2)}, u32[]{:S(2)}) collective-permute-start(bf16[1040,128]{1,0:T(8,128)(2,1)S(1)} %copy-done.17), channel_id=1, source_target_pairs={{0,12},{1,13},{4,0},{5,1},{8,4},{9,5},{12,8},{13,9},{2,14},{3,15},... | collective-permute-start | bytes 798728 | tf_op jit(solution)/shard_map/ppermute | solution.py:497
  53.1 32.2 %collective-permute-start.6 = (bf16[1040,128]{1,0:T(8,128)(2,1)S(1)}, bf16[1040,128]{1,0:T(8,128)(2,1)S(1)}, u32[]{:S(2)}, u32[]{:S(2)}) collective-permute-start(bf16[1040,128]{1,0:T(8,128)(2,1)S(1)} %copy-done.16), channel_id=1, source_target_pairs={{0,13},{1,12},{4,1},{5,0},{8,5},{9,4},{12,9},{13,8},{2,15},{3,14},... | collective-permute-start | bytes 798728 | tf_op jit(solution)/shard_map/ppermute | solution.py:497
  85.3 1.0 copy-start.14
  116.1 70.7 %all-to-all-start.1 = ((bf16[8,544,128]{2,1,0:T(8,128)(2,1)}), bf16[8,544,128]{2,1,0:T(8,128)(2,1)S(1)}, u32[]{:S(2)}, u32[]{:S(2)}) async-start(bf16[8,544,128]{2,1,0:T(8,128)(2,1)} %query_grad.1), calls=%async_computation.1 | async-start | bytes 2228224 | tf_op jit(solution)/shard_map/all_to_all | solution.py:511
  130.5 6.0 %collective-permute-start.7 = (bf16[512,128]{1,0:T(8,128)(2,1)S(1)}, bf16[512,128]{1,0:T(8,128)(2,1)S(1)}, u32[]{:S(2)}, u32[]{:S(2)}) collective-permute-start(bf16[512,128]{1,0:T(8,128)(2,1)S(1)} %get-tuple-element.54), channel_id=1, source_target_pairs={{0,1},{1,0},{4,5},{5,4},{8,9},{9,8},{12,13},{13,12},{2,3},{3,2},{6... | collective-permute-start | bytes 393224 | tf_op jit(solution)/shard_map/ppermute | solution.py:497
  131.0 25.8 %collective-permute-start.8 = (bf16[512,128]{1,0:T(8,128)(2,1)S(1)}, bf16[512,128]{1,0:T(8,128)(2,1)S(1)}, u32[]{:S(2)}, u32[]{:S(2)}) collective-permute-start(bf16[512,128]{1,0:T(8,128)(2,1)S(1)} %get-tuple-element.55), channel_id=1, source_target_pairs={{0,4},{1,5},{4,8},{5,9},{8,12},{9,13},{12,0},{13,1},{2,6},{3,7},{6... | collective-permute-start | bytes 393224 | tf_op jit(solution)/shard_map/ppermute | solution.py:497
  132.7 26.0 %collective-permute-start.9 = (bf16[512,128]{1,0:T(8,128)(2,1)S(1)}, bf16[512,128]{1,0:T(8,128)(2,1)S(1)}, u32[]{:S(2)}, u32[]{:S(2)}) collective-permute-start(bf16[512,128]{1,0:T(8,128)(2,1)S(1)} %get-tuple-element.56), channel_id=1, source_target_pairs={{0,5},{1,4},{4,9},{5,8},{8,13},{9,12},{12,1},{13,0},{2,7},{3,6},{6... | collective-permute-start | bytes 393224 | tf_op jit(solution)/shard_map/ppermute | solution.py:497
  133.8 39.3 %collective-permute-start.10 = (bf16[512,128]{1,0:T(8,128)(2,1)S(1)}, bf16[512,128]{1,0:T(8,128)(2,1)S(1)}, u32[]{:S(2)}, u32[]{:S(2)}) collective-permute-start(bf16[512,128]{1,0:T(8,128)(2,1)S(1)} %get-tuple-element.57), channel_id=1, source_target_pairs={{0,8},{1,9},{4,12},{5,13},{8,0},{9,1},{12,4},{13,5},{2,10},{3,11},... | collective-permute-start | bytes 393224 | tf_op jit(solution)/shard_map/ppermute | solution.py:497
  135.1 39.9 %collective-permute-start.11 = (bf16[512,128]{1,0:T(8,128)(2,1)S(1)}, bf16[512,128]{1,0:T(8,128)(2,1)S(1)}, u32[]{:S(2)}, u32[]{:S(2)}) collective-permute-start(bf16[512,128]{1,0:T(8,128)(2,1)S(1)} %get-tuple-element.58), channel_id=1, source_target_pairs={{0,9},{1,8},{4,13},{5,12},{8,1},{9,0},{12,5},{13,4},{2,11},{3,10},... | collective-permute-start | bytes 393224 | tf_op jit(solution)/shard_map/ppermute | solution.py:497
  136.5 38.5 %collective-permute-start.12 = (bf16[512,128]{1,0:T(8,128)(2,1)S(1)}, bf16[512,128]{1,0:T(8,128)(2,1)S(1)}, u32[]{:S(2)}, u32[]{:S(2)}) collective-permute-start(bf16[512,128]{1,0:T(8,128)(2,1)S(1)} %get-tuple-element.59), channel_id=1, source_target_pairs={{0,12},{1,13},{4,0},{5,1},{8,4},{9,5},{12,8},{13,9},{2,14},{3,15},... | collective-permute-start | bytes 393224 | tf_op jit(solution)/shard_map/ppermute | solution.py:497
  156.9 21.3 %collective-permute-start.13 = (bf16[512,128]{1,0:T(8,128)(2,1)S(1)}, bf16[512,128]{1,0:T(8,128)(2,1)S(1)}, u32[]{:S(2)}, u32[]{:S(2)}) collective-permute-start(bf16[512,128]{1,0:T(8,128)(2,1)S(1)} %get-tuple-element.60), channel_id=1, source_target_pairs={{0,13},{1,12},{4,1},{5,0},{8,5},{9,4},{12,9},{13,8},{2,15},{3,14},... | collective-permute-start | bytes 393224 | tf_op jit(solution)/shard_map/ppermute | solution.py:497
  178.1 1.6 copy-start.9
  179.7 1.6 copy-start.12
  185.2 0.8 copy-start.2
  186.0 0.8 copy-start.6
  186.8 1.6 copy-start.10
  188.4 1.6 copy-start.13
  190.0 4.4 %copy-start = (bf16[1024,512]{1,0:T(8,128)(2,1)S(1)}, bf16[1024,512]{1,0:T(8,128)(2,1)}, u32[]{:S(2)}) copy-start(bf16[1024,512]{1,0:T(8,128)(2,1)} %refs_3_.5) | copy-start | bytes 3145732
  194.4 3.6 %copy-start.7 = (bf16[4,128,512]{2,1,0:T(8,128)(2,1)S(1)}, bf16[4,128,512]{2,1,0:T(8,128)(2,1)}, u32[]{:S(2)}) copy-start(bf16[4,128,512]{2,1,0:T(8,128)(2,1)} %copy-done.6) | copy-start | bytes 1572868
  194.4 6.3 %copy-start.3 = (bf16[4,128,512]{2,1,0:T(8,128)(2,1)S(1)}, bf16[4,128,512]{2,1,0:T(8,128)(2,1)}, u32[]{:S(2)}) copy-start(bf16[4,128,512]{2,1,0:T(8,128)(2,1)} %copy-done.2) | copy-start | bytes 1572868
  196.4 28.0 %collective-permute-start.16 = (bf16[1024,512]{1,0:T(8,128)(2,1)S(1)}, bf16[1024,512]{1,0:T(8,128)(2,1)S(1)}, u32[]{:S(2)}, u32[]{:S(2)}) collective-permute-start(bf16[1024,512]{1,0:T(8,128)(2,1)S(1)} %input_others.1.refs_5_), channel_id=1, source_target_pairs={{0,2},{2,0},{1,3},{3,1},{4,6},{6,4},{5,7},{7,5},{8,10},{10,8},{9,1... | collective-permute-start | bytes 3145736 | tf_op jit(solution)/shard_map/ppermute | solution.py:503
  198.0 1.9 collective-permute-start.14
  198.0 2.7 %collective-permute-start.15 = (bf16[4,128,512]{2,1,0:T(8,128)(2,1)S(1)}, bf16[4,128,512]{2,1,0:T(8,128)(2,1)S(1)}, u32[]{:S(2)}, u32[]{:S(2)}) collective-permute-start(bf16[4,128,512]{2,1,0:T(8,128)(2,1)S(1)} %get-tuple-element.66), channel_id=1, source_target_pairs={{0,1},{1,0},{2,3},{3,2},{4,5},{5,4},{6,7},{7,6},{8,9},{9,8},{10,11... | collective-permute-start | bytes 1572872 | tf_op jit(solution)/shard_map/ppermute | solution.py:503
  201.4 11.4 %collective-permute-start.17 = (bf16[2,128,512]{2,1,0:T(8,128)(2,1)S(1)}, bf16[2,128,512]{2,1,0:T(8,128)(2,1)S(1)}, u32[]{:S(2)}, u32[]{:S(2)}) collective-permute-start(bf16[2,128,512]{2,1,0:T(8,128)(2,1)S(1)} %get-tuple-element.68), channel_id=1, source_target_pairs={{0,4},{4,8},{8,12},{12,0},{1,5},{5,9},{9,13},{13,1},{2,6},{6,10},{... | collective-permute-start | bytes 786440 | tf_op jit(solution)/shard_map/ppermute | solution.py:503
  204.5 19.1 %collective-permute-start.18 = (bf16[2,128,512]{2,1,0:T(8,128)(2,1)S(1)}, bf16[2,128,512]{2,1,0:T(8,128)(2,1)S(1)}, u32[]{:S(2)}, u32[]{:S(2)}) collective-permute-start(bf16[2,128,512]{2,1,0:T(8,128)(2,1)S(1)} %get-tuple-element.69), channel_id=1, source_target_pairs={{0,8},{4,12},{8,0},{12,4},{1,9},{5,13},{9,1},{13,5},{2,10},{6,14},... | collective-permute-start | bytes 786440 | tf_op jit(solution)/shard_map/ppermute | solution.py:503
  206.1 17.4 %collective-permute-start.19 = (bf16[2,128,512]{2,1,0:T(8,128)(2,1)S(1)}, bf16[2,128,512]{2,1,0:T(8,128)(2,1)S(1)}, u32[]{:S(2)}, u32[]{:S(2)}) collective-permute-start(bf16[2,128,512]{2,1,0:T(8,128)(2,1)S(1)} %get-tuple-element.70), channel_id=1, source_target_pairs={{0,12},{4,0},{8,4},{12,8},{1,13},{5,1},{9,5},{13,9},{2,14},{6,2},{... | collective-permute-start | bytes 786440 | tf_op jit(solution)/shard_map/ppermute | solution.py:503

commit v8 on v7

--- a/solution.py
+++ b/solution.py
@@ -56,7 +56,9 @@
 
 
 def steps_of(sizes):
-    return [(seq, sub) for seq in range(sizes[0]) for sub in range(sizes[1])]
+    far = sorted(range(1, sizes[0]), key=lambda seq: -min(seq, sizes[0] - seq))
+    subs = range(sizes[1])
+    return [(0, 0)] + [(seq, sub) for seq in far for sub in subs] + [(0, sub) for sub in subs if sub]
 
 
 def slots_of(assign, groups, rows):
@@ -292,11 +294,11 @@
         out_ref[...] = jnp.where(low_half((half, LANES)), swap_halves(up), down).astype(BF16)
 
 
-def query_grad_kernel(
-    owners, per_group, slot_rows, me_ref, counts_ref, dense_ref, value_in_ref, out_ref, place_ref, wide_ref, block_ref, *rest
-):
-    sums_ref, centroid_ref = rest[:2]
-    score_refs, grad_probs_refs, both_refs = rest[2:4], rest[4:6], rest[6:8]
+def query_grad_kernel(sizes, per_group, slot_rows, me_ref, counts_ref, dense_ref, value_in_ref, *refs):
+    owners = sizes[0] * sizes[1]
+    out_refs, rest = refs[:owners], refs[owners:]
+    place_ref, wide_ref, block_ref, sums_ref, centroid_ref = rest[:5]
+    score_refs, grad_probs_refs, both_refs = rest[5:7], rest[7:9], rest[9:11]
     half = value_in_ref.shape[1]
     rows = 2 * half
     for source in range(owners):
@@ -346,14 +348,15 @@
             wide_ref[source, pl.ds(start, slot_rows), :] = block_ref[pl.ds(row, slot_rows), :]
 
     for_each_cluster(counts_ref, me_ref, place_ref, owners, per_group, scatter)
-    extra = out_ref.shape[1] - half
+    extra = out_refs[0].shape[0] - half
     centroid = jnp.where(
         low_half((extra, LANES)), centroid_ref[:extra, :], swap_halves(centroid_ref[extra:, :])
     ).astype(BF16)
-    for source in range(owners):
+    for ahead, out_ref in zip(steps_of(sizes), out_refs):
+        source = owner_of(me_ref, ahead, sizes)
         up, down = wide_ref[source, :half, :], wide_ref[source, half:rows, :]
-        out_ref[source, :half, :] = jnp.where(low_half((half, LANES)), up, swap_halves(down)).astype(BF16)
-        out_ref[source, half:, :] = centroid
+        out_ref[:half, :] = jnp.where(low_half((half, LANES)), up, swap_halves(down)).astype(BF16)
+        out_ref[half:, :] = centroid
 
 
 def unfold(home_ref, out_ref, heads, start, half, finish):
@@ -374,8 +377,10 @@
     return x.astype(BF16)
 
 
-def bring_home(heads, home_ref, unsort_ref, sorted_ref, rows_ref):
-    half = sorted_ref.shape[0] * heads // home_ref.shape[0] // 2
+def bring_home(sizes, heads, pieces, unsort_ref, home_ref, sorted_ref, rows_ref):
+    for source, piece in pieces:
+        home_ref[source] = piece
+    half = sorted_ref.shape[0] * heads // (sizes[0] * sizes[1]) // 2
     unfold(home_ref, sorted_ref, heads, 0, half, to_half)
     toks = rows_ref.shape[0]
     step = min(512, toks)
@@ -406,57 +411,70 @@
 def value_home_kernel(sizes, heads, me_ref, turned_ref, unsort_ref, *refs):
     part_refs, rows_ref, sub_refs = refs[: -4 - sizes[1]], refs[-4 - sizes[1]], refs[-3 - sizes[1] : -3]
     home_ref, sorted_ref, whole_ref = refs[-3:]
-    for ahead, part_ref in zip(steps_of(sizes), part_refs):
-        home_ref[source_of(me_ref, ahead, sizes)] = part_ref[...]
-    bring_home(heads, home_ref, unsort_ref, sorted_ref, rows_ref)
+    pieces = [
+        (source_of(me_ref, ahead, sizes), part_ref[...]) for ahead, part_ref in zip(steps_of(sizes), part_refs)
+    ]
+    bring_home(sizes, heads, pieces, unsort_ref, home_ref, sorted_ref, rows_ref)
     weight_partial(sizes, me_ref, turned_ref, rows_ref, whole_ref, sub_refs)
 
 
-def query_home_kernel(sizes, heads, factor, me_ref, turned_ref, unsort_ref, home_ref, *refs):
-    sub_refs, (rows_ref, centroid_ref, sorted_ref, whole_ref) = refs[:-4], refs[-4:]
-    bring_home(heads, home_ref, unsort_ref, sorted_ref, rows_ref)
-    half = sorted_ref.shape[0] * heads // (sizes[0] * sizes[1]) // 2
-    unfold(home_ref, centroid_ref, heads, half, home_ref.shape[1] - half, lambda x: x * factor)
-    weight_partial(sizes, me_ref, turned_ref, rows_ref, whole_ref, sub_refs)
-
-
-def input_grad_kernel(first, parts, me_ref, rows_ref, value_rows_ref, w_query_ref, w_value_ref, *out_refs):
+def input_partial(me_ref, ahead, parts, rows_ref, value_rows_ref, w_query_ref, w_value_ref, out_ref):
     toks = rows_ref.shape[0]
     columns = w_query_ref.shape[0] // parts
     step = min(512, toks)
-    for k, out_ref in enumerate(out_refs):
-        dest = lax.rem(me_ref[2] + (first + k), jnp.int32(parts))
-        mine = pl.ds(pl.multiple_of(dest * columns, columns), columns)
-
-        @pl.loop(0, toks // step)
-        def _(i):
-            where = pl.ds(pl.multiple_of(i * step, step), step)
-            total = dot_nt(rows_ref[where, :], w_query_ref[mine, :])
-            total = total + dot_nt(value_rows_ref[where, :], w_value_ref[mine, :])
-            out_ref[where, :] = total.astype(BF16)
+    dest = lax.rem(me_ref[2] + ahead, jnp.int32(parts))
+    mine = pl.ds(pl.multiple_of(dest * columns, columns), columns)
+
+    @pl.loop(0, toks // step)
+    def _(i):
+        where = pl.ds(pl.multiple_of(i * step, step), step)
+        total = dot_nt(rows_ref[where, :], w_query_ref[mine, :])
+        total = total + dot_nt(value_rows_ref[where, :], w_value_ref[mine, :])
+        out_ref[where, :] = total.astype(BF16)
+
+
+def query_home_kernel(
+    sizes, heads, factor, parts, me_ref, unsort_ref, value_rows_ref, w_query_ref, w_value_ref, *refs
+):
+    part_refs, out_refs, (rows_ref, centroid_ref, home_ref, sorted_ref) = (
+        refs[: -3 - parts],
+        refs[-3 - parts : -4],
+        refs[-4:],
+    )
+    pieces = [
+        (source_of(me_ref, ahead, sizes), part_ref[...]) for ahead, part_ref in zip(steps_of(sizes), part_refs)
+    ]
+    bring_home(sizes, heads, pieces, unsort_ref, home_ref, sorted_ref, rows_ref)
+    half = sorted_ref.shape[0] * heads // (sizes[0] * sizes[1]) // 2
+    unfold(home_ref, centroid_ref, heads, half, home_ref.shape[1] - half, lambda x: x * factor)
+    for ahead, out_ref in enumerate(out_refs):
+        input_partial(me_ref, ahead + 1, parts, rows_ref, value_rows_ref, w_query_ref, w_value_ref, out_ref)
+
+
+def query_weight_kernel(
+    sizes, parts, me_ref, turned_ref, rows_ref, value_rows_ref, w_query_ref, w_value_ref, *refs
+):
+    sub_refs, out_ref, whole_ref = refs[:-2], refs[-2], refs[-1]
+    weight_partial(sizes, me_ref, turned_ref, rows_ref, whole_ref, sub_refs)
+    input_partial(me_ref, 0, parts, rows_ref, value_rows_ref, w_query_ref, w_value_ref, out_ref)
 
 
 def fold_subs_kernel(me_ref, *refs):
     seqs = refs[0].shape[0]
     terms, out_refs = refs[:-seqs], refs[-seqs:]
-    each = len(terms) // 2
     for ahead, out_ref in enumerate(out_refs):
         seq = lax.rem(me_ref[0] + ahead, jnp.int32(seqs))
-        for which in range(2):
-            total = terms[which * each][seq].astype(F32)
-            for term in terms[which * each + 1 : (which + 1) * each]:
-                total = total + term[seq].astype(F32)
-            out_ref[which] = total.astype(BF16)
+        total = terms[0][seq].astype(F32)
+        for term in terms[1:]:
+            total = total + term[seq].astype(F32)
+        out_ref[...] = total.astype(BF16)
 
 
 def sum_kernel(*refs):
-    outs = 2 if len(refs[0].shape) == 3 else 1
-    terms, out_refs = refs[:-outs], refs[-outs:]
-    for which, out_ref in enumerate(out_refs):
-        total = (terms[0][which] if outs == 2 else terms[0][...]).astype(F32)
-        for term in terms[1:]:
-            total = total + (term[which] if outs == 2 else term[...]).astype(F32)
-        out_ref[...] = total.astype(out_ref.dtype)
+    total = refs[0][...].astype(F32)
+    for ref in refs[1:-1]:
+        total = total + ref[...].astype(F32)
+    refs[-1][...] = total.astype(refs[-1].dtype)
 
 
 def call(kernel, outs, inputs, smem=(0,), in_place=(), after=(), scratch=(), flops=0, vmem=24, name=None):
@@ -507,8 +525,23 @@
     return [parts[0]] + [shift(parts[ahead], axis, ahead) for ahead in range(1, len(parts))]
 
 
+def fold_subs(me, by_sub, name, after=()):
+    seqs, piece, columns = by_sub[0].shape
+    return call(
+        fold_subs_kernel,
+        (jax.ShapeDtypeStruct((piece, columns), BF16),) * seqs,
+        (me, *pass_round(by_sub, "sub")),
+        after=after,
+        name=name,
+    )
+
+
 def all_to_all(rows):
     return lax.all_to_all(rows, OWNERS, split_axis=0, concat_axis=0, tiled=True)
+
+
+def add_up(terms, dtype, name):
+    return call(sum_kernel, jax.ShapeDtypeStruct(terms[0].shape, dtype), tuple(terms), smem=(), name=name)
 
 
 def on_device(tokens_in, w_query, w_value, cotangent, assignment):
@@ -566,6 +599,7 @@
         flops=2 * toks * width * width_dev + 2 * slots * toks * width_dev,
         name="project_value",
     )
+    send_value, _ = lax.optimization_barrier((send_value, got_mixed[1:4]))
     got_value = all_to_all(send_value)
     blocks = per_group * capacity // BLOCK_ROWS
     held = blocks + (LEAD + 4) * UNROLL
@@ -581,6 +615,7 @@
         + several(1, held * BLOCK_ROWS, LANES)
         + (shape((owners, LANES), jnp.int32),),
         (me, *got_mixed),
+        after=[unsort],
         scratch=[pltpu.SMEM((owners, LANES), jnp.int32), place, tall, dense_rows, tall]
         + [group_f32] * 2
         + [group_b16] * 2,
@@ -590,8 +625,8 @@
     )
     home_value = exchange(back_value, sizes)
     back_query = call(
-        functools.partial(query_grad_kernel, owners, per_group, slot_rows),
-        shape((owners, half + extra, LANES), BF16),
+        functools.partial(query_grad_kernel, sizes, per_group, slot_rows),
+        several(owners, half + extra, LANES),
         (me, counts, dense, got_value),
         smem=(0, 1),
         scratch=[place, tall, dense_rows, pltpu.VMEM((held, LANES), F32), pltpu.VMEM((2 * extra, LANES), F32)]
@@ -601,63 +636,48 @@
         vmem=48,
         name="query_grad",
     )
-    home_query = all_to_all(back_query)
+    home_query = exchange(back_query, sizes)
     weight_flops = 2 * toks * width * width_dev
     home_flops = 2 * slots * toks * width_dev
-    piece = width // owners
-    sub_shapes = several(sizes[1], sizes[0], piece, width_dev)
+    sub_shapes = several(sizes[1], sizes[0], width // owners, width_dev)
     whole = pltpu.VMEM((width, width_dev), BF16)
     sorted_rows = pltpu.VMEM((slots, width_dev), BF16)
     value_rows, *value_weight = call(
         functools.partial(value_home_kernel, sizes, heads),
         several(1, toks, width_dev) + sub_shapes,
         (me, turned, unsort, *home_value),
+        after=back_query[:1],
         scratch=[pltpu.VMEM((owners, half, LANES), BF16), sorted_rows, whole],
         flops=weight_flops + home_flops,
         name="value_home",
     )
-    *query_weight, query_rows, centroid_grad = call(
-        functools.partial(query_home_kernel, sizes, heads, (CLUSTERS / (toks * owners)) ** 0.5),
-        sub_shapes + several(1, toks, width_dev) + (shape((groups * 2 * extra, width_dev), F32),),
-        (me, turned, unsort, home_query),
-        after=[value_rows],
-        scratch=[sorted_rows, whole],
+    value_weight = fold_subs(me, value_weight, "value_subs")
+    *partials, query_rows, centroid_grad = call(
+        functools.partial(query_home_kernel, sizes, heads, (CLUSTERS / (toks * owners)) ** 0.5, parts),
+        several(parts - 1, toks, columns)
+        + several(1, toks, width_dev)
+        + (shape((groups * 2 * extra, width_dev), F32),),
+        (me, unsort, value_rows, w_query, w_value, *home_query),
+        after=value_weight,
+        scratch=[pltpu.VMEM((owners, half + extra, LANES), BF16), sorted_rows],
         flops=weight_flops + home_flops,
         name="query_home",
     )
-    partials = call(
-        functools.partial(input_grad_kernel, 1, parts),
-        several(parts - 1, toks, columns),
-        (me, query_rows, value_rows, w_query, w_value),
-        flops=weight_flops * (parts - 1) * 2 // parts,
-        name="input_others",
-    )
     arrived = [shift(partial, "head", k + 1) for k, partial in enumerate(partials)]
-    by_seq = call(
-        fold_subs_kernel,
-        several(sizes[0], 2, piece, width_dev),
-        (me, *pass_round(value_weight, "sub"), *pass_round(query_weight, "sub")),
-        after=partials,
-        name="weight_subs",
-    )
-    own = call(
-        functools.partial(input_grad_kernel, 0, parts),
-        several(1, toks, columns),
-        (me, query_rows, value_rows, w_query, w_value),
-        after=by_seq[:1],
-        flops=weight_flops * 2 // parts,
-        name="input_own",
-    )
-    grad_wv, grad_wq = call(
-        sum_kernel,
-        (shape((piece, width_dev), F32),) * 2,
-        tuple(pass_round(by_seq, "seq")),
-        smem=(),
-        name="weight_sum",
-    )
-    grad_input = call(
-        sum_kernel, shape((toks, columns), BF16), tuple(list(own) + arrived), smem=(), name="input_sum"
-    )
+    value_weight, _ = lax.optimization_barrier((value_weight, home_query))
+    value_weight = pass_round(value_weight, "seq")
+    *query_weight, own = call(
+        functools.partial(query_weight_kernel, sizes, parts),
+        sub_shapes + several(1, toks, columns),
+        (me, turned, query_rows, value_rows, w_query, w_value),
+        scratch=[whole],
+        flops=2 * weight_flops,
+        name="query_weight",
+    )
+    query_weight = pass_round(fold_subs(me, query_weight, "query_subs"), "seq")
+    grad_wv = add_up(value_weight, F32, "value_sum")
+    grad_wq = add_up(query_weight, F32, "query_sum")
+    grad_input = add_up([own] + arrived, BF16, "input_sum")
     if groups > 1:
         centroid_grad = centroid_grad.reshape(groups, 2 * extra, width_dev)[:, :per_group]
         centroid_grad = centroid_grad.reshape(CLUSTERS, width_dev)

time: 230 us -> 210 us (0.913); the launches traced: 226 us -> 210 us
  waiting for transfers between devices: 108 us -> 99.4 us
  local copies, waits for them, and re-layouts: 12.4 us -> 6.61 us
  starting transfers between devices: 45.2 us -> 42.6 us
    all_to_all x2 -> x1, starting transfers between devices: 20.9 us -> 4.75 us  [all_to_all(): return lax.all_to_all(rows, OWNERS, split_axis=0, concat_axis=0, tiled=True)]
    ppermute x14 -> x21, starting transfers between devices: 16.8 us -> 28.8 us  [exchange(): out.append(part if ahead == (0, 0) else lax.ppermute(part, OWNERS, moves))]
    ppermute x14 -> x21, waiting for transfers between devices: 91.2 us -> 83.5 us  [exchange(): out.append(part if ahead == (0, 0) else lax.ppermute(part, OWNERS, moves))]
    unnamed x40 -> x26, local copies, waits for them, and re-layouts: 12.4 us -> 6.61 us
    ppermute x6 -> x9, starting transfers between devices: 7.56 us -> 9.03 us  [shift(): lax.ppermute(part, axis, [(i, (i + ahead) % size) for i in range(size)])]
    pallas_call x11 -> x12, Pallas kernels: 58.7 us -> 59.8 us  [call(): pl.pallas_call(body, out_shape=outs, in_specs=specs, out_specs=jax.tree.m...]
    ppermute x6 -> x9, waiting for transfers between devices: 16.7 us -> 15.9 us  [shift(): lax.ppermute(part, axis, [(i, (i + ahead) % size) for i in range(size)])]
  transfers between devices with their start and end apart: 22 -> 31, of which waited for: 13 -> 14; matrix products, arithmetic and copies ran while one was open for 0% -> 0% of each run, Pallas kernels for 9% -> 20%
where the time goes in v8:
time: 210 us
  waiting for transfers between devices  99.4 us (47%)
  Pallas kernels  59.8 us (28%)
  starting transfers between devices  42.6 us (20%)
  local copies, waits for them, and re-layouts  6.61 us (3%)
    ppermute x21, waiting for transfers between devices, exchange(): out.append(part if ahead == (0, 0) else lax.ppermute(part, OWNERS, moves))  83.5 us
    pallas_call x12, Pallas kernels, call(): pl.pallas_call(body, out_shape=outs, in_specs=specs, out_specs=jax.tree.m...  59.8 us
    ppermute x21, starting transfers between devices, exchange(): out.append(part if ahead == (0, 0) else lax.ppermute(part, OWNERS, moves))  28.8 us
    ppermute x9, waiting for transfers between devices, shift(): lax.ppermute(part, axis, [(i, (i + ahead) % size) for i in range(size)])  15.9 us
    ppermute x9, starting transfers between devices, shift(): lax.ppermute(part, axis, [(i, (i + ahead) % size) for i in range(size)])  9.03 us
    unnamed x26, local copies, waits for them, and re-layouts  6.61 us
    all_to_all x1, starting transfers between devices, all_to_all(): return lax.all_to_all(rows, OWNERS, split_axis=0, concat_axis=0, tiled=True)  4.75 us
  transfers between devices with their start and end apart: 31, of which 14 were waited for; matrix products, arithmetic and copies ran while one was open for 0% of the time, Pallas kernels for 20%

profile of v8, /device:TPU:0, one launch (start us, length us, event | category | flops | bytes accessed | tf_op | source)
XLA Modules:
  0.0 209.9 jit_solution(16862008759929583498)
XLA Ops:
  0.6 0.7 pad_add_fusion.refs_0_
  1.3 8.6 %project_query.1 = (bf16[1040,128]{1,0:T(8,128)(2,1)}, bf16[1040,128]{1,0:T(8,128)(2,1)}, bf16[1040,128]{1,0:T(8,128)(2,1)}, bf16[1040,128]{1,0:T(8,128)(2,1)}, ...) custom-call(s32[4]{0:T(128)} %pad_add_fusion.refs_0_, ...), custom_call_target="tpu_custom_call" | custom-call | flops 3221225472 | bytes 6332432 | tf_op jit(solution)/shard_map/project_query/pallas_call | solution.py:493
  9.9 4.1 %collective-permute-start = (bf16[1040,128]{1,0:T(8,128)(2,1)}, bf16[1040,128]{1,0:T(8,128)(2,1)S(1)}, u32[]{:S(2)}, u32[]{:S(2)}) collective-permute-start(bf16[1040,128]{1,0:T(8,128)(2,1)} %get-tuple-element.60), channel_id=1, source_target_pairs={{0,8},{8,0},{9,1},{4,12},{5,13},{12,4},{13,5},{1,9},{2,10},{10,2},... | collective-permute-start | bytes 798728 | tf_op jit(solution)/shard_map/ppermute | solution.py:515
  14.0 1.6 collective-permute-start.2
  15.6 0.7 copy-done.12
  16.3 5.1 %project_value.1 = (bf16[8,512,128]{2,1,0:T(8,128)(2,1)}, bf16[1024,1024]{1,0:T(8,128)(2,1)S(1)}, bf16[1024,1024]{1,0:T(8,128)(2,1)S(1)}) custom-call(s32[1,1024]{1,0:T(1,128)S(1)} %copy-done.12, bf16[1024,1024]{1,0:T(8,128)(2,1)S(1)} %copy-done.1, bf16[1024,512]{1,0:T(8,128)(2,1)S(1)} %copy-done.3), custom_call_target="tpu_custom_call" | custom-call | flops 2147483648 | bytes 8392704 | tf_op jit(solution)/shard_map/project_value/pallas_call | solution.py:493
  21.4 1.4 copy-done.4
  22.8 1.3 copy-done.7
  24.1 14.5 %collective-permute-done.refs_2_ = bf16[1040,128]{1,0:T(8,128)(2,1)S(1)} collective-permute-done((bf16[1040,128]{1,0:T(8,128)(2,1)}, bf16[1040,128]{1,0:T(8,128)(2,1)S(1)}, u32[]{:S(2)}, u32[]{:S(2)}) %collective-permute-start) | collective-permute-done | bytes 266272 | tf_op jit(solution)/shard_map/ppermute | solution.py:515
  38.5 4.0 %collective-permute-done.1.refs_3_ = bf16[1040,128]{1,0:T(8,128)(2,1)S(1)} collective-permute-done((bf16[1040,128]{1,0:T(8,128)(2,1)}, bf16[1040,128]{1,0:T(8,128)(2,1)S(1)}, u32[]{:S(2)}, u32[]{:S(2)}) %collective-permute-start.1) | collective-permute-done | bytes 266272 | tf_op jit(solution)/shard_map/ppermute | solution.py:515
  42.6 4.7 %all-to-all-start = ((bf16[8,512,128]{2,1,0:T(8,128)(2,1)}), bf16[8,512,128]{2,1,0:T(8,128)(2,1)S(1)}, u32[]{:S(2)}, u32[]{:S(2)}) async-start(bf16[8,512,128]{2,1,0:T(8,128)(2,1)} %get-tuple-element.78), calls=%async_computation | async-start | bytes 2097152 | tf_op jit(solution)/shard_map/all_to_all | solution.py:540
  47.3 1.8 collective-permute-start.3
  49.1 2.2 %collective-permute-start.4 = (bf16[1040,128]{1,0:T(8,128)(2,1)}, bf16[1040,128]{1,0:T(8,128)(2,1)S(1)}, u32[]{:S(2)}, u32[]{:S(2)}) collective-permute-start(bf16[1040,128]{1,0:T(8,128)(2,1)} %get-tuple-element.64), channel_id=1, source_target_pairs={{0,12},{8,4},{9,5},{4,0},{5,1},{12,8},{13,9},{1,13},{2,14},{10,6},... | collective-permute-start | bytes 798728 | tf_op jit(solution)/shard_map/ppermute | solution.py:515
  51.3 1.4 collective-permute-start.5
  53.1 21.6 %collective-permute-done.3.refs_5_ = bf16[1040,128]{1,0:T(8,128)(2,1)S(1)} collective-permute-done((bf16[1040,128]{1,0:T(8,128)(2,1)}, bf16[1040,128]{1,0:T(8,128)(2,1)S(1)}, u32[]{:S(2)}, u32[]{:S(2)}) %collective-permute-start.3) | collective-permute-done | bytes 266272 | tf_op jit(solution)/shard_map/ppermute | solution.py:515
  74.7 2.4 %collective-permute-done.4.refs_6_ = bf16[1040,128]{1,0:T(8,128)(2,1)S(1)} collective-permute-done((bf16[1040,128]{1,0:T(8,128)(2,1)}, bf16[1040,128]{1,0:T(8,128)(2,1)S(1)}, u32[]{:S(2)}, u32[]{:S(2)}) %collective-permute-start.4) | collective-permute-done | bytes 266272 | tf_op jit(solution)/shard_map/ppermute | solution.py:515
  77.1 7.0 %collective-permute-done.5.refs_7_ = bf16[1040,128]{1,0:T(8,128)(2,1)S(1)} collective-permute-done((bf16[1040,128]{1,0:T(8,128)(2,1)}, bf16[1040,128]{1,0:T(8,128)(2,1)S(1)}, u32[]{:S(2)}, u32[]{:S(2)}) %collective-permute-start.5) | collective-permute-done | bytes 266272 | tf_op jit(solution)/shard_map/ppermute | solution.py:515
  84.1 1.6 copy-done.5
  85.7 0.9 copy-done.11
  86.6 13.6 %value_grad.1 = (bf16[512,128]{1,0:T(8,128)(2,1)S(1)}, bf16[512,128]{1,0:T(8,128)(2,1)S(1)}, bf16[512,128]{1,0:T(8,128)(2,1)S(1)}, bf16[512,128]{1,0:T(8,128)(2,...) custom-call(s32[4]{0:T(128)S(1)} %copy-done, ...), custom_call_target="tpu_custom_call" | custom-call | flops 2147483648 | bytes 8163344 | tf_op jit(solution)/shard_map/value_grad/pallas_call | solution.py:493
  100.9 7.4 %collective-permute-start.7 = (bf16[512,128]{1,0:T(8,128)(2,1)S(1)}, bf16[512,128]{1,0:T(8,128)(2,1)S(1)}, u32[]{:S(2)}, u32[]{:S(2)}) collective-permute-start(bf16[512,128]{1,0:T(8,128)(2,1)S(1)} %get-tuple-element.68), channel_id=1, source_target_pairs={{0,8},{8,0},{9,1},{4,12},{5,13},{12,4},{13,5},{1,9},{2,10},{10,2},... | collective-permute-start | bytes 393224 | tf_op jit(solution)/shard_map/ppermute | solution.py:515
  108.3 2.3 %collective-permute-start.9 = (bf16[512,128]{1,0:T(8,128)(2,1)}, bf16[512,128]{1,0:T(8,128)(2,1)S(1)}, u32[]{:S(2)}, u32[]{:S(2)}) collective-permute-start(bf16[512,128]{1,0:T(8,128)(2,1)} %get-tuple-element.70), channel_id=1, source_target_pairs={{0,4},{8,12},{9,13},{4,8},{5,9},{12,0},{13,1},{1,5},{2,6},{10,14},... | collective-permute-start | bytes 393224 | tf_op jit(solution)/shard_map/ppermute | solution.py:515
  111.2 3.0 %collective-permute-start.11 = (bf16[512,128]{1,0:T(8,128)(2,1)}, bf16[512,128]{1,0:T(8,128)(2,1)S(1)}, u32[]{:S(2)}, u32[]{:S(2)}) collective-permute-start(bf16[512,128]{1,0:T(8,128)(2,1)} %get-tuple-element.72), channel_id=1, source_target_pairs={{0,12},{8,4},{9,5},{4,0},{5,1},{12,8},{13,9},{1,13},{2,14},{10,6},... | collective-permute-start | bytes 393224 | tf_op jit(solution)/shard_map/ppermute | solution.py:515
  114.2 9.6 %collective-permute-done.7.refs_4_ = bf16[512,128]{1,0:T(8,128)(2,1)S(1)} collective-permute-done((bf16[512,128]{1,0:T(8,128)(2,1)S(1)}, bf16[512,128]{1,0:T(8,128)(2,1)S(1)}, u32[]{:S(2)}, u32[]{:S(2)}) %collective-permute-start.7) | collective-permute-done | bytes 131104 | tf_op jit(solution)/shard_map/ppermute | solution.py:515
  123.8 1.8 collective-permute-done.8.refs_5_
  125.6 0.8 collective-permute-start.13
  126.4 16.6 %query_grad.1 = (bf16[544,128]{1,0:T(8,128)(2,1)S(1)}, bf16[544,128]{1,0:T(8,128)(2,1)S(1)}, bf16[544,128]{1,0:T(8,128)(2,1)S(1)}, bf16[544,128]{1,0:T(8,128)(2,...) custom-call(s32[4]{0:T(128)S(1)} %copy-done, ...), custom_call_target="tpu_custom_call" | custom-call | flops 3221225472 | bytes 7147536 | tf_op jit(solution)/shard_map/query_grad/pallas_call | solution.py:493
  143.1 4.4 %value_home.1 = (bf16[1024,512]{1,0:T(8,128)(2,1)S(1)}, bf16[4,128,512]{2,1,0:T(8,128)(2,1)S(1)}, bf16[4,128,512]{2,1,0:T(8,128)(2,1)S(1)}) custom-call(s32[4]{0:T(128)S(1)} %copy-done, bf16[1024,1024]{1,0:T(8,128)(2,1)S(1)} %copy-done.8, bf16[1024,1024]{1,0:T(8,128)(2,1)S(1)} %copy-done.6, bf16[512,128]{1,0:T(8,128)(2,1)S(1)} %copy-done.10, ...), custom_call_target="tpu_custom_call" | custom-call | flops 2147483648 | bytes 7340048 | tf_op jit(solution)/shard_map/value_home/pallas_call | solution.py:493
  147.8 2.5 %collective-permute-start.15 = (bf16[544,128]{1,0:T(8,128)(2,1)S(1)}, bf16[544,128]{1,0:T(8,128)(2,1)S(1)}, u32[]{:S(2)}, u32[]{:S(2)}) collective-permute-start(bf16[544,128]{1,0:T(8,128)(2,1)S(1)} %get-tuple-element.82), channel_id=1, source_target_pairs={{0,9},{8,1},{9,0},{4,13},{5,12},{12,5},{13,4},{1,8},{2,11},{10,3},... | collective-permute-start | bytes 417800 | tf_op jit(solution)/shard_map/ppermute | solution.py:515
  150.7 14.8 %collective-permute-done.14.refs_6_ = bf16[544,128]{1,0:T(8,128)(2,1)S(1)} collective-permute-done((bf16[544,128]{1,0:T(8,128)(2,1)S(1)}, bf16[544,128]{1,0:T(8,128)(2,1)S(1)}, u32[]{:S(2)}, u32[]{:S(2)}) %collective-permute-start.14) | collective-permute-done | bytes 139296 | tf_op jit(solution)/shard_map/ppermute | solution.py:515
  165.5 2.9 %collective-permute-done.15.refs_7_ = bf16[544,128]{1,0:T(8,128)(2,1)S(1)} collective-permute-done((bf16[544,128]{1,0:T(8,128)(2,1)S(1)}, bf16[544,128]{1,0:T(8,128)(2,1)S(1)}, u32[]{:S(2)}, u32[]{:S(2)}) %collective-permute-start.15) | collective-permute-done | bytes 139296 | tf_op jit(solution)/shard_map/ppermute | solution.py:515
  168.5 0.7 value_subs.1
  169.2 2.2 %collective-permute-done.18.refs_10_ = bf16[544,128]{1,0:T(8,128)(2,1)S(1)} collective-permute-done((bf16[544,128]{1,0:T(8,128)(2,1)S(1)}, bf16[544,128]{1,0:T(8,128)(2,1)S(1)}, u32[]{:S(2)}, u32[]{:S(2)}) %collective-permute-start.18) | collective-permute-done | bytes 139296 | tf_op jit(solution)/shard_map/ppermute | solution.py:515
  171.4 2.7 %collective-permute-done.19.refs_11_ = bf16[544,128]{1,0:T(8,128)(2,1)S(1)} collective-permute-done((bf16[544,128]{1,0:T(8,128)(2,1)S(1)}, bf16[544,128]{1,0:T(8,128)(2,1)S(1)}, u32[]{:S(2)}, u32[]{:S(2)}) %collective-permute-start.19) | collective-permute-done | bytes 139296 | tf_op jit(solution)/shard_map/ppermute | solution.py:515
  174.1 4.0 %query_home.1 = (bf16[1024,512]{1,0:T(8,128)(2,1)S(1)}, bf16[1024,512]{1,0:T(8,128)(2,1)S(1)}, f32[64,512]{1,0:T(8,128)}) custom-call(s32[4]{0:T(128)S(1)} %copy-done, bf16[1024,1024]{1,0:T(8,128)(2,1)S(1)} %copy-done.6, bf16[1024,512]{1,0:T(8,128)(2,1)S(1)} %get-tuple-element.80.refs_2_.refs_3_, bf16[1024,512]{1,0:T(8,128)(2,1)S(1)} %copy-done.2, ...), custom_call_target="tpu_custom_call" | custom-call | flops 2147483648 | bytes 8585232 | tf_op jit(solution)/shard_map/query_home/pallas_call | solution.py:493
  178.1 1.6 collective-permute-start.22
  179.7 3.5 %query_weight.1 = (bf16[4,128,512]{2,1,0:T(8,128)(2,1)S(1)}, bf16[4,128,512]{2,1,0:T(8,128)(2,1)S(1)}, bf16[1024,512]{1,0:T(8,128)(2,1)S(1)}) custom-call(s32[4]{0:T(128)S(1)} %copy-done, bf16[1024,1024]{1,0:T(8,128)(2,1)S(1)} %copy-done.8, bf16[1024,512]{1,0:T(8,128)(2,1)S(1)} %get-tuple-element.94.refs_2_, ...), custom_call_target="tpu_custom_call" | custom-call | flops 2147483648 | bytes 8388624 | tf_op jit(solution)/shard_map/query_weight/pallas_call | solution.py:493
  183.3 0.8 collective-permute-start.27
  184.1 1.3 collective-permute-start.28
  185.4 1.8 collective-permute-start.29
  187.1 0.7 query_subs.1
  188.4 3.1 %collective-permute-done.27.refs_1_ = bf16[128,512]{1,0:T(8,128)(2,1)S(1)} collective-permute-done((bf16[128,512]{1,0:T(8,128)(2,1)S(1)}, bf16[128,512]{1,0:T(8,128)(2,1)S(1)}, u32[]{:S(2)}, u32[]{:S(2)}) %collective-permute-start.27) | collective-permute-done | bytes 131104 | tf_op jit(solution)/shard_map/ppermute | solution.py:521
  191.6 5.6 %collective-permute-done.28.refs_2_ = bf16[128,512]{1,0:T(8,128)(2,1)S(1)} collective-permute-done((bf16[128,512]{1,0:T(8,128)(2,1)S(1)}, bf16[128,512]{1,0:T(8,128)(2,1)S(1)}, u32[]{:S(2)}, u32[]{:S(2)}) %collective-permute-start.28) | collective-permute-done | bytes 131104 | tf_op jit(solution)/shard_map/ppermute | solution.py:521
  197.2 2.8 %collective-permute-start.26 = (bf16[128,512]{1,0:T(8,128)(2,1)S(1)}, bf16[128,512]{1,0:T(8,128)(2,1)S(1)}, u32[]{:S(2)}, u32[]{:S(2)}) collective-permute-start(bf16[128,512]{1,0:T(8,128)(2,1)S(1)} %get-tuple-element.102), channel_id=1, source_target_pairs={{0,12},{4,0},{8,4},{12,8},{1,13},{5,1},{9,5},{13,9},{2,14},{6,2},{... | collective-permute-start | bytes 393224 | tf_op jit(solution)/shard_map/ppermute | solution.py:521
  200.0 0.8 value_sum.1
  200.7 7.2 %collective-permute-done.25.refs_2_ = bf16[128,512]{1,0:T(8,128)(2,1)S(1)} collective-permute-done((bf16[128,512]{1,0:T(8,128)(2,1)S(1)}, bf16[128,512]{1,0:T(8,128)(2,1)S(1)}, u32[]{:S(2)}, u32[]{:S(2)}) %collective-permute-start.25) | collective-permute-done | bytes 131104 | tf_op jit(solution)/shard_map/ppermute | solution.py:521
  207.9 0.8 query_sum.1
  208.7 1.2 input_sum.1
  (53 shorter events, 3.3 us)
Async XLA Ops:
  1.3 14.3 %copy-start.1 = (bf16[1024,1024]{1,0:T(8,128)(2,1)S(1)}, bf16[1024,1024]{1,0:T(8,128)(2,1)}, u32[]{:S(2)}) copy-start(bf16[1024,1024]{1,0:T(8,128)(2,1)} %refs_1_.1) | copy-start | bytes 6291460
  1.3 14.3 %copy-start.3 = (bf16[1024,512]{1,0:T(8,128)(2,1)S(1)}, bf16[1024,512]{1,0:T(8,128)(2,1)}, u32[]{:S(2)}) copy-start(bf16[1024,512]{1,0:T(8,128)(2,1)} %refs_5_.1) | copy-start | bytes 3145732
  9.9 28.6 %collective-permute-start = (bf16[1040,128]{1,0:T(8,128)(2,1)}, bf16[1040,128]{1,0:T(8,128)(2,1)S(1)}, u32[]{:S(2)}, u32[]{:S(2)}) collective-permute-start(bf16[1040,128]{1,0:T(8,128)(2,1)} %get-tuple-element.60), channel_id=1, source_target_pairs={{0,8},{8,0},{9,1},{4,12},{5,13},{12,4},{13,5},{1,9},{2,10},{10,2},... | collective-permute-start | bytes 798728 | tf_op jit(solution)/shard_map/ppermute | solution.py:515
  14.0 28.6 %collective-permute-start.1 = (bf16[1040,128]{1,0:T(8,128)(2,1)}, bf16[1040,128]{1,0:T(8,128)(2,1)S(1)}, u32[]{:S(2)}, u32[]{:S(2)}) collective-permute-start(bf16[1040,128]{1,0:T(8,128)(2,1)} %get-tuple-element.61), channel_id=1, source_target_pairs={{0,9},{8,1},{9,0},{4,13},{5,12},{12,5},{13,4},{1,8},{2,11},{10,3},... | collective-permute-start | bytes 798728 | tf_op jit(solution)/shard_map/ppermute | solution.py:515
  14.0 28.6 %collective-permute-start.2 = (bf16[1040,128]{1,0:T(8,128)(2,1)}, bf16[1040,128]{1,0:T(8,128)(2,1)S(1)}, u32[]{:S(2)}, u32[]{:S(2)}) collective-permute-start(bf16[1040,128]{1,0:T(8,128)(2,1)} %get-tuple-element.62), channel_id=1, source_target_pairs={{0,4},{8,12},{9,13},{4,8},{5,9},{12,0},{13,1},{1,5},{2,6},{10,14},... | collective-permute-start | bytes 798728 | tf_op jit(solution)/shard_map/ppermute | solution.py:515
  15.6 0.7 copy-start.12
  21.4 1.4 copy-start.4
  22.8 1.3 copy-start.7
  24.1 60.0 %copy-start = (s32[4]{0:T(128)S(1)}, s32[4]{0:T(128)}, u32[]{:S(2)}) copy-start(s32[4]{0:T(128)} %pad_add_fusion.refs_0_) | copy-start | bytes 52
  42.6 83.8 %all-to-all-start = ((bf16[8,512,128]{2,1,0:T(8,128)(2,1)}), bf16[8,512,128]{2,1,0:T(8,128)(2,1)S(1)}, u32[]{:S(2)}, u32[]{:S(2)}) async-start(bf16[8,512,128]{2,1,0:T(8,128)(2,1)} %get-tuple-element.78), calls=%async_computation | async-start | bytes 2097152 | tf_op jit(solution)/shard_map/all_to_all | solution.py:540
  47.3 27.3 %collective-permute-start.3 = (bf16[1040,128]{1,0:T(8,128)(2,1)}, bf16[1040,128]{1,0:T(8,128)(2,1)S(1)}, u32[]{:S(2)}, u32[]{:S(2)}) collective-permute-start(bf16[1040,128]{1,0:T(8,128)(2,1)} %get-tuple-element.63), channel_id=1, source_target_pairs={{0,5},{8,13},{9,12},{4,9},{5,8},{12,1},{13,0},{1,4},{2,7},{10,15},... | collective-permute-start | bytes 798728 | tf_op jit(solution)/shard_map/ppermute | solution.py:515
  49.1 28.0 %collective-permute-start.4 = (bf16[1040,128]{1,0:T(8,128)(2,1)}, bf16[1040,128]{1,0:T(8,128)(2,1)S(1)}, u32[]{:S(2)}, u32[]{:S(2)}) collective-permute-start(bf16[1040,128]{1,0:T(8,128)(2,1)} %get-tuple-element.64), channel_id=1, source_target_pairs={{0,12},{8,4},{9,5},{4,0},{5,1},{12,8},{13,9},{1,13},{2,14},{10,6},... | collective-permute-start | bytes 798728 | tf_op jit(solution)/shard_map/ppermute | solution.py:515
  51.3 32.8 %collective-permute-start.5 = (bf16[1040,128]{1,0:T(8,128)(2,1)}, bf16[1040,128]{1,0:T(8,128)(2,1)S(1)}, u32[]{:S(2)}, u32[]{:S(2)}) collective-permute-start(bf16[1040,128]{1,0:T(8,128)(2,1)} %get-tuple-element.65), channel_id=1, source_target_pairs={{0,13},{8,5},{9,4},{4,1},{5,0},{12,9},{13,8},{1,12},{2,15},{10,7},... | collective-permute-start | bytes 798728 | tf_op jit(solution)/shard_map/ppermute | solution.py:515
  52.6 31.4 %collective-permute-start.6 = (bf16[1040,128]{1,0:T(8,128)(2,1)}, bf16[1040,128]{1,0:T(8,128)(2,1)S(1)}, u32[]{:S(2)}, u32[]{:S(2)}) collective-permute-start(bf16[1040,128]{1,0:T(8,128)(2,1)} %get-tuple-element.66), channel_id=1, source_target_pairs={{0,1},{8,9},{9,8},{4,5},{5,4},{12,13},{13,12},{1,0},{2,3},{10,11},... | collective-permute-start | bytes 798728 | tf_op jit(solution)/shard_map/ppermute | solution.py:515
  84.1 1.6 copy-start.5
  85.7 1.0 copy-start.11
  100.3 0.6 copy-start.9
  100.9 22.9 %collective-permute-start.7 = (bf16[512,128]{1,0:T(8,128)(2,1)S(1)}, bf16[512,128]{1,0:T(8,128)(2,1)S(1)}, u32[]{:S(2)}, u32[]{:S(2)}) collective-permute-start(bf16[512,128]{1,0:T(8,128)(2,1)S(1)} %get-tuple-element.68), channel_id=1, source_target_pairs={{0,8},{8,0},{9,1},{4,12},{5,13},{12,4},{13,5},{1,9},{2,10},{10,2},... | collective-permute-start | bytes 393224 | tf_op jit(solution)/shard_map/ppermute | solution.py:515
  108.3 17.3 %collective-permute-start.8 = (bf16[512,128]{1,0:T(8,128)(2,1)S(1)}, bf16[512,128]{1,0:T(8,128)(2,1)S(1)}, u32[]{:S(2)}, u32[]{:S(2)}) collective-permute-start(bf16[512,128]{1,0:T(8,128)(2,1)S(1)} %get-tuple-element.69), channel_id=1, source_target_pairs={{0,9},{8,1},{9,0},{4,13},{5,12},{12,5},{13,4},{1,8},{2,11},{10,3},... | collective-permute-start | bytes 393224 | tf_op jit(solution)/shard_map/ppermute | solution.py:515
  108.3 34.8 %collective-permute-start.9 = (bf16[512,128]{1,0:T(8,128)(2,1)}, bf16[512,128]{1,0:T(8,128)(2,1)S(1)}, u32[]{:S(2)}, u32[]{:S(2)}) collective-permute-start(bf16[512,128]{1,0:T(8,128)(2,1)} %get-tuple-element.70), channel_id=1, source_target_pairs={{0,4},{8,12},{9,13},{4,8},{5,9},{12,0},{13,1},{1,5},{2,6},{10,14},... | collective-permute-start | bytes 393224 | tf_op jit(solution)/shard_map/ppermute | solution.py:515
  110.6 32.5 %collective-permute-start.10 = (bf16[512,128]{1,0:T(8,128)(2,1)}, bf16[512,128]{1,0:T(8,128)(2,1)S(1)}, u32[]{:S(2)}, u32[]{:S(2)}) collective-permute-start(bf16[512,128]{1,0:T(8,128)(2,1)} %get-tuple-element.71), channel_id=1, source_target_pairs={{0,5},{8,13},{9,12},{4,9},{5,8},{12,1},{13,0},{1,4},{2,7},{10,15},... | collective-permute-start | bytes 393224 | tf_op jit(solution)/shard_map/ppermute | solution.py:515
  111.2 31.8 %collective-permute-start.11 = (bf16[512,128]{1,0:T(8,128)(2,1)}, bf16[512,128]{1,0:T(8,128)(2,1)S(1)}, u32[]{:S(2)}, u32[]{:S(2)}) collective-permute-start(bf16[512,128]{1,0:T(8,128)(2,1)} %get-tuple-element.72), channel_id=1, source_target_pairs={{0,12},{8,4},{9,5},{4,0},{5,1},{12,8},{13,9},{1,13},{2,14},{10,6},... | collective-permute-start | bytes 393224 | tf_op jit(solution)/shard_map/ppermute | solution.py:515
  123.8 19.3 %collective-permute-start.12 = (bf16[512,128]{1,0:T(8,128)(2,1)}, bf16[512,128]{1,0:T(8,128)(2,1)S(1)}, u32[]{:S(2)}, u32[]{:S(2)}) collective-permute-start(bf16[512,128]{1,0:T(8,128)(2,1)} %get-tuple-element.73), channel_id=1, source_target_pairs={{0,13},{8,5},{9,4},{4,1},{5,0},{12,9},{13,8},{1,12},{2,15},{10,7},... | collective-permute-start | bytes 393224 | tf_op jit(solution)/shard_map/ppermute | solution.py:515
  125.6 17.5 %collective-permute-start.13 = (bf16[512,128]{1,0:T(8,128)(2,1)S(1)}, bf16[512,128]{1,0:T(8,128)(2,1)}, u32[]{:S(2)}, u32[]{:S(2)}) collective-permute-start(bf16[512,128]{1,0:T(8,128)(2,1)S(1)} %get-tuple-element.74), channel_id=1, source_target_pairs={{0,1},{8,9},{9,8},{4,5},{5,4},{12,13},{13,12},{1,0},{2,3},{10,11},... | collective-permute-start | bytes 393224 | tf_op jit(solution)/shard_map/ppermute | solution.py:515
  126.4 16.7 %copy-start.6 = (bf16[1024,1024]{1,0:T(8,128)(2,1)S(1)}, bf16[1024,1024]{1,0:T(8,128)(2,1)}, u32[]{:S(2)}) copy-start(bf16[1024,1024]{1,0:T(8,128)(2,1)} %copy-done.4) | copy-start | bytes 6291460
  126.4 16.7 %copy-start.8 = (bf16[1024,1024]{1,0:T(8,128)(2,1)S(1)}, bf16[1024,1024]{1,0:T(8,128)(2,1)}, u32[]{:S(2)}) copy-start(bf16[1024,1024]{1,0:T(8,128)(2,1)} %copy-done.7) | copy-start | bytes 6291460
  126.4 16.7 %copy-start.10 = (bf16[512,128]{1,0:T(8,128)(2,1)S(1)}, bf16[512,128]{1,0:T(8,128)(2,1)}, u32[]{:S(2)}) copy-start(bf16[512,128]{1,0:T(8,128)(2,1)} %copy-done.9) | copy-start | bytes 393220
  143.1 31.0 %copy-start.2 = (bf16[1024,512]{1,0:T(8,128)(2,1)S(1)}, bf16[1024,512]{1,0:T(8,128)(2,1)}, u32[]{:S(2)}) copy-start(bf16[1024,512]{1,0:T(8,128)(2,1)} %refs_4_.5) | copy-start | bytes 3145732
  147.5 20.9 %collective-permute-start.21 = (bf16[4,128,512]{2,1,0:T(8,128)(2,1)S(1)}, bf16[4,128,512]{2,1,0:T(8,128)(2,1)S(1)}, u32[]{:S(2)}, u32[]{:S(2)}) collective-permute-start(bf16[4,128,512]{2,1,0:T(8,128)(2,1)S(1)} %get-tuple-element.89), channel_id=1, source_target_pairs={{0,1},{1,0},{2,3},{3,2},{4,5},{5,4},{6,7},{7,6},{8,9},{9,8},{10,11... | collective-permute-start | bytes 1572872 | tf_op jit(solution)/shard_map/ppermute | solution.py:521
  147.6 17.9 %collective-permute-start.14 = (bf16[544,128]{1,0:T(8,128)(2,1)S(1)}, bf16[544,128]{1,0:T(8,128)(2,1)S(1)}, u32[]{:S(2)}, u32[]{:S(2)}) collective-permute-start(bf16[544,128]{1,0:T(8,128)(2,1)S(1)} %get-tuple-element.81), channel_id=1, source_target_pairs={{0,8},{8,0},{9,1},{4,12},{5,13},{12,4},{13,5},{1,9},{2,10},{10,2},... | collective-permute-start | bytes 417800 | tf_op jit(solution)/shard_map/ppermute | solution.py:515
  147.8 20.6 %collective-permute-start.15 = (bf16[544,128]{1,0:T(8,128)(2,1)S(1)}, bf16[544,128]{1,0:T(8,128)(2,1)S(1)}, u32[]{:S(2)}, u32[]{:S(2)}) collective-permute-start(bf16[544,128]{1,0:T(8,128)(2,1)S(1)} %get-tuple-element.82), channel_id=1, source_target_pairs={{0,9},{8,1},{9,0},{4,13},{5,12},{12,5},{13,4},{1,8},{2,11},{10,3},... | collective-permute-start | bytes 417800 | tf_op jit(solution)/shard_map/ppermute | solution.py:515
  150.3 18.9 %collective-permute-start.16 = (bf16[544,128]{1,0:T(8,128)(2,1)S(1)}, bf16[544,128]{1,0:T(8,128)(2,1)S(1)}, u32[]{:S(2)}, u32[]{:S(2)}) collective-permute-start(bf16[544,128]{1,0:T(8,128)(2,1)S(1)} %get-tuple-element.83), channel_id=1, source_target_pairs={{0,4},{8,12},{9,13},{4,8},{5,9},{12,0},{13,1},{1,5},{2,6},{10,14},... | collective-permute-start | bytes 417800 | tf_op jit(solution)/shard_map/ppermute | solution.py:515
  150.3 18.9 %collective-permute-start.17 = (bf16[544,128]{1,0:T(8,128)(2,1)S(1)}, bf16[544,128]{1,0:T(8,128)(2,1)S(1)}, u32[]{:S(2)}, u32[]{:S(2)}) collective-permute-start(bf16[544,128]{1,0:T(8,128)(2,1)S(1)} %get-tuple-element.84), channel_id=1, source_target_pairs={{0,5},{8,13},{9,12},{4,9},{5,8},{12,1},{13,0},{1,4},{2,7},{10,15},... | collective-permute-start | bytes 417800 | tf_op jit(solution)/shard_map/ppermute | solution.py:515
  165.5 5.9 %collective-permute-start.18 = (bf16[544,128]{1,0:T(8,128)(2,1)S(1)}, bf16[544,128]{1,0:T(8,128)(2,1)S(1)}, u32[]{:S(2)}, u32[]{:S(2)}) collective-permute-start(bf16[544,128]{1,0:T(8,128)(2,1)S(1)} %get-tuple-element.85), channel_id=1, source_target_pairs={{0,12},{8,4},{9,5},{4,0},{5,1},{12,8},{13,9},{1,13},{2,14},{10,6},... | collective-permute-start | bytes 417800 | tf_op jit(solution)/shard_map/ppermute | solution.py:515
  168.4 5.7 %collective-permute-start.19 = (bf16[544,128]{1,0:T(8,128)(2,1)S(1)}, bf16[544,128]{1,0:T(8,128)(2,1)S(1)}, u32[]{:S(2)}, u32[]{:S(2)}) collective-permute-start(bf16[544,128]{1,0:T(8,128)(2,1)S(1)} %get-tuple-element.86), channel_id=1, source_target_pairs={{0,13},{8,5},{9,4},{4,1},{5,0},{12,9},{13,8},{1,12},{2,15},{10,7},... | collective-permute-start | bytes 417800 | tf_op jit(solution)/shard_map/ppermute | solution.py:515
  168.4 5.7 %collective-permute-start.20 = (bf16[544,128]{1,0:T(8,128)(2,1)S(1)}, bf16[544,128]{1,0:T(8,128)(2,1)S(1)}, u32[]{:S(2)}, u32[]{:S(2)}) collective-permute-start(bf16[544,128]{1,0:T(8,128)(2,1)S(1)} %get-tuple-element.87), channel_id=1, source_target_pairs={{0,1},{8,9},{9,8},{4,5},{5,4},{12,13},{13,12},{1,0},{2,3},{10,11},... | collective-permute-start | bytes 417800 | tf_op jit(solution)/shard_map/ppermute | solution.py:515
  178.1 30.6 %collective-permute-start.22 = (bf16[1024,512]{1,0:T(8,128)(2,1)S(1)}, bf16[1024,512]{1,0:T(8,128)(2,1)S(1)}, u32[]{:S(2)}, u32[]{:S(2)}) collective-permute-start(bf16[1024,512]{1,0:T(8,128)(2,1)S(1)} %get-tuple-element.96), channel_id=1, source_target_pairs={{0,2},{2,0},{1,3},{3,1},{4,6},{6,4},{5,7},{7,5},{8,10},{10,8},{9,1... | collective-permute-start | bytes 3145736 | tf_op jit(solution)/shard_map/ppermute | solution.py:521
  183.2 4.0 %collective-permute-start.23 = (bf16[4,128,512]{2,1,0:T(8,128)(2,1)S(1)}, bf16[4,128,512]{2,1,0:T(8,128)(2,1)S(1)}, u32[]{:S(2)}, u32[]{:S(2)}) collective-permute-start(bf16[4,128,512]{2,1,0:T(8,128)(2,1)S(1)} %get-tuple-element.98), channel_id=1, source_target_pairs={{0,1},{1,0},{2,3},{3,2},{4,5},{5,4},{6,7},{7,6},{8,9},{9,8},{10,11... | collective-permute-start | bytes 1572872 | tf_op jit(solution)/shard_map/ppermute | solution.py:521
  183.3 8.3 %collective-permute-start.27 = (bf16[128,512]{1,0:T(8,128)(2,1)S(1)}, bf16[128,512]{1,0:T(8,128)(2,1)S(1)}, u32[]{:S(2)}, u32[]{:S(2)}) collective-permute-start(bf16[128,512]{1,0:T(8,128)(2,1)S(1)} %get-tuple-element.104.refs_14_), channel_id=1, source_target_pairs={{0,4},{4,8},{8,12},{12,0},{1,5},{5,9},{9,13},{13,1},{2,6},{6,10},{... | collective-permute-start | bytes 393224 | tf_op jit(solution)/shard_map/ppermute | solution.py:521
  184.1 13.1 %collective-permute-start.28 = (bf16[128,512]{1,0:T(8,128)(2,1)S(1)}, bf16[128,512]{1,0:T(8,128)(2,1)S(1)}, u32[]{:S(2)}, u32[]{:S(2)}) collective-permute-start(bf16[128,512]{1,0:T(8,128)(2,1)S(1)} %get-tuple-element.105.refs_15_), channel_id=1, source_target_pairs={{0,8},{4,12},{8,0},{12,4},{1,9},{5,13},{9,1},{13,5},{2,10},{6,14},... | collective-permute-start | bytes 393224 | tf_op jit(solution)/shard_map/ppermute | solution.py:521
  185.4 14.6 %collective-permute-start.29 = (bf16[128,512]{1,0:T(8,128)(2,1)S(1)}, bf16[128,512]{1,0:T(8,128)(2,1)S(1)}, u32[]{:S(2)}, u32[]{:S(2)}) collective-permute-start(bf16[128,512]{1,0:T(8,128)(2,1)S(1)} %get-tuple-element.106.refs_16_), channel_id=1, source_target_pairs={{0,12},{4,0},{8,4},{12,8},{1,13},{5,1},{9,5},{13,9},{2,14},{6,2},{... | collective-permute-start | bytes 393224 | tf_op jit(solution)/shard_map/ppermute | solution.py:521
  187.8 12.9 %collective-permute-start.24 = (bf16[128,512]{1,0:T(8,128)(2,1)S(1)}, bf16[128,512]{1,0:T(8,128)(2,1)S(1)}, u32[]{:S(2)}, u32[]{:S(2)}) collective-permute-start(bf16[128,512]{1,0:T(8,128)(2,1)S(1)} %get-tuple-element.100), channel_id=1, source_target_pairs={{0,4},{4,8},{8,12},{12,0},{1,5},{5,9},{9,13},{13,1},{2,6},{6,10},{... | collective-permute-start | bytes 393224 | tf_op jit(solution)/shard_map/ppermute | solution.py:521
  191.6 16.4 %collective-permute-start.25 = (bf16[128,512]{1,0:T(8,128)(2,1)S(1)}, bf16[128,512]{1,0:T(8,128)(2,1)S(1)}, u32[]{:S(2)}, u32[]{:S(2)}) collective-permute-start(bf16[128,512]{1,0:T(8,128)(2,1)S(1)} %get-tuple-element.101), channel_id=1, source_target_pairs={{0,8},{4,12},{8,0},{12,4},{1,9},{5,13},{9,1},{13,5},{2,10},{6,14},... | collective-permute-start | bytes 393224 | tf_op jit(solution)/shard_map/ppermute | solution.py:521
  197.2 10.8 %collective-permute-start.26 = (bf16[128,512]{1,0:T(8,128)(2,1)S(1)}, bf16[128,512]{1,0:T(8,128)(2,1)S(1)}, u32[]{:S(2)}, u32[]{:S(2)}) collective-permute-start(bf16[128,512]{1,0:T(8,128)(2,1)S(1)} %get-tuple-element.102), channel_id=1, source_target_pairs={{0,12},{4,0},{8,4},{12,8},{1,13},{5,1},{9,5},{13,9},{2,14},{6,2},{... | collective-permute-start | bytes 393224 | tf_op jit(solution)/shard_map/ppermute | solution.py:521

commit v9 on v8

--- a/solution.py
+++ b/solution.py
@@ -59,6 +59,11 @@
     far = sorted(range(1, sizes[0]), key=lambda seq: -min(seq, sizes[0] - seq))
     subs = range(sizes[1])
     return [(0, 0)] + [(seq, sub) for seq in far for sub in subs] + [(0, sub) for sub in subs if sub]
+
+
+def hand_out(by_owner_ref, out_refs, me_ref, sizes):
+    for ahead, out_ref in zip(steps_of(sizes), out_refs):
+        out_ref[...] = by_owner_ref[owner_of(me_ref, ahead, sizes)]
 
 
 def slots_of(assign, groups, rows):
@@ -142,7 +147,8 @@
         copy.wait()
 
 
-def project_value_kernel(groups, rows, slot_ref, tokens_ref, weight_ref, sorted_ref, turned_ref, unsort_ref, value_ref):
+def project_value_kernel(sizes, groups, rows, me_ref, slot_ref, tokens_ref, weight_ref, *rest):
+    out_refs, (turned_ref, unsort_ref, value_ref, sorted_ref) = rest[:-4], rest[-4:]
     toks = tokens_ref.shape[0]
     heads = weight_ref.shape[1] // HD
     step = min(512, toks)
@@ -172,6 +178,7 @@
             sorted_ref[group * heads + 2 * pair, pl.ds(first, part), :] = even
             sorted_ref[group * heads + 2 * pair + 1, pl.ds(first, part), :] = odd
 
+    hand_out(sorted_ref, out_refs, me_ref, sizes)
     turned_ref[...] = tokens_ref[...].T
     slots = unsort_ref.shape[1]
     part = min(256, slots)
@@ -294,15 +301,16 @@
         out_ref[...] = jnp.where(low_half((half, LANES)), swap_halves(up), down).astype(BF16)
 
 
-def query_grad_kernel(sizes, per_group, slot_rows, me_ref, counts_ref, dense_ref, value_in_ref, *refs):
+def query_grad_kernel(sizes, per_group, slot_rows, me_ref, counts_ref, dense_ref, *refs):
     owners = sizes[0] * sizes[1]
-    out_refs, rest = refs[:owners], refs[owners:]
+    value_refs, out_refs, rest = refs[:owners], refs[owners : 2 * owners], refs[2 * owners :]
     place_ref, wide_ref, block_ref, sums_ref, centroid_ref = rest[:5]
     score_refs, grad_probs_refs, both_refs = rest[5:7], rest[7:9], rest[9:11]
-    half = value_in_ref.shape[1]
+    half = value_refs[0].shape[0]
     rows = 2 * half
-    for source in range(owners):
-        value = value_in_ref[source].astype(F32)
+    for ahead, value_ref in zip(steps_of(sizes), value_refs):
+        source = source_of(me_ref, ahead, sizes)
+        value = value_ref[...].astype(F32)
         wide_ref[source, :half, :] = swap_halves(value)
         wide_ref[source, half:rows, :] = value
         wide_ref[source, rows:, :] = jnp.zeros((slot_rows, LANES), F32)
@@ -377,9 +385,9 @@
     return x.astype(BF16)
 
 
-def bring_home(sizes, heads, pieces, unsort_ref, home_ref, sorted_ref, rows_ref):
-    for source, piece in pieces:
-        home_ref[source] = piece
+def bring_home(sizes, heads, me_ref, part_refs, unsort_ref, home_ref, sorted_ref, rows_ref):
+    for ahead, part_ref in zip(steps_of(sizes), part_refs):
+        home_ref[source_of(me_ref, ahead, sizes)] = part_ref[...]
     half = sorted_ref.shape[0] * heads // (sizes[0] * sizes[1]) // 2
     unfold(home_ref, sorted_ref, heads, 0, half, to_half)
     toks = rows_ref.shape[0]
@@ -411,10 +419,7 @@
 def value_home_kernel(sizes, heads, me_ref, turned_ref, unsort_ref, *refs):
     part_refs, rows_ref, sub_refs = refs[: -4 - sizes[1]], refs[-4 - sizes[1]], refs[-3 - sizes[1] : -3]
     home_ref, sorted_ref, whole_ref = refs[-3:]
-    pieces = [
-        (source_of(me_ref, ahead, sizes), part_ref[...]) for ahead, part_ref in zip(steps_of(sizes), part_refs)
-    ]
-    bring_home(sizes, heads, pieces, unsort_ref, home_ref, sorted_ref, rows_ref)
+    bring_home(sizes, heads, me_ref, part_refs, unsort_ref, home_ref, sorted_ref, rows_ref)
     weight_partial(sizes, me_ref, turned_ref, rows_ref, whole_ref, sub_refs)
 
 
@@ -441,22 +446,19 @@
         refs[-3 - parts : -4],
         refs[-4:],
     )
-    pieces = [
-        (source_of(me_ref, ahead, sizes), part_ref[...]) for ahead, part_ref in zip(steps_of(sizes), part_refs)
-    ]
-    bring_home(sizes, heads, pieces, unsort_ref, home_ref, sorted_ref, rows_ref)
+    bring_home(sizes, heads, me_ref, part_refs, unsort_ref, home_ref, sorted_ref, rows_ref)
     half = sorted_ref.shape[0] * heads // (sizes[0] * sizes[1]) // 2
     unfold(home_ref, centroid_ref, heads, half, home_ref.shape[1] - half, lambda x: x * factor)
     for ahead, out_ref in enumerate(out_refs):
         input_partial(me_ref, ahead + 1, parts, rows_ref, value_rows_ref, w_query_ref, w_value_ref, out_ref)
 
 
-def query_weight_kernel(
-    sizes, parts, me_ref, turned_ref, rows_ref, value_rows_ref, w_query_ref, w_value_ref, *refs
-):
-    sub_refs, out_ref, whole_ref = refs[:-2], refs[-2], refs[-1]
-    weight_partial(sizes, me_ref, turned_ref, rows_ref, whole_ref, sub_refs)
-    input_partial(me_ref, 0, parts, rows_ref, value_rows_ref, w_query_ref, w_value_ref, out_ref)
+def query_weight_kernel(sizes, me_ref, turned_ref, rows_ref, *refs):
+    weight_partial(sizes, me_ref, turned_ref, rows_ref, refs[-1], refs[:-1])
+
+
+def input_own_kernel(parts, me_ref, *refs):
+    input_partial(me_ref, 0, parts, *refs)
 
 
 def fold_subs_kernel(me_ref, *refs):
@@ -525,19 +527,14 @@
     return [parts[0]] + [shift(parts[ahead], axis, ahead) for ahead in range(1, len(parts))]
 
 
-def fold_subs(me, by_sub, name, after=()):
+def fold_subs(me, by_sub, name):
     seqs, piece, columns = by_sub[0].shape
     return call(
         fold_subs_kernel,
         (jax.ShapeDtypeStruct((piece, columns), BF16),) * seqs,
         (me, *pass_round(by_sub, "sub")),
-        after=after,
         name=name,
     )
-
-
-def all_to_all(rows):
-    return lax.all_to_all(rows, OWNERS, split_axis=0, concat_axis=0, tiled=True)
 
 
 def add_up(terms, dtype, name):
@@ -590,17 +587,15 @@
         name="project_query",
     )
     got_mixed = exchange(send_mixed, sizes)
-    send_value, turned, unsort = call(
-        functools.partial(project_value_kernel, groups, rows),
-        several(1, owners, half, LANES) + several(1, width, toks) + several(1, toks, slots),
-        (slot_row, tokens_in, w_value),
-        smem=(),
-        scratch=[pltpu.VMEM((toks, width_dev), BF16)],
+    *send_value, turned, unsort = call(
+        functools.partial(project_value_kernel, sizes, groups, rows),
+        several(owners, half, LANES) + several(1, width, toks) + several(1, toks, slots),
+        (me, slot_row, tokens_in, w_value),
+        scratch=[pltpu.VMEM((toks, width_dev), BF16), pltpu.VMEM((owners, half, LANES), BF16)],
         flops=2 * toks * width * width_dev + 2 * slots * toks * width_dev,
         name="project_value",
     )
-    send_value, _ = lax.optimization_barrier((send_value, got_mixed[1:4]))
-    got_value = all_to_all(send_value)
+    got_value = exchange(send_value, sizes)
     blocks = per_group * capacity // BLOCK_ROWS
     held = blocks + (LEAD + 4) * UNROLL
     block_flops = 2 * BLOCK_ROWS * BLOCK_ROWS * LANES
@@ -615,7 +610,6 @@
         + several(1, held * BLOCK_ROWS, LANES)
         + (shape((owners, LANES), jnp.int32),),
         (me, *got_mixed),
-        after=[unsort],
         scratch=[pltpu.SMEM((owners, LANES), jnp.int32), place, tall, dense_rows, tall]
         + [group_f32] * 2
         + [group_b16] * 2,
@@ -627,7 +621,7 @@
     back_query = call(
         functools.partial(query_grad_kernel, sizes, per_group, slot_rows),
         several(owners, half + extra, LANES),
-        (me, counts, dense, got_value),
+        (me, counts, dense, *got_value),
         smem=(0, 1),
         scratch=[place, tall, dense_rows, pltpu.VMEM((held, LANES), F32), pltpu.VMEM((2 * extra, LANES), F32)]
         + [group_f32] * 4
@@ -646,7 +640,6 @@
         functools.partial(value_home_kernel, sizes, heads),
         several(1, toks, width_dev) + sub_shapes,
         (me, turned, unsort, *home_value),
-        after=back_query[:1],
         scratch=[pltpu.VMEM((owners, half, LANES), BF16), sorted_rows, whole],
         flops=weight_flops + home_flops,
         name="value_home",
@@ -658,7 +651,6 @@
         + several(1, toks, width_dev)
         + (shape((groups * 2 * extra, width_dev), F32),),
         (me, unsort, value_rows, w_query, w_value, *home_query),
-        after=value_weight,
         scratch=[pltpu.VMEM((owners, half + extra, LANES), BF16), sorted_rows],
         flops=weight_flops + home_flops,
         name="query_home",
@@ -666,15 +658,24 @@
     arrived = [shift(partial, "head", k + 1) for k, partial in enumerate(partials)]
     value_weight, _ = lax.optimization_barrier((value_weight, home_query))
     value_weight = pass_round(value_weight, "seq")
-    *query_weight, own = call(
-        functools.partial(query_weight_kernel, sizes, parts),
-        sub_shapes + several(1, toks, columns),
-        (me, turned, query_rows, value_rows, w_query, w_value),
+    query_weight = call(
+        functools.partial(query_weight_kernel, sizes),
+        sub_shapes,
+        (me, turned, query_rows),
         scratch=[whole],
-        flops=2 * weight_flops,
+        flops=weight_flops,
         name="query_weight",
     )
-    query_weight = pass_round(fold_subs(me, query_weight, "query_subs"), "seq")
+    query_weight = fold_subs(me, query_weight, "query_subs")
+    own = call(
+        functools.partial(input_own_kernel, parts),
+        shape((toks, columns), BF16),
+        (me, query_rows, value_rows, w_query, w_value),
+        after=query_weight[:1],
+        flops=weight_flops * 2 // parts,
+        name="input_own",
+    )
+    query_weight = pass_round(query_weight, "seq")
     grad_wv = add_up(value_weight, F32, "value_sum")
     grad_wq = add_up(query_weight, F32, "query_sum")
     grad_input = add_up([own] + arrived, BF16, "input_sum")

time: 210 us -> 179 us (0.85)
  waiting for transfers between devices: 99.4 us -> 56.3 us
  starting transfers between devices: 42.6 us -> 61.9 us
  local copies, waits for them, and re-layouts: 6.61 us -> 0.72 us
    ppermute x21 -> x28, waiting for transfers between devices: 83.5 us -> 48.4 us  [exchange(): out.append(part if ahead == (0, 0) else lax.ppermute(part, OWNERS, moves))]
    ppermute x21 -> x28, starting transfers between devices: 28.8 us -> 47.2 us  [exchange(): out.append(part if ahead == (0, 0) else lax.ppermute(part, OWNERS, moves))]
    ppermute x9, waiting for transfers between devices: 15.9 us -> 7.83 us  [shift(): lax.ppermute(part, axis, [(i, (i + ahead) % size) for i in range(size)])]
    unnamed x26 -> x22, local copies, waits for them, and re-layouts: 6.61 us -> 0.72 us
    ppermute x9, starting transfers between devices: 9.03 us -> 14.7 us  [shift(): lax.ppermute(part, axis, [(i, (i + ahead) % size) for i in range(size)])]
    all_to_all x1 -> x0, starting transfers between devices: 4.75 us -> none  [all_to_all(): return lax.all_to_all(rows, OWNERS, split_axis=0, concat_axis=0, tiled=True)]
    pallas_call x12 -> x13, Pallas kernels: 59.8 us -> 58.2 us  [call(): pl.pallas_call(body, out_shape=outs, in_specs=specs, out_specs=jax.tree.m...]
  transfers between devices with their start and end apart: 31 -> 37, of which waited for: 14 -> 11; matrix products, arithmetic and copies ran while one was open for 0% -> 0% of each run, Pallas kernels for 20% -> 25%
where the time goes in v9:
time: 179 us; the launch traced here: 178 us
  starting transfers between devices  61.9 us (35%)
  Pallas kernels  58.2 us (33%)
  waiting for transfers between devices  56.3 us (31%)
    pallas_call x13, Pallas kernels, call(): pl.pallas_call(body, out_shape=outs, in_specs=specs, out_specs=jax.tree.m...  58.2 us
    ppermute x28, waiting for transfers between devices, exchange(): out.append(part if ahead == (0, 0) else lax.ppermute(part, OWNERS, moves))  48.4 us
    ppermute x28, starting transfers between devices, exchange(): out.append(part if ahead == (0, 0) else lax.ppermute(part, OWNERS, moves))  47.2 us
    ppermute x9, starting transfers between devices, shift(): lax.ppermute(part, axis, [(i, (i + ahead) % size) for i in range(size)])  14.7 us
    ppermute x9, waiting for transfers between devices, shift(): lax.ppermute(part, axis, [(i, (i + ahead) % size) for i in range(size)])  7.83 us
  transfers between devices with their start and end apart: 37, of which 11 were waited for; matrix products, arithmetic and copies ran while one was open for 0% of the time, Pallas kernels for 25%

profile of v9, /device:TPU:0, one launch (start us, length us, event | category | flops | bytes accessed | tf_op | source)
XLA Modules:
  0.0 178.5 jit_solution(4632901537454180464)
XLA Ops:
  0.6 0.7 pad_add_fusion.refs_0_
  1.3 8.5 %project_query.1 = (bf16[1040,128]{1,0:T(8,128)(2,1)}, bf16[1040,128]{1,0:T(8,128)(2,1)}, bf16[1040,128]{1,0:T(8,128)(2,1)}, bf16[1040,128]{1,0:T(8,128)(2,1)}, ...) custom-call(s32[4]{0:T(128)} %pad_add_fusion.refs_0_, ...), custom_call_target="tpu_custom_call" | custom-call | flops 3221225472 | bytes 6332432 | tf_op jit(solution)/shard_map/project_query/pallas_call | solution.py:495
  9.8 4.1 %collective-permute-start = (bf16[1040,128]{1,0:T(8,128)(2,1)}, bf16[1040,128]{1,0:T(8,128)(2,1)S(1)}, u32[]{:S(2)}, u32[]{:S(2)}) collective-permute-start(bf16[1040,128]{1,0:T(8,128)(2,1)} %get-tuple-element.65), channel_id=1, source_target_pairs={{0,8},{8,0},{9,1},{4,12},{5,13},{12,4},{13,5},{1,9},{2,10},{10,2},... | collective-permute-start | bytes 798728 | tf_op jit(solution)/shard_map/ppermute | solution.py:517
  14.0 0.7 copy-done.5
  14.7 4.8 %project_value.1 = (bf16[512,128]{1,0:T(8,128)(2,1)S(1)}, bf16[512,128]{1,0:T(8,128)(2,1)S(1)}, bf16[512,128]{1,0:T(8,128)(2,1)S(1)}, bf16[512,128]{1,0:T(8,128)...) custom-call(s32[4]{0:T(128)S(1)} %copy-done.2, ...), custom_call_target="tpu_custom_call" | custom-call | flops 2147483648 | bytes 8392720 | tf_op jit(solution)/shard_map/project_value/pallas_call | solution.py:495
  19.5 2.1 %collective-permute-start.14 = (bf16[512,128]{1,0:T(8,128)(2,1)S(1)}, bf16[512,128]{1,0:T(8,128)(2,1)S(1)}, u32[]{:S(2)}, u32[]{:S(2)}) collective-permute-start(bf16[512,128]{1,0:T(8,128)(2,1)S(1)} %get-tuple-element.84), channel_id=1, source_target_pairs={{0,8},{8,0},{9,1},{4,12},{5,13},{12,4},{13,5},{1,9},{2,10},{10,2},... | collective-permute-start | bytes 393224 | tf_op jit(solution)/shard_map/ppermute | solution.py:517
  21.6 0.6 collective-permute-start.15
  22.3 1.6 collective-permute-start.2
  23.9 28.8 %collective-permute-done.14.refs_4_ = bf16[512,128]{1,0:T(8,128)(2,1)S(1)} collective-permute-done((bf16[512,128]{1,0:T(8,128)(2,1)S(1)}, bf16[512,128]{1,0:T(8,128)(2,1)S(1)}, u32[]{:S(2)}, u32[]{:S(2)}) %collective-permute-start.14) | collective-permute-done | bytes 131104 | tf_op jit(solution)/shard_map/ppermute | solution.py:517
  52.6 1.1 collective-permute-done.15.refs_5_
  53.8 0.7 collective-permute-start.4
  54.5 1.7 collective-permute-start.5
  56.4 1.6 collective-permute-start.16
  58.0 5.2 %collective-permute-done.3.refs_5_ = bf16[1040,128]{1,0:T(8,128)(2,1)S(1)} collective-permute-done((bf16[1040,128]{1,0:T(8,128)(2,1)S(1)}, bf16[1040,128]{1,0:T(8,128)(2,1)S(1)}, u32[]{:S(2)}, u32[]{:S(2)}) %collective-permute-start.3) | collective-permute-done | bytes 266272 | tf_op jit(solution)/shard_map/ppermute | solution.py:517
  63.2 8.9 %collective-permute-start.17 = (bf16[512,128]{1,0:T(8,128)(2,1)S(1)}, bf16[512,128]{1,0:T(8,128)(2,1)S(1)}, u32[]{:S(2)}, u32[]{:S(2)}) collective-permute-start(bf16[512,128]{1,0:T(8,128)(2,1)S(1)} %get-tuple-element.87), channel_id=1, source_target_pairs={{0,5},{8,13},{9,12},{4,9},{5,8},{12,1},{13,0},{1,4},{2,7},{10,15},... | collective-permute-start | bytes 393224 | tf_op jit(solution)/shard_map/ppermute | solution.py:517
  72.1 2.5 %collective-permute-done.5.refs_7_ = bf16[1040,128]{1,0:T(8,128)(2,1)S(1)} collective-permute-done((bf16[1040,128]{1,0:T(8,128)(2,1)S(1)}, bf16[1040,128]{1,0:T(8,128)(2,1)S(1)}, u32[]{:S(2)}, u32[]{:S(2)}) %collective-permute-start.5) | collective-permute-done | bytes 266272 | tf_op jit(solution)/shard_map/ppermute | solution.py:517
  74.6 0.8 collective-permute-start.19
  75.8 13.0 %value_grad.1 = (bf16[512,128]{1,0:T(8,128)(2,1)S(1)}, bf16[512,128]{1,0:T(8,128)(2,1)S(1)}, bf16[512,128]{1,0:T(8,128)(2,1)S(1)}, bf16[512,128]{1,0:T(8,128)(2,...) custom-call(s32[4]{0:T(128)S(1)} %copy-done.2, ...), custom_call_target="tpu_custom_call" | custom-call | flops 2147483648 | bytes 8163344 | tf_op jit(solution)/shard_map/value_grad/pallas_call | solution.py:495
  88.9 0.5 collective-permute-start.7
  89.4 1.8 collective-permute-start.8
  91.2 1.0 collective-permute-start.9
  92.5 15.8 %query_grad.1 = (bf16[544,128]{1,0:T(8,128)(2,1)S(1)}, bf16[544,128]{1,0:T(8,128)(2,1)S(1)}, bf16[544,128]{1,0:T(8,128)(2,1)S(1)}, bf16[544,128]{1,0:T(8,128)(2,...) custom-call(s32[4]{0:T(128)S(1)} %copy-done.2, ...), custom_call_target="tpu_custom_call" | custom-call | flops 3221225472 | bytes 7147536 | tf_op jit(solution)/shard_map/query_grad/pallas_call | solution.py:495
  108.3 3.2 %collective-permute-start.21 = (bf16[544,128]{1,0:T(8,128)(2,1)S(1)}, bf16[544,128]{1,0:T(8,128)(2,1)S(1)}, u32[]{:S(2)}, u32[]{:S(2)}) collective-permute-start(bf16[544,128]{1,0:T(8,128)(2,1)S(1)} %get-tuple-element.92), channel_id=1, source_target_pairs={{0,8},{8,0},{9,1},{4,12},{5,13},{12,4},{13,5},{1,9},{2,10},{10,2},... | collective-permute-start | bytes 417800 | tf_op jit(solution)/shard_map/ppermute | solution.py:517
  111.5 2.7 %collective-permute-start.11 = (bf16[512,128]{1,0:T(8,128)(2,1)S(1)}, bf16[512,128]{1,0:T(8,128)(2,1)S(1)}, u32[]{:S(2)}, u32[]{:S(2)}) collective-permute-start(bf16[512,128]{1,0:T(8,128)(2,1)S(1)} %get-tuple-element.77), channel_id=1, source_target_pairs={{0,12},{8,4},{9,5},{4,0},{5,1},{12,8},{13,9},{1,13},{2,14},{10,6},... | collective-permute-start | bytes 393224 | tf_op jit(solution)/shard_map/ppermute | solution.py:517
  114.3 1.1 collective-permute-start.12
  115.4 6.0 %collective-permute-done.11.refs_8_ = bf16[512,128]{1,0:T(8,128)(2,1)S(1)} collective-permute-done((bf16[512,128]{1,0:T(8,128)(2,1)S(1)}, bf16[512,128]{1,0:T(8,128)(2,1)S(1)}, u32[]{:S(2)}, u32[]{:S(2)}) %collective-permute-start.11) | collective-permute-done | bytes 131104 | tf_op jit(solution)/shard_map/ppermute | solution.py:517
  121.4 9.9 %collective-permute-start.23 = (bf16[544,128]{1,0:T(8,128)(2,1)S(1)}, bf16[544,128]{1,0:T(8,128)(2,1)S(1)}, u32[]{:S(2)}, u32[]{:S(2)}) collective-permute-start(bf16[544,128]{1,0:T(8,128)(2,1)S(1)} %get-tuple-element.94), channel_id=1, source_target_pairs={{0,4},{8,12},{9,13},{4,8},{5,9},{12,0},{13,1},{1,5},{2,6},{10,14},... | collective-permute-start | bytes 417800 | tf_op jit(solution)/shard_map/ppermute | solution.py:517
  131.3 1.6 collective-permute-start.24
  133.4 1.7 collective-permute-start.26
  135.1 3.9 %value_home.1 = (bf16[1024,512]{1,0:T(8,128)(2,1)S(1)}, bf16[4,128,512]{2,1,0:T(8,128)(2,1)S(1)}, bf16[4,128,512]{2,1,0:T(8,128)(2,1)S(1)}) custom-call(s32[4]{0:T(128)S(1)} %copy-done.2, bf16[1024,1024]{1,0:T(8,128)(2,1)S(1)} %get-tuple-element.63.refs_1_, bf16[1024,1024]{1,0:T(8,128)(2,1)S(1)} %get-tuple-element.62.refs_2_.refs_1_, ...), custom_call_target="tpu_custom_call" | custom-call | flops 2147483648 | bytes 7340048 | tf_op jit(solution)/shard_map/value_home/pallas_call | solution.py:495
  139.1 1.9 %collective-permute-done.25.refs_10_ = bf16[544,128]{1,0:T(8,128)(2,1)S(1)} collective-permute-done((bf16[544,128]{1,0:T(8,128)(2,1)S(1)}, bf16[544,128]{1,0:T(8,128)(2,1)S(1)}, u32[]{:S(2)}, u32[]{:S(2)}) %collective-permute-start.25) | collective-permute-done | bytes 139296 | tf_op jit(solution)/shard_map/ppermute | solution.py:517
  141.0 2.8 %collective-permute-done.26.refs_11_ = bf16[544,128]{1,0:T(8,128)(2,1)S(1)} collective-permute-done((bf16[544,128]{1,0:T(8,128)(2,1)S(1)}, bf16[544,128]{1,0:T(8,128)(2,1)S(1)}, u32[]{:S(2)}, u32[]{:S(2)}) %collective-permute-start.26) | collective-permute-done | bytes 139296 | tf_op jit(solution)/shard_map/ppermute | solution.py:517
  143.8 4.0 %query_home.1 = (bf16[1024,512]{1,0:T(8,128)(2,1)S(1)}, bf16[1024,512]{1,0:T(8,128)(2,1)S(1)}, f32[64,512]{1,0:T(8,128)}) custom-call(s32[4]{0:T(128)S(1)} %copy-done.2, bf16[1024,1024]{1,0:T(8,128)(2,1)S(1)} %get-tuple-element.62.refs_2_.refs_1_, bf16[1024,512]{1,0:T(8,128)(2,1)S(1)} %get-tuple-element.80.refs_2_, bf16[1024,512]{1,0:T(8,128)(2,1)S(1)} %copy-done, ...), custom_call_target="tpu_custom_call" | custom-call | flops 2147483648 | bytes 8585232 | tf_op jit(solution)/shard_map/query_home/pallas_call | solution.py:495
  147.8 1.2 collective-permute-start.29
  149.0 2.0 %query_weight.1 = (bf16[4,128,512]{2,1,0:T(8,128)(2,1)S(1)}, bf16[4,128,512]{2,1,0:T(8,128)(2,1)S(1)}) custom-call(s32[4]{0:T(128)S(1)} %copy-done.2, bf16[1024,1024]{1,0:T(8,128)(2,1)S(1)} %get-tuple-element.63.refs_1_, bf16[1024,512]{1,0:T(8,128)(2,1)S(1)} %get-tuple-element.99.refs_2_.refs_1_), custom_call_target="tpu_custom_call" | custom-call | flops 1073741824 | bytes 4194320 | tf_op jit(solution)/shard_map/query_weight/pallas_call | solution.py:495
  151.1 0.6 collective-permute-start.28
  151.7 0.7 value_subs.1
  152.3 0.8 collective-permute-start.34
  153.1 2.8 %collective-permute-start.35 = (bf16[128,512]{1,0:T(8,128)(2,1)S(1)}, bf16[128,512]{1,0:T(8,128)(2,1)S(1)}, u32[]{:S(2)}, u32[]{:S(2)}) collective-permute-start(bf16[128,512]{1,0:T(8,128)(2,1)S(1)} %get-tuple-element.115), channel_id=1, source_target_pairs={{0,8},{4,12},{8,0},{12,4},{1,9},{5,13},{9,1},{13,5},{2,10},{6,14},... | collective-permute-start | bytes 393224 | tf_op jit(solution)/shard_map/ppermute | solution.py:523
  156.2 0.7 query_subs.1
  156.9 1.8 collective-permute-start.30
  158.6 2.0 %collective-permute-done.34.refs_1_ = bf16[128,512]{1,0:T(8,128)(2,1)S(1)} collective-permute-done((bf16[128,512]{1,0:T(8,128)(2,1)S(1)}, bf16[128,512]{1,0:T(8,128)(2,1)S(1)}, u32[]{:S(2)}, u32[]{:S(2)}) %collective-permute-start.34) | collective-permute-done | bytes 131104 | tf_op jit(solution)/shard_map/ppermute | solution.py:523
  160.9 5.4 %collective-permute-done.35.refs_2_ = bf16[128,512]{1,0:T(8,128)(2,1)S(1)} collective-permute-done((bf16[128,512]{1,0:T(8,128)(2,1)S(1)}, bf16[128,512]{1,0:T(8,128)(2,1)S(1)}, u32[]{:S(2)}, u32[]{:S(2)}) %collective-permute-start.35) | collective-permute-done | bytes 131104 | tf_op jit(solution)/shard_map/ppermute | solution.py:523
  166.2 7.0 %collective-permute-start.32 = (bf16[128,512]{1,0:T(8,128)(2,1)S(1)}, bf16[128,512]{1,0:T(8,128)(2,1)S(1)}, u32[]{:S(2)}, u32[]{:S(2)}) collective-permute-start(bf16[128,512]{1,0:T(8,128)(2,1)S(1)} %get-tuple-element.106), channel_id=1, source_target_pairs={{0,12},{4,0},{8,4},{12,8},{1,13},{5,1},{9,5},{13,9},{2,14},{6,2},{... | collective-permute-start | bytes 393224 | tf_op jit(solution)/shard_map/ppermute | solution.py:523
  173.2 2.0 %input_own.1.refs_0_ = bf16[1024,512]{1,0:T(8,128)(2,1)S(1)} custom-call(s32[4]{0:T(128)S(1)} %copy-done.2, bf16[1024,512]{1,0:T(8,128)(2,1)S(1)} %get-tuple-element.99.refs_2_.refs_1_, bf16[1024,512]{1,0:T(8,128)(2,1)S(1)} %get-tuple-element.80.refs_2_, bf16[1024,512]{1,0:T(8,128)(2,1)S(1)} %copy-done, bf16[1024,512]{1,0:T(8,128)(2,1)S(1)} %copy-done.1, ...), custom_call_target="tpu_custom_call" | custom-call | flops 1073741824 | bytes 5242896 | tf_op jit(solution)/shard_map/input_own/pallas_call | solution.py:495
  175.3 0.8 value_sum.1
  176.5 0.8 query_sum.1
  177.3 1.2 input_sum.1
  (62 shorter events, 2.5 us)
Async XLA Ops:
  1.3 12.6 %copy-start.1 = (bf16[1024,512]{1,0:T(8,128)(2,1)S(1)}, bf16[1024,512]{1,0:T(8,128)(2,1)}, u32[]{:S(2)}) copy-start(bf16[1024,512]{1,0:T(8,128)(2,1)} %refs_4_.5) | copy-start | bytes 3145732
  1.3 12.6 %copy-start.2 = (s32[4]{0:T(128)S(1)}, s32[4]{0:T(128)}, u32[]{:S(2)}) copy-start(s32[4]{0:T(128)} %pad_add_fusion.refs_0_) | copy-start | bytes 52
  1.3 12.6 %copy-start.3 = (bf16[1024,1024]{1,0:T(8,128)(2,1)S(1)}, bf16[1024,1024]{1,0:T(8,128)(2,1)}, u32[]{:S(2)}) copy-start(bf16[1024,1024]{1,0:T(8,128)(2,1)} %refs_2_.3) | copy-start | bytes 6291460
  9.8 44.7 %collective-permute-start = (bf16[1040,128]{1,0:T(8,128)(2,1)}, bf16[1040,128]{1,0:T(8,128)(2,1)S(1)}, u32[]{:S(2)}, u32[]{:S(2)}) collective-permute-start(bf16[1040,128]{1,0:T(8,128)(2,1)} %get-tuple-element.65), channel_id=1, source_target_pairs={{0,8},{8,0},{9,1},{4,12},{5,13},{12,4},{13,5},{1,9},{2,10},{10,2},... | collective-permute-start | bytes 798728 | tf_op jit(solution)/shard_map/ppermute | solution.py:517
  13.9 42.3 %collective-permute-start.1 = (bf16[1040,128]{1,0:T(8,128)(2,1)}, bf16[1040,128]{1,0:T(8,128)(2,1)S(1)}, u32[]{:S(2)}, u32[]{:S(2)}) collective-permute-start(bf16[1040,128]{1,0:T(8,128)(2,1)} %get-tuple-element.66), channel_id=1, source_target_pairs={{0,9},{8,1},{9,0},{4,13},{5,12},{12,5},{13,4},{1,8},{2,11},{10,3},... | collective-permute-start | bytes 798728 | tf_op jit(solution)/shard_map/ppermute | solution.py:517
  14.0 0.7 copy-start.5
  14.6 7.6 %copy-start.10 = (bf16[1040,128]{1,0:T(8,128)(2,1)S(1)}, bf16[1040,128]{1,0:T(8,128)(2,1)}, u32[]{:S(2)}) copy-start(bf16[1040,128]{1,0:T(8,128)(2,1)} %get-tuple-element.67) | copy-start | bytes 798724
  14.6 38.0 %copy-start.9 = (bf16[1040,128]{1,0:T(8,128)(2,1)S(1)}, bf16[1040,128]{1,0:T(8,128)(2,1)}, u32[]{:S(2)}) copy-start(bf16[1040,128]{1,0:T(8,128)(2,1)} %get-tuple-element.68) | copy-start | bytes 798724
  14.6 39.1 %copy-start.8 = (bf16[1040,128]{1,0:T(8,128)(2,1)S(1)}, bf16[1040,128]{1,0:T(8,128)(2,1)}, u32[]{:S(2)}) copy-start(bf16[1040,128]{1,0:T(8,128)(2,1)} %get-tuple-element.69) | copy-start | bytes 798724
  14.6 39.9 %copy-start.7 = (bf16[1040,128]{1,0:T(8,128)(2,1)S(1)}, bf16[1040,128]{1,0:T(8,128)(2,1)}, u32[]{:S(2)}) copy-start(bf16[1040,128]{1,0:T(8,128)(2,1)} %get-tuple-element.70) | copy-start | bytes 798724
  14.7 41.6 %copy-start.6 = (bf16[1040,128]{1,0:T(8,128)(2,1)S(1)}, bf16[1040,128]{1,0:T(8,128)(2,1)}, u32[]{:S(2)}) copy-start(bf16[1040,128]{1,0:T(8,128)(2,1)} %get-tuple-element.71) | copy-start | bytes 798724
  14.7 61.2 %copy-start.4 = (bf16[1040,128]{1,0:T(8,128)(2,1)S(1)}, bf16[1040,128]{1,0:T(8,128)(2,1)}, u32[]{:S(2)}) copy-start(bf16[1040,128]{1,0:T(8,128)(2,1)} %get-tuple-element.64.refs_1_) | copy-start | bytes 798724
  19.5 33.1 %collective-permute-start.14 = (bf16[512,128]{1,0:T(8,128)(2,1)S(1)}, bf16[512,128]{1,0:T(8,128)(2,1)S(1)}, u32[]{:S(2)}, u32[]{:S(2)}) collective-permute-start(bf16[512,128]{1,0:T(8,128)(2,1)S(1)} %get-tuple-element.84), channel_id=1, source_target_pairs={{0,8},{8,0},{9,1},{4,12},{5,13},{12,4},{13,5},{1,9},{2,10},{10,2},... | collective-permute-start | bytes 393224 | tf_op jit(solution)/shard_map/ppermute | solution.py:517
  21.6 32.1 %collective-permute-start.15 = (bf16[512,128]{1,0:T(8,128)(2,1)S(1)}, bf16[512,128]{1,0:T(8,128)(2,1)S(1)}, u32[]{:S(2)}, u32[]{:S(2)}) collective-permute-start(bf16[512,128]{1,0:T(8,128)(2,1)S(1)} %get-tuple-element.85), channel_id=1, source_target_pairs={{0,9},{8,1},{9,0},{4,13},{5,12},{12,5},{13,4},{1,8},{2,11},{10,3},... | collective-permute-start | bytes 393224 | tf_op jit(solution)/shard_map/ppermute | solution.py:517
  22.3 34.1 %collective-permute-start.2 = (bf16[1040,128]{1,0:T(8,128)(2,1)S(1)}, bf16[1040,128]{1,0:T(8,128)(2,1)S(1)}, u32[]{:S(2)}, u32[]{:S(2)}) collective-permute-start(bf16[1040,128]{1,0:T(8,128)(2,1)S(1)} %copy-done.10), channel_id=1, source_target_pairs={{0,4},{8,12},{9,13},{4,8},{5,9},{12,0},{13,1},{1,5},{2,6},{10,14},... | collective-permute-start | bytes 798728 | tf_op jit(solution)/shard_map/ppermute | solution.py:517
  52.6 10.6 %collective-permute-start.3 = (bf16[1040,128]{1,0:T(8,128)(2,1)S(1)}, bf16[1040,128]{1,0:T(8,128)(2,1)S(1)}, u32[]{:S(2)}, u32[]{:S(2)}) collective-permute-start(bf16[1040,128]{1,0:T(8,128)(2,1)S(1)} %copy-done.9), channel_id=1, source_target_pairs={{0,5},{8,13},{9,12},{4,9},{5,8},{12,1},{13,0},{1,4},{2,7},{10,15},... | collective-permute-start | bytes 798728 | tf_op jit(solution)/shard_map/ppermute | solution.py:517
  53.8 18.3 %collective-permute-start.4 = (bf16[1040,128]{1,0:T(8,128)(2,1)S(1)}, bf16[1040,128]{1,0:T(8,128)(2,1)S(1)}, u32[]{:S(2)}, u32[]{:S(2)}) collective-permute-start(bf16[1040,128]{1,0:T(8,128)(2,1)S(1)} %copy-done.8), channel_id=1, source_target_pairs={{0,12},{8,4},{9,5},{4,0},{5,1},{12,8},{13,9},{1,13},{2,14},{10,6},... | collective-permute-start | bytes 798728 | tf_op jit(solution)/shard_map/ppermute | solution.py:517
  54.5 20.1 %collective-permute-start.5 = (bf16[1040,128]{1,0:T(8,128)(2,1)S(1)}, bf16[1040,128]{1,0:T(8,128)(2,1)S(1)}, u32[]{:S(2)}, u32[]{:S(2)}) collective-permute-start(bf16[1040,128]{1,0:T(8,128)(2,1)S(1)} %copy-done.7), channel_id=1, source_target_pairs={{0,13},{8,5},{9,4},{4,1},{5,0},{12,9},{13,8},{1,12},{2,15},{10,7},... | collective-permute-start | bytes 798728 | tf_op jit(solution)/shard_map/ppermute | solution.py:517
  56.2 19.1 %collective-permute-start.6 = (bf16[1040,128]{1,0:T(8,128)(2,1)S(1)}, bf16[1040,128]{1,0:T(8,128)(2,1)S(1)}, u32[]{:S(2)}, u32[]{:S(2)}) collective-permute-start(bf16[1040,128]{1,0:T(8,128)(2,1)S(1)} %copy-done.6), channel_id=1, source_target_pairs={{0,1},{8,9},{9,8},{4,5},{5,4},{12,13},{13,12},{1,0},{2,3},{10,11},... | collective-permute-start | bytes 798728 | tf_op jit(solution)/shard_map/ppermute | solution.py:517
  56.4 32.5 %collective-permute-start.16 = (bf16[512,128]{1,0:T(8,128)(2,1)S(1)}, bf16[512,128]{1,0:T(8,128)(2,1)S(1)}, u32[]{:S(2)}, u32[]{:S(2)}) collective-permute-start(bf16[512,128]{1,0:T(8,128)(2,1)S(1)} %get-tuple-element.86), channel_id=1, source_target_pairs={{0,4},{8,12},{9,13},{4,8},{5,9},{12,0},{13,1},{1,5},{2,6},{10,14},... | collective-permute-start | bytes 393224 | tf_op jit(solution)/shard_map/ppermute | solution.py:517
  63.2 26.2 %collective-permute-start.17 = (bf16[512,128]{1,0:T(8,128)(2,1)S(1)}, bf16[512,128]{1,0:T(8,128)(2,1)S(1)}, u32[]{:S(2)}, u32[]{:S(2)}) collective-permute-start(bf16[512,128]{1,0:T(8,128)(2,1)S(1)} %get-tuple-element.87), channel_id=1, source_target_pairs={{0,5},{8,13},{9,12},{4,9},{5,8},{12,1},{13,0},{1,4},{2,7},{10,15},... | collective-permute-start | bytes 393224 | tf_op jit(solution)/shard_map/ppermute | solution.py:517
  72.1 19.1 %collective-permute-start.18 = (bf16[512,128]{1,0:T(8,128)(2,1)S(1)}, bf16[512,128]{1,0:T(8,128)(2,1)S(1)}, u32[]{:S(2)}, u32[]{:S(2)}) collective-permute-start(bf16[512,128]{1,0:T(8,128)(2,1)S(1)} %get-tuple-element.88), channel_id=1, source_target_pairs={{0,12},{8,4},{9,5},{4,0},{5,1},{12,8},{13,9},{1,13},{2,14},{10,6},... | collective-permute-start | bytes 393224 | tf_op jit(solution)/shard_map/ppermute | solution.py:517
  74.6 17.6 %collective-permute-start.19 = (bf16[512,128]{1,0:T(8,128)(2,1)S(1)}, bf16[512,128]{1,0:T(8,128)(2,1)S(1)}, u32[]{:S(2)}, u32[]{:S(2)}) collective-permute-start(bf16[512,128]{1,0:T(8,128)(2,1)S(1)} %get-tuple-element.89), channel_id=1, source_target_pairs={{0,13},{8,5},{9,4},{4,1},{5,0},{12,9},{13,8},{1,12},{2,15},{10,7},... | collective-permute-start | bytes 393224 | tf_op jit(solution)/shard_map/ppermute | solution.py:517
  75.4 17.1 %collective-permute-start.20 = (bf16[512,128]{1,0:T(8,128)(2,1)S(1)}, bf16[512,128]{1,0:T(8,128)(2,1)S(1)}, u32[]{:S(2)}, u32[]{:S(2)}) collective-permute-start(bf16[512,128]{1,0:T(8,128)(2,1)S(1)} %get-tuple-element.90), channel_id=1, source_target_pairs={{0,1},{8,9},{9,8},{4,5},{5,4},{12,13},{13,12},{1,0},{2,3},{10,11},... | collective-permute-start | bytes 393224 | tf_op jit(solution)/shard_map/ppermute | solution.py:517
  88.9 22.6 %collective-permute-start.7 = (bf16[512,128]{1,0:T(8,128)(2,1)S(1)}, bf16[512,128]{1,0:T(8,128)(2,1)S(1)}, u32[]{:S(2)}, u32[]{:S(2)}) collective-permute-start(bf16[512,128]{1,0:T(8,128)(2,1)S(1)} %get-tuple-element.73), channel_id=1, source_target_pairs={{0,8},{8,0},{9,1},{4,12},{5,13},{12,4},{13,5},{1,9},{2,10},{10,2},... | collective-permute-start | bytes 393224 | tf_op jit(solution)/shard_map/ppermute | solution.py:517
  89.4 22.1 %collective-permute-start.8 = (bf16[512,128]{1,0:T(8,128)(2,1)S(1)}, bf16[512,128]{1,0:T(8,128)(2,1)S(1)}, u32[]{:S(2)}, u32[]{:S(2)}) collective-permute-start(bf16[512,128]{1,0:T(8,128)(2,1)S(1)} %get-tuple-element.74), channel_id=1, source_target_pairs={{0,9},{8,1},{9,0},{4,13},{5,12},{12,5},{13,4},{1,8},{2,11},{10,3},... | collective-permute-start | bytes 393224 | tf_op jit(solution)/shard_map/ppermute | solution.py:517
  91.2 23.1 %collective-permute-start.9 = (bf16[512,128]{1,0:T(8,128)(2,1)S(1)}, bf16[512,128]{1,0:T(8,128)(2,1)S(1)}, u32[]{:S(2)}, u32[]{:S(2)}) collective-permute-start(bf16[512,128]{1,0:T(8,128)(2,1)S(1)} %get-tuple-element.75), channel_id=1, source_target_pairs={{0,4},{8,12},{9,13},{4,8},{5,9},{12,0},{13,1},{1,5},{2,6},{10,14},... | collective-permute-start | bytes 393224 | tf_op jit(solution)/shard_map/ppermute | solution.py:517
  92.2 23.1 %collective-permute-start.10 = (bf16[512,128]{1,0:T(8,128)(2,1)S(1)}, bf16[512,128]{1,0:T(8,128)(2,1)S(1)}, u32[]{:S(2)}, u32[]{:S(2)}) collective-permute-start(bf16[512,128]{1,0:T(8,128)(2,1)S(1)} %get-tuple-element.76), channel_id=1, source_target_pairs={{0,5},{8,13},{9,12},{4,9},{5,8},{12,1},{13,0},{1,4},{2,7},{10,15},... | collective-permute-start | bytes 393224 | tf_op jit(solution)/shard_map/ppermute | solution.py:517
  108.3 25.1 %collective-permute-start.21 = (bf16[544,128]{1,0:T(8,128)(2,1)S(1)}, bf16[544,128]{1,0:T(8,128)(2,1)S(1)}, u32[]{:S(2)}, u32[]{:S(2)}) collective-permute-start(bf16[544,128]{1,0:T(8,128)(2,1)S(1)} %get-tuple-element.92), channel_id=1, source_target_pairs={{0,8},{8,0},{9,1},{4,12},{5,13},{12,4},{13,5},{1,9},{2,10},{10,2},... | collective-permute-start | bytes 417800 | tf_op jit(solution)/shard_map/ppermute | solution.py:517
  111.5 23.6 %collective-permute-start.22 = (bf16[544,128]{1,0:T(8,128)(2,1)S(1)}, bf16[544,128]{1,0:T(8,128)(2,1)S(1)}, u32[]{:S(2)}, u32[]{:S(2)}) collective-permute-start(bf16[544,128]{1,0:T(8,128)(2,1)S(1)} %get-tuple-element.93), channel_id=1, source_target_pairs={{0,9},{8,1},{9,0},{4,13},{5,12},{12,5},{13,4},{1,8},{2,11},{10,3},... | collective-permute-start | bytes 417800 | tf_op jit(solution)/shard_map/ppermute | solution.py:517
  111.5 9.9 %collective-permute-start.11 = (bf16[512,128]{1,0:T(8,128)(2,1)S(1)}, bf16[512,128]{1,0:T(8,128)(2,1)S(1)}, u32[]{:S(2)}, u32[]{:S(2)}) collective-permute-start(bf16[512,128]{1,0:T(8,128)(2,1)S(1)} %get-tuple-element.77), channel_id=1, source_target_pairs={{0,12},{8,4},{9,5},{4,0},{5,1},{12,8},{13,9},{1,13},{2,14},{10,6},... | collective-permute-start | bytes 393224 | tf_op jit(solution)/shard_map/ppermute | solution.py:517
  114.3 17.1 %collective-permute-start.12 = (bf16[512,128]{1,0:T(8,128)(2,1)S(1)}, bf16[512,128]{1,0:T(8,128)(2,1)S(1)}, u32[]{:S(2)}, u32[]{:S(2)}) collective-permute-start(bf16[512,128]{1,0:T(8,128)(2,1)S(1)} %get-tuple-element.78), channel_id=1, source_target_pairs={{0,13},{8,5},{9,4},{4,1},{5,0},{12,9},{13,8},{1,12},{2,15},{10,7},... | collective-permute-start | bytes 393224 | tf_op jit(solution)/shard_map/ppermute | solution.py:517
  115.4 17.6 %collective-permute-start.13 = (bf16[512,128]{1,0:T(8,128)(2,1)S(1)}, bf16[512,128]{1,0:T(8,128)(2,1)S(1)}, u32[]{:S(2)}, u32[]{:S(2)}) collective-permute-start(bf16[512,128]{1,0:T(8,128)(2,1)S(1)} %get-tuple-element.79), channel_id=1, source_target_pairs={{0,1},{8,9},{9,8},{4,5},{5,4},{12,13},{13,12},{1,0},{2,3},{10,11},... | collective-permute-start | bytes 393224 | tf_op jit(solution)/shard_map/ppermute | solution.py:517
  121.4 17.7 %collective-permute-start.23 = (bf16[544,128]{1,0:T(8,128)(2,1)S(1)}, bf16[544,128]{1,0:T(8,128)(2,1)S(1)}, u32[]{:S(2)}, u32[]{:S(2)}) collective-permute-start(bf16[544,128]{1,0:T(8,128)(2,1)S(1)} %get-tuple-element.94), channel_id=1, source_target_pairs={{0,4},{8,12},{9,13},{4,8},{5,9},{12,0},{13,1},{1,5},{2,6},{10,14},... | collective-permute-start | bytes 417800 | tf_op jit(solution)/shard_map/ppermute | solution.py:517
  131.3 7.8 %collective-permute-start.24 = (bf16[544,128]{1,0:T(8,128)(2,1)S(1)}, bf16[544,128]{1,0:T(8,128)(2,1)S(1)}, u32[]{:S(2)}, u32[]{:S(2)}) collective-permute-start(bf16[544,128]{1,0:T(8,128)(2,1)S(1)} %get-tuple-element.95), channel_id=1, source_target_pairs={{0,5},{8,13},{9,12},{4,9},{5,8},{12,1},{13,0},{1,4},{2,7},{10,15},... | collective-permute-start | bytes 417800 | tf_op jit(solution)/shard_map/ppermute | solution.py:517
  133.0 8.0 %collective-permute-start.25 = (bf16[544,128]{1,0:T(8,128)(2,1)S(1)}, bf16[544,128]{1,0:T(8,128)(2,1)S(1)}, u32[]{:S(2)}, u32[]{:S(2)}) collective-permute-start(bf16[544,128]{1,0:T(8,128)(2,1)S(1)} %get-tuple-element.96), channel_id=1, source_target_pairs={{0,12},{8,4},{9,5},{4,0},{5,1},{12,8},{13,9},{1,13},{2,14},{10,6},... | collective-permute-start | bytes 417800 | tf_op jit(solution)/shard_map/ppermute | solution.py:517
  133.4 10.4 %collective-permute-start.26 = (bf16[544,128]{1,0:T(8,128)(2,1)S(1)}, bf16[544,128]{1,0:T(8,128)(2,1)S(1)}, u32[]{:S(2)}, u32[]{:S(2)}) collective-permute-start(bf16[544,128]{1,0:T(8,128)(2,1)S(1)} %get-tuple-element.97), channel_id=1, source_target_pairs={{0,13},{8,5},{9,4},{4,1},{5,0},{12,9},{13,8},{1,12},{2,15},{10,7},... | collective-permute-start | bytes 417800 | tf_op jit(solution)/shard_map/ppermute | solution.py:517
  135.1 8.7 %collective-permute-start.27 = (bf16[544,128]{1,0:T(8,128)(2,1)S(1)}, bf16[544,128]{1,0:T(8,128)(2,1)S(1)}, u32[]{:S(2)}, u32[]{:S(2)}) collective-permute-start(bf16[544,128]{1,0:T(8,128)(2,1)S(1)} %get-tuple-element.98), channel_id=1, source_target_pairs={{0,1},{8,9},{9,8},{4,5},{5,4},{12,13},{13,12},{1,0},{2,3},{10,11},... | collective-permute-start | bytes 417800 | tf_op jit(solution)/shard_map/ppermute | solution.py:517
  135.1 8.7 %copy-start = (bf16[1024,512]{1,0:T(8,128)(2,1)S(1)}, bf16[1024,512]{1,0:T(8,128)(2,1)}, u32[]{:S(2)}) copy-start(bf16[1024,512]{1,0:T(8,128)(2,1)} %refs_3_.7) | copy-start | bytes 3145732
  147.8 29.5 %collective-permute-start.29 = (bf16[1024,512]{1,0:T(8,128)(2,1)S(1)}, bf16[1024,512]{1,0:T(8,128)(2,1)S(1)}, u32[]{:S(2)}, u32[]{:S(2)}) collective-permute-start(bf16[1024,512]{1,0:T(8,128)(2,1)S(1)} %get-tuple-element.103), channel_id=1, source_target_pairs={{0,2},{2,0},{1,3},{3,1},{4,6},{6,4},{5,7},{7,5},{8,10},{10,8},{9,1... | collective-permute-start | bytes 3145736 | tf_op jit(solution)/shard_map/ppermute | solution.py:523
  149.0 2.6 %collective-permute-start.33 = (bf16[4,128,512]{2,1,0:T(8,128)(2,1)S(1)}, bf16[4,128,512]{2,1,0:T(8,128)(2,1)S(1)}, u32[]{:S(2)}, u32[]{:S(2)}) collective-permute-start(bf16[4,128,512]{2,1,0:T(8,128)(2,1)S(1)} %get-tuple-element.108), channel_id=1, source_target_pairs={{0,1},{1,0},{2,3},{3,2},{4,5},{5,4},{6,7},{7,6},{8,9},{9,8},{10,11... | collective-permute-start | bytes 1572872 | tf_op jit(solution)/shard_map/ppermute | solution.py:523
  151.1 5.1 %collective-permute-start.28 = (bf16[4,128,512]{2,1,0:T(8,128)(2,1)S(1)}, bf16[4,128,512]{2,1,0:T(8,128)(2,1)S(1)}, u32[]{:S(2)}, u32[]{:S(2)}) collective-permute-start(bf16[4,128,512]{2,1,0:T(8,128)(2,1)S(1)} %get-tuple-element.101), channel_id=1, source_target_pairs={{0,1},{1,0},{2,3},{3,2},{4,5},{5,4},{6,7},{7,6},{8,9},{9,8},{10,11... | collective-permute-start | bytes 1572872 | tf_op jit(solution)/shard_map/ppermute | solution.py:523
  152.3 8.3 %collective-permute-start.34 = (bf16[128,512]{1,0:T(8,128)(2,1)S(1)}, bf16[128,512]{1,0:T(8,128)(2,1)S(1)}, u32[]{:S(2)}, u32[]{:S(2)}) collective-permute-start(bf16[128,512]{1,0:T(8,128)(2,1)S(1)} %get-tuple-element.114), channel_id=1, source_target_pairs={{0,4},{4,8},{8,12},{12,0},{1,5},{5,9},{9,13},{13,1},{2,6},{6,10},{... | collective-permute-start | bytes 393224 | tf_op jit(solution)/shard_map/ppermute | solution.py:523
  153.1 13.1 %collective-permute-start.35 = (bf16[128,512]{1,0:T(8,128)(2,1)S(1)}, bf16[128,512]{1,0:T(8,128)(2,1)S(1)}, u32[]{:S(2)}, u32[]{:S(2)}) collective-permute-start(bf16[128,512]{1,0:T(8,128)(2,1)S(1)} %get-tuple-element.115), channel_id=1, source_target_pairs={{0,8},{4,12},{8,0},{12,4},{1,9},{5,13},{9,1},{13,5},{2,10},{6,14},... | collective-permute-start | bytes 393224 | tf_op jit(solution)/shard_map/ppermute | solution.py:523
  155.9 19.4 %collective-permute-start.36 = (bf16[128,512]{1,0:T(8,128)(2,1)S(1)}, bf16[128,512]{1,0:T(8,128)(2,1)S(1)}, u32[]{:S(2)}, u32[]{:S(2)}) collective-permute-start(bf16[128,512]{1,0:T(8,128)(2,1)S(1)} %get-tuple-element.116), channel_id=1, source_target_pairs={{0,12},{4,0},{8,4},{12,8},{1,13},{5,1},{9,5},{13,9},{2,14},{6,2},{... | collective-permute-start | bytes 393224 | tf_op jit(solution)/shard_map/ppermute | solution.py:523
  156.9 19.2 %collective-permute-start.30 = (bf16[128,512]{1,0:T(8,128)(2,1)S(1)}, bf16[128,512]{1,0:T(8,128)(2,1)S(1)}, u32[]{:S(2)}, u32[]{:S(2)}) collective-permute-start(bf16[128,512]{1,0:T(8,128)(2,1)S(1)} %get-tuple-element.104), channel_id=1, source_target_pairs={{0,4},{4,8},{8,12},{12,0},{1,5},{5,9},{9,13},{13,1},{2,6},{6,10},{... | collective-permute-start | bytes 393224 | tf_op jit(solution)/shard_map/ppermute | solution.py:523
  160.6 15.9 %collective-permute-start.31 = (bf16[128,512]{1,0:T(8,128)(2,1)S(1)}, bf16[128,512]{1,0:T(8,128)(2,1)S(1)}, u32[]{:S(2)}, u32[]{:S(2)}) collective-permute-start(bf16[128,512]{1,0:T(8,128)(2,1)S(1)} %get-tuple-element.105), channel_id=1, source_target_pairs={{0,8},{4,12},{8,0},{12,4},{1,9},{5,13},{9,1},{13,5},{2,10},{6,14},... | collective-permute-start | bytes 393224 | tf_op jit(solution)/shard_map/ppermute | solution.py:523
  166.2 10.3 %collective-permute-start.32 = (bf16[128,512]{1,0:T(8,128)(2,1)S(1)}, bf16[128,512]{1,0:T(8,128)(2,1)S(1)}, u32[]{:S(2)}, u32[]{:S(2)}) collective-permute-start(bf16[128,512]{1,0:T(8,128)(2,1)S(1)} %get-tuple-element.106), channel_id=1, source_target_pairs={{0,12},{4,0},{8,4},{12,8},{1,13},{5,1},{9,5},{13,9},{2,14},{6,2},{... | collective-permute-start | bytes 393224 | tf_op jit(solution)/shard_map/ppermute | solution.py:523

commit v10 on v9

--- a/solution.py
+++ b/solution.py
@@ -89,62 +89,99 @@
     return slot, dot_nt(jnp.ones((COUNT_ROWS, toks), BF16), spread).astype(BF16)
 
 
-def project_query_kernel(sizes, groups, rows, me_ref, assign_ref, tokens_hbm, weight_hbm, cotan_hbm, *rest):
-    out_refs, rest = rest[:-10], rest[-10:]
-    slot_ref, tokens_ref, weight_ref, cotan_ref, query_ref, pick_ref, part_ref, sorted_ref, in_sems, out_sems = rest
-    toks, width = tokens_ref.shape
-    heads = weight_ref.shape[1] // HD
-    fine = min(256, toks, width)
-
-    def load(kind):
-        source, target = ((cotan_hbm, cotan_ref), (weight_hbm, weight_ref), (tokens_hbm, tokens_ref))[kind]
-        return [
-            pltpu.make_async_copy(
-                source.at[pl.ds(row, fine), :], target.at[pl.ds(row, fine), :], in_sems.at[kind, row // fine]
-            )
-            for row in range(0, source.shape[0], fine)
-        ]
-
-    for copy in load(0) + load(1) + load(2):
-        copy.start()
+def beside(query, cotan):
+    low = low_half(query.shape)
+    even = jnp.where(low, query, swap_halves(cotan)).astype(BF16)
+    return even, jnp.where(low, swap_halves(query), cotan).astype(BF16)
+
+
+def load_rows(source, target, sems, fine):
+    return [
+        pltpu.make_async_copy(source.at[pl.ds(row, fine), :], target.at[pl.ds(row, fine), :], sems.at[row // fine])
+        for row in range(0, target.shape[0], fine)
+    ]
+
+
+def project_far_kernel(sizes, groups, rows, heads, assign_ref, tokens_hbm, weight_hbm, cotan_hbm, *refs):
+    out_refs, refs = refs[: sizes[1]], refs[sizes[1] :]
+    slot_ref, tokens_ref, weight_ref, cotan_ref, mixed_ref, sems = refs
+    toks = tokens_ref.shape[0]
+    fine = min(256, toks)
+    me = (lax.axis_index("seq"), lax.axis_index("sub"))
+    owner = owner_of(me, steps_of(sizes)[1], sizes) - me[1]
+    group, head = lax.div(owner, jnp.int32(heads)), lax.rem(owner, jnp.int32(heads))
+    columns = pl.ds(pl.multiple_of(head * HD, LANES), sizes[1] * HD)
+    loads = [
+        load_rows(source, target, sems.at[kind], fine)
+        for kind, (source, target) in enumerate(
+            ((weight_hbm.at[:, columns], weight_ref), (tokens_hbm, tokens_ref), (cotan_hbm.at[:, columns], cotan_ref))
+        )
+    ]
+    for load in loads:
+        for copy in load:
+            copy.start()
     slot, tallies = slots_of(assign_ref[...], groups, rows)
     slot_ref[...] = slot
+    pick = ones_where(iota((rows, toks), 0) + group * rows == slot)
+    for copy in loads[0] + loads[2]:
+        copy.wait()
+    step = min(512, toks)
+    for first in range(0, toks, step):
+        for copy in loads[1][first // fine : (first + step) // fine]:
+            copy.wait()
+        where = slice(first, first + step)
+        query, cotan = dot(tokens_ref[where, :], weight_ref[...]), cotan_ref[where, :].astype(F32)
+        for pair in range(sizes[1] // 2):
+            pair_columns = slice(pair * LANES, (pair + 1) * LANES)
+            even, odd = beside(query[:, pair_columns], cotan[:, pair_columns])
+            mixed_ref[where, 2 * pair * LANES : (2 * pair + 1) * LANES] = even
+            mixed_ref[where, (2 * pair + 1) * LANES : (2 * pair + 2) * LANES] = odd
+    in_order = dot(pick, mixed_ref[...]).astype(BF16)
+    for ahead, out_ref in enumerate(out_refs):
+        sub = lax.rem(me[1] + ahead, jnp.int32(sizes[1]))
+        for other in range(sizes[1]):
+
+            @pl.when(sub == other)
+            def _():
+                out_ref[:rows, :] = in_order[:, other * LANES : (other + 1) * LANES]
+
+        out_ref[rows:, :] = tallies
+
+
+def project_query_kernel(sizes, groups, rows, me_ref, slot_ref, assign_ref, tokens_ref, weight_ref, cotan_ref, *rest):
+    out_refs, (mixed_ref, sorted_ref) = rest[:-2], rest[-2:]
+    toks = tokens_ref.shape[0]
+    heads = weight_ref.shape[1] // HD
+    step = min(512, toks)
+    for first in range(0, toks, step):
+        where = slice(first, first + step)
+        query, cotan = dot(tokens_ref[where, :], weight_ref[...]), cotan_ref[where, :].astype(F32)
+        for pair in range(heads // 2):
+            columns = slice(pair * LANES, (pair + 1) * LANES)
+            even, odd = beside(query[:, columns], cotan[:, columns])
+            mixed_ref[where, 2 * pair * LANES : (2 * pair + 1) * LANES] = even
+            mixed_ref[where, (2 * pair + 1) * LANES : (2 * pair + 2) * LANES] = odd
+    part = min(512, rows)
+    pieces = rows // part
+
+    @pl.loop(0, groups * pieces)
+    def _(i):
+        group, piece = lax.div(i, jnp.int32(pieces)), lax.rem(i, jnp.int32(pieces))
+        first = pl.multiple_of(piece * part, part)
+        pick = ones_where(iota((part, toks), 0) + i * part == slot_ref[...])
+        sorted_rows = dot(pick, mixed_ref[...]).astype(BF16)
+        for head in range(heads):
+            sorted_ref[group * heads + head, pl.ds(first, part), :] = sorted_rows[
+                :, head * LANES : (head + 1) * LANES
+            ]
+
+    member = jnp.where(iota((LANES, toks), 0) == assign_ref[...], 1.0, 0.0).astype(BF16)
+    tallies = dot_nt(jnp.ones((COUNT_ROWS, toks), BF16), member).astype(BF16)
     for owner in range(sorted_ref.shape[0]):
         sorted_ref[owner, rows:, :] = tallies
-    slots = pick_ref.shape[0]
-    step = min(512, slots)
-    for first in range(0, slots, step):
-        pick_ref[first : first + step, :] = ones_where(iota((step, toks), 0) + first == slot)
-    for copy in load(0):
-        copy.wait()
-    for first in range(0, slots, step):
-        part_ref[first : first + step, :] = dot(pick_ref[first : first + step, :], cotan_ref[...])
-    for copy in load(1):
-        copy.wait()
-    tokens = load(2)
-    for index, first in enumerate(range(0, toks, fine)):
-        tokens[index].wait()
-        query_ref[first : first + fine, :] = dot(tokens_ref[first : first + fine, :], weight_ref[...]).astype(BF16)
-    part = min(512, rows)
-    low = low_half((part, LANES))
-    for first in range(0, slots, part):
-        group, start = first // rows, first % rows
-        query = dot(pick_ref[first : first + part, :], query_ref[...])
-        for pair in range(heads // 2):
-            columns = slice(pair * LANES, (pair + 1) * LANES)
-            q_tile, c_tile = query[:, columns], part_ref[first : first + part, columns]
-            even = jnp.where(low, q_tile, swap_halves(c_tile)).astype(BF16)
-            odd = jnp.where(low, swap_halves(q_tile), c_tile).astype(BF16)
-            sorted_ref[group * heads + 2 * pair, start : start + part, :] = even
-            sorted_ref[group * heads + 2 * pair + 1, start : start + part, :] = odd
-    copies = [
-        pltpu.make_async_copy(sorted_ref.at[owner_of(me_ref, ahead, sizes)], out_ref, out_sems.at[k])
-        for k, (ahead, out_ref) in enumerate(zip(steps_of(sizes), out_refs))
-    ]
-    for copy in copies:
-        copy.start()
-    for copy in copies:
-        copy.wait()
+    steps = steps_of(sizes)
+    for ahead, out_ref in zip(steps[:1] + steps[1 + sizes[1] :], out_refs):
+        out_ref[...] = sorted_ref[owner_of(me_ref, ahead, sizes)]
 
 
 def project_value_kernel(sizes, groups, rows, me_ref, slot_ref, tokens_ref, weight_ref, *rest):
@@ -491,12 +528,11 @@
     moved = sum(x.size * x.dtype.itemsize for x in inputs) + sum(
         x.size * x.dtype.itemsize for x in jax.tree.leaves(outs)
     )
-    out_space = lambda x: pl.ANY if in_place and x.dtype == BF16 else pltpu.VMEM
     return pl.pallas_call(
         body,
         out_shape=outs,
         in_specs=specs,
-        out_specs=jax.tree.map(lambda x: pl.BlockSpec(memory_space=out_space(x)), outs),
+        out_specs=jax.tree.map(lambda _: pl.BlockSpec(memory_space=pltpu.VMEM), outs),
         scratch_shapes=list(scratch),
         compiler_params=pltpu.CompilerParams(vmem_limit_bytes=vmem * 2**20),
         cost_estimate=pl.CostEstimate(flops=flops, bytes_accessed=moved, transcendentals=0),
@@ -566,31 +602,39 @@
     def several(count, *dims):
         return (shape(dims, BF16),) * count
 
-    *send_mixed, slot_row = call(
-        functools.partial(project_query_kernel, sizes, groups, rows),
-        several(owners, rows + COUNT_ROWS, LANES) + (shape((1, toks), jnp.int32),),
-        (me, assignment.reshape(1, toks), tokens_in, w_query, cotangent),
-        in_place=(2, 3, 4),
+    assign_row = assignment.reshape(1, toks)
+    *far_mixed, slot_row = call(
+        functools.partial(project_far_kernel, sizes, groups, rows, heads),
+        several(sizes[1], rows + COUNT_ROWS, LANES) + (shape((1, toks), jnp.int32),),
+        (assign_row, tokens_in, w_query, cotangent),
+        smem=(),
+        in_place=(1, 2, 3),
         scratch=[
             pltpu.VMEM((toks, width), BF16),
-            pltpu.VMEM((width, width_dev), BF16),
-            pltpu.VMEM((toks, width_dev), BF16),
-            pltpu.VMEM((toks, width_dev), BF16),
-            pltpu.VMEM((slots, toks), BF16),
-            pltpu.VMEM((slots, width_dev), F32),
-            pltpu.VMEM((owners, rows + COUNT_ROWS, LANES), BF16),
-            pltpu.SemaphoreType.DMA((3, max(toks, width) // min(256, toks, width))),
-            pltpu.SemaphoreType.DMA((owners,)),
+            pltpu.VMEM((width, sizes[1] * HD), BF16),
+            pltpu.VMEM((toks, sizes[1] * HD), BF16),
+            pltpu.VMEM((toks, sizes[1] * LANES), BF16),
+            pltpu.SemaphoreType.DMA((3, max(toks, width) // min(256, toks))),
         ],
+        flops=2 * toks * width * sizes[1] * HD + 2 * rows * toks * sizes[1] * LANES,
+        vmem=60,
+        name="project_far",
+    )
+    own_mixed, *near_mixed = call(
+        functools.partial(project_query_kernel, sizes, groups, rows),
+        several(owners - sizes[1], rows + COUNT_ROWS, LANES),
+        (me, slot_row, assign_row, tokens_in, w_query, cotangent),
+        scratch=[pltpu.VMEM((toks, 2 * width_dev), BF16), pltpu.VMEM((owners, rows + COUNT_ROWS, LANES), BF16)],
         flops=2 * toks * width * width_dev + 4 * slots * toks * width_dev,
-        vmem=60,
         name="project_query",
     )
+    send_mixed = [own_mixed, *far_mixed, *near_mixed]
     got_mixed = exchange(send_mixed, sizes)
     *send_value, turned, unsort = call(
         functools.partial(project_value_kernel, sizes, groups, rows),
         several(owners, half, LANES) + several(1, width, toks) + several(1, toks, slots),
         (me, slot_row, tokens_in, w_value),
+        after=near_mixed[:1],
         scratch=[pltpu.VMEM((toks, width_dev), BF16), pltpu.VMEM((owners, half, LANES), BF16)],
         flops=2 * toks * width * width_dev + 2 * slots * toks * width_dev,
         name="project_value",

time: 179 us -> 181 us (1.011)
  waiting for transfers between devices: 56.3 us -> 53.4 us
  Pallas kernels: 58.2 us -> 60.5 us
    ppermute x28, waiting for transfers between devices: 48.4 us -> 43 us  [exchange(): out.append(part if ahead == (0, 0) else lax.ppermute(part, OWNERS, moves))]
    ppermute x28, starting transfers between devices: 47.2 us -> 50.6 us  [exchange(): out.append(part if ahead == (0, 0) else lax.ppermute(part, OWNERS, moves))]
    ppermute x9, waiting for transfers between devices: 7.83 us -> 10.4 us  [shift(): lax.ppermute(part, axis, [(i, (i + ahead) % size) for i in range(size)])]
    pallas_call x13 -> x14, Pallas kernels: 58.2 us -> 60.5 us  [call(): pl.pallas_call(body, out_shape=outs, in_specs=specs, out_specs=jax.tree.m...]
    ppermute x9, starting transfers between devices: 14.7 us -> 12.6 us  [shift(): lax.ppermute(part, axis, [(i, (i + ahead) % size) for i in range(size)])]
  transfers between devices with their start and end apart: 37 -> 37, of which waited for: 11 -> 10; matrix products, arithmetic and copies ran while one was open for 0% -> 0% of each run, Pallas kernels for 25% -> 28%
where the time goes in v10:
time: 181 us; the launch traced here: 180 us
  starting transfers between devices  63.2 us (35%)
  Pallas kernels  60.5 us (33%)
  waiting for transfers between devices  53.4 us (30%)
  local copies, waits for them, and re-layouts  1.92 us (1%)
    pallas_call x14, Pallas kernels, call(): pl.pallas_call(body, out_shape=outs, in_specs=specs, out_specs=jax.tree.m...  60.5 us
    ppermute x28, starting transfers between devices, exchange(): out.append(part if ahead == (0, 0) else lax.ppermute(part, OWNERS, moves))  50.6 us
    ppermute x28, waiting for transfers between devices, exchange(): out.append(part if ahead == (0, 0) else lax.ppermute(part, OWNERS, moves))  43 us
    ppermute x9, starting transfers between devices, shift(): lax.ppermute(part, axis, [(i, (i + ahead) % size) for i in range(size)])  12.6 us
    ppermute x9, waiting for transfers between devices, shift(): lax.ppermute(part, axis, [(i, (i + ahead) % size) for i in range(size)])  10.4 us
  transfers between devices with their start and end apart: 37, of which 10 were waited for; matrix products, arithmetic and copies ran while one was open for 0% of the time, Pallas kernels for 28%

profile of v10, /device:TPU:0, one launch (start us, length us, event | category | flops | bytes accessed | tf_op | source)
XLA Modules:
  0.0 179.9 jit_solution(14810762518111123859)
XLA Ops:
  0.7 5.6 %project_far.1 = (bf16[1040,128]{1,0:T(8,128)(2,1)}, bf16[1040,128]{1,0:T(8,128)(2,1)}, s32[1,1024]{1,0:T(1,128)}) custom-call(s32[1,1024]{1,0:T(1,128)} %bitcast.5, bf16[1024,1024]{1,0:T(8,128)(2,1)} %refs_2_.3, bf16[1024,512]{1,0:T(8,128)(2,1)} %refs_3_.9, bf16[1024,512]{1,0:T(8,128)(2,1)} %refs_5_.1), custom_call_target="tpu_custom_call" | custom-call | flops 805306368 | bytes 4734976 | tf_op jit(solution)/shard_map/project_far/pallas_call | solution.py:531
  6.2 4.1 %collective-permute-start = (bf16[1040,128]{1,0:T(8,128)(2,1)}, bf16[1040,128]{1,0:T(8,128)(2,1)S(1)}, u32[]{:S(2)}, u32[]{:S(2)}) collective-permute-start(bf16[1040,128]{1,0:T(8,128)(2,1)} %get-tuple-element.66), channel_id=1, source_target_pairs={{0,8},{8,0},{9,1},{4,12},{5,13},{12,4},{13,5},{1,9},{2,10},{10,2},... | collective-permute-start | bytes 798728 | tf_op jit(solution)/shard_map/ppermute | solution.py:553
  10.4 1.2 copy-done.2
  11.7 0.7 copy-done.5
  12.4 4.8 %project_query.1 = (bf16[1040,128]{1,0:T(8,128)(2,1)S(1)}, bf16[1040,128]{1,0:T(8,128)(2,1)S(1)}, bf16[1040,128]{1,0:T(8,128)(2,1)S(1)}, bf16[1040,128]{1,0:T(8,...) custom-call(s32[4]{0:T(128)S(1)} %pad_add_fusion.refs_0_, s32[1,1024]{1,0:T(1,128)S(1)} %copy-done.5, ...), custom_call_target="tpu_custom_call" | custom-call | flops 3221225472 | bytes 5799952 | tf_op jit(solution)/shard_map/project_query/pallas_call | solution.py:531
  17.2 4.8 %project_value.1 = (bf16[512,128]{1,0:T(8,128)(2,1)S(1)}, bf16[512,128]{1,0:T(8,128)(2,1)S(1)}, bf16[512,128]{1,0:T(8,128)(2,1)S(1)}, bf16[512,128]{1,0:T(8,128)...) custom-call(s32[4]{0:T(128)S(1)} %pad_add_fusion.refs_0_, ...), custom_call_target="tpu_custom_call" | custom-call | flops 2147483648 | bytes 8392720 | tf_op jit(solution)/shard_map/project_value/pallas_call | solution.py:531
  22.0 2.1 %collective-permute-start.14 = (bf16[512,128]{1,0:T(8,128)(2,1)S(1)}, bf16[512,128]{1,0:T(8,128)(2,1)S(1)}, u32[]{:S(2)}, u32[]{:S(2)}) collective-permute-start(bf16[512,128]{1,0:T(8,128)(2,1)S(1)} %get-tuple-element.84), channel_id=1, source_target_pairs={{0,8},{8,0},{9,1},{4,12},{5,13},{12,4},{13,5},{1,9},{2,10},{10,2},... | collective-permute-start | bytes 393224 | tf_op jit(solution)/shard_map/ppermute | solution.py:553
  24.8 1.5 collective-permute-start.3
  26.3 22.7 %collective-permute-done.14.refs_4_ = bf16[512,128]{1,0:T(8,128)(2,1)S(1)} collective-permute-done((bf16[512,128]{1,0:T(8,128)(2,1)S(1)}, bf16[512,128]{1,0:T(8,128)(2,1)S(1)}, u32[]{:S(2)}, u32[]{:S(2)}) %collective-permute-start.14) | collective-permute-done | bytes 131104 | tf_op jit(solution)/shard_map/ppermute | solution.py:553
  49.0 1.1 collective-permute-done.15.refs_5_
  50.2 1.5 collective-permute-start.6
  51.7 1.7 collective-permute-start.2
  53.4 9.9 %collective-permute-start.16 = (bf16[512,128]{1,0:T(8,128)(2,1)S(1)}, bf16[512,128]{1,0:T(8,128)(2,1)S(1)}, u32[]{:S(2)}, u32[]{:S(2)}) collective-permute-start(bf16[512,128]{1,0:T(8,128)(2,1)S(1)} %get-tuple-element.86), channel_id=1, source_target_pairs={{0,4},{8,12},{9,13},{4,8},{5,9},{12,0},{13,1},{1,5},{2,6},{10,14},... | collective-permute-start | bytes 393224 | tf_op jit(solution)/shard_map/ppermute | solution.py:553
  63.3 1.7 collective-permute-start.17
  65.0 7.1 %collective-permute-done.5.refs_7_ = bf16[1040,128]{1,0:T(8,128)(2,1)S(1)} collective-permute-done((bf16[1040,128]{1,0:T(8,128)(2,1)S(1)}, bf16[1040,128]{1,0:T(8,128)(2,1)S(1)}, u32[]{:S(2)}, u32[]{:S(2)}) %collective-permute-start.5) | collective-permute-done | bytes 266272 | tf_op jit(solution)/shard_map/ppermute | solution.py:553
  72.1 1.3 collective-permute-start.19
  73.4 1.5 collective-permute-start.20
  74.9 13.5 %value_grad.1 = (bf16[512,128]{1,0:T(8,128)(2,1)S(1)}, bf16[512,128]{1,0:T(8,128)(2,1)S(1)}, bf16[512,128]{1,0:T(8,128)(2,1)S(1)}, bf16[512,128]{1,0:T(8,128)(2,...) custom-call(s32[4]{0:T(128)S(1)} %pad_add_fusion.refs_0_, ...), custom_call_target="tpu_custom_call" | custom-call | flops 2147483648 | bytes 8163344 | tf_op jit(solution)/shard_map/value_grad/pallas_call | solution.py:531
  88.4 1.5 collective-permute-start.7
  89.9 0.7 collective-permute-start.8
  90.7 0.9 collective-permute-start.9
  91.5 1.3 collective-permute-start.10
  92.9 15.8 %query_grad.1 = (bf16[544,128]{1,0:T(8,128)(2,1)S(1)}, bf16[544,128]{1,0:T(8,128)(2,1)S(1)}, bf16[544,128]{1,0:T(8,128)(2,1)S(1)}, bf16[544,128]{1,0:T(8,128)(2,...) custom-call(s32[4]{0:T(128)S(1)} %pad_add_fusion.refs_0_, ...), custom_call_target="tpu_custom_call" | custom-call | flops 3221225472 | bytes 7147536 | tf_op jit(solution)/shard_map/query_grad/pallas_call | solution.py:531
  108.6 2.4 %collective-permute-start.21 = (bf16[544,128]{1,0:T(8,128)(2,1)S(1)}, bf16[544,128]{1,0:T(8,128)(2,1)S(1)}, u32[]{:S(2)}, u32[]{:S(2)}) collective-permute-start(bf16[544,128]{1,0:T(8,128)(2,1)S(1)} %get-tuple-element.92), channel_id=1, source_target_pairs={{0,8},{8,0},{9,1},{4,12},{5,13},{12,4},{13,5},{1,9},{2,10},{10,2},... | collective-permute-start | bytes 417800 | tf_op jit(solution)/shard_map/ppermute | solution.py:553
  111.5 2.1 %collective-permute-start.11 = (bf16[512,128]{1,0:T(8,128)(2,1)S(1)}, bf16[512,128]{1,0:T(8,128)(2,1)S(1)}, u32[]{:S(2)}, u32[]{:S(2)}) collective-permute-start(bf16[512,128]{1,0:T(8,128)(2,1)S(1)} %get-tuple-element.77), channel_id=1, source_target_pairs={{0,12},{8,4},{9,5},{4,0},{5,1},{12,8},{13,9},{1,13},{2,14},{10,6},... | collective-permute-start | bytes 393224 | tf_op jit(solution)/shard_map/ppermute | solution.py:553
  113.6 1.3 collective-permute-start.12
  114.9 6.0 %collective-permute-done.11.refs_8_ = bf16[512,128]{1,0:T(8,128)(2,1)S(1)} collective-permute-done((bf16[512,128]{1,0:T(8,128)(2,1)S(1)}, bf16[512,128]{1,0:T(8,128)(2,1)S(1)}, u32[]{:S(2)}, u32[]{:S(2)}) %collective-permute-start.11) | collective-permute-done | bytes 131104 | tf_op jit(solution)/shard_map/ppermute | solution.py:553
  120.9 10.2 %collective-permute-start.23 = (bf16[544,128]{1,0:T(8,128)(2,1)S(1)}, bf16[544,128]{1,0:T(8,128)(2,1)S(1)}, u32[]{:S(2)}, u32[]{:S(2)}) collective-permute-start(bf16[544,128]{1,0:T(8,128)(2,1)S(1)} %get-tuple-element.94), channel_id=1, source_target_pairs={{0,4},{8,12},{9,13},{4,8},{5,9},{12,0},{13,1},{1,5},{2,6},{10,14},... | collective-permute-start | bytes 417800 | tf_op jit(solution)/shard_map/ppermute | solution.py:553
  131.1 2.4 %collective-permute-start.24 = (bf16[544,128]{1,0:T(8,128)(2,1)S(1)}, bf16[544,128]{1,0:T(8,128)(2,1)S(1)}, u32[]{:S(2)}, u32[]{:S(2)}) collective-permute-start(bf16[544,128]{1,0:T(8,128)(2,1)S(1)} %get-tuple-element.95), channel_id=1, source_target_pairs={{0,5},{8,13},{9,12},{4,9},{5,8},{12,1},{13,0},{1,4},{2,7},{10,15},... | collective-permute-start | bytes 417800 | tf_op jit(solution)/shard_map/ppermute | solution.py:553
  133.5 0.7 collective-permute-start.25
  134.9 3.9 %value_home.1 = (bf16[1024,512]{1,0:T(8,128)(2,1)S(1)}, bf16[4,128,512]{2,1,0:T(8,128)(2,1)S(1)}, bf16[4,128,512]{2,1,0:T(8,128)(2,1)S(1)}) custom-call(s32[4]{0:T(128)S(1)} %pad_add_fusion.refs_0_, bf16[1024,1024]{1,0:T(8,128)(2,1)S(1)} %get-tuple-element.64.refs_1_, bf16[1024,1024]{1,0:T(8,128)(2,1)S(1)} %get-tuple-element.63.refs_2_.refs_1_, ...), custom_call_target="tpu_custom_call" | custom-call | flops 2147483648 | bytes 7340048 | tf_op jit(solution)/shard_map/value_home/pallas_call | solution.py:531
  139.0 2.9 %collective-permute-done.25.refs_10_ = bf16[544,128]{1,0:T(8,128)(2,1)S(1)} collective-permute-done((bf16[544,128]{1,0:T(8,128)(2,1)S(1)}, bf16[544,128]{1,0:T(8,128)(2,1)S(1)}, u32[]{:S(2)}, u32[]{:S(2)}) %collective-permute-start.25) | collective-permute-done | bytes 139296 | tf_op jit(solution)/shard_map/ppermute | solution.py:553
  141.9 2.9 %collective-permute-done.26.refs_11_ = bf16[544,128]{1,0:T(8,128)(2,1)S(1)} collective-permute-done((bf16[544,128]{1,0:T(8,128)(2,1)S(1)}, bf16[544,128]{1,0:T(8,128)(2,1)S(1)}, u32[]{:S(2)}, u32[]{:S(2)}) %collective-permute-start.26) | collective-permute-done | bytes 139296 | tf_op jit(solution)/shard_map/ppermute | solution.py:553
  144.8 4.0 %query_home.1 = (bf16[1024,512]{1,0:T(8,128)(2,1)S(1)}, bf16[1024,512]{1,0:T(8,128)(2,1)S(1)}, f32[64,512]{1,0:T(8,128)}) custom-call(s32[4]{0:T(128)S(1)} %pad_add_fusion.refs_0_, bf16[1024,1024]{1,0:T(8,128)(2,1)S(1)} %get-tuple-element.63.refs_2_.refs_1_, bf16[1024,512]{1,0:T(8,128)(2,1)S(1)} %get-tuple-element.80.refs_2_, bf16[1024,512]{1,0:T(8,128)(2,1)S(1)} %copy-done, ...), custom_call_target="tpu_custom_call" | custom-call | flops 2147483648 | bytes 8585232 | tf_op jit(solution)/shard_map/query_home/pallas_call | solution.py:531
  148.7 1.6 collective-permute-start.29
  150.3 2.0 %query_weight.1 = (bf16[4,128,512]{2,1,0:T(8,128)(2,1)S(1)}, bf16[4,128,512]{2,1,0:T(8,128)(2,1)S(1)}) custom-call(s32[4]{0:T(128)S(1)} %pad_add_fusion.refs_0_, bf16[1024,1024]{1,0:T(8,128)(2,1)S(1)} %get-tuple-element.64.refs_1_, bf16[1024,512]{1,0:T(8,128)(2,1)S(1)} %get-tuple-element.99.refs_2_.refs_1_), custom_call_target="tpu_custom_call" | custom-call | flops 1073741824 | bytes 4194320 | tf_op jit(solution)/shard_map/query_weight/pallas_call | solution.py:531
  153.0 0.7 value_subs.1
  154.2 2.6 %collective-permute-start.35 = (bf16[128,512]{1,0:T(8,128)(2,1)S(1)}, bf16[128,512]{1,0:T(8,128)(2,1)S(1)}, u32[]{:S(2)}, u32[]{:S(2)}) collective-permute-start(bf16[128,512]{1,0:T(8,128)(2,1)S(1)} %get-tuple-element.115), channel_id=1, source_target_pairs={{0,8},{4,12},{8,0},{12,4},{1,9},{5,13},{9,1},{13,5},{2,10},{6,14},... | collective-permute-start | bytes 393224 | tf_op jit(solution)/shard_map/ppermute | solution.py:559
  156.8 0.8 collective-permute-start.36
  158.2 1.3 collective-permute-start.30
  159.5 2.4 %collective-permute-done.34.refs_1_ = bf16[128,512]{1,0:T(8,128)(2,1)S(1)} collective-permute-done((bf16[128,512]{1,0:T(8,128)(2,1)S(1)}, bf16[128,512]{1,0:T(8,128)(2,1)S(1)}, u32[]{:S(2)}, u32[]{:S(2)}) %collective-permute-start.34) | collective-permute-done | bytes 131104 | tf_op jit(solution)/shard_map/ppermute | solution.py:559
  162.0 5.6 %collective-permute-done.35.refs_2_ = bf16[128,512]{1,0:T(8,128)(2,1)S(1)} collective-permute-done((bf16[128,512]{1,0:T(8,128)(2,1)S(1)}, bf16[128,512]{1,0:T(8,128)(2,1)S(1)}, u32[]{:S(2)}, u32[]{:S(2)}) %collective-permute-start.35) | collective-permute-done | bytes 131104 | tf_op jit(solution)/shard_map/ppermute | solution.py:559
  167.6 5.2 %collective-permute-start.32 = (bf16[128,512]{1,0:T(8,128)(2,1)S(1)}, bf16[128,512]{1,0:T(8,128)(2,1)S(1)}, u32[]{:S(2)}, u32[]{:S(2)}) collective-permute-start(bf16[128,512]{1,0:T(8,128)(2,1)S(1)} %get-tuple-element.106), channel_id=1, source_target_pairs={{0,12},{4,0},{8,4},{12,8},{1,13},{5,1},{9,5},{13,9},{2,14},{6,2},{... | collective-permute-start | bytes 393224 | tf_op jit(solution)/shard_map/ppermute | solution.py:559
  172.8 2.0 %input_own.1.refs_0_ = bf16[1024,512]{1,0:T(8,128)(2,1)S(1)} custom-call(s32[4]{0:T(128)S(1)} %pad_add_fusion.refs_0_, bf16[1024,512]{1,0:T(8,128)(2,1)S(1)} %get-tuple-element.99.refs_2_.refs_1_, bf16[1024,512]{1,0:T(8,128)(2,1)S(1)} %get-tuple-element.80.refs_2_, bf16[1024,512]{1,0:T(8,128)(2,1)S(1)} %copy-done, bf16[1024,512]{1,0:T(8,128)(2,1)S(1)} %copy-done.3, ...), custom_call_target="tpu_custom_call" | custom-call | flops 1073741824 | bytes 5242896 | tf_op jit(solution)/shard_map/input_own/pallas_call | solution.py:531
  174.8 0.8 value_sum.1
  175.6 2.3 %collective-permute-done.31.refs_2_ = bf16[128,512]{1,0:T(8,128)(2,1)S(1)} collective-permute-done((bf16[128,512]{1,0:T(8,128)(2,1)S(1)}, bf16[128,512]{1,0:T(8,128)(2,1)S(1)}, u32[]{:S(2)}, u32[]{:S(2)}) %collective-permute-start.31) | collective-permute-done | bytes 131104 | tf_op jit(solution)/shard_map/ppermute | solution.py:559
  177.9 0.8 query_sum.1
  178.7 1.2 input_sum.1
  (53 shorter events, 3.8 us)
Async XLA Ops:
  0.6 9.8 %copy-start = (bf16[1024,512]{1,0:T(8,128)(2,1)S(1)}, bf16[1024,512]{1,0:T(8,128)(2,1)}, u32[]{:S(2)}) copy-start(bf16[1024,512]{1,0:T(8,128)(2,1)} %refs_3_.9) | copy-start | bytes 3145732
  0.6 9.8 %copy-start.1 = (bf16[1024,1024]{1,0:T(8,128)(2,1)S(1)}, bf16[1024,1024]{1,0:T(8,128)(2,1)}, u32[]{:S(2)}) copy-start(bf16[1024,1024]{1,0:T(8,128)(2,1)} %refs_2_.3) | copy-start | bytes 6291460
  0.7 9.8 %copy-start.4 = (s32[1024,1]{0,1:T(1,128)S(1)}, s32[1024,1]{0,1:T(1,128)}, u32[]{:S(2)}) copy-start(s32[1024,1]{0,1:T(1,128)} %param.9) | copy-start | bytes 12292
  6.2 43.9 %collective-permute-start = (bf16[1040,128]{1,0:T(8,128)(2,1)}, bf16[1040,128]{1,0:T(8,128)(2,1)S(1)}, u32[]{:S(2)}, u32[]{:S(2)}) collective-permute-start(bf16[1040,128]{1,0:T(8,128)(2,1)} %get-tuple-element.66), channel_id=1, source_target_pairs={{0,8},{8,0},{9,1},{4,12},{5,13},{12,4},{13,5},{1,9},{2,10},{10,2},... | collective-permute-start | bytes 798728 | tf_op jit(solution)/shard_map/ppermute | solution.py:553
  10.3 41.3 %collective-permute-start.1 = (bf16[1040,128]{1,0:T(8,128)(2,1)}, bf16[1040,128]{1,0:T(8,128)(2,1)}, u32[]{:S(2)}, u32[]{:S(2)}) collective-permute-start(bf16[1040,128]{1,0:T(8,128)(2,1)} %get-tuple-element.67), channel_id=1, source_target_pairs={{0,9},{8,1},{9,0},{4,13},{5,12},{12,5},{13,4},{1,8},{2,11},{10,3},... | collective-permute-start | bytes 798728 | tf_op jit(solution)/shard_map/ppermute | solution.py:553
  10.4 1.2 copy-start.2
  11.7 0.7 copy-start.5
  12.3 4.8 %copy-start.3 = (bf16[1024,512]{1,0:T(8,128)(2,1)S(1)}, bf16[1024,512]{1,0:T(8,128)(2,1)}, u32[]{:S(2)}) copy-start(bf16[1024,512]{1,0:T(8,128)(2,1)} %refs_4_.5) | copy-start | bytes 3145732
  22.0 27.0 %collective-permute-start.14 = (bf16[512,128]{1,0:T(8,128)(2,1)S(1)}, bf16[512,128]{1,0:T(8,128)(2,1)S(1)}, u32[]{:S(2)}, u32[]{:S(2)}) collective-permute-start(bf16[512,128]{1,0:T(8,128)(2,1)S(1)} %get-tuple-element.84), channel_id=1, source_target_pairs={{0,8},{8,0},{9,1},{4,12},{5,13},{12,4},{13,5},{1,9},{2,10},{10,2},... | collective-permute-start | bytes 393224 | tf_op jit(solution)/shard_map/ppermute | solution.py:553
  24.1 26.0 %collective-permute-start.15 = (bf16[512,128]{1,0:T(8,128)(2,1)S(1)}, bf16[512,128]{1,0:T(8,128)(2,1)S(1)}, u32[]{:S(2)}, u32[]{:S(2)}) collective-permute-start(bf16[512,128]{1,0:T(8,128)(2,1)S(1)} %get-tuple-element.85), channel_id=1, source_target_pairs={{0,9},{8,1},{9,0},{4,13},{5,12},{12,5},{13,4},{1,8},{2,11},{10,3},... | collective-permute-start | bytes 393224 | tf_op jit(solution)/shard_map/ppermute | solution.py:553
  24.8 28.6 %collective-permute-start.3 = (bf16[1040,128]{1,0:T(8,128)(2,1)S(1)}, bf16[1040,128]{1,0:T(8,128)(2,1)S(1)}, u32[]{:S(2)}, u32[]{:S(2)}) collective-permute-start(bf16[1040,128]{1,0:T(8,128)(2,1)S(1)} %get-tuple-element.68), channel_id=1, source_target_pairs={{0,5},{8,13},{9,12},{4,9},{5,8},{12,1},{13,0},{1,4},{2,7},{10,15},... | collective-permute-start | bytes 798728 | tf_op jit(solution)/shard_map/ppermute | solution.py:553
  49.0 14.3 %collective-permute-start.4 = (bf16[1040,128]{1,0:T(8,128)(2,1)S(1)}, bf16[1040,128]{1,0:T(8,128)(2,1)S(1)}, u32[]{:S(2)}, u32[]{:S(2)}) collective-permute-start(bf16[1040,128]{1,0:T(8,128)(2,1)S(1)} %get-tuple-element.69), channel_id=1, source_target_pairs={{0,12},{8,4},{9,5},{4,0},{5,1},{12,8},{13,9},{1,13},{2,14},{10,6},... | collective-permute-start | bytes 798728 | tf_op jit(solution)/shard_map/ppermute | solution.py:553
  50.2 21.9 %collective-permute-start.5 = (bf16[1040,128]{1,0:T(8,128)(2,1)S(1)}, bf16[1040,128]{1,0:T(8,128)(2,1)S(1)}, u32[]{:S(2)}, u32[]{:S(2)}) collective-permute-start(bf16[1040,128]{1,0:T(8,128)(2,1)S(1)} %get-tuple-element.70), channel_id=1, source_target_pairs={{0,13},{8,5},{9,4},{4,1},{5,0},{12,9},{13,8},{1,12},{2,15},{10,7},... | collective-permute-start | bytes 798728 | tf_op jit(solution)/shard_map/ppermute | solution.py:553
  50.2 21.9 %collective-permute-start.6 = (bf16[1040,128]{1,0:T(8,128)(2,1)S(1)}, bf16[1040,128]{1,0:T(8,128)(2,1)S(1)}, u32[]{:S(2)}, u32[]{:S(2)}) collective-permute-start(bf16[1040,128]{1,0:T(8,128)(2,1)S(1)} %get-tuple-element.71), channel_id=1, source_target_pairs={{0,1},{8,9},{9,8},{4,5},{5,4},{12,13},{13,12},{1,0},{2,3},{10,11},... | collective-permute-start | bytes 798728 | tf_op jit(solution)/shard_map/ppermute | solution.py:553
  51.7 21.7 %collective-permute-start.2 = (bf16[1040,128]{1,0:T(8,128)(2,1)S(1)}, bf16[1040,128]{1,0:T(8,128)(2,1)S(1)}, u32[]{:S(2)}, u32[]{:S(2)}) collective-permute-start(bf16[1040,128]{1,0:T(8,128)(2,1)S(1)} %get-tuple-element.62.refs_4_), channel_id=1, source_target_pairs={{0,4},{8,12},{9,13},{4,8},{5,9},{12,0},{13,1},{1,5},{2,6},{10,14},... | collective-permute-start | bytes 798728 | tf_op jit(solution)/shard_map/ppermute | solution.py:553
  53.4 35.0 %collective-permute-start.16 = (bf16[512,128]{1,0:T(8,128)(2,1)S(1)}, bf16[512,128]{1,0:T(8,128)(2,1)S(1)}, u32[]{:S(2)}, u32[]{:S(2)}) collective-permute-start(bf16[512,128]{1,0:T(8,128)(2,1)S(1)} %get-tuple-element.86), channel_id=1, source_target_pairs={{0,4},{8,12},{9,13},{4,8},{5,9},{12,0},{13,1},{1,5},{2,6},{10,14},... | collective-permute-start | bytes 393224 | tf_op jit(solution)/shard_map/ppermute | solution.py:553
  63.3 26.6 %collective-permute-start.17 = (bf16[512,128]{1,0:T(8,128)(2,1)S(1)}, bf16[512,128]{1,0:T(8,128)(2,1)S(1)}, u32[]{:S(2)}, u32[]{:S(2)}) collective-permute-start(bf16[512,128]{1,0:T(8,128)(2,1)S(1)} %get-tuple-element.87), channel_id=1, source_target_pairs={{0,5},{8,13},{9,12},{4,9},{5,8},{12,1},{13,0},{1,4},{2,7},{10,15},... | collective-permute-start | bytes 393224 | tf_op jit(solution)/shard_map/ppermute | solution.py:553
  72.1 18.6 %collective-permute-start.18 = (bf16[512,128]{1,0:T(8,128)(2,1)S(1)}, bf16[512,128]{1,0:T(8,128)(2,1)S(1)}, u32[]{:S(2)}, u32[]{:S(2)}) collective-permute-start(bf16[512,128]{1,0:T(8,128)(2,1)S(1)} %get-tuple-element.88), channel_id=1, source_target_pairs={{0,12},{8,4},{9,5},{4,0},{5,1},{12,8},{13,9},{1,13},{2,14},{10,6},... | collective-permute-start | bytes 393224 | tf_op jit(solution)/shard_map/ppermute | solution.py:553
  72.1 19.4 %collective-permute-start.19 = (bf16[512,128]{1,0:T(8,128)(2,1)S(1)}, bf16[512,128]{1,0:T(8,128)(2,1)S(1)}, u32[]{:S(2)}, u32[]{:S(2)}) collective-permute-start(bf16[512,128]{1,0:T(8,128)(2,1)S(1)} %get-tuple-element.89), channel_id=1, source_target_pairs={{0,13},{8,5},{9,4},{4,1},{5,0},{12,9},{13,8},{1,12},{2,15},{10,7},... | collective-permute-start | bytes 393224 | tf_op jit(solution)/shard_map/ppermute | solution.py:553
  73.4 19.5 %collective-permute-start.20 = (bf16[512,128]{1,0:T(8,128)(2,1)S(1)}, bf16[512,128]{1,0:T(8,128)(2,1)S(1)}, u32[]{:S(2)}, u32[]{:S(2)}) collective-permute-start(bf16[512,128]{1,0:T(8,128)(2,1)S(1)} %get-tuple-element.90), channel_id=1, source_target_pairs={{0,1},{8,9},{9,8},{4,5},{5,4},{12,13},{13,12},{1,0},{2,3},{10,11},... | collective-permute-start | bytes 393224 | tf_op jit(solution)/shard_map/ppermute | solution.py:553
  88.4 22.6 %collective-permute-start.7 = (bf16[512,128]{1,0:T(8,128)(2,1)S(1)}, bf16[512,128]{1,0:T(8,128)(2,1)S(1)}, u32[]{:S(2)}, u32[]{:S(2)}) collective-permute-start(bf16[512,128]{1,0:T(8,128)(2,1)S(1)} %get-tuple-element.73), channel_id=1, source_target_pairs={{0,8},{8,0},{9,1},{4,12},{5,13},{12,4},{13,5},{1,9},{2,10},{10,2},... | collective-permute-start | bytes 393224 | tf_op jit(solution)/shard_map/ppermute | solution.py:553
  89.9 21.6 %collective-permute-start.8 = (bf16[512,128]{1,0:T(8,128)(2,1)S(1)}, bf16[512,128]{1,0:T(8,128)(2,1)S(1)}, u32[]{:S(2)}, u32[]{:S(2)}) collective-permute-start(bf16[512,128]{1,0:T(8,128)(2,1)S(1)} %get-tuple-element.74), channel_id=1, source_target_pairs={{0,9},{8,1},{9,0},{4,13},{5,12},{12,5},{13,4},{1,8},{2,11},{10,3},... | collective-permute-start | bytes 393224 | tf_op jit(solution)/shard_map/ppermute | solution.py:553
  90.7 22.9 %collective-permute-start.9 = (bf16[512,128]{1,0:T(8,128)(2,1)S(1)}, bf16[512,128]{1,0:T(8,128)(2,1)S(1)}, u32[]{:S(2)}, u32[]{:S(2)}) collective-permute-start(bf16[512,128]{1,0:T(8,128)(2,1)S(1)} %get-tuple-element.75), channel_id=1, source_target_pairs={{0,4},{8,12},{9,13},{4,8},{5,9},{12,0},{13,1},{1,5},{2,6},{10,14},... | collective-permute-start | bytes 393224 | tf_op jit(solution)/shard_map/ppermute | solution.py:553
  91.5 23.3 %collective-permute-start.10 = (bf16[512,128]{1,0:T(8,128)(2,1)S(1)}, bf16[512,128]{1,0:T(8,128)(2,1)S(1)}, u32[]{:S(2)}, u32[]{:S(2)}) collective-permute-start(bf16[512,128]{1,0:T(8,128)(2,1)S(1)} %get-tuple-element.76), channel_id=1, source_target_pairs={{0,5},{8,13},{9,12},{4,9},{5,8},{12,1},{13,0},{1,4},{2,7},{10,15},... | collective-permute-start | bytes 393224 | tf_op jit(solution)/shard_map/ppermute | solution.py:553
  108.6 25.6 %collective-permute-start.21 = (bf16[544,128]{1,0:T(8,128)(2,1)S(1)}, bf16[544,128]{1,0:T(8,128)(2,1)S(1)}, u32[]{:S(2)}, u32[]{:S(2)}) collective-permute-start(bf16[544,128]{1,0:T(8,128)(2,1)S(1)} %get-tuple-element.92), channel_id=1, source_target_pairs={{0,8},{8,0},{9,1},{4,12},{5,13},{12,4},{13,5},{1,9},{2,10},{10,2},... | collective-permute-start | bytes 417800 | tf_op jit(solution)/shard_map/ppermute | solution.py:553
  111.0 23.9 %collective-permute-start.22 = (bf16[544,128]{1,0:T(8,128)(2,1)S(1)}, bf16[544,128]{1,0:T(8,128)(2,1)S(1)}, u32[]{:S(2)}, u32[]{:S(2)}) collective-permute-start(bf16[544,128]{1,0:T(8,128)(2,1)S(1)} %get-tuple-element.93), channel_id=1, source_target_pairs={{0,9},{8,1},{9,0},{4,13},{5,12},{12,5},{13,4},{1,8},{2,11},{10,3},... | collective-permute-start | bytes 417800 | tf_op jit(solution)/shard_map/ppermute | solution.py:553
  111.5 9.4 %collective-permute-start.11 = (bf16[512,128]{1,0:T(8,128)(2,1)S(1)}, bf16[512,128]{1,0:T(8,128)(2,1)S(1)}, u32[]{:S(2)}, u32[]{:S(2)}) collective-permute-start(bf16[512,128]{1,0:T(8,128)(2,1)S(1)} %get-tuple-element.77), channel_id=1, source_target_pairs={{0,12},{8,4},{9,5},{4,0},{5,1},{12,8},{13,9},{1,13},{2,14},{10,6},... | collective-permute-start | bytes 393224 | tf_op jit(solution)/shard_map/ppermute | solution.py:553
  113.6 17.5 %collective-permute-start.12 = (bf16[512,128]{1,0:T(8,128)(2,1)S(1)}, bf16[512,128]{1,0:T(8,128)(2,1)S(1)}, u32[]{:S(2)}, u32[]{:S(2)}) collective-permute-start(bf16[512,128]{1,0:T(8,128)(2,1)S(1)} %get-tuple-element.78), channel_id=1, source_target_pairs={{0,13},{8,5},{9,4},{4,1},{5,0},{12,9},{13,8},{1,12},{2,15},{10,7},... | collective-permute-start | bytes 393224 | tf_op jit(solution)/shard_map/ppermute | solution.py:553
  114.9 18.7 %collective-permute-start.13 = (bf16[512,128]{1,0:T(8,128)(2,1)S(1)}, bf16[512,128]{1,0:T(8,128)(2,1)S(1)}, u32[]{:S(2)}, u32[]{:S(2)}) collective-permute-start(bf16[512,128]{1,0:T(8,128)(2,1)S(1)} %get-tuple-element.79), channel_id=1, source_target_pairs={{0,1},{8,9},{9,8},{4,5},{5,4},{12,13},{13,12},{1,0},{2,3},{10,11},... | collective-permute-start | bytes 393224 | tf_op jit(solution)/shard_map/ppermute | solution.py:553
  120.9 17.9 %collective-permute-start.23 = (bf16[544,128]{1,0:T(8,128)(2,1)S(1)}, bf16[544,128]{1,0:T(8,128)(2,1)S(1)}, u32[]{:S(2)}, u32[]{:S(2)}) collective-permute-start(bf16[544,128]{1,0:T(8,128)(2,1)S(1)} %get-tuple-element.94), channel_id=1, source_target_pairs={{0,4},{8,12},{9,13},{4,8},{5,9},{12,0},{13,1},{1,5},{2,6},{10,14},... | collective-permute-start | bytes 417800 | tf_op jit(solution)/shard_map/ppermute | solution.py:553
  131.1 7.9 %collective-permute-start.24 = (bf16[544,128]{1,0:T(8,128)(2,1)S(1)}, bf16[544,128]{1,0:T(8,128)(2,1)S(1)}, u32[]{:S(2)}, u32[]{:S(2)}) collective-permute-start(bf16[544,128]{1,0:T(8,128)(2,1)S(1)} %get-tuple-element.95), channel_id=1, source_target_pairs={{0,5},{8,13},{9,12},{4,9},{5,8},{12,1},{13,0},{1,4},{2,7},{10,15},... | collective-permute-start | bytes 417800 | tf_op jit(solution)/shard_map/ppermute | solution.py:553
  133.5 8.3 %collective-permute-start.25 = (bf16[544,128]{1,0:T(8,128)(2,1)S(1)}, bf16[544,128]{1,0:T(8,128)(2,1)S(1)}, u32[]{:S(2)}, u32[]{:S(2)}) collective-permute-start(bf16[544,128]{1,0:T(8,128)(2,1)S(1)} %get-tuple-element.96), channel_id=1, source_target_pairs={{0,12},{8,4},{9,5},{4,0},{5,1},{12,8},{13,9},{1,13},{2,14},{10,6},... | collective-permute-start | bytes 417800 | tf_op jit(solution)/shard_map/ppermute | solution.py:553
  134.3 10.5 %collective-permute-start.26 = (bf16[544,128]{1,0:T(8,128)(2,1)S(1)}, bf16[544,128]{1,0:T(8,128)(2,1)S(1)}, u32[]{:S(2)}, u32[]{:S(2)}) collective-permute-start(bf16[544,128]{1,0:T(8,128)(2,1)S(1)} %get-tuple-element.97), channel_id=1, source_target_pairs={{0,13},{8,5},{9,4},{4,1},{5,0},{12,9},{13,8},{1,12},{2,15},{10,7},... | collective-permute-start | bytes 417800 | tf_op jit(solution)/shard_map/ppermute | solution.py:553
  134.9 9.9 %collective-permute-start.27 = (bf16[544,128]{1,0:T(8,128)(2,1)S(1)}, bf16[544,128]{1,0:T(8,128)(2,1)S(1)}, u32[]{:S(2)}, u32[]{:S(2)}) collective-permute-start(bf16[544,128]{1,0:T(8,128)(2,1)S(1)} %get-tuple-element.98), channel_id=1, source_target_pairs={{0,1},{8,9},{9,8},{4,5},{5,4},{12,13},{13,12},{1,0},{2,3},{10,11},... | collective-permute-start | bytes 417800 | tf_op jit(solution)/shard_map/ppermute | solution.py:553
  148.7 29.9 %collective-permute-start.29 = (bf16[1024,512]{1,0:T(8,128)(2,1)S(1)}, bf16[1024,512]{1,0:T(8,128)(2,1)S(1)}, u32[]{:S(2)}, u32[]{:S(2)}) collective-permute-start(bf16[1024,512]{1,0:T(8,128)(2,1)S(1)} %get-tuple-element.103), channel_id=1, source_target_pairs={{0,2},{2,0},{1,3},{3,1},{4,6},{6,4},{5,7},{7,5},{8,10},{10,8},{9,1... | collective-permute-start | bytes 3145736 | tf_op jit(solution)/shard_map/ppermute | solution.py:559
  150.3 2.6 %collective-permute-start.33 = (bf16[4,128,512]{2,1,0:T(8,128)(2,1)S(1)}, bf16[4,128,512]{2,1,0:T(8,128)(2,1)S(1)}, u32[]{:S(2)}, u32[]{:S(2)}) collective-permute-start(bf16[4,128,512]{2,1,0:T(8,128)(2,1)S(1)} %get-tuple-element.108), channel_id=1, source_target_pairs={{0,1},{1,0},{2,3},{3,2},{4,5},{5,4},{6,7},{7,6},{8,9},{9,8},{10,11... | collective-permute-start | bytes 1572872 | tf_op jit(solution)/shard_map/ppermute | solution.py:559
  152.4 5.1 %collective-permute-start.28 = (bf16[4,128,512]{2,1,0:T(8,128)(2,1)S(1)}, bf16[4,128,512]{2,1,0:T(8,128)(2,1)S(1)}, u32[]{:S(2)}, u32[]{:S(2)}) collective-permute-start(bf16[4,128,512]{2,1,0:T(8,128)(2,1)S(1)} %get-tuple-element.101), channel_id=1, source_target_pairs={{0,1},{1,0},{2,3},{3,2},{4,5},{5,4},{6,7},{7,6},{8,9},{9,8},{10,11... | collective-permute-start | bytes 1572872 | tf_op jit(solution)/shard_map/ppermute | solution.py:559
  153.6 8.3 %collective-permute-start.34 = (bf16[128,512]{1,0:T(8,128)(2,1)S(1)}, bf16[128,512]{1,0:T(8,128)(2,1)S(1)}, u32[]{:S(2)}, u32[]{:S(2)}) collective-permute-start(bf16[128,512]{1,0:T(8,128)(2,1)S(1)} %get-tuple-element.114), channel_id=1, source_target_pairs={{0,4},{4,8},{8,12},{12,0},{1,5},{5,9},{9,13},{13,1},{2,6},{6,10},{... | collective-permute-start | bytes 393224 | tf_op jit(solution)/shard_map/ppermute | solution.py:559
  154.2 13.4 %collective-permute-start.35 = (bf16[128,512]{1,0:T(8,128)(2,1)S(1)}, bf16[128,512]{1,0:T(8,128)(2,1)S(1)}, u32[]{:S(2)}, u32[]{:S(2)}) collective-permute-start(bf16[128,512]{1,0:T(8,128)(2,1)S(1)} %get-tuple-element.115), channel_id=1, source_target_pairs={{0,8},{4,12},{8,0},{12,4},{1,9},{5,13},{9,1},{13,5},{2,10},{6,14},... | collective-permute-start | bytes 393224 | tf_op jit(solution)/shard_map/ppermute | solution.py:559
  156.8 18.1 %collective-permute-start.36 = (bf16[128,512]{1,0:T(8,128)(2,1)S(1)}, bf16[128,512]{1,0:T(8,128)(2,1)S(1)}, u32[]{:S(2)}, u32[]{:S(2)}) collective-permute-start(bf16[128,512]{1,0:T(8,128)(2,1)S(1)} %get-tuple-element.116), channel_id=1, source_target_pairs={{0,12},{4,0},{8,4},{12,8},{1,13},{5,1},{9,5},{13,9},{2,14},{6,2},{... | collective-permute-start | bytes 393224 | tf_op jit(solution)/shard_map/ppermute | solution.py:559
  158.2 17.4 %collective-permute-start.30 = (bf16[128,512]{1,0:T(8,128)(2,1)S(1)}, bf16[128,512]{1,0:T(8,128)(2,1)S(1)}, u32[]{:S(2)}, u32[]{:S(2)}) collective-permute-start(bf16[128,512]{1,0:T(8,128)(2,1)S(1)} %get-tuple-element.104), channel_id=1, source_target_pairs={{0,4},{4,8},{8,12},{12,0},{1,5},{5,9},{9,13},{13,1},{2,6},{6,10},{... | collective-permute-start | bytes 393224 | tf_op jit(solution)/shard_map/ppermute | solution.py:559
  162.0 15.9 %collective-permute-start.31 = (bf16[128,512]{1,0:T(8,128)(2,1)S(1)}, bf16[128,512]{1,0:T(8,128)(2,1)S(1)}, u32[]{:S(2)}, u32[]{:S(2)}) collective-permute-start(bf16[128,512]{1,0:T(8,128)(2,1)S(1)} %get-tuple-element.105), channel_id=1, source_target_pairs={{0,8},{4,12},{8,0},{12,4},{1,9},{5,13},{9,1},{13,5},{2,10},{6,14},... | collective-permute-start | bytes 393224 | tf_op jit(solution)/shard_map/ppermute | solution.py:559
  167.6 10.3 %collective-permute-start.32 = (bf16[128,512]{1,0:T(8,128)(2,1)S(1)}, bf16[128,512]{1,0:T(8,128)(2,1)S(1)}, u32[]{:S(2)}, u32[]{:S(2)}) collective-permute-start(bf16[128,512]{1,0:T(8,128)(2,1)S(1)} %get-tuple-element.106), channel_id=1, source_target_pairs={{0,12},{4,0},{8,4},{12,8},{1,13},{5,1},{9,5},{13,9},{2,14},{6,2},{... | collective-permute-start | bytes 393224 | tf_op jit(solution)/shard_map/ppermute | solution.py:559

commit v11 on v10

--- a/solution.py
+++ b/solution.py
@@ -639,6 +639,8 @@
         flops=2 * toks * width * width_dev + 2 * slots * toks * width_dev,
         name="project_value",
     )
+    behind = [got_mixed[min(k + 2, owners - 1)] for k in range(owners)]
+    send_value = [lax.optimization_barrier(pair)[0] for pair in zip(send_value, behind)]
     got_value = exchange(send_value, sizes)
     blocks = per_group * capacity // BLOCK_ROWS
     held = blocks + (LEAD + 4) * UNROLL
@@ -654,6 +656,7 @@
         + several(1, held * BLOCK_ROWS, LANES)
         + (shape((owners, LANES), jnp.int32),),
         (me, *got_mixed),
+        after=[unsort],
         scratch=[pltpu.SMEM((owners, LANES), jnp.int32), place, tall, dense_rows, tall]
         + [group_f32] * 2
         + [group_b16] * 2,

time: 181 us -> 173 us (0.956)
  waiting for transfers between devices: 53.4 us -> 30.5 us
  starting transfers between devices: 63.2 us -> 78.6 us
    ppermute x28, waiting for transfers between devices: 43 us -> 20.2 us  [exchange(): out.append(part if ahead == (0, 0) else lax.ppermute(part, OWNERS, moves))]
    ppermute x28, starting transfers between devices: 50.6 us -> 66.1 us  [exchange(): out.append(part if ahead == (0, 0) else lax.ppermute(part, OWNERS, moves))]
  transfers between devices with their start and end apart: 37 -> 37, of which waited for: 10 -> 9; matrix products, arithmetic and copies ran while one was open for 0% -> 0% of each run, Pallas kernels for 28% -> 29%
where the time goes in v11:
time: 173 us
  starting transfers between devices  78.6 us (45%)
  Pallas kernels  61.2 us (35%)
  waiting for transfers between devices  30.5 us (18%)
  local copies, waits for them, and re-layouts  1.93 us (1%)
    ppermute x28, starting transfers between devices, exchange(): out.append(part if ahead == (0, 0) else lax.ppermute(part, OWNERS, moves))  66.1 us
    pallas_call x14, Pallas kernels, call(): pl.pallas_call(body, out_shape=outs, in_specs=specs, out_specs=jax.tree.m...  61.2 us
    ppermute x28, waiting for transfers between devices, exchange(): out.append(part if ahead == (0, 0) else lax.ppermute(part, OWNERS, moves))  20.2 us
    ppermute x9, starting transfers between devices, shift(): lax.ppermute(part, axis, [(i, (i + ahead) % size) for i in range(size)])  12.5 us
    ppermute x9, waiting for transfers between devices, shift(): lax.ppermute(part, axis, [(i, (i + ahead) % size) for i in range(size)])  10.4 us
  transfers between devices with their start and end apart: 37, of which 9 were waited for; matrix products, arithmetic and copies ran while one was open for 0% of the time, Pallas kernels for 29%

profile of v11, /device:TPU:0, one launch (start us, length us, event | category | flops | bytes accessed | tf_op | source)
XLA Modules:
  0.0 173.3 jit_solution(14197989067929890493)
XLA Ops:
  0.7 5.6 %project_far.1 = (bf16[1040,128]{1,0:T(8,128)(2,1)}, bf16[1040,128]{1,0:T(8,128)(2,1)}, s32[1,1024]{1,0:T(1,128)}) custom-call(s32[1,1024]{1,0:T(1,128)} %bitcast.5, bf16[1024,1024]{1,0:T(8,128)(2,1)} %refs_2_.3, bf16[1024,512]{1,0:T(8,128)(2,1)} %refs_3_.9, bf16[1024,512]{1,0:T(8,128)(2,1)} %refs_5_.1), custom_call_target="tpu_custom_call" | custom-call | flops 805306368 | bytes 4734976 | tf_op jit(solution)/shard_map/project_far/pallas_call | solution.py:531
  6.2 3.5 %collective-permute-start.1 = (bf16[1040,128]{1,0:T(8,128)(2,1)}, bf16[1040,128]{1,0:T(8,128)(2,1)S(1)}, u32[]{:S(2)}, u32[]{:S(2)}) collective-permute-start(bf16[1040,128]{1,0:T(8,128)(2,1)} %get-tuple-element.75), channel_id=1, source_target_pairs={{0,9},{8,1},{9,0},{4,13},{5,12},{12,5},{13,4},{1,8},{2,11},{10,3},... | collective-permute-start | bytes 798728 | tf_op jit(solution)/shard_map/ppermute | solution.py:553
  9.9 1.2 copy-done.2
  11.1 0.7 copy-done.5
  11.8 4.8 %project_query.1 = (bf16[1040,128]{1,0:T(8,128)(2,1)S(1)}, bf16[1040,128]{1,0:T(8,128)(2,1)S(1)}, bf16[1040,128]{1,0:T(8,128)(2,1)S(1)}, bf16[1040,128]{1,0:T(8,...) custom-call(s32[4]{0:T(128)S(1)} %pad_add_fusion.refs_0_, s32[1,1024]{1,0:T(1,128)S(1)} %copy-done.5, ...), custom_call_target="tpu_custom_call" | custom-call | flops 3221225472 | bytes 5799952 | tf_op jit(solution)/shard_map/project_query/pallas_call | solution.py:531
  16.6 0.7 collective-permute-start.6
  17.4 1.2 collective-permute-start.3
  19.0 2.4 %collective-permute-start = (bf16[1040,128]{1,0:T(8,128)(2,1)S(1)}, bf16[1040,128]{1,0:T(8,128)(2,1)S(1)}, u32[]{:S(2)}, u32[]{:S(2)}) collective-permute-start(bf16[1040,128]{1,0:T(8,128)(2,1)S(1)} %copy-done.8), channel_id=1, source_target_pairs={{0,8},{8,0},{9,1},{4,12},{5,13},{12,4},{13,5},{1,9},{2,10},{10,2},... | collective-permute-start | bytes 798728 | tf_op jit(solution)/shard_map/ppermute | solution.py:553
  21.8 5.0 %collective-permute-start.4 = (bf16[1040,128]{1,0:T(8,128)(2,1)S(1)}, bf16[1040,128]{1,0:T(8,128)(2,1)S(1)}, u32[]{:S(2)}, u32[]{:S(2)}) collective-permute-start(bf16[1040,128]{1,0:T(8,128)(2,1)S(1)} %get-tuple-element.77), channel_id=1, source_target_pairs={{0,12},{8,4},{9,5},{4,0},{5,1},{12,8},{13,9},{1,13},{2,14},{10,6},... | collective-permute-start | bytes 798728 | tf_op jit(solution)/shard_map/ppermute | solution.py:553
  26.9 4.8 %project_value.1 = (bf16[512,128]{1,0:T(8,128)(2,1)S(1)}, bf16[512,128]{1,0:T(8,128)(2,1)S(1)}, bf16[512,128]{1,0:T(8,128)(2,1)S(1)}, bf16[512,128]{1,0:T(8,128)...) custom-call(s32[4]{0:T(128)S(1)} %pad_add_fusion.refs_0_, ...), custom_call_target="tpu_custom_call" | custom-call | flops 2147483648 | bytes 8392720 | tf_op jit(solution)/shard_map/project_value/pallas_call | solution.py:531
  31.7 14.4 %collective-permute-start.20 = (bf16[512,128]{1,0:T(8,128)(2,1)S(1)}, bf16[512,128]{1,0:T(8,128)(2,1)S(1)}, u32[]{:S(2)}, u32[]{:S(2)}) collective-permute-start(bf16[512,128]{1,0:T(8,128)(2,1)S(1)} %get-tuple-element.106), channel_id=1, source_target_pairs={{0,1},{8,9},{9,8},{4,5},{5,4},{12,13},{13,12},{1,0},{2,3},{10,11},... | collective-permute-start | bytes 393224 | tf_op jit(solution)/shard_map/ppermute | solution.py:553
  46.2 7.9 %collective-permute-done.5.refs_7_ = bf16[1040,128]{1,0:T(8,128)(2,1)S(1)} collective-permute-done((bf16[1040,128]{1,0:T(8,128)(2,1)S(1)}, bf16[1040,128]{1,0:T(8,128)(2,1)S(1)}, u32[]{:S(2)}, u32[]{:S(2)}) %collective-permute-start.5) | collective-permute-done | bytes 266272 | tf_op jit(solution)/shard_map/ppermute | solution.py:553
  54.1 4.3 %collective-permute-start.18 = (bf16[512,128]{1,0:T(8,128)(2,1)S(1)}, bf16[512,128]{1,0:T(8,128)(2,1)S(1)}, u32[]{:S(2)}, u32[]{:S(2)}) collective-permute-start(bf16[512,128]{1,0:T(8,128)(2,1)S(1)} %get-tuple-element.102), channel_id=1, source_target_pairs={{0,12},{8,4},{9,5},{4,0},{5,1},{12,8},{13,9},{1,13},{2,14},{10,6},... | collective-permute-start | bytes 393224 | tf_op jit(solution)/shard_map/ppermute | solution.py:553
  58.4 5.0 %collective-permute-start.16 = (bf16[512,128]{1,0:T(8,128)(2,1)S(1)}, bf16[512,128]{1,0:T(8,128)(2,1)S(1)}, u32[]{:S(2)}, u32[]{:S(2)}) collective-permute-start(bf16[512,128]{1,0:T(8,128)(2,1)S(1)} %get-tuple-element.98), channel_id=1, source_target_pairs={{0,4},{8,12},{9,13},{4,8},{5,9},{12,0},{13,1},{1,5},{2,6},{10,14},... | collective-permute-start | bytes 393224 | tf_op jit(solution)/shard_map/ppermute | solution.py:553
  63.4 3.2 %collective-permute-start.15 = (bf16[512,128]{1,0:T(8,128)(2,1)S(1)}, bf16[512,128]{1,0:T(8,128)(2,1)S(1)}, u32[]{:S(2)}, u32[]{:S(2)}) collective-permute-start(bf16[512,128]{1,0:T(8,128)(2,1)S(1)} %get-tuple-element.96), channel_id=1, source_target_pairs={{0,9},{8,1},{9,0},{4,13},{5,12},{12,5},{13,4},{1,8},{2,11},{10,3},... | collective-permute-start | bytes 393224 | tf_op jit(solution)/shard_map/ppermute | solution.py:553
  66.7 0.7 collective-permute-start.14
  67.4 13.5 %value_grad.1 = (bf16[512,128]{1,0:T(8,128)(2,1)S(1)}, bf16[512,128]{1,0:T(8,128)(2,1)S(1)}, bf16[512,128]{1,0:T(8,128)(2,1)S(1)}, bf16[512,128]{1,0:T(8,128)(2,...) custom-call(s32[4]{0:T(128)S(1)} %pad_add_fusion.refs_0_, ...), custom_call_target="tpu_custom_call" | custom-call | flops 2147483648 | bytes 8163344 | tf_op jit(solution)/shard_map/value_grad/pallas_call | solution.py:531
  80.8 2.2 %collective-permute-start.7 = (bf16[512,128]{1,0:T(8,128)(2,1)S(1)}, bf16[512,128]{1,0:T(8,128)(2,1)S(1)}, u32[]{:S(2)}, u32[]{:S(2)}) collective-permute-start(bf16[512,128]{1,0:T(8,128)(2,1)S(1)} %get-tuple-element.81), channel_id=1, source_target_pairs={{0,8},{8,0},{9,1},{4,12},{5,13},{12,4},{13,5},{1,9},{2,10},{10,2},... | collective-permute-start | bytes 393224 | tf_op jit(solution)/shard_map/ppermute | solution.py:553
  83.4 2.6 %collective-permute-start.10 = (bf16[512,128]{1,0:T(8,128)(2,1)S(1)}, bf16[512,128]{1,0:T(8,128)(2,1)S(1)}, u32[]{:S(2)}, u32[]{:S(2)}) collective-permute-start(bf16[512,128]{1,0:T(8,128)(2,1)S(1)} %get-tuple-element.84), channel_id=1, source_target_pairs={{0,5},{8,13},{9,12},{4,9},{5,8},{12,1},{13,0},{1,4},{2,7},{10,15},... | collective-permute-start | bytes 393224 | tf_op jit(solution)/shard_map/ppermute | solution.py:553
  86.0 16.6 %query_grad.1 = (bf16[544,128]{1,0:T(8,128)(2,1)S(1)}, bf16[544,128]{1,0:T(8,128)(2,1)S(1)}, bf16[544,128]{1,0:T(8,128)(2,1)S(1)}, bf16[544,128]{1,0:T(8,128)(2,...) custom-call(s32[4]{0:T(128)S(1)} %pad_add_fusion.refs_0_, ...), custom_call_target="tpu_custom_call" | custom-call | flops 3221225472 | bytes 7147536 | tf_op jit(solution)/shard_map/query_grad/pallas_call | solution.py:531
  102.6 1.7 collective-permute-start.21
  104.3 1.1 collective-permute-start.22
  105.4 1.0 collective-permute-start.11
  106.4 1.7 %collective-permute-start.12 = (bf16[512,128]{1,0:T(8,128)(2,1)S(1)}, bf16[512,128]{1,0:T(8,128)(2,1)S(1)}, u32[]{:S(2)}, u32[]{:S(2)}) collective-permute-start(bf16[512,128]{1,0:T(8,128)(2,1)S(1)} %get-tuple-element.86), channel_id=1, source_target_pairs={{0,13},{8,5},{9,4},{4,1},{5,0},{12,9},{13,8},{1,12},{2,15},{10,7},... | collective-permute-start | bytes 393224 | tf_op jit(solution)/shard_map/ppermute | solution.py:553
  108.3 5.9 %collective-permute-done.11.refs_8_ = bf16[512,128]{1,0:T(8,128)(2,1)S(1)} collective-permute-done((bf16[512,128]{1,0:T(8,128)(2,1)S(1)}, bf16[512,128]{1,0:T(8,128)(2,1)S(1)}, u32[]{:S(2)}, u32[]{:S(2)}) %collective-permute-start.11) | collective-permute-done | bytes 131104 | tf_op jit(solution)/shard_map/ppermute | solution.py:553
  114.2 10.4 %collective-permute-start.23 = (bf16[544,128]{1,0:T(8,128)(2,1)S(1)}, bf16[544,128]{1,0:T(8,128)(2,1)S(1)}, u32[]{:S(2)}, u32[]{:S(2)}) collective-permute-start(bf16[544,128]{1,0:T(8,128)(2,1)S(1)} %get-tuple-element.110), channel_id=1, source_target_pairs={{0,4},{8,12},{9,13},{4,8},{5,9},{12,0},{13,1},{1,5},{2,6},{10,14},... | collective-permute-start | bytes 417800 | tf_op jit(solution)/shard_map/ppermute | solution.py:553
  124.5 2.4 %collective-permute-start.24 = (bf16[544,128]{1,0:T(8,128)(2,1)S(1)}, bf16[544,128]{1,0:T(8,128)(2,1)S(1)}, u32[]{:S(2)}, u32[]{:S(2)}) collective-permute-start(bf16[544,128]{1,0:T(8,128)(2,1)S(1)} %get-tuple-element.111), channel_id=1, source_target_pairs={{0,5},{8,13},{9,12},{4,9},{5,8},{12,1},{13,0},{1,4},{2,7},{10,15},... | collective-permute-start | bytes 417800 | tf_op jit(solution)/shard_map/ppermute | solution.py:553
  127.0 0.7 collective-permute-start.25
  127.7 0.6 collective-permute-start.26
  128.3 3.9 %value_home.1 = (bf16[1024,512]{1,0:T(8,128)(2,1)S(1)}, bf16[4,128,512]{2,1,0:T(8,128)(2,1)S(1)}, bf16[4,128,512]{2,1,0:T(8,128)(2,1)S(1)}) custom-call(s32[4]{0:T(128)S(1)} %pad_add_fusion.refs_0_, bf16[1024,1024]{1,0:T(8,128)(2,1)S(1)} %get-tuple-element.72.refs_1_, bf16[1024,1024]{1,0:T(8,128)(2,1)S(1)} %copy-done.7, ...), custom_call_target="tpu_custom_call" | custom-call | flops 2147483648 | bytes 7340048 | tf_op jit(solution)/shard_map/value_home/pallas_call | solution.py:531
  132.4 2.9 %collective-permute-done.25.refs_10_ = bf16[544,128]{1,0:T(8,128)(2,1)S(1)} collective-permute-done((bf16[544,128]{1,0:T(8,128)(2,1)S(1)}, bf16[544,128]{1,0:T(8,128)(2,1)S(1)}, u32[]{:S(2)}, u32[]{:S(2)}) %collective-permute-start.25) | collective-permute-done | bytes 139296 | tf_op jit(solution)/shard_map/ppermute | solution.py:553
  135.3 2.9 %collective-permute-done.26.refs_11_ = bf16[544,128]{1,0:T(8,128)(2,1)S(1)} collective-permute-done((bf16[544,128]{1,0:T(8,128)(2,1)S(1)}, bf16[544,128]{1,0:T(8,128)(2,1)S(1)}, u32[]{:S(2)}, u32[]{:S(2)}) %collective-permute-start.26) | collective-permute-done | bytes 139296 | tf_op jit(solution)/shard_map/ppermute | solution.py:553
  138.2 4.0 %query_home.1 = (bf16[1024,512]{1,0:T(8,128)(2,1)S(1)}, bf16[1024,512]{1,0:T(8,128)(2,1)S(1)}, f32[64,512]{1,0:T(8,128)}) custom-call(s32[4]{0:T(128)S(1)} %pad_add_fusion.refs_0_, bf16[1024,1024]{1,0:T(8,128)(2,1)S(1)} %copy-done.7, bf16[1024,512]{1,0:T(8,128)(2,1)S(1)} %get-tuple-element.88.refs_2_, bf16[1024,512]{1,0:T(8,128)(2,1)S(1)} %copy-done, ...), custom_call_target="tpu_custom_call" | custom-call | flops 2147483648 | bytes 8585232 | tf_op jit(solution)/shard_map/query_home/pallas_call | solution.py:531
  142.2 1.6 collective-permute-start.29
  143.7 2.0 %query_weight.1 = (bf16[4,128,512]{2,1,0:T(8,128)(2,1)S(1)}, bf16[4,128,512]{2,1,0:T(8,128)(2,1)S(1)}) custom-call(s32[4]{0:T(128)S(1)} %pad_add_fusion.refs_0_, bf16[1024,1024]{1,0:T(8,128)(2,1)S(1)} %get-tuple-element.72.refs_1_, bf16[1024,512]{1,0:T(8,128)(2,1)S(1)} %get-tuple-element.115.refs_2_.refs_1_), custom_call_target="tpu_custom_call" | custom-call | flops 1073741824 | bytes 4194320 | tf_op jit(solution)/shard_map/query_weight/pallas_call | solution.py:531
  146.3 0.7 value_subs.1
  147.6 2.6 %collective-permute-start.35 = (bf16[128,512]{1,0:T(8,128)(2,1)S(1)}, bf16[128,512]{1,0:T(8,128)(2,1)S(1)}, u32[]{:S(2)}, u32[]{:S(2)}) collective-permute-start(bf16[128,512]{1,0:T(8,128)(2,1)S(1)} %get-tuple-element.131), channel_id=1, source_target_pairs={{0,8},{4,12},{8,0},{12,4},{1,9},{5,13},{9,1},{13,5},{2,10},{6,14},... | collective-permute-start | bytes 393224 | tf_op jit(solution)/shard_map/ppermute | solution.py:559
  150.1 0.8 collective-permute-start.36
  150.9 0.7 query_subs.1
  151.6 1.3 collective-permute-start.30
  152.9 2.4 %collective-permute-done.34.refs_1_ = bf16[128,512]{1,0:T(8,128)(2,1)S(1)} collective-permute-done((bf16[128,512]{1,0:T(8,128)(2,1)S(1)}, bf16[128,512]{1,0:T(8,128)(2,1)S(1)}, u32[]{:S(2)}, u32[]{:S(2)}) %collective-permute-start.34) | collective-permute-done | bytes 131104 | tf_op jit(solution)/shard_map/ppermute | solution.py:559
  155.3 5.6 %collective-permute-done.35.refs_2_ = bf16[128,512]{1,0:T(8,128)(2,1)S(1)} collective-permute-done((bf16[128,512]{1,0:T(8,128)(2,1)S(1)}, bf16[128,512]{1,0:T(8,128)(2,1)S(1)}, u32[]{:S(2)}, u32[]{:S(2)}) %collective-permute-start.35) | collective-permute-done | bytes 131104 | tf_op jit(solution)/shard_map/ppermute | solution.py:559
  161.0 5.2 %collective-permute-start.32 = (bf16[128,512]{1,0:T(8,128)(2,1)S(1)}, bf16[128,512]{1,0:T(8,128)(2,1)S(1)}, u32[]{:S(2)}, u32[]{:S(2)}) collective-permute-start(bf16[128,512]{1,0:T(8,128)(2,1)S(1)} %get-tuple-element.122), channel_id=1, source_target_pairs={{0,12},{4,0},{8,4},{12,8},{1,13},{5,1},{9,5},{13,9},{2,14},{6,2},{... | collective-permute-start | bytes 393224 | tf_op jit(solution)/shard_map/ppermute | solution.py:559
  166.2 0.8 value_sum.1
  166.9 2.0 %input_own.1.refs_0_ = bf16[1024,512]{1,0:T(8,128)(2,1)S(1)} custom-call(s32[4]{0:T(128)S(1)} %pad_add_fusion.refs_0_, bf16[1024,512]{1,0:T(8,128)(2,1)S(1)} %get-tuple-element.115.refs_2_.refs_1_, bf16[1024,512]{1,0:T(8,128)(2,1)S(1)} %get-tuple-element.88.refs_2_, bf16[1024,512]{1,0:T(8,128)(2,1)S(1)} %copy-done, bf16[1024,512]{1,0:T(8,128)(2,1)S(1)} %copy-done.3, ...), custom_call_target="tpu_custom_call" | custom-call | flops 1073741824 | bytes 5242896 | tf_op jit(solution)/shard_map/input_own/pallas_call | solution.py:531
  169.0 2.3 %collective-permute-done.31.refs_2_ = bf16[128,512]{1,0:T(8,128)(2,1)S(1)} collective-permute-done((bf16[128,512]{1,0:T(8,128)(2,1)S(1)}, bf16[128,512]{1,0:T(8,128)(2,1)S(1)}, u32[]{:S(2)}, u32[]{:S(2)}) %collective-permute-start.31) | collective-permute-done | bytes 131104 | tf_op jit(solution)/shard_map/ppermute | solution.py:559
  171.3 0.8 query_sum.1
  172.0 1.2 input_sum.1
  (59 shorter events, 2.7 us)
Async XLA Ops:
  0.6 9.2 %copy-start = (bf16[1024,512]{1,0:T(8,128)(2,1)S(1)}, bf16[1024,512]{1,0:T(8,128)(2,1)}, u32[]{:S(2)}) copy-start(bf16[1024,512]{1,0:T(8,128)(2,1)} %refs_3_.9) | copy-start | bytes 3145732
  0.6 9.2 %copy-start.1 = (bf16[1024,1024]{1,0:T(8,128)(2,1)S(1)}, bf16[1024,1024]{1,0:T(8,128)(2,1)}, u32[]{:S(2)}) copy-start(bf16[1024,1024]{1,0:T(8,128)(2,1)} %refs_2_.3) | copy-start | bytes 6291460
  0.7 9.2 %copy-start.4 = (s32[1024,1]{0,1:T(1,128)S(1)}, s32[1024,1]{0,1:T(1,128)}, u32[]{:S(2)}) copy-start(s32[1024,1]{0,1:T(1,128)} %param.9) | copy-start | bytes 12292
  6.2 15.6 %collective-permute-start.1 = (bf16[1040,128]{1,0:T(8,128)(2,1)}, bf16[1040,128]{1,0:T(8,128)(2,1)S(1)}, u32[]{:S(2)}, u32[]{:S(2)}) collective-permute-start(bf16[1040,128]{1,0:T(8,128)(2,1)} %get-tuple-element.75), channel_id=1, source_target_pairs={{0,9},{8,1},{9,0},{4,13},{5,12},{12,5},{13,4},{1,8},{2,11},{10,3},... | collective-permute-start | bytes 798728 | tf_op jit(solution)/shard_map/ppermute | solution.py:553
  9.9 1.2 copy-start.2
  11.1 0.7 copy-start.5
  11.8 7.2 %copy-start.8 = (bf16[1040,128]{1,0:T(8,128)(2,1)S(1)}, bf16[1040,128]{1,0:T(8,128)(2,1)}, u32[]{:S(2)}) copy-start(bf16[1040,128]{1,0:T(8,128)(2,1)} %get-tuple-element.74) | copy-start | bytes 798724
  11.8 15.1 %copy-start.3 = (bf16[1024,512]{1,0:T(8,128)(2,1)S(1)}, bf16[1024,512]{1,0:T(8,128)(2,1)}, u32[]{:S(2)}) copy-start(bf16[1024,512]{1,0:T(8,128)(2,1)} %refs_4_.5) | copy-start | bytes 3145732
  16.6 10.3 %collective-permute-start.6 = (bf16[1040,128]{1,0:T(8,128)(2,1)S(1)}, bf16[1040,128]{1,0:T(8,128)(2,1)S(1)}, u32[]{:S(2)}, u32[]{:S(2)}) collective-permute-start(bf16[1040,128]{1,0:T(8,128)(2,1)S(1)} %get-tuple-element.79), channel_id=1, source_target_pairs={{0,1},{8,9},{9,8},{4,5},{5,4},{12,13},{13,12},{1,0},{2,3},{10,11},... | collective-permute-start | bytes 798728 | tf_op jit(solution)/shard_map/ppermute | solution.py:553
  17.4 14.3 %collective-permute-start.3 = (bf16[1040,128]{1,0:T(8,128)(2,1)S(1)}, bf16[1040,128]{1,0:T(8,128)(2,1)S(1)}, u32[]{:S(2)}, u32[]{:S(2)}) collective-permute-start(bf16[1040,128]{1,0:T(8,128)(2,1)S(1)} %get-tuple-element.76), channel_id=1, source_target_pairs={{0,5},{8,13},{9,12},{4,9},{5,8},{12,1},{13,0},{1,4},{2,7},{10,15},... | collective-permute-start | bytes 798728 | tf_op jit(solution)/shard_map/ppermute | solution.py:553
  18.6 27.5 %collective-permute-start.2 = (bf16[1040,128]{1,0:T(8,128)(2,1)S(1)}, bf16[1040,128]{1,0:T(8,128)(2,1)S(1)}, u32[]{:S(2)}, u32[]{:S(2)}) collective-permute-start(bf16[1040,128]{1,0:T(8,128)(2,1)S(1)} %get-tuple-element.70.refs_4_), channel_id=1, source_target_pairs={{0,4},{8,12},{9,13},{4,8},{5,9},{12,0},{13,1},{1,5},{2,6},{10,14},... | collective-permute-start | bytes 798728 | tf_op jit(solution)/shard_map/ppermute | solution.py:553
  19.0 39.5 %collective-permute-start = (bf16[1040,128]{1,0:T(8,128)(2,1)S(1)}, bf16[1040,128]{1,0:T(8,128)(2,1)S(1)}, u32[]{:S(2)}, u32[]{:S(2)}) collective-permute-start(bf16[1040,128]{1,0:T(8,128)(2,1)S(1)} %copy-done.8), channel_id=1, source_target_pairs={{0,8},{8,0},{9,1},{4,12},{5,13},{12,4},{13,5},{1,9},{2,10},{10,2},... | collective-permute-start | bytes 798728 | tf_op jit(solution)/shard_map/ppermute | solution.py:553
  21.8 24.3 %collective-permute-start.4 = (bf16[1040,128]{1,0:T(8,128)(2,1)S(1)}, bf16[1040,128]{1,0:T(8,128)(2,1)S(1)}, u32[]{:S(2)}, u32[]{:S(2)}) collective-permute-start(bf16[1040,128]{1,0:T(8,128)(2,1)S(1)} %get-tuple-element.77), channel_id=1, source_target_pairs={{0,12},{8,4},{9,5},{4,0},{5,1},{12,8},{13,9},{1,13},{2,14},{10,6},... | collective-permute-start | bytes 798728 | tf_op jit(solution)/shard_map/ppermute | solution.py:553
  26.9 27.2 %collective-permute-start.5 = (bf16[1040,128]{1,0:T(8,128)(2,1)S(1)}, bf16[1040,128]{1,0:T(8,128)(2,1)S(1)}, u32[]{:S(2)}, u32[]{:S(2)}) collective-permute-start(bf16[1040,128]{1,0:T(8,128)(2,1)S(1)} %get-tuple-element.78), channel_id=1, source_target_pairs={{0,13},{8,5},{9,4},{4,1},{5,0},{12,9},{13,8},{1,12},{2,15},{10,7},... | collective-permute-start | bytes 798728 | tf_op jit(solution)/shard_map/ppermute | solution.py:553
  31.7 49.2 %copy-start.6 = (bf16[1024,1024]{1,0:T(8,128)(2,1)}, bf16[1024,1024]{1,0:T(8,128)(2,1)S(1)}, u32[]{:S(2)}) copy-start(bf16[1024,1024]{1,0:T(8,128)(2,1)S(1)} %get-tuple-element.71.refs_9_.refs_2_.refs_1_) | copy-start | bytes 6291460
  31.7 31.7 %collective-permute-start.20 = (bf16[512,128]{1,0:T(8,128)(2,1)S(1)}, bf16[512,128]{1,0:T(8,128)(2,1)S(1)}, u32[]{:S(2)}, u32[]{:S(2)}) collective-permute-start(bf16[512,128]{1,0:T(8,128)(2,1)S(1)} %get-tuple-element.106), channel_id=1, source_target_pairs={{0,1},{8,9},{9,8},{4,5},{5,4},{12,13},{13,12},{1,0},{2,3},{10,11},... | collective-permute-start | bytes 393224 | tf_op jit(solution)/shard_map/ppermute | solution.py:553
  46.1 20.5 %collective-permute-start.19 = (bf16[512,128]{1,0:T(8,128)(2,1)S(1)}, bf16[512,128]{1,0:T(8,128)(2,1)S(1)}, u32[]{:S(2)}, u32[]{:S(2)}) collective-permute-start(bf16[512,128]{1,0:T(8,128)(2,1)S(1)} %get-tuple-element.104), channel_id=1, source_target_pairs={{0,13},{8,5},{9,4},{4,1},{5,0},{12,9},{13,8},{1,12},{2,15},{10,7},... | collective-permute-start | bytes 393224 | tf_op jit(solution)/shard_map/ppermute | solution.py:553
  54.1 26.8 %collective-permute-start.18 = (bf16[512,128]{1,0:T(8,128)(2,1)S(1)}, bf16[512,128]{1,0:T(8,128)(2,1)S(1)}, u32[]{:S(2)}, u32[]{:S(2)}) collective-permute-start(bf16[512,128]{1,0:T(8,128)(2,1)S(1)} %get-tuple-element.102), channel_id=1, source_target_pairs={{0,12},{8,4},{9,5},{4,0},{5,1},{12,8},{13,9},{1,13},{2,14},{10,6},... | collective-permute-start | bytes 393224 | tf_op jit(solution)/shard_map/ppermute | solution.py:553
  58.4 24.7 %collective-permute-start.17 = (bf16[512,128]{1,0:T(8,128)(2,1)S(1)}, bf16[512,128]{1,0:T(8,128)(2,1)S(1)}, u32[]{:S(2)}, u32[]{:S(2)}) collective-permute-start(bf16[512,128]{1,0:T(8,128)(2,1)S(1)} %get-tuple-element.100), channel_id=1, source_target_pairs={{0,5},{8,13},{9,12},{4,9},{5,8},{12,1},{13,0},{1,4},{2,7},{10,15},... | collective-permute-start | bytes 393224 | tf_op jit(solution)/shard_map/ppermute | solution.py:553
  58.4 24.8 %collective-permute-start.16 = (bf16[512,128]{1,0:T(8,128)(2,1)S(1)}, bf16[512,128]{1,0:T(8,128)(2,1)S(1)}, u32[]{:S(2)}, u32[]{:S(2)}) collective-permute-start(bf16[512,128]{1,0:T(8,128)(2,1)S(1)} %get-tuple-element.98), channel_id=1, source_target_pairs={{0,4},{8,12},{9,13},{4,8},{5,9},{12,0},{13,1},{1,5},{2,6},{10,14},... | collective-permute-start | bytes 393224 | tf_op jit(solution)/shard_map/ppermute | solution.py:553
  63.4 20.0 %collective-permute-start.15 = (bf16[512,128]{1,0:T(8,128)(2,1)S(1)}, bf16[512,128]{1,0:T(8,128)(2,1)S(1)}, u32[]{:S(2)}, u32[]{:S(2)}) collective-permute-start(bf16[512,128]{1,0:T(8,128)(2,1)S(1)} %get-tuple-element.96), channel_id=1, source_target_pairs={{0,9},{8,1},{9,0},{4,13},{5,12},{12,5},{13,4},{1,8},{2,11},{10,3},... | collective-permute-start | bytes 393224 | tf_op jit(solution)/shard_map/ppermute | solution.py:553
  66.7 19.3 %collective-permute-start.14 = (bf16[512,128]{1,0:T(8,128)(2,1)S(1)}, bf16[512,128]{1,0:T(8,128)(2,1)S(1)}, u32[]{:S(2)}, u32[]{:S(2)}) collective-permute-start(bf16[512,128]{1,0:T(8,128)(2,1)S(1)} %get-tuple-element.94), channel_id=1, source_target_pairs={{0,8},{8,0},{9,1},{4,12},{5,13},{12,4},{13,5},{1,9},{2,10},{10,2},... | collective-permute-start | bytes 393224 | tf_op jit(solution)/shard_map/ppermute | solution.py:553
  80.8 23.5 %collective-permute-start.7 = (bf16[512,128]{1,0:T(8,128)(2,1)S(1)}, bf16[512,128]{1,0:T(8,128)(2,1)S(1)}, u32[]{:S(2)}, u32[]{:S(2)}) collective-permute-start(bf16[512,128]{1,0:T(8,128)(2,1)S(1)} %get-tuple-element.81), channel_id=1, source_target_pairs={{0,8},{8,0},{9,1},{4,12},{5,13},{12,4},{13,5},{1,9},{2,10},{10,2},... | collective-permute-start | bytes 393224 | tf_op jit(solution)/shard_map/ppermute | solution.py:553
  83.1 22.3 %collective-permute-start.8 = (bf16[512,128]{1,0:T(8,128)(2,1)S(1)}, bf16[512,128]{1,0:T(8,128)(2,1)S(1)}, u32[]{:S(2)}, u32[]{:S(2)}) collective-permute-start(bf16[512,128]{1,0:T(8,128)(2,1)S(1)} %get-tuple-element.82), channel_id=1, source_target_pairs={{0,9},{8,1},{9,0},{4,13},{5,12},{12,5},{13,4},{1,8},{2,11},{10,3},... | collective-permute-start | bytes 393224 | tf_op jit(solution)/shard_map/ppermute | solution.py:553
  83.2 23.2 %collective-permute-start.9 = (bf16[512,128]{1,0:T(8,128)(2,1)S(1)}, bf16[512,128]{1,0:T(8,128)(2,1)S(1)}, u32[]{:S(2)}, u32[]{:S(2)}) collective-permute-start(bf16[512,128]{1,0:T(8,128)(2,1)S(1)} %get-tuple-element.83), channel_id=1, source_target_pairs={{0,4},{8,12},{9,13},{4,8},{5,9},{12,0},{13,1},{1,5},{2,6},{10,14},... | collective-permute-start | bytes 393224 | tf_op jit(solution)/shard_map/ppermute | solution.py:553
  83.4 24.7 %collective-permute-start.10 = (bf16[512,128]{1,0:T(8,128)(2,1)S(1)}, bf16[512,128]{1,0:T(8,128)(2,1)S(1)}, u32[]{:S(2)}, u32[]{:S(2)}) collective-permute-start(bf16[512,128]{1,0:T(8,128)(2,1)S(1)} %get-tuple-element.84), channel_id=1, source_target_pairs={{0,5},{8,13},{9,12},{4,9},{5,8},{12,1},{13,0},{1,4},{2,7},{10,15},... | collective-permute-start | bytes 393224 | tf_op jit(solution)/shard_map/ppermute | solution.py:553
  86.0 42.3 %copy-start.7 = (bf16[1024,1024]{1,0:T(8,128)(2,1)S(1)}, bf16[1024,1024]{1,0:T(8,128)(2,1)}, u32[]{:S(2)}) copy-start(bf16[1024,1024]{1,0:T(8,128)(2,1)} %copy-done.6) | copy-start | bytes 6291460
  102.6 25.1 %collective-permute-start.21 = (bf16[544,128]{1,0:T(8,128)(2,1)S(1)}, bf16[544,128]{1,0:T(8,128)(2,1)S(1)}, u32[]{:S(2)}, u32[]{:S(2)}) collective-permute-start(bf16[544,128]{1,0:T(8,128)(2,1)S(1)} %get-tuple-element.108), channel_id=1, source_target_pairs={{0,8},{8,0},{9,1},{4,12},{5,13},{12,4},{13,5},{1,9},{2,10},{10,2},... | collective-permute-start | bytes 417800 | tf_op jit(solution)/shard_map/ppermute | solution.py:553
  104.3 24.0 %collective-permute-start.22 = (bf16[544,128]{1,0:T(8,128)(2,1)S(1)}, bf16[544,128]{1,0:T(8,128)(2,1)S(1)}, u32[]{:S(2)}, u32[]{:S(2)}) collective-permute-start(bf16[544,128]{1,0:T(8,128)(2,1)S(1)} %get-tuple-element.109), channel_id=1, source_target_pairs={{0,9},{8,1},{9,0},{4,13},{5,12},{12,5},{13,4},{1,8},{2,11},{10,3},... | collective-permute-start | bytes 417800 | tf_op jit(solution)/shard_map/ppermute | solution.py:553
  105.4 8.8 %collective-permute-start.11 = (bf16[512,128]{1,0:T(8,128)(2,1)S(1)}, bf16[512,128]{1,0:T(8,128)(2,1)S(1)}, u32[]{:S(2)}, u32[]{:S(2)}) collective-permute-start(bf16[512,128]{1,0:T(8,128)(2,1)S(1)} %get-tuple-element.85), channel_id=1, source_target_pairs={{0,12},{8,4},{9,5},{4,0},{5,1},{12,8},{13,9},{1,13},{2,14},{10,6},... | collective-permute-start | bytes 393224 | tf_op jit(solution)/shard_map/ppermute | solution.py:553
  106.4 18.1 %collective-permute-start.12 = (bf16[512,128]{1,0:T(8,128)(2,1)S(1)}, bf16[512,128]{1,0:T(8,128)(2,1)S(1)}, u32[]{:S(2)}, u32[]{:S(2)}) collective-permute-start(bf16[512,128]{1,0:T(8,128)(2,1)S(1)} %get-tuple-element.86), channel_id=1, source_target_pairs={{0,13},{8,5},{9,4},{4,1},{5,0},{12,9},{13,8},{1,12},{2,15},{10,7},... | collective-permute-start | bytes 393224 | tf_op jit(solution)/shard_map/ppermute | solution.py:553
  108.2 18.8 %collective-permute-start.13 = (bf16[512,128]{1,0:T(8,128)(2,1)S(1)}, bf16[512,128]{1,0:T(8,128)(2,1)S(1)}, u32[]{:S(2)}, u32[]{:S(2)}) collective-permute-start(bf16[512,128]{1,0:T(8,128)(2,1)S(1)} %get-tuple-element.87), channel_id=1, source_target_pairs={{0,1},{8,9},{9,8},{4,5},{5,4},{12,13},{13,12},{1,0},{2,3},{10,11},... | collective-permute-start | bytes 393224 | tf_op jit(solution)/shard_map/ppermute | solution.py:553
  114.2 18.1 %collective-permute-start.23 = (bf16[544,128]{1,0:T(8,128)(2,1)S(1)}, bf16[544,128]{1,0:T(8,128)(2,1)S(1)}, u32[]{:S(2)}, u32[]{:S(2)}) collective-permute-start(bf16[544,128]{1,0:T(8,128)(2,1)S(1)} %get-tuple-element.110), channel_id=1, source_target_pairs={{0,4},{8,12},{9,13},{4,8},{5,9},{12,0},{13,1},{1,5},{2,6},{10,14},... | collective-permute-start | bytes 417800 | tf_op jit(solution)/shard_map/ppermute | solution.py:553
  124.5 7.9 %collective-permute-start.24 = (bf16[544,128]{1,0:T(8,128)(2,1)S(1)}, bf16[544,128]{1,0:T(8,128)(2,1)S(1)}, u32[]{:S(2)}, u32[]{:S(2)}) collective-permute-start(bf16[544,128]{1,0:T(8,128)(2,1)S(1)} %get-tuple-element.111), channel_id=1, source_target_pairs={{0,5},{8,13},{9,12},{4,9},{5,8},{12,1},{13,0},{1,4},{2,7},{10,15},... | collective-permute-start | bytes 417800 | tf_op jit(solution)/shard_map/ppermute | solution.py:553
  127.0 8.3 %collective-permute-start.25 = (bf16[544,128]{1,0:T(8,128)(2,1)S(1)}, bf16[544,128]{1,0:T(8,128)(2,1)S(1)}, u32[]{:S(2)}, u32[]{:S(2)}) collective-permute-start(bf16[544,128]{1,0:T(8,128)(2,1)S(1)} %get-tuple-element.112), channel_id=1, source_target_pairs={{0,12},{8,4},{9,5},{4,0},{5,1},{12,8},{13,9},{1,13},{2,14},{10,6},... | collective-permute-start | bytes 417800 | tf_op jit(solution)/shard_map/ppermute | solution.py:553
  127.7 10.5 %collective-permute-start.26 = (bf16[544,128]{1,0:T(8,128)(2,1)S(1)}, bf16[544,128]{1,0:T(8,128)(2,1)S(1)}, u32[]{:S(2)}, u32[]{:S(2)}) collective-permute-start(bf16[544,128]{1,0:T(8,128)(2,1)S(1)} %get-tuple-element.113), channel_id=1, source_target_pairs={{0,13},{8,5},{9,4},{4,1},{5,0},{12,9},{13,8},{1,12},{2,15},{10,7},... | collective-permute-start | bytes 417800 | tf_op jit(solution)/shard_map/ppermute | solution.py:553
  128.3 9.9 %collective-permute-start.27 = (bf16[544,128]{1,0:T(8,128)(2,1)S(1)}, bf16[544,128]{1,0:T(8,128)(2,1)S(1)}, u32[]{:S(2)}, u32[]{:S(2)}) collective-permute-start(bf16[544,128]{1,0:T(8,128)(2,1)S(1)} %get-tuple-element.114), channel_id=1, source_target_pairs={{0,1},{8,9},{9,8},{4,5},{5,4},{12,13},{13,12},{1,0},{2,3},{10,11},... | collective-permute-start | bytes 417800 | tf_op jit(solution)/shard_map/ppermute | solution.py:553
  142.2 29.9 %collective-permute-start.29 = (bf16[1024,512]{1,0:T(8,128)(2,1)S(1)}, bf16[1024,512]{1,0:T(8,128)(2,1)S(1)}, u32[]{:S(2)}, u32[]{:S(2)}) collective-permute-start(bf16[1024,512]{1,0:T(8,128)(2,1)S(1)} %get-tuple-element.119), channel_id=1, source_target_pairs={{0,2},{2,0},{1,3},{3,1},{4,6},{6,4},{5,7},{7,5},{8,10},{10,8},{9,1... | collective-permute-start | bytes 3145736 | tf_op jit(solution)/shard_map/ppermute | solution.py:559
  143.7 2.6 %collective-permute-start.33 = (bf16[4,128,512]{2,1,0:T(8,128)(2,1)S(1)}, bf16[4,128,512]{2,1,0:T(8,128)(2,1)S(1)}, u32[]{:S(2)}, u32[]{:S(2)}) collective-permute-start(bf16[4,128,512]{2,1,0:T(8,128)(2,1)S(1)} %get-tuple-element.124), channel_id=1, source_target_pairs={{0,1},{1,0},{2,3},{3,2},{4,5},{5,4},{6,7},{7,6},{8,9},{9,8},{10,11... | collective-permute-start | bytes 1572872 | tf_op jit(solution)/shard_map/ppermute | solution.py:559
  145.8 5.1 %collective-permute-start.28 = (bf16[4,128,512]{2,1,0:T(8,128)(2,1)S(1)}, bf16[4,128,512]{2,1,0:T(8,128)(2,1)S(1)}, u32[]{:S(2)}, u32[]{:S(2)}) collective-permute-start(bf16[4,128,512]{2,1,0:T(8,128)(2,1)S(1)} %get-tuple-element.117), channel_id=1, source_target_pairs={{0,1},{1,0},{2,3},{3,2},{4,5},{5,4},{6,7},{7,6},{8,9},{9,8},{10,11... | collective-permute-start | bytes 1572872 | tf_op jit(solution)/shard_map/ppermute | solution.py:559
  147.0 8.3 %collective-permute-start.34 = (bf16[128,512]{1,0:T(8,128)(2,1)S(1)}, bf16[128,512]{1,0:T(8,128)(2,1)S(1)}, u32[]{:S(2)}, u32[]{:S(2)}) collective-permute-start(bf16[128,512]{1,0:T(8,128)(2,1)S(1)} %get-tuple-element.130), channel_id=1, source_target_pairs={{0,4},{4,8},{8,12},{12,0},{1,5},{5,9},{9,13},{13,1},{2,6},{6,10},{... | collective-permute-start | bytes 393224 | tf_op jit(solution)/shard_map/ppermute | solution.py:559
  147.6 13.4 %collective-permute-start.35 = (bf16[128,512]{1,0:T(8,128)(2,1)S(1)}, bf16[128,512]{1,0:T(8,128)(2,1)S(1)}, u32[]{:S(2)}, u32[]{:S(2)}) collective-permute-start(bf16[128,512]{1,0:T(8,128)(2,1)S(1)} %get-tuple-element.131), channel_id=1, source_target_pairs={{0,8},{4,12},{8,0},{12,4},{1,9},{5,13},{9,1},{13,5},{2,10},{6,14},... | collective-permute-start | bytes 393224 | tf_op jit(solution)/shard_map/ppermute | solution.py:559
  150.1 16.0 %collective-permute-start.36 = (bf16[128,512]{1,0:T(8,128)(2,1)S(1)}, bf16[128,512]{1,0:T(8,128)(2,1)S(1)}, u32[]{:S(2)}, u32[]{:S(2)}) collective-permute-start(bf16[128,512]{1,0:T(8,128)(2,1)S(1)} %get-tuple-element.132), channel_id=1, source_target_pairs={{0,12},{4,0},{8,4},{12,8},{1,13},{5,1},{9,5},{13,9},{2,14},{6,2},{... | collective-permute-start | bytes 393224 | tf_op jit(solution)/shard_map/ppermute | solution.py:559
  151.6 17.4 %collective-permute-start.30 = (bf16[128,512]{1,0:T(8,128)(2,1)S(1)}, bf16[128,512]{1,0:T(8,128)(2,1)S(1)}, u32[]{:S(2)}, u32[]{:S(2)}) collective-permute-start(bf16[128,512]{1,0:T(8,128)(2,1)S(1)} %get-tuple-element.120), channel_id=1, source_target_pairs={{0,4},{4,8},{8,12},{12,0},{1,5},{5,9},{9,13},{13,1},{2,6},{6,10},{... | collective-permute-start | bytes 393224 | tf_op jit(solution)/shard_map/ppermute | solution.py:559
  155.3 15.9 %collective-permute-start.31 = (bf16[128,512]{1,0:T(8,128)(2,1)S(1)}, bf16[128,512]{1,0:T(8,128)(2,1)S(1)}, u32[]{:S(2)}, u32[]{:S(2)}) collective-permute-start(bf16[128,512]{1,0:T(8,128)(2,1)S(1)} %get-tuple-element.121), channel_id=1, source_target_pairs={{0,8},{4,12},{8,0},{12,4},{1,9},{5,13},{9,1},{13,5},{2,10},{6,14},... | collective-permute-start | bytes 393224 | tf_op jit(solution)/shard_map/ppermute | solution.py:559
  161.0 10.3 %collective-permute-start.32 = (bf16[128,512]{1,0:T(8,128)(2,1)S(1)}, bf16[128,512]{1,0:T(8,128)(2,1)S(1)}, u32[]{:S(2)}, u32[]{:S(2)}) collective-permute-start(bf16[128,512]{1,0:T(8,128)(2,1)S(1)} %get-tuple-element.122), channel_id=1, source_target_pairs={{0,12},{4,0},{8,4},{12,8},{1,13},{5,1},{9,5},{13,9},{2,14},{6,2},{... | collective-permute-start | bytes 393224 | tf_op jit(solution)/shard_map/ppermute | solution.py:559

commit v12 on v11

--- a/solution.py
+++ b/solution.py
@@ -216,12 +216,13 @@
             sorted_ref[group * heads + 2 * pair + 1, pl.ds(first, part), :] = odd
 
     hand_out(sorted_ref, out_refs, me_ref, sizes)
-    turned_ref[...] = tokens_ref[...].T
+    turned = tokens_ref[...].T
     slots = unsort_ref.shape[1]
     part = min(256, slots)
     for i in range(slots // part):
         pick = ones_where(iota((part, toks), 0) + i * part == slot_ref[...])
         unsort_ref[:, i * part : (i + 1) * part] = pick.T
+        turned_ref[:, i * part : (i + 1) * part] = dot_nt(turned, pick).astype(BF16)
 
 
 def score(mixed):
@@ -422,18 +423,10 @@
     return x.astype(BF16)
 
 
-def bring_home(sizes, heads, me_ref, part_refs, unsort_ref, home_ref, sorted_ref, rows_ref):
+def bring_home(sizes, heads, me_ref, part_refs, home_ref, rows_ref):
     for ahead, part_ref in zip(steps_of(sizes), part_refs):
         home_ref[source_of(me_ref, ahead, sizes)] = part_ref[...]
-    half = sorted_ref.shape[0] * heads // (sizes[0] * sizes[1]) // 2
-    unfold(home_ref, sorted_ref, heads, 0, half, to_half)
-    toks = rows_ref.shape[0]
-    step = min(512, toks)
-
-    @pl.loop(0, toks // step)
-    def _(i):
-        where = pl.ds(pl.multiple_of(i * step, step), step)
-        rows_ref[where, :] = dot(unsort_ref[where, :], sorted_ref[...]).astype(BF16)
+    unfold(home_ref, rows_ref, heads, 0, rows_ref.shape[0] * heads // home_ref.shape[0] // 2, to_half)
 
 
 def weight_partial(sizes, me_ref, turned_ref, rows_ref, whole_ref, sub_refs):
@@ -453,49 +446,43 @@
             sub_ref[seq] = whole_ref[pl.ds(first, piece), :]
 
 
-def value_home_kernel(sizes, heads, me_ref, turned_ref, unsort_ref, *refs):
-    part_refs, rows_ref, sub_refs = refs[: -4 - sizes[1]], refs[-4 - sizes[1]], refs[-3 - sizes[1] : -3]
-    home_ref, sorted_ref, whole_ref = refs[-3:]
-    bring_home(sizes, heads, me_ref, part_refs, unsort_ref, home_ref, sorted_ref, rows_ref)
+def input_columns(me_ref, ahead, parts, width):
+    columns = width // parts
+    dest = lax.rem(me_ref[2] + ahead, jnp.int32(parts))
+    return pl.ds(pl.multiple_of(dest * columns, columns), columns)
+
+
+def value_home_kernel(sizes, heads, parts, me_ref, turned_ref, weight_ref, *refs):
+    part_refs, refs = refs[: sizes[0] * sizes[1]], refs[sizes[0] * sizes[1] :]
+    rows_ref, term_refs, refs = refs[0], refs[1:parts], refs[parts:]
+    sub_refs, (home_ref, whole_ref) = refs[: sizes[1]], refs[sizes[1] :]
+    bring_home(sizes, heads, me_ref, part_refs, home_ref, rows_ref)
+    for k, term_ref in enumerate(term_refs):
+        mine = input_columns(me_ref, k + 1, parts, weight_ref.shape[0])
+        term_ref[...] = dot_nt(rows_ref[...], weight_ref[mine, :])
     weight_partial(sizes, me_ref, turned_ref, rows_ref, whole_ref, sub_refs)
 
 
-def input_partial(me_ref, ahead, parts, rows_ref, value_rows_ref, w_query_ref, w_value_ref, out_ref):
-    toks = rows_ref.shape[0]
-    columns = w_query_ref.shape[0] // parts
-    step = min(512, toks)
-    dest = lax.rem(me_ref[2] + ahead, jnp.int32(parts))
-    mine = pl.ds(pl.multiple_of(dest * columns, columns), columns)
-
-    @pl.loop(0, toks // step)
-    def _(i):
-        where = pl.ds(pl.multiple_of(i * step, step), step)
-        total = dot_nt(rows_ref[where, :], w_query_ref[mine, :])
-        total = total + dot_nt(value_rows_ref[where, :], w_value_ref[mine, :])
-        out_ref[where, :] = total.astype(BF16)
-
-
-def query_home_kernel(
-    sizes, heads, factor, parts, me_ref, unsort_ref, value_rows_ref, w_query_ref, w_value_ref, *refs
-):
-    part_refs, out_refs, (rows_ref, centroid_ref, home_ref, sorted_ref) = (
-        refs[: -3 - parts],
-        refs[-3 - parts : -4],
-        refs[-4:],
-    )
-    bring_home(sizes, heads, me_ref, part_refs, unsort_ref, home_ref, sorted_ref, rows_ref)
-    half = sorted_ref.shape[0] * heads // (sizes[0] * sizes[1]) // 2
+def query_home_kernel(sizes, heads, factor, parts, me_ref, weight_ref, *refs):
+    term_refs, refs = refs[: parts - 1], refs[parts - 1 :]
+    part_refs, refs = refs[: sizes[0] * sizes[1]], refs[sizes[0] * sizes[1] :]
+    out_refs, (rows_ref, centroid_ref, home_ref) = refs[: parts - 1], refs[parts - 1 :]
+    bring_home(sizes, heads, me_ref, part_refs, home_ref, rows_ref)
+    for k, (term_ref, out_ref) in enumerate(zip(term_refs, out_refs)):
+        mine = input_columns(me_ref, k + 1, parts, weight_ref.shape[0])
+        out_ref[...] = (dot_nt(rows_ref[...], weight_ref[mine, :]) + term_ref[...]).astype(BF16)
+    half = rows_ref.shape[0] * heads // home_ref.shape[0] // 2
     unfold(home_ref, centroid_ref, heads, half, home_ref.shape[1] - half, lambda x: x * factor)
-    for ahead, out_ref in enumerate(out_refs):
-        input_partial(me_ref, ahead + 1, parts, rows_ref, value_rows_ref, w_query_ref, w_value_ref, out_ref)
 
 
 def query_weight_kernel(sizes, me_ref, turned_ref, rows_ref, *refs):
     weight_partial(sizes, me_ref, turned_ref, rows_ref, refs[-1], refs[:-1])
 
 
-def input_own_kernel(parts, me_ref, *refs):
-    input_partial(me_ref, 0, parts, *refs)
+def input_own_kernel(parts, me_ref, rows_ref, value_rows_ref, w_query_ref, w_value_ref, out_ref):
+    mine = input_columns(me_ref, 0, parts, w_query_ref.shape[0])
+    total = dot_nt(rows_ref[...], w_query_ref[mine, :]) + dot_nt(value_rows_ref[...], w_value_ref[mine, :])
+    out_ref[...] = total.astype(BF16)
 
 
 def fold_subs_kernel(me_ref, *refs):
@@ -514,6 +501,15 @@
     for ref in refs[1:-1]:
         total = total + ref[...].astype(F32)
     refs[-1][...] = total.astype(refs[-1].dtype)
+
+
+def input_sum_kernel(unsort_ref, *refs):
+    part_refs, out_ref, total_ref = refs[:-2], refs[-2], refs[-1]
+    total = part_refs[0][...].astype(F32)
+    for part_ref in part_refs[1:]:
+        total = total + part_ref[...].astype(F32)
+    total_ref[...] = total.astype(BF16)
+    out_ref[...] = dot(unsort_ref[...], total_ref[...]).astype(BF16)
 
 
 def call(kernel, outs, inputs, smem=(0,), in_place=(), after=(), scratch=(), flops=0, vmem=24, name=None):
@@ -632,14 +628,14 @@
     got_mixed = exchange(send_mixed, sizes)
     *send_value, turned, unsort = call(
         functools.partial(project_value_kernel, sizes, groups, rows),
-        several(owners, half, LANES) + several(1, width, toks) + several(1, toks, slots),
+        several(owners, half, LANES) + several(1, width, slots) + several(1, toks, slots),
         (me, slot_row, tokens_in, w_value),
         after=near_mixed[:1],
         scratch=[pltpu.VMEM((toks, width_dev), BF16), pltpu.VMEM((owners, half, LANES), BF16)],
         flops=2 * toks * width * width_dev + 2 * slots * toks * width_dev,
         name="project_value",
     )
-    behind = [got_mixed[min(k + 2, owners - 1)] for k in range(owners)]
+    behind = [got_mixed[owners - k if k else 0] for k in range(owners)]
     send_value = [lax.optimization_barrier(pair)[0] for pair in zip(send_value, behind)]
     got_value = exchange(send_value, sizes)
     blocks = per_group * capacity // BLOCK_ROWS
@@ -678,28 +674,28 @@
         name="query_grad",
     )
     home_query = exchange(back_query, sizes)
-    weight_flops = 2 * toks * width * width_dev
-    home_flops = 2 * slots * toks * width_dev
+    weight_flops = 2 * slots * width * width_dev
+    home_flops = weight_flops // parts * (parts - 1)
     sub_shapes = several(sizes[1], sizes[0], width // owners, width_dev)
     whole = pltpu.VMEM((width, width_dev), BF16)
-    sorted_rows = pltpu.VMEM((slots, width_dev), BF16)
-    value_rows, *value_weight = call(
-        functools.partial(value_home_kernel, sizes, heads),
-        several(1, toks, width_dev) + sub_shapes,
-        (me, turned, unsort, *home_value),
-        scratch=[pltpu.VMEM((owners, half, LANES), BF16), sorted_rows, whole],
+    value_rows, *refs = call(
+        functools.partial(value_home_kernel, sizes, heads, parts),
+        several(1, slots, width_dev) + (shape((slots, columns), F32),) * (parts - 1) + sub_shapes,
+        (me, turned, w_value, *home_value),
+        scratch=[pltpu.VMEM((owners, half, LANES), BF16), whole],
         flops=weight_flops + home_flops,
         name="value_home",
     )
+    value_terms, value_weight = refs[: parts - 1], refs[parts - 1 :]
     value_weight = fold_subs(me, value_weight, "value_subs")
     *partials, query_rows, centroid_grad = call(
         functools.partial(query_home_kernel, sizes, heads, (CLUSTERS / (toks * owners)) ** 0.5, parts),
-        several(parts - 1, toks, columns)
-        + several(1, toks, width_dev)
+        several(parts - 1, slots, columns)
+        + several(1, slots, width_dev)
         + (shape((groups * 2 * extra, width_dev), F32),),
-        (me, unsort, value_rows, w_query, w_value, *home_query),
-        scratch=[pltpu.VMEM((owners, half + extra, LANES), BF16), sorted_rows],
-        flops=weight_flops + home_flops,
+        (me, w_query, *value_terms, *home_query),
+        scratch=[pltpu.VMEM((owners, half + extra, LANES), BF16)],
+        flops=home_flops,
         name="query_home",
     )
     arrived = [shift(partial, "head", k + 1) for k, partial in enumerate(partials)]
@@ -716,7 +712,7 @@
     query_weight = fold_subs(me, query_weight, "query_subs")
     own = call(
         functools.partial(input_own_kernel, parts),
-        shape((toks, columns), BF16),
+        shape((slots, columns), BF16),
         (me, query_rows, value_rows, w_query, w_value),
         after=query_weight[:1],
         flops=weight_flops * 2 // parts,
@@ -725,7 +721,15 @@
     query_weight = pass_round(query_weight, "seq")
     grad_wv = add_up(value_weight, F32, "value_sum")
     grad_wq = add_up(query_weight, F32, "query_sum")
-    grad_input = add_up([own] + arrived, BF16, "input_sum")
+    grad_input = call(
+        input_sum_kernel,
+        shape((toks, columns), BF16),
+        (unsort, own, *arrived),
+        smem=(),
+        scratch=[pltpu.VMEM((slots, columns), BF16)],
+        flops=2 * toks * slots * columns,
+        name="input_sum",
+    )
     if groups > 1:
         centroid_grad = centroid_grad.reshape(groups, 2 * extra, width_dev)[:, :per_group]
         centroid_grad = centroid_grad.reshape(CLUSTERS, width_dev)

time: 173 us -> 173 us (level)
    ppermute x28, starting transfers between devices: 66.1 us -> 63.3 us  [exchange(): out.append(part if ahead == (0, 0) else lax.ppermute(part, OWNERS, moves))]
    ppermute x28, waiting for transfers between devices: 20.2 us -> 22.7 us  [exchange(): out.append(part if ahead == (0, 0) else lax.ppermute(part, OWNERS, moves))]
    ppermute x9, starting transfers between devices: 12.5 us -> 14.4 us  [shift(): lax.ppermute(part, axis, [(i, (i + ahead) % size) for i in range(size)])]
    ppermute x9, waiting for transfers between devices: 10.4 us -> 8.55 us  [shift(): lax.ppermute(part, axis, [(i, (i + ahead) % size) for i in range(size)])]
  transfers between devices with their start and end apart: 37 -> 37, of which waited for: 9 -> 10; matrix products, arithmetic and copies ran while one was open for 0% -> 0% of each run, Pallas kernels for 29% -> 30%
where the time goes in v12:
time: 173 us
  starting transfers between devices  77.7 us (45%)
  Pallas kernels  60.8 us (35%)
  waiting for transfers between devices  31.3 us (18%)
  local copies, waits for them, and re-layouts  1.93 us (1%)
    ppermute x28, starting transfers between devices, exchange(): out.append(part if ahead == (0, 0) else lax.ppermute(part, OWNERS, moves))  63.3 us
    pallas_call x14, Pallas kernels, call(): pl.pallas_call(body, out_shape=outs, in_specs=specs, out_specs=jax.tree.m...  60.8 us
    ppermute x28, waiting for transfers between devices, exchange(): out.append(part if ahead == (0, 0) else lax.ppermute(part, OWNERS, moves))  22.7 us
    ppermute x9, starting transfers between devices, shift(): lax.ppermute(part, axis, [(i, (i + ahead) % size) for i in range(size)])  14.4 us
    ppermute x9, waiting for transfers between devices, shift(): lax.ppermute(part, axis, [(i, (i + ahead) % size) for i in range(size)])  8.55 us
  transfers between devices with their start and end apart: 37, of which 10 were waited for; matrix products, arithmetic and copies ran while one was open for 0% of the time, Pallas kernels for 30%

profile of v12, /device:TPU:0, one launch (start us, length us, event | category | flops | bytes accessed | tf_op | source)
XLA Modules:
  0.0 172.6 jit_solution(11441484752133664920)
XLA Ops:
  0.7 5.6 %project_far.1 = (bf16[1040,128]{1,0:T(8,128)(2,1)}, bf16[1040,128]{1,0:T(8,128)(2,1)}, s32[1,1024]{1,0:T(1,128)}) custom-call(s32[1,1024]{1,0:T(1,128)} %bitcast.5, bf16[1024,1024]{1,0:T(8,128)(2,1)} %refs_2_.4, bf16[1024,512]{1,0:T(8,128)(2,1)} %refs_3_.7, bf16[1024,512]{1,0:T(8,128)(2,1)} %refs_5_.1), custom_call_target="tpu_custom_call" | custom-call | flops 805306368 | bytes 4734976 | tf_op jit(solution)/shard_map/project_far/pallas_call | solution.py:527
  6.2 4.1 %collective-permute-start = (bf16[1040,128]{1,0:T(8,128)(2,1)}, bf16[1040,128]{1,0:T(8,128)(2,1)S(1)}, u32[]{:S(2)}, u32[]{:S(2)}) collective-permute-start(bf16[1040,128]{1,0:T(8,128)(2,1)} %get-tuple-element.75), channel_id=1, source_target_pairs={{0,8},{8,0},{9,1},{4,12},{5,13},{12,4},{13,5},{1,9},{2,10},{10,2},... | collective-permute-start | bytes 798728 | tf_op jit(solution)/shard_map/ppermute | solution.py:549
  10.4 1.2 copy-done.2
  11.7 0.7 copy-done.5
  12.4 4.8 %project_query.1 = (bf16[1040,128]{1,0:T(8,128)(2,1)S(1)}, bf16[1040,128]{1,0:T(8,128)(2,1)S(1)}, bf16[1040,128]{1,0:T(8,128)(2,1)S(1)}, bf16[1040,128]{1,0:T(8,...) custom-call(s32[4]{0:T(128)S(1)} %pad_add_fusion.refs_0_, s32[1,1024]{1,0:T(1,128)S(1)} %copy-done.5, ...), custom_call_target="tpu_custom_call" | custom-call | flops 3221225472 | bytes 5799952 | tf_op jit(solution)/shard_map/project_query/pallas_call | solution.py:527
  17.2 3.7 %collective-permute-start.5 = (bf16[1040,128]{1,0:T(8,128)(2,1)S(1)}, bf16[1040,128]{1,0:T(8,128)(2,1)S(1)}, u32[]{:S(2)}, u32[]{:S(2)}) collective-permute-start(bf16[1040,128]{1,0:T(8,128)(2,1)S(1)} %get-tuple-element.79), channel_id=1, source_target_pairs={{0,13},{8,5},{9,4},{4,1},{5,0},{12,9},{13,8},{1,12},{2,15},{10,7},... | collective-permute-start | bytes 798728 | tf_op jit(solution)/shard_map/ppermute | solution.py:549
  20.9 9.3 %collective-permute-done.refs_2_ = bf16[1040,128]{1,0:T(8,128)(2,1)S(1)} collective-permute-done((bf16[1040,128]{1,0:T(8,128)(2,1)}, bf16[1040,128]{1,0:T(8,128)(2,1)S(1)}, u32[]{:S(2)}, u32[]{:S(2)}) %collective-permute-start) | collective-permute-done | bytes 266272 | tf_op jit(solution)/shard_map/ppermute | solution.py:549
  30.2 7.6 %collective-permute-start.4 = (bf16[1040,128]{1,0:T(8,128)(2,1)S(1)}, bf16[1040,128]{1,0:T(8,128)(2,1)S(1)}, u32[]{:S(2)}, u32[]{:S(2)}) collective-permute-start(bf16[1040,128]{1,0:T(8,128)(2,1)S(1)} %get-tuple-element.78), channel_id=1, source_target_pairs={{0,12},{8,4},{9,5},{4,0},{5,1},{12,8},{13,9},{1,13},{2,14},{10,6},... | collective-permute-start | bytes 798728 | tf_op jit(solution)/shard_map/ppermute | solution.py:549
  37.8 1.3 collective-permute-done.1.refs_3_
  39.1 7.3 %collective-permute-start.2 = (bf16[1040,128]{1,0:T(8,128)(2,1)S(1)}, bf16[1040,128]{1,0:T(8,128)(2,1)S(1)}, u32[]{:S(2)}, u32[]{:S(2)}) collective-permute-start(bf16[1040,128]{1,0:T(8,128)(2,1)S(1)} %get-tuple-element.71.refs_4_), channel_id=1, source_target_pairs={{0,4},{8,12},{9,13},{4,8},{5,9},{12,0},{13,1},{1,5},{2,6},{10,14},... | collective-permute-start | bytes 798728 | tf_op jit(solution)/shard_map/ppermute | solution.py:549
  46.4 6.0 %project_value.1 = (bf16[512,128]{1,0:T(8,128)(2,1)S(1)}, bf16[512,128]{1,0:T(8,128)(2,1)S(1)}, bf16[512,128]{1,0:T(8,128)(2,1)S(1)}, bf16[512,128]{1,0:T(8,128)...) custom-call(s32[4]{0:T(128)S(1)} %pad_add_fusion.refs_0_, ...), custom_call_target="tpu_custom_call" | custom-call | flops 2147483648 | bytes 8392720 | tf_op jit(solution)/shard_map/project_value/pallas_call | solution.py:527
  52.6 2.8 %collective-permute-start.19 = (bf16[512,128]{1,0:T(8,128)(2,1)S(1)}, bf16[512,128]{1,0:T(8,128)(2,1)S(1)}, u32[]{:S(2)}, u32[]{:S(2)}) collective-permute-start(bf16[512,128]{1,0:T(8,128)(2,1)S(1)} %get-tuple-element.105), channel_id=1, source_target_pairs={{0,13},{8,5},{9,4},{4,1},{5,0},{12,9},{13,8},{1,12},{2,15},{10,7},... | collective-permute-start | bytes 393224 | tf_op jit(solution)/shard_map/ppermute | solution.py:549
  55.9 2.6 %collective-permute-start.18 = (bf16[512,128]{1,0:T(8,128)(2,1)S(1)}, bf16[512,128]{1,0:T(8,128)(2,1)S(1)}, u32[]{:S(2)}, u32[]{:S(2)}) collective-permute-start(bf16[512,128]{1,0:T(8,128)(2,1)S(1)} %get-tuple-element.103), channel_id=1, source_target_pairs={{0,12},{8,4},{9,5},{4,0},{5,1},{12,8},{13,9},{1,13},{2,14},{10,6},... | collective-permute-start | bytes 393224 | tf_op jit(solution)/shard_map/ppermute | solution.py:549
  58.5 6.9 %collective-permute-start.16 = (bf16[512,128]{1,0:T(8,128)(2,1)S(1)}, bf16[512,128]{1,0:T(8,128)(2,1)S(1)}, u32[]{:S(2)}, u32[]{:S(2)}) collective-permute-start(bf16[512,128]{1,0:T(8,128)(2,1)S(1)} %get-tuple-element.99), channel_id=1, source_target_pairs={{0,4},{8,12},{9,13},{4,8},{5,9},{12,0},{13,1},{1,5},{2,6},{10,14},... | collective-permute-start | bytes 393224 | tf_op jit(solution)/shard_map/ppermute | solution.py:549
  65.4 1.6 collective-permute-start.15
  66.9 1.2 collective-permute-start.14
  68.1 13.9 %value_grad.1 = (bf16[512,128]{1,0:T(8,128)(2,1)S(1)}, bf16[512,128]{1,0:T(8,128)(2,1)S(1)}, bf16[512,128]{1,0:T(8,128)(2,1)S(1)}, bf16[512,128]{1,0:T(8,128)(2,...) custom-call(s32[4]{0:T(128)S(1)} %pad_add_fusion.refs_0_, ...), custom_call_target="tpu_custom_call" | custom-call | flops 2147483648 | bytes 8163344 | tf_op jit(solution)/shard_map/value_grad/pallas_call | solution.py:527
  82.1 1.7 %collective-permute-start.7 = (bf16[512,128]{1,0:T(8,128)(2,1)S(1)}, bf16[512,128]{1,0:T(8,128)(2,1)S(1)}, u32[]{:S(2)}, u32[]{:S(2)}) collective-permute-start(bf16[512,128]{1,0:T(8,128)(2,1)S(1)} %get-tuple-element.82), channel_id=1, source_target_pairs={{0,8},{8,0},{9,1},{4,12},{5,13},{12,4},{13,5},{1,9},{2,10},{10,2},... | collective-permute-start | bytes 393224 | tf_op jit(solution)/shard_map/ppermute | solution.py:549
  84.3 1.7 %collective-permute-start.9 = (bf16[512,128]{1,0:T(8,128)(2,1)S(1)}, bf16[512,128]{1,0:T(8,128)(2,1)S(1)}, u32[]{:S(2)}, u32[]{:S(2)}) collective-permute-start(bf16[512,128]{1,0:T(8,128)(2,1)S(1)} %get-tuple-element.84), channel_id=1, source_target_pairs={{0,4},{8,12},{9,13},{4,8},{5,9},{12,0},{13,1},{1,5},{2,6},{10,14},... | collective-permute-start | bytes 393224 | tf_op jit(solution)/shard_map/ppermute | solution.py:549
  86.1 0.7 collective-permute-start.10
  86.8 16.6 %query_grad.1 = (bf16[544,128]{1,0:T(8,128)(2,1)S(1)}, bf16[544,128]{1,0:T(8,128)(2,1)S(1)}, bf16[544,128]{1,0:T(8,128)(2,1)S(1)}, bf16[544,128]{1,0:T(8,128)(2,...) custom-call(s32[4]{0:T(128)S(1)} %pad_add_fusion.refs_0_, ...), custom_call_target="tpu_custom_call" | custom-call | flops 3221225472 | bytes 7147536 | tf_op jit(solution)/shard_map/query_grad/pallas_call | solution.py:527
  103.4 2.1 %collective-permute-start.21 = (bf16[544,128]{1,0:T(8,128)(2,1)S(1)}, bf16[544,128]{1,0:T(8,128)(2,1)S(1)}, u32[]{:S(2)}, u32[]{:S(2)}) collective-permute-start(bf16[544,128]{1,0:T(8,128)(2,1)S(1)} %get-tuple-element.109), channel_id=1, source_target_pairs={{0,8},{8,0},{9,1},{4,12},{5,13},{12,4},{13,5},{1,9},{2,10},{10,2},... | collective-permute-start | bytes 417800 | tf_op jit(solution)/shard_map/ppermute | solution.py:549
  105.9 3.1 %collective-permute-start.11 = (bf16[512,128]{1,0:T(8,128)(2,1)S(1)}, bf16[512,128]{1,0:T(8,128)(2,1)S(1)}, u32[]{:S(2)}, u32[]{:S(2)}) collective-permute-start(bf16[512,128]{1,0:T(8,128)(2,1)S(1)} %get-tuple-element.86), channel_id=1, source_target_pairs={{0,12},{8,4},{9,5},{4,0},{5,1},{12,8},{13,9},{1,13},{2,14},{10,6},... | collective-permute-start | bytes 393224 | tf_op jit(solution)/shard_map/ppermute | solution.py:549
  109.0 0.7 collective-permute-start.12
  109.8 5.6 %collective-permute-done.11.refs_8_ = bf16[512,128]{1,0:T(8,128)(2,1)S(1)} collective-permute-done((bf16[512,128]{1,0:T(8,128)(2,1)S(1)}, bf16[512,128]{1,0:T(8,128)(2,1)S(1)}, u32[]{:S(2)}, u32[]{:S(2)}) %collective-permute-start.11) | collective-permute-done | bytes 131104 | tf_op jit(solution)/shard_map/ppermute | solution.py:549
  115.4 10.6 %collective-permute-start.23 = (bf16[544,128]{1,0:T(8,128)(2,1)S(1)}, bf16[544,128]{1,0:T(8,128)(2,1)S(1)}, u32[]{:S(2)}, u32[]{:S(2)}) collective-permute-start(bf16[544,128]{1,0:T(8,128)(2,1)S(1)} %get-tuple-element.111), channel_id=1, source_target_pairs={{0,4},{8,12},{9,13},{4,8},{5,9},{12,0},{13,1},{1,5},{2,6},{10,14},... | collective-permute-start | bytes 417800 | tf_op jit(solution)/shard_map/ppermute | solution.py:549
  126.0 1.7 collective-permute-start.24
  128.2 1.4 collective-permute-start.26
  129.7 2.9 %value_home.1 = (bf16[1024,512]{1,0:T(8,128)(2,1)S(1)}, f32[1024,512]{1,0:T(8,128)S(1)}, bf16[4,128,512]{2,1,0:T(8,128)(2,1)S(1)}, bf16[4,128,512]{2,1,0:T(8,128)(2,1)S(1)}) custom-call(s32[4]{0:T(128)S(1)} %pad_add_fusion.refs_0_, bf16[1024,1024]{1,0:T(8,128)(2,1)S(1)} %copy-done.7, bf16[1024,512]{1,0:T(8,128)(2,1)S(1)} %copy-done.3, ...), custom_call_target="tpu_custom_call" | custom-call | flops 1610612736 | bytes 8388624 | tf_op jit(solution)/shard_map/value_home/pallas_call | solution.py:527
  132.6 1.1 collective-permute-done.24.refs_7_
  133.8 2.0 %collective-permute-done.25.refs_8_ = bf16[544,128]{1,0:T(8,128)(2,1)S(1)} collective-permute-done((bf16[544,128]{1,0:T(8,128)(2,1)S(1)}, bf16[544,128]{1,0:T(8,128)(2,1)S(1)}, u32[]{:S(2)}, u32[]{:S(2)}) %collective-permute-start.25) | collective-permute-done | bytes 139296 | tf_op jit(solution)/shard_map/ppermute | solution.py:549
  135.8 2.8 %collective-permute-done.26.refs_9_ = bf16[544,128]{1,0:T(8,128)(2,1)S(1)} collective-permute-done((bf16[544,128]{1,0:T(8,128)(2,1)S(1)}, bf16[544,128]{1,0:T(8,128)(2,1)S(1)}, u32[]{:S(2)}, u32[]{:S(2)}) %collective-permute-start.26) | collective-permute-done | bytes 139296 | tf_op jit(solution)/shard_map/ppermute | solution.py:549
  138.6 2.0 %query_home.1 = (bf16[1024,512]{1,0:T(8,128)(2,1)S(1)}, bf16[1024,512]{1,0:T(8,128)(2,1)S(1)}, f32[64,512]{1,0:T(8,128)}) custom-call(s32[4]{0:T(128)S(1)} %pad_add_fusion.refs_0_, bf16[1024,512]{1,0:T(8,128)(2,1)S(1)} %copy-done, f32[1024,512]{1,0:T(8,128)S(1)} %get-tuple-element.89.refs_2_, bf16[544,128]{1,0:T(8,128)(2,1)S(1)} %get-tuple-element.108.refs_3_, ...), custom_call_target="tpu_custom_call" | custom-call | flops 536870912 | bytes 6488080 | tf_op jit(solution)/shard_map/query_home/pallas_call | solution.py:527
  140.6 1.5 collective-permute-start.29
  142.1 2.0 %query_weight.1 = (bf16[4,128,512]{2,1,0:T(8,128)(2,1)S(1)}, bf16[4,128,512]{2,1,0:T(8,128)(2,1)S(1)}) custom-call(s32[4]{0:T(128)S(1)} %pad_add_fusion.refs_0_, bf16[1024,1024]{1,0:T(8,128)(2,1)S(1)} %copy-done.7, bf16[1024,512]{1,0:T(8,128)(2,1)S(1)} %get-tuple-element.116.refs_2_.refs_1_), custom_call_target="tpu_custom_call" | custom-call | flops 1073741824 | bytes 4194320 | tf_op jit(solution)/shard_map/query_weight/pallas_call | solution.py:527
  144.7 0.7 value_subs.1
  145.4 0.7 collective-permute-start.34
  146.1 2.9 %collective-permute-start.35 = (bf16[128,512]{1,0:T(8,128)(2,1)S(1)}, bf16[128,512]{1,0:T(8,128)(2,1)S(1)}, u32[]{:S(2)}, u32[]{:S(2)}) collective-permute-start(bf16[128,512]{1,0:T(8,128)(2,1)S(1)} %get-tuple-element.133), channel_id=1, source_target_pairs={{0,8},{4,12},{8,0},{12,4},{1,9},{5,13},{9,1},{13,5},{2,10},{6,14},... | collective-permute-start | bytes 393224 | tf_op jit(solution)/shard_map/ppermute | solution.py:555
  149.3 0.7 query_subs.1
  149.9 1.7 %collective-permute-start.30 = (bf16[128,512]{1,0:T(8,128)(2,1)S(1)}, bf16[128,512]{1,0:T(8,128)(2,1)S(1)}, u32[]{:S(2)}, u32[]{:S(2)}) collective-permute-start(bf16[128,512]{1,0:T(8,128)(2,1)S(1)} %get-tuple-element.122), channel_id=1, source_target_pairs={{0,4},{4,8},{8,12},{12,0},{1,5},{5,9},{9,13},{13,1},{2,6},{6,10},{... | collective-permute-start | bytes 393224 | tf_op jit(solution)/shard_map/ppermute | solution.py:555
  151.7 2.0 %collective-permute-done.34.refs_1_ = bf16[128,512]{1,0:T(8,128)(2,1)S(1)} collective-permute-done((bf16[128,512]{1,0:T(8,128)(2,1)S(1)}, bf16[128,512]{1,0:T(8,128)(2,1)S(1)}, u32[]{:S(2)}, u32[]{:S(2)}) %collective-permute-start.34) | collective-permute-done | bytes 131104 | tf_op jit(solution)/shard_map/ppermute | solution.py:555
  153.7 5.6 %collective-permute-done.35.refs_2_ = bf16[128,512]{1,0:T(8,128)(2,1)S(1)} collective-permute-done((bf16[128,512]{1,0:T(8,128)(2,1)S(1)}, bf16[128,512]{1,0:T(8,128)(2,1)S(1)}, u32[]{:S(2)}, u32[]{:S(2)}) %collective-permute-start.35) | collective-permute-done | bytes 131104 | tf_op jit(solution)/shard_map/ppermute | solution.py:555
  159.3 6.8 %collective-permute-start.32 = (bf16[128,512]{1,0:T(8,128)(2,1)S(1)}, bf16[128,512]{1,0:T(8,128)(2,1)S(1)}, u32[]{:S(2)}, u32[]{:S(2)}) collective-permute-start(bf16[128,512]{1,0:T(8,128)(2,1)S(1)} %get-tuple-element.124), channel_id=1, source_target_pairs={{0,12},{4,0},{8,4},{12,8},{1,13},{5,1},{9,5},{13,9},{2,14},{6,2},{... | collective-permute-start | bytes 393224 | tf_op jit(solution)/shard_map/ppermute | solution.py:555
  166.1 0.8 value_sum.1
  166.9 1.8 %input_own.1.refs_1_ = bf16[1024,512]{1,0:T(8,128)(2,1)S(1)} custom-call(s32[4]{0:T(128)S(1)} %pad_add_fusion.refs_0_, bf16[1024,512]{1,0:T(8,128)(2,1)S(1)} %get-tuple-element.116.refs_2_.refs_1_, bf16[1024,512]{1,0:T(8,128)(2,1)S(1)} %get-tuple-element.117.refs_2_, bf16[1024,512]{1,0:T(8,128)(2,1)S(1)} %copy-done, bf16[1024,512]{1,0:T(8,128)(2,1)S(1)} %copy-done.3, ...), custom_call_target="tpu_custom_call" | custom-call | flops 1073741824 | bytes 5242896 | tf_op jit(solution)/shard_map/input_own/pallas_call | solution.py:527
  168.7 0.9 collective-permute-done.31.refs_2_
  169.6 0.8 query_sum.1
  170.4 2.3 %input_sum.1 = bf16[1024,512]{1,0:T(8,128)(2,1)} custom-call(bf16[1024,1024]{1,0:T(8,128)(2,1)S(1)} %get-tuple-element.72.refs_9_.refs_0_, bf16[1024,512]{1,0:T(8,128)(2,1)S(1)} %input_own.1.refs_1_, bf16[1024,512]{1,0:T(8,128)(2,1)S(1)} %collective-permute-done.29.refs_2_), custom_call_target="tpu_custom_call" | custom-call | flops 1073741824 | bytes 5242880 | tf_op jit(solution)/shard_map/input_sum/pallas_call | solution.py:527
  (57 shorter events, 3.3 us)
Async XLA Ops:
  0.6 9.8 %copy-start = (bf16[1024,512]{1,0:T(8,128)(2,1)S(1)}, bf16[1024,512]{1,0:T(8,128)(2,1)}, u32[]{:S(2)}) copy-start(bf16[1024,512]{1,0:T(8,128)(2,1)} %refs_3_.7) | copy-start | bytes 3145732
  0.6 9.8 %copy-start.1 = (bf16[1024,1024]{1,0:T(8,128)(2,1)S(1)}, bf16[1024,1024]{1,0:T(8,128)(2,1)}, u32[]{:S(2)}) copy-start(bf16[1024,1024]{1,0:T(8,128)(2,1)} %refs_2_.4) | copy-start | bytes 6291460
  0.7 9.8 %copy-start.4 = (s32[1024,1]{0,1:T(1,128)S(1)}, s32[1024,1]{0,1:T(1,128)}, u32[]{:S(2)}) copy-start(s32[1024,1]{0,1:T(1,128)} %param.9) | copy-start | bytes 12292
  6.2 23.9 %collective-permute-start = (bf16[1040,128]{1,0:T(8,128)(2,1)}, bf16[1040,128]{1,0:T(8,128)(2,1)S(1)}, u32[]{:S(2)}, u32[]{:S(2)}) collective-permute-start(bf16[1040,128]{1,0:T(8,128)(2,1)} %get-tuple-element.75), channel_id=1, source_target_pairs={{0,8},{8,0},{9,1},{4,12},{5,13},{12,4},{13,5},{1,9},{2,10},{10,2},... | collective-permute-start | bytes 798728 | tf_op jit(solution)/shard_map/ppermute | solution.py:549
  10.3 28.8 %collective-permute-start.1 = (bf16[1040,128]{1,0:T(8,128)(2,1)}, bf16[1040,128]{1,0:T(8,128)(2,1)}, u32[]{:S(2)}, u32[]{:S(2)}) collective-permute-start(bf16[1040,128]{1,0:T(8,128)(2,1)} %get-tuple-element.76), channel_id=1, source_target_pairs={{0,9},{8,1},{9,0},{4,13},{5,12},{12,5},{13,4},{1,8},{2,11},{10,3},... | collective-permute-start | bytes 798728 | tf_op jit(solution)/shard_map/ppermute | solution.py:549
  10.4 1.2 copy-start.2
  11.7 0.7 copy-start.5
  12.3 34.1 %copy-start.3 = (bf16[1024,512]{1,0:T(8,128)(2,1)S(1)}, bf16[1024,512]{1,0:T(8,128)(2,1)}, u32[]{:S(2)}) copy-start(bf16[1024,512]{1,0:T(8,128)(2,1)} %refs_4_.3) | copy-start | bytes 3145732
  17.2 35.3 %collective-permute-start.5 = (bf16[1040,128]{1,0:T(8,128)(2,1)S(1)}, bf16[1040,128]{1,0:T(8,128)(2,1)S(1)}, u32[]{:S(2)}, u32[]{:S(2)}) collective-permute-start(bf16[1040,128]{1,0:T(8,128)(2,1)S(1)} %get-tuple-element.79), channel_id=1, source_target_pairs={{0,13},{8,5},{9,4},{4,1},{5,0},{12,9},{13,8},{1,12},{2,15},{10,7},... | collective-permute-start | bytes 798728 | tf_op jit(solution)/shard_map/ppermute | solution.py:549
  20.9 31.7 %collective-permute-start.6 = (bf16[1040,128]{1,0:T(8,128)(2,1)S(1)}, bf16[1040,128]{1,0:T(8,128)(2,1)S(1)}, u32[]{:S(2)}, u32[]{:S(2)}) collective-permute-start(bf16[1040,128]{1,0:T(8,128)(2,1)S(1)} %get-tuple-element.80), channel_id=1, source_target_pairs={{0,1},{8,9},{9,8},{4,5},{5,4},{12,13},{13,12},{1,0},{2,3},{10,11},... | collective-permute-start | bytes 798728 | tf_op jit(solution)/shard_map/ppermute | solution.py:549
  20.9 34.5 %collective-permute-start.3 = (bf16[1040,128]{1,0:T(8,128)(2,1)S(1)}, bf16[1040,128]{1,0:T(8,128)(2,1)S(1)}, u32[]{:S(2)}, u32[]{:S(2)}) collective-permute-start(bf16[1040,128]{1,0:T(8,128)(2,1)S(1)} %get-tuple-element.77), channel_id=1, source_target_pairs={{0,5},{8,13},{9,12},{4,9},{5,8},{12,1},{13,0},{1,4},{2,7},{10,15},... | collective-permute-start | bytes 798728 | tf_op jit(solution)/shard_map/ppermute | solution.py:549
  30.2 25.2 %collective-permute-start.4 = (bf16[1040,128]{1,0:T(8,128)(2,1)S(1)}, bf16[1040,128]{1,0:T(8,128)(2,1)S(1)}, u32[]{:S(2)}, u32[]{:S(2)}) collective-permute-start(bf16[1040,128]{1,0:T(8,128)(2,1)S(1)} %get-tuple-element.78), channel_id=1, source_target_pairs={{0,12},{8,4},{9,5},{4,0},{5,1},{12,8},{13,9},{1,13},{2,14},{10,6},... | collective-permute-start | bytes 798728 | tf_op jit(solution)/shard_map/ppermute | solution.py:549
  39.1 16.7 %collective-permute-start.2 = (bf16[1040,128]{1,0:T(8,128)(2,1)S(1)}, bf16[1040,128]{1,0:T(8,128)(2,1)S(1)}, u32[]{:S(2)}, u32[]{:S(2)}) collective-permute-start(bf16[1040,128]{1,0:T(8,128)(2,1)S(1)} %get-tuple-element.71.refs_4_), channel_id=1, source_target_pairs={{0,4},{8,12},{9,13},{4,8},{5,9},{12,0},{13,1},{1,5},{2,6},{10,14},... | collective-permute-start | bytes 798728 | tf_op jit(solution)/shard_map/ppermute | solution.py:549
  52.5 29.6 %copy-start.6 = (bf16[1024,1024]{1,0:T(8,128)(2,1)}, bf16[1024,1024]{1,0:T(8,128)(2,1)S(1)}, u32[]{:S(2)}) copy-start(bf16[1024,1024]{1,0:T(8,128)(2,1)S(1)} %get-tuple-element.73.refs_1_) | copy-start | bytes 6291460
  52.5 12.9 %collective-permute-start.20 = (bf16[512,128]{1,0:T(8,128)(2,1)S(1)}, bf16[512,128]{1,0:T(8,128)(2,1)S(1)}, u32[]{:S(2)}, u32[]{:S(2)}) collective-permute-start(bf16[512,128]{1,0:T(8,128)(2,1)S(1)} %get-tuple-element.107), channel_id=1, source_target_pairs={{0,1},{8,9},{9,8},{4,5},{5,4},{12,13},{13,12},{1,0},{2,3},{10,11},... | collective-permute-start | bytes 393224 | tf_op jit(solution)/shard_map/ppermute | solution.py:549
  52.6 14.4 %collective-permute-start.19 = (bf16[512,128]{1,0:T(8,128)(2,1)S(1)}, bf16[512,128]{1,0:T(8,128)(2,1)S(1)}, u32[]{:S(2)}, u32[]{:S(2)}) collective-permute-start(bf16[512,128]{1,0:T(8,128)(2,1)S(1)} %get-tuple-element.105), channel_id=1, source_target_pairs={{0,13},{8,5},{9,4},{4,1},{5,0},{12,9},{13,8},{1,12},{2,15},{10,7},... | collective-permute-start | bytes 393224 | tf_op jit(solution)/shard_map/ppermute | solution.py:549
  55.9 26.2 %collective-permute-start.18 = (bf16[512,128]{1,0:T(8,128)(2,1)S(1)}, bf16[512,128]{1,0:T(8,128)(2,1)S(1)}, u32[]{:S(2)}, u32[]{:S(2)}) collective-permute-start(bf16[512,128]{1,0:T(8,128)(2,1)S(1)} %get-tuple-element.103), channel_id=1, source_target_pairs={{0,12},{8,4},{9,5},{4,0},{5,1},{12,8},{13,9},{1,13},{2,14},{10,6},... | collective-permute-start | bytes 393224 | tf_op jit(solution)/shard_map/ppermute | solution.py:549
  58.5 25.3 %collective-permute-start.17 = (bf16[512,128]{1,0:T(8,128)(2,1)S(1)}, bf16[512,128]{1,0:T(8,128)(2,1)S(1)}, u32[]{:S(2)}, u32[]{:S(2)}) collective-permute-start(bf16[512,128]{1,0:T(8,128)(2,1)S(1)} %get-tuple-element.101), channel_id=1, source_target_pairs={{0,5},{8,13},{9,12},{4,9},{5,8},{12,1},{13,0},{1,4},{2,7},{10,15},... | collective-permute-start | bytes 393224 | tf_op jit(solution)/shard_map/ppermute | solution.py:549
  58.5 25.9 %collective-permute-start.16 = (bf16[512,128]{1,0:T(8,128)(2,1)S(1)}, bf16[512,128]{1,0:T(8,128)(2,1)S(1)}, u32[]{:S(2)}, u32[]{:S(2)}) collective-permute-start(bf16[512,128]{1,0:T(8,128)(2,1)S(1)} %get-tuple-element.99), channel_id=1, source_target_pairs={{0,4},{8,12},{9,13},{4,8},{5,9},{12,0},{13,1},{1,5},{2,6},{10,14},... | collective-permute-start | bytes 393224 | tf_op jit(solution)/shard_map/ppermute | solution.py:549
  65.4 20.7 %collective-permute-start.15 = (bf16[512,128]{1,0:T(8,128)(2,1)S(1)}, bf16[512,128]{1,0:T(8,128)(2,1)S(1)}, u32[]{:S(2)}, u32[]{:S(2)}) collective-permute-start(bf16[512,128]{1,0:T(8,128)(2,1)S(1)} %get-tuple-element.97), channel_id=1, source_target_pairs={{0,9},{8,1},{9,0},{4,13},{5,12},{12,5},{13,4},{1,8},{2,11},{10,3},... | collective-permute-start | bytes 393224 | tf_op jit(solution)/shard_map/ppermute | solution.py:549
  66.9 19.9 %collective-permute-start.14 = (bf16[512,128]{1,0:T(8,128)(2,1)S(1)}, bf16[512,128]{1,0:T(8,128)(2,1)S(1)}, u32[]{:S(2)}, u32[]{:S(2)}) collective-permute-start(bf16[512,128]{1,0:T(8,128)(2,1)S(1)} %get-tuple-element.95), channel_id=1, source_target_pairs={{0,8},{8,0},{9,1},{4,12},{5,13},{12,4},{13,5},{1,9},{2,10},{10,2},... | collective-permute-start | bytes 393224 | tf_op jit(solution)/shard_map/ppermute | solution.py:549
  82.1 23.5 %collective-permute-start.7 = (bf16[512,128]{1,0:T(8,128)(2,1)S(1)}, bf16[512,128]{1,0:T(8,128)(2,1)S(1)}, u32[]{:S(2)}, u32[]{:S(2)}) collective-permute-start(bf16[512,128]{1,0:T(8,128)(2,1)S(1)} %get-tuple-element.82), channel_id=1, source_target_pairs={{0,8},{8,0},{9,1},{4,12},{5,13},{12,4},{13,5},{1,9},{2,10},{10,2},... | collective-permute-start | bytes 393224 | tf_op jit(solution)/shard_map/ppermute | solution.py:549
  83.8 22.1 %collective-permute-start.8 = (bf16[512,128]{1,0:T(8,128)(2,1)S(1)}, bf16[512,128]{1,0:T(8,128)(2,1)S(1)}, u32[]{:S(2)}, u32[]{:S(2)}) collective-permute-start(bf16[512,128]{1,0:T(8,128)(2,1)S(1)} %get-tuple-element.83), channel_id=1, source_target_pairs={{0,9},{8,1},{9,0},{4,13},{5,12},{12,5},{13,4},{1,8},{2,11},{10,3},... | collective-permute-start | bytes 393224 | tf_op jit(solution)/shard_map/ppermute | solution.py:549
  84.3 24.6 %collective-permute-start.9 = (bf16[512,128]{1,0:T(8,128)(2,1)S(1)}, bf16[512,128]{1,0:T(8,128)(2,1)S(1)}, u32[]{:S(2)}, u32[]{:S(2)}) collective-permute-start(bf16[512,128]{1,0:T(8,128)(2,1)S(1)} %get-tuple-element.84), channel_id=1, source_target_pairs={{0,4},{8,12},{9,13},{4,8},{5,9},{12,0},{13,1},{1,5},{2,6},{10,14},... | collective-permute-start | bytes 393224 | tf_op jit(solution)/shard_map/ppermute | solution.py:549
  86.1 23.6 %collective-permute-start.10 = (bf16[512,128]{1,0:T(8,128)(2,1)S(1)}, bf16[512,128]{1,0:T(8,128)(2,1)S(1)}, u32[]{:S(2)}, u32[]{:S(2)}) collective-permute-start(bf16[512,128]{1,0:T(8,128)(2,1)S(1)} %get-tuple-element.85), channel_id=1, source_target_pairs={{0,5},{8,13},{9,12},{4,9},{5,8},{12,1},{13,0},{1,4},{2,7},{10,15},... | collective-permute-start | bytes 393224 | tf_op jit(solution)/shard_map/ppermute | solution.py:549
  86.8 42.9 %copy-start.7 = (bf16[1024,1024]{1,0:T(8,128)(2,1)S(1)}, bf16[1024,1024]{1,0:T(8,128)(2,1)}, u32[]{:S(2)}) copy-start(bf16[1024,1024]{1,0:T(8,128)(2,1)} %copy-done.6) | copy-start | bytes 6291460
  103.4 24.7 %collective-permute-start.21 = (bf16[544,128]{1,0:T(8,128)(2,1)S(1)}, bf16[544,128]{1,0:T(8,128)(2,1)S(1)}, u32[]{:S(2)}, u32[]{:S(2)}) collective-permute-start(bf16[544,128]{1,0:T(8,128)(2,1)S(1)} %get-tuple-element.109), channel_id=1, source_target_pairs={{0,8},{8,0},{9,1},{4,12},{5,13},{12,4},{13,5},{1,9},{2,10},{10,2},... | collective-permute-start | bytes 417800 | tf_op jit(solution)/shard_map/ppermute | solution.py:549
  105.5 24.1 %collective-permute-start.22 = (bf16[544,128]{1,0:T(8,128)(2,1)S(1)}, bf16[544,128]{1,0:T(8,128)(2,1)S(1)}, u32[]{:S(2)}, u32[]{:S(2)}) collective-permute-start(bf16[544,128]{1,0:T(8,128)(2,1)S(1)} %get-tuple-element.110), channel_id=1, source_target_pairs={{0,9},{8,1},{9,0},{4,13},{5,12},{12,5},{13,4},{1,8},{2,11},{10,3},... | collective-permute-start | bytes 417800 | tf_op jit(solution)/shard_map/ppermute | solution.py:549
  105.9 9.5 %collective-permute-start.11 = (bf16[512,128]{1,0:T(8,128)(2,1)S(1)}, bf16[512,128]{1,0:T(8,128)(2,1)S(1)}, u32[]{:S(2)}, u32[]{:S(2)}) collective-permute-start(bf16[512,128]{1,0:T(8,128)(2,1)S(1)} %get-tuple-element.86), channel_id=1, source_target_pairs={{0,12},{8,4},{9,5},{4,0},{5,1},{12,8},{13,9},{1,13},{2,14},{10,6},... | collective-permute-start | bytes 393224 | tf_op jit(solution)/shard_map/ppermute | solution.py:549
  109.0 17.0 %collective-permute-start.12 = (bf16[512,128]{1,0:T(8,128)(2,1)S(1)}, bf16[512,128]{1,0:T(8,128)(2,1)S(1)}, u32[]{:S(2)}, u32[]{:S(2)}) collective-permute-start(bf16[512,128]{1,0:T(8,128)(2,1)S(1)} %get-tuple-element.87), channel_id=1, source_target_pairs={{0,13},{8,5},{9,4},{4,1},{5,0},{12,9},{13,8},{1,12},{2,15},{10,7},... | collective-permute-start | bytes 393224 | tf_op jit(solution)/shard_map/ppermute | solution.py:549
  109.7 18.0 %collective-permute-start.13 = (bf16[512,128]{1,0:T(8,128)(2,1)S(1)}, bf16[512,128]{1,0:T(8,128)(2,1)S(1)}, u32[]{:S(2)}, u32[]{:S(2)}) collective-permute-start(bf16[512,128]{1,0:T(8,128)(2,1)S(1)} %get-tuple-element.88), channel_id=1, source_target_pairs={{0,1},{8,9},{9,8},{4,5},{5,4},{12,13},{13,12},{1,0},{2,3},{10,11},... | collective-permute-start | bytes 393224 | tf_op jit(solution)/shard_map/ppermute | solution.py:549
  115.4 17.2 %collective-permute-start.23 = (bf16[544,128]{1,0:T(8,128)(2,1)S(1)}, bf16[544,128]{1,0:T(8,128)(2,1)S(1)}, u32[]{:S(2)}, u32[]{:S(2)}) collective-permute-start(bf16[544,128]{1,0:T(8,128)(2,1)S(1)} %get-tuple-element.111), channel_id=1, source_target_pairs={{0,4},{8,12},{9,13},{4,8},{5,9},{12,0},{13,1},{1,5},{2,6},{10,14},... | collective-permute-start | bytes 417800 | tf_op jit(solution)/shard_map/ppermute | solution.py:549
  126.0 7.8 %collective-permute-start.24 = (bf16[544,128]{1,0:T(8,128)(2,1)S(1)}, bf16[544,128]{1,0:T(8,128)(2,1)S(1)}, u32[]{:S(2)}, u32[]{:S(2)}) collective-permute-start(bf16[544,128]{1,0:T(8,128)(2,1)S(1)} %get-tuple-element.112), channel_id=1, source_target_pairs={{0,5},{8,13},{9,12},{4,9},{5,8},{12,1},{13,0},{1,4},{2,7},{10,15},... | collective-permute-start | bytes 417800 | tf_op jit(solution)/shard_map/ppermute | solution.py:549
  127.7 8.1 %collective-permute-start.25 = (bf16[544,128]{1,0:T(8,128)(2,1)S(1)}, bf16[544,128]{1,0:T(8,128)(2,1)S(1)}, u32[]{:S(2)}, u32[]{:S(2)}) collective-permute-start(bf16[544,128]{1,0:T(8,128)(2,1)S(1)} %get-tuple-element.113), channel_id=1, source_target_pairs={{0,12},{8,4},{9,5},{4,0},{5,1},{12,8},{13,9},{1,13},{2,14},{10,6},... | collective-permute-start | bytes 417800 | tf_op jit(solution)/shard_map/ppermute | solution.py:549
  128.2 10.4 %collective-permute-start.26 = (bf16[544,128]{1,0:T(8,128)(2,1)S(1)}, bf16[544,128]{1,0:T(8,128)(2,1)S(1)}, u32[]{:S(2)}, u32[]{:S(2)}) collective-permute-start(bf16[544,128]{1,0:T(8,128)(2,1)S(1)} %get-tuple-element.114), channel_id=1, source_target_pairs={{0,13},{8,5},{9,4},{4,1},{5,0},{12,9},{13,8},{1,12},{2,15},{10,7},... | collective-permute-start | bytes 417800 | tf_op jit(solution)/shard_map/ppermute | solution.py:549
  129.6 9.0 %collective-permute-start.27 = (bf16[544,128]{1,0:T(8,128)(2,1)S(1)}, bf16[544,128]{1,0:T(8,128)(2,1)S(1)}, u32[]{:S(2)}, u32[]{:S(2)}) collective-permute-start(bf16[544,128]{1,0:T(8,128)(2,1)S(1)} %get-tuple-element.115), channel_id=1, source_target_pairs={{0,1},{8,9},{9,8},{4,5},{5,4},{12,13},{13,12},{1,0},{2,3},{10,11},... | collective-permute-start | bytes 417800 | tf_op jit(solution)/shard_map/ppermute | solution.py:549
  140.6 29.8 %collective-permute-start.29 = (bf16[1024,512]{1,0:T(8,128)(2,1)S(1)}, bf16[1024,512]{1,0:T(8,128)(2,1)S(1)}, u32[]{:S(2)}, u32[]{:S(2)}) collective-permute-start(bf16[1024,512]{1,0:T(8,128)(2,1)S(1)} %get-tuple-element.121), channel_id=1, source_target_pairs={{0,2},{2,0},{1,3},{3,1},{4,6},{6,4},{5,7},{7,5},{8,10},{10,8},{9,1... | collective-permute-start | bytes 3145736 | tf_op jit(solution)/shard_map/ppermute | solution.py:555
  142.1 2.6 %collective-permute-start.33 = (bf16[4,128,512]{2,1,0:T(8,128)(2,1)S(1)}, bf16[4,128,512]{2,1,0:T(8,128)(2,1)S(1)}, u32[]{:S(2)}, u32[]{:S(2)}) collective-permute-start(bf16[4,128,512]{2,1,0:T(8,128)(2,1)S(1)} %get-tuple-element.126), channel_id=1, source_target_pairs={{0,1},{1,0},{2,3},{3,2},{4,5},{5,4},{6,7},{7,6},{8,9},{9,8},{10,11... | collective-permute-start | bytes 1572872 | tf_op jit(solution)/shard_map/ppermute | solution.py:555
  144.1 5.1 %collective-permute-start.28 = (bf16[4,128,512]{2,1,0:T(8,128)(2,1)S(1)}, bf16[4,128,512]{2,1,0:T(8,128)(2,1)S(1)}, u32[]{:S(2)}, u32[]{:S(2)}) collective-permute-start(bf16[4,128,512]{2,1,0:T(8,128)(2,1)S(1)} %get-tuple-element.119), channel_id=1, source_target_pairs={{0,1},{1,0},{2,3},{3,2},{4,5},{5,4},{6,7},{7,6},{8,9},{9,8},{10,11... | collective-permute-start | bytes 1572872 | tf_op jit(solution)/shard_map/ppermute | solution.py:555
  145.4 8.3 %collective-permute-start.34 = (bf16[128,512]{1,0:T(8,128)(2,1)S(1)}, bf16[128,512]{1,0:T(8,128)(2,1)S(1)}, u32[]{:S(2)}, u32[]{:S(2)}) collective-permute-start(bf16[128,512]{1,0:T(8,128)(2,1)S(1)} %get-tuple-element.132), channel_id=1, source_target_pairs={{0,4},{4,8},{8,12},{12,0},{1,5},{5,9},{9,13},{13,1},{2,6},{6,10},{... | collective-permute-start | bytes 393224 | tf_op jit(solution)/shard_map/ppermute | solution.py:555
  146.1 13.3 %collective-permute-start.35 = (bf16[128,512]{1,0:T(8,128)(2,1)S(1)}, bf16[128,512]{1,0:T(8,128)(2,1)S(1)}, u32[]{:S(2)}, u32[]{:S(2)}) collective-permute-start(bf16[128,512]{1,0:T(8,128)(2,1)S(1)} %get-tuple-element.133), channel_id=1, source_target_pairs={{0,8},{4,12},{8,0},{12,4},{1,9},{5,13},{9,1},{13,5},{2,10},{6,14},... | collective-permute-start | bytes 393224 | tf_op jit(solution)/shard_map/ppermute | solution.py:555
  148.9 17.2 %collective-permute-start.36 = (bf16[128,512]{1,0:T(8,128)(2,1)S(1)}, bf16[128,512]{1,0:T(8,128)(2,1)S(1)}, u32[]{:S(2)}, u32[]{:S(2)}) collective-permute-start(bf16[128,512]{1,0:T(8,128)(2,1)S(1)} %get-tuple-element.134), channel_id=1, source_target_pairs={{0,12},{4,0},{8,4},{12,8},{1,13},{5,1},{9,5},{13,9},{2,14},{6,2},{... | collective-permute-start | bytes 393224 | tf_op jit(solution)/shard_map/ppermute | solution.py:555
  149.9 18.7 %collective-permute-start.30 = (bf16[128,512]{1,0:T(8,128)(2,1)S(1)}, bf16[128,512]{1,0:T(8,128)(2,1)S(1)}, u32[]{:S(2)}, u32[]{:S(2)}) collective-permute-start(bf16[128,512]{1,0:T(8,128)(2,1)S(1)} %get-tuple-element.122), channel_id=1, source_target_pairs={{0,4},{4,8},{8,12},{12,0},{1,5},{5,9},{9,13},{13,1},{2,6},{6,10},{... | collective-permute-start | bytes 393224 | tf_op jit(solution)/shard_map/ppermute | solution.py:555
  153.7 15.9 %collective-permute-start.31 = (bf16[128,512]{1,0:T(8,128)(2,1)S(1)}, bf16[128,512]{1,0:T(8,128)(2,1)S(1)}, u32[]{:S(2)}, u32[]{:S(2)}) collective-permute-start(bf16[128,512]{1,0:T(8,128)(2,1)S(1)} %get-tuple-element.123), channel_id=1, source_target_pairs={{0,8},{4,12},{8,0},{12,4},{1,9},{5,13},{9,1},{13,5},{2,10},{6,14},... | collective-permute-start | bytes 393224 | tf_op jit(solution)/shard_map/ppermute | solution.py:555
  159.3 10.3 %collective-permute-start.32 = (bf16[128,512]{1,0:T(8,128)(2,1)S(1)}, bf16[128,512]{1,0:T(8,128)(2,1)S(1)}, u32[]{:S(2)}, u32[]{:S(2)}) collective-permute-start(bf16[128,512]{1,0:T(8,128)(2,1)S(1)} %get-tuple-element.124), channel_id=1, source_target_pairs={{0,12},{4,0},{8,4},{12,8},{1,13},{5,1},{9,5},{13,9},{2,14},{6,2},{... | collective-permute-start | bytes 393224 | tf_op jit(solution)/shard_map/ppermute | solution.py:555

commit v13 on v12

--- a/solution.py
+++ b/solution.py
@@ -429,21 +429,15 @@
     unfold(home_ref, rows_ref, heads, 0, rows_ref.shape[0] * heads // home_ref.shape[0] // 2, to_half)
 
 
-def weight_partial(sizes, me_ref, turned_ref, rows_ref, whole_ref, sub_refs):
-    width = turned_ref.shape[0]
-    step = min(512, width)
-
-    @pl.loop(0, width // step)
-    def _(i):
-        where = pl.ds(pl.multiple_of(i * step, step), step)
-        whole_ref[where, :] = dot(turned_ref[where, :], rows_ref[...]).astype(BF16)
-
-    piece = width // (sizes[0] * sizes[1])
+def weight_partial(sizes, me_ref, turned_ref, rows_ref, sub_refs):
+    piece = turned_ref.shape[0] // (sizes[0] * sizes[1])
     for ahead, sub_ref in enumerate(sub_refs):
         sub = lax.rem(me_ref[1] + ahead, jnp.int32(sizes[1]))
+        first = [pl.multiple_of((seq * sizes[1] + sub) * piece, piece) for seq in range(sizes[0])]
+        turned = jnp.concatenate([turned_ref[pl.ds(row, piece), :] for row in first], axis=0)
+        partial = dot(turned, rows_ref[...]).astype(BF16)
         for seq in range(sizes[0]):
-            first = pl.multiple_of((seq * sizes[1] + sub) * piece, piece)
-            sub_ref[seq] = whole_ref[pl.ds(first, piece), :]
+            sub_ref[seq] = partial[seq * piece : (seq + 1) * piece, :]
 
 
 def input_columns(me_ref, ahead, parts, width):
@@ -455,12 +449,12 @@
 def value_home_kernel(sizes, heads, parts, me_ref, turned_ref, weight_ref, *refs):
     part_refs, refs = refs[: sizes[0] * sizes[1]], refs[sizes[0] * sizes[1] :]
     rows_ref, term_refs, refs = refs[0], refs[1:parts], refs[parts:]
-    sub_refs, (home_ref, whole_ref) = refs[: sizes[1]], refs[sizes[1] :]
+    sub_refs, home_ref = refs[: sizes[1]], refs[sizes[1]]
     bring_home(sizes, heads, me_ref, part_refs, home_ref, rows_ref)
     for k, term_ref in enumerate(term_refs):
         mine = input_columns(me_ref, k + 1, parts, weight_ref.shape[0])
         term_ref[...] = dot_nt(rows_ref[...], weight_ref[mine, :])
-    weight_partial(sizes, me_ref, turned_ref, rows_ref, whole_ref, sub_refs)
+    weight_partial(sizes, me_ref, turned_ref, rows_ref, sub_refs)
 
 
 def query_home_kernel(sizes, heads, factor, parts, me_ref, weight_ref, *refs):
@@ -475,8 +469,8 @@
     unfold(home_ref, centroid_ref, heads, half, home_ref.shape[1] - half, lambda x: x * factor)
 
 
-def query_weight_kernel(sizes, me_ref, turned_ref, rows_ref, *refs):
-    weight_partial(sizes, me_ref, turned_ref, rows_ref, refs[-1], refs[:-1])
+def query_weight_kernel(sizes, me_ref, turned_ref, rows_ref, *sub_refs):
+    weight_partial(sizes, me_ref, turned_ref, rows_ref, sub_refs)
 
 
 def input_own_kernel(parts, me_ref, rows_ref, value_rows_ref, w_query_ref, w_value_ref, out_ref):
@@ -569,8 +563,9 @@
     )
 
 
-def add_up(terms, dtype, name):
-    return call(sum_kernel, jax.ShapeDtypeStruct(terms[0].shape, dtype), tuple(terms), smem=(), name=name)
+def add_up(terms, dtype, name, after=()):
+    out = jax.ShapeDtypeStruct(terms[0].shape, dtype)
+    return call(sum_kernel, out, tuple(terms), smem=(), after=after, name=name)
 
 
 def on_device(tokens_in, w_query, w_value, cotangent, assignment):
@@ -635,8 +630,8 @@
         flops=2 * toks * width * width_dev + 2 * slots * toks * width_dev,
         name="project_value",
     )
-    behind = [got_mixed[owners - k if k else 0] for k in range(owners)]
-    send_value = [lax.optimization_barrier(pair)[0] for pair in zip(send_value, behind)]
+    behind = [0, *range(3, owners), 2, 1][:owners]
+    send_value = [lax.optimization_barrier((part, got_mixed[k]))[0] for part, k in zip(send_value, behind)]
     got_value = exchange(send_value, sizes)
     blocks = per_group * capacity // BLOCK_ROWS
     held = blocks + (LEAD + 4) * UNROLL
@@ -677,12 +672,11 @@
     weight_flops = 2 * slots * width * width_dev
     home_flops = weight_flops // parts * (parts - 1)
     sub_shapes = several(sizes[1], sizes[0], width // owners, width_dev)
-    whole = pltpu.VMEM((width, width_dev), BF16)
     value_rows, *refs = call(
         functools.partial(value_home_kernel, sizes, heads, parts),
         several(1, slots, width_dev) + (shape((slots, columns), F32),) * (parts - 1) + sub_shapes,
         (me, turned, w_value, *home_value),
-        scratch=[pltpu.VMEM((owners, half, LANES), BF16), whole],
+        scratch=[pltpu.VMEM((owners, half, LANES), BF16)],
         flops=weight_flops + home_flops,
         name="value_home",
     )
@@ -705,7 +699,6 @@
         functools.partial(query_weight_kernel, sizes),
         sub_shapes,
         (me, turned, query_rows),
-        scratch=[whole],
         flops=weight_flops,
         name="query_weight",
     )
@@ -719,8 +712,7 @@
         name="input_own",
     )
     query_weight = pass_round(query_weight, "seq")
-    grad_wv = add_up(value_weight, F32, "value_sum")
-    grad_wq = add_up(query_weight, F32, "query_sum")
+    grad_wv = add_up(value_weight, F32, "value_sum", [own])
     grad_input = call(
         input_sum_kernel,
         shape((toks, columns), BF16),
@@ -730,6 +722,7 @@
         flops=2 * toks * slots * columns,
         name="input_sum",
     )
+    grad_wq = add_up(query_weight, F32, "query_sum", [grad_input])
     if groups > 1:
         centroid_grad = centroid_grad.reshape(groups, 2 * extra, width_dev)[:, :per_group]
         centroid_grad = centroid_grad.reshape(CLUSTERS, width_dev)

time: 173 us -> 172 us (level)
  starting transfers between devices: 77.7 us -> 49.1 us
  waiting for transfers between devices: 31.3 us -> 59 us
    ppermute x28, waiting for transfers between devices: 22.7 us -> 47.7 us  [exchange(): out.append(part if ahead == (0, 0) else lax.ppermute(part, OWNERS, moves))]
    ppermute x28, starting transfers between devices: 63.3 us -> 39.7 us  [exchange(): out.append(part if ahead == (0, 0) else lax.ppermute(part, OWNERS, moves))]
    ppermute x9, starting transfers between devices: 14.4 us -> 9.43 us  [shift(): lax.ppermute(part, axis, [(i, (i + ahead) % size) for i in range(size)])]
    ppermute x9, waiting for transfers between devices: 8.55 us -> 11.4 us  [shift(): lax.ppermute(part, axis, [(i, (i + ahead) % size) for i in range(size)])]
    pallas_call x14, Pallas kernels: 60.8 us -> 59.1 us  [call(): pl.pallas_call(body, out_shape=outs, in_specs=specs, out_specs=jax.tree.m...]
  transfers between devices with their start and end apart: 37 -> 37, of which waited for: 10 -> 12; matrix products, arithmetic and copies ran while one was open for 0% -> 0% of each run, Pallas kernels for 30% -> 30%
where the time goes in v13:
time: 172 us; the launch traced here: 171 us
  Pallas kernels  59.1 us (34%)
  waiting for transfers between devices  59 us (34%)
  starting transfers between devices  49.1 us (29%)
  local copies, waits for them, and re-layouts  3.16 us (2%)
    pallas_call x14, Pallas kernels, call(): pl.pallas_call(body, out_shape=outs, in_specs=specs, out_specs=jax.tree.m...  59.1 us
    ppermute x28, waiting for transfers between devices, exchange(): out.append(part if ahead == (0, 0) else lax.ppermute(part, OWNERS, moves))  47.7 us
    ppermute x28, starting transfers between devices, exchange(): out.append(part if ahead == (0, 0) else lax.ppermute(part, OWNERS, moves))  39.7 us
    ppermute x9, waiting for transfers between devices, shift(): lax.ppermute(part, axis, [(i, (i + ahead) % size) for i in range(size)])  11.4 us
    ppermute x9, starting transfers between devices, shift(): lax.ppermute(part, axis, [(i, (i + ahead) % size) for i in range(size)])  9.43 us
  transfers between devices with their start and end apart: 37, of which 12 were waited for; matrix products, arithmetic and copies ran while one was open for 0% of the time, Pallas kernels for 30%

profile of v13, /device:TPU:0, one launch (start us, length us, event | category | flops | bytes accessed | tf_op | source)
XLA Modules:
  0.0 171.3 jit_solution(3139933306281639431)
XLA Ops:
  0.7 5.6 %project_far.1 = (bf16[1040,128]{1,0:T(8,128)(2,1)}, bf16[1040,128]{1,0:T(8,128)(2,1)}, s32[1,1024]{1,0:T(1,128)}) custom-call(s32[1,1024]{1,0:T(1,128)} %bitcast.5, bf16[1024,1024]{1,0:T(8,128)(2,1)} %refs_2_.4, bf16[1024,512]{1,0:T(8,128)(2,1)} %refs_3_.7, bf16[1024,512]{1,0:T(8,128)(2,1)} %refs_5_.1), custom_call_target="tpu_custom_call" | custom-call | flops 805306368 | bytes 4734976 | tf_op jit(solution)/shard_map/project_far/pallas_call | solution.py:521
  6.2 4.1 %collective-permute-start = (bf16[1040,128]{1,0:T(8,128)(2,1)}, bf16[1040,128]{1,0:T(8,128)(2,1)S(1)}, u32[]{:S(2)}, u32[]{:S(2)}) collective-permute-start(bf16[1040,128]{1,0:T(8,128)(2,1)} %get-tuple-element.75), channel_id=1, source_target_pairs={{0,8},{8,0},{9,1},{4,12},{5,13},{12,4},{13,5},{1,9},{2,10},{10,2},... | collective-permute-start | bytes 798728 | tf_op jit(solution)/shard_map/ppermute | solution.py:543
  10.4 1.2 copy-done.3
  11.7 0.7 copy-done.6
  12.4 4.8 %project_query.1 = (bf16[1040,128]{1,0:T(8,128)(2,1)S(1)}, bf16[1040,128]{1,0:T(8,128)(2,1)S(1)}, bf16[1040,128]{1,0:T(8,128)(2,1)S(1)}, bf16[1040,128]{1,0:T(8,...) custom-call(s32[4]{0:T(128)S(1)} %pad_add_fusion.refs_0_, s32[1,1024]{1,0:T(1,128)S(1)} %copy-done.6, ...), custom_call_target="tpu_custom_call" | custom-call | flops 3221225472 | bytes 5799952 | tf_op jit(solution)/shard_map/project_query/pallas_call | solution.py:521
  17.2 1.7 collective-permute-start.3
  18.9 1.6 collective-permute-start.2
  20.4 2.2 %collective-permute-start.4 = (bf16[1040,128]{1,0:T(8,128)(2,1)S(1)}, bf16[1040,128]{1,0:T(8,128)(2,1)S(1)}, u32[]{:S(2)}, u32[]{:S(2)}) collective-permute-start(bf16[1040,128]{1,0:T(8,128)(2,1)S(1)} %get-tuple-element.78), channel_id=1, source_target_pairs={{0,12},{8,4},{9,5},{4,0},{5,1},{12,8},{13,9},{1,13},{2,14},{10,6},... | collective-permute-start | bytes 798728 | tf_op jit(solution)/shard_map/ppermute | solution.py:543
  22.7 18.0 %collective-permute-done.refs_2_ = bf16[1040,128]{1,0:T(8,128)(2,1)S(1)} collective-permute-done((bf16[1040,128]{1,0:T(8,128)(2,1)}, bf16[1040,128]{1,0:T(8,128)(2,1)S(1)}, u32[]{:S(2)}, u32[]{:S(2)}) %collective-permute-start) | collective-permute-done | bytes 266272 | tf_op jit(solution)/shard_map/ppermute | solution.py:543
  40.7 4.1 %collective-permute-done.1.refs_3_ = bf16[1040,128]{1,0:T(8,128)(2,1)} collective-permute-done((bf16[1040,128]{1,0:T(8,128)(2,1)}, bf16[1040,128]{1,0:T(8,128)(2,1)}, u32[]{:S(2)}, u32[]{:S(2)}) %collective-permute-start.1) | collective-permute-done | bytes 266272 | tf_op jit(solution)/shard_map/ppermute | solution.py:543
  44.8 1.4 collective-permute-start.6
  46.3 6.0 %project_value.1 = (bf16[512,128]{1,0:T(8,128)(2,1)S(1)}, bf16[512,128]{1,0:T(8,128)(2,1)S(1)}, bf16[512,128]{1,0:T(8,128)(2,1)S(1)}, bf16[512,128]{1,0:T(8,128)...) custom-call(s32[4]{0:T(128)S(1)} %pad_add_fusion.refs_0_, ...), custom_call_target="tpu_custom_call" | custom-call | flops 2147483648 | bytes 8392720 | tf_op jit(solution)/shard_map/project_value/pallas_call | solution.py:521
  52.4 3.6 %collective-permute-start.19 = (bf16[512,128]{1,0:T(8,128)(2,1)S(1)}, bf16[512,128]{1,0:T(8,128)(2,1)S(1)}, u32[]{:S(2)}, u32[]{:S(2)}) collective-permute-start(bf16[512,128]{1,0:T(8,128)(2,1)S(1)} %get-tuple-element.105), channel_id=1, source_target_pairs={{0,13},{8,5},{9,4},{4,1},{5,0},{12,9},{13,8},{1,12},{2,15},{10,7},... | collective-permute-start | bytes 393224 | tf_op jit(solution)/shard_map/ppermute | solution.py:543
  56.0 4.7 %collective-permute-start.18 = (bf16[512,128]{1,0:T(8,128)(2,1)S(1)}, bf16[512,128]{1,0:T(8,128)(2,1)S(1)}, u32[]{:S(2)}, u32[]{:S(2)}) collective-permute-start(bf16[512,128]{1,0:T(8,128)(2,1)S(1)} %get-tuple-element.103), channel_id=1, source_target_pairs={{0,12},{8,4},{9,5},{4,0},{5,1},{12,8},{13,9},{1,13},{2,14},{10,6},... | collective-permute-start | bytes 393224 | tf_op jit(solution)/shard_map/ppermute | solution.py:543
  60.7 3.8 %collective-permute-start.15 = (bf16[512,128]{1,0:T(8,128)(2,1)S(1)}, bf16[512,128]{1,0:T(8,128)(2,1)S(1)}, u32[]{:S(2)}, u32[]{:S(2)}) collective-permute-start(bf16[512,128]{1,0:T(8,128)(2,1)S(1)} %get-tuple-element.97), channel_id=1, source_target_pairs={{0,9},{8,1},{9,0},{4,13},{5,12},{12,5},{13,4},{1,8},{2,11},{10,3},... | collective-permute-start | bytes 393224 | tf_op jit(solution)/shard_map/ppermute | solution.py:543
  65.2 13.5 %value_grad.1 = (bf16[512,128]{1,0:T(8,128)(2,1)S(1)}, bf16[512,128]{1,0:T(8,128)(2,1)S(1)}, bf16[512,128]{1,0:T(8,128)(2,1)S(1)}, bf16[512,128]{1,0:T(8,128)(2,...) custom-call(s32[4]{0:T(128)S(1)} %pad_add_fusion.refs_0_, ...), custom_call_target="tpu_custom_call" | custom-call | flops 2147483648 | bytes 8163344 | tf_op jit(solution)/shard_map/value_grad/pallas_call | solution.py:521
  78.7 2.3 %collective-permute-start.7 = (bf16[512,128]{1,0:T(8,128)(2,1)S(1)}, bf16[512,128]{1,0:T(8,128)(2,1)S(1)}, u32[]{:S(2)}, u32[]{:S(2)}) collective-permute-start(bf16[512,128]{1,0:T(8,128)(2,1)S(1)} %get-tuple-element.82), channel_id=1, source_target_pairs={{0,8},{8,0},{9,1},{4,12},{5,13},{12,4},{13,5},{1,9},{2,10},{10,2},... | collective-permute-start | bytes 393224 | tf_op jit(solution)/shard_map/ppermute | solution.py:543
  81.3 2.6 %collective-permute-start.10 = (bf16[512,128]{1,0:T(8,128)(2,1)S(1)}, bf16[512,128]{1,0:T(8,128)(2,1)S(1)}, u32[]{:S(2)}, u32[]{:S(2)}) collective-permute-start(bf16[512,128]{1,0:T(8,128)(2,1)S(1)} %get-tuple-element.85), channel_id=1, source_target_pairs={{0,5},{8,13},{9,12},{4,9},{5,8},{12,1},{13,0},{1,4},{2,7},{10,15},... | collective-permute-start | bytes 393224 | tf_op jit(solution)/shard_map/ppermute | solution.py:543
  83.9 10.6 %collective-permute-done.14.refs_4_ = bf16[512,128]{1,0:T(8,128)(2,1)S(1)} collective-permute-done((bf16[512,128]{1,0:T(8,128)(2,1)S(1)}, bf16[512,128]{1,0:T(8,128)(2,1)S(1)}, u32[]{:S(2)}, u32[]{:S(2)}) %collective-permute-start.14) | collective-permute-done | bytes 131104 | tf_op jit(solution)/shard_map/ppermute | solution.py:543
  94.5 15.9 %query_grad.1 = (bf16[544,128]{1,0:T(8,128)(2,1)S(1)}, bf16[544,128]{1,0:T(8,128)(2,1)S(1)}, bf16[544,128]{1,0:T(8,128)(2,1)S(1)}, bf16[544,128]{1,0:T(8,128)(2,...) custom-call(s32[4]{0:T(128)S(1)} %pad_add_fusion.refs_0_, ...), custom_call_target="tpu_custom_call" | custom-call | flops 3221225472 | bytes 7147536 | tf_op jit(solution)/shard_map/query_grad/pallas_call | solution.py:521
  110.5 1.6 collective-permute-start.22
  112.2 2.3 %collective-permute-start.12 = (bf16[512,128]{1,0:T(8,128)(2,1)S(1)}, bf16[512,128]{1,0:T(8,128)(2,1)S(1)}, u32[]{:S(2)}, u32[]{:S(2)}) collective-permute-start(bf16[512,128]{1,0:T(8,128)(2,1)S(1)} %get-tuple-element.87), channel_id=1, source_target_pairs={{0,13},{8,5},{9,4},{4,1},{5,0},{12,9},{13,8},{1,12},{2,15},{10,7},... | collective-permute-start | bytes 393224 | tf_op jit(solution)/shard_map/ppermute | solution.py:543
  114.4 0.8 collective-permute-start.13
  115.3 6.9 %collective-permute-done.11.refs_8_ = bf16[512,128]{1,0:T(8,128)(2,1)S(1)} collective-permute-done((bf16[512,128]{1,0:T(8,128)(2,1)S(1)}, bf16[512,128]{1,0:T(8,128)(2,1)S(1)}, u32[]{:S(2)}, u32[]{:S(2)}) %collective-permute-start.11) | collective-permute-done | bytes 131104 | tf_op jit(solution)/shard_map/ppermute | solution.py:543
  122.1 2.0 %collective-permute-start.23 = (bf16[544,128]{1,0:T(8,128)(2,1)S(1)}, bf16[544,128]{1,0:T(8,128)(2,1)S(1)}, u32[]{:S(2)}, u32[]{:S(2)}) collective-permute-start(bf16[544,128]{1,0:T(8,128)(2,1)S(1)} %get-tuple-element.111), channel_id=1, source_target_pairs={{0,4},{8,12},{9,13},{4,8},{5,9},{12,0},{13,1},{1,5},{2,6},{10,14},... | collective-permute-start | bytes 417800 | tf_op jit(solution)/shard_map/ppermute | solution.py:543
  124.2 0.8 collective-permute-done.12.refs_9_
  125.0 3.5 %collective-permute-start.25 = (bf16[544,128]{1,0:T(8,128)(2,1)S(1)}, bf16[544,128]{1,0:T(8,128)(2,1)S(1)}, u32[]{:S(2)}, u32[]{:S(2)}) collective-permute-start(bf16[544,128]{1,0:T(8,128)(2,1)S(1)} %get-tuple-element.113), channel_id=1, source_target_pairs={{0,12},{8,4},{9,5},{4,0},{5,1},{12,8},{13,9},{1,13},{2,14},{10,6},... | collective-permute-start | bytes 417800 | tf_op jit(solution)/shard_map/ppermute | solution.py:543
  128.7 2.5 %value_home.1 = (bf16[1024,512]{1,0:T(8,128)(2,1)S(1)}, f32[1024,512]{1,0:T(8,128)S(1)}, bf16[4,128,512]{2,1,0:T(8,128)(2,1)S(1)}, bf16[4,128,512]{2,1,0:T(8,128)(2,1)S(1)}) custom-call(s32[4]{0:T(128)S(1)} %pad_add_fusion.refs_0_, bf16[1024,1024]{1,0:T(8,128)(2,1)S(1)} %copy-done.8, bf16[1024,512]{1,0:T(8,128)(2,1)S(1)} %copy-done.4, ...), custom_call_target="tpu_custom_call" | custom-call | flops 1610612736 | bytes 8388624 | tf_op jit(solution)/shard_map/value_home/pallas_call | solution.py:521
  131.2 1.4 collective-permute-done.24.refs_7_
  132.6 3.1 %collective-permute-done.25.refs_8_ = bf16[544,128]{1,0:T(8,128)(2,1)S(1)} collective-permute-done((bf16[544,128]{1,0:T(8,128)(2,1)S(1)}, bf16[544,128]{1,0:T(8,128)(2,1)S(1)}, u32[]{:S(2)}, u32[]{:S(2)}) %collective-permute-start.25) | collective-permute-done | bytes 139296 | tf_op jit(solution)/shard_map/ppermute | solution.py:543
  135.7 2.8 %collective-permute-done.26.refs_9_ = bf16[544,128]{1,0:T(8,128)(2,1)S(1)} collective-permute-done((bf16[544,128]{1,0:T(8,128)(2,1)S(1)}, bf16[544,128]{1,0:T(8,128)(2,1)S(1)}, u32[]{:S(2)}, u32[]{:S(2)}) %collective-permute-start.26) | collective-permute-done | bytes 139296 | tf_op jit(solution)/shard_map/ppermute | solution.py:543
  138.5 2.0 %query_home.1 = (bf16[1024,512]{1,0:T(8,128)(2,1)S(1)}, bf16[1024,512]{1,0:T(8,128)(2,1)S(1)}, f32[64,512]{1,0:T(8,128)}) custom-call(s32[4]{0:T(128)S(1)} %pad_add_fusion.refs_0_, bf16[1024,512]{1,0:T(8,128)(2,1)S(1)} %copy-done, f32[1024,512]{1,0:T(8,128)S(1)} %get-tuple-element.89.refs_2_, bf16[544,128]{1,0:T(8,128)(2,1)S(1)} %get-tuple-element.108.refs_3_, ...), custom_call_target="tpu_custom_call" | custom-call | flops 536870912 | bytes 6488080 | tf_op jit(solution)/shard_map/query_home/pallas_call | solution.py:521
  140.5 1.5 collective-permute-start.29
  142.0 1.8 %query_weight.1 = (bf16[4,128,512]{2,1,0:T(8,128)(2,1)S(1)}, bf16[4,128,512]{2,1,0:T(8,128)(2,1)S(1)}) custom-call(s32[4]{0:T(128)S(1)} %pad_add_fusion.refs_0_, bf16[1024,1024]{1,0:T(8,128)(2,1)S(1)} %copy-done.8, bf16[1024,512]{1,0:T(8,128)(2,1)S(1)} %get-tuple-element.116.refs_2_.refs_1_), custom_call_target="tpu_custom_call" | custom-call | flops 1073741824 | bytes 4194320 | tf_op jit(solution)/shard_map/query_weight/pallas_call | solution.py:521
  144.4 0.7 value_subs.1
  145.1 0.7 collective-permute-start.34
  145.8 0.8 collective-permute-start.35
  146.6 2.4 %collective-permute-start.36 = (bf16[128,512]{1,0:T(8,128)(2,1)S(1)}, bf16[128,512]{1,0:T(8,128)(2,1)S(1)}, u32[]{:S(2)}, u32[]{:S(2)}) collective-permute-start(bf16[128,512]{1,0:T(8,128)(2,1)S(1)} %get-tuple-element.134), channel_id=1, source_target_pairs={{0,12},{4,0},{8,4},{12,8},{1,13},{5,1},{9,5},{13,9},{2,14},{6,2},{... | collective-permute-start | bytes 393224 | tf_op jit(solution)/shard_map/ppermute | solution.py:549
  150.2 3.2 %collective-permute-done.34.refs_1_ = bf16[128,512]{1,0:T(8,128)(2,1)S(1)} collective-permute-done((bf16[128,512]{1,0:T(8,128)(2,1)S(1)}, bf16[128,512]{1,0:T(8,128)(2,1)S(1)}, u32[]{:S(2)}, u32[]{:S(2)}) %collective-permute-start.34) | collective-permute-done | bytes 131104 | tf_op jit(solution)/shard_map/ppermute | solution.py:549
  153.4 5.6 %collective-permute-done.35.refs_2_ = bf16[128,512]{1,0:T(8,128)(2,1)S(1)} collective-permute-done((bf16[128,512]{1,0:T(8,128)(2,1)S(1)}, bf16[128,512]{1,0:T(8,128)(2,1)S(1)}, u32[]{:S(2)}, u32[]{:S(2)}) %collective-permute-start.35) | collective-permute-done | bytes 131104 | tf_op jit(solution)/shard_map/ppermute | solution.py:549
  159.1 2.9 %collective-permute-start.32 = (bf16[128,512]{1,0:T(8,128)(2,1)S(1)}, bf16[128,512]{1,0:T(8,128)(2,1)S(1)}, u32[]{:S(2)}, u32[]{:S(2)}) collective-permute-start(bf16[128,512]{1,0:T(8,128)(2,1)S(1)} %get-tuple-element.124), channel_id=1, source_target_pairs={{0,12},{4,0},{8,4},{12,8},{1,13},{5,1},{9,5},{13,9},{2,14},{6,2},{... | collective-permute-start | bytes 393224 | tf_op jit(solution)/shard_map/ppermute | solution.py:549
  161.9 1.8 %input_own.1.refs_1_.refs_4_ = bf16[1024,512]{1,0:T(8,128)(2,1)S(1)} custom-call(s32[4]{0:T(128)S(1)} %pad_add_fusion.refs_0_, bf16[1024,512]{1,0:T(8,128)(2,1)S(1)} %get-tuple-element.116.refs_2_.refs_1_, bf16[1024,512]{1,0:T(8,128)(2,1)S(1)} %get-tuple-element.117.refs_2_, bf16[1024,512]{1,0:T(8,128)(2,1)S(1)} %copy-done, bf16[1024,512]{1,0:T(8,128)(2,1)S(1)} %copy-done.4, ...), custom_call_target="tpu_custom_call" | custom-call | flops 1073741824 | bytes 5242896 | tf_op jit(solution)/shard_map/input_own/pallas_call | solution.py:521
  163.8 0.8 value_sum.1
  164.5 1.2 collective-permute-done.29.refs_2_
  165.7 2.3 %input_sum.1.refs_4_ = bf16[1024,512]{1,0:T(8,128)(2,1)} custom-call(bf16[1024,1024]{1,0:T(8,128)(2,1)S(1)} %get-tuple-element.72.refs_9_.refs_0_, bf16[1024,512]{1,0:T(8,128)(2,1)S(1)} %input_own.1.refs_1_.refs_4_, bf16[1024,512]{1,0:T(8,128)(2,1)S(1)} %collective-permute-done.29.refs_2_), custom_call_target="tpu_custom_call" | custom-call | flops 1073741824 | bytes 5242880 | tf_op jit(solution)/shard_map/input_sum/pallas_call | solution.py:521
  168.0 1.4 collective-permute-done.31.refs_2_
  169.3 1.2 copy-done.1
  170.6 0.8 query_sum.1
  (59 shorter events, 3.4 us)
Async XLA Ops:
  0.6 9.8 %copy-start = (bf16[1024,512]{1,0:T(8,128)(2,1)S(1)}, bf16[1024,512]{1,0:T(8,128)(2,1)}, u32[]{:S(2)}) copy-start(bf16[1024,512]{1,0:T(8,128)(2,1)} %refs_3_.7) | copy-start | bytes 3145732
  0.6 9.8 %copy-start.2 = (bf16[1024,1024]{1,0:T(8,128)(2,1)S(1)}, bf16[1024,1024]{1,0:T(8,128)(2,1)}, u32[]{:S(2)}) copy-start(bf16[1024,1024]{1,0:T(8,128)(2,1)} %refs_2_.4) | copy-start | bytes 6291460
  0.7 9.8 %copy-start.5 = (s32[1024,1]{0,1:T(1,128)S(1)}, s32[1024,1]{0,1:T(1,128)}, u32[]{:S(2)}) copy-start(s32[1024,1]{0,1:T(1,128)} %param.9) | copy-start | bytes 12292
  6.2 34.5 %collective-permute-start = (bf16[1040,128]{1,0:T(8,128)(2,1)}, bf16[1040,128]{1,0:T(8,128)(2,1)S(1)}, u32[]{:S(2)}, u32[]{:S(2)}) collective-permute-start(bf16[1040,128]{1,0:T(8,128)(2,1)} %get-tuple-element.75), channel_id=1, source_target_pairs={{0,8},{8,0},{9,1},{4,12},{5,13},{12,4},{13,5},{1,9},{2,10},{10,2},... | collective-permute-start | bytes 798728 | tf_op jit(solution)/shard_map/ppermute | solution.py:543
  10.3 34.5 %collective-permute-start.1 = (bf16[1040,128]{1,0:T(8,128)(2,1)}, bf16[1040,128]{1,0:T(8,128)(2,1)}, u32[]{:S(2)}, u32[]{:S(2)}) collective-permute-start(bf16[1040,128]{1,0:T(8,128)(2,1)} %get-tuple-element.76), channel_id=1, source_target_pairs={{0,9},{8,1},{9,0},{4,13},{5,12},{12,5},{13,4},{1,8},{2,11},{10,3},... | collective-permute-start | bytes 798728 | tf_op jit(solution)/shard_map/ppermute | solution.py:543
  10.4 1.2 copy-start.3
  11.7 0.7 copy-start.6
  12.3 33.9 %copy-start.4 = (bf16[1024,512]{1,0:T(8,128)(2,1)S(1)}, bf16[1024,512]{1,0:T(8,128)(2,1)}, u32[]{:S(2)}) copy-start(bf16[1024,512]{1,0:T(8,128)(2,1)} %refs_4_.3) | copy-start | bytes 3145732
  17.2 35.1 %collective-permute-start.3 = (bf16[1040,128]{1,0:T(8,128)(2,1)S(1)}, bf16[1040,128]{1,0:T(8,128)(2,1)S(1)}, u32[]{:S(2)}, u32[]{:S(2)}) collective-permute-start(bf16[1040,128]{1,0:T(8,128)(2,1)S(1)} %get-tuple-element.77), channel_id=1, source_target_pairs={{0,5},{8,13},{9,12},{4,9},{5,8},{12,1},{13,0},{1,4},{2,7},{10,15},... | collective-permute-start | bytes 798728 | tf_op jit(solution)/shard_map/ppermute | solution.py:543
  18.9 33.5 %collective-permute-start.2 = (bf16[1040,128]{1,0:T(8,128)(2,1)S(1)}, bf16[1040,128]{1,0:T(8,128)(2,1)S(1)}, u32[]{:S(2)}, u32[]{:S(2)}) collective-permute-start(bf16[1040,128]{1,0:T(8,128)(2,1)S(1)} %get-tuple-element.71.refs_4_), channel_id=1, source_target_pairs={{0,4},{8,12},{9,13},{4,8},{5,9},{12,0},{13,1},{1,5},{2,6},{10,14},... | collective-permute-start | bytes 798728 | tf_op jit(solution)/shard_map/ppermute | solution.py:543
  20.4 35.6 %collective-permute-start.4 = (bf16[1040,128]{1,0:T(8,128)(2,1)S(1)}, bf16[1040,128]{1,0:T(8,128)(2,1)S(1)}, u32[]{:S(2)}, u32[]{:S(2)}) collective-permute-start(bf16[1040,128]{1,0:T(8,128)(2,1)S(1)} %get-tuple-element.78), channel_id=1, source_target_pairs={{0,12},{8,4},{9,5},{4,0},{5,1},{12,8},{13,9},{1,13},{2,14},{10,6},... | collective-permute-start | bytes 798728 | tf_op jit(solution)/shard_map/ppermute | solution.py:543
  40.7 15.3 %collective-permute-start.5 = (bf16[1040,128]{1,0:T(8,128)(2,1)S(1)}, bf16[1040,128]{1,0:T(8,128)(2,1)S(1)}, u32[]{:S(2)}, u32[]{:S(2)}) collective-permute-start(bf16[1040,128]{1,0:T(8,128)(2,1)S(1)} %get-tuple-element.79), channel_id=1, source_target_pairs={{0,13},{8,5},{9,4},{4,1},{5,0},{12,9},{13,8},{1,12},{2,15},{10,7},... | collective-permute-start | bytes 798728 | tf_op jit(solution)/shard_map/ppermute | solution.py:543
  44.8 11.2 %collective-permute-start.6 = (bf16[1040,128]{1,0:T(8,128)(2,1)S(1)}, bf16[1040,128]{1,0:T(8,128)(2,1)S(1)}, u32[]{:S(2)}, u32[]{:S(2)}) collective-permute-start(bf16[1040,128]{1,0:T(8,128)(2,1)S(1)} %get-tuple-element.80), channel_id=1, source_target_pairs={{0,1},{8,9},{9,8},{4,5},{5,4},{12,13},{13,12},{1,0},{2,3},{10,11},... | collective-permute-start | bytes 798728 | tf_op jit(solution)/shard_map/ppermute | solution.py:543
  52.3 26.4 %copy-start.7 = (bf16[1024,1024]{1,0:T(8,128)(2,1)}, bf16[1024,1024]{1,0:T(8,128)(2,1)S(1)}, u32[]{:S(2)}) copy-start(bf16[1024,1024]{1,0:T(8,128)(2,1)S(1)} %get-tuple-element.73.refs_1_) | copy-start | bytes 6291460
  52.3 8.4 %collective-permute-start.20 = (bf16[512,128]{1,0:T(8,128)(2,1)S(1)}, bf16[512,128]{1,0:T(8,128)(2,1)S(1)}, u32[]{:S(2)}, u32[]{:S(2)}) collective-permute-start(bf16[512,128]{1,0:T(8,128)(2,1)S(1)} %get-tuple-element.107), channel_id=1, source_target_pairs={{0,1},{8,9},{9,8},{4,5},{5,4},{12,13},{13,12},{1,0},{2,3},{10,11},... | collective-permute-start | bytes 393224 | tf_op jit(solution)/shard_map/ppermute | solution.py:543
  52.4 12.1 %collective-permute-start.19 = (bf16[512,128]{1,0:T(8,128)(2,1)S(1)}, bf16[512,128]{1,0:T(8,128)(2,1)S(1)}, u32[]{:S(2)}, u32[]{:S(2)}) collective-permute-start(bf16[512,128]{1,0:T(8,128)(2,1)S(1)} %get-tuple-element.105), channel_id=1, source_target_pairs={{0,13},{8,5},{9,4},{4,1},{5,0},{12,9},{13,8},{1,12},{2,15},{10,7},... | collective-permute-start | bytes 393224 | tf_op jit(solution)/shard_map/ppermute | solution.py:543
  56.0 22.7 %collective-permute-start.18 = (bf16[512,128]{1,0:T(8,128)(2,1)S(1)}, bf16[512,128]{1,0:T(8,128)(2,1)S(1)}, u32[]{:S(2)}, u32[]{:S(2)}) collective-permute-start(bf16[512,128]{1,0:T(8,128)(2,1)S(1)} %get-tuple-element.103), channel_id=1, source_target_pairs={{0,12},{8,4},{9,5},{4,0},{5,1},{12,8},{13,9},{1,13},{2,14},{10,6},... | collective-permute-start | bytes 393224 | tf_op jit(solution)/shard_map/ppermute | solution.py:543
  60.7 20.3 %collective-permute-start.17 = (bf16[512,128]{1,0:T(8,128)(2,1)S(1)}, bf16[512,128]{1,0:T(8,128)(2,1)S(1)}, u32[]{:S(2)}, u32[]{:S(2)}) collective-permute-start(bf16[512,128]{1,0:T(8,128)(2,1)S(1)} %get-tuple-element.101), channel_id=1, source_target_pairs={{0,5},{8,13},{9,12},{4,9},{5,8},{12,1},{13,0},{1,4},{2,7},{10,15},... | collective-permute-start | bytes 393224 | tf_op jit(solution)/shard_map/ppermute | solution.py:543
  60.7 20.4 %collective-permute-start.16 = (bf16[512,128]{1,0:T(8,128)(2,1)S(1)}, bf16[512,128]{1,0:T(8,128)(2,1)S(1)}, u32[]{:S(2)}, u32[]{:S(2)}) collective-permute-start(bf16[512,128]{1,0:T(8,128)(2,1)S(1)} %get-tuple-element.99), channel_id=1, source_target_pairs={{0,4},{8,12},{9,13},{4,8},{5,9},{12,0},{13,1},{1,5},{2,6},{10,14},... | collective-permute-start | bytes 393224 | tf_op jit(solution)/shard_map/ppermute | solution.py:543
  60.7 20.6 %collective-permute-start.15 = (bf16[512,128]{1,0:T(8,128)(2,1)S(1)}, bf16[512,128]{1,0:T(8,128)(2,1)S(1)}, u32[]{:S(2)}, u32[]{:S(2)}) collective-permute-start(bf16[512,128]{1,0:T(8,128)(2,1)S(1)} %get-tuple-element.97), channel_id=1, source_target_pairs={{0,9},{8,1},{9,0},{4,13},{5,12},{12,5},{13,4},{1,8},{2,11},{10,3},... | collective-permute-start | bytes 393224 | tf_op jit(solution)/shard_map/ppermute | solution.py:543
  64.6 30.0 %collective-permute-start.14 = (bf16[512,128]{1,0:T(8,128)(2,1)S(1)}, bf16[512,128]{1,0:T(8,128)(2,1)S(1)}, u32[]{:S(2)}, u32[]{:S(2)}) collective-permute-start(bf16[512,128]{1,0:T(8,128)(2,1)S(1)} %get-tuple-element.95), channel_id=1, source_target_pairs={{0,8},{8,0},{9,1},{4,12},{5,13},{12,4},{13,5},{1,9},{2,10},{10,2},... | collective-permute-start | bytes 393224 | tf_op jit(solution)/shard_map/ppermute | solution.py:543
  78.7 31.8 %collective-permute-start.7 = (bf16[512,128]{1,0:T(8,128)(2,1)S(1)}, bf16[512,128]{1,0:T(8,128)(2,1)S(1)}, u32[]{:S(2)}, u32[]{:S(2)}) collective-permute-start(bf16[512,128]{1,0:T(8,128)(2,1)S(1)} %get-tuple-element.82), channel_id=1, source_target_pairs={{0,8},{8,0},{9,1},{4,12},{5,13},{12,4},{13,5},{1,9},{2,10},{10,2},... | collective-permute-start | bytes 393224 | tf_op jit(solution)/shard_map/ppermute | solution.py:543
  81.0 31.1 %collective-permute-start.8 = (bf16[512,128]{1,0:T(8,128)(2,1)S(1)}, bf16[512,128]{1,0:T(8,128)(2,1)S(1)}, u32[]{:S(2)}, u32[]{:S(2)}) collective-permute-start(bf16[512,128]{1,0:T(8,128)(2,1)S(1)} %get-tuple-element.83), channel_id=1, source_target_pairs={{0,9},{8,1},{9,0},{4,13},{5,12},{12,5},{13,4},{1,8},{2,11},{10,3},... | collective-permute-start | bytes 393224 | tf_op jit(solution)/shard_map/ppermute | solution.py:543
  81.2 31.0 %collective-permute-start.9 = (bf16[512,128]{1,0:T(8,128)(2,1)S(1)}, bf16[512,128]{1,0:T(8,128)(2,1)S(1)}, u32[]{:S(2)}, u32[]{:S(2)}) collective-permute-start(bf16[512,128]{1,0:T(8,128)(2,1)S(1)} %get-tuple-element.84), channel_id=1, source_target_pairs={{0,4},{8,12},{9,13},{4,8},{5,9},{12,0},{13,1},{1,5},{2,6},{10,14},... | collective-permute-start | bytes 393224 | tf_op jit(solution)/shard_map/ppermute | solution.py:543
  81.3 33.1 %collective-permute-start.10 = (bf16[512,128]{1,0:T(8,128)(2,1)S(1)}, bf16[512,128]{1,0:T(8,128)(2,1)S(1)}, u32[]{:S(2)}, u32[]{:S(2)}) collective-permute-start(bf16[512,128]{1,0:T(8,128)(2,1)S(1)} %get-tuple-element.85), channel_id=1, source_target_pairs={{0,5},{8,13},{9,12},{4,9},{5,8},{12,1},{13,0},{1,4},{2,7},{10,15},... | collective-permute-start | bytes 393224 | tf_op jit(solution)/shard_map/ppermute | solution.py:543
  94.5 34.2 %copy-start.8 = (bf16[1024,1024]{1,0:T(8,128)(2,1)S(1)}, bf16[1024,1024]{1,0:T(8,128)(2,1)}, u32[]{:S(2)}) copy-start(bf16[1024,1024]{1,0:T(8,128)(2,1)} %copy-done.7) | copy-start | bytes 6291460
  110.4 18.0 %collective-permute-start.21 = (bf16[544,128]{1,0:T(8,128)(2,1)S(1)}, bf16[544,128]{1,0:T(8,128)(2,1)S(1)}, u32[]{:S(2)}, u32[]{:S(2)}) collective-permute-start(bf16[544,128]{1,0:T(8,128)(2,1)S(1)} %get-tuple-element.109), channel_id=1, source_target_pairs={{0,8},{8,0},{9,1},{4,12},{5,13},{12,4},{13,5},{1,9},{2,10},{10,2},... | collective-permute-start | bytes 417800 | tf_op jit(solution)/shard_map/ppermute | solution.py:543
  110.5 18.1 %collective-permute-start.22 = (bf16[544,128]{1,0:T(8,128)(2,1)S(1)}, bf16[544,128]{1,0:T(8,128)(2,1)S(1)}, u32[]{:S(2)}, u32[]{:S(2)}) collective-permute-start(bf16[544,128]{1,0:T(8,128)(2,1)S(1)} %get-tuple-element.110), channel_id=1, source_target_pairs={{0,9},{8,1},{9,0},{4,13},{5,12},{12,5},{13,4},{1,8},{2,11},{10,3},... | collective-permute-start | bytes 417800 | tf_op jit(solution)/shard_map/ppermute | solution.py:543
  112.1 10.0 %collective-permute-start.11 = (bf16[512,128]{1,0:T(8,128)(2,1)S(1)}, bf16[512,128]{1,0:T(8,128)(2,1)S(1)}, u32[]{:S(2)}, u32[]{:S(2)}) collective-permute-start(bf16[512,128]{1,0:T(8,128)(2,1)S(1)} %get-tuple-element.86), channel_id=1, source_target_pairs={{0,12},{8,4},{9,5},{4,0},{5,1},{12,8},{13,9},{1,13},{2,14},{10,6},... | collective-permute-start | bytes 393224 | tf_op jit(solution)/shard_map/ppermute | solution.py:543
  112.2 12.8 %collective-permute-start.12 = (bf16[512,128]{1,0:T(8,128)(2,1)S(1)}, bf16[512,128]{1,0:T(8,128)(2,1)S(1)}, u32[]{:S(2)}, u32[]{:S(2)}) collective-permute-start(bf16[512,128]{1,0:T(8,128)(2,1)S(1)} %get-tuple-element.87), channel_id=1, source_target_pairs={{0,13},{8,5},{9,4},{4,1},{5,0},{12,9},{13,8},{1,12},{2,15},{10,7},... | collective-permute-start | bytes 393224 | tf_op jit(solution)/shard_map/ppermute | solution.py:543
  114.4 10.6 %collective-permute-start.13 = (bf16[512,128]{1,0:T(8,128)(2,1)S(1)}, bf16[512,128]{1,0:T(8,128)(2,1)S(1)}, u32[]{:S(2)}, u32[]{:S(2)}) collective-permute-start(bf16[512,128]{1,0:T(8,128)(2,1)S(1)} %get-tuple-element.88), channel_id=1, source_target_pairs={{0,1},{8,9},{9,8},{4,5},{5,4},{12,13},{13,12},{1,0},{2,3},{10,11},... | collective-permute-start | bytes 393224 | tf_op jit(solution)/shard_map/ppermute | solution.py:543
  122.1 9.1 %collective-permute-start.23 = (bf16[544,128]{1,0:T(8,128)(2,1)S(1)}, bf16[544,128]{1,0:T(8,128)(2,1)S(1)}, u32[]{:S(2)}, u32[]{:S(2)}) collective-permute-start(bf16[544,128]{1,0:T(8,128)(2,1)S(1)} %get-tuple-element.111), channel_id=1, source_target_pairs={{0,4},{8,12},{9,13},{4,8},{5,9},{12,0},{13,1},{1,5},{2,6},{10,14},... | collective-permute-start | bytes 417800 | tf_op jit(solution)/shard_map/ppermute | solution.py:543
  125.0 7.6 %collective-permute-start.24 = (bf16[544,128]{1,0:T(8,128)(2,1)S(1)}, bf16[544,128]{1,0:T(8,128)(2,1)S(1)}, u32[]{:S(2)}, u32[]{:S(2)}) collective-permute-start(bf16[544,128]{1,0:T(8,128)(2,1)S(1)} %get-tuple-element.112), channel_id=1, source_target_pairs={{0,5},{8,13},{9,12},{4,9},{5,8},{12,1},{13,0},{1,4},{2,7},{10,15},... | collective-permute-start | bytes 417800 | tf_op jit(solution)/shard_map/ppermute | solution.py:543
  125.0 10.7 %collective-permute-start.25 = (bf16[544,128]{1,0:T(8,128)(2,1)S(1)}, bf16[544,128]{1,0:T(8,128)(2,1)S(1)}, u32[]{:S(2)}, u32[]{:S(2)}) collective-permute-start(bf16[544,128]{1,0:T(8,128)(2,1)S(1)} %get-tuple-element.113), channel_id=1, source_target_pairs={{0,12},{8,4},{9,5},{4,0},{5,1},{12,8},{13,9},{1,13},{2,14},{10,6},... | collective-permute-start | bytes 417800 | tf_op jit(solution)/shard_map/ppermute | solution.py:543
  128.5 10.0 %collective-permute-start.26 = (bf16[544,128]{1,0:T(8,128)(2,1)S(1)}, bf16[544,128]{1,0:T(8,128)(2,1)S(1)}, u32[]{:S(2)}, u32[]{:S(2)}) collective-permute-start(bf16[544,128]{1,0:T(8,128)(2,1)S(1)} %get-tuple-element.114), channel_id=1, source_target_pairs={{0,13},{8,5},{9,4},{4,1},{5,0},{12,9},{13,8},{1,12},{2,15},{10,7},... | collective-permute-start | bytes 417800 | tf_op jit(solution)/shard_map/ppermute | solution.py:543
  128.6 9.9 %collective-permute-start.27 = (bf16[544,128]{1,0:T(8,128)(2,1)S(1)}, bf16[544,128]{1,0:T(8,128)(2,1)S(1)}, u32[]{:S(2)}, u32[]{:S(2)}) collective-permute-start(bf16[544,128]{1,0:T(8,128)(2,1)S(1)} %get-tuple-element.115), channel_id=1, source_target_pairs={{0,1},{8,9},{9,8},{4,5},{5,4},{12,13},{13,12},{1,0},{2,3},{10,11},... | collective-permute-start | bytes 417800 | tf_op jit(solution)/shard_map/ppermute | solution.py:543
  140.5 25.2 %collective-permute-start.29 = (bf16[1024,512]{1,0:T(8,128)(2,1)S(1)}, bf16[1024,512]{1,0:T(8,128)(2,1)S(1)}, u32[]{:S(2)}, u32[]{:S(2)}) collective-permute-start(bf16[1024,512]{1,0:T(8,128)(2,1)S(1)} %get-tuple-element.121), channel_id=1, source_target_pairs={{0,2},{2,0},{1,3},{3,1},{4,6},{6,4},{5,7},{7,5},{8,10},{10,8},{9,1... | collective-permute-start | bytes 3145736 | tf_op jit(solution)/shard_map/ppermute | solution.py:549
  142.0 2.4 %collective-permute-start.33 = (bf16[4,128,512]{2,1,0:T(8,128)(2,1)S(1)}, bf16[4,128,512]{2,1,0:T(8,128)(2,1)S(1)}, u32[]{:S(2)}, u32[]{:S(2)}) collective-permute-start(bf16[4,128,512]{2,1,0:T(8,128)(2,1)S(1)} %get-tuple-element.126), channel_id=1, source_target_pairs={{0,1},{1,0},{2,3},{3,2},{4,5},{5,4},{6,7},{7,6},{8,9},{9,8},{10,11... | collective-permute-start | bytes 1572872 | tf_op jit(solution)/shard_map/ppermute | solution.py:549
  143.8 5.1 %collective-permute-start.28 = (bf16[4,128,512]{2,1,0:T(8,128)(2,1)S(1)}, bf16[4,128,512]{2,1,0:T(8,128)(2,1)S(1)}, u32[]{:S(2)}, u32[]{:S(2)}) collective-permute-start(bf16[4,128,512]{2,1,0:T(8,128)(2,1)S(1)} %get-tuple-element.119), channel_id=1, source_target_pairs={{0,1},{1,0},{2,3},{3,2},{4,5},{5,4},{6,7},{7,6},{8,9},{9,8},{10,11... | collective-permute-start | bytes 1572872 | tf_op jit(solution)/shard_map/ppermute | solution.py:549
  145.1 8.3 %collective-permute-start.34 = (bf16[128,512]{1,0:T(8,128)(2,1)S(1)}, bf16[128,512]{1,0:T(8,128)(2,1)S(1)}, u32[]{:S(2)}, u32[]{:S(2)}) collective-permute-start(bf16[128,512]{1,0:T(8,128)(2,1)S(1)} %get-tuple-element.132), channel_id=1, source_target_pairs={{0,4},{4,8},{8,12},{12,0},{1,5},{5,9},{9,13},{13,1},{2,6},{6,10},{... | collective-permute-start | bytes 393224 | tf_op jit(solution)/shard_map/ppermute | solution.py:549
  145.8 13.3 %collective-permute-start.35 = (bf16[128,512]{1,0:T(8,128)(2,1)S(1)}, bf16[128,512]{1,0:T(8,128)(2,1)S(1)}, u32[]{:S(2)}, u32[]{:S(2)}) collective-permute-start(bf16[128,512]{1,0:T(8,128)(2,1)S(1)} %get-tuple-element.133), channel_id=1, source_target_pairs={{0,8},{4,12},{8,0},{12,4},{1,9},{5,13},{9,1},{13,5},{2,10},{6,14},... | collective-permute-start | bytes 393224 | tf_op jit(solution)/shard_map/ppermute | solution.py:549
  146.6 17.2 %collective-permute-start.36 = (bf16[128,512]{1,0:T(8,128)(2,1)S(1)}, bf16[128,512]{1,0:T(8,128)(2,1)S(1)}, u32[]{:S(2)}, u32[]{:S(2)}) collective-permute-start(bf16[128,512]{1,0:T(8,128)(2,1)S(1)} %get-tuple-element.134), channel_id=1, source_target_pairs={{0,12},{4,0},{8,4},{12,8},{1,13},{5,1},{9,5},{13,9},{2,14},{6,2},{... | collective-permute-start | bytes 393224 | tf_op jit(solution)/shard_map/ppermute | solution.py:549
  149.6 18.3 %collective-permute-start.30 = (bf16[128,512]{1,0:T(8,128)(2,1)S(1)}, bf16[128,512]{1,0:T(8,128)(2,1)S(1)}, u32[]{:S(2)}, u32[]{:S(2)}) collective-permute-start(bf16[128,512]{1,0:T(8,128)(2,1)S(1)} %get-tuple-element.122), channel_id=1, source_target_pairs={{0,4},{4,8},{8,12},{12,0},{1,5},{5,9},{9,13},{13,1},{2,6},{6,10},{... | collective-permute-start | bytes 393224 | tf_op jit(solution)/shard_map/ppermute | solution.py:549
  153.4 15.9 %collective-permute-start.31 = (bf16[128,512]{1,0:T(8,128)(2,1)S(1)}, bf16[128,512]{1,0:T(8,128)(2,1)S(1)}, u32[]{:S(2)}, u32[]{:S(2)}) collective-permute-start(bf16[128,512]{1,0:T(8,128)(2,1)S(1)} %get-tuple-element.123), channel_id=1, source_target_pairs={{0,8},{4,12},{8,0},{12,4},{1,9},{5,13},{9,1},{13,5},{2,10},{6,14},... | collective-permute-start | bytes 393224 | tf_op jit(solution)/shard_map/ppermute | solution.py:549
  159.1 10.3 %collective-permute-start.32 = (bf16[128,512]{1,0:T(8,128)(2,1)S(1)}, bf16[128,512]{1,0:T(8,128)(2,1)S(1)}, u32[]{:S(2)}, u32[]{:S(2)}) collective-permute-start(bf16[128,512]{1,0:T(8,128)(2,1)S(1)} %get-tuple-element.124), channel_id=1, source_target_pairs={{0,12},{4,0},{8,4},{12,8},{1,13},{5,1},{9,5},{13,9},{2,14},{6,2},{... | collective-permute-start | bytes 393224 | tf_op jit(solution)/shard_map/ppermute | solution.py:549
  169.3 1.2 copy-start.1

commit v14 on v13

--- a/solution.py
+++ b/solution.py
@@ -565,7 +565,7 @@
 
 def add_up(terms, dtype, name, after=()):
     out = jax.ShapeDtypeStruct(terms[0].shape, dtype)
-    return call(sum_kernel, out, tuple(terms), smem=(), after=after, name=name)
+    return call(sum_kernel, out, tuple(terms), smem=(), after=after, vmem=60, name=name)
 
 
 def on_device(tokens_in, w_query, w_value, cotangent, assignment):

time: 172 us -> 173 us (level)
  Pallas kernels: 59.1 us -> 63.4 us
  waiting for transfers between devices: 59 us -> 56 us
    pallas_call x14, Pallas kernels: 59.1 us -> 63.4 us  [call(): pl.pallas_call(body, out_shape=outs, in_specs=specs, out_specs=jax.tree.m...]
    ppermute x9, waiting for transfers between devices: 11.4 us -> 8.29 us  [shift(): lax.ppermute(part, axis, [(i, (i + ahead) % size) for i in range(size)])]
  transfers between devices with their start and end apart: 37 -> 37, of which waited for: 12 -> 10; matrix products, arithmetic and copies ran while one was open for 0% -> 0% of each run, Pallas kernels for 30% -> 31%
where the time goes in v14:
time: 173 us; the launch traced here: 172 us
  Pallas kernels  63.4 us (37%)
  waiting for transfers between devices  56 us (32%)
  starting transfers between devices  49.1 us (28%)
  local copies, waits for them, and re-layouts  2.92 us (2%)
    pallas_call x14, Pallas kernels, call(): pl.pallas_call(body, out_shape=outs, in_specs=specs, out_specs=jax.tree.m...  63.4 us
    ppermute x28, waiting for transfers between devices, exchange(): out.append(part if ahead == (0, 0) else lax.ppermute(part, OWNERS, moves))  47.7 us
    ppermute x28, starting transfers between devices, exchange(): out.append(part if ahead == (0, 0) else lax.ppermute(part, OWNERS, moves))  39.7 us
    ppermute x9, starting transfers between devices, shift(): lax.ppermute(part, axis, [(i, (i + ahead) % size) for i in range(size)])  9.38 us
    ppermute x9, waiting for transfers between devices, shift(): lax.ppermute(part, axis, [(i, (i + ahead) % size) for i in range(size)])  8.29 us
  transfers between devices with their start and end apart: 37, of which 10 were waited for; matrix products, arithmetic and copies ran while one was open for 0% of the time, Pallas kernels for 31%

profile of v14, /device:TPU:0, one launch (start us, length us, event | category | flops | bytes accessed | tf_op | source)
XLA Modules:
  0.0 172.3 jit_solution(5210736275569995657)
XLA Ops:
  0.7 5.6 %project_far.1 = (bf16[1040,128]{1,0:T(8,128)(2,1)}, bf16[1040,128]{1,0:T(8,128)(2,1)}, s32[1,1024]{1,0:T(1,128)}) custom-call(s32[1,1024]{1,0:T(1,128)} %bitcast.5, bf16[1024,1024]{1,0:T(8,128)(2,1)} %refs_2_.4, bf16[1024,512]{1,0:T(8,128)(2,1)} %refs_3_.7, bf16[1024,512]{1,0:T(8,128)(2,1)} %refs_5_.1), custom_call_target="tpu_custom_call" | custom-call | flops 805306368 | bytes 4734976 | tf_op jit(solution)/shard_map/project_far/pallas_call | solution.py:521
  6.2 4.1 %collective-permute-start = (bf16[1040,128]{1,0:T(8,128)(2,1)}, bf16[1040,128]{1,0:T(8,128)(2,1)S(1)}, u32[]{:S(2)}, u32[]{:S(2)}) collective-permute-start(bf16[1040,128]{1,0:T(8,128)(2,1)} %get-tuple-element.75), channel_id=1, source_target_pairs={{0,8},{8,0},{9,1},{4,12},{5,13},{12,4},{13,5},{1,9},{2,10},{10,2},... | collective-permute-start | bytes 798728 | tf_op jit(solution)/shard_map/ppermute | solution.py:543
  10.4 1.2 copy-done.6
  11.7 0.7 copy-done.11
  12.4 4.8 %project_query.1 = (bf16[1040,128]{1,0:T(8,128)(2,1)S(1)}, bf16[1040,128]{1,0:T(8,128)(2,1)S(1)}, bf16[1040,128]{1,0:T(8,128)(2,1)S(1)}, bf16[1040,128]{1,0:T(8,...) custom-call(s32[4]{0:T(128)S(1)} %pad_add_fusion.refs_0_, s32[1,1024]{1,0:T(1,128)S(1)} %copy-done.11, ...), custom_call_target="tpu_custom_call" | custom-call | flops 3221225472 | bytes 5799952 | tf_op jit(solution)/shard_map/project_query/pallas_call | solution.py:521
  17.2 1.7 collective-permute-start.3
  18.9 1.6 collective-permute-start.2
  20.4 2.2 %collective-permute-start.4 = (bf16[1040,128]{1,0:T(8,128)(2,1)S(1)}, bf16[1040,128]{1,0:T(8,128)(2,1)S(1)}, u32[]{:S(2)}, u32[]{:S(2)}) collective-permute-start(bf16[1040,128]{1,0:T(8,128)(2,1)S(1)} %get-tuple-element.78), channel_id=1, source_target_pairs={{0,12},{8,4},{9,5},{4,0},{5,1},{12,8},{13,9},{1,13},{2,14},{10,6},... | collective-permute-start | bytes 798728 | tf_op jit(solution)/shard_map/ppermute | solution.py:543
  22.7 18.0 %collective-permute-done.refs_2_ = bf16[1040,128]{1,0:T(8,128)(2,1)S(1)} collective-permute-done((bf16[1040,128]{1,0:T(8,128)(2,1)}, bf16[1040,128]{1,0:T(8,128)(2,1)S(1)}, u32[]{:S(2)}, u32[]{:S(2)}) %collective-permute-start) | collective-permute-done | bytes 266272 | tf_op jit(solution)/shard_map/ppermute | solution.py:543
  40.7 4.1 %collective-permute-done.1.refs_3_ = bf16[1040,128]{1,0:T(8,128)(2,1)} collective-permute-done((bf16[1040,128]{1,0:T(8,128)(2,1)}, bf16[1040,128]{1,0:T(8,128)(2,1)}, u32[]{:S(2)}, u32[]{:S(2)}) %collective-permute-start.1) | collective-permute-done | bytes 266272 | tf_op jit(solution)/shard_map/ppermute | solution.py:543
  44.8 1.4 collective-permute-start.6
  46.3 6.0 %project_value.1 = (bf16[512,128]{1,0:T(8,128)(2,1)S(1)}, bf16[512,128]{1,0:T(8,128)(2,1)S(1)}, bf16[512,128]{1,0:T(8,128)(2,1)S(1)}, bf16[512,128]{1,0:T(8,128)...) custom-call(s32[4]{0:T(128)S(1)} %pad_add_fusion.refs_0_, ...), custom_call_target="tpu_custom_call" | custom-call | flops 2147483648 | bytes 8392720 | tf_op jit(solution)/shard_map/project_value/pallas_call | solution.py:521
  52.4 3.6 %collective-permute-start.19 = (bf16[512,128]{1,0:T(8,128)(2,1)S(1)}, bf16[512,128]{1,0:T(8,128)(2,1)S(1)}, u32[]{:S(2)}, u32[]{:S(2)}) collective-permute-start(bf16[512,128]{1,0:T(8,128)(2,1)S(1)} %get-tuple-element.105), channel_id=1, source_target_pairs={{0,13},{8,5},{9,4},{4,1},{5,0},{12,9},{13,8},{1,12},{2,15},{10,7},... | collective-permute-start | bytes 393224 | tf_op jit(solution)/shard_map/ppermute | solution.py:543
  56.0 4.7 %collective-permute-start.18 = (bf16[512,128]{1,0:T(8,128)(2,1)S(1)}, bf16[512,128]{1,0:T(8,128)(2,1)S(1)}, u32[]{:S(2)}, u32[]{:S(2)}) collective-permute-start(bf16[512,128]{1,0:T(8,128)(2,1)S(1)} %get-tuple-element.103), channel_id=1, source_target_pairs={{0,12},{8,4},{9,5},{4,0},{5,1},{12,8},{13,9},{1,13},{2,14},{10,6},... | collective-permute-start | bytes 393224 | tf_op jit(solution)/shard_map/ppermute | solution.py:543
  60.7 3.8 %collective-permute-start.15 = (bf16[512,128]{1,0:T(8,128)(2,1)S(1)}, bf16[512,128]{1,0:T(8,128)(2,1)S(1)}, u32[]{:S(2)}, u32[]{:S(2)}) collective-permute-start(bf16[512,128]{1,0:T(8,128)(2,1)S(1)} %get-tuple-element.97), channel_id=1, source_target_pairs={{0,9},{8,1},{9,0},{4,13},{5,12},{12,5},{13,4},{1,8},{2,11},{10,3},... | collective-permute-start | bytes 393224 | tf_op jit(solution)/shard_map/ppermute | solution.py:543
  64.6 0.6 collective-permute-start.14
  65.2 13.5 %value_grad.1 = (bf16[512,128]{1,0:T(8,128)(2,1)S(1)}, bf16[512,128]{1,0:T(8,128)(2,1)S(1)}, bf16[512,128]{1,0:T(8,128)(2,1)S(1)}, bf16[512,128]{1,0:T(8,128)(2,...) custom-call(s32[4]{0:T(128)S(1)} %pad_add_fusion.refs_0_, ...), custom_call_target="tpu_custom_call" | custom-call | flops 2147483648 | bytes 8163344 | tf_op jit(solution)/shard_map/value_grad/pallas_call | solution.py:521
  78.7 2.3 %collective-permute-start.7 = (bf16[512,128]{1,0:T(8,128)(2,1)S(1)}, bf16[512,128]{1,0:T(8,128)(2,1)S(1)}, u32[]{:S(2)}, u32[]{:S(2)}) collective-permute-start(bf16[512,128]{1,0:T(8,128)(2,1)S(1)} %get-tuple-element.82), channel_id=1, source_target_pairs={{0,8},{8,0},{9,1},{4,12},{5,13},{12,4},{13,5},{1,9},{2,10},{10,2},... | collective-permute-start | bytes 393224 | tf_op jit(solution)/shard_map/ppermute | solution.py:543
  81.3 2.6 %collective-permute-start.10 = (bf16[512,128]{1,0:T(8,128)(2,1)S(1)}, bf16[512,128]{1,0:T(8,128)(2,1)S(1)}, u32[]{:S(2)}, u32[]{:S(2)}) collective-permute-start(bf16[512,128]{1,0:T(8,128)(2,1)S(1)} %get-tuple-element.85), channel_id=1, source_target_pairs={{0,5},{8,13},{9,12},{4,9},{5,8},{12,1},{13,0},{1,4},{2,7},{10,15},... | collective-permute-start | bytes 393224 | tf_op jit(solution)/shard_map/ppermute | solution.py:543
  83.9 10.6 %collective-permute-done.14.refs_4_ = bf16[512,128]{1,0:T(8,128)(2,1)S(1)} collective-permute-done((bf16[512,128]{1,0:T(8,128)(2,1)S(1)}, bf16[512,128]{1,0:T(8,128)(2,1)S(1)}, u32[]{:S(2)}, u32[]{:S(2)}) %collective-permute-start.14) | collective-permute-done | bytes 131104 | tf_op jit(solution)/shard_map/ppermute | solution.py:543
  94.5 15.8 %query_grad.1 = (bf16[544,128]{1,0:T(8,128)(2,1)S(1)}, bf16[544,128]{1,0:T(8,128)(2,1)S(1)}, bf16[544,128]{1,0:T(8,128)(2,1)S(1)}, bf16[544,128]{1,0:T(8,128)(2,...) custom-call(s32[4]{0:T(128)S(1)} %pad_add_fusion.refs_0_, ...), custom_call_target="tpu_custom_call" | custom-call | flops 3221225472 | bytes 7147536 | tf_op jit(solution)/shard_map/query_grad/pallas_call | solution.py:521
  110.4 1.6 collective-permute-start.22
  112.0 2.3 %collective-permute-start.12 = (bf16[512,128]{1,0:T(8,128)(2,1)S(1)}, bf16[512,128]{1,0:T(8,128)(2,1)S(1)}, u32[]{:S(2)}, u32[]{:S(2)}) collective-permute-start(bf16[512,128]{1,0:T(8,128)(2,1)S(1)} %get-tuple-element.87), channel_id=1, source_target_pairs={{0,13},{8,5},{9,4},{4,1},{5,0},{12,9},{13,8},{1,12},{2,15},{10,7},... | collective-permute-start | bytes 393224 | tf_op jit(solution)/shard_map/ppermute | solution.py:543
  114.3 0.8 collective-permute-start.13
  115.1 6.9 %collective-permute-done.11.refs_8_ = bf16[512,128]{1,0:T(8,128)(2,1)S(1)} collective-permute-done((bf16[512,128]{1,0:T(8,128)(2,1)S(1)}, bf16[512,128]{1,0:T(8,128)(2,1)S(1)}, u32[]{:S(2)}, u32[]{:S(2)}) %collective-permute-start.11) | collective-permute-done | bytes 131104 | tf_op jit(solution)/shard_map/ppermute | solution.py:543
  122.0 2.0 %collective-permute-start.23 = (bf16[544,128]{1,0:T(8,128)(2,1)S(1)}, bf16[544,128]{1,0:T(8,128)(2,1)S(1)}, u32[]{:S(2)}, u32[]{:S(2)}) collective-permute-start(bf16[544,128]{1,0:T(8,128)(2,1)S(1)} %get-tuple-element.111), channel_id=1, source_target_pairs={{0,4},{8,12},{9,13},{4,8},{5,9},{12,0},{13,1},{1,5},{2,6},{10,14},... | collective-permute-start | bytes 417800 | tf_op jit(solution)/shard_map/ppermute | solution.py:543
  124.0 0.8 collective-permute-done.12.refs_9_
  124.9 3.5 %collective-permute-start.25 = (bf16[544,128]{1,0:T(8,128)(2,1)S(1)}, bf16[544,128]{1,0:T(8,128)(2,1)S(1)}, u32[]{:S(2)}, u32[]{:S(2)}) collective-permute-start(bf16[544,128]{1,0:T(8,128)(2,1)S(1)} %get-tuple-element.113), channel_id=1, source_target_pairs={{0,12},{8,4},{9,5},{4,0},{5,1},{12,8},{13,9},{1,13},{2,14},{10,6},... | collective-permute-start | bytes 417800 | tf_op jit(solution)/shard_map/ppermute | solution.py:543
  128.6 2.5 %value_home.1 = (bf16[1024,512]{1,0:T(8,128)(2,1)S(1)}, f32[1024,512]{1,0:T(8,128)S(1)}, bf16[4,128,512]{2,1,0:T(8,128)(2,1)S(1)}, bf16[4,128,512]{2,1,0:T(8,128)(2,1)S(1)}) custom-call(s32[4]{0:T(128)S(1)} %pad_add_fusion.refs_0_, bf16[1024,1024]{1,0:T(8,128)(2,1)S(1)} %get-tuple-element.73.refs_1_, bf16[1024,512]{1,0:T(8,128)(2,1)S(1)} %copy-done.7, ...), custom_call_target="tpu_custom_call" | custom-call | flops 1610612736 | bytes 8388624 | tf_op jit(solution)/shard_map/value_home/pallas_call | solution.py:521
  131.1 1.3 collective-permute-done.24.refs_7_
  132.4 3.1 %collective-permute-done.25.refs_8_ = bf16[544,128]{1,0:T(8,128)(2,1)S(1)} collective-permute-done((bf16[544,128]{1,0:T(8,128)(2,1)S(1)}, bf16[544,128]{1,0:T(8,128)(2,1)S(1)}, u32[]{:S(2)}, u32[]{:S(2)}) %collective-permute-start.25) | collective-permute-done | bytes 139296 | tf_op jit(solution)/shard_map/ppermute | solution.py:543
  135.5 2.8 %collective-permute-done.26.refs_9_ = bf16[544,128]{1,0:T(8,128)(2,1)S(1)} collective-permute-done((bf16[544,128]{1,0:T(8,128)(2,1)S(1)}, bf16[544,128]{1,0:T(8,128)(2,1)S(1)}, u32[]{:S(2)}, u32[]{:S(2)}) %collective-permute-start.26) | collective-permute-done | bytes 139296 | tf_op jit(solution)/shard_map/ppermute | solution.py:543
  138.3 2.4 %query_home.1 = (bf16[1024,512]{1,0:T(8,128)(2,1)}, bf16[1024,512]{1,0:T(8,128)(2,1)S(1)}, f32[64,512]{1,0:T(8,128)}) custom-call(s32[4]{0:T(128)S(1)} %pad_add_fusion.refs_0_, bf16[1024,512]{1,0:T(8,128)(2,1)S(1)} %copy-done, f32[1024,512]{1,0:T(8,128)S(1)} %get-tuple-element.89.refs_2_, bf16[544,128]{1,0:T(8,128)(2,1)S(1)} %get-tuple-element.108.refs_3_, ...), custom_call_target="tpu_custom_call" | custom-call | flops 536870912 | bytes 6488080 | tf_op jit(solution)/shard_map/query_home/pallas_call | solution.py:521
  140.7 1.5 collective-permute-start.29
  142.2 1.8 %query_weight.1 = (bf16[4,128,512]{2,1,0:T(8,128)(2,1)S(1)}, bf16[4,128,512]{2,1,0:T(8,128)(2,1)S(1)}) custom-call(s32[4]{0:T(128)S(1)} %pad_add_fusion.refs_0_, bf16[1024,1024]{1,0:T(8,128)(2,1)S(1)} %get-tuple-element.73.refs_1_, bf16[1024,512]{1,0:T(8,128)(2,1)S(1)} %get-tuple-element.116.refs_2_.refs_1_), custom_call_target="tpu_custom_call" | custom-call | flops 1073741824 | bytes 4194320 | tf_op jit(solution)/shard_map/query_weight/pallas_call | solution.py:521
  144.6 0.7 value_subs.1
  145.3 0.7 collective-permute-start.34
  146.0 0.8 collective-permute-start.35
  146.8 2.4 %collective-permute-start.36 = (bf16[128,512]{1,0:T(8,128)(2,1)S(1)}, bf16[128,512]{1,0:T(8,128)(2,1)}, u32[]{:S(2)}, u32[]{:S(2)}) collective-permute-start(bf16[128,512]{1,0:T(8,128)(2,1)S(1)} %get-tuple-element.134), channel_id=1, source_target_pairs={{0,12},{4,0},{8,4},{12,8},{1,13},{5,1},{9,5},{13,9},{2,14},{6,2},{... | collective-permute-start | bytes 393224 | tf_op jit(solution)/shard_map/ppermute | solution.py:549
  149.2 1.3 query_subs.1
  151.0 2.6 %collective-permute-done.34.refs_1_ = bf16[128,512]{1,0:T(8,128)(2,1)S(1)} collective-permute-done((bf16[128,512]{1,0:T(8,128)(2,1)S(1)}, bf16[128,512]{1,0:T(8,128)(2,1)S(1)}, u32[]{:S(2)}, u32[]{:S(2)}) %collective-permute-start.34) | collective-permute-done | bytes 131104 | tf_op jit(solution)/shard_map/ppermute | solution.py:549
  153.6 5.6 %collective-permute-done.35.refs_2_ = bf16[128,512]{1,0:T(8,128)(2,1)S(1)} collective-permute-done((bf16[128,512]{1,0:T(8,128)(2,1)S(1)}, bf16[128,512]{1,0:T(8,128)(2,1)S(1)}, u32[]{:S(2)}, u32[]{:S(2)}) %collective-permute-start.35) | collective-permute-done | bytes 131104 | tf_op jit(solution)/shard_map/ppermute | solution.py:549
  159.3 2.9 %collective-permute-start.32 = (bf16[128,512]{1,0:T(8,128)(2,1)S(1)}, bf16[128,512]{1,0:T(8,128)(2,1)}, u32[]{:S(2)}, u32[]{:S(2)}) collective-permute-start(bf16[128,512]{1,0:T(8,128)(2,1)S(1)} %get-tuple-element.124), channel_id=1, source_target_pairs={{0,12},{4,0},{8,4},{12,8},{1,13},{5,1},{9,5},{13,9},{2,14},{6,2},{... | collective-permute-start | bytes 393224 | tf_op jit(solution)/shard_map/ppermute | solution.py:549
  162.1 1.8 %input_own.1.refs_1_.refs_4_ = bf16[1024,512]{1,0:T(8,128)(2,1)S(1)} custom-call(s32[4]{0:T(128)S(1)} %pad_add_fusion.refs_0_, bf16[1024,512]{1,0:T(8,128)(2,1)S(1)} %get-tuple-element.116.refs_2_.refs_1_, bf16[1024,512]{1,0:T(8,128)(2,1)S(1)} %get-tuple-element.117.refs_2_, bf16[1024,512]{1,0:T(8,128)(2,1)S(1)} %copy-done, bf16[1024,512]{1,0:T(8,128)(2,1)S(1)} %copy-done.7, ...), custom_call_target="tpu_custom_call" | custom-call | flops 1073741824 | bytes 5242896 | tf_op jit(solution)/shard_map/input_own/pallas_call | solution.py:521
  164.0 1.0 copy-done.1
  165.0 1.9 %value_sum.1 = f32[128,512]{1,0:T(8,128)} custom-call(bf16[128,512]{1,0:T(8,128)(2,1)} %copy-done.9, bf16[128,512]{1,0:T(8,128)(2,1)} %copy-done.12, bf16[128,512]{1,0:T(8,128)(2,1)} %copy-done.13, bf16[128,512]{1,0:T(8,128)(2,1)} %collective-permute-done.36.refs_3_, bf16[1024,512]{1,0:T(8,128)(2,1)} %copy-done.1), custom_call_target="tpu_custom_call" | custom-call | bytes 786432 | tf_op jit(solution)/shard_map/value_sum/pallas_call | solution.py:521
  167.0 3.5 %input_sum.1.refs_4_ = bf16[1024,512]{1,0:T(8,128)(2,1)} custom-call(bf16[1024,1024]{1,0:T(8,128)(2,1)S(1)} %copy-done.5, bf16[1024,512]{1,0:T(8,128)(2,1)S(1)} %copy-done.2, bf16[1024,512]{1,0:T(8,128)(2,1)} %collective-permute-done.29.refs_2_), custom_call_target="tpu_custom_call" | custom-call | flops 1073741824 | bytes 5242880 | tf_op jit(solution)/shard_map/input_sum/pallas_call | solution.py:521
  170.4 1.9 %query_sum.1 = f32[128,512]{1,0:T(8,128)} custom-call(bf16[128,512]{1,0:T(8,128)(2,1)} %copy-done.8, bf16[128,512]{1,0:T(8,128)(2,1)} %collective-permute-done.30.refs_1_, bf16[128,512]{1,0:T(8,128)(2,1)} %collective-permute-done.31.refs_2_, bf16[128,512]{1,0:T(8,128)(2,1)} %collective-permute-done.32.refs_3_, bf16[1024,512]{1,0:T(8,128)(2,1)} %input_sum.1.refs_4_), custom_call_target="tpu_custom_call" | custom-call | bytes 786432 | tf_op jit(solution)/shard_map/query_sum/pallas_call | solution.py:521
  (69 shorter events, 2.1 us)
Async XLA Ops:
  0.6 9.8 %copy-start = (bf16[1024,512]{1,0:T(8,128)(2,1)S(1)}, bf16[1024,512]{1,0:T(8,128)(2,1)}, u32[]{:S(2)}) copy-start(bf16[1024,512]{1,0:T(8,128)(2,1)} %refs_3_.7) | copy-start | bytes 3145732
  0.6 9.8 %copy-start.3 = (bf16[1024,1024]{1,0:T(8,128)(2,1)S(1)}, bf16[1024,1024]{1,0:T(8,128)(2,1)}, u32[]{:S(2)}) copy-start(bf16[1024,1024]{1,0:T(8,128)(2,1)} %refs_2_.4) | copy-start | bytes 6291460
  0.7 9.8 %copy-start.10 = (s32[1024,1]{0,1:T(1,128)S(1)}, s32[1024,1]{0,1:T(1,128)}, u32[]{:S(2)}) copy-start(s32[1024,1]{0,1:T(1,128)} %param.9) | copy-start | bytes 12292
  6.2 34.5 %collective-permute-start = (bf16[1040,128]{1,0:T(8,128)(2,1)}, bf16[1040,128]{1,0:T(8,128)(2,1)S(1)}, u32[]{:S(2)}, u32[]{:S(2)}) collective-permute-start(bf16[1040,128]{1,0:T(8,128)(2,1)} %get-tuple-element.75), channel_id=1, source_target_pairs={{0,8},{8,0},{9,1},{4,12},{5,13},{12,4},{13,5},{1,9},{2,10},{10,2},... | collective-permute-start | bytes 798728 | tf_op jit(solution)/shard_map/ppermute | solution.py:543
  10.3 34.5 %collective-permute-start.1 = (bf16[1040,128]{1,0:T(8,128)(2,1)}, bf16[1040,128]{1,0:T(8,128)(2,1)}, u32[]{:S(2)}, u32[]{:S(2)}) collective-permute-start(bf16[1040,128]{1,0:T(8,128)(2,1)} %get-tuple-element.76), channel_id=1, source_target_pairs={{0,9},{8,1},{9,0},{4,13},{5,12},{12,5},{13,4},{1,8},{2,11},{10,3},... | collective-permute-start | bytes 798728 | tf_op jit(solution)/shard_map/ppermute | solution.py:543
  12.3 33.9 %copy-start.7 = (bf16[1024,512]{1,0:T(8,128)(2,1)S(1)}, bf16[1024,512]{1,0:T(8,128)(2,1)}, u32[]{:S(2)}) copy-start(bf16[1024,512]{1,0:T(8,128)(2,1)} %refs_4_.3) | copy-start | bytes 3145732
  17.2 35.1 %collective-permute-start.3 = (bf16[1040,128]{1,0:T(8,128)(2,1)S(1)}, bf16[1040,128]{1,0:T(8,128)(2,1)S(1)}, u32[]{:S(2)}, u32[]{:S(2)}) collective-permute-start(bf16[1040,128]{1,0:T(8,128)(2,1)S(1)} %get-tuple-element.77), channel_id=1, source_target_pairs={{0,5},{8,13},{9,12},{4,9},{5,8},{12,1},{13,0},{1,4},{2,7},{10,15},... | collective-permute-start | bytes 798728 | tf_op jit(solution)/shard_map/ppermute | solution.py:543
  18.9 33.5 %collective-permute-start.2 = (bf16[1040,128]{1,0:T(8,128)(2,1)S(1)}, bf16[1040,128]{1,0:T(8,128)(2,1)S(1)}, u32[]{:S(2)}, u32[]{:S(2)}) collective-permute-start(bf16[1040,128]{1,0:T(8,128)(2,1)S(1)} %get-tuple-element.71.refs_4_), channel_id=1, source_target_pairs={{0,4},{8,12},{9,13},{4,8},{5,9},{12,0},{13,1},{1,5},{2,6},{10,14},... | collective-permute-start | bytes 798728 | tf_op jit(solution)/shard_map/ppermute | solution.py:543
  20.4 35.6 %collective-permute-start.4 = (bf16[1040,128]{1,0:T(8,128)(2,1)S(1)}, bf16[1040,128]{1,0:T(8,128)(2,1)S(1)}, u32[]{:S(2)}, u32[]{:S(2)}) collective-permute-start(bf16[1040,128]{1,0:T(8,128)(2,1)S(1)} %get-tuple-element.78), channel_id=1, source_target_pairs={{0,12},{8,4},{9,5},{4,0},{5,1},{12,8},{13,9},{1,13},{2,14},{10,6},... | collective-permute-start | bytes 798728 | tf_op jit(solution)/shard_map/ppermute | solution.py:543
  40.7 15.3 %collective-permute-start.5 = (bf16[1040,128]{1,0:T(8,128)(2,1)S(1)}, bf16[1040,128]{1,0:T(8,128)(2,1)S(1)}, u32[]{:S(2)}, u32[]{:S(2)}) collective-permute-start(bf16[1040,128]{1,0:T(8,128)(2,1)S(1)} %get-tuple-element.79), channel_id=1, source_target_pairs={{0,13},{8,5},{9,4},{4,1},{5,0},{12,9},{13,8},{1,12},{2,15},{10,7},... | collective-permute-start | bytes 798728 | tf_op jit(solution)/shard_map/ppermute | solution.py:543
  44.8 11.2 %collective-permute-start.6 = (bf16[1040,128]{1,0:T(8,128)(2,1)S(1)}, bf16[1040,128]{1,0:T(8,128)(2,1)S(1)}, u32[]{:S(2)}, u32[]{:S(2)}) collective-permute-start(bf16[1040,128]{1,0:T(8,128)(2,1)S(1)} %get-tuple-element.80), channel_id=1, source_target_pairs={{0,1},{8,9},{9,8},{4,5},{5,4},{12,13},{13,12},{1,0},{2,3},{10,11},... | collective-permute-start | bytes 798728 | tf_op jit(solution)/shard_map/ppermute | solution.py:543
  52.3 26.4 %copy-start.4 = (bf16[1024,1024]{1,0:T(8,128)(2,1)}, bf16[1024,1024]{1,0:T(8,128)(2,1)S(1)}, u32[]{:S(2)}) copy-start(bf16[1024,1024]{1,0:T(8,128)(2,1)S(1)} %get-tuple-element.72.refs_9_.refs_0_) | copy-start | bytes 6291460
  52.3 8.4 %collective-permute-start.20 = (bf16[512,128]{1,0:T(8,128)(2,1)S(1)}, bf16[512,128]{1,0:T(8,128)(2,1)S(1)}, u32[]{:S(2)}, u32[]{:S(2)}) collective-permute-start(bf16[512,128]{1,0:T(8,128)(2,1)S(1)} %get-tuple-element.107), channel_id=1, source_target_pairs={{0,1},{8,9},{9,8},{4,5},{5,4},{12,13},{13,12},{1,0},{2,3},{10,11},... | collective-permute-start | bytes 393224 | tf_op jit(solution)/shard_map/ppermute | solution.py:543
  52.4 12.1 %collective-permute-start.19 = (bf16[512,128]{1,0:T(8,128)(2,1)S(1)}, bf16[512,128]{1,0:T(8,128)(2,1)S(1)}, u32[]{:S(2)}, u32[]{:S(2)}) collective-permute-start(bf16[512,128]{1,0:T(8,128)(2,1)S(1)} %get-tuple-element.105), channel_id=1, source_target_pairs={{0,13},{8,5},{9,4},{4,1},{5,0},{12,9},{13,8},{1,12},{2,15},{10,7},... | collective-permute-start | bytes 393224 | tf_op jit(solution)/shard_map/ppermute | solution.py:543
  56.0 22.7 %collective-permute-start.18 = (bf16[512,128]{1,0:T(8,128)(2,1)S(1)}, bf16[512,128]{1,0:T(8,128)(2,1)S(1)}, u32[]{:S(2)}, u32[]{:S(2)}) collective-permute-start(bf16[512,128]{1,0:T(8,128)(2,1)S(1)} %get-tuple-element.103), channel_id=1, source_target_pairs={{0,12},{8,4},{9,5},{4,0},{5,1},{12,8},{13,9},{1,13},{2,14},{10,6},... | collective-permute-start | bytes 393224 | tf_op jit(solution)/shard_map/ppermute | solution.py:543
  60.7 20.3 %collective-permute-start.17 = (bf16[512,128]{1,0:T(8,128)(2,1)S(1)}, bf16[512,128]{1,0:T(8,128)(2,1)S(1)}, u32[]{:S(2)}, u32[]{:S(2)}) collective-permute-start(bf16[512,128]{1,0:T(8,128)(2,1)S(1)} %get-tuple-element.101), channel_id=1, source_target_pairs={{0,5},{8,13},{9,12},{4,9},{5,8},{12,1},{13,0},{1,4},{2,7},{10,15},... | collective-permute-start | bytes 393224 | tf_op jit(solution)/shard_map/ppermute | solution.py:543
  60.7 20.4 %collective-permute-start.16 = (bf16[512,128]{1,0:T(8,128)(2,1)S(1)}, bf16[512,128]{1,0:T(8,128)(2,1)S(1)}, u32[]{:S(2)}, u32[]{:S(2)}) collective-permute-start(bf16[512,128]{1,0:T(8,128)(2,1)S(1)} %get-tuple-element.99), channel_id=1, source_target_pairs={{0,4},{8,12},{9,13},{4,8},{5,9},{12,0},{13,1},{1,5},{2,6},{10,14},... | collective-permute-start | bytes 393224 | tf_op jit(solution)/shard_map/ppermute | solution.py:543
  60.7 20.6 %collective-permute-start.15 = (bf16[512,128]{1,0:T(8,128)(2,1)S(1)}, bf16[512,128]{1,0:T(8,128)(2,1)S(1)}, u32[]{:S(2)}, u32[]{:S(2)}) collective-permute-start(bf16[512,128]{1,0:T(8,128)(2,1)S(1)} %get-tuple-element.97), channel_id=1, source_target_pairs={{0,9},{8,1},{9,0},{4,13},{5,12},{12,5},{13,4},{1,8},{2,11},{10,3},... | collective-permute-start | bytes 393224 | tf_op jit(solution)/shard_map/ppermute | solution.py:543
  64.6 30.0 %collective-permute-start.14 = (bf16[512,128]{1,0:T(8,128)(2,1)S(1)}, bf16[512,128]{1,0:T(8,128)(2,1)S(1)}, u32[]{:S(2)}, u32[]{:S(2)}) collective-permute-start(bf16[512,128]{1,0:T(8,128)(2,1)S(1)} %get-tuple-element.95), channel_id=1, source_target_pairs={{0,8},{8,0},{9,1},{4,12},{5,13},{12,4},{13,5},{1,9},{2,10},{10,2},... | collective-permute-start | bytes 393224 | tf_op jit(solution)/shard_map/ppermute | solution.py:543
  78.7 31.7 %collective-permute-start.7 = (bf16[512,128]{1,0:T(8,128)(2,1)S(1)}, bf16[512,128]{1,0:T(8,128)(2,1)S(1)}, u32[]{:S(2)}, u32[]{:S(2)}) collective-permute-start(bf16[512,128]{1,0:T(8,128)(2,1)S(1)} %get-tuple-element.82), channel_id=1, source_target_pairs={{0,8},{8,0},{9,1},{4,12},{5,13},{12,4},{13,5},{1,9},{2,10},{10,2},... | collective-permute-start | bytes 393224 | tf_op jit(solution)/shard_map/ppermute | solution.py:543
  81.0 31.0 %collective-permute-start.8 = (bf16[512,128]{1,0:T(8,128)(2,1)S(1)}, bf16[512,128]{1,0:T(8,128)(2,1)S(1)}, u32[]{:S(2)}, u32[]{:S(2)}) collective-permute-start(bf16[512,128]{1,0:T(8,128)(2,1)S(1)} %get-tuple-element.83), channel_id=1, source_target_pairs={{0,9},{8,1},{9,0},{4,13},{5,12},{12,5},{13,4},{1,8},{2,11},{10,3},... | collective-permute-start | bytes 393224 | tf_op jit(solution)/shard_map/ppermute | solution.py:543
  81.2 30.8 %collective-permute-start.9 = (bf16[512,128]{1,0:T(8,128)(2,1)S(1)}, bf16[512,128]{1,0:T(8,128)(2,1)S(1)}, u32[]{:S(2)}, u32[]{:S(2)}) collective-permute-start(bf16[512,128]{1,0:T(8,128)(2,1)S(1)} %get-tuple-element.84), channel_id=1, source_target_pairs={{0,4},{8,12},{9,13},{4,8},{5,9},{12,0},{13,1},{1,5},{2,6},{10,14},... | collective-permute-start | bytes 393224 | tf_op jit(solution)/shard_map/ppermute | solution.py:543
  81.3 32.9 %collective-permute-start.10 = (bf16[512,128]{1,0:T(8,128)(2,1)S(1)}, bf16[512,128]{1,0:T(8,128)(2,1)S(1)}, u32[]{:S(2)}, u32[]{:S(2)}) collective-permute-start(bf16[512,128]{1,0:T(8,128)(2,1)S(1)} %get-tuple-element.85), channel_id=1, source_target_pairs={{0,5},{8,13},{9,12},{4,9},{5,8},{12,1},{13,0},{1,4},{2,7},{10,15},... | collective-permute-start | bytes 393224 | tf_op jit(solution)/shard_map/ppermute | solution.py:543
  110.3 18.0 %collective-permute-start.21 = (bf16[544,128]{1,0:T(8,128)(2,1)S(1)}, bf16[544,128]{1,0:T(8,128)(2,1)S(1)}, u32[]{:S(2)}, u32[]{:S(2)}) collective-permute-start(bf16[544,128]{1,0:T(8,128)(2,1)S(1)} %get-tuple-element.109), channel_id=1, source_target_pairs={{0,8},{8,0},{9,1},{4,12},{5,13},{12,4},{13,5},{1,9},{2,10},{10,2},... | collective-permute-start | bytes 417800 | tf_op jit(solution)/shard_map/ppermute | solution.py:543
  110.4 18.1 %collective-permute-start.22 = (bf16[544,128]{1,0:T(8,128)(2,1)S(1)}, bf16[544,128]{1,0:T(8,128)(2,1)S(1)}, u32[]{:S(2)}, u32[]{:S(2)}) collective-permute-start(bf16[544,128]{1,0:T(8,128)(2,1)S(1)} %get-tuple-element.110), channel_id=1, source_target_pairs={{0,9},{8,1},{9,0},{4,13},{5,12},{12,5},{13,4},{1,8},{2,11},{10,3},... | collective-permute-start | bytes 417800 | tf_op jit(solution)/shard_map/ppermute | solution.py:543
  112.0 10.0 %collective-permute-start.11 = (bf16[512,128]{1,0:T(8,128)(2,1)S(1)}, bf16[512,128]{1,0:T(8,128)(2,1)S(1)}, u32[]{:S(2)}, u32[]{:S(2)}) collective-permute-start(bf16[512,128]{1,0:T(8,128)(2,1)S(1)} %get-tuple-element.86), channel_id=1, source_target_pairs={{0,12},{8,4},{9,5},{4,0},{5,1},{12,8},{13,9},{1,13},{2,14},{10,6},... | collective-permute-start | bytes 393224 | tf_op jit(solution)/shard_map/ppermute | solution.py:543
  112.0 12.8 %collective-permute-start.12 = (bf16[512,128]{1,0:T(8,128)(2,1)S(1)}, bf16[512,128]{1,0:T(8,128)(2,1)S(1)}, u32[]{:S(2)}, u32[]{:S(2)}) collective-permute-start(bf16[512,128]{1,0:T(8,128)(2,1)S(1)} %get-tuple-element.87), channel_id=1, source_target_pairs={{0,13},{8,5},{9,4},{4,1},{5,0},{12,9},{13,8},{1,12},{2,15},{10,7},... | collective-permute-start | bytes 393224 | tf_op jit(solution)/shard_map/ppermute | solution.py:543
  114.3 10.6 %collective-permute-start.13 = (bf16[512,128]{1,0:T(8,128)(2,1)S(1)}, bf16[512,128]{1,0:T(8,128)(2,1)S(1)}, u32[]{:S(2)}, u32[]{:S(2)}) collective-permute-start(bf16[512,128]{1,0:T(8,128)(2,1)S(1)} %get-tuple-element.88), channel_id=1, source_target_pairs={{0,1},{8,9},{9,8},{4,5},{5,4},{12,13},{13,12},{1,0},{2,3},{10,11},... | collective-permute-start | bytes 393224 | tf_op jit(solution)/shard_map/ppermute | solution.py:543
  122.0 9.1 %collective-permute-start.23 = (bf16[544,128]{1,0:T(8,128)(2,1)S(1)}, bf16[544,128]{1,0:T(8,128)(2,1)S(1)}, u32[]{:S(2)}, u32[]{:S(2)}) collective-permute-start(bf16[544,128]{1,0:T(8,128)(2,1)S(1)} %get-tuple-element.111), channel_id=1, source_target_pairs={{0,4},{8,12},{9,13},{4,8},{5,9},{12,0},{13,1},{1,5},{2,6},{10,14},... | collective-permute-start | bytes 417800 | tf_op jit(solution)/shard_map/ppermute | solution.py:543
  124.8 7.6 %collective-permute-start.24 = (bf16[544,128]{1,0:T(8,128)(2,1)S(1)}, bf16[544,128]{1,0:T(8,128)(2,1)S(1)}, u32[]{:S(2)}, u32[]{:S(2)}) collective-permute-start(bf16[544,128]{1,0:T(8,128)(2,1)S(1)} %get-tuple-element.112), channel_id=1, source_target_pairs={{0,5},{8,13},{9,12},{4,9},{5,8},{12,1},{13,0},{1,4},{2,7},{10,15},... | collective-permute-start | bytes 417800 | tf_op jit(solution)/shard_map/ppermute | solution.py:543
  124.9 10.7 %collective-permute-start.25 = (bf16[544,128]{1,0:T(8,128)(2,1)S(1)}, bf16[544,128]{1,0:T(8,128)(2,1)S(1)}, u32[]{:S(2)}, u32[]{:S(2)}) collective-permute-start(bf16[544,128]{1,0:T(8,128)(2,1)S(1)} %get-tuple-element.113), channel_id=1, source_target_pairs={{0,12},{8,4},{9,5},{4,0},{5,1},{12,8},{13,9},{1,13},{2,14},{10,6},... | collective-permute-start | bytes 417800 | tf_op jit(solution)/shard_map/ppermute | solution.py:543
  128.3 10.0 %collective-permute-start.26 = (bf16[544,128]{1,0:T(8,128)(2,1)S(1)}, bf16[544,128]{1,0:T(8,128)(2,1)S(1)}, u32[]{:S(2)}, u32[]{:S(2)}) collective-permute-start(bf16[544,128]{1,0:T(8,128)(2,1)S(1)} %get-tuple-element.114), channel_id=1, source_target_pairs={{0,13},{8,5},{9,4},{4,1},{5,0},{12,9},{13,8},{1,12},{2,15},{10,7},... | collective-permute-start | bytes 417800 | tf_op jit(solution)/shard_map/ppermute | solution.py:543
  128.4 9.9 %collective-permute-start.27 = (bf16[544,128]{1,0:T(8,128)(2,1)S(1)}, bf16[544,128]{1,0:T(8,128)(2,1)S(1)}, u32[]{:S(2)}, u32[]{:S(2)}) collective-permute-start(bf16[544,128]{1,0:T(8,128)(2,1)S(1)} %get-tuple-element.115), channel_id=1, source_target_pairs={{0,1},{8,9},{9,8},{4,5},{5,4},{12,13},{13,12},{1,0},{2,3},{10,11},... | collective-permute-start | bytes 417800 | tf_op jit(solution)/shard_map/ppermute | solution.py:543
  140.7 26.2 %collective-permute-start.29 = (bf16[1024,512]{1,0:T(8,128)(2,1)}, bf16[1024,512]{1,0:T(8,128)(2,1)}, u32[]{:S(2)}, u32[]{:S(2)}) collective-permute-start(bf16[1024,512]{1,0:T(8,128)(2,1)} %get-tuple-element.121), channel_id=1, source_target_pairs={{0,2},{2,0},{1,3},{3,1},{4,6},{6,4},{5,7},{7,5},{8,10},{10,8},{9,1... | collective-permute-start | bytes 3145736 | tf_op jit(solution)/shard_map/ppermute | solution.py:549
  142.2 2.4 %collective-permute-start.33 = (bf16[4,128,512]{2,1,0:T(8,128)(2,1)S(1)}, bf16[4,128,512]{2,1,0:T(8,128)(2,1)S(1)}, u32[]{:S(2)}, u32[]{:S(2)}) collective-permute-start(bf16[4,128,512]{2,1,0:T(8,128)(2,1)S(1)} %get-tuple-element.126), channel_id=1, source_target_pairs={{0,1},{1,0},{2,3},{3,2},{4,5},{5,4},{6,7},{7,6},{8,9},{9,8},{10,11... | collective-permute-start | bytes 1572872 | tf_op jit(solution)/shard_map/ppermute | solution.py:549
  144.0 5.1 %collective-permute-start.28 = (bf16[4,128,512]{2,1,0:T(8,128)(2,1)S(1)}, bf16[4,128,512]{2,1,0:T(8,128)(2,1)S(1)}, u32[]{:S(2)}, u32[]{:S(2)}) collective-permute-start(bf16[4,128,512]{2,1,0:T(8,128)(2,1)S(1)} %get-tuple-element.119), channel_id=1, source_target_pairs={{0,1},{1,0},{2,3},{3,2},{4,5},{5,4},{6,7},{7,6},{8,9},{9,8},{10,11... | collective-permute-start | bytes 1572872 | tf_op jit(solution)/shard_map/ppermute | solution.py:549
  145.3 18.7 %copy-start.9 = (bf16[128,512]{1,0:T(8,128)(2,1)}, bf16[128,512]{1,0:T(8,128)(2,1)S(1)}, u32[]{:S(2)}) copy-start(bf16[128,512]{1,0:T(8,128)(2,1)S(1)} %get-tuple-element.131.refs_0_) | copy-start | bytes 393220
  145.3 8.3 %collective-permute-start.34 = (bf16[128,512]{1,0:T(8,128)(2,1)S(1)}, bf16[128,512]{1,0:T(8,128)(2,1)S(1)}, u32[]{:S(2)}, u32[]{:S(2)}) collective-permute-start(bf16[128,512]{1,0:T(8,128)(2,1)S(1)} %get-tuple-element.132), channel_id=1, source_target_pairs={{0,4},{4,8},{8,12},{12,0},{1,5},{5,9},{9,13},{13,1},{2,6},{6,10},{... | collective-permute-start | bytes 393224 | tf_op jit(solution)/shard_map/ppermute | solution.py:549
  146.0 13.3 %collective-permute-start.35 = (bf16[128,512]{1,0:T(8,128)(2,1)S(1)}, bf16[128,512]{1,0:T(8,128)(2,1)S(1)}, u32[]{:S(2)}, u32[]{:S(2)}) collective-permute-start(bf16[128,512]{1,0:T(8,128)(2,1)S(1)} %get-tuple-element.133), channel_id=1, source_target_pairs={{0,8},{4,12},{8,0},{12,4},{1,9},{5,13},{9,1},{13,5},{2,10},{6,14},... | collective-permute-start | bytes 393224 | tf_op jit(solution)/shard_map/ppermute | solution.py:549
  146.8 18.2 %collective-permute-start.36 = (bf16[128,512]{1,0:T(8,128)(2,1)S(1)}, bf16[128,512]{1,0:T(8,128)(2,1)}, u32[]{:S(2)}, u32[]{:S(2)}) collective-permute-start(bf16[128,512]{1,0:T(8,128)(2,1)S(1)} %get-tuple-element.134), channel_id=1, source_target_pairs={{0,12},{4,0},{8,4},{12,8},{1,13},{5,1},{9,5},{13,9},{2,14},{6,2},{... | collective-permute-start | bytes 393224 | tf_op jit(solution)/shard_map/ppermute | solution.py:549
  150.4 13.6 %copy-start.8 = (bf16[128,512]{1,0:T(8,128)(2,1)}, bf16[128,512]{1,0:T(8,128)(2,1)S(1)}, u32[]{:S(2)}) copy-start(bf16[128,512]{1,0:T(8,128)(2,1)S(1)} %get-tuple-element.120.refs_5_.refs_0_) | copy-start | bytes 393220
  150.4 20.0 %collective-permute-start.30 = (bf16[128,512]{1,0:T(8,128)(2,1)}, bf16[128,512]{1,0:T(8,128)(2,1)}, u32[]{:S(2)}, u32[]{:S(2)}) collective-permute-start(bf16[128,512]{1,0:T(8,128)(2,1)} %get-tuple-element.122), channel_id=1, source_target_pairs={{0,4},{4,8},{8,12},{12,0},{1,5},{5,9},{9,13},{13,1},{2,6},{6,10},{... | collective-permute-start | bytes 393224 | tf_op jit(solution)/shard_map/ppermute | solution.py:549
  153.6 10.4 %copy-start.12 = (bf16[128,512]{1,0:T(8,128)(2,1)}, bf16[128,512]{1,0:T(8,128)(2,1)S(1)}, u32[]{:S(2)}) copy-start(bf16[128,512]{1,0:T(8,128)(2,1)S(1)} %collective-permute-done.34.refs_1_) | copy-start | bytes 393220
  153.6 16.8 %collective-permute-start.31 = (bf16[128,512]{1,0:T(8,128)(2,1)S(1)}, bf16[128,512]{1,0:T(8,128)(2,1)}, u32[]{:S(2)}, u32[]{:S(2)}) collective-permute-start(bf16[128,512]{1,0:T(8,128)(2,1)S(1)} %get-tuple-element.123), channel_id=1, source_target_pairs={{0,8},{4,12},{8,0},{12,4},{1,9},{5,13},{9,1},{13,5},{2,10},{6,14},... | collective-permute-start | bytes 393224 | tf_op jit(solution)/shard_map/ppermute | solution.py:549
  159.3 4.7 %copy-start.13 = (bf16[128,512]{1,0:T(8,128)(2,1)}, bf16[128,512]{1,0:T(8,128)(2,1)S(1)}, u32[]{:S(2)}) copy-start(bf16[128,512]{1,0:T(8,128)(2,1)S(1)} %collective-permute-done.35.refs_2_) | copy-start | bytes 393220
  159.3 11.2 %collective-permute-start.32 = (bf16[128,512]{1,0:T(8,128)(2,1)S(1)}, bf16[128,512]{1,0:T(8,128)(2,1)}, u32[]{:S(2)}, u32[]{:S(2)}) collective-permute-start(bf16[128,512]{1,0:T(8,128)(2,1)S(1)} %get-tuple-element.124), channel_id=1, source_target_pairs={{0,12},{4,0},{8,4},{12,8},{1,13},{5,1},{9,5},{13,9},{2,14},{6,2},{... | collective-permute-start | bytes 393224 | tf_op jit(solution)/shard_map/ppermute | solution.py:549
  162.1 4.8 %copy-start.5 = (bf16[1024,1024]{1,0:T(8,128)(2,1)S(1)}, bf16[1024,1024]{1,0:T(8,128)(2,1)}, u32[]{:S(2)}) copy-start(bf16[1024,1024]{1,0:T(8,128)(2,1)} %copy-done.4) | copy-start | bytes 6291460
  165.0 2.0 %copy-start.2 = (bf16[1024,512]{1,0:T(8,128)(2,1)S(1)}, bf16[1024,512]{1,0:T(8,128)(2,1)}, u32[]{:S(2)}) copy-start(bf16[1024,512]{1,0:T(8,128)(2,1)} %copy-done.1) | copy-start | bytes 3145732
  (3 other events, 2.9 us)

commit v15 on v13

--- a/solution.py
+++ b/solution.py
@@ -497,13 +497,14 @@
     refs[-1][...] = total.astype(refs[-1].dtype)
 
 
-def input_sum_kernel(unsort_ref, *refs):
-    part_refs, out_ref, total_ref = refs[:-2], refs[-2], refs[-1]
+def input_sum_kernel(unsort_ref, weight_ref, *refs):
+    part_refs, out_ref, weight_out_ref, total_ref = refs[:-3], refs[-3], refs[-2], refs[-1]
     total = part_refs[0][...].astype(F32)
     for part_ref in part_refs[1:]:
         total = total + part_ref[...].astype(F32)
     total_ref[...] = total.astype(BF16)
     out_ref[...] = dot(unsort_ref[...], total_ref[...]).astype(BF16)
+    weight_out_ref[...] = weight_ref[...]
 
 
 def call(kernel, outs, inputs, smem=(0,), in_place=(), after=(), scratch=(), flops=0, vmem=24, name=None):
@@ -671,7 +672,8 @@
     home_query = exchange(back_query, sizes)
     weight_flops = 2 * slots * width * width_dev
     home_flops = weight_flops // parts * (parts - 1)
-    sub_shapes = several(sizes[1], sizes[0], width // owners, width_dev)
+    piece = width // owners
+    sub_shapes = several(sizes[1], sizes[0], piece, width_dev)
     value_rows, *refs = call(
         functools.partial(value_home_kernel, sizes, heads, parts),
         several(1, slots, width_dev) + (shape((slots, columns), F32),) * (parts - 1) + sub_shapes,
@@ -713,16 +715,16 @@
     )
     query_weight = pass_round(query_weight, "seq")
     grad_wv = add_up(value_weight, F32, "value_sum", [own])
-    grad_input = call(
+    grad_input, own_weight = call(
         input_sum_kernel,
-        shape((toks, columns), BF16),
-        (unsort, own, *arrived),
+        several(1, toks, columns) + several(1, piece, width_dev),
+        (unsort, query_weight[0], own, *arrived),
         smem=(),
         scratch=[pltpu.VMEM((slots, columns), BF16)],
         flops=2 * toks * slots * columns,
         name="input_sum",
     )
-    grad_wq = add_up(query_weight, F32, "query_sum", [grad_input])
+    grad_wq = add_up([own_weight, *query_weight[1:]], F32, "query_sum")
     if groups > 1:
         centroid_grad = centroid_grad.reshape(groups, 2 * extra, width_dev)[:, :per_group]
         centroid_grad = centroid_grad.reshape(CLUSTERS, width_dev)

time: 172 us -> 171 us (level)
  no operation moved by 1% of the time
where the time goes in v15:
time: 171 us; the launch traced here: 170 us
  Pallas kernels  59.1 us (35%)
  waiting for transfers between devices  59 us (35%)
  starting transfers between devices  47.8 us (28%)
  local copies, waits for them, and re-layouts  3.23 us (2%)
    pallas_call x14, Pallas kernels, call(): pl.pallas_call(body, out_shape=outs, in_specs=specs, out_specs=jax.tree.m...  59.1 us
    ppermute x28, waiting for transfers between devices, exchange(): out.append(part if ahead == (0, 0) else lax.ppermute(part, OWNERS, moves))  47.7 us
    ppermute x28, starting transfers between devices, exchange(): out.append(part if ahead == (0, 0) else lax.ppermute(part, OWNERS, moves))  38.4 us
    ppermute x9, waiting for transfers between devices, shift(): lax.ppermute(part, axis, [(i, (i + ahead) % size) for i in range(size)])  11.4 us
    ppermute x9, starting transfers between devices, shift(): lax.ppermute(part, axis, [(i, (i + ahead) % size) for i in range(size)])  9.43 us
  transfers between devices with their start and end apart: 37, of which 12 were waited for; matrix products, arithmetic and copies ran while one was open for 0% of the time, Pallas kernels for 30%

profile of v15, /device:TPU:0, one launch (start us, length us, event | category | flops | bytes accessed | tf_op | source)
XLA Modules:
  0.0 170.1 jit_solution(126728798202922358)
XLA Ops:
  0.7 5.6 %project_far.1 = (bf16[1040,128]{1,0:T(8,128)(2,1)}, bf16[1040,128]{1,0:T(8,128)(2,1)}, s32[1,1024]{1,0:T(1,128)}) custom-call(s32[1,1024]{1,0:T(1,128)} %bitcast.5, bf16[1024,1024]{1,0:T(8,128)(2,1)} %refs_2_.4, bf16[1024,512]{1,0:T(8,128)(2,1)} %refs_3_.7, bf16[1024,512]{1,0:T(8,128)(2,1)} %refs_5_.1), custom_call_target="tpu_custom_call" | custom-call | flops 805306368 | bytes 4734976 | tf_op jit(solution)/shard_map/project_far/pallas_call | solution.py:522
  6.2 4.1 %collective-permute-start = (bf16[1040,128]{1,0:T(8,128)(2,1)}, bf16[1040,128]{1,0:T(8,128)(2,1)S(1)}, u32[]{:S(2)}, u32[]{:S(2)}) collective-permute-start(bf16[1040,128]{1,0:T(8,128)(2,1)} %get-tuple-element.77), channel_id=1, source_target_pairs={{0,8},{8,0},{9,1},{4,12},{5,13},{12,4},{13,5},{1,9},{2,10},{10,2},... | collective-permute-start | bytes 798728 | tf_op jit(solution)/shard_map/ppermute | solution.py:544
  10.4 1.2 copy-done.2
  11.7 0.7 copy-done.5
  12.4 4.8 %project_query.1 = (bf16[1040,128]{1,0:T(8,128)(2,1)S(1)}, bf16[1040,128]{1,0:T(8,128)(2,1)S(1)}, bf16[1040,128]{1,0:T(8,128)(2,1)S(1)}, bf16[1040,128]{1,0:T(8,...) custom-call(s32[4]{0:T(128)S(1)} %pad_add_fusion.refs_0_, s32[1,1024]{1,0:T(1,128)S(1)} %copy-done.5, ...), custom_call_target="tpu_custom_call" | custom-call | flops 3221225472 | bytes 5799952 | tf_op jit(solution)/shard_map/project_query/pallas_call | solution.py:522
  17.2 1.7 collective-permute-start.3
  18.9 1.6 collective-permute-start.2
  20.4 2.2 %collective-permute-start.4 = (bf16[1040,128]{1,0:T(8,128)(2,1)S(1)}, bf16[1040,128]{1,0:T(8,128)(2,1)S(1)}, u32[]{:S(2)}, u32[]{:S(2)}) collective-permute-start(bf16[1040,128]{1,0:T(8,128)(2,1)S(1)} %get-tuple-element.80), channel_id=1, source_target_pairs={{0,12},{8,4},{9,5},{4,0},{5,1},{12,8},{13,9},{1,13},{2,14},{10,6},... | collective-permute-start | bytes 798728 | tf_op jit(solution)/shard_map/ppermute | solution.py:544
  22.7 18.0 %collective-permute-done.refs_2_ = bf16[1040,128]{1,0:T(8,128)(2,1)S(1)} collective-permute-done((bf16[1040,128]{1,0:T(8,128)(2,1)}, bf16[1040,128]{1,0:T(8,128)(2,1)S(1)}, u32[]{:S(2)}, u32[]{:S(2)}) %collective-permute-start) | collective-permute-done | bytes 266272 | tf_op jit(solution)/shard_map/ppermute | solution.py:544
  40.7 4.1 %collective-permute-done.1.refs_3_ = bf16[1040,128]{1,0:T(8,128)(2,1)} collective-permute-done((bf16[1040,128]{1,0:T(8,128)(2,1)}, bf16[1040,128]{1,0:T(8,128)(2,1)}, u32[]{:S(2)}, u32[]{:S(2)}) %collective-permute-start.1) | collective-permute-done | bytes 266272 | tf_op jit(solution)/shard_map/ppermute | solution.py:544
  44.8 1.4 collective-permute-start.6
  46.3 6.0 %project_value.1 = (bf16[512,128]{1,0:T(8,128)(2,1)S(1)}, bf16[512,128]{1,0:T(8,128)(2,1)S(1)}, bf16[512,128]{1,0:T(8,128)(2,1)S(1)}, bf16[512,128]{1,0:T(8,128)...) custom-call(s32[4]{0:T(128)S(1)} %pad_add_fusion.refs_0_, ...), custom_call_target="tpu_custom_call" | custom-call | flops 2147483648 | bytes 8392720 | tf_op jit(solution)/shard_map/project_value/pallas_call | solution.py:522
  52.3 1.3 copy-done.6
  53.6 2.4 %collective-permute-start.19 = (bf16[512,128]{1,0:T(8,128)(2,1)S(1)}, bf16[512,128]{1,0:T(8,128)(2,1)S(1)}, u32[]{:S(2)}, u32[]{:S(2)}) collective-permute-start(bf16[512,128]{1,0:T(8,128)(2,1)S(1)} %get-tuple-element.107), channel_id=1, source_target_pairs={{0,13},{8,5},{9,4},{4,1},{5,0},{12,9},{13,8},{1,12},{2,15},{10,7},... | collective-permute-start | bytes 393224 | tf_op jit(solution)/shard_map/ppermute | solution.py:544
  56.0 4.7 %collective-permute-start.18 = (bf16[512,128]{1,0:T(8,128)(2,1)S(1)}, bf16[512,128]{1,0:T(8,128)(2,1)S(1)}, u32[]{:S(2)}, u32[]{:S(2)}) collective-permute-start(bf16[512,128]{1,0:T(8,128)(2,1)S(1)} %get-tuple-element.105), channel_id=1, source_target_pairs={{0,12},{8,4},{9,5},{4,0},{5,1},{12,8},{13,9},{1,13},{2,14},{10,6},... | collective-permute-start | bytes 393224 | tf_op jit(solution)/shard_map/ppermute | solution.py:544
  60.7 3.8 %collective-permute-start.15 = (bf16[512,128]{1,0:T(8,128)(2,1)S(1)}, bf16[512,128]{1,0:T(8,128)(2,1)S(1)}, u32[]{:S(2)}, u32[]{:S(2)}) collective-permute-start(bf16[512,128]{1,0:T(8,128)(2,1)S(1)} %get-tuple-element.99), channel_id=1, source_target_pairs={{0,9},{8,1},{9,0},{4,13},{5,12},{12,5},{13,4},{1,8},{2,11},{10,3},... | collective-permute-start | bytes 393224 | tf_op jit(solution)/shard_map/ppermute | solution.py:544
  65.2 13.5 %value_grad.1 = (bf16[512,128]{1,0:T(8,128)(2,1)S(1)}, bf16[512,128]{1,0:T(8,128)(2,1)S(1)}, bf16[512,128]{1,0:T(8,128)(2,1)S(1)}, bf16[512,128]{1,0:T(8,128)(2,...) custom-call(s32[4]{0:T(128)S(1)} %pad_add_fusion.refs_0_, ...), custom_call_target="tpu_custom_call" | custom-call | flops 2147483648 | bytes 8163344 | tf_op jit(solution)/shard_map/value_grad/pallas_call | solution.py:522
  78.7 2.3 %collective-permute-start.7 = (bf16[512,128]{1,0:T(8,128)(2,1)S(1)}, bf16[512,128]{1,0:T(8,128)(2,1)S(1)}, u32[]{:S(2)}, u32[]{:S(2)}) collective-permute-start(bf16[512,128]{1,0:T(8,128)(2,1)S(1)} %get-tuple-element.84), channel_id=1, source_target_pairs={{0,8},{8,0},{9,1},{4,12},{5,13},{12,4},{13,5},{1,9},{2,10},{10,2},... | collective-permute-start | bytes 393224 | tf_op jit(solution)/shard_map/ppermute | solution.py:544
  81.3 2.6 %collective-permute-start.10 = (bf16[512,128]{1,0:T(8,128)(2,1)S(1)}, bf16[512,128]{1,0:T(8,128)(2,1)S(1)}, u32[]{:S(2)}, u32[]{:S(2)}) collective-permute-start(bf16[512,128]{1,0:T(8,128)(2,1)S(1)} %get-tuple-element.87), channel_id=1, source_target_pairs={{0,5},{8,13},{9,12},{4,9},{5,8},{12,1},{13,0},{1,4},{2,7},{10,15},... | collective-permute-start | bytes 393224 | tf_op jit(solution)/shard_map/ppermute | solution.py:544
  83.9 10.6 %collective-permute-done.14.refs_4_ = bf16[512,128]{1,0:T(8,128)(2,1)S(1)} collective-permute-done((bf16[512,128]{1,0:T(8,128)(2,1)S(1)}, bf16[512,128]{1,0:T(8,128)(2,1)S(1)}, u32[]{:S(2)}, u32[]{:S(2)}) %collective-permute-start.14) | collective-permute-done | bytes 131104 | tf_op jit(solution)/shard_map/ppermute | solution.py:544
  94.5 15.9 %query_grad.1 = (bf16[544,128]{1,0:T(8,128)(2,1)S(1)}, bf16[544,128]{1,0:T(8,128)(2,1)S(1)}, bf16[544,128]{1,0:T(8,128)(2,1)S(1)}, bf16[544,128]{1,0:T(8,128)(2,...) custom-call(s32[4]{0:T(128)S(1)} %pad_add_fusion.refs_0_, ...), custom_call_target="tpu_custom_call" | custom-call | flops 3221225472 | bytes 7147536 | tf_op jit(solution)/shard_map/query_grad/pallas_call | solution.py:522
  110.5 1.6 collective-permute-start.22
  112.2 2.3 %collective-permute-start.12 = (bf16[512,128]{1,0:T(8,128)(2,1)S(1)}, bf16[512,128]{1,0:T(8,128)(2,1)S(1)}, u32[]{:S(2)}, u32[]{:S(2)}) collective-permute-start(bf16[512,128]{1,0:T(8,128)(2,1)S(1)} %get-tuple-element.89), channel_id=1, source_target_pairs={{0,13},{8,5},{9,4},{4,1},{5,0},{12,9},{13,8},{1,12},{2,15},{10,7},... | collective-permute-start | bytes 393224 | tf_op jit(solution)/shard_map/ppermute | solution.py:544
  114.4 0.8 collective-permute-start.13
  115.3 6.9 %collective-permute-done.11.refs_8_ = bf16[512,128]{1,0:T(8,128)(2,1)S(1)} collective-permute-done((bf16[512,128]{1,0:T(8,128)(2,1)S(1)}, bf16[512,128]{1,0:T(8,128)(2,1)S(1)}, u32[]{:S(2)}, u32[]{:S(2)}) %collective-permute-start.11) | collective-permute-done | bytes 131104 | tf_op jit(solution)/shard_map/ppermute | solution.py:544
  122.1 2.0 %collective-permute-start.23 = (bf16[544,128]{1,0:T(8,128)(2,1)S(1)}, bf16[544,128]{1,0:T(8,128)(2,1)S(1)}, u32[]{:S(2)}, u32[]{:S(2)}) collective-permute-start(bf16[544,128]{1,0:T(8,128)(2,1)S(1)} %get-tuple-element.113), channel_id=1, source_target_pairs={{0,4},{8,12},{9,13},{4,8},{5,9},{12,0},{13,1},{1,5},{2,6},{10,14},... | collective-permute-start | bytes 417800 | tf_op jit(solution)/shard_map/ppermute | solution.py:544
  124.2 0.8 collective-permute-done.12.refs_9_
  125.0 3.5 %collective-permute-start.25 = (bf16[544,128]{1,0:T(8,128)(2,1)S(1)}, bf16[544,128]{1,0:T(8,128)(2,1)S(1)}, u32[]{:S(2)}, u32[]{:S(2)}) collective-permute-start(bf16[544,128]{1,0:T(8,128)(2,1)S(1)} %get-tuple-element.115), channel_id=1, source_target_pairs={{0,12},{8,4},{9,5},{4,0},{5,1},{12,8},{13,9},{1,13},{2,14},{10,6},... | collective-permute-start | bytes 417800 | tf_op jit(solution)/shard_map/ppermute | solution.py:544
  128.7 2.5 %value_home.1 = (bf16[1024,512]{1,0:T(8,128)(2,1)S(1)}, f32[1024,512]{1,0:T(8,128)S(1)}, bf16[4,128,512]{2,1,0:T(8,128)(2,1)S(1)}, bf16[4,128,512]{2,1,0:T(8,128)(2,1)S(1)}) custom-call(s32[4]{0:T(128)S(1)} %pad_add_fusion.refs_0_, bf16[1024,1024]{1,0:T(8,128)(2,1)S(1)} %copy-done.7, bf16[1024,512]{1,0:T(8,128)(2,1)S(1)} %copy-done.3, ...), custom_call_target="tpu_custom_call" | custom-call | flops 1610612736 | bytes 8388624 | tf_op jit(solution)/shard_map/value_home/pallas_call | solution.py:522
  131.2 1.4 collective-permute-done.24.refs_7_
  132.6 3.1 %collective-permute-done.25.refs_8_ = bf16[544,128]{1,0:T(8,128)(2,1)S(1)} collective-permute-done((bf16[544,128]{1,0:T(8,128)(2,1)S(1)}, bf16[544,128]{1,0:T(8,128)(2,1)S(1)}, u32[]{:S(2)}, u32[]{:S(2)}) %collective-permute-start.25) | collective-permute-done | bytes 139296 | tf_op jit(solution)/shard_map/ppermute | solution.py:544
  135.7 2.8 %collective-permute-done.26.refs_9_ = bf16[544,128]{1,0:T(8,128)(2,1)S(1)} collective-permute-done((bf16[544,128]{1,0:T(8,128)(2,1)S(1)}, bf16[544,128]{1,0:T(8,128)(2,1)S(1)}, u32[]{:S(2)}, u32[]{:S(2)}) %collective-permute-start.26) | collective-permute-done | bytes 139296 | tf_op jit(solution)/shard_map/ppermute | solution.py:544
  138.5 2.0 %query_home.1 = (bf16[1024,512]{1,0:T(8,128)(2,1)S(1)}, bf16[1024,512]{1,0:T(8,128)(2,1)S(1)}, f32[64,512]{1,0:T(8,128)}) custom-call(s32[4]{0:T(128)S(1)} %pad_add_fusion.refs_0_, bf16[1024,512]{1,0:T(8,128)(2,1)S(1)} %copy-done, f32[1024,512]{1,0:T(8,128)S(1)} %get-tuple-element.91.refs_2_, bf16[544,128]{1,0:T(8,128)(2,1)S(1)} %get-tuple-element.110.refs_3_, ...), custom_call_target="tpu_custom_call" | custom-call | flops 536870912 | bytes 6488080 | tf_op jit(solution)/shard_map/query_home/pallas_call | solution.py:522
  140.5 1.5 collective-permute-start.29
  142.0 1.8 %query_weight.1 = (bf16[4,128,512]{2,1,0:T(8,128)(2,1)S(1)}, bf16[4,128,512]{2,1,0:T(8,128)(2,1)S(1)}) custom-call(s32[4]{0:T(128)S(1)} %pad_add_fusion.refs_0_, bf16[1024,1024]{1,0:T(8,128)(2,1)S(1)} %copy-done.7, bf16[1024,512]{1,0:T(8,128)(2,1)S(1)} %get-tuple-element.118.refs_2_.refs_1_), custom_call_target="tpu_custom_call" | custom-call | flops 1073741824 | bytes 4194320 | tf_op jit(solution)/shard_map/query_weight/pallas_call | solution.py:522
  144.4 0.7 value_subs.1
  145.1 0.7 collective-permute-start.34
  145.8 0.8 collective-permute-start.35
  146.6 2.4 %collective-permute-start.36 = (bf16[128,512]{1,0:T(8,128)(2,1)S(1)}, bf16[128,512]{1,0:T(8,128)(2,1)S(1)}, u32[]{:S(2)}, u32[]{:S(2)}) collective-permute-start(bf16[128,512]{1,0:T(8,128)(2,1)S(1)} %get-tuple-element.138), channel_id=1, source_target_pairs={{0,12},{4,0},{8,4},{12,8},{1,13},{5,1},{9,5},{13,9},{2,14},{6,2},{... | collective-permute-start | bytes 393224 | tf_op jit(solution)/shard_map/ppermute | solution.py:550
  150.2 3.2 %collective-permute-done.34.refs_1_ = bf16[128,512]{1,0:T(8,128)(2,1)S(1)} collective-permute-done((bf16[128,512]{1,0:T(8,128)(2,1)S(1)}, bf16[128,512]{1,0:T(8,128)(2,1)S(1)}, u32[]{:S(2)}, u32[]{:S(2)}) %collective-permute-start.34) | collective-permute-done | bytes 131104 | tf_op jit(solution)/shard_map/ppermute | solution.py:550
  153.4 5.6 %collective-permute-done.35.refs_2_ = bf16[128,512]{1,0:T(8,128)(2,1)S(1)} collective-permute-done((bf16[128,512]{1,0:T(8,128)(2,1)S(1)}, bf16[128,512]{1,0:T(8,128)(2,1)S(1)}, u32[]{:S(2)}, u32[]{:S(2)}) %collective-permute-start.35) | collective-permute-done | bytes 131104 | tf_op jit(solution)/shard_map/ppermute | solution.py:550
  159.1 2.9 %collective-permute-start.32 = (bf16[128,512]{1,0:T(8,128)(2,1)S(1)}, bf16[128,512]{1,0:T(8,128)(2,1)S(1)}, u32[]{:S(2)}, u32[]{:S(2)}) collective-permute-start(bf16[128,512]{1,0:T(8,128)(2,1)S(1)} %get-tuple-element.128), channel_id=1, source_target_pairs={{0,12},{4,0},{8,4},{12,8},{1,13},{5,1},{9,5},{13,9},{2,14},{6,2},{... | collective-permute-start | bytes 393224 | tf_op jit(solution)/shard_map/ppermute | solution.py:550
  161.9 1.8 %input_own.1.refs_2_.refs_4_ = bf16[1024,512]{1,0:T(8,128)(2,1)S(1)} custom-call(s32[4]{0:T(128)S(1)} %pad_add_fusion.refs_0_, bf16[1024,512]{1,0:T(8,128)(2,1)S(1)} %get-tuple-element.118.refs_2_.refs_1_, bf16[1024,512]{1,0:T(8,128)(2,1)S(1)} %get-tuple-element.122.refs_2_, bf16[1024,512]{1,0:T(8,128)(2,1)S(1)} %copy-done, bf16[1024,512]{1,0:T(8,128)(2,1)S(1)} %copy-done.3, ...), custom_call_target="tpu_custom_call" | custom-call | flops 1073741824 | bytes 5242896 | tf_op jit(solution)/shard_map/input_own/pallas_call | solution.py:522
  163.8 0.8 value_sum.1
  164.5 1.2 collective-permute-done.29.refs_3_
  165.7 2.3 %input_sum.1 = (bf16[1024,512]{1,0:T(8,128)(2,1)}, bf16[128,512]{1,0:T(8,128)(2,1)S(1)}) custom-call(bf16[1024,1024]{1,0:T(8,128)(2,1)S(1)} %get-tuple-element.74.refs_9_.refs_0_, bf16[128,512]{1,0:T(8,128)(2,1)S(1)} %get-tuple-element.121.refs_5_.refs_1_, bf16[1024,512]{1,0:T(8,128)(2,1)S(1)} %input_own.1.refs_2_.refs_4_, ...), custom_call_target="tpu_custom_call" | custom-call | flops 1073741824 | bytes 5505024 | tf_op jit(solution)/shard_map/input_sum/pallas_call | solution.py:522
  168.0 1.4 collective-permute-done.31.refs_2_
  169.3 0.8 query_sum.1
  (57 shorter events, 3.3 us)
Async XLA Ops:
  0.6 9.8 %copy-start = (bf16[1024,512]{1,0:T(8,128)(2,1)S(1)}, bf16[1024,512]{1,0:T(8,128)(2,1)}, u32[]{:S(2)}) copy-start(bf16[1024,512]{1,0:T(8,128)(2,1)} %refs_3_.7) | copy-start | bytes 3145732
  0.6 9.8 %copy-start.1 = (bf16[1024,1024]{1,0:T(8,128)(2,1)S(1)}, bf16[1024,1024]{1,0:T(8,128)(2,1)}, u32[]{:S(2)}) copy-start(bf16[1024,1024]{1,0:T(8,128)(2,1)} %refs_2_.4) | copy-start | bytes 6291460
  0.7 9.8 %copy-start.4 = (s32[1024,1]{0,1:T(1,128)S(1)}, s32[1024,1]{0,1:T(1,128)}, u32[]{:S(2)}) copy-start(s32[1024,1]{0,1:T(1,128)} %param.9) | copy-start | bytes 12292
  6.2 34.5 %collective-permute-start = (bf16[1040,128]{1,0:T(8,128)(2,1)}, bf16[1040,128]{1,0:T(8,128)(2,1)S(1)}, u32[]{:S(2)}, u32[]{:S(2)}) collective-permute-start(bf16[1040,128]{1,0:T(8,128)(2,1)} %get-tuple-element.77), channel_id=1, source_target_pairs={{0,8},{8,0},{9,1},{4,12},{5,13},{12,4},{13,5},{1,9},{2,10},{10,2},... | collective-permute-start | bytes 798728 | tf_op jit(solution)/shard_map/ppermute | solution.py:544
  10.3 34.5 %collective-permute-start.1 = (bf16[1040,128]{1,0:T(8,128)(2,1)}, bf16[1040,128]{1,0:T(8,128)(2,1)}, u32[]{:S(2)}, u32[]{:S(2)}) collective-permute-start(bf16[1040,128]{1,0:T(8,128)(2,1)} %get-tuple-element.78), channel_id=1, source_target_pairs={{0,9},{8,1},{9,0},{4,13},{5,12},{12,5},{13,4},{1,8},{2,11},{10,3},... | collective-permute-start | bytes 798728 | tf_op jit(solution)/shard_map/ppermute | solution.py:544
  10.4 1.2 copy-start.2
  11.7 0.7 copy-start.5
  12.3 33.9 %copy-start.3 = (bf16[1024,512]{1,0:T(8,128)(2,1)S(1)}, bf16[1024,512]{1,0:T(8,128)(2,1)}, u32[]{:S(2)}) copy-start(bf16[1024,512]{1,0:T(8,128)(2,1)} %refs_4_.3) | copy-start | bytes 3145732
  17.2 36.4 %collective-permute-start.3 = (bf16[1040,128]{1,0:T(8,128)(2,1)S(1)}, bf16[1040,128]{1,0:T(8,128)(2,1)S(1)}, u32[]{:S(2)}, u32[]{:S(2)}) collective-permute-start(bf16[1040,128]{1,0:T(8,128)(2,1)S(1)} %get-tuple-element.79), channel_id=1, source_target_pairs={{0,5},{8,13},{9,12},{4,9},{5,8},{12,1},{13,0},{1,4},{2,7},{10,15},... | collective-permute-start | bytes 798728 | tf_op jit(solution)/shard_map/ppermute | solution.py:544
  18.9 34.8 %collective-permute-start.2 = (bf16[1040,128]{1,0:T(8,128)(2,1)S(1)}, bf16[1040,128]{1,0:T(8,128)(2,1)S(1)}, u32[]{:S(2)}, u32[]{:S(2)}) collective-permute-start(bf16[1040,128]{1,0:T(8,128)(2,1)S(1)} %get-tuple-element.73.refs_4_), channel_id=1, source_target_pairs={{0,4},{8,12},{9,13},{4,8},{5,9},{12,0},{13,1},{1,5},{2,6},{10,14},... | collective-permute-start | bytes 798728 | tf_op jit(solution)/shard_map/ppermute | solution.py:544
  20.4 35.6 %collective-permute-start.4 = (bf16[1040,128]{1,0:T(8,128)(2,1)S(1)}, bf16[1040,128]{1,0:T(8,128)(2,1)S(1)}, u32[]{:S(2)}, u32[]{:S(2)}) collective-permute-start(bf16[1040,128]{1,0:T(8,128)(2,1)S(1)} %get-tuple-element.80), channel_id=1, source_target_pairs={{0,12},{8,4},{9,5},{4,0},{5,1},{12,8},{13,9},{1,13},{2,14},{10,6},... | collective-permute-start | bytes 798728 | tf_op jit(solution)/shard_map/ppermute | solution.py:544
  40.7 15.3 %collective-permute-start.5 = (bf16[1040,128]{1,0:T(8,128)(2,1)S(1)}, bf16[1040,128]{1,0:T(8,128)(2,1)S(1)}, u32[]{:S(2)}, u32[]{:S(2)}) collective-permute-start(bf16[1040,128]{1,0:T(8,128)(2,1)S(1)} %get-tuple-element.81), channel_id=1, source_target_pairs={{0,13},{8,5},{9,4},{4,1},{5,0},{12,9},{13,8},{1,12},{2,15},{10,7},... | collective-permute-start | bytes 798728 | tf_op jit(solution)/shard_map/ppermute | solution.py:544
  44.8 11.2 %collective-permute-start.6 = (bf16[1040,128]{1,0:T(8,128)(2,1)S(1)}, bf16[1040,128]{1,0:T(8,128)(2,1)S(1)}, u32[]{:S(2)}, u32[]{:S(2)}) collective-permute-start(bf16[1040,128]{1,0:T(8,128)(2,1)S(1)} %get-tuple-element.82), channel_id=1, source_target_pairs={{0,1},{8,9},{9,8},{4,5},{5,4},{12,13},{13,12},{1,0},{2,3},{10,11},... | collective-permute-start | bytes 798728 | tf_op jit(solution)/shard_map/ppermute | solution.py:544
  52.3 1.3 copy-start.6
  53.6 7.1 %collective-permute-start.20 = (bf16[512,128]{1,0:T(8,128)(2,1)S(1)}, bf16[512,128]{1,0:T(8,128)(2,1)S(1)}, u32[]{:S(2)}, u32[]{:S(2)}) collective-permute-start(bf16[512,128]{1,0:T(8,128)(2,1)S(1)} %get-tuple-element.109), channel_id=1, source_target_pairs={{0,1},{8,9},{9,8},{4,5},{5,4},{12,13},{13,12},{1,0},{2,3},{10,11},... | collective-permute-start | bytes 393224 | tf_op jit(solution)/shard_map/ppermute | solution.py:544
  53.6 10.9 %collective-permute-start.19 = (bf16[512,128]{1,0:T(8,128)(2,1)S(1)}, bf16[512,128]{1,0:T(8,128)(2,1)S(1)}, u32[]{:S(2)}, u32[]{:S(2)}) collective-permute-start(bf16[512,128]{1,0:T(8,128)(2,1)S(1)} %get-tuple-element.107), channel_id=1, source_target_pairs={{0,13},{8,5},{9,4},{4,1},{5,0},{12,9},{13,8},{1,12},{2,15},{10,7},... | collective-permute-start | bytes 393224 | tf_op jit(solution)/shard_map/ppermute | solution.py:544
  56.0 22.7 %collective-permute-start.18 = (bf16[512,128]{1,0:T(8,128)(2,1)S(1)}, bf16[512,128]{1,0:T(8,128)(2,1)S(1)}, u32[]{:S(2)}, u32[]{:S(2)}) collective-permute-start(bf16[512,128]{1,0:T(8,128)(2,1)S(1)} %get-tuple-element.105), channel_id=1, source_target_pairs={{0,12},{8,4},{9,5},{4,0},{5,1},{12,8},{13,9},{1,13},{2,14},{10,6},... | collective-permute-start | bytes 393224 | tf_op jit(solution)/shard_map/ppermute | solution.py:544
  60.7 20.3 %collective-permute-start.17 = (bf16[512,128]{1,0:T(8,128)(2,1)S(1)}, bf16[512,128]{1,0:T(8,128)(2,1)S(1)}, u32[]{:S(2)}, u32[]{:S(2)}) collective-permute-start(bf16[512,128]{1,0:T(8,128)(2,1)S(1)} %get-tuple-element.103), channel_id=1, source_target_pairs={{0,5},{8,13},{9,12},{4,9},{5,8},{12,1},{13,0},{1,4},{2,7},{10,15},... | collective-permute-start | bytes 393224 | tf_op jit(solution)/shard_map/ppermute | solution.py:544
  60.7 20.4 %collective-permute-start.16 = (bf16[512,128]{1,0:T(8,128)(2,1)S(1)}, bf16[512,128]{1,0:T(8,128)(2,1)S(1)}, u32[]{:S(2)}, u32[]{:S(2)}) collective-permute-start(bf16[512,128]{1,0:T(8,128)(2,1)S(1)} %get-tuple-element.101), channel_id=1, source_target_pairs={{0,4},{8,12},{9,13},{4,8},{5,9},{12,0},{13,1},{1,5},{2,6},{10,14},... | collective-permute-start | bytes 393224 | tf_op jit(solution)/shard_map/ppermute | solution.py:544
  60.7 20.6 %collective-permute-start.15 = (bf16[512,128]{1,0:T(8,128)(2,1)S(1)}, bf16[512,128]{1,0:T(8,128)(2,1)S(1)}, u32[]{:S(2)}, u32[]{:S(2)}) collective-permute-start(bf16[512,128]{1,0:T(8,128)(2,1)S(1)} %get-tuple-element.99), channel_id=1, source_target_pairs={{0,9},{8,1},{9,0},{4,13},{5,12},{12,5},{13,4},{1,8},{2,11},{10,3},... | collective-permute-start | bytes 393224 | tf_op jit(solution)/shard_map/ppermute | solution.py:544
  64.6 30.0 %collective-permute-start.14 = (bf16[512,128]{1,0:T(8,128)(2,1)S(1)}, bf16[512,128]{1,0:T(8,128)(2,1)S(1)}, u32[]{:S(2)}, u32[]{:S(2)}) collective-permute-start(bf16[512,128]{1,0:T(8,128)(2,1)S(1)} %get-tuple-element.97), channel_id=1, source_target_pairs={{0,8},{8,0},{9,1},{4,12},{5,13},{12,4},{13,5},{1,9},{2,10},{10,2},... | collective-permute-start | bytes 393224 | tf_op jit(solution)/shard_map/ppermute | solution.py:544
  78.7 31.8 %collective-permute-start.7 = (bf16[512,128]{1,0:T(8,128)(2,1)S(1)}, bf16[512,128]{1,0:T(8,128)(2,1)S(1)}, u32[]{:S(2)}, u32[]{:S(2)}) collective-permute-start(bf16[512,128]{1,0:T(8,128)(2,1)S(1)} %get-tuple-element.84), channel_id=1, source_target_pairs={{0,8},{8,0},{9,1},{4,12},{5,13},{12,4},{13,5},{1,9},{2,10},{10,2},... | collective-permute-start | bytes 393224 | tf_op jit(solution)/shard_map/ppermute | solution.py:544
  81.0 31.1 %collective-permute-start.8 = (bf16[512,128]{1,0:T(8,128)(2,1)S(1)}, bf16[512,128]{1,0:T(8,128)(2,1)S(1)}, u32[]{:S(2)}, u32[]{:S(2)}) collective-permute-start(bf16[512,128]{1,0:T(8,128)(2,1)S(1)} %get-tuple-element.85), channel_id=1, source_target_pairs={{0,9},{8,1},{9,0},{4,13},{5,12},{12,5},{13,4},{1,8},{2,11},{10,3},... | collective-permute-start | bytes 393224 | tf_op jit(solution)/shard_map/ppermute | solution.py:544
  81.2 31.0 %collective-permute-start.9 = (bf16[512,128]{1,0:T(8,128)(2,1)S(1)}, bf16[512,128]{1,0:T(8,128)(2,1)S(1)}, u32[]{:S(2)}, u32[]{:S(2)}) collective-permute-start(bf16[512,128]{1,0:T(8,128)(2,1)S(1)} %get-tuple-element.86), channel_id=1, source_target_pairs={{0,4},{8,12},{9,13},{4,8},{5,9},{12,0},{13,1},{1,5},{2,6},{10,14},... | collective-permute-start | bytes 393224 | tf_op jit(solution)/shard_map/ppermute | solution.py:544
  81.3 33.1 %collective-permute-start.10 = (bf16[512,128]{1,0:T(8,128)(2,1)S(1)}, bf16[512,128]{1,0:T(8,128)(2,1)S(1)}, u32[]{:S(2)}, u32[]{:S(2)}) collective-permute-start(bf16[512,128]{1,0:T(8,128)(2,1)S(1)} %get-tuple-element.87), channel_id=1, source_target_pairs={{0,5},{8,13},{9,12},{4,9},{5,8},{12,1},{13,0},{1,4},{2,7},{10,15},... | collective-permute-start | bytes 393224 | tf_op jit(solution)/shard_map/ppermute | solution.py:544
  94.5 34.2 %copy-start.7 = (bf16[1024,1024]{1,0:T(8,128)(2,1)S(1)}, bf16[1024,1024]{1,0:T(8,128)(2,1)}, u32[]{:S(2)}) copy-start(bf16[1024,1024]{1,0:T(8,128)(2,1)} %copy-done.6) | copy-start | bytes 6291460
  110.4 18.0 %collective-permute-start.21 = (bf16[544,128]{1,0:T(8,128)(2,1)S(1)}, bf16[544,128]{1,0:T(8,128)(2,1)S(1)}, u32[]{:S(2)}, u32[]{:S(2)}) collective-permute-start(bf16[544,128]{1,0:T(8,128)(2,1)S(1)} %get-tuple-element.111), channel_id=1, source_target_pairs={{0,8},{8,0},{9,1},{4,12},{5,13},{12,4},{13,5},{1,9},{2,10},{10,2},... | collective-permute-start | bytes 417800 | tf_op jit(solution)/shard_map/ppermute | solution.py:544
  110.5 18.1 %collective-permute-start.22 = (bf16[544,128]{1,0:T(8,128)(2,1)S(1)}, bf16[544,128]{1,0:T(8,128)(2,1)S(1)}, u32[]{:S(2)}, u32[]{:S(2)}) collective-permute-start(bf16[544,128]{1,0:T(8,128)(2,1)S(1)} %get-tuple-element.112), channel_id=1, source_target_pairs={{0,9},{8,1},{9,0},{4,13},{5,12},{12,5},{13,4},{1,8},{2,11},{10,3},... | collective-permute-start | bytes 417800 | tf_op jit(solution)/shard_map/ppermute | solution.py:544
  112.1 10.0 %collective-permute-start.11 = (bf16[512,128]{1,0:T(8,128)(2,1)S(1)}, bf16[512,128]{1,0:T(8,128)(2,1)S(1)}, u32[]{:S(2)}, u32[]{:S(2)}) collective-permute-start(bf16[512,128]{1,0:T(8,128)(2,1)S(1)} %get-tuple-element.88), channel_id=1, source_target_pairs={{0,12},{8,4},{9,5},{4,0},{5,1},{12,8},{13,9},{1,13},{2,14},{10,6},... | collective-permute-start | bytes 393224 | tf_op jit(solution)/shard_map/ppermute | solution.py:544
  112.2 12.8 %collective-permute-start.12 = (bf16[512,128]{1,0:T(8,128)(2,1)S(1)}, bf16[512,128]{1,0:T(8,128)(2,1)S(1)}, u32[]{:S(2)}, u32[]{:S(2)}) collective-permute-start(bf16[512,128]{1,0:T(8,128)(2,1)S(1)} %get-tuple-element.89), channel_id=1, source_target_pairs={{0,13},{8,5},{9,4},{4,1},{5,0},{12,9},{13,8},{1,12},{2,15},{10,7},... | collective-permute-start | bytes 393224 | tf_op jit(solution)/shard_map/ppermute | solution.py:544
  114.4 10.6 %collective-permute-start.13 = (bf16[512,128]{1,0:T(8,128)(2,1)S(1)}, bf16[512,128]{1,0:T(8,128)(2,1)S(1)}, u32[]{:S(2)}, u32[]{:S(2)}) collective-permute-start(bf16[512,128]{1,0:T(8,128)(2,1)S(1)} %get-tuple-element.90), channel_id=1, source_target_pairs={{0,1},{8,9},{9,8},{4,5},{5,4},{12,13},{13,12},{1,0},{2,3},{10,11},... | collective-permute-start | bytes 393224 | tf_op jit(solution)/shard_map/ppermute | solution.py:544
  122.1 9.1 %collective-permute-start.23 = (bf16[544,128]{1,0:T(8,128)(2,1)S(1)}, bf16[544,128]{1,0:T(8,128)(2,1)S(1)}, u32[]{:S(2)}, u32[]{:S(2)}) collective-permute-start(bf16[544,128]{1,0:T(8,128)(2,1)S(1)} %get-tuple-element.113), channel_id=1, source_target_pairs={{0,4},{8,12},{9,13},{4,8},{5,9},{12,0},{13,1},{1,5},{2,6},{10,14},... | collective-permute-start | bytes 417800 | tf_op jit(solution)/shard_map/ppermute | solution.py:544
  125.0 7.6 %collective-permute-start.24 = (bf16[544,128]{1,0:T(8,128)(2,1)S(1)}, bf16[544,128]{1,0:T(8,128)(2,1)S(1)}, u32[]{:S(2)}, u32[]{:S(2)}) collective-permute-start(bf16[544,128]{1,0:T(8,128)(2,1)S(1)} %get-tuple-element.114), channel_id=1, source_target_pairs={{0,5},{8,13},{9,12},{4,9},{5,8},{12,1},{13,0},{1,4},{2,7},{10,15},... | collective-permute-start | bytes 417800 | tf_op jit(solution)/shard_map/ppermute | solution.py:544
  125.0 10.7 %collective-permute-start.25 = (bf16[544,128]{1,0:T(8,128)(2,1)S(1)}, bf16[544,128]{1,0:T(8,128)(2,1)S(1)}, u32[]{:S(2)}, u32[]{:S(2)}) collective-permute-start(bf16[544,128]{1,0:T(8,128)(2,1)S(1)} %get-tuple-element.115), channel_id=1, source_target_pairs={{0,12},{8,4},{9,5},{4,0},{5,1},{12,8},{13,9},{1,13},{2,14},{10,6},... | collective-permute-start | bytes 417800 | tf_op jit(solution)/shard_map/ppermute | solution.py:544
  128.5 10.0 %collective-permute-start.26 = (bf16[544,128]{1,0:T(8,128)(2,1)S(1)}, bf16[544,128]{1,0:T(8,128)(2,1)S(1)}, u32[]{:S(2)}, u32[]{:S(2)}) collective-permute-start(bf16[544,128]{1,0:T(8,128)(2,1)S(1)} %get-tuple-element.116), channel_id=1, source_target_pairs={{0,13},{8,5},{9,4},{4,1},{5,0},{12,9},{13,8},{1,12},{2,15},{10,7},... | collective-permute-start | bytes 417800 | tf_op jit(solution)/shard_map/ppermute | solution.py:544
  128.6 9.9 %collective-permute-start.27 = (bf16[544,128]{1,0:T(8,128)(2,1)S(1)}, bf16[544,128]{1,0:T(8,128)(2,1)S(1)}, u32[]{:S(2)}, u32[]{:S(2)}) collective-permute-start(bf16[544,128]{1,0:T(8,128)(2,1)S(1)} %get-tuple-element.117), channel_id=1, source_target_pairs={{0,1},{8,9},{9,8},{4,5},{5,4},{12,13},{13,12},{1,0},{2,3},{10,11},... | collective-permute-start | bytes 417800 | tf_op jit(solution)/shard_map/ppermute | solution.py:544
  140.5 25.2 %collective-permute-start.29 = (bf16[1024,512]{1,0:T(8,128)(2,1)S(1)}, bf16[1024,512]{1,0:T(8,128)(2,1)S(1)}, u32[]{:S(2)}, u32[]{:S(2)}) collective-permute-start(bf16[1024,512]{1,0:T(8,128)(2,1)S(1)} %get-tuple-element.123), channel_id=1, source_target_pairs={{0,2},{2,0},{1,3},{3,1},{4,6},{6,4},{5,7},{7,5},{8,10},{10,8},{9,1... | collective-permute-start | bytes 3145736 | tf_op jit(solution)/shard_map/ppermute | solution.py:550
  142.0 2.4 %collective-permute-start.33 = (bf16[4,128,512]{2,1,0:T(8,128)(2,1)S(1)}, bf16[4,128,512]{2,1,0:T(8,128)(2,1)S(1)}, u32[]{:S(2)}, u32[]{:S(2)}) collective-permute-start(bf16[4,128,512]{2,1,0:T(8,128)(2,1)S(1)} %get-tuple-element.130), channel_id=1, source_target_pairs={{0,1},{1,0},{2,3},{3,2},{4,5},{5,4},{6,7},{7,6},{8,9},{9,8},{10,11... | collective-permute-start | bytes 1572872 | tf_op jit(solution)/shard_map/ppermute | solution.py:550
  143.8 5.1 %collective-permute-start.28 = (bf16[4,128,512]{2,1,0:T(8,128)(2,1)S(1)}, bf16[4,128,512]{2,1,0:T(8,128)(2,1)S(1)}, u32[]{:S(2)}, u32[]{:S(2)}) collective-permute-start(bf16[4,128,512]{2,1,0:T(8,128)(2,1)S(1)} %get-tuple-element.120), channel_id=1, source_target_pairs={{0,1},{1,0},{2,3},{3,2},{4,5},{5,4},{6,7},{7,6},{8,9},{9,8},{10,11... | collective-permute-start | bytes 1572872 | tf_op jit(solution)/shard_map/ppermute | solution.py:550
  145.1 8.3 %collective-permute-start.34 = (bf16[128,512]{1,0:T(8,128)(2,1)S(1)}, bf16[128,512]{1,0:T(8,128)(2,1)S(1)}, u32[]{:S(2)}, u32[]{:S(2)}) collective-permute-start(bf16[128,512]{1,0:T(8,128)(2,1)S(1)} %get-tuple-element.136), channel_id=1, source_target_pairs={{0,4},{4,8},{8,12},{12,0},{1,5},{5,9},{9,13},{13,1},{2,6},{6,10},{... | collective-permute-start | bytes 393224 | tf_op jit(solution)/shard_map/ppermute | solution.py:550
  145.8 13.3 %collective-permute-start.35 = (bf16[128,512]{1,0:T(8,128)(2,1)S(1)}, bf16[128,512]{1,0:T(8,128)(2,1)S(1)}, u32[]{:S(2)}, u32[]{:S(2)}) collective-permute-start(bf16[128,512]{1,0:T(8,128)(2,1)S(1)} %get-tuple-element.137), channel_id=1, source_target_pairs={{0,8},{4,12},{8,0},{12,4},{1,9},{5,13},{9,1},{13,5},{2,10},{6,14},... | collective-permute-start | bytes 393224 | tf_op jit(solution)/shard_map/ppermute | solution.py:550
  146.6 17.2 %collective-permute-start.36 = (bf16[128,512]{1,0:T(8,128)(2,1)S(1)}, bf16[128,512]{1,0:T(8,128)(2,1)S(1)}, u32[]{:S(2)}, u32[]{:S(2)}) collective-permute-start(bf16[128,512]{1,0:T(8,128)(2,1)S(1)} %get-tuple-element.138), channel_id=1, source_target_pairs={{0,12},{4,0},{8,4},{12,8},{1,13},{5,1},{9,5},{13,9},{2,14},{6,2},{... | collective-permute-start | bytes 393224 | tf_op jit(solution)/shard_map/ppermute | solution.py:550
  149.6 18.3 %collective-permute-start.30 = (bf16[128,512]{1,0:T(8,128)(2,1)S(1)}, bf16[128,512]{1,0:T(8,128)(2,1)S(1)}, u32[]{:S(2)}, u32[]{:S(2)}) collective-permute-start(bf16[128,512]{1,0:T(8,128)(2,1)S(1)} %get-tuple-element.126), channel_id=1, source_target_pairs={{0,4},{4,8},{8,12},{12,0},{1,5},{5,9},{9,13},{13,1},{2,6},{6,10},{... | collective-permute-start | bytes 393224 | tf_op jit(solution)/shard_map/ppermute | solution.py:550
  153.4 15.9 %collective-permute-start.31 = (bf16[128,512]{1,0:T(8,128)(2,1)S(1)}, bf16[128,512]{1,0:T(8,128)(2,1)S(1)}, u32[]{:S(2)}, u32[]{:S(2)}) collective-permute-start(bf16[128,512]{1,0:T(8,128)(2,1)S(1)} %get-tuple-element.127), channel_id=1, source_target_pairs={{0,8},{4,12},{8,0},{12,4},{1,9},{5,13},{9,1},{13,5},{2,10},{6,14},... | collective-permute-start | bytes 393224 | tf_op jit(solution)/shard_map/ppermute | solution.py:550
  159.1 10.3 %collective-permute-start.32 = (bf16[128,512]{1,0:T(8,128)(2,1)S(1)}, bf16[128,512]{1,0:T(8,128)(2,1)S(1)}, u32[]{:S(2)}, u32[]{:S(2)}) collective-permute-start(bf16[128,512]{1,0:T(8,128)(2,1)S(1)} %get-tuple-element.128), channel_id=1, source_target_pairs={{0,12},{4,0},{8,4},{12,8},{1,13},{5,1},{9,5},{13,9},{2,14},{6,2},{... | collective-permute-start | bytes 393224 | tf_op jit(solution)/shard_map/ppermute | solution.py:550

commit v16 on v15

--- a/solution.py
+++ b/solution.py
@@ -656,6 +656,7 @@
         vmem=48,
         name="value_grad",
     )
+    back_value, _ = lax.optimization_barrier((back_value, got_value[1:]))
     home_value = exchange(back_value, sizes)
     back_query = call(
         functools.partial(query_grad_kernel, sizes, per_group, slot_rows),

time: 171 us -> 170 us (level)
  waiting for transfers between devices: 59 us -> 47.9 us
  starting transfers between devices: 47.8 us -> 58.6 us
    ppermute x28, waiting for transfers between devices: 47.7 us -> 39.6 us  [exchange(): out.append(part if ahead == (0, 0) else lax.ppermute(part, OWNERS, moves))]
    ppermute x28, starting transfers between devices: 38.4 us -> 46.2 us  [exchange(): out.append(part if ahead == (0, 0) else lax.ppermute(part, OWNERS, moves))]
    ppermute x9, waiting for transfers between devices: 11.4 us -> 8.31 us  [shift(): lax.ppermute(part, axis, [(i, (i + ahead) % size) for i in range(size)])]
    ppermute x9, starting transfers between devices: 9.43 us -> 12.4 us  [shift(): lax.ppermute(part, axis, [(i, (i + ahead) % size) for i in range(size)])]
  transfers between devices with their start and end apart: 37 -> 37, of which waited for: 12 -> 11; matrix products, arithmetic and copies ran while one was open for 0% -> 0% of each run, Pallas kernels for 30% -> 30%
where the time goes in v16:
time: 170 us
  Pallas kernels  59.1 us (35%)
  starting transfers between devices  58.6 us (34%)
  waiting for transfers between devices  47.9 us (28%)
  local copies, waits for them, and re-layouts  3.23 us (2%)
    pallas_call x14, Pallas kernels, call(): pl.pallas_call(body, out_shape=outs, in_specs=specs, out_specs=jax.tree.m...  59.1 us
    ppermute x28, starting transfers between devices, exchange(): out.append(part if ahead == (0, 0) else lax.ppermute(part, OWNERS, moves))  46.2 us
    ppermute x28, waiting for transfers between devices, exchange(): out.append(part if ahead == (0, 0) else lax.ppermute(part, OWNERS, moves))  39.6 us
    ppermute x9, starting transfers between devices, shift(): lax.ppermute(part, axis, [(i, (i + ahead) % size) for i in range(size)])  12.4 us
    ppermute x9, waiting for transfers between devices, shift(): lax.ppermute(part, axis, [(i, (i + ahead) % size) for i in range(size)])  8.31 us
  transfers between devices with their start and end apart: 37, of which 11 were waited for; matrix products, arithmetic and copies ran while one was open for 0% of the time, Pallas kernels for 30%

profile of v16, /device:TPU:0, one launch (start us, length us, event | category | flops | bytes accessed | tf_op | source)
XLA Modules:
  0.0 169.8 jit_solution(3984497137594280275)
XLA Ops:
  0.7 5.6 %project_far.1 = (bf16[1040,128]{1,0:T(8,128)(2,1)}, bf16[1040,128]{1,0:T(8,128)(2,1)}, s32[1,1024]{1,0:T(1,128)}) custom-call(s32[1,1024]{1,0:T(1,128)} %bitcast.5, bf16[1024,1024]{1,0:T(8,128)(2,1)} %refs_2_.4, bf16[1024,512]{1,0:T(8,128)(2,1)} %refs_3_.7, bf16[1024,512]{1,0:T(8,128)(2,1)} %refs_5_.1), custom_call_target="tpu_custom_call" | custom-call | flops 805306368 | bytes 4734976 | tf_op jit(solution)/shard_map/project_far/pallas_call | solution.py:522
  6.2 4.1 %collective-permute-start = (bf16[1040,128]{1,0:T(8,128)(2,1)}, bf16[1040,128]{1,0:T(8,128)(2,1)S(1)}, u32[]{:S(2)}, u32[]{:S(2)}) collective-permute-start(bf16[1040,128]{1,0:T(8,128)(2,1)} %get-tuple-element.85), channel_id=1, source_target_pairs={{0,8},{8,0},{9,1},{4,12},{5,13},{12,4},{13,5},{1,9},{2,10},{10,2},... | collective-permute-start | bytes 798728 | tf_op jit(solution)/shard_map/ppermute | solution.py:544
  10.4 1.2 copy-done.2
  11.7 0.7 copy-done.5
  12.4 4.8 %project_query.1 = (bf16[1040,128]{1,0:T(8,128)(2,1)S(1)}, bf16[1040,128]{1,0:T(8,128)(2,1)S(1)}, bf16[1040,128]{1,0:T(8,128)(2,1)S(1)}, bf16[1040,128]{1,0:T(8,...) custom-call(s32[4]{0:T(128)S(1)} %pad_add_fusion.refs_0_, s32[1,1024]{1,0:T(1,128)S(1)} %copy-done.5, ...), custom_call_target="tpu_custom_call" | custom-call | flops 3221225472 | bytes 5799952 | tf_op jit(solution)/shard_map/project_query/pallas_call | solution.py:522
  17.2 1.7 collective-permute-start.3
  18.9 1.6 collective-permute-start.2
  20.4 2.2 %collective-permute-start.4 = (bf16[1040,128]{1,0:T(8,128)(2,1)S(1)}, bf16[1040,128]{1,0:T(8,128)(2,1)S(1)}, u32[]{:S(2)}, u32[]{:S(2)}) collective-permute-start(bf16[1040,128]{1,0:T(8,128)(2,1)S(1)} %get-tuple-element.88), channel_id=1, source_target_pairs={{0,12},{8,4},{9,5},{4,0},{5,1},{12,8},{13,9},{1,13},{2,14},{10,6},... | collective-permute-start | bytes 798728 | tf_op jit(solution)/shard_map/ppermute | solution.py:544
  22.7 18.0 %collective-permute-done.refs_2_ = bf16[1040,128]{1,0:T(8,128)(2,1)S(1)} collective-permute-done((bf16[1040,128]{1,0:T(8,128)(2,1)}, bf16[1040,128]{1,0:T(8,128)(2,1)S(1)}, u32[]{:S(2)}, u32[]{:S(2)}) %collective-permute-start) | collective-permute-done | bytes 266272 | tf_op jit(solution)/shard_map/ppermute | solution.py:544
  40.7 4.1 %collective-permute-done.1.refs_3_ = bf16[1040,128]{1,0:T(8,128)(2,1)} collective-permute-done((bf16[1040,128]{1,0:T(8,128)(2,1)}, bf16[1040,128]{1,0:T(8,128)(2,1)}, u32[]{:S(2)}, u32[]{:S(2)}) %collective-permute-start.1) | collective-permute-done | bytes 266272 | tf_op jit(solution)/shard_map/ppermute | solution.py:544
  44.8 1.4 collective-permute-start.6
  46.3 6.0 %project_value.1 = (bf16[512,128]{1,0:T(8,128)(2,1)S(1)}, bf16[512,128]{1,0:T(8,128)(2,1)S(1)}, bf16[512,128]{1,0:T(8,128)(2,1)S(1)}, bf16[512,128]{1,0:T(8,128)...) custom-call(s32[4]{0:T(128)S(1)} %pad_add_fusion.refs_0_, ...), custom_call_target="tpu_custom_call" | custom-call | flops 2147483648 | bytes 8392720 | tf_op jit(solution)/shard_map/project_value/pallas_call | solution.py:522
  52.3 1.3 copy-done.6
  53.6 2.4 %collective-permute-start.12 = (bf16[512,128]{1,0:T(8,128)(2,1)S(1)}, bf16[512,128]{1,0:T(8,128)(2,1)S(1)}, u32[]{:S(2)}, u32[]{:S(2)}) collective-permute-start(bf16[512,128]{1,0:T(8,128)(2,1)S(1)} %get-tuple-element.110), channel_id=1, source_target_pairs={{0,13},{8,5},{9,4},{4,1},{5,0},{12,9},{13,8},{1,12},{2,15},{10,7},... | collective-permute-start | bytes 393224 | tf_op jit(solution)/shard_map/ppermute | solution.py:544
  56.0 4.7 %collective-permute-start.11 = (bf16[512,128]{1,0:T(8,128)(2,1)S(1)}, bf16[512,128]{1,0:T(8,128)(2,1)S(1)}, u32[]{:S(2)}, u32[]{:S(2)}) collective-permute-start(bf16[512,128]{1,0:T(8,128)(2,1)S(1)} %get-tuple-element.108), channel_id=1, source_target_pairs={{0,12},{8,4},{9,5},{4,0},{5,1},{12,8},{13,9},{1,13},{2,14},{10,6},... | collective-permute-start | bytes 393224 | tf_op jit(solution)/shard_map/ppermute | solution.py:544
  60.7 3.8 %collective-permute-start.8 = (bf16[512,128]{1,0:T(8,128)(2,1)S(1)}, bf16[512,128]{1,0:T(8,128)(2,1)S(1)}, u32[]{:S(2)}, u32[]{:S(2)}) collective-permute-start(bf16[512,128]{1,0:T(8,128)(2,1)S(1)} %get-tuple-element.102), channel_id=1, source_target_pairs={{0,9},{8,1},{9,0},{4,13},{5,12},{12,5},{13,4},{1,8},{2,11},{10,3},... | collective-permute-start | bytes 393224 | tf_op jit(solution)/shard_map/ppermute | solution.py:544
  65.2 13.5 %value_grad.1 = (bf16[512,128]{1,0:T(8,128)(2,1)S(1)}, bf16[512,128]{1,0:T(8,128)(2,1)S(1)}, bf16[512,128]{1,0:T(8,128)(2,1)S(1)}, bf16[512,128]{1,0:T(8,128)(2,...) custom-call(s32[4]{0:T(128)S(1)} %pad_add_fusion.refs_0_, ...), custom_call_target="tpu_custom_call" | custom-call | flops 2147483648 | bytes 8163344 | tf_op jit(solution)/shard_map/value_grad/pallas_call | solution.py:522
  78.7 1.0 collective-permute-done.8.refs_5_
  79.7 3.2 %collective-permute-done.7.refs_4_ = bf16[512,128]{1,0:T(8,128)(2,1)S(1)} collective-permute-done((bf16[512,128]{1,0:T(8,128)(2,1)S(1)}, bf16[512,128]{1,0:T(8,128)(2,1)S(1)}, u32[]{:S(2)}, u32[]{:S(2)}) %collective-permute-start.7) | collective-permute-done | bytes 131104 | tf_op jit(solution)/shard_map/ppermute | solution.py:544
  82.9 2.0 %collective-permute-start.15 = (bf16[512,128]{1,0:T(8,128)(2,1)S(1)}, bf16[512,128]{1,0:T(8,128)(2,1)S(1)}, u32[]{:S(2)}, u32[]{:S(2)}) collective-permute-start(bf16[512,128]{1,0:T(8,128)(2,1)S(1)} %get-tuple-element.115), channel_id=1, source_target_pairs={{0,9},{8,1},{9,0},{4,13},{5,12},{12,5},{13,4},{1,8},{2,11},{10,3},... | collective-permute-start | bytes 393224 | tf_op jit(solution)/shard_map/ppermute | solution.py:544
  84.9 1.0 collective-permute-start.17
  85.9 15.9 %query_grad.1 = (bf16[544,128]{1,0:T(8,128)(2,1)S(1)}, bf16[544,128]{1,0:T(8,128)(2,1)S(1)}, bf16[544,128]{1,0:T(8,128)(2,1)S(1)}, bf16[544,128]{1,0:T(8,128)(2,...) custom-call(s32[4]{0:T(128)S(1)} %pad_add_fusion.refs_0_, ...), custom_call_target="tpu_custom_call" | custom-call | flops 3221225472 | bytes 7147536 | tf_op jit(solution)/shard_map/query_grad/pallas_call | solution.py:522
  101.8 3.9 %collective-permute-start.21 = (bf16[544,128]{1,0:T(8,128)(2,1)S(1)}, bf16[544,128]{1,0:T(8,128)(2,1)S(1)}, u32[]{:S(2)}, u32[]{:S(2)}) collective-permute-start(bf16[544,128]{1,0:T(8,128)(2,1)S(1)} %get-tuple-element.127), channel_id=1, source_target_pairs={{0,8},{8,0},{9,1},{4,12},{5,13},{12,4},{13,5},{1,9},{2,10},{10,2},... | collective-permute-start | bytes 417800 | tf_op jit(solution)/shard_map/ppermute | solution.py:544
  105.7 2.1 %collective-permute-start.18 = (bf16[512,128]{1,0:T(8,128)(2,1)S(1)}, bf16[512,128]{1,0:T(8,128)(2,1)S(1)}, u32[]{:S(2)}, u32[]{:S(2)}) collective-permute-start(bf16[512,128]{1,0:T(8,128)(2,1)S(1)} %get-tuple-element.118), channel_id=1, source_target_pairs={{0,12},{8,4},{9,5},{4,0},{5,1},{12,8},{13,9},{1,13},{2,14},{10,6},... | collective-permute-start | bytes 393224 | tf_op jit(solution)/shard_map/ppermute | solution.py:544
  107.8 1.7 %collective-permute-start.19 = (bf16[512,128]{1,0:T(8,128)(2,1)S(1)}, bf16[512,128]{1,0:T(8,128)(2,1)S(1)}, u32[]{:S(2)}, u32[]{:S(2)}) collective-permute-start(bf16[512,128]{1,0:T(8,128)(2,1)S(1)} %get-tuple-element.119), channel_id=1, source_target_pairs={{0,13},{8,5},{9,4},{4,1},{5,0},{12,9},{13,8},{1,12},{2,15},{10,7},... | collective-permute-start | bytes 393224 | tf_op jit(solution)/shard_map/ppermute | solution.py:544
  109.5 6.0 %collective-permute-done.18.refs_8_ = bf16[512,128]{1,0:T(8,128)(2,1)S(1)} collective-permute-done((bf16[512,128]{1,0:T(8,128)(2,1)S(1)}, bf16[512,128]{1,0:T(8,128)(2,1)S(1)}, u32[]{:S(2)}, u32[]{:S(2)}) %collective-permute-start.18) | collective-permute-done | bytes 131104 | tf_op jit(solution)/shard_map/ppermute | solution.py:544
  115.5 9.2 %collective-permute-start.23 = (bf16[544,128]{1,0:T(8,128)(2,1)S(1)}, bf16[544,128]{1,0:T(8,128)(2,1)S(1)}, u32[]{:S(2)}, u32[]{:S(2)}) collective-permute-start(bf16[544,128]{1,0:T(8,128)(2,1)S(1)} %get-tuple-element.129), channel_id=1, source_target_pairs={{0,4},{8,12},{9,13},{4,8},{5,9},{12,0},{13,1},{1,5},{2,6},{10,14},... | collective-permute-start | bytes 417800 | tf_op jit(solution)/shard_map/ppermute | solution.py:544
  124.8 2.1 %collective-permute-start.24 = (bf16[544,128]{1,0:T(8,128)(2,1)S(1)}, bf16[544,128]{1,0:T(8,128)(2,1)S(1)}, u32[]{:S(2)}, u32[]{:S(2)}) collective-permute-start(bf16[544,128]{1,0:T(8,128)(2,1)S(1)} %get-tuple-element.130), channel_id=1, source_target_pairs={{0,5},{8,13},{9,12},{4,9},{5,8},{12,1},{13,0},{1,4},{2,7},{10,15},... | collective-permute-start | bytes 417800 | tf_op jit(solution)/shard_map/ppermute | solution.py:544
  126.9 0.7 collective-permute-start.25
  127.7 0.7 collective-permute-start.26
  128.5 2.5 %value_home.1 = (bf16[1024,512]{1,0:T(8,128)(2,1)S(1)}, f32[1024,512]{1,0:T(8,128)S(1)}, bf16[4,128,512]{2,1,0:T(8,128)(2,1)S(1)}, bf16[4,128,512]{2,1,0:T(8,128)(2,1)S(1)}) custom-call(s32[4]{0:T(128)S(1)} %pad_add_fusion.refs_0_, bf16[1024,1024]{1,0:T(8,128)(2,1)S(1)} %copy-done.7, bf16[1024,512]{1,0:T(8,128)(2,1)S(1)} %copy-done.3, ...), custom_call_target="tpu_custom_call" | custom-call | flops 1610612736 | bytes 8388624 | tf_op jit(solution)/shard_map/value_home/pallas_call | solution.py:522
  131.0 1.5 collective-permute-done.24.refs_7_
  132.5 2.8 %collective-permute-done.25.refs_8_ = bf16[544,128]{1,0:T(8,128)(2,1)S(1)} collective-permute-done((bf16[544,128]{1,0:T(8,128)(2,1)S(1)}, bf16[544,128]{1,0:T(8,128)(2,1)S(1)}, u32[]{:S(2)}, u32[]{:S(2)}) %collective-permute-start.25) | collective-permute-done | bytes 139296 | tf_op jit(solution)/shard_map/ppermute | solution.py:544
  135.3 2.9 %collective-permute-done.26.refs_9_ = bf16[544,128]{1,0:T(8,128)(2,1)S(1)} collective-permute-done((bf16[544,128]{1,0:T(8,128)(2,1)S(1)}, bf16[544,128]{1,0:T(8,128)(2,1)S(1)}, u32[]{:S(2)}, u32[]{:S(2)}) %collective-permute-start.26) | collective-permute-done | bytes 139296 | tf_op jit(solution)/shard_map/ppermute | solution.py:544
  138.2 2.0 %query_home.1 = (bf16[1024,512]{1,0:T(8,128)(2,1)S(1)}, bf16[1024,512]{1,0:T(8,128)(2,1)S(1)}, f32[64,512]{1,0:T(8,128)}) custom-call(s32[4]{0:T(128)S(1)} %pad_add_fusion.refs_0_, bf16[1024,512]{1,0:T(8,128)(2,1)S(1)} %copy-done, f32[1024,512]{1,0:T(8,128)S(1)} %get-tuple-element.121.refs_2_, bf16[544,128]{1,0:T(8,128)(2,1)S(1)} %get-tuple-element.126.refs_3_, ...), custom_call_target="tpu_custom_call" | custom-call | flops 536870912 | bytes 6488080 | tf_op jit(solution)/shard_map/query_home/pallas_call | solution.py:522
  140.2 1.5 collective-permute-start.29
  141.7 1.8 %query_weight.1 = (bf16[4,128,512]{2,1,0:T(8,128)(2,1)S(1)}, bf16[4,128,512]{2,1,0:T(8,128)(2,1)S(1)}) custom-call(s32[4]{0:T(128)S(1)} %pad_add_fusion.refs_0_, bf16[1024,1024]{1,0:T(8,128)(2,1)S(1)} %copy-done.7, bf16[1024,512]{1,0:T(8,128)(2,1)S(1)} %get-tuple-element.134.refs_2_.refs_1_), custom_call_target="tpu_custom_call" | custom-call | flops 1073741824 | bytes 4194320 | tf_op jit(solution)/shard_map/query_weight/pallas_call | solution.py:522
  144.1 0.7 value_subs.1
  145.3 2.6 %collective-permute-start.35 = (bf16[128,512]{1,0:T(8,128)(2,1)S(1)}, bf16[128,512]{1,0:T(8,128)(2,1)S(1)}, u32[]{:S(2)}, u32[]{:S(2)}) collective-permute-start(bf16[128,512]{1,0:T(8,128)(2,1)S(1)} %get-tuple-element.153), channel_id=1, source_target_pairs={{0,8},{4,12},{8,0},{12,4},{1,9},{5,13},{9,1},{13,5},{2,10},{6,14},... | collective-permute-start | bytes 393224 | tf_op jit(solution)/shard_map/ppermute | solution.py:550
  147.9 0.8 collective-permute-start.36
  149.3 1.3 collective-permute-start.30
  150.6 2.4 %collective-permute-done.34.refs_1_ = bf16[128,512]{1,0:T(8,128)(2,1)S(1)} collective-permute-done((bf16[128,512]{1,0:T(8,128)(2,1)S(1)}, bf16[128,512]{1,0:T(8,128)(2,1)S(1)}, u32[]{:S(2)}, u32[]{:S(2)}) %collective-permute-start.34) | collective-permute-done | bytes 131104 | tf_op jit(solution)/shard_map/ppermute | solution.py:550
  153.1 5.6 %collective-permute-done.35.refs_2_ = bf16[128,512]{1,0:T(8,128)(2,1)S(1)} collective-permute-done((bf16[128,512]{1,0:T(8,128)(2,1)S(1)}, bf16[128,512]{1,0:T(8,128)(2,1)S(1)}, u32[]{:S(2)}, u32[]{:S(2)}) %collective-permute-start.35) | collective-permute-done | bytes 131104 | tf_op jit(solution)/shard_map/ppermute | solution.py:550
  158.7 5.2 %collective-permute-start.32 = (bf16[128,512]{1,0:T(8,128)(2,1)S(1)}, bf16[128,512]{1,0:T(8,128)(2,1)S(1)}, u32[]{:S(2)}, u32[]{:S(2)}) collective-permute-start(bf16[128,512]{1,0:T(8,128)(2,1)S(1)} %get-tuple-element.144), channel_id=1, source_target_pairs={{0,12},{4,0},{8,4},{12,8},{1,13},{5,1},{9,5},{13,9},{2,14},{6,2},{... | collective-permute-start | bytes 393224 | tf_op jit(solution)/shard_map/ppermute | solution.py:550
  163.9 1.8 %input_own.1.refs_2_.refs_4_ = bf16[1024,512]{1,0:T(8,128)(2,1)S(1)} custom-call(s32[4]{0:T(128)S(1)} %pad_add_fusion.refs_0_, bf16[1024,512]{1,0:T(8,128)(2,1)S(1)} %get-tuple-element.134.refs_2_.refs_1_, bf16[1024,512]{1,0:T(8,128)(2,1)S(1)} %get-tuple-element.138.refs_2_, bf16[1024,512]{1,0:T(8,128)(2,1)S(1)} %copy-done, bf16[1024,512]{1,0:T(8,128)(2,1)S(1)} %copy-done.3, ...), custom_call_target="tpu_custom_call" | custom-call | flops 1073741824 | bytes 5242896 | tf_op jit(solution)/shard_map/input_own/pallas_call | solution.py:522
  165.7 0.8 value_sum.1
  166.5 2.3 %input_sum.1 = (bf16[1024,512]{1,0:T(8,128)(2,1)}, bf16[128,512]{1,0:T(8,128)(2,1)S(1)}) custom-call(bf16[1024,1024]{1,0:T(8,128)(2,1)S(1)} %get-tuple-element.82.refs_9_.refs_0_, bf16[128,512]{1,0:T(8,128)(2,1)S(1)} %get-tuple-element.137.refs_5_.refs_1_, bf16[1024,512]{1,0:T(8,128)(2,1)S(1)} %input_own.1.refs_2_.refs_4_, ...), custom_call_target="tpu_custom_call" | custom-call | flops 1073741824 | bytes 5505024 | tf_op jit(solution)/shard_map/input_sum/pallas_call | solution.py:522
  169.0 0.8 query_sum.1
  (57 shorter events, 2.9 us)
Async XLA Ops:
  0.6 9.8 %copy-start = (bf16[1024,512]{1,0:T(8,128)(2,1)S(1)}, bf16[1024,512]{1,0:T(8,128)(2,1)}, u32[]{:S(2)}) copy-start(bf16[1024,512]{1,0:T(8,128)(2,1)} %refs_3_.7) | copy-start | bytes 3145732
  0.6 9.8 %copy-start.1 = (bf16[1024,1024]{1,0:T(8,128)(2,1)S(1)}, bf16[1024,1024]{1,0:T(8,128)(2,1)}, u32[]{:S(2)}) copy-start(bf16[1024,1024]{1,0:T(8,128)(2,1)} %refs_2_.4) | copy-start | bytes 6291460
  0.7 9.8 %copy-start.4 = (s32[1024,1]{0,1:T(1,128)S(1)}, s32[1024,1]{0,1:T(1,128)}, u32[]{:S(2)}) copy-start(s32[1024,1]{0,1:T(1,128)} %param.9) | copy-start | bytes 12292
  6.2 34.5 %collective-permute-start = (bf16[1040,128]{1,0:T(8,128)(2,1)}, bf16[1040,128]{1,0:T(8,128)(2,1)S(1)}, u32[]{:S(2)}, u32[]{:S(2)}) collective-permute-start(bf16[1040,128]{1,0:T(8,128)(2,1)} %get-tuple-element.85), channel_id=1, source_target_pairs={{0,8},{8,0},{9,1},{4,12},{5,13},{12,4},{13,5},{1,9},{2,10},{10,2},... | collective-permute-start | bytes 798728 | tf_op jit(solution)/shard_map/ppermute | solution.py:544
  10.3 34.5 %collective-permute-start.1 = (bf16[1040,128]{1,0:T(8,128)(2,1)}, bf16[1040,128]{1,0:T(8,128)(2,1)}, u32[]{:S(2)}, u32[]{:S(2)}) collective-permute-start(bf16[1040,128]{1,0:T(8,128)(2,1)} %get-tuple-element.86), channel_id=1, source_target_pairs={{0,9},{8,1},{9,0},{4,13},{5,12},{12,5},{13,4},{1,8},{2,11},{10,3},... | collective-permute-start | bytes 798728 | tf_op jit(solution)/shard_map/ppermute | solution.py:544
  10.4 1.2 copy-start.2
  11.7 0.7 copy-start.5
  12.3 33.9 %copy-start.3 = (bf16[1024,512]{1,0:T(8,128)(2,1)S(1)}, bf16[1024,512]{1,0:T(8,128)(2,1)}, u32[]{:S(2)}) copy-start(bf16[1024,512]{1,0:T(8,128)(2,1)} %refs_4_.3) | copy-start | bytes 3145732
  17.2 36.4 %collective-permute-start.3 = (bf16[1040,128]{1,0:T(8,128)(2,1)S(1)}, bf16[1040,128]{1,0:T(8,128)(2,1)S(1)}, u32[]{:S(2)}, u32[]{:S(2)}) collective-permute-start(bf16[1040,128]{1,0:T(8,128)(2,1)S(1)} %get-tuple-element.87), channel_id=1, source_target_pairs={{0,5},{8,13},{9,12},{4,9},{5,8},{12,1},{13,0},{1,4},{2,7},{10,15},... | collective-permute-start | bytes 798728 | tf_op jit(solution)/shard_map/ppermute | solution.py:544
  18.9 34.8 %collective-permute-start.2 = (bf16[1040,128]{1,0:T(8,128)(2,1)S(1)}, bf16[1040,128]{1,0:T(8,128)(2,1)S(1)}, u32[]{:S(2)}, u32[]{:S(2)}) collective-permute-start(bf16[1040,128]{1,0:T(8,128)(2,1)S(1)} %get-tuple-element.81.refs_4_), channel_id=1, source_target_pairs={{0,4},{8,12},{9,13},{4,8},{5,9},{12,0},{13,1},{1,5},{2,6},{10,14},... | collective-permute-start | bytes 798728 | tf_op jit(solution)/shard_map/ppermute | solution.py:544
  20.4 35.6 %collective-permute-start.4 = (bf16[1040,128]{1,0:T(8,128)(2,1)S(1)}, bf16[1040,128]{1,0:T(8,128)(2,1)S(1)}, u32[]{:S(2)}, u32[]{:S(2)}) collective-permute-start(bf16[1040,128]{1,0:T(8,128)(2,1)S(1)} %get-tuple-element.88), channel_id=1, source_target_pairs={{0,12},{8,4},{9,5},{4,0},{5,1},{12,8},{13,9},{1,13},{2,14},{10,6},... | collective-permute-start | bytes 798728 | tf_op jit(solution)/shard_map/ppermute | solution.py:544
  40.7 15.3 %collective-permute-start.5 = (bf16[1040,128]{1,0:T(8,128)(2,1)S(1)}, bf16[1040,128]{1,0:T(8,128)(2,1)S(1)}, u32[]{:S(2)}, u32[]{:S(2)}) collective-permute-start(bf16[1040,128]{1,0:T(8,128)(2,1)S(1)} %get-tuple-element.89), channel_id=1, source_target_pairs={{0,13},{8,5},{9,4},{4,1},{5,0},{12,9},{13,8},{1,12},{2,15},{10,7},... | collective-permute-start | bytes 798728 | tf_op jit(solution)/shard_map/ppermute | solution.py:544
  44.8 11.2 %collective-permute-start.6 = (bf16[1040,128]{1,0:T(8,128)(2,1)S(1)}, bf16[1040,128]{1,0:T(8,128)(2,1)S(1)}, u32[]{:S(2)}, u32[]{:S(2)}) collective-permute-start(bf16[1040,128]{1,0:T(8,128)(2,1)S(1)} %get-tuple-element.90), channel_id=1, source_target_pairs={{0,1},{8,9},{9,8},{4,5},{5,4},{12,13},{13,12},{1,0},{2,3},{10,11},... | collective-permute-start | bytes 798728 | tf_op jit(solution)/shard_map/ppermute | solution.py:544
  52.3 1.3 copy-start.6
  53.6 7.1 %collective-permute-start.13 = (bf16[512,128]{1,0:T(8,128)(2,1)S(1)}, bf16[512,128]{1,0:T(8,128)(2,1)S(1)}, u32[]{:S(2)}, u32[]{:S(2)}) collective-permute-start(bf16[512,128]{1,0:T(8,128)(2,1)S(1)} %get-tuple-element.112), channel_id=1, source_target_pairs={{0,1},{8,9},{9,8},{4,5},{5,4},{12,13},{13,12},{1,0},{2,3},{10,11},... | collective-permute-start | bytes 393224 | tf_op jit(solution)/shard_map/ppermute | solution.py:544
  53.6 10.9 %collective-permute-start.12 = (bf16[512,128]{1,0:T(8,128)(2,1)S(1)}, bf16[512,128]{1,0:T(8,128)(2,1)S(1)}, u32[]{:S(2)}, u32[]{:S(2)}) collective-permute-start(bf16[512,128]{1,0:T(8,128)(2,1)S(1)} %get-tuple-element.110), channel_id=1, source_target_pairs={{0,13},{8,5},{9,4},{4,1},{5,0},{12,9},{13,8},{1,12},{2,15},{10,7},... | collective-permute-start | bytes 393224 | tf_op jit(solution)/shard_map/ppermute | solution.py:544
  56.0 22.7 %collective-permute-start.11 = (bf16[512,128]{1,0:T(8,128)(2,1)S(1)}, bf16[512,128]{1,0:T(8,128)(2,1)S(1)}, u32[]{:S(2)}, u32[]{:S(2)}) collective-permute-start(bf16[512,128]{1,0:T(8,128)(2,1)S(1)} %get-tuple-element.108), channel_id=1, source_target_pairs={{0,12},{8,4},{9,5},{4,0},{5,1},{12,8},{13,9},{1,13},{2,14},{10,6},... | collective-permute-start | bytes 393224 | tf_op jit(solution)/shard_map/ppermute | solution.py:544
  60.7 18.0 %collective-permute-start.10 = (bf16[512,128]{1,0:T(8,128)(2,1)S(1)}, bf16[512,128]{1,0:T(8,128)(2,1)S(1)}, u32[]{:S(2)}, u32[]{:S(2)}) collective-permute-start(bf16[512,128]{1,0:T(8,128)(2,1)S(1)} %get-tuple-element.106), channel_id=1, source_target_pairs={{0,5},{8,13},{9,12},{4,9},{5,8},{12,1},{13,0},{1,4},{2,7},{10,15},... | collective-permute-start | bytes 393224 | tf_op jit(solution)/shard_map/ppermute | solution.py:544
  60.7 18.0 %collective-permute-start.9 = (bf16[512,128]{1,0:T(8,128)(2,1)S(1)}, bf16[512,128]{1,0:T(8,128)(2,1)S(1)}, u32[]{:S(2)}, u32[]{:S(2)}) collective-permute-start(bf16[512,128]{1,0:T(8,128)(2,1)S(1)} %get-tuple-element.104), channel_id=1, source_target_pairs={{0,4},{8,12},{9,13},{4,8},{5,9},{12,0},{13,1},{1,5},{2,6},{10,14},... | collective-permute-start | bytes 393224 | tf_op jit(solution)/shard_map/ppermute | solution.py:544
  60.7 19.0 %collective-permute-start.8 = (bf16[512,128]{1,0:T(8,128)(2,1)S(1)}, bf16[512,128]{1,0:T(8,128)(2,1)S(1)}, u32[]{:S(2)}, u32[]{:S(2)}) collective-permute-start(bf16[512,128]{1,0:T(8,128)(2,1)S(1)} %get-tuple-element.102), channel_id=1, source_target_pairs={{0,9},{8,1},{9,0},{4,13},{5,12},{12,5},{13,4},{1,8},{2,11},{10,3},... | collective-permute-start | bytes 393224 | tf_op jit(solution)/shard_map/ppermute | solution.py:544
  64.6 18.4 %collective-permute-start.7 = (bf16[512,128]{1,0:T(8,128)(2,1)S(1)}, bf16[512,128]{1,0:T(8,128)(2,1)S(1)}, u32[]{:S(2)}, u32[]{:S(2)}) collective-permute-start(bf16[512,128]{1,0:T(8,128)(2,1)S(1)} %get-tuple-element.100), channel_id=1, source_target_pairs={{0,8},{8,0},{9,1},{4,12},{5,13},{12,4},{13,5},{1,9},{2,10},{10,2},... | collective-permute-start | bytes 393224 | tf_op jit(solution)/shard_map/ppermute | solution.py:544
  82.9 22.8 %collective-permute-start.14 = (bf16[512,128]{1,0:T(8,128)(2,1)S(1)}, bf16[512,128]{1,0:T(8,128)(2,1)S(1)}, u32[]{:S(2)}, u32[]{:S(2)}) collective-permute-start(bf16[512,128]{1,0:T(8,128)(2,1)S(1)} %get-tuple-element.114), channel_id=1, source_target_pairs={{0,8},{8,0},{9,1},{4,12},{5,13},{12,4},{13,5},{1,9},{2,10},{10,2},... | collective-permute-start | bytes 393224 | tf_op jit(solution)/shard_map/ppermute | solution.py:544
  82.9 22.8 %collective-permute-start.15 = (bf16[512,128]{1,0:T(8,128)(2,1)S(1)}, bf16[512,128]{1,0:T(8,128)(2,1)S(1)}, u32[]{:S(2)}, u32[]{:S(2)}) collective-permute-start(bf16[512,128]{1,0:T(8,128)(2,1)S(1)} %get-tuple-element.115), channel_id=1, source_target_pairs={{0,9},{8,1},{9,0},{4,13},{5,12},{12,5},{13,4},{1,8},{2,11},{10,3},... | collective-permute-start | bytes 393224 | tf_op jit(solution)/shard_map/ppermute | solution.py:544
  84.9 22.8 %collective-permute-start.16 = (bf16[512,128]{1,0:T(8,128)(2,1)S(1)}, bf16[512,128]{1,0:T(8,128)(2,1)S(1)}, u32[]{:S(2)}, u32[]{:S(2)}) collective-permute-start(bf16[512,128]{1,0:T(8,128)(2,1)S(1)} %get-tuple-element.116), channel_id=1, source_target_pairs={{0,4},{8,12},{9,13},{4,8},{5,9},{12,0},{13,1},{1,5},{2,6},{10,14},... | collective-permute-start | bytes 393224 | tf_op jit(solution)/shard_map/ppermute | solution.py:544
  84.9 24.6 %collective-permute-start.17 = (bf16[512,128]{1,0:T(8,128)(2,1)S(1)}, bf16[512,128]{1,0:T(8,128)(2,1)S(1)}, u32[]{:S(2)}, u32[]{:S(2)}) collective-permute-start(bf16[512,128]{1,0:T(8,128)(2,1)S(1)} %get-tuple-element.117), channel_id=1, source_target_pairs={{0,5},{8,13},{9,12},{4,9},{5,8},{12,1},{13,0},{1,4},{2,7},{10,15},... | collective-permute-start | bytes 393224 | tf_op jit(solution)/shard_map/ppermute | solution.py:544
  85.9 42.7 %copy-start.7 = (bf16[1024,1024]{1,0:T(8,128)(2,1)S(1)}, bf16[1024,1024]{1,0:T(8,128)(2,1)}, u32[]{:S(2)}) copy-start(bf16[1024,1024]{1,0:T(8,128)(2,1)} %copy-done.6) | copy-start | bytes 6291460
  101.8 25.9 %collective-permute-start.21 = (bf16[544,128]{1,0:T(8,128)(2,1)S(1)}, bf16[544,128]{1,0:T(8,128)(2,1)S(1)}, u32[]{:S(2)}, u32[]{:S(2)}) collective-permute-start(bf16[544,128]{1,0:T(8,128)(2,1)S(1)} %get-tuple-element.127), channel_id=1, source_target_pairs={{0,8},{8,0},{9,1},{4,12},{5,13},{12,4},{13,5},{1,9},{2,10},{10,2},... | collective-permute-start | bytes 417800 | tf_op jit(solution)/shard_map/ppermute | solution.py:544
  105.7 22.7 %collective-permute-start.22 = (bf16[544,128]{1,0:T(8,128)(2,1)S(1)}, bf16[544,128]{1,0:T(8,128)(2,1)S(1)}, u32[]{:S(2)}, u32[]{:S(2)}) collective-permute-start(bf16[544,128]{1,0:T(8,128)(2,1)S(1)} %get-tuple-element.128), channel_id=1, source_target_pairs={{0,9},{8,1},{9,0},{4,13},{5,12},{12,5},{13,4},{1,8},{2,11},{10,3},... | collective-permute-start | bytes 417800 | tf_op jit(solution)/shard_map/ppermute | solution.py:544
  105.7 9.9 %collective-permute-start.18 = (bf16[512,128]{1,0:T(8,128)(2,1)S(1)}, bf16[512,128]{1,0:T(8,128)(2,1)S(1)}, u32[]{:S(2)}, u32[]{:S(2)}) collective-permute-start(bf16[512,128]{1,0:T(8,128)(2,1)S(1)} %get-tuple-element.118), channel_id=1, source_target_pairs={{0,12},{8,4},{9,5},{4,0},{5,1},{12,8},{13,9},{1,13},{2,14},{10,6},... | collective-permute-start | bytes 393224 | tf_op jit(solution)/shard_map/ppermute | solution.py:544
  107.8 17.0 %collective-permute-start.19 = (bf16[512,128]{1,0:T(8,128)(2,1)S(1)}, bf16[512,128]{1,0:T(8,128)(2,1)S(1)}, u32[]{:S(2)}, u32[]{:S(2)}) collective-permute-start(bf16[512,128]{1,0:T(8,128)(2,1)S(1)} %get-tuple-element.119), channel_id=1, source_target_pairs={{0,13},{8,5},{9,4},{4,1},{5,0},{12,9},{13,8},{1,12},{2,15},{10,7},... | collective-permute-start | bytes 393224 | tf_op jit(solution)/shard_map/ppermute | solution.py:544
  109.5 17.4 %collective-permute-start.20 = (bf16[512,128]{1,0:T(8,128)(2,1)S(1)}, bf16[512,128]{1,0:T(8,128)(2,1)S(1)}, u32[]{:S(2)}, u32[]{:S(2)}) collective-permute-start(bf16[512,128]{1,0:T(8,128)(2,1)S(1)} %get-tuple-element.120), channel_id=1, source_target_pairs={{0,1},{8,9},{9,8},{4,5},{5,4},{12,13},{13,12},{1,0},{2,3},{10,11},... | collective-permute-start | bytes 393224 | tf_op jit(solution)/shard_map/ppermute | solution.py:544
  115.5 15.5 %collective-permute-start.23 = (bf16[544,128]{1,0:T(8,128)(2,1)S(1)}, bf16[544,128]{1,0:T(8,128)(2,1)S(1)}, u32[]{:S(2)}, u32[]{:S(2)}) collective-permute-start(bf16[544,128]{1,0:T(8,128)(2,1)S(1)} %get-tuple-element.129), channel_id=1, source_target_pairs={{0,4},{8,12},{9,13},{4,8},{5,9},{12,0},{13,1},{1,5},{2,6},{10,14},... | collective-permute-start | bytes 417800 | tf_op jit(solution)/shard_map/ppermute | solution.py:544
  124.8 7.7 %collective-permute-start.24 = (bf16[544,128]{1,0:T(8,128)(2,1)S(1)}, bf16[544,128]{1,0:T(8,128)(2,1)S(1)}, u32[]{:S(2)}, u32[]{:S(2)}) collective-permute-start(bf16[544,128]{1,0:T(8,128)(2,1)S(1)} %get-tuple-element.130), channel_id=1, source_target_pairs={{0,5},{8,13},{9,12},{4,9},{5,8},{12,1},{13,0},{1,4},{2,7},{10,15},... | collective-permute-start | bytes 417800 | tf_op jit(solution)/shard_map/ppermute | solution.py:544
  126.9 8.3 %collective-permute-start.25 = (bf16[544,128]{1,0:T(8,128)(2,1)S(1)}, bf16[544,128]{1,0:T(8,128)(2,1)S(1)}, u32[]{:S(2)}, u32[]{:S(2)}) collective-permute-start(bf16[544,128]{1,0:T(8,128)(2,1)S(1)} %get-tuple-element.131), channel_id=1, source_target_pairs={{0,12},{8,4},{9,5},{4,0},{5,1},{12,8},{13,9},{1,13},{2,14},{10,6},... | collective-permute-start | bytes 417800 | tf_op jit(solution)/shard_map/ppermute | solution.py:544
  127.7 10.5 %collective-permute-start.26 = (bf16[544,128]{1,0:T(8,128)(2,1)S(1)}, bf16[544,128]{1,0:T(8,128)(2,1)S(1)}, u32[]{:S(2)}, u32[]{:S(2)}) collective-permute-start(bf16[544,128]{1,0:T(8,128)(2,1)S(1)} %get-tuple-element.132), channel_id=1, source_target_pairs={{0,13},{8,5},{9,4},{4,1},{5,0},{12,9},{13,8},{1,12},{2,15},{10,7},... | collective-permute-start | bytes 417800 | tf_op jit(solution)/shard_map/ppermute | solution.py:544
  128.4 9.8 %collective-permute-start.27 = (bf16[544,128]{1,0:T(8,128)(2,1)S(1)}, bf16[544,128]{1,0:T(8,128)(2,1)S(1)}, u32[]{:S(2)}, u32[]{:S(2)}) collective-permute-start(bf16[544,128]{1,0:T(8,128)(2,1)S(1)} %get-tuple-element.133), channel_id=1, source_target_pairs={{0,1},{8,9},{9,8},{4,5},{5,4},{12,13},{13,12},{1,0},{2,3},{10,11},... | collective-permute-start | bytes 417800 | tf_op jit(solution)/shard_map/ppermute | solution.py:544
  140.2 26.3 %collective-permute-start.29 = (bf16[1024,512]{1,0:T(8,128)(2,1)S(1)}, bf16[1024,512]{1,0:T(8,128)(2,1)S(1)}, u32[]{:S(2)}, u32[]{:S(2)}) collective-permute-start(bf16[1024,512]{1,0:T(8,128)(2,1)S(1)} %get-tuple-element.139), channel_id=1, source_target_pairs={{0,2},{2,0},{1,3},{3,1},{4,6},{6,4},{5,7},{7,5},{8,10},{10,8},{9,1... | collective-permute-start | bytes 3145736 | tf_op jit(solution)/shard_map/ppermute | solution.py:550
  141.7 2.4 %collective-permute-start.33 = (bf16[4,128,512]{2,1,0:T(8,128)(2,1)S(1)}, bf16[4,128,512]{2,1,0:T(8,128)(2,1)S(1)}, u32[]{:S(2)}, u32[]{:S(2)}) collective-permute-start(bf16[4,128,512]{2,1,0:T(8,128)(2,1)S(1)} %get-tuple-element.146), channel_id=1, source_target_pairs={{0,1},{1,0},{2,3},{3,2},{4,5},{5,4},{6,7},{7,6},{8,9},{9,8},{10,11... | collective-permute-start | bytes 1572872 | tf_op jit(solution)/shard_map/ppermute | solution.py:550
  143.5 5.1 %collective-permute-start.28 = (bf16[4,128,512]{2,1,0:T(8,128)(2,1)S(1)}, bf16[4,128,512]{2,1,0:T(8,128)(2,1)S(1)}, u32[]{:S(2)}, u32[]{:S(2)}) collective-permute-start(bf16[4,128,512]{2,1,0:T(8,128)(2,1)S(1)} %get-tuple-element.136), channel_id=1, source_target_pairs={{0,1},{1,0},{2,3},{3,2},{4,5},{5,4},{6,7},{7,6},{8,9},{9,8},{10,11... | collective-permute-start | bytes 1572872 | tf_op jit(solution)/shard_map/ppermute | solution.py:550
  144.7 8.3 %collective-permute-start.34 = (bf16[128,512]{1,0:T(8,128)(2,1)S(1)}, bf16[128,512]{1,0:T(8,128)(2,1)S(1)}, u32[]{:S(2)}, u32[]{:S(2)}) collective-permute-start(bf16[128,512]{1,0:T(8,128)(2,1)S(1)} %get-tuple-element.152), channel_id=1, source_target_pairs={{0,4},{4,8},{8,12},{12,0},{1,5},{5,9},{9,13},{13,1},{2,6},{6,10},{... | collective-permute-start | bytes 393224 | tf_op jit(solution)/shard_map/ppermute | solution.py:550
  145.3 13.4 %collective-permute-start.35 = (bf16[128,512]{1,0:T(8,128)(2,1)S(1)}, bf16[128,512]{1,0:T(8,128)(2,1)S(1)}, u32[]{:S(2)}, u32[]{:S(2)}) collective-permute-start(bf16[128,512]{1,0:T(8,128)(2,1)S(1)} %get-tuple-element.153), channel_id=1, source_target_pairs={{0,8},{4,12},{8,0},{12,4},{1,9},{5,13},{9,1},{13,5},{2,10},{6,14},... | collective-permute-start | bytes 393224 | tf_op jit(solution)/shard_map/ppermute | solution.py:550
  147.9 17.9 %collective-permute-start.36 = (bf16[128,512]{1,0:T(8,128)(2,1)S(1)}, bf16[128,512]{1,0:T(8,128)(2,1)S(1)}, u32[]{:S(2)}, u32[]{:S(2)}) collective-permute-start(bf16[128,512]{1,0:T(8,128)(2,1)S(1)} %get-tuple-element.154), channel_id=1, source_target_pairs={{0,12},{4,0},{8,4},{12,8},{1,13},{5,1},{9,5},{13,9},{2,14},{6,2},{... | collective-permute-start | bytes 393224 | tf_op jit(solution)/shard_map/ppermute | solution.py:550
  149.3 19.5 %collective-permute-start.30 = (bf16[128,512]{1,0:T(8,128)(2,1)S(1)}, bf16[128,512]{1,0:T(8,128)(2,1)S(1)}, u32[]{:S(2)}, u32[]{:S(2)}) collective-permute-start(bf16[128,512]{1,0:T(8,128)(2,1)S(1)} %get-tuple-element.142), channel_id=1, source_target_pairs={{0,4},{4,8},{8,12},{12,0},{1,5},{5,9},{9,13},{13,1},{2,6},{6,10},{... | collective-permute-start | bytes 393224 | tf_op jit(solution)/shard_map/ppermute | solution.py:550
  153.1 15.9 %collective-permute-start.31 = (bf16[128,512]{1,0:T(8,128)(2,1)S(1)}, bf16[128,512]{1,0:T(8,128)(2,1)S(1)}, u32[]{:S(2)}, u32[]{:S(2)}) collective-permute-start(bf16[128,512]{1,0:T(8,128)(2,1)S(1)} %get-tuple-element.143), channel_id=1, source_target_pairs={{0,8},{4,12},{8,0},{12,4},{1,9},{5,13},{9,1},{13,5},{2,10},{6,14},... | collective-permute-start | bytes 393224 | tf_op jit(solution)/shard_map/ppermute | solution.py:550
  158.7 10.3 %collective-permute-start.32 = (bf16[128,512]{1,0:T(8,128)(2,1)S(1)}, bf16[128,512]{1,0:T(8,128)(2,1)S(1)}, u32[]{:S(2)}, u32[]{:S(2)}) collective-permute-start(bf16[128,512]{1,0:T(8,128)(2,1)S(1)} %get-tuple-element.144), channel_id=1, source_target_pairs={{0,12},{4,0},{8,4},{12,8},{1,13},{5,1},{9,5},{13,9},{2,14},{6,2},{... | collective-permute-start | bytes 393224 | tf_op jit(solution)/shard_map/ppermute | solution.py:550

commit v17 on v16

--- a/solution.py
+++ b/solution.py
@@ -87,6 +87,23 @@
     slot = jnp.sum(member * (running - 1.0 + base), axis=0, keepdims=True).astype(jnp.int32)
     spread = jnp.concatenate([member_b, jnp.zeros((LANES - CLUSTERS, toks), BF16)], axis=0)
     return slot, dot_nt(jnp.ones((COUNT_ROWS, toks), BF16), spread).astype(BF16)
+
+
+def arrivals(sizes, me_ref, refs):
+    seqs, subs = sizes
+    for ahead in steps_of(sizes):
+        if ahead[1] == 0:
+            piece = refs[ahead[0]][me_ref[1]]
+        else:
+            piece = refs[seqs + ahead[1] - 1][ahead[0]]
+        yield source_of(me_ref, ahead, sizes), piece
+
+
+def swap_kernel(sizes, me_ref, *refs):
+    for k, out_ref in enumerate(refs[sizes[0] :]):
+        sub = lax.rem(me_ref[1] + (k + 1), jnp.int32(sizes[1]))
+        for seq in range(sizes[0]):
+            out_ref[seq] = refs[seq][sub]
 
 
 def beside(query, cotan):
@@ -295,10 +312,10 @@
 
 def value_grad_kernel(sizes, per_group, slot_rows, me_ref, *refs):
     owners = sizes[0] * sizes[1]
-    mixed_refs, out_refs, rest = refs[:owners], refs[owners : 2 * owners], refs[2 * owners :]
+    mixed_refs, out_refs, rest = refs[:owners], refs[owners : owners + sizes[0]], refs[owners + sizes[0] :]
     dense_ref, counts_out_ref, counts_ref, place_ref, wide_ref, block_ref, home_ref = rest[:7]
     score_refs, probs_refs = rest[7:9], rest[9:11]
-    half = out_refs[0].shape[0]
+    half = out_refs[0].shape[1]
     rows = 2 * half
     for ahead, mixed_ref in zip(steps_of(sizes), mixed_refs):
         source = source_of(me_ref, ahead, sizes)
@@ -333,10 +350,11 @@
             wide_ref[source, pl.ds(start, slot_rows), :] = block_ref[pl.ds(row, slot_rows), :]
 
     for_each_cluster(counts_ref, me_ref, place_ref, owners, per_group, scatter)
-    for ahead, out_ref in zip(steps_of(sizes), out_refs):
-        source = owner_of(me_ref, ahead, sizes)
-        up, down = wide_ref[source, :half, :], wide_ref[source, half:rows, :]
-        out_ref[...] = jnp.where(low_half((half, LANES)), swap_halves(up), down).astype(BF16)
+    for ahead, out_ref in enumerate(out_refs):
+        for sub in range(sizes[1]):
+            source = owner_of(me_ref, (ahead, 0), sizes) - me_ref[1] + sub
+            up, down = wide_ref[source, :half, :], wide_ref[source, half:rows, :]
+            out_ref[sub] = jnp.where(low_half((half, LANES)), swap_halves(up), down).astype(BF16)
 
 
 def query_grad_kernel(sizes, per_group, slot_rows, me_ref, counts_ref, dense_ref, *refs):
@@ -423,9 +441,9 @@
     return x.astype(BF16)
 
 
-def bring_home(sizes, heads, me_ref, part_refs, home_ref, rows_ref):
-    for ahead, part_ref in zip(steps_of(sizes), part_refs):
-        home_ref[source_of(me_ref, ahead, sizes)] = part_ref[...]
+def bring_home(sizes, heads, pieces, home_ref, rows_ref):
+    for source, piece in pieces:
+        home_ref[source] = piece
     unfold(home_ref, rows_ref, heads, 0, rows_ref.shape[0] * heads // home_ref.shape[0] // 2, to_half)
 
 
@@ -447,10 +465,11 @@
 
 
 def value_home_kernel(sizes, heads, parts, me_ref, turned_ref, weight_ref, *refs):
-    part_refs, refs = refs[: sizes[0] * sizes[1]], refs[sizes[0] * sizes[1] :]
+    came = sizes[0] + sizes[1] - 1
+    part_refs, refs = refs[:came], refs[came:]
     rows_ref, term_refs, refs = refs[0], refs[1:parts], refs[parts:]
     sub_refs, home_ref = refs[: sizes[1]], refs[sizes[1]]
-    bring_home(sizes, heads, me_ref, part_refs, home_ref, rows_ref)
+    bring_home(sizes, heads, arrivals(sizes, me_ref, part_refs), home_ref, rows_ref)
     for k, term_ref in enumerate(term_refs):
         mine = input_columns(me_ref, k + 1, parts, weight_ref.shape[0])
         term_ref[...] = dot_nt(rows_ref[...], weight_ref[mine, :])
@@ -461,7 +480,10 @@
     term_refs, refs = refs[: parts - 1], refs[parts - 1 :]
     part_refs, refs = refs[: sizes[0] * sizes[1]], refs[sizes[0] * sizes[1] :]
     out_refs, (rows_ref, centroid_ref, home_ref) = refs[: parts - 1], refs[parts - 1 :]
-    bring_home(sizes, heads, me_ref, part_refs, home_ref, rows_ref)
+    pieces = [
+        (source_of(me_ref, ahead, sizes), part_ref[...]) for ahead, part_ref in zip(steps_of(sizes), part_refs)
+    ]
+    bring_home(sizes, heads, pieces, home_ref, rows_ref)
     for k, (term_ref, out_ref) in enumerate(zip(term_refs, out_refs)):
         mine = input_columns(me_ref, k + 1, parts, weight_ref.shape[0])
         out_ref[...] = (dot_nt(rows_ref[...], weight_ref[mine, :]) + term_ref[...]).astype(BF16)
@@ -552,6 +574,18 @@
 
 def pass_round(parts, axis):
     return [parts[0]] + [shift(parts[ahead], axis, ahead) for ahead in range(1, len(parts))]
+
+
+def exchange_by_chip(me, parts, sizes, name, after=()):
+    came = pass_round(parts, "seq")
+    swapped = call(
+        functools.partial(swap_kernel, sizes),
+        (jax.ShapeDtypeStruct((sizes[0], *parts[0].shape[1:]), BF16),) * (sizes[1] - 1),
+        (me, *came),
+        after=after,
+        name=name,
+    )
+    return came + [shift(part, "sub", k + 1) for k, part in enumerate(swapped)]
 
 
 def fold_subs(me, by_sub, name):
@@ -644,7 +678,7 @@
     place = pltpu.SMEM((owners,), jnp.int32)
     *back_value, dense, counts = call(
         functools.partial(value_grad_kernel, sizes, per_group, slot_rows),
-        several(owners, half, LANES)
+        several(sizes[0], sizes[1], half, LANES)
         + several(1, held * BLOCK_ROWS, LANES)
         + (shape((owners, LANES), jnp.int32),),
         (me, *got_mixed),
@@ -657,7 +691,6 @@
         name="value_grad",
     )
     back_value, _ = lax.optimization_barrier((back_value, got_value[1:]))
-    home_value = exchange(back_value, sizes)
     back_query = call(
         functools.partial(query_grad_kernel, sizes, per_group, slot_rows),
         several(owners, half + extra, LANES),
@@ -671,6 +704,7 @@
         name="query_grad",
     )
     home_query = exchange(back_query, sizes)
+    home_value = exchange_by_chip(me, back_value, sizes, "swap", home_query[1:3])
     weight_flops = 2 * slots * width * width_dev
     home_flops = weight_flops // parts * (parts - 1)
     piece = width // owners

time: 170 us -> 168 us (0.988)
  starting transfers between devices: 58.6 us -> 47.2 us
  waiting for transfers between devices: 47.9 us -> 57.9 us
    ppermute x28 -> x21, starting transfers between devices: 46.2 us -> 31.5 us  [exchange(): out.append(part if ahead == (0, 0) else lax.ppermute(part, OWNERS, moves))]
    ppermute x28 -> x21, waiting for transfers between devices: 39.6 us -> 48.1 us  [exchange(): out.append(part if ahead == (0, 0) else lax.ppermute(part, OWNERS, moves))]
    ppermute x9 -> x13, starting transfers between devices: 12.4 us -> 15.7 us  [shift(): lax.ppermute(part, axis, [(i, (i + ahead) % size) for i in range(size)])]
    ppermute x9 -> x13, waiting for transfers between devices: 8.31 us -> 9.77 us  [shift(): lax.ppermute(part, axis, [(i, (i + ahead) % size) for i in range(size)])]
    pallas_call x14 -> x15, Pallas kernels: 59.1 us -> 59.6 us  [call(): pl.pallas_call(body, out_shape=outs, in_specs=specs, out_specs=jax.tree.m...]
  transfers between devices with their start and end apart: 37 -> 34, of which waited for: 11 -> 14; matrix products, arithmetic and copies ran while one was open for 0% -> 0% of each run, Pallas kernels for 30% -> 30%
where the time goes in v17:
time: 168 us
  Pallas kernels  59.6 us (35%)
  waiting for transfers between devices  57.9 us (34%)
  starting transfers between devices  47.2 us (28%)
  local copies, waits for them, and re-layouts  1.93 us (1%)
    pallas_call x15, Pallas kernels, call(): pl.pallas_call(body, out_shape=outs, in_specs=specs, out_specs=jax.tree.m...  59.6 us
    ppermute x21, waiting for transfers between devices, exchange(): out.append(part if ahead == (0, 0) else lax.ppermute(part, OWNERS, moves))  48.1 us
    ppermute x21, starting transfers between devices, exchange(): out.append(part if ahead == (0, 0) else lax.ppermute(part, OWNERS, moves))  31.5 us
    ppermute x13, starting transfers between devices, shift(): lax.ppermute(part, axis, [(i, (i + ahead) % size) for i in range(size)])  15.7 us
    ppermute x13, waiting for transfers between devices, shift(): lax.ppermute(part, axis, [(i, (i + ahead) % size) for i in range(size)])  9.77 us
  transfers between devices with their start and end apart: 34, of which 14 were waited for; matrix products, arithmetic and copies ran while one was open for 0% of the time, Pallas kernels for 30%

profile of v17, /device:TPU:0, one launch (start us, length us, event | category | flops | bytes accessed | tf_op | source)
XLA Modules:
  0.0 167.5 jit_solution(701557026341994888)
XLA Ops:
  0.7 5.6 %project_far.1 = (bf16[1040,128]{1,0:T(8,128)(2,1)}, bf16[1040,128]{1,0:T(8,128)(2,1)}, s32[1,1024]{1,0:T(1,128)}) custom-call(s32[1,1024]{1,0:T(1,128)} %bitcast.5, bf16[1024,1024]{1,0:T(8,128)(2,1)} %refs_2_.4, bf16[1024,512]{1,0:T(8,128)(2,1)} %refs_3_.7, bf16[1024,512]{1,0:T(8,128)(2,1)} %refs_5_.1), custom_call_target="tpu_custom_call" | custom-call | flops 805306368 | bytes 4734976 | tf_op jit(solution)/shard_map/project_far/pallas_call | solution.py:544
  6.2 4.1 %collective-permute-start = (bf16[1040,128]{1,0:T(8,128)(2,1)}, bf16[1040,128]{1,0:T(8,128)(2,1)S(1)}, u32[]{:S(2)}, u32[]{:S(2)}) collective-permute-start(bf16[1040,128]{1,0:T(8,128)(2,1)} %get-tuple-element.77), channel_id=1, source_target_pairs={{0,8},{8,0},{9,1},{4,12},{5,13},{12,4},{13,5},{1,9},{2,10},{10,2},... | collective-permute-start | bytes 798728 | tf_op jit(solution)/shard_map/ppermute | solution.py:566
  10.4 1.2 copy-done.2
  11.7 0.7 copy-done.5
  12.4 4.8 %project_query.1 = (bf16[1040,128]{1,0:T(8,128)(2,1)S(1)}, bf16[1040,128]{1,0:T(8,128)(2,1)S(1)}, bf16[1040,128]{1,0:T(8,128)(2,1)S(1)}, bf16[1040,128]{1,0:T(8,...) custom-call(s32[4]{0:T(128)S(1)} %pad_add_fusion.refs_0_, s32[1,1024]{1,0:T(1,128)S(1)} %copy-done.5, ...), custom_call_target="tpu_custom_call" | custom-call | flops 3221225472 | bytes 5799952 | tf_op jit(solution)/shard_map/project_query/pallas_call | solution.py:544
  17.2 1.7 %collective-permute-start.3 = (bf16[1040,128]{1,0:T(8,128)(2,1)S(1)}, bf16[1040,128]{1,0:T(8,128)(2,1)S(1)}, u32[]{:S(2)}, u32[]{:S(2)}) collective-permute-start(bf16[1040,128]{1,0:T(8,128)(2,1)S(1)} %get-tuple-element.79), channel_id=1, source_target_pairs={{0,5},{8,13},{9,12},{4,9},{5,8},{12,1},{13,0},{1,4},{2,7},{10,15},... | collective-permute-start | bytes 798728 | tf_op jit(solution)/shard_map/ppermute | solution.py:566
  18.9 1.6 collective-permute-start.2
  20.4 2.2 %collective-permute-start.4 = (bf16[1040,128]{1,0:T(8,128)(2,1)S(1)}, bf16[1040,128]{1,0:T(8,128)(2,1)S(1)}, u32[]{:S(2)}, u32[]{:S(2)}) collective-permute-start(bf16[1040,128]{1,0:T(8,128)(2,1)S(1)} %get-tuple-element.80), channel_id=1, source_target_pairs={{0,12},{8,4},{9,5},{4,0},{5,1},{12,8},{13,9},{1,13},{2,14},{10,6},... | collective-permute-start | bytes 798728 | tf_op jit(solution)/shard_map/ppermute | solution.py:566
  22.7 18.0 %collective-permute-done.refs_2_ = bf16[1040,128]{1,0:T(8,128)(2,1)S(1)} collective-permute-done((bf16[1040,128]{1,0:T(8,128)(2,1)}, bf16[1040,128]{1,0:T(8,128)(2,1)S(1)}, u32[]{:S(2)}, u32[]{:S(2)}) %collective-permute-start) | collective-permute-done | bytes 266272 | tf_op jit(solution)/shard_map/ppermute | solution.py:566
  40.7 4.1 %collective-permute-done.1.refs_3_ = bf16[1040,128]{1,0:T(8,128)(2,1)} collective-permute-done((bf16[1040,128]{1,0:T(8,128)(2,1)}, bf16[1040,128]{1,0:T(8,128)(2,1)}, u32[]{:S(2)}, u32[]{:S(2)}) %collective-permute-start.1) | collective-permute-done | bytes 266272 | tf_op jit(solution)/shard_map/ppermute | solution.py:566
  44.8 1.4 collective-permute-start.6
  46.3 6.0 %project_value.1 = (bf16[512,128]{1,0:T(8,128)(2,1)S(1)}, bf16[512,128]{1,0:T(8,128)(2,1)S(1)}, bf16[512,128]{1,0:T(8,128)(2,1)S(1)}, bf16[512,128]{1,0:T(8,128)...) custom-call(s32[4]{0:T(128)S(1)} %pad_add_fusion.refs_0_, ...), custom_call_target="tpu_custom_call" | custom-call | flops 2147483648 | bytes 8392720 | tf_op jit(solution)/shard_map/project_value/pallas_call | solution.py:544
  52.4 3.6 %collective-permute-start.12 = (bf16[512,128]{1,0:T(8,128)(2,1)S(1)}, bf16[512,128]{1,0:T(8,128)(2,1)S(1)}, u32[]{:S(2)}, u32[]{:S(2)}) collective-permute-start(bf16[512,128]{1,0:T(8,128)(2,1)S(1)} %get-tuple-element.98), channel_id=1, source_target_pairs={{0,13},{8,5},{9,4},{4,1},{5,0},{12,9},{13,8},{1,12},{2,15},{10,7},... | collective-permute-start | bytes 393224 | tf_op jit(solution)/shard_map/ppermute | solution.py:566
  56.0 4.7 %collective-permute-start.11 = (bf16[512,128]{1,0:T(8,128)(2,1)S(1)}, bf16[512,128]{1,0:T(8,128)(2,1)S(1)}, u32[]{:S(2)}, u32[]{:S(2)}) collective-permute-start(bf16[512,128]{1,0:T(8,128)(2,1)S(1)} %get-tuple-element.96), channel_id=1, source_target_pairs={{0,12},{8,4},{9,5},{4,0},{5,1},{12,8},{13,9},{1,13},{2,14},{10,6},... | collective-permute-start | bytes 393224 | tf_op jit(solution)/shard_map/ppermute | solution.py:566
  60.7 3.8 %collective-permute-start.8 = (bf16[512,128]{1,0:T(8,128)(2,1)S(1)}, bf16[512,128]{1,0:T(8,128)(2,1)S(1)}, u32[]{:S(2)}, u32[]{:S(2)}) collective-permute-start(bf16[512,128]{1,0:T(8,128)(2,1)S(1)} %get-tuple-element.90), channel_id=1, source_target_pairs={{0,9},{8,1},{9,0},{4,13},{5,12},{12,5},{13,4},{1,8},{2,11},{10,3},... | collective-permute-start | bytes 393224 | tf_op jit(solution)/shard_map/ppermute | solution.py:566
  64.6 0.6 collective-permute-start.7
  65.2 13.5 %value_grad.1 = (bf16[2,512,128]{2,1,0:T(8,128)(2,1)S(1)}, bf16[2,512,128]{2,1,0:T(8,128)(2,1)S(1)}, bf16[2,512,128]{2,1,0:T(8,128)(2,1)S(1)}, bf16[2,512,128]{2...) custom-call(s32[4]{0:T(128)S(1)} %pad_add_fusion.refs_0_, ...), custom_call_target="tpu_custom_call" | custom-call | flops 2147483648 | bytes 8163344 | tf_op jit(solution)/shard_map/value_grad/pallas_call | solution.py:544
  78.7 1.1 collective-permute-done.8.refs_5_
  79.7 3.2 %collective-permute-done.7.refs_4_ = bf16[512,128]{1,0:T(8,128)(2,1)S(1)} collective-permute-done((bf16[512,128]{1,0:T(8,128)(2,1)S(1)}, bf16[512,128]{1,0:T(8,128)(2,1)S(1)}, u32[]{:S(2)}, u32[]{:S(2)}) %collective-permute-start.7) | collective-permute-done | bytes 131104 | tf_op jit(solution)/shard_map/ppermute | solution.py:566
  82.9 1.5 collective-permute-start.15
  84.4 2.3 %collective-permute-start.16 = (bf16[2,512,128]{2,1,0:T(8,128)(2,1)S(1)}, bf16[2,512,128]{2,1,0:T(8,128)(2,1)S(1)}, u32[]{:S(2)}, u32[]{:S(2)}) collective-permute-start(bf16[2,512,128]{2,1,0:T(8,128)(2,1)S(1)} %get-tuple-element.104), channel_id=1, source_target_pairs={{0,12},{4,0},{8,4},{12,8},{1,13},{5,1},{9,5},{13,9},{2,14},{6,2},{... | collective-permute-start | bytes 786440 | tf_op jit(solution)/shard_map/ppermute | solution.py:572
  86.7 15.8 %query_grad.1 = (bf16[544,128]{1,0:T(8,128)(2,1)S(1)}, bf16[544,128]{1,0:T(8,128)(2,1)S(1)}, bf16[544,128]{1,0:T(8,128)(2,1)S(1)}, bf16[544,128]{1,0:T(8,128)(2,...) custom-call(s32[4]{0:T(128)S(1)} %pad_add_fusion.refs_0_, ...), custom_call_target="tpu_custom_call" | custom-call | flops 3221225472 | bytes 7147536 | tf_op jit(solution)/shard_map/query_grad/pallas_call | solution.py:544
  102.5 2.1 %collective-permute-start.17 = (bf16[544,128]{1,0:T(8,128)(2,1)S(1)}, bf16[544,128]{1,0:T(8,128)(2,1)S(1)}, u32[]{:S(2)}, u32[]{:S(2)}) collective-permute-start(bf16[544,128]{1,0:T(8,128)(2,1)S(1)} %get-tuple-element.109), channel_id=1, source_target_pairs={{0,8},{8,0},{9,1},{4,12},{5,13},{12,4},{13,5},{1,9},{2,10},{10,2},... | collective-permute-start | bytes 417800 | tf_op jit(solution)/shard_map/ppermute | solution.py:566
  104.6 14.0 %collective-permute-done.17.refs_5_.refs_4_ = bf16[544,128]{1,0:T(8,128)(2,1)S(1)} collective-permute-done((bf16[544,128]{1,0:T(8,128)(2,1)S(1)}, bf16[544,128]{1,0:T(8,128)(2,1)S(1)}, u32[]{:S(2)}, u32[]{:S(2)}) %collective-permute-start.17) | collective-permute-done | bytes 139296 | tf_op jit(solution)/shard_map/ppermute | solution.py:566
  118.6 0.9 collective-permute-done.18.refs_6_.refs_5_
  119.6 0.6 swap.1
  120.2 0.9 collective-permute-start.19
  121.2 3.7 %collective-permute-start.22 = (bf16[544,128]{1,0:T(8,128)(2,1)S(1)}, bf16[544,128]{1,0:T(8,128)(2,1)S(1)}, u32[]{:S(2)}, u32[]{:S(2)}) collective-permute-start(bf16[544,128]{1,0:T(8,128)(2,1)S(1)} %get-tuple-element.115), channel_id=1, source_target_pairs={{0,12},{8,4},{9,5},{4,0},{5,1},{12,8},{13,9},{1,13},{2,14},{10,6},... | collective-permute-start | bytes 417800 | tf_op jit(solution)/shard_map/ppermute | solution.py:566
  124.9 1.5 collective-permute-start.23
  126.6 2.5 %value_home.1 = (bf16[1024,512]{1,0:T(8,128)(2,1)S(1)}, f32[1024,512]{1,0:T(8,128)S(1)}, bf16[4,128,512]{2,1,0:T(8,128)(2,1)S(1)}, bf16[4,128,512]{2,1,0:T(8,128)(2,1)S(1)}) custom-call(s32[4]{0:T(128)S(1)} %pad_add_fusion.refs_0_, bf16[1024,1024]{1,0:T(8,128)(2,1)S(1)} %get-tuple-element.75.refs_1_, bf16[1024,512]{1,0:T(8,128)(2,1)S(1)} %copy-done.3, ...), custom_call_target="tpu_custom_call" | custom-call | flops 1610612736 | bytes 8912912 | tf_op jit(solution)/shard_map/value_home/pallas_call | solution.py:544
  129.6 1.6 collective-permute-done.21.refs_7_
  131.2 2.5 %collective-permute-done.22.refs_8_ = bf16[544,128]{1,0:T(8,128)(2,1)S(1)} collective-permute-done((bf16[544,128]{1,0:T(8,128)(2,1)S(1)}, bf16[544,128]{1,0:T(8,128)(2,1)S(1)}, u32[]{:S(2)}, u32[]{:S(2)}) %collective-permute-start.22) | collective-permute-done | bytes 139296 | tf_op jit(solution)/shard_map/ppermute | solution.py:566
  133.6 2.3 %collective-permute-done.23.refs_9_ = bf16[544,128]{1,0:T(8,128)(2,1)S(1)} collective-permute-done((bf16[544,128]{1,0:T(8,128)(2,1)S(1)}, bf16[544,128]{1,0:T(8,128)(2,1)S(1)}, u32[]{:S(2)}, u32[]{:S(2)}) %collective-permute-start.23) | collective-permute-done | bytes 139296 | tf_op jit(solution)/shard_map/ppermute | solution.py:566
  135.9 2.0 %query_home.1 = (bf16[1024,512]{1,0:T(8,128)(2,1)S(1)}, bf16[1024,512]{1,0:T(8,128)(2,1)S(1)}, f32[64,512]{1,0:T(8,128)}) custom-call(s32[4]{0:T(128)S(1)} %pad_add_fusion.refs_0_, bf16[1024,512]{1,0:T(8,128)(2,1)S(1)} %copy-done, f32[1024,512]{1,0:T(8,128)S(1)} %get-tuple-element.111.refs_2_, bf16[544,128]{1,0:T(8,128)(2,1)S(1)} %get-tuple-element.112.refs_3_, ...), custom_call_target="tpu_custom_call" | custom-call | flops 536870912 | bytes 6488080 | tf_op jit(solution)/shard_map/query_home/pallas_call | solution.py:544
  138.0 1.5 collective-permute-start.26
  139.5 1.8 %query_weight.1 = (bf16[4,128,512]{2,1,0:T(8,128)(2,1)S(1)}, bf16[4,128,512]{2,1,0:T(8,128)(2,1)S(1)}) custom-call(s32[4]{0:T(128)S(1)} %pad_add_fusion.refs_0_, bf16[1024,1024]{1,0:T(8,128)(2,1)S(1)} %copy-done.7, bf16[1024,512]{1,0:T(8,128)(2,1)S(1)} %get-tuple-element.118.refs_2_.refs_1_), custom_call_target="tpu_custom_call" | custom-call | flops 1073741824 | bytes 4194320 | tf_op jit(solution)/shard_map/query_weight/pallas_call | solution.py:544
  141.8 0.7 value_subs.1
  142.5 2.4 %collective-permute-start.31 = (bf16[128,512]{1,0:T(8,128)(2,1)S(1)}, bf16[128,512]{1,0:T(8,128)(2,1)S(1)}, u32[]{:S(2)}, u32[]{:S(2)}) collective-permute-start(bf16[128,512]{1,0:T(8,128)(2,1)S(1)} %get-tuple-element.136), channel_id=1, source_target_pairs={{0,4},{4,8},{8,12},{12,0},{1,5},{5,9},{9,13},{13,1},{2,6},{6,10},{... | collective-permute-start | bytes 393224 | tf_op jit(solution)/shard_map/ppermute | solution.py:572
  144.9 2.4 %collective-permute-start.33 = (bf16[128,512]{1,0:T(8,128)(2,1)S(1)}, bf16[128,512]{1,0:T(8,128)(2,1)S(1)}, u32[]{:S(2)}, u32[]{:S(2)}) collective-permute-start(bf16[128,512]{1,0:T(8,128)(2,1)S(1)} %get-tuple-element.138), channel_id=1, source_target_pairs={{0,12},{4,0},{8,4},{12,8},{1,13},{5,1},{9,5},{13,9},{2,14},{6,2},{... | collective-permute-start | bytes 393224 | tf_op jit(solution)/shard_map/ppermute | solution.py:572
  147.3 0.7 query_subs.1
  148.1 2.8 %collective-permute-done.31.refs_1_ = bf16[128,512]{1,0:T(8,128)(2,1)S(1)} collective-permute-done((bf16[128,512]{1,0:T(8,128)(2,1)S(1)}, bf16[128,512]{1,0:T(8,128)(2,1)S(1)}, u32[]{:S(2)}, u32[]{:S(2)}) %collective-permute-start.31) | collective-permute-done | bytes 131104 | tf_op jit(solution)/shard_map/ppermute | solution.py:572
  151.0 5.5 %collective-permute-done.32.refs_2_ = bf16[128,512]{1,0:T(8,128)(2,1)S(1)} collective-permute-done((bf16[128,512]{1,0:T(8,128)(2,1)S(1)}, bf16[128,512]{1,0:T(8,128)(2,1)S(1)}, u32[]{:S(2)}, u32[]{:S(2)}) %collective-permute-start.32) | collective-permute-done | bytes 131104 | tf_op jit(solution)/shard_map/ppermute | solution.py:572
  156.5 3.9 %collective-permute-start.29 = (bf16[128,512]{1,0:T(8,128)(2,1)S(1)}, bf16[128,512]{1,0:T(8,128)(2,1)S(1)}, u32[]{:S(2)}, u32[]{:S(2)}) collective-permute-start(bf16[128,512]{1,0:T(8,128)(2,1)S(1)} %get-tuple-element.128), channel_id=1, source_target_pairs={{0,12},{4,0},{8,4},{12,8},{1,13},{5,1},{9,5},{13,9},{2,14},{6,2},{... | collective-permute-start | bytes 393224 | tf_op jit(solution)/shard_map/ppermute | solution.py:572
  160.4 1.8 %input_own.1.refs_2_.refs_4_ = bf16[1024,512]{1,0:T(8,128)(2,1)S(1)} custom-call(s32[4]{0:T(128)S(1)} %pad_add_fusion.refs_0_, bf16[1024,512]{1,0:T(8,128)(2,1)S(1)} %get-tuple-element.118.refs_2_.refs_1_, bf16[1024,512]{1,0:T(8,128)(2,1)S(1)} %get-tuple-element.122.refs_2_, bf16[1024,512]{1,0:T(8,128)(2,1)S(1)} %copy-done, bf16[1024,512]{1,0:T(8,128)(2,1)S(1)} %copy-done.3, ...), custom_call_target="tpu_custom_call" | custom-call | flops 1073741824 | bytes 5242896 | tf_op jit(solution)/shard_map/input_own/pallas_call | solution.py:544
  162.2 0.8 value_sum.1
  163.2 2.3 %input_sum.1 = (bf16[1024,512]{1,0:T(8,128)(2,1)}, bf16[128,512]{1,0:T(8,128)(2,1)S(1)}) custom-call(bf16[1024,1024]{1,0:T(8,128)(2,1)S(1)} %get-tuple-element.74.refs_9_.refs_0_, bf16[128,512]{1,0:T(8,128)(2,1)S(1)} %get-tuple-element.121.refs_5_.refs_1_, bf16[1024,512]{1,0:T(8,128)(2,1)S(1)} %input_own.1.refs_2_.refs_4_, ...), custom_call_target="tpu_custom_call" | custom-call | flops 1073741824 | bytes 5505024 | tf_op jit(solution)/shard_map/input_sum/pallas_call | solution.py:544
  165.5 1.3 collective-permute-done.28.refs_2_
  166.8 0.8 query_sum.1
  (52 shorter events, 2.0 us)
Async XLA Ops:
  0.6 9.8 %copy-start = (bf16[1024,512]{1,0:T(8,128)(2,1)S(1)}, bf16[1024,512]{1,0:T(8,128)(2,1)}, u32[]{:S(2)}) copy-start(bf16[1024,512]{1,0:T(8,128)(2,1)} %refs_3_.7) | copy-start | bytes 3145732
  0.6 9.8 %copy-start.1 = (bf16[1024,1024]{1,0:T(8,128)(2,1)S(1)}, bf16[1024,1024]{1,0:T(8,128)(2,1)}, u32[]{:S(2)}) copy-start(bf16[1024,1024]{1,0:T(8,128)(2,1)} %refs_2_.4) | copy-start | bytes 6291460
  0.7 9.8 %copy-start.4 = (s32[1024,1]{0,1:T(1,128)S(1)}, s32[1024,1]{0,1:T(1,128)}, u32[]{:S(2)}) copy-start(s32[1024,1]{0,1:T(1,128)} %param.9) | copy-start | bytes 12292
  6.2 34.5 %collective-permute-start = (bf16[1040,128]{1,0:T(8,128)(2,1)}, bf16[1040,128]{1,0:T(8,128)(2,1)S(1)}, u32[]{:S(2)}, u32[]{:S(2)}) collective-permute-start(bf16[1040,128]{1,0:T(8,128)(2,1)} %get-tuple-element.77), channel_id=1, source_target_pairs={{0,8},{8,0},{9,1},{4,12},{5,13},{12,4},{13,5},{1,9},{2,10},{10,2},... | collective-permute-start | bytes 798728 | tf_op jit(solution)/shard_map/ppermute | solution.py:566
  10.3 34.5 %collective-permute-start.1 = (bf16[1040,128]{1,0:T(8,128)(2,1)}, bf16[1040,128]{1,0:T(8,128)(2,1)}, u32[]{:S(2)}, u32[]{:S(2)}) collective-permute-start(bf16[1040,128]{1,0:T(8,128)(2,1)} %get-tuple-element.78), channel_id=1, source_target_pairs={{0,9},{8,1},{9,0},{4,13},{5,12},{12,5},{13,4},{1,8},{2,11},{10,3},... | collective-permute-start | bytes 798728 | tf_op jit(solution)/shard_map/ppermute | solution.py:566
  10.4 1.2 copy-start.2
  11.7 0.7 copy-start.5
  12.3 33.9 %copy-start.3 = (bf16[1024,512]{1,0:T(8,128)(2,1)S(1)}, bf16[1024,512]{1,0:T(8,128)(2,1)}, u32[]{:S(2)}) copy-start(bf16[1024,512]{1,0:T(8,128)(2,1)} %refs_4_.3) | copy-start | bytes 3145732
  17.2 35.1 %collective-permute-start.3 = (bf16[1040,128]{1,0:T(8,128)(2,1)S(1)}, bf16[1040,128]{1,0:T(8,128)(2,1)S(1)}, u32[]{:S(2)}, u32[]{:S(2)}) collective-permute-start(bf16[1040,128]{1,0:T(8,128)(2,1)S(1)} %get-tuple-element.79), channel_id=1, source_target_pairs={{0,5},{8,13},{9,12},{4,9},{5,8},{12,1},{13,0},{1,4},{2,7},{10,15},... | collective-permute-start | bytes 798728 | tf_op jit(solution)/shard_map/ppermute | solution.py:566
  18.9 33.5 %collective-permute-start.2 = (bf16[1040,128]{1,0:T(8,128)(2,1)S(1)}, bf16[1040,128]{1,0:T(8,128)(2,1)S(1)}, u32[]{:S(2)}, u32[]{:S(2)}) collective-permute-start(bf16[1040,128]{1,0:T(8,128)(2,1)S(1)} %get-tuple-element.73.refs_4_), channel_id=1, source_target_pairs={{0,4},{8,12},{9,13},{4,8},{5,9},{12,0},{13,1},{1,5},{2,6},{10,14},... | collective-permute-start | bytes 798728 | tf_op jit(solution)/shard_map/ppermute | solution.py:566
  20.4 35.6 %collective-permute-start.4 = (bf16[1040,128]{1,0:T(8,128)(2,1)S(1)}, bf16[1040,128]{1,0:T(8,128)(2,1)S(1)}, u32[]{:S(2)}, u32[]{:S(2)}) collective-permute-start(bf16[1040,128]{1,0:T(8,128)(2,1)S(1)} %get-tuple-element.80), channel_id=1, source_target_pairs={{0,12},{8,4},{9,5},{4,0},{5,1},{12,8},{13,9},{1,13},{2,14},{10,6},... | collective-permute-start | bytes 798728 | tf_op jit(solution)/shard_map/ppermute | solution.py:566
  40.7 15.3 %collective-permute-start.5 = (bf16[1040,128]{1,0:T(8,128)(2,1)S(1)}, bf16[1040,128]{1,0:T(8,128)(2,1)S(1)}, u32[]{:S(2)}, u32[]{:S(2)}) collective-permute-start(bf16[1040,128]{1,0:T(8,128)(2,1)S(1)} %get-tuple-element.81), channel_id=1, source_target_pairs={{0,13},{8,5},{9,4},{4,1},{5,0},{12,9},{13,8},{1,12},{2,15},{10,7},... | collective-permute-start | bytes 798728 | tf_op jit(solution)/shard_map/ppermute | solution.py:566
  44.8 11.2 %collective-permute-start.6 = (bf16[1040,128]{1,0:T(8,128)(2,1)S(1)}, bf16[1040,128]{1,0:T(8,128)(2,1)S(1)}, u32[]{:S(2)}, u32[]{:S(2)}) collective-permute-start(bf16[1040,128]{1,0:T(8,128)(2,1)S(1)} %get-tuple-element.82), channel_id=1, source_target_pairs={{0,1},{8,9},{9,8},{4,5},{5,4},{12,13},{13,12},{1,0},{2,3},{10,11},... | collective-permute-start | bytes 798728 | tf_op jit(solution)/shard_map/ppermute | solution.py:566
  52.3 74.3 %copy-start.6 = (bf16[1024,1024]{1,0:T(8,128)(2,1)}, bf16[1024,1024]{1,0:T(8,128)(2,1)S(1)}, u32[]{:S(2)}) copy-start(bf16[1024,1024]{1,0:T(8,128)(2,1)S(1)} %get-tuple-element.75.refs_1_) | copy-start | bytes 6291460
  52.3 8.4 %collective-permute-start.13 = (bf16[512,128]{1,0:T(8,128)(2,1)S(1)}, bf16[512,128]{1,0:T(8,128)(2,1)S(1)}, u32[]{:S(2)}, u32[]{:S(2)}) collective-permute-start(bf16[512,128]{1,0:T(8,128)(2,1)S(1)} %get-tuple-element.100), channel_id=1, source_target_pairs={{0,1},{8,9},{9,8},{4,5},{5,4},{12,13},{13,12},{1,0},{2,3},{10,11},... | collective-permute-start | bytes 393224 | tf_op jit(solution)/shard_map/ppermute | solution.py:566
  52.4 12.1 %collective-permute-start.12 = (bf16[512,128]{1,0:T(8,128)(2,1)S(1)}, bf16[512,128]{1,0:T(8,128)(2,1)S(1)}, u32[]{:S(2)}, u32[]{:S(2)}) collective-permute-start(bf16[512,128]{1,0:T(8,128)(2,1)S(1)} %get-tuple-element.98), channel_id=1, source_target_pairs={{0,13},{8,5},{9,4},{4,1},{5,0},{12,9},{13,8},{1,12},{2,15},{10,7},... | collective-permute-start | bytes 393224 | tf_op jit(solution)/shard_map/ppermute | solution.py:566
  56.0 22.6 %collective-permute-start.11 = (bf16[512,128]{1,0:T(8,128)(2,1)S(1)}, bf16[512,128]{1,0:T(8,128)(2,1)S(1)}, u32[]{:S(2)}, u32[]{:S(2)}) collective-permute-start(bf16[512,128]{1,0:T(8,128)(2,1)S(1)} %get-tuple-element.96), channel_id=1, source_target_pairs={{0,12},{8,4},{9,5},{4,0},{5,1},{12,8},{13,9},{1,13},{2,14},{10,6},... | collective-permute-start | bytes 393224 | tf_op jit(solution)/shard_map/ppermute | solution.py:566
  60.7 17.9 %collective-permute-start.10 = (bf16[512,128]{1,0:T(8,128)(2,1)S(1)}, bf16[512,128]{1,0:T(8,128)(2,1)S(1)}, u32[]{:S(2)}, u32[]{:S(2)}) collective-permute-start(bf16[512,128]{1,0:T(8,128)(2,1)S(1)} %get-tuple-element.94), channel_id=1, source_target_pairs={{0,5},{8,13},{9,12},{4,9},{5,8},{12,1},{13,0},{1,4},{2,7},{10,15},... | collective-permute-start | bytes 393224 | tf_op jit(solution)/shard_map/ppermute | solution.py:566
  60.7 17.9 %collective-permute-start.9 = (bf16[512,128]{1,0:T(8,128)(2,1)S(1)}, bf16[512,128]{1,0:T(8,128)(2,1)S(1)}, u32[]{:S(2)}, u32[]{:S(2)}) collective-permute-start(bf16[512,128]{1,0:T(8,128)(2,1)S(1)} %get-tuple-element.92), channel_id=1, source_target_pairs={{0,4},{8,12},{9,13},{4,8},{5,9},{12,0},{13,1},{1,5},{2,6},{10,14},... | collective-permute-start | bytes 393224 | tf_op jit(solution)/shard_map/ppermute | solution.py:566
  60.7 19.0 %collective-permute-start.8 = (bf16[512,128]{1,0:T(8,128)(2,1)S(1)}, bf16[512,128]{1,0:T(8,128)(2,1)S(1)}, u32[]{:S(2)}, u32[]{:S(2)}) collective-permute-start(bf16[512,128]{1,0:T(8,128)(2,1)S(1)} %get-tuple-element.90), channel_id=1, source_target_pairs={{0,9},{8,1},{9,0},{4,13},{5,12},{12,5},{13,4},{1,8},{2,11},{10,3},... | collective-permute-start | bytes 393224 | tf_op jit(solution)/shard_map/ppermute | solution.py:566
  64.6 18.4 %collective-permute-start.7 = (bf16[512,128]{1,0:T(8,128)(2,1)S(1)}, bf16[512,128]{1,0:T(8,128)(2,1)S(1)}, u32[]{:S(2)}, u32[]{:S(2)}) collective-permute-start(bf16[512,128]{1,0:T(8,128)(2,1)S(1)} %get-tuple-element.88), channel_id=1, source_target_pairs={{0,8},{8,0},{9,1},{4,12},{5,13},{12,4},{13,5},{1,9},{2,10},{10,2},... | collective-permute-start | bytes 393224 | tf_op jit(solution)/shard_map/ppermute | solution.py:566
  82.9 36.7 %collective-permute-start.14 = (bf16[2,512,128]{2,1,0:T(8,128)(2,1)S(1)}, bf16[2,512,128]{2,1,0:T(8,128)(2,1)S(1)}, u32[]{:S(2)}, u32[]{:S(2)}) collective-permute-start(bf16[2,512,128]{2,1,0:T(8,128)(2,1)S(1)} %get-tuple-element.102), channel_id=1, source_target_pairs={{0,4},{4,8},{8,12},{12,0},{1,5},{5,9},{9,13},{13,1},{2,6},{6,10},{... | collective-permute-start | bytes 786440 | tf_op jit(solution)/shard_map/ppermute | solution.py:572
  82.9 36.7 %collective-permute-start.15 = (bf16[2,512,128]{2,1,0:T(8,128)(2,1)S(1)}, bf16[2,512,128]{2,1,0:T(8,128)(2,1)S(1)}, u32[]{:S(2)}, u32[]{:S(2)}) collective-permute-start(bf16[2,512,128]{2,1,0:T(8,128)(2,1)S(1)} %get-tuple-element.103), channel_id=1, source_target_pairs={{0,8},{4,12},{8,0},{12,4},{1,9},{5,13},{9,1},{13,5},{2,10},{6,14},... | collective-permute-start | bytes 786440 | tf_op jit(solution)/shard_map/ppermute | solution.py:572
  84.4 35.2 %collective-permute-start.16 = (bf16[2,512,128]{2,1,0:T(8,128)(2,1)S(1)}, bf16[2,512,128]{2,1,0:T(8,128)(2,1)S(1)}, u32[]{:S(2)}, u32[]{:S(2)}) collective-permute-start(bf16[2,512,128]{2,1,0:T(8,128)(2,1)S(1)} %get-tuple-element.104), channel_id=1, source_target_pairs={{0,12},{4,0},{8,4},{12,8},{1,13},{5,1},{9,5},{13,9},{2,14},{6,2},{... | collective-permute-start | bytes 786440 | tf_op jit(solution)/shard_map/ppermute | solution.py:572
  102.5 16.1 %collective-permute-start.17 = (bf16[544,128]{1,0:T(8,128)(2,1)S(1)}, bf16[544,128]{1,0:T(8,128)(2,1)S(1)}, u32[]{:S(2)}, u32[]{:S(2)}) collective-permute-start(bf16[544,128]{1,0:T(8,128)(2,1)S(1)} %get-tuple-element.109), channel_id=1, source_target_pairs={{0,8},{8,0},{9,1},{4,12},{5,13},{12,4},{13,5},{1,9},{2,10},{10,2},... | collective-permute-start | bytes 417800 | tf_op jit(solution)/shard_map/ppermute | solution.py:566
  104.6 15.0 %collective-permute-start.18 = (bf16[544,128]{1,0:T(8,128)(2,1)S(1)}, bf16[544,128]{1,0:T(8,128)(2,1)S(1)}, u32[]{:S(2)}, u32[]{:S(2)}) collective-permute-start(bf16[544,128]{1,0:T(8,128)(2,1)S(1)} %get-tuple-element.110), channel_id=1, source_target_pairs={{0,9},{8,1},{9,0},{4,13},{5,12},{12,5},{13,4},{1,8},{2,11},{10,3},... | collective-permute-start | bytes 417800 | tf_op jit(solution)/shard_map/ppermute | solution.py:566
  120.2 6.2 %collective-permute-start.19 = (bf16[4,512,128]{2,1,0:T(8,128)(2,1)S(1)}, bf16[4,512,128]{2,1,0:T(8,128)(2,1)S(1)}, u32[]{:S(2)}, u32[]{:S(2)}) collective-permute-start(bf16[4,512,128]{2,1,0:T(8,128)(2,1)S(1)} %swap.1), channel_id=1, source_target_pairs={{0,1},{1,0},{2,3},{3,2},{4,5},{5,4},{6,7},{7,6},{8,9},{9,8},{10,11... | collective-permute-start | bytes 1572872 | tf_op jit(solution)/shard_map/ppermute | solution.py:572
  121.1 8.5 %collective-permute-start.20 = (bf16[544,128]{1,0:T(8,128)(2,1)S(1)}, bf16[544,128]{1,0:T(8,128)(2,1)S(1)}, u32[]{:S(2)}, u32[]{:S(2)}) collective-permute-start(bf16[544,128]{1,0:T(8,128)(2,1)S(1)} %get-tuple-element.113), channel_id=1, source_target_pairs={{0,4},{8,12},{9,13},{4,8},{5,9},{12,0},{13,1},{1,5},{2,6},{10,14},... | collective-permute-start | bytes 417800 | tf_op jit(solution)/shard_map/ppermute | solution.py:566
  121.1 10.1 %collective-permute-start.21 = (bf16[544,128]{1,0:T(8,128)(2,1)S(1)}, bf16[544,128]{1,0:T(8,128)(2,1)S(1)}, u32[]{:S(2)}, u32[]{:S(2)}) collective-permute-start(bf16[544,128]{1,0:T(8,128)(2,1)S(1)} %get-tuple-element.114), channel_id=1, source_target_pairs={{0,5},{8,13},{9,12},{4,9},{5,8},{12,1},{13,0},{1,4},{2,7},{10,15},... | collective-permute-start | bytes 417800 | tf_op jit(solution)/shard_map/ppermute | solution.py:566
  121.2 12.4 %collective-permute-start.22 = (bf16[544,128]{1,0:T(8,128)(2,1)S(1)}, bf16[544,128]{1,0:T(8,128)(2,1)S(1)}, u32[]{:S(2)}, u32[]{:S(2)}) collective-permute-start(bf16[544,128]{1,0:T(8,128)(2,1)S(1)} %get-tuple-element.115), channel_id=1, source_target_pairs={{0,12},{8,4},{9,5},{4,0},{5,1},{12,8},{13,9},{1,13},{2,14},{10,6},... | collective-permute-start | bytes 417800 | tf_op jit(solution)/shard_map/ppermute | solution.py:566
  124.9 11.0 %collective-permute-start.23 = (bf16[544,128]{1,0:T(8,128)(2,1)S(1)}, bf16[544,128]{1,0:T(8,128)(2,1)S(1)}, u32[]{:S(2)}, u32[]{:S(2)}) collective-permute-start(bf16[544,128]{1,0:T(8,128)(2,1)S(1)} %get-tuple-element.116), channel_id=1, source_target_pairs={{0,13},{8,5},{9,4},{4,1},{5,0},{12,9},{13,8},{1,12},{2,15},{10,7},... | collective-permute-start | bytes 417800 | tf_op jit(solution)/shard_map/ppermute | solution.py:566
  126.4 9.5 %collective-permute-start.24 = (bf16[544,128]{1,0:T(8,128)(2,1)S(1)}, bf16[544,128]{1,0:T(8,128)(2,1)S(1)}, u32[]{:S(2)}, u32[]{:S(2)}) collective-permute-start(bf16[544,128]{1,0:T(8,128)(2,1)S(1)} %get-tuple-element.117), channel_id=1, source_target_pairs={{0,1},{8,9},{9,8},{4,5},{5,4},{12,13},{13,12},{1,0},{2,3},{10,11},... | collective-permute-start | bytes 417800 | tf_op jit(solution)/shard_map/ppermute | solution.py:566
  135.9 3.5 %copy-start.7 = (bf16[1024,1024]{1,0:T(8,128)(2,1)S(1)}, bf16[1024,1024]{1,0:T(8,128)(2,1)}, u32[]{:S(2)}) copy-start(bf16[1024,1024]{1,0:T(8,128)(2,1)} %copy-done.6) | copy-start | bytes 6291460
  138.0 25.2 %collective-permute-start.26 = (bf16[1024,512]{1,0:T(8,128)(2,1)S(1)}, bf16[1024,512]{1,0:T(8,128)(2,1)S(1)}, u32[]{:S(2)}, u32[]{:S(2)}) collective-permute-start(bf16[1024,512]{1,0:T(8,128)(2,1)S(1)} %get-tuple-element.123), channel_id=1, source_target_pairs={{0,2},{2,0},{1,3},{3,1},{4,6},{6,4},{5,7},{7,5},{8,10},{10,8},{9,1... | collective-permute-start | bytes 3145736 | tf_op jit(solution)/shard_map/ppermute | solution.py:572
  139.5 2.4 %collective-permute-start.30 = (bf16[4,128,512]{2,1,0:T(8,128)(2,1)S(1)}, bf16[4,128,512]{2,1,0:T(8,128)(2,1)S(1)}, u32[]{:S(2)}, u32[]{:S(2)}) collective-permute-start(bf16[4,128,512]{2,1,0:T(8,128)(2,1)S(1)} %get-tuple-element.130), channel_id=1, source_target_pairs={{0,1},{1,0},{2,3},{3,2},{4,5},{5,4},{6,7},{7,6},{8,9},{9,8},{10,11... | collective-permute-start | bytes 1572872 | tf_op jit(solution)/shard_map/ppermute | solution.py:572
  141.3 6.1 %collective-permute-start.25 = (bf16[4,128,512]{2,1,0:T(8,128)(2,1)S(1)}, bf16[4,128,512]{2,1,0:T(8,128)(2,1)S(1)}, u32[]{:S(2)}, u32[]{:S(2)}) collective-permute-start(bf16[4,128,512]{2,1,0:T(8,128)(2,1)S(1)} %get-tuple-element.120), channel_id=1, source_target_pairs={{0,1},{1,0},{2,3},{3,2},{4,5},{5,4},{6,7},{7,6},{8,9},{9,8},{10,11... | collective-permute-start | bytes 1572872 | tf_op jit(solution)/shard_map/ppermute | solution.py:572
  142.5 8.3 %collective-permute-start.31 = (bf16[128,512]{1,0:T(8,128)(2,1)S(1)}, bf16[128,512]{1,0:T(8,128)(2,1)S(1)}, u32[]{:S(2)}, u32[]{:S(2)}) collective-permute-start(bf16[128,512]{1,0:T(8,128)(2,1)S(1)} %get-tuple-element.136), channel_id=1, source_target_pairs={{0,4},{4,8},{8,12},{12,0},{1,5},{5,9},{9,13},{13,1},{2,6},{6,10},{... | collective-permute-start | bytes 393224 | tf_op jit(solution)/shard_map/ppermute | solution.py:572
  144.9 11.6 %collective-permute-start.32 = (bf16[128,512]{1,0:T(8,128)(2,1)S(1)}, bf16[128,512]{1,0:T(8,128)(2,1)S(1)}, u32[]{:S(2)}, u32[]{:S(2)}) collective-permute-start(bf16[128,512]{1,0:T(8,128)(2,1)S(1)} %get-tuple-element.137), channel_id=1, source_target_pairs={{0,8},{4,12},{8,0},{12,4},{1,9},{5,13},{9,1},{13,5},{2,10},{6,14},... | collective-permute-start | bytes 393224 | tf_op jit(solution)/shard_map/ppermute | solution.py:572
  144.9 17.3 %collective-permute-start.33 = (bf16[128,512]{1,0:T(8,128)(2,1)S(1)}, bf16[128,512]{1,0:T(8,128)(2,1)S(1)}, u32[]{:S(2)}, u32[]{:S(2)}) collective-permute-start(bf16[128,512]{1,0:T(8,128)(2,1)S(1)} %get-tuple-element.138), channel_id=1, source_target_pairs={{0,12},{4,0},{8,4},{12,8},{1,13},{5,1},{9,5},{13,9},{2,14},{6,2},{... | collective-permute-start | bytes 393224 | tf_op jit(solution)/shard_map/ppermute | solution.py:572
  148.0 17.5 %collective-permute-start.27 = (bf16[128,512]{1,0:T(8,128)(2,1)S(1)}, bf16[128,512]{1,0:T(8,128)(2,1)S(1)}, u32[]{:S(2)}, u32[]{:S(2)}) collective-permute-start(bf16[128,512]{1,0:T(8,128)(2,1)S(1)} %get-tuple-element.126), channel_id=1, source_target_pairs={{0,4},{4,8},{8,12},{12,0},{1,5},{5,9},{9,13},{13,1},{2,6},{6,10},{... | collective-permute-start | bytes 393224 | tf_op jit(solution)/shard_map/ppermute | solution.py:572
  150.9 15.9 %collective-permute-start.28 = (bf16[128,512]{1,0:T(8,128)(2,1)S(1)}, bf16[128,512]{1,0:T(8,128)(2,1)S(1)}, u32[]{:S(2)}, u32[]{:S(2)}) collective-permute-start(bf16[128,512]{1,0:T(8,128)(2,1)S(1)} %get-tuple-element.127), channel_id=1, source_target_pairs={{0,8},{4,12},{8,0},{12,4},{1,9},{5,13},{9,1},{13,5},{2,10},{6,14},... | collective-permute-start | bytes 393224 | tf_op jit(solution)/shard_map/ppermute | solution.py:572
  156.5 10.3 %collective-permute-start.29 = (bf16[128,512]{1,0:T(8,128)(2,1)S(1)}, bf16[128,512]{1,0:T(8,128)(2,1)S(1)}, u32[]{:S(2)}, u32[]{:S(2)}) collective-permute-start(bf16[128,512]{1,0:T(8,128)(2,1)S(1)} %get-tuple-element.128), channel_id=1, source_target_pairs={{0,12},{4,0},{8,4},{12,8},{1,13},{5,1},{9,5},{13,9},{2,14},{6,2},{... | collective-permute-start | bytes 393224 | tf_op jit(solution)/shard_map/ppermute | solution.py:572

commit v18 on v17

--- a/solution.py
+++ b/solution.py
@@ -359,7 +359,8 @@
 
 def query_grad_kernel(sizes, per_group, slot_rows, me_ref, counts_ref, dense_ref, *refs):
     owners = sizes[0] * sizes[1]
-    value_refs, out_refs, rest = refs[:owners], refs[owners : 2 * owners], refs[2 * owners :]
+    mid = owners + sizes[0]
+    value_refs, out_refs, rest = refs[:owners], refs[owners:mid], refs[mid:]
     place_ref, wide_ref, block_ref, sums_ref, centroid_ref = rest[:5]
     score_refs, grad_probs_refs, both_refs = rest[5:7], rest[7:9], rest[9:11]
     half = value_refs[0].shape[0]
@@ -412,15 +413,16 @@
             wide_ref[source, pl.ds(start, slot_rows), :] = block_ref[pl.ds(row, slot_rows), :]
 
     for_each_cluster(counts_ref, me_ref, place_ref, owners, per_group, scatter)
-    extra = out_refs[0].shape[0] - half
+    extra = out_refs[0].shape[1] - half
     centroid = jnp.where(
         low_half((extra, LANES)), centroid_ref[:extra, :], swap_halves(centroid_ref[extra:, :])
     ).astype(BF16)
-    for ahead, out_ref in zip(steps_of(sizes), out_refs):
-        source = owner_of(me_ref, ahead, sizes)
-        up, down = wide_ref[source, :half, :], wide_ref[source, half:rows, :]
-        out_ref[:half, :] = jnp.where(low_half((half, LANES)), up, swap_halves(down)).astype(BF16)
-        out_ref[half:, :] = centroid
+    for ahead, out_ref in enumerate(out_refs):
+        for sub in range(sizes[1]):
+            source = owner_of(me_ref, (ahead, 0), sizes) - me_ref[1] + sub
+            up, down = wide_ref[source, :half, :], wide_ref[source, half:rows, :]
+            out_ref[sub, :half, :] = jnp.where(low_half((half, LANES)), up, swap_halves(down)).astype(BF16)
+            out_ref[sub, half:, :] = centroid
 
 
 def unfold(home_ref, out_ref, heads, start, half, finish):
@@ -478,12 +480,10 @@
 
 def query_home_kernel(sizes, heads, factor, parts, me_ref, weight_ref, *refs):
     term_refs, refs = refs[: parts - 1], refs[parts - 1 :]
-    part_refs, refs = refs[: sizes[0] * sizes[1]], refs[sizes[0] * sizes[1] :]
+    came = sizes[0] + sizes[1] - 1
+    part_refs, refs = refs[:came], refs[came:]
     out_refs, (rows_ref, centroid_ref, home_ref) = refs[: parts - 1], refs[parts - 1 :]
-    pieces = [
-        (source_of(me_ref, ahead, sizes), part_ref[...]) for ahead, part_ref in zip(steps_of(sizes), part_refs)
-    ]
-    bring_home(sizes, heads, pieces, home_ref, rows_ref)
+    bring_home(sizes, heads, arrivals(sizes, me_ref, part_refs), home_ref, rows_ref)
     for k, (term_ref, out_ref) in enumerate(zip(term_refs, out_refs)):
         mine = input_columns(me_ref, k + 1, parts, weight_ref.shape[0])
         out_ref[...] = (dot_nt(rows_ref[...], weight_ref[mine, :]) + term_ref[...]).astype(BF16)
@@ -693,7 +693,7 @@
     back_value, _ = lax.optimization_barrier((back_value, got_value[1:]))
     back_query = call(
         functools.partial(query_grad_kernel, sizes, per_group, slot_rows),
-        several(owners, half + extra, LANES),
+        several(sizes[0], sizes[1], half + extra, LANES),
         (me, counts, dense, *got_value),
         smem=(0, 1),
         scratch=[place, tall, dense_rows, pltpu.VMEM((held, LANES), F32), pltpu.VMEM((2 * extra, LANES), F32)]
@@ -703,8 +703,8 @@
         vmem=48,
         name="query_grad",
     )
-    home_query = exchange(back_query, sizes)
-    home_value = exchange_by_chip(me, back_value, sizes, "swap", home_query[1:3])
+    home_query = exchange_by_chip(me, back_query, sizes, "swap_query")
+    home_value = exchange_by_chip(me, back_value, sizes, "swap_value", back_query[:1])
     weight_flops = 2 * slots * width * width_dev
     home_flops = weight_flops // parts * (parts - 1)
     piece = width // owners

time: 168 us -> 165 us (0.982)
  waiting for transfers between devices: 57.9 us -> 50.6 us
  starting transfers between devices: 47.2 us -> 50.3 us
    ppermute x21 -> x14, waiting for transfers between devices: 48.1 us -> 26.4 us  [exchange(): out.append(part if ahead == (0, 0) else lax.ppermute(part, OWNERS, moves))]
    ppermute x13 -> x17, waiting for transfers between devices: 9.77 us -> 24.2 us  [shift(): lax.ppermute(part, axis, [(i, (i + ahead) % size) for i in range(size)])]
    ppermute x13 -> x17, starting transfers between devices: 15.7 us -> 26.4 us  [shift(): lax.ppermute(part, axis, [(i, (i + ahead) % size) for i in range(size)])]
    ppermute x21 -> x14, starting transfers between devices: 31.5 us -> 23.9 us  [exchange(): out.append(part if ahead == (0, 0) else lax.ppermute(part, OWNERS, moves))]
    pallas_call x15 -> x16, Pallas kernels: 59.6 us -> 60.1 us  [call(): pl.pallas_call(body, out_shape=outs, in_specs=specs, out_specs=jax.tree.m...]
  transfers between devices with their start and end apart: 34 -> 31, of which waited for: 14 -> 9; matrix products, arithmetic and copies ran while one was open for 0% -> 0% of each run, Pallas kernels for 30% -> 32%
where the time goes in v18:
time: 165 us; the launch traced here: 164 us
  Pallas kernels  60.1 us (36%)
  waiting for transfers between devices  50.6 us (31%)
  starting transfers between devices  50.3 us (30%)
  local copies, waits for them, and re-layouts  1.92 us (1%)
    pallas_call x16, Pallas kernels, call(): pl.pallas_call(body, out_shape=outs, in_specs=specs, out_specs=jax.tree.m...  60.1 us
    ppermute x14, waiting for transfers between devices, exchange(): out.append(part if ahead == (0, 0) else lax.ppermute(part, OWNERS, moves))  26.4 us
    ppermute x17, starting transfers between devices, shift(): lax.ppermute(part, axis, [(i, (i + ahead) % size) for i in range(size)])  26.4 us
    ppermute x17, waiting for transfers between devices, shift(): lax.ppermute(part, axis, [(i, (i + ahead) % size) for i in range(size)])  24.2 us
    ppermute x14, starting transfers between devices, exchange(): out.append(part if ahead == (0, 0) else lax.ppermute(part, OWNERS, moves))  23.9 us
  transfers between devices with their start and end apart: 31, of which 9 were waited for; matrix products, arithmetic and copies ran while one was open for 0% of the time, Pallas kernels for 32%

profile of v18, /device:TPU:0, one launch (start us, length us, event | category | flops | bytes accessed | tf_op | source)
XLA Modules:
  0.0 163.9 jit_solution(12261081129139211035)
XLA Ops:
  0.7 5.6 %project_far.1 = (bf16[1040,128]{1,0:T(8,128)(2,1)}, bf16[1040,128]{1,0:T(8,128)(2,1)}, s32[1,1024]{1,0:T(1,128)}) custom-call(s32[1,1024]{1,0:T(1,128)} %bitcast.5, bf16[1024,1024]{1,0:T(8,128)(2,1)} %refs_2_.4, bf16[1024,512]{1,0:T(8,128)(2,1)} %refs_3_.7, bf16[1024,512]{1,0:T(8,128)(2,1)} %refs_5_.1), custom_call_target="tpu_custom_call" | custom-call | flops 805306368 | bytes 4734976 | tf_op jit(solution)/shard_map/project_far/pallas_call | solution.py:544
  6.2 4.1 %collective-permute-start = (bf16[1040,128]{1,0:T(8,128)(2,1)}, bf16[1040,128]{1,0:T(8,128)(2,1)S(1)}, u32[]{:S(2)}, u32[]{:S(2)}) collective-permute-start(bf16[1040,128]{1,0:T(8,128)(2,1)} %get-tuple-element.73), channel_id=1, source_target_pairs={{0,8},{8,0},{9,1},{4,12},{5,13},{12,4},{13,5},{1,9},{2,10},{10,2},... | collective-permute-start | bytes 798728 | tf_op jit(solution)/shard_map/ppermute | solution.py:566
  10.4 1.2 copy-done.2
  11.7 0.7 copy-done.5
  12.4 4.8 %project_query.1 = (bf16[1040,128]{1,0:T(8,128)(2,1)S(1)}, bf16[1040,128]{1,0:T(8,128)(2,1)S(1)}, bf16[1040,128]{1,0:T(8,128)(2,1)S(1)}, bf16[1040,128]{1,0:T(8,...) custom-call(s32[4]{0:T(128)S(1)} %pad_add_fusion.refs_0_, s32[1,1024]{1,0:T(1,128)S(1)} %copy-done.5, ...), custom_call_target="tpu_custom_call" | custom-call | flops 3221225472 | bytes 5799952 | tf_op jit(solution)/shard_map/project_query/pallas_call | solution.py:544
  17.2 1.7 %collective-permute-start.3 = (bf16[1040,128]{1,0:T(8,128)(2,1)S(1)}, bf16[1040,128]{1,0:T(8,128)(2,1)S(1)}, u32[]{:S(2)}, u32[]{:S(2)}) collective-permute-start(bf16[1040,128]{1,0:T(8,128)(2,1)S(1)} %get-tuple-element.75), channel_id=1, source_target_pairs={{0,5},{8,13},{9,12},{4,9},{5,8},{12,1},{13,0},{1,4},{2,7},{10,15},... | collective-permute-start | bytes 798728 | tf_op jit(solution)/shard_map/ppermute | solution.py:566
  18.9 1.6 collective-permute-start.2
  20.4 2.2 %collective-permute-start.4 = (bf16[1040,128]{1,0:T(8,128)(2,1)S(1)}, bf16[1040,128]{1,0:T(8,128)(2,1)S(1)}, u32[]{:S(2)}, u32[]{:S(2)}) collective-permute-start(bf16[1040,128]{1,0:T(8,128)(2,1)S(1)} %get-tuple-element.76), channel_id=1, source_target_pairs={{0,12},{8,4},{9,5},{4,0},{5,1},{12,8},{13,9},{1,13},{2,14},{10,6},... | collective-permute-start | bytes 798728 | tf_op jit(solution)/shard_map/ppermute | solution.py:566
  22.7 18.0 %collective-permute-done.refs_2_ = bf16[1040,128]{1,0:T(8,128)(2,1)S(1)} collective-permute-done((bf16[1040,128]{1,0:T(8,128)(2,1)}, bf16[1040,128]{1,0:T(8,128)(2,1)S(1)}, u32[]{:S(2)}, u32[]{:S(2)}) %collective-permute-start) | collective-permute-done | bytes 266272 | tf_op jit(solution)/shard_map/ppermute | solution.py:566
  40.7 4.1 %collective-permute-done.1.refs_3_ = bf16[1040,128]{1,0:T(8,128)(2,1)} collective-permute-done((bf16[1040,128]{1,0:T(8,128)(2,1)}, bf16[1040,128]{1,0:T(8,128)(2,1)}, u32[]{:S(2)}, u32[]{:S(2)}) %collective-permute-start.1) | collective-permute-done | bytes 266272 | tf_op jit(solution)/shard_map/ppermute | solution.py:566
  44.8 1.4 collective-permute-start.6
  46.3 6.0 %project_value.1 = (bf16[512,128]{1,0:T(8,128)(2,1)S(1)}, bf16[512,128]{1,0:T(8,128)(2,1)S(1)}, bf16[512,128]{1,0:T(8,128)(2,1)S(1)}, bf16[512,128]{1,0:T(8,128)...) custom-call(s32[4]{0:T(128)S(1)} %pad_add_fusion.refs_0_, ...), custom_call_target="tpu_custom_call" | custom-call | flops 2147483648 | bytes 8392720 | tf_op jit(solution)/shard_map/project_value/pallas_call | solution.py:544
  52.4 3.6 %collective-permute-start.12 = (bf16[512,128]{1,0:T(8,128)(2,1)S(1)}, bf16[512,128]{1,0:T(8,128)(2,1)S(1)}, u32[]{:S(2)}, u32[]{:S(2)}) collective-permute-start(bf16[512,128]{1,0:T(8,128)(2,1)S(1)} %get-tuple-element.94), channel_id=1, source_target_pairs={{0,13},{8,5},{9,4},{4,1},{5,0},{12,9},{13,8},{1,12},{2,15},{10,7},... | collective-permute-start | bytes 393224 | tf_op jit(solution)/shard_map/ppermute | solution.py:566
  56.0 4.7 %collective-permute-start.11 = (bf16[512,128]{1,0:T(8,128)(2,1)S(1)}, bf16[512,128]{1,0:T(8,128)(2,1)S(1)}, u32[]{:S(2)}, u32[]{:S(2)}) collective-permute-start(bf16[512,128]{1,0:T(8,128)(2,1)S(1)} %get-tuple-element.92), channel_id=1, source_target_pairs={{0,12},{8,4},{9,5},{4,0},{5,1},{12,8},{13,9},{1,13},{2,14},{10,6},... | collective-permute-start | bytes 393224 | tf_op jit(solution)/shard_map/ppermute | solution.py:566
  60.7 3.8 %collective-permute-start.8 = (bf16[512,128]{1,0:T(8,128)(2,1)S(1)}, bf16[512,128]{1,0:T(8,128)(2,1)S(1)}, u32[]{:S(2)}, u32[]{:S(2)}) collective-permute-start(bf16[512,128]{1,0:T(8,128)(2,1)S(1)} %get-tuple-element.86), channel_id=1, source_target_pairs={{0,9},{8,1},{9,0},{4,13},{5,12},{12,5},{13,4},{1,8},{2,11},{10,3},... | collective-permute-start | bytes 393224 | tf_op jit(solution)/shard_map/ppermute | solution.py:566
  64.6 0.6 collective-permute-start.7
  65.2 13.5 %value_grad.1 = (bf16[2,512,128]{2,1,0:T(8,128)(2,1)S(1)}, bf16[2,512,128]{2,1,0:T(8,128)(2,1)S(1)}, bf16[2,512,128]{2,1,0:T(8,128)(2,1)S(1)}, bf16[2,512,128]{2...) custom-call(s32[4]{0:T(128)S(1)} %pad_add_fusion.refs_0_, ...), custom_call_target="tpu_custom_call" | custom-call | flops 2147483648 | bytes 8163344 | tf_op jit(solution)/shard_map/value_grad/pallas_call | solution.py:544
  78.7 1.1 collective-permute-done.8.refs_5_
  79.7 3.2 %collective-permute-done.7.refs_4_ = bf16[512,128]{1,0:T(8,128)(2,1)S(1)} collective-permute-done((bf16[512,128]{1,0:T(8,128)(2,1)S(1)}, bf16[512,128]{1,0:T(8,128)(2,1)S(1)}, u32[]{:S(2)}, u32[]{:S(2)}) %collective-permute-start.7) | collective-permute-done | bytes 131104 | tf_op jit(solution)/shard_map/ppermute | solution.py:566
  82.9 1.5 collective-permute-start.15
  84.4 2.3 %collective-permute-start.16 = (bf16[2,512,128]{2,1,0:T(8,128)(2,1)S(1)}, bf16[2,512,128]{2,1,0:T(8,128)(2,1)S(1)}, u32[]{:S(2)}, u32[]{:S(2)}) collective-permute-start(bf16[2,512,128]{2,1,0:T(8,128)(2,1)S(1)} %get-tuple-element.100), channel_id=1, source_target_pairs={{0,12},{4,0},{8,4},{12,8},{1,13},{5,1},{9,5},{13,9},{2,14},{6,2},{... | collective-permute-start | bytes 786440 | tf_op jit(solution)/shard_map/ppermute | solution.py:572
  86.7 15.8 %query_grad.1 = (bf16[2,544,128]{2,1,0:T(8,128)(2,1)S(1)}, bf16[2,544,128]{2,1,0:T(8,128)(2,1)S(1)}, bf16[2,544,128]{2,1,0:T(8,128)(2,1)S(1)}, bf16[2,544,128]{2,1,0:T(8,128)(2,1)S(1)}) custom-call(s32[4]{0:T(128)S(1)} %pad_add_fusion.refs_0_, s32[8,128]{1,0:T(8,128)S(1)} %get-tuple-element.101.refs_1_, bf16[19456,128]{1,0:T(8,128)(2,1)} %get-tuple-element.102.refs_2_, ...), custom_call_target="tpu_custom_call" | custom-call | flops 3221225472 | bytes 7147536 | tf_op jit(solution)/shard_map/query_grad/pallas_call | solution.py:544
  102.5 0.6 collective-permute-start.18
  103.1 1.5 collective-permute-start.19
  104.7 2.8 %collective-permute-start.20 = (bf16[2,544,128]{2,1,0:T(8,128)(2,1)S(1)}, bf16[2,544,128]{2,1,0:T(8,128)(2,1)S(1)}, u32[]{:S(2)}, u32[]{:S(2)}) collective-permute-start(bf16[2,544,128]{2,1,0:T(8,128)(2,1)S(1)} %get-tuple-element.109), channel_id=1, source_target_pairs={{0,12},{4,0},{8,4},{12,8},{1,13},{5,1},{9,5},{13,9},{2,14},{6,2},{... | collective-permute-start | bytes 835592 | tf_op jit(solution)/shard_map/ppermute | solution.py:572
  107.5 0.6 swap_value.1
  108.2 5.9 %collective-permute-done.18.refs_2_.refs_4_ = bf16[2,544,128]{2,1,0:T(8,128)(2,1)S(1)} collective-permute-done((bf16[2,544,128]{2,1,0:T(8,128)(2,1)S(1)}, bf16[2,544,128]{2,1,0:T(8,128)(2,1)S(1)}, u32[]{:S(2)}, u32[]{:S(2)}) %collective-permute-start.18) | collective-permute-done | bytes 278560 | tf_op jit(solution)/shard_map/ppermute | solution.py:572
  114.1 13.5 %collective-permute-done.19.refs_3_.refs_5_ = bf16[2,544,128]{2,1,0:T(8,128)(2,1)S(1)} collective-permute-done((bf16[2,544,128]{2,1,0:T(8,128)(2,1)S(1)}, bf16[2,544,128]{2,1,0:T(8,128)(2,1)S(1)}, u32[]{:S(2)}, u32[]{:S(2)}) %collective-permute-start.19) | collective-permute-done | bytes 278560 | tf_op jit(solution)/shard_map/ppermute | solution.py:572
  127.6 0.6 swap_query.1
  128.3 2.5 %value_home.1 = (bf16[1024,512]{1,0:T(8,128)(2,1)S(1)}, f32[1024,512]{1,0:T(8,128)S(1)}, bf16[4,128,512]{2,1,0:T(8,128)(2,1)S(1)}, bf16[4,128,512]{2,1,0:T(8,128)(2,1)S(1)}) custom-call(s32[4]{0:T(128)S(1)} %pad_add_fusion.refs_0_, bf16[1024,1024]{1,0:T(8,128)(2,1)S(1)} %get-tuple-element.71.refs_1_, bf16[1024,512]{1,0:T(8,128)(2,1)S(1)} %copy-done.3, ...), custom_call_target="tpu_custom_call" | custom-call | flops 1610612736 | bytes 8912912 | tf_op jit(solution)/shard_map/value_home/pallas_call | solution.py:544
  130.8 2.0 %query_home.1 = (bf16[1024,512]{1,0:T(8,128)(2,1)S(1)}, bf16[1024,512]{1,0:T(8,128)(2,1)S(1)}, f32[64,512]{1,0:T(8,128)}) custom-call(s32[4]{0:T(128)S(1)} %pad_add_fusion.refs_0_, bf16[1024,512]{1,0:T(8,128)(2,1)S(1)} %copy-done, f32[1024,512]{1,0:T(8,128)S(1)} %get-tuple-element.106.refs_2_, ...), custom_call_target="tpu_custom_call" | custom-call | flops 536870912 | bytes 7045136 | tf_op jit(solution)/shard_map/query_home/pallas_call | solution.py:544
  132.8 1.5 collective-permute-start.23
  134.3 0.2 collective-permute-start.27
  134.5 1.8 %query_weight.1 = (bf16[4,128,512]{2,1,0:T(8,128)(2,1)S(1)}, bf16[4,128,512]{2,1,0:T(8,128)(2,1)S(1)}) custom-call(s32[4]{0:T(128)S(1)} %pad_add_fusion.refs_0_, bf16[1024,1024]{1,0:T(8,128)(2,1)S(1)} %get-tuple-element.71.refs_1_, bf16[1024,512]{1,0:T(8,128)(2,1)S(1)} %get-tuple-element.110.refs_2_.refs_1_), custom_call_target="tpu_custom_call" | custom-call | flops 1073741824 | bytes 4194320 | tf_op jit(solution)/shard_map/query_weight/pallas_call | solution.py:544
  136.3 0.4 collective-permute-start.22
  136.7 0.7 value_subs.1
  137.4 5.6 %collective-permute-start.28 = (bf16[128,512]{1,0:T(8,128)(2,1)S(1)}, bf16[128,512]{1,0:T(8,128)(2,1)S(1)}, u32[]{:S(2)}, u32[]{:S(2)}) collective-permute-start(bf16[128,512]{1,0:T(8,128)(2,1)S(1)} %get-tuple-element.128), channel_id=1, source_target_pairs={{0,4},{4,8},{8,12},{12,0},{1,5},{5,9},{9,13},{13,1},{2,6},{6,10},{... | collective-permute-start | bytes 393224 | tf_op jit(solution)/shard_map/ppermute | solution.py:572
  143.0 2.4 %collective-permute-start.30 = (bf16[128,512]{1,0:T(8,128)(2,1)S(1)}, bf16[128,512]{1,0:T(8,128)(2,1)S(1)}, u32[]{:S(2)}, u32[]{:S(2)}) collective-permute-start(bf16[128,512]{1,0:T(8,128)(2,1)S(1)} %get-tuple-element.130), channel_id=1, source_target_pairs={{0,12},{4,0},{8,4},{12,8},{1,13},{5,1},{9,5},{13,9},{2,14},{6,2},{... | collective-permute-start | bytes 393224 | tf_op jit(solution)/shard_map/ppermute | solution.py:572
  145.4 0.7 query_subs.1
  146.1 0.7 collective-permute-done.28.refs_1_
  146.8 1.9 %collective-permute-start.25 = (bf16[128,512]{1,0:T(8,128)(2,1)S(1)}, bf16[128,512]{1,0:T(8,128)(2,1)S(1)}, u32[]{:S(2)}, u32[]{:S(2)}) collective-permute-start(bf16[128,512]{1,0:T(8,128)(2,1)S(1)} %get-tuple-element.119), channel_id=1, source_target_pairs={{0,8},{4,12},{8,0},{12,4},{1,9},{5,13},{9,1},{13,5},{2,10},{6,14},... | collective-permute-start | bytes 393224 | tf_op jit(solution)/shard_map/ppermute | solution.py:572
  148.7 3.9 %collective-permute-done.29.refs_2_ = bf16[128,512]{1,0:T(8,128)(2,1)S(1)} collective-permute-done((bf16[128,512]{1,0:T(8,128)(2,1)S(1)}, bf16[128,512]{1,0:T(8,128)(2,1)S(1)}, u32[]{:S(2)}, u32[]{:S(2)}) %collective-permute-start.29) | collective-permute-done | bytes 131104 | tf_op jit(solution)/shard_map/ppermute | solution.py:572
  152.6 5.4 %collective-permute-start.26 = (bf16[128,512]{1,0:T(8,128)(2,1)S(1)}, bf16[128,512]{1,0:T(8,128)(2,1)S(1)}, u32[]{:S(2)}, u32[]{:S(2)}) collective-permute-start(bf16[128,512]{1,0:T(8,128)(2,1)S(1)} %get-tuple-element.120), channel_id=1, source_target_pairs={{0,12},{4,0},{8,4},{12,8},{1,13},{5,1},{9,5},{13,9},{2,14},{6,2},{... | collective-permute-start | bytes 393224 | tf_op jit(solution)/shard_map/ppermute | solution.py:572
  158.1 1.8 %input_own.1.refs_2_.refs_4_ = bf16[1024,512]{1,0:T(8,128)(2,1)S(1)} custom-call(s32[4]{0:T(128)S(1)} %pad_add_fusion.refs_0_, bf16[1024,512]{1,0:T(8,128)(2,1)S(1)} %get-tuple-element.110.refs_2_.refs_1_, bf16[1024,512]{1,0:T(8,128)(2,1)S(1)} %get-tuple-element.114.refs_2_, bf16[1024,512]{1,0:T(8,128)(2,1)S(1)} %copy-done, bf16[1024,512]{1,0:T(8,128)(2,1)S(1)} %copy-done.3, ...), custom_call_target="tpu_custom_call" | custom-call | flops 1073741824 | bytes 5242896 | tf_op jit(solution)/shard_map/input_own/pallas_call | solution.py:544
  159.9 0.8 value_sum.1
  160.7 2.3 %input_sum.1 = (bf16[1024,512]{1,0:T(8,128)(2,1)}, bf16[128,512]{1,0:T(8,128)(2,1)S(1)}) custom-call(bf16[1024,1024]{1,0:T(8,128)(2,1)S(1)} %get-tuple-element.70.refs_9_.refs_0_, bf16[128,512]{1,0:T(8,128)(2,1)S(1)} %get-tuple-element.113.refs_5_.refs_1_, bf16[1024,512]{1,0:T(8,128)(2,1)S(1)} %input_own.1.refs_2_.refs_4_, ...), custom_call_target="tpu_custom_call" | custom-call | flops 1073741824 | bytes 5505024 | tf_op jit(solution)/shard_map/input_sum/pallas_call | solution.py:544
  162.9 0.2 collective-permute-done.25.refs_2_
  163.1 0.8 query_sum.1
  (43 shorter events, 0.4 us)
Async XLA Ops:
  0.6 9.8 %copy-start = (bf16[1024,512]{1,0:T(8,128)(2,1)S(1)}, bf16[1024,512]{1,0:T(8,128)(2,1)}, u32[]{:S(2)}) copy-start(bf16[1024,512]{1,0:T(8,128)(2,1)} %refs_3_.7) | copy-start | bytes 3145732
  0.6 9.8 %copy-start.1 = (bf16[1024,1024]{1,0:T(8,128)(2,1)S(1)}, bf16[1024,1024]{1,0:T(8,128)(2,1)}, u32[]{:S(2)}) copy-start(bf16[1024,1024]{1,0:T(8,128)(2,1)} %refs_2_.4) | copy-start | bytes 6291460
  0.7 9.8 %copy-start.4 = (s32[1024,1]{0,1:T(1,128)S(1)}, s32[1024,1]{0,1:T(1,128)}, u32[]{:S(2)}) copy-start(s32[1024,1]{0,1:T(1,128)} %param.9) | copy-start | bytes 12292
  6.2 34.5 %collective-permute-start = (bf16[1040,128]{1,0:T(8,128)(2,1)}, bf16[1040,128]{1,0:T(8,128)(2,1)S(1)}, u32[]{:S(2)}, u32[]{:S(2)}) collective-permute-start(bf16[1040,128]{1,0:T(8,128)(2,1)} %get-tuple-element.73), channel_id=1, source_target_pairs={{0,8},{8,0},{9,1},{4,12},{5,13},{12,4},{13,5},{1,9},{2,10},{10,2},... | collective-permute-start | bytes 798728 | tf_op jit(solution)/shard_map/ppermute | solution.py:566
  10.3 34.5 %collective-permute-start.1 = (bf16[1040,128]{1,0:T(8,128)(2,1)}, bf16[1040,128]{1,0:T(8,128)(2,1)}, u32[]{:S(2)}, u32[]{:S(2)}) collective-permute-start(bf16[1040,128]{1,0:T(8,128)(2,1)} %get-tuple-element.74), channel_id=1, source_target_pairs={{0,9},{8,1},{9,0},{4,13},{5,12},{12,5},{13,4},{1,8},{2,11},{10,3},... | collective-permute-start | bytes 798728 | tf_op jit(solution)/shard_map/ppermute | solution.py:566
  10.4 1.2 copy-start.2
  11.7 0.7 copy-start.5
  12.3 33.9 %copy-start.3 = (bf16[1024,512]{1,0:T(8,128)(2,1)S(1)}, bf16[1024,512]{1,0:T(8,128)(2,1)}, u32[]{:S(2)}) copy-start(bf16[1024,512]{1,0:T(8,128)(2,1)} %refs_4_.3) | copy-start | bytes 3145732
  17.2 35.1 %collective-permute-start.3 = (bf16[1040,128]{1,0:T(8,128)(2,1)S(1)}, bf16[1040,128]{1,0:T(8,128)(2,1)S(1)}, u32[]{:S(2)}, u32[]{:S(2)}) collective-permute-start(bf16[1040,128]{1,0:T(8,128)(2,1)S(1)} %get-tuple-element.75), channel_id=1, source_target_pairs={{0,5},{8,13},{9,12},{4,9},{5,8},{12,1},{13,0},{1,4},{2,7},{10,15},... | collective-permute-start | bytes 798728 | tf_op jit(solution)/shard_map/ppermute | solution.py:566
  18.9 33.5 %collective-permute-start.2 = (bf16[1040,128]{1,0:T(8,128)(2,1)S(1)}, bf16[1040,128]{1,0:T(8,128)(2,1)S(1)}, u32[]{:S(2)}, u32[]{:S(2)}) collective-permute-start(bf16[1040,128]{1,0:T(8,128)(2,1)S(1)} %get-tuple-element.69.refs_4_), channel_id=1, source_target_pairs={{0,4},{8,12},{9,13},{4,8},{5,9},{12,0},{13,1},{1,5},{2,6},{10,14},... | collective-permute-start | bytes 798728 | tf_op jit(solution)/shard_map/ppermute | solution.py:566
  20.4 35.6 %collective-permute-start.4 = (bf16[1040,128]{1,0:T(8,128)(2,1)S(1)}, bf16[1040,128]{1,0:T(8,128)(2,1)S(1)}, u32[]{:S(2)}, u32[]{:S(2)}) collective-permute-start(bf16[1040,128]{1,0:T(8,128)(2,1)S(1)} %get-tuple-element.76), channel_id=1, source_target_pairs={{0,12},{8,4},{9,5},{4,0},{5,1},{12,8},{13,9},{1,13},{2,14},{10,6},... | collective-permute-start | bytes 798728 | tf_op jit(solution)/shard_map/ppermute | solution.py:566
  40.7 15.3 %collective-permute-start.5 = (bf16[1040,128]{1,0:T(8,128)(2,1)S(1)}, bf16[1040,128]{1,0:T(8,128)(2,1)S(1)}, u32[]{:S(2)}, u32[]{:S(2)}) collective-permute-start(bf16[1040,128]{1,0:T(8,128)(2,1)S(1)} %get-tuple-element.77), channel_id=1, source_target_pairs={{0,13},{8,5},{9,4},{4,1},{5,0},{12,9},{13,8},{1,12},{2,15},{10,7},... | collective-permute-start | bytes 798728 | tf_op jit(solution)/shard_map/ppermute | solution.py:566
  44.8 11.2 %collective-permute-start.6 = (bf16[1040,128]{1,0:T(8,128)(2,1)S(1)}, bf16[1040,128]{1,0:T(8,128)(2,1)S(1)}, u32[]{:S(2)}, u32[]{:S(2)}) collective-permute-start(bf16[1040,128]{1,0:T(8,128)(2,1)S(1)} %get-tuple-element.78), channel_id=1, source_target_pairs={{0,1},{8,9},{9,8},{4,5},{5,4},{12,13},{13,12},{1,0},{2,3},{10,11},... | collective-permute-start | bytes 798728 | tf_op jit(solution)/shard_map/ppermute | solution.py:566
  52.3 8.4 %collective-permute-start.13 = (bf16[512,128]{1,0:T(8,128)(2,1)S(1)}, bf16[512,128]{1,0:T(8,128)(2,1)S(1)}, u32[]{:S(2)}, u32[]{:S(2)}) collective-permute-start(bf16[512,128]{1,0:T(8,128)(2,1)S(1)} %get-tuple-element.96), channel_id=1, source_target_pairs={{0,1},{8,9},{9,8},{4,5},{5,4},{12,13},{13,12},{1,0},{2,3},{10,11},... | collective-permute-start | bytes 393224 | tf_op jit(solution)/shard_map/ppermute | solution.py:566
  52.4 12.2 %collective-permute-start.12 = (bf16[512,128]{1,0:T(8,128)(2,1)S(1)}, bf16[512,128]{1,0:T(8,128)(2,1)S(1)}, u32[]{:S(2)}, u32[]{:S(2)}) collective-permute-start(bf16[512,128]{1,0:T(8,128)(2,1)S(1)} %get-tuple-element.94), channel_id=1, source_target_pairs={{0,13},{8,5},{9,4},{4,1},{5,0},{12,9},{13,8},{1,12},{2,15},{10,7},... | collective-permute-start | bytes 393224 | tf_op jit(solution)/shard_map/ppermute | solution.py:566
  56.0 22.6 %collective-permute-start.11 = (bf16[512,128]{1,0:T(8,128)(2,1)S(1)}, bf16[512,128]{1,0:T(8,128)(2,1)S(1)}, u32[]{:S(2)}, u32[]{:S(2)}) collective-permute-start(bf16[512,128]{1,0:T(8,128)(2,1)S(1)} %get-tuple-element.92), channel_id=1, source_target_pairs={{0,12},{8,4},{9,5},{4,0},{5,1},{12,8},{13,9},{1,13},{2,14},{10,6},... | collective-permute-start | bytes 393224 | tf_op jit(solution)/shard_map/ppermute | solution.py:566
  60.7 17.9 %collective-permute-start.10 = (bf16[512,128]{1,0:T(8,128)(2,1)S(1)}, bf16[512,128]{1,0:T(8,128)(2,1)S(1)}, u32[]{:S(2)}, u32[]{:S(2)}) collective-permute-start(bf16[512,128]{1,0:T(8,128)(2,1)S(1)} %get-tuple-element.90), channel_id=1, source_target_pairs={{0,5},{8,13},{9,12},{4,9},{5,8},{12,1},{13,0},{1,4},{2,7},{10,15},... | collective-permute-start | bytes 393224 | tf_op jit(solution)/shard_map/ppermute | solution.py:566
  60.7 17.9 %collective-permute-start.9 = (bf16[512,128]{1,0:T(8,128)(2,1)S(1)}, bf16[512,128]{1,0:T(8,128)(2,1)S(1)}, u32[]{:S(2)}, u32[]{:S(2)}) collective-permute-start(bf16[512,128]{1,0:T(8,128)(2,1)S(1)} %get-tuple-element.88), channel_id=1, source_target_pairs={{0,4},{8,12},{9,13},{4,8},{5,9},{12,0},{13,1},{1,5},{2,6},{10,14},... | collective-permute-start | bytes 393224 | tf_op jit(solution)/shard_map/ppermute | solution.py:566
  60.7 19.0 %collective-permute-start.8 = (bf16[512,128]{1,0:T(8,128)(2,1)S(1)}, bf16[512,128]{1,0:T(8,128)(2,1)S(1)}, u32[]{:S(2)}, u32[]{:S(2)}) collective-permute-start(bf16[512,128]{1,0:T(8,128)(2,1)S(1)} %get-tuple-element.86), channel_id=1, source_target_pairs={{0,9},{8,1},{9,0},{4,13},{5,12},{12,5},{13,4},{1,8},{2,11},{10,3},... | collective-permute-start | bytes 393224 | tf_op jit(solution)/shard_map/ppermute | solution.py:566
  64.6 18.4 %collective-permute-start.7 = (bf16[512,128]{1,0:T(8,128)(2,1)S(1)}, bf16[512,128]{1,0:T(8,128)(2,1)S(1)}, u32[]{:S(2)}, u32[]{:S(2)}) collective-permute-start(bf16[512,128]{1,0:T(8,128)(2,1)S(1)} %get-tuple-element.84), channel_id=1, source_target_pairs={{0,8},{8,0},{9,1},{4,12},{5,13},{12,4},{13,5},{1,9},{2,10},{10,2},... | collective-permute-start | bytes 393224 | tf_op jit(solution)/shard_map/ppermute | solution.py:566
  82.9 21.8 %collective-permute-start.14 = (bf16[2,512,128]{2,1,0:T(8,128)(2,1)S(1)}, bf16[2,512,128]{2,1,0:T(8,128)(2,1)S(1)}, u32[]{:S(2)}, u32[]{:S(2)}) collective-permute-start(bf16[2,512,128]{2,1,0:T(8,128)(2,1)S(1)} %get-tuple-element.98), channel_id=1, source_target_pairs={{0,4},{4,8},{8,12},{12,0},{1,5},{5,9},{9,13},{13,1},{2,6},{6,10},{... | collective-permute-start | bytes 786440 | tf_op jit(solution)/shard_map/ppermute | solution.py:572
  82.9 24.6 %collective-permute-start.15 = (bf16[2,512,128]{2,1,0:T(8,128)(2,1)S(1)}, bf16[2,512,128]{2,1,0:T(8,128)(2,1)S(1)}, u32[]{:S(2)}, u32[]{:S(2)}) collective-permute-start(bf16[2,512,128]{2,1,0:T(8,128)(2,1)S(1)} %get-tuple-element.99), channel_id=1, source_target_pairs={{0,8},{4,12},{8,0},{12,4},{1,9},{5,13},{9,1},{13,5},{2,10},{6,14},... | collective-permute-start | bytes 786440 | tf_op jit(solution)/shard_map/ppermute | solution.py:572
  84.4 23.1 %collective-permute-start.16 = (bf16[2,512,128]{2,1,0:T(8,128)(2,1)S(1)}, bf16[2,512,128]{2,1,0:T(8,128)(2,1)S(1)}, u32[]{:S(2)}, u32[]{:S(2)}) collective-permute-start(bf16[2,512,128]{2,1,0:T(8,128)(2,1)S(1)} %get-tuple-element.100), channel_id=1, source_target_pairs={{0,12},{4,0},{8,4},{12,8},{1,13},{5,1},{9,5},{13,9},{2,14},{6,2},{... | collective-permute-start | bytes 786440 | tf_op jit(solution)/shard_map/ppermute | solution.py:572
  102.5 11.5 %collective-permute-start.18 = (bf16[2,544,128]{2,1,0:T(8,128)(2,1)S(1)}, bf16[2,544,128]{2,1,0:T(8,128)(2,1)S(1)}, u32[]{:S(2)}, u32[]{:S(2)}) collective-permute-start(bf16[2,544,128]{2,1,0:T(8,128)(2,1)S(1)} %get-tuple-element.107), channel_id=1, source_target_pairs={{0,4},{4,8},{8,12},{12,0},{1,5},{5,9},{9,13},{13,1},{2,6},{6,10},{... | collective-permute-start | bytes 835592 | tf_op jit(solution)/shard_map/ppermute | solution.py:572
  103.1 24.5 %collective-permute-start.19 = (bf16[2,544,128]{2,1,0:T(8,128)(2,1)S(1)}, bf16[2,544,128]{2,1,0:T(8,128)(2,1)S(1)}, u32[]{:S(2)}, u32[]{:S(2)}) collective-permute-start(bf16[2,544,128]{2,1,0:T(8,128)(2,1)S(1)} %get-tuple-element.108), channel_id=1, source_target_pairs={{0,8},{4,12},{8,0},{12,4},{1,9},{5,13},{9,1},{13,5},{2,10},{6,14},... | collective-permute-start | bytes 835592 | tf_op jit(solution)/shard_map/ppermute | solution.py:572
  104.7 22.9 %collective-permute-start.20 = (bf16[2,544,128]{2,1,0:T(8,128)(2,1)S(1)}, bf16[2,544,128]{2,1,0:T(8,128)(2,1)S(1)}, u32[]{:S(2)}, u32[]{:S(2)}) collective-permute-start(bf16[2,544,128]{2,1,0:T(8,128)(2,1)S(1)} %get-tuple-element.109), channel_id=1, source_target_pairs={{0,12},{4,0},{8,4},{12,8},{1,13},{5,1},{9,5},{13,9},{2,14},{6,2},{... | collective-permute-start | bytes 835592 | tf_op jit(solution)/shard_map/ppermute | solution.py:572
  108.1 20.1 %collective-permute-start.17 = (bf16[4,512,128]{2,1,0:T(8,128)(2,1)S(1)}, bf16[4,512,128]{2,1,0:T(8,128)(2,1)S(1)}, u32[]{:S(2)}, u32[]{:S(2)}) collective-permute-start(bf16[4,512,128]{2,1,0:T(8,128)(2,1)S(1)} %swap_value.1), channel_id=1, source_target_pairs={{0,1},{1,0},{2,3},{3,2},{4,5},{5,4},{6,7},{7,6},{8,9},{9,8},{10,11... | collective-permute-start | bytes 1572872 | tf_op jit(solution)/shard_map/ppermute | solution.py:572
  128.2 2.6 %collective-permute-start.21 = (bf16[4,544,128]{2,1,0:T(8,128)(2,1)S(1)}, bf16[4,544,128]{2,1,0:T(8,128)(2,1)S(1)}, u32[]{:S(2)}, u32[]{:S(2)}) collective-permute-start(bf16[4,544,128]{2,1,0:T(8,128)(2,1)S(1)} %swap_query.1), channel_id=1, source_target_pairs={{0,1},{1,0},{2,3},{3,2},{4,5},{5,4},{6,7},{7,6},{8,9},{9,8},{10,11... | collective-permute-start | bytes 1671176 | tf_op jit(solution)/shard_map/ppermute | solution.py:572
  132.8 27.8 %collective-permute-start.23 = (bf16[1024,512]{1,0:T(8,128)(2,1)S(1)}, bf16[1024,512]{1,0:T(8,128)(2,1)S(1)}, u32[]{:S(2)}, u32[]{:S(2)}) collective-permute-start(bf16[1024,512]{1,0:T(8,128)(2,1)S(1)} %get-tuple-element.115), channel_id=1, source_target_pairs={{0,2},{2,0},{1,3},{3,1},{4,6},{6,4},{5,7},{7,5},{8,10},{10,8},{9,1... | collective-permute-start | bytes 3145736 | tf_op jit(solution)/shard_map/ppermute | solution.py:572
  134.3 2.4 %collective-permute-start.27 = (bf16[4,128,512]{2,1,0:T(8,128)(2,1)S(1)}, bf16[4,128,512]{2,1,0:T(8,128)(2,1)S(1)}, u32[]{:S(2)}, u32[]{:S(2)}) collective-permute-start(bf16[4,128,512]{2,1,0:T(8,128)(2,1)S(1)} %get-tuple-element.122), channel_id=1, source_target_pairs={{0,1},{1,0},{2,3},{3,2},{4,5},{5,4},{6,7},{7,6},{8,9},{9,8},{10,11... | collective-permute-start | bytes 1572872 | tf_op jit(solution)/shard_map/ppermute | solution.py:572
  136.3 9.1 %collective-permute-start.22 = (bf16[4,128,512]{2,1,0:T(8,128)(2,1)S(1)}, bf16[4,128,512]{2,1,0:T(8,128)(2,1)S(1)}, u32[]{:S(2)}, u32[]{:S(2)}) collective-permute-start(bf16[4,128,512]{2,1,0:T(8,128)(2,1)S(1)} %get-tuple-element.112), channel_id=1, source_target_pairs={{0,1},{1,0},{2,3},{3,2},{4,5},{5,4},{6,7},{7,6},{8,9},{9,8},{10,11... | collective-permute-start | bytes 1572872 | tf_op jit(solution)/shard_map/ppermute | solution.py:572
  137.4 9.4 %collective-permute-start.28 = (bf16[128,512]{1,0:T(8,128)(2,1)S(1)}, bf16[128,512]{1,0:T(8,128)(2,1)S(1)}, u32[]{:S(2)}, u32[]{:S(2)}) collective-permute-start(bf16[128,512]{1,0:T(8,128)(2,1)S(1)} %get-tuple-element.128), channel_id=1, source_target_pairs={{0,4},{4,8},{8,12},{12,0},{1,5},{5,9},{9,13},{13,1},{2,6},{6,10},{... | collective-permute-start | bytes 393224 | tf_op jit(solution)/shard_map/ppermute | solution.py:572
  142.9 9.7 %collective-permute-start.29 = (bf16[128,512]{1,0:T(8,128)(2,1)S(1)}, bf16[128,512]{1,0:T(8,128)(2,1)S(1)}, u32[]{:S(2)}, u32[]{:S(2)}) collective-permute-start(bf16[128,512]{1,0:T(8,128)(2,1)S(1)} %get-tuple-element.129), channel_id=1, source_target_pairs={{0,8},{4,12},{8,0},{12,4},{1,9},{5,13},{9,1},{13,5},{2,10},{6,14},... | collective-permute-start | bytes 393224 | tf_op jit(solution)/shard_map/ppermute | solution.py:572
  143.0 16.9 %collective-permute-start.30 = (bf16[128,512]{1,0:T(8,128)(2,1)S(1)}, bf16[128,512]{1,0:T(8,128)(2,1)S(1)}, u32[]{:S(2)}, u32[]{:S(2)}) collective-permute-start(bf16[128,512]{1,0:T(8,128)(2,1)S(1)} %get-tuple-element.130), channel_id=1, source_target_pairs={{0,12},{4,0},{8,4},{12,8},{1,13},{5,1},{9,5},{13,9},{2,14},{6,2},{... | collective-permute-start | bytes 393224 | tf_op jit(solution)/shard_map/ppermute | solution.py:572
  146.1 16.9 %collective-permute-start.24 = (bf16[128,512]{1,0:T(8,128)(2,1)S(1)}, bf16[128,512]{1,0:T(8,128)(2,1)S(1)}, u32[]{:S(2)}, u32[]{:S(2)}) collective-permute-start(bf16[128,512]{1,0:T(8,128)(2,1)S(1)} %get-tuple-element.118), channel_id=1, source_target_pairs={{0,4},{4,8},{8,12},{12,0},{1,5},{5,9},{9,13},{13,1},{2,6},{6,10},{... | collective-permute-start | bytes 393224 | tf_op jit(solution)/shard_map/ppermute | solution.py:572
  146.8 16.3 %collective-permute-start.25 = (bf16[128,512]{1,0:T(8,128)(2,1)S(1)}, bf16[128,512]{1,0:T(8,128)(2,1)S(1)}, u32[]{:S(2)}, u32[]{:S(2)}) collective-permute-start(bf16[128,512]{1,0:T(8,128)(2,1)S(1)} %get-tuple-element.119), channel_id=1, source_target_pairs={{0,8},{4,12},{8,0},{12,4},{1,9},{5,13},{9,1},{13,5},{2,10},{6,14},... | collective-permute-start | bytes 393224 | tf_op jit(solution)/shard_map/ppermute | solution.py:572
  152.6 10.5 %collective-permute-start.26 = (bf16[128,512]{1,0:T(8,128)(2,1)S(1)}, bf16[128,512]{1,0:T(8,128)(2,1)S(1)}, u32[]{:S(2)}, u32[]{:S(2)}) collective-permute-start(bf16[128,512]{1,0:T(8,128)(2,1)S(1)} %get-tuple-element.120), channel_id=1, source_target_pairs={{0,12},{4,0},{8,4},{12,8},{1,13},{5,1},{9,5},{13,9},{2,14},{6,2},{... | collective-permute-start | bytes 393224 | tf_op jit(solution)/shard_map/ppermute | solution.py:572

commit v19 on v18

--- a/solution.py
+++ b/solution.py
@@ -142,7 +142,7 @@
     pick = ones_where(iota((rows, toks), 0) + group * rows == slot)
     for copy in loads[0] + loads[2]:
         copy.wait()
-    step = min(512, toks)
+    step = fine
     for first in range(0, toks, step):
         for copy in loads[1][first // fine : (first + step) // fine]:
             copy.wait()
@@ -153,15 +153,17 @@
             even, odd = beside(query[:, pair_columns], cotan[:, pair_columns])
             mixed_ref[where, 2 * pair * LANES : (2 * pair + 1) * LANES] = even
             mixed_ref[where, (2 * pair + 1) * LANES : (2 * pair + 2) * LANES] = odd
-    in_order = dot(pick, mixed_ref[...]).astype(BF16)
-    for ahead, out_ref in enumerate(out_refs):
-        sub = lax.rem(me[1] + ahead, jnp.int32(sizes[1]))
-        for other in range(sizes[1]):
-
-            @pl.when(sub == other)
-            def _():
-                out_ref[:rows, :] = in_order[:, other * LANES : (other + 1) * LANES]
-
+    part = min(256, rows)
+    for first in range(0, rows, part):
+        where = slice(first, first + part)
+        in_order = dot(pick[where, :], mixed_ref[...]).astype(BF16)
+        for ahead, out_ref in enumerate(out_refs):
+            sub = lax.rem(me[1] + ahead, jnp.int32(sizes[1]))
+            piece = in_order[:, :LANES]
+            for other in range(1, sizes[1]):
+                piece = jnp.where(sub == other, in_order[:, other * LANES : (other + 1) * LANES], piece)
+            out_ref[where, :] = piece
+    for out_ref in out_refs:
         out_ref[rows:, :] = tallies
 
 
@@ -486,7 +488,10 @@
     bring_home(sizes, heads, arrivals(sizes, me_ref, part_refs), home_ref, rows_ref)
     for k, (term_ref, out_ref) in enumerate(zip(term_refs, out_refs)):
         mine = input_columns(me_ref, k + 1, parts, weight_ref.shape[0])
-        out_ref[...] = (dot_nt(rows_ref[...], weight_ref[mine, :]) + term_ref[...]).astype(BF16)
+        step = min(256, rows_ref.shape[0])
+        for first in range(0, rows_ref.shape[0], step):
+            where = slice(first, first + step)
+            out_ref[where, :] = (dot_nt(rows_ref[where, :], weight_ref[mine, :]) + term_ref[where, :]).astype(BF16)
     half = rows_ref.shape[0] * heads // home_ref.shape[0] // 2
     unfold(home_ref, centroid_ref, heads, half, home_ref.shape[1] - half, lambda x: x * factor)
 
@@ -525,7 +530,10 @@
     for part_ref in part_refs[1:]:
         total = total + part_ref[...].astype(F32)
     total_ref[...] = total.astype(BF16)
-    out_ref[...] = dot(unsort_ref[...], total_ref[...]).astype(BF16)
+    step = min(256, out_ref.shape[0])
+    for first in range(0, out_ref.shape[0], step):
+        where = slice(first, first + step)
+        out_ref[where, :] = dot(unsort_ref[where, :], total_ref[...]).astype(BF16)
     weight_out_ref[...] = weight_ref[...]
 
 

time: 165 us -> 165 us (level)
  no operation moved by 1% of the time
where the time goes in v19:
time: 165 us; the launch traced here: 164 us
  Pallas kernels  61.2 us (37%)
  starting transfers between devices  50.3 us (30%)
  waiting for transfers between devices  49.5 us (30%)
  local copies, waits for them, and re-layouts  1.92 us (1%)
    pallas_call x16, Pallas kernels, call(): pl.pallas_call(body, out_shape=outs, in_specs=specs, out_specs=jax.tree.m...  61.2 us
    ppermute x17, starting transfers between devices, shift(): lax.ppermute(part, axis, [(i, (i + ahead) % size) for i in range(size)])  26.4 us
    ppermute x14, waiting for transfers between devices, exchange(): out.append(part if ahead == (0, 0) else lax.ppermute(part, OWNERS, moves))  26 us
    ppermute x14, starting transfers between devices, exchange(): out.append(part if ahead == (0, 0) else lax.ppermute(part, OWNERS, moves))  23.9 us
    ppermute x17, waiting for transfers between devices, shift(): lax.ppermute(part, axis, [(i, (i + ahead) % size) for i in range(size)])  23.5 us
  transfers between devices with their start and end apart: 31, of which 9 were waited for; matrix products, arithmetic and copies ran while one was open for 0% of the time, Pallas kernels for 32%

profile of v19, /device:TPU:0, one launch (start us, length us, event | category | flops | bytes accessed | tf_op | source)
XLA Modules:
  0.0 163.8 jit_solution(6768023889948828833)
XLA Ops:
  0.7 5.5 %project_far.1 = (bf16[1040,128]{1,0:T(8,128)(2,1)}, bf16[1040,128]{1,0:T(8,128)(2,1)}, s32[1,1024]{1,0:T(1,128)}) custom-call(s32[1,1024]{1,0:T(1,128)} %bitcast.5, bf16[1024,1024]{1,0:T(8,128)(2,1)} %refs_2_.4, bf16[1024,512]{1,0:T(8,128)(2,1)} %refs_3_.7, bf16[1024,512]{1,0:T(8,128)(2,1)} %refs_5_.1), custom_call_target="tpu_custom_call" | custom-call | flops 805306368 | bytes 4734976 | tf_op jit(solution)/shard_map/project_far/pallas_call | solution.py:552
  6.1 4.1 %collective-permute-start = (bf16[1040,128]{1,0:T(8,128)(2,1)}, bf16[1040,128]{1,0:T(8,128)(2,1)S(1)}, u32[]{:S(2)}, u32[]{:S(2)}) collective-permute-start(bf16[1040,128]{1,0:T(8,128)(2,1)} %get-tuple-element.73), channel_id=1, source_target_pairs={{0,8},{8,0},{9,1},{4,12},{5,13},{12,4},{13,5},{1,9},{2,10},{10,2},... | collective-permute-start | bytes 798728 | tf_op jit(solution)/shard_map/ppermute | solution.py:574
  10.4 1.2 copy-done.2
  11.6 0.7 copy-done.5
  12.3 4.8 %project_query.1 = (bf16[1040,128]{1,0:T(8,128)(2,1)S(1)}, bf16[1040,128]{1,0:T(8,128)(2,1)S(1)}, bf16[1040,128]{1,0:T(8,128)(2,1)S(1)}, bf16[1040,128]{1,0:T(8,...) custom-call(s32[4]{0:T(128)S(1)} %pad_add_fusion.refs_0_, s32[1,1024]{1,0:T(1,128)S(1)} %copy-done.5, ...), custom_call_target="tpu_custom_call" | custom-call | flops 3221225472 | bytes 5799952 | tf_op jit(solution)/shard_map/project_query/pallas_call | solution.py:552
  17.1 1.7 %collective-permute-start.3 = (bf16[1040,128]{1,0:T(8,128)(2,1)S(1)}, bf16[1040,128]{1,0:T(8,128)(2,1)S(1)}, u32[]{:S(2)}, u32[]{:S(2)}) collective-permute-start(bf16[1040,128]{1,0:T(8,128)(2,1)S(1)} %get-tuple-element.75), channel_id=1, source_target_pairs={{0,5},{8,13},{9,12},{4,9},{5,8},{12,1},{13,0},{1,4},{2,7},{10,15},... | collective-permute-start | bytes 798728 | tf_op jit(solution)/shard_map/ppermute | solution.py:574
  18.8 1.6 collective-permute-start.2
  20.3 2.3 %collective-permute-start.4 = (bf16[1040,128]{1,0:T(8,128)(2,1)S(1)}, bf16[1040,128]{1,0:T(8,128)(2,1)S(1)}, u32[]{:S(2)}, u32[]{:S(2)}) collective-permute-start(bf16[1040,128]{1,0:T(8,128)(2,1)S(1)} %get-tuple-element.76), channel_id=1, source_target_pairs={{0,12},{8,4},{9,5},{4,0},{5,1},{12,8},{13,9},{1,13},{2,14},{10,6},... | collective-permute-start | bytes 798728 | tf_op jit(solution)/shard_map/ppermute | solution.py:574
  22.6 18.0 %collective-permute-done.refs_2_ = bf16[1040,128]{1,0:T(8,128)(2,1)S(1)} collective-permute-done((bf16[1040,128]{1,0:T(8,128)(2,1)}, bf16[1040,128]{1,0:T(8,128)(2,1)S(1)}, u32[]{:S(2)}, u32[]{:S(2)}) %collective-permute-start) | collective-permute-done | bytes 266272 | tf_op jit(solution)/shard_map/ppermute | solution.py:574
  40.6 4.1 %collective-permute-done.1.refs_3_ = bf16[1040,128]{1,0:T(8,128)(2,1)} collective-permute-done((bf16[1040,128]{1,0:T(8,128)(2,1)}, bf16[1040,128]{1,0:T(8,128)(2,1)}, u32[]{:S(2)}, u32[]{:S(2)}) %collective-permute-start.1) | collective-permute-done | bytes 266272 | tf_op jit(solution)/shard_map/ppermute | solution.py:574
  44.8 1.4 collective-permute-start.6
  46.2 6.0 %project_value.1 = (bf16[512,128]{1,0:T(8,128)(2,1)S(1)}, bf16[512,128]{1,0:T(8,128)(2,1)S(1)}, bf16[512,128]{1,0:T(8,128)(2,1)S(1)}, bf16[512,128]{1,0:T(8,128)...) custom-call(s32[4]{0:T(128)S(1)} %pad_add_fusion.refs_0_, ...), custom_call_target="tpu_custom_call" | custom-call | flops 2147483648 | bytes 8392720 | tf_op jit(solution)/shard_map/project_value/pallas_call | solution.py:552
  52.3 3.6 %collective-permute-start.12 = (bf16[512,128]{1,0:T(8,128)(2,1)S(1)}, bf16[512,128]{1,0:T(8,128)(2,1)S(1)}, u32[]{:S(2)}, u32[]{:S(2)}) collective-permute-start(bf16[512,128]{1,0:T(8,128)(2,1)S(1)} %get-tuple-element.94), channel_id=1, source_target_pairs={{0,13},{8,5},{9,4},{4,1},{5,0},{12,9},{13,8},{1,12},{2,15},{10,7},... | collective-permute-start | bytes 393224 | tf_op jit(solution)/shard_map/ppermute | solution.py:574
  55.9 4.7 %collective-permute-start.11 = (bf16[512,128]{1,0:T(8,128)(2,1)S(1)}, bf16[512,128]{1,0:T(8,128)(2,1)S(1)}, u32[]{:S(2)}, u32[]{:S(2)}) collective-permute-start(bf16[512,128]{1,0:T(8,128)(2,1)S(1)} %get-tuple-element.92), channel_id=1, source_target_pairs={{0,12},{8,4},{9,5},{4,0},{5,1},{12,8},{13,9},{1,13},{2,14},{10,6},... | collective-permute-start | bytes 393224 | tf_op jit(solution)/shard_map/ppermute | solution.py:574
  60.6 3.8 %collective-permute-start.8 = (bf16[512,128]{1,0:T(8,128)(2,1)S(1)}, bf16[512,128]{1,0:T(8,128)(2,1)S(1)}, u32[]{:S(2)}, u32[]{:S(2)}) collective-permute-start(bf16[512,128]{1,0:T(8,128)(2,1)S(1)} %get-tuple-element.86), channel_id=1, source_target_pairs={{0,9},{8,1},{9,0},{4,13},{5,12},{12,5},{13,4},{1,8},{2,11},{10,3},... | collective-permute-start | bytes 393224 | tf_op jit(solution)/shard_map/ppermute | solution.py:574
  64.5 0.6 collective-permute-start.7
  65.1 13.9 %value_grad.1 = (bf16[2,512,128]{2,1,0:T(8,128)(2,1)S(1)}, bf16[2,512,128]{2,1,0:T(8,128)(2,1)S(1)}, bf16[2,512,128]{2,1,0:T(8,128)(2,1)S(1)}, bf16[2,512,128]{2...) custom-call(s32[4]{0:T(128)S(1)} %pad_add_fusion.refs_0_, ...), custom_call_target="tpu_custom_call" | custom-call | flops 2147483648 | bytes 8163344 | tf_op jit(solution)/shard_map/value_grad/pallas_call | solution.py:552
  79.0 0.7 collective-permute-done.8.refs_5_
  79.6 3.2 %collective-permute-done.7.refs_4_ = bf16[512,128]{1,0:T(8,128)(2,1)S(1)} collective-permute-done((bf16[512,128]{1,0:T(8,128)(2,1)S(1)}, bf16[512,128]{1,0:T(8,128)(2,1)S(1)}, u32[]{:S(2)}, u32[]{:S(2)}) %collective-permute-start.7) | collective-permute-done | bytes 131104 | tf_op jit(solution)/shard_map/ppermute | solution.py:574
  82.8 1.5 collective-permute-start.15
  84.3 2.4 %collective-permute-start.16 = (bf16[2,512,128]{2,1,0:T(8,128)(2,1)S(1)}, bf16[2,512,128]{2,1,0:T(8,128)(2,1)S(1)}, u32[]{:S(2)}, u32[]{:S(2)}) collective-permute-start(bf16[2,512,128]{2,1,0:T(8,128)(2,1)S(1)} %get-tuple-element.100), channel_id=1, source_target_pairs={{0,12},{4,0},{8,4},{12,8},{1,13},{5,1},{9,5},{13,9},{2,14},{6,2},{... | collective-permute-start | bytes 786440 | tf_op jit(solution)/shard_map/ppermute | solution.py:580
  86.6 16.5 %query_grad.1 = (bf16[2,544,128]{2,1,0:T(8,128)(2,1)S(1)}, bf16[2,544,128]{2,1,0:T(8,128)(2,1)S(1)}, bf16[2,544,128]{2,1,0:T(8,128)(2,1)S(1)}, bf16[2,544,128]{2,1,0:T(8,128)(2,1)S(1)}) custom-call(s32[4]{0:T(128)S(1)} %pad_add_fusion.refs_0_, s32[8,128]{1,0:T(8,128)S(1)} %get-tuple-element.101.refs_1_, bf16[19456,128]{1,0:T(8,128)(2,1)} %get-tuple-element.102.refs_2_, ...), custom_call_target="tpu_custom_call" | custom-call | flops 3221225472 | bytes 7147536 | tf_op jit(solution)/shard_map/query_grad/pallas_call | solution.py:552
  103.1 0.6 collective-permute-start.18
  103.7 1.5 collective-permute-start.19
  105.3 2.8 %collective-permute-start.20 = (bf16[2,544,128]{2,1,0:T(8,128)(2,1)S(1)}, bf16[2,544,128]{2,1,0:T(8,128)(2,1)S(1)}, u32[]{:S(2)}, u32[]{:S(2)}) collective-permute-start(bf16[2,544,128]{2,1,0:T(8,128)(2,1)S(1)} %get-tuple-element.109), channel_id=1, source_target_pairs={{0,12},{4,0},{8,4},{12,8},{1,13},{5,1},{9,5},{13,9},{2,14},{6,2},{... | collective-permute-start | bytes 835592 | tf_op jit(solution)/shard_map/ppermute | solution.py:580
  108.1 0.6 swap_value.1
  108.8 5.9 %collective-permute-done.18.refs_2_.refs_4_ = bf16[2,544,128]{2,1,0:T(8,128)(2,1)S(1)} collective-permute-done((bf16[2,544,128]{2,1,0:T(8,128)(2,1)S(1)}, bf16[2,544,128]{2,1,0:T(8,128)(2,1)S(1)}, u32[]{:S(2)}, u32[]{:S(2)}) %collective-permute-start.18) | collective-permute-done | bytes 278560 | tf_op jit(solution)/shard_map/ppermute | solution.py:580
  114.7 12.8 %collective-permute-done.19.refs_3_.refs_5_ = bf16[2,544,128]{2,1,0:T(8,128)(2,1)S(1)} collective-permute-done((bf16[2,544,128]{2,1,0:T(8,128)(2,1)S(1)}, bf16[2,544,128]{2,1,0:T(8,128)(2,1)S(1)}, u32[]{:S(2)}, u32[]{:S(2)}) %collective-permute-start.19) | collective-permute-done | bytes 278560 | tf_op jit(solution)/shard_map/ppermute | solution.py:580
  127.5 0.6 swap_query.1
  128.2 2.5 %value_home.1 = (bf16[1024,512]{1,0:T(8,128)(2,1)S(1)}, f32[1024,512]{1,0:T(8,128)S(1)}, bf16[4,128,512]{2,1,0:T(8,128)(2,1)S(1)}, bf16[4,128,512]{2,1,0:T(8,128)(2,1)S(1)}) custom-call(s32[4]{0:T(128)S(1)} %pad_add_fusion.refs_0_, bf16[1024,1024]{1,0:T(8,128)(2,1)S(1)} %get-tuple-element.71.refs_1_, bf16[1024,512]{1,0:T(8,128)(2,1)S(1)} %copy-done.3, ...), custom_call_target="tpu_custom_call" | custom-call | flops 1610612736 | bytes 8912912 | tf_op jit(solution)/shard_map/value_home/pallas_call | solution.py:552
  130.7 2.1 %query_home.1 = (bf16[1024,512]{1,0:T(8,128)(2,1)S(1)}, bf16[1024,512]{1,0:T(8,128)(2,1)S(1)}, f32[64,512]{1,0:T(8,128)}) custom-call(s32[4]{0:T(128)S(1)} %pad_add_fusion.refs_0_, bf16[1024,512]{1,0:T(8,128)(2,1)S(1)} %copy-done, f32[1024,512]{1,0:T(8,128)S(1)} %get-tuple-element.106.refs_2_, ...), custom_call_target="tpu_custom_call" | custom-call | flops 536870912 | bytes 7045136 | tf_op jit(solution)/shard_map/query_home/pallas_call | solution.py:552
  132.8 1.5 collective-permute-start.23
  134.3 0.2 collective-permute-start.27
  134.5 1.8 %query_weight.1 = (bf16[4,128,512]{2,1,0:T(8,128)(2,1)S(1)}, bf16[4,128,512]{2,1,0:T(8,128)(2,1)S(1)}) custom-call(s32[4]{0:T(128)S(1)} %pad_add_fusion.refs_0_, bf16[1024,1024]{1,0:T(8,128)(2,1)S(1)} %get-tuple-element.71.refs_1_, bf16[1024,512]{1,0:T(8,128)(2,1)S(1)} %get-tuple-element.110.refs_2_.refs_1_), custom_call_target="tpu_custom_call" | custom-call | flops 1073741824 | bytes 4194320 | tf_op jit(solution)/shard_map/query_weight/pallas_call | solution.py:552
  136.3 0.4 collective-permute-start.22
  136.6 0.7 value_subs.1
  137.3 5.6 %collective-permute-start.28 = (bf16[128,512]{1,0:T(8,128)(2,1)S(1)}, bf16[128,512]{1,0:T(8,128)(2,1)S(1)}, u32[]{:S(2)}, u32[]{:S(2)}) collective-permute-start(bf16[128,512]{1,0:T(8,128)(2,1)S(1)} %get-tuple-element.128), channel_id=1, source_target_pairs={{0,4},{4,8},{8,12},{12,0},{1,5},{5,9},{9,13},{13,1},{2,6},{6,10},{... | collective-permute-start | bytes 393224 | tf_op jit(solution)/shard_map/ppermute | solution.py:580
  142.9 2.4 %collective-permute-start.30 = (bf16[128,512]{1,0:T(8,128)(2,1)S(1)}, bf16[128,512]{1,0:T(8,128)(2,1)S(1)}, u32[]{:S(2)}, u32[]{:S(2)}) collective-permute-start(bf16[128,512]{1,0:T(8,128)(2,1)S(1)} %get-tuple-element.130), channel_id=1, source_target_pairs={{0,12},{4,0},{8,4},{12,8},{1,13},{5,1},{9,5},{13,9},{2,14},{6,2},{... | collective-permute-start | bytes 393224 | tf_op jit(solution)/shard_map/ppermute | solution.py:580
  145.3 0.7 query_subs.1
  146.1 0.7 collective-permute-done.28.refs_1_
  146.7 1.9 %collective-permute-start.25 = (bf16[128,512]{1,0:T(8,128)(2,1)S(1)}, bf16[128,512]{1,0:T(8,128)(2,1)S(1)}, u32[]{:S(2)}, u32[]{:S(2)}) collective-permute-start(bf16[128,512]{1,0:T(8,128)(2,1)S(1)} %get-tuple-element.119), channel_id=1, source_target_pairs={{0,8},{4,12},{8,0},{12,4},{1,9},{5,13},{9,1},{13,5},{2,10},{6,14},... | collective-permute-start | bytes 393224 | tf_op jit(solution)/shard_map/ppermute | solution.py:580
  148.6 3.9 %collective-permute-done.29.refs_2_ = bf16[128,512]{1,0:T(8,128)(2,1)S(1)} collective-permute-done((bf16[128,512]{1,0:T(8,128)(2,1)S(1)}, bf16[128,512]{1,0:T(8,128)(2,1)S(1)}, u32[]{:S(2)}, u32[]{:S(2)}) %collective-permute-start.29) | collective-permute-done | bytes 131104 | tf_op jit(solution)/shard_map/ppermute | solution.py:580
  152.5 5.4 %collective-permute-start.26 = (bf16[128,512]{1,0:T(8,128)(2,1)S(1)}, bf16[128,512]{1,0:T(8,128)(2,1)S(1)}, u32[]{:S(2)}, u32[]{:S(2)}) collective-permute-start(bf16[128,512]{1,0:T(8,128)(2,1)S(1)} %get-tuple-element.120), channel_id=1, source_target_pairs={{0,12},{4,0},{8,4},{12,8},{1,13},{5,1},{9,5},{13,9},{2,14},{6,2},{... | collective-permute-start | bytes 393224 | tf_op jit(solution)/shard_map/ppermute | solution.py:580
  158.0 1.8 %input_own.1.refs_2_.refs_4_ = bf16[1024,512]{1,0:T(8,128)(2,1)S(1)} custom-call(s32[4]{0:T(128)S(1)} %pad_add_fusion.refs_0_, bf16[1024,512]{1,0:T(8,128)(2,1)S(1)} %get-tuple-element.110.refs_2_.refs_1_, bf16[1024,512]{1,0:T(8,128)(2,1)S(1)} %get-tuple-element.114.refs_2_, bf16[1024,512]{1,0:T(8,128)(2,1)S(1)} %copy-done, bf16[1024,512]{1,0:T(8,128)(2,1)S(1)} %copy-done.3, ...), custom_call_target="tpu_custom_call" | custom-call | flops 1073741824 | bytes 5242896 | tf_op jit(solution)/shard_map/input_own/pallas_call | solution.py:552
  159.8 0.8 value_sum.1
  160.6 2.3 %input_sum.1 = (bf16[1024,512]{1,0:T(8,128)(2,1)}, bf16[128,512]{1,0:T(8,128)(2,1)S(1)}) custom-call(bf16[1024,1024]{1,0:T(8,128)(2,1)S(1)} %get-tuple-element.70.refs_9_.refs_0_, bf16[128,512]{1,0:T(8,128)(2,1)S(1)} %get-tuple-element.113.refs_5_.refs_1_, bf16[1024,512]{1,0:T(8,128)(2,1)S(1)} %input_own.1.refs_2_.refs_4_, ...), custom_call_target="tpu_custom_call" | custom-call | flops 1073741824 | bytes 5505024 | tf_op jit(solution)/shard_map/input_sum/pallas_call | solution.py:552
  162.9 0.1 collective-permute-done.25.refs_2_
  163.0 0.8 query_sum.1
  (43 shorter events, 0.4 us)
Async XLA Ops:
  0.6 9.7 %copy-start = (bf16[1024,512]{1,0:T(8,128)(2,1)S(1)}, bf16[1024,512]{1,0:T(8,128)(2,1)}, u32[]{:S(2)}) copy-start(bf16[1024,512]{1,0:T(8,128)(2,1)} %refs_3_.7) | copy-start | bytes 3145732
  0.6 9.7 %copy-start.1 = (bf16[1024,1024]{1,0:T(8,128)(2,1)S(1)}, bf16[1024,1024]{1,0:T(8,128)(2,1)}, u32[]{:S(2)}) copy-start(bf16[1024,1024]{1,0:T(8,128)(2,1)} %refs_2_.4) | copy-start | bytes 6291460
  0.7 9.7 %copy-start.4 = (s32[1024,1]{0,1:T(1,128)S(1)}, s32[1024,1]{0,1:T(1,128)}, u32[]{:S(2)}) copy-start(s32[1024,1]{0,1:T(1,128)} %param.9) | copy-start | bytes 12292
  6.1 34.5 %collective-permute-start = (bf16[1040,128]{1,0:T(8,128)(2,1)}, bf16[1040,128]{1,0:T(8,128)(2,1)S(1)}, u32[]{:S(2)}, u32[]{:S(2)}) collective-permute-start(bf16[1040,128]{1,0:T(8,128)(2,1)} %get-tuple-element.73), channel_id=1, source_target_pairs={{0,8},{8,0},{9,1},{4,12},{5,13},{12,4},{13,5},{1,9},{2,10},{10,2},... | collective-permute-start | bytes 798728 | tf_op jit(solution)/shard_map/ppermute | solution.py:574
  10.2 34.5 %collective-permute-start.1 = (bf16[1040,128]{1,0:T(8,128)(2,1)}, bf16[1040,128]{1,0:T(8,128)(2,1)}, u32[]{:S(2)}, u32[]{:S(2)}) collective-permute-start(bf16[1040,128]{1,0:T(8,128)(2,1)} %get-tuple-element.74), channel_id=1, source_target_pairs={{0,9},{8,1},{9,0},{4,13},{5,12},{12,5},{13,4},{1,8},{2,11},{10,3},... | collective-permute-start | bytes 798728 | tf_op jit(solution)/shard_map/ppermute | solution.py:574
  10.3 1.2 copy-start.2
  11.6 0.7 copy-start.5
  12.3 33.9 %copy-start.3 = (bf16[1024,512]{1,0:T(8,128)(2,1)S(1)}, bf16[1024,512]{1,0:T(8,128)(2,1)}, u32[]{:S(2)}) copy-start(bf16[1024,512]{1,0:T(8,128)(2,1)} %refs_4_.3) | copy-start | bytes 3145732
  17.1 35.1 %collective-permute-start.3 = (bf16[1040,128]{1,0:T(8,128)(2,1)S(1)}, bf16[1040,128]{1,0:T(8,128)(2,1)S(1)}, u32[]{:S(2)}, u32[]{:S(2)}) collective-permute-start(bf16[1040,128]{1,0:T(8,128)(2,1)S(1)} %get-tuple-element.75), channel_id=1, source_target_pairs={{0,5},{8,13},{9,12},{4,9},{5,8},{12,1},{13,0},{1,4},{2,7},{10,15},... | collective-permute-start | bytes 798728 | tf_op jit(solution)/shard_map/ppermute | solution.py:574
  18.8 33.5 %collective-permute-start.2 = (bf16[1040,128]{1,0:T(8,128)(2,1)S(1)}, bf16[1040,128]{1,0:T(8,128)(2,1)S(1)}, u32[]{:S(2)}, u32[]{:S(2)}) collective-permute-start(bf16[1040,128]{1,0:T(8,128)(2,1)S(1)} %get-tuple-element.69.refs_4_), channel_id=1, source_target_pairs={{0,4},{8,12},{9,13},{4,8},{5,9},{12,0},{13,1},{1,5},{2,6},{10,14},... | collective-permute-start | bytes 798728 | tf_op jit(solution)/shard_map/ppermute | solution.py:574
  20.3 35.6 %collective-permute-start.4 = (bf16[1040,128]{1,0:T(8,128)(2,1)S(1)}, bf16[1040,128]{1,0:T(8,128)(2,1)S(1)}, u32[]{:S(2)}, u32[]{:S(2)}) collective-permute-start(bf16[1040,128]{1,0:T(8,128)(2,1)S(1)} %get-tuple-element.76), channel_id=1, source_target_pairs={{0,12},{8,4},{9,5},{4,0},{5,1},{12,8},{13,9},{1,13},{2,14},{10,6},... | collective-permute-start | bytes 798728 | tf_op jit(solution)/shard_map/ppermute | solution.py:574
  40.6 15.3 %collective-permute-start.5 = (bf16[1040,128]{1,0:T(8,128)(2,1)S(1)}, bf16[1040,128]{1,0:T(8,128)(2,1)S(1)}, u32[]{:S(2)}, u32[]{:S(2)}) collective-permute-start(bf16[1040,128]{1,0:T(8,128)(2,1)S(1)} %get-tuple-element.77), channel_id=1, source_target_pairs={{0,13},{8,5},{9,4},{4,1},{5,0},{12,9},{13,8},{1,12},{2,15},{10,7},... | collective-permute-start | bytes 798728 | tf_op jit(solution)/shard_map/ppermute | solution.py:574
  44.8 11.2 %collective-permute-start.6 = (bf16[1040,128]{1,0:T(8,128)(2,1)S(1)}, bf16[1040,128]{1,0:T(8,128)(2,1)S(1)}, u32[]{:S(2)}, u32[]{:S(2)}) collective-permute-start(bf16[1040,128]{1,0:T(8,128)(2,1)S(1)} %get-tuple-element.78), channel_id=1, source_target_pairs={{0,1},{8,9},{9,8},{4,5},{5,4},{12,13},{13,12},{1,0},{2,3},{10,11},... | collective-permute-start | bytes 798728 | tf_op jit(solution)/shard_map/ppermute | solution.py:574
  52.2 8.4 %collective-permute-start.13 = (bf16[512,128]{1,0:T(8,128)(2,1)S(1)}, bf16[512,128]{1,0:T(8,128)(2,1)S(1)}, u32[]{:S(2)}, u32[]{:S(2)}) collective-permute-start(bf16[512,128]{1,0:T(8,128)(2,1)S(1)} %get-tuple-element.96), channel_id=1, source_target_pairs={{0,1},{8,9},{9,8},{4,5},{5,4},{12,13},{13,12},{1,0},{2,3},{10,11},... | collective-permute-start | bytes 393224 | tf_op jit(solution)/shard_map/ppermute | solution.py:574
  52.3 12.2 %collective-permute-start.12 = (bf16[512,128]{1,0:T(8,128)(2,1)S(1)}, bf16[512,128]{1,0:T(8,128)(2,1)S(1)}, u32[]{:S(2)}, u32[]{:S(2)}) collective-permute-start(bf16[512,128]{1,0:T(8,128)(2,1)S(1)} %get-tuple-element.94), channel_id=1, source_target_pairs={{0,13},{8,5},{9,4},{4,1},{5,0},{12,9},{13,8},{1,12},{2,15},{10,7},... | collective-permute-start | bytes 393224 | tf_op jit(solution)/shard_map/ppermute | solution.py:574
  55.9 23.1 %collective-permute-start.11 = (bf16[512,128]{1,0:T(8,128)(2,1)S(1)}, bf16[512,128]{1,0:T(8,128)(2,1)S(1)}, u32[]{:S(2)}, u32[]{:S(2)}) collective-permute-start(bf16[512,128]{1,0:T(8,128)(2,1)S(1)} %get-tuple-element.92), channel_id=1, source_target_pairs={{0,12},{8,4},{9,5},{4,0},{5,1},{12,8},{13,9},{1,13},{2,14},{10,6},... | collective-permute-start | bytes 393224 | tf_op jit(solution)/shard_map/ppermute | solution.py:574
  60.6 18.3 %collective-permute-start.10 = (bf16[512,128]{1,0:T(8,128)(2,1)S(1)}, bf16[512,128]{1,0:T(8,128)(2,1)S(1)}, u32[]{:S(2)}, u32[]{:S(2)}) collective-permute-start(bf16[512,128]{1,0:T(8,128)(2,1)S(1)} %get-tuple-element.90), channel_id=1, source_target_pairs={{0,5},{8,13},{9,12},{4,9},{5,8},{12,1},{13,0},{1,4},{2,7},{10,15},... | collective-permute-start | bytes 393224 | tf_op jit(solution)/shard_map/ppermute | solution.py:574
  60.6 18.3 %collective-permute-start.9 = (bf16[512,128]{1,0:T(8,128)(2,1)S(1)}, bf16[512,128]{1,0:T(8,128)(2,1)S(1)}, u32[]{:S(2)}, u32[]{:S(2)}) collective-permute-start(bf16[512,128]{1,0:T(8,128)(2,1)S(1)} %get-tuple-element.88), channel_id=1, source_target_pairs={{0,4},{8,12},{9,13},{4,8},{5,9},{12,0},{13,1},{1,5},{2,6},{10,14},... | collective-permute-start | bytes 393224 | tf_op jit(solution)/shard_map/ppermute | solution.py:574
  60.6 19.0 %collective-permute-start.8 = (bf16[512,128]{1,0:T(8,128)(2,1)S(1)}, bf16[512,128]{1,0:T(8,128)(2,1)S(1)}, u32[]{:S(2)}, u32[]{:S(2)}) collective-permute-start(bf16[512,128]{1,0:T(8,128)(2,1)S(1)} %get-tuple-element.86), channel_id=1, source_target_pairs={{0,9},{8,1},{9,0},{4,13},{5,12},{12,5},{13,4},{1,8},{2,11},{10,3},... | collective-permute-start | bytes 393224 | tf_op jit(solution)/shard_map/ppermute | solution.py:574
  64.5 18.4 %collective-permute-start.7 = (bf16[512,128]{1,0:T(8,128)(2,1)S(1)}, bf16[512,128]{1,0:T(8,128)(2,1)S(1)}, u32[]{:S(2)}, u32[]{:S(2)}) collective-permute-start(bf16[512,128]{1,0:T(8,128)(2,1)S(1)} %get-tuple-element.84), channel_id=1, source_target_pairs={{0,8},{8,0},{9,1},{4,12},{5,13},{12,4},{13,5},{1,9},{2,10},{10,2},... | collective-permute-start | bytes 393224 | tf_op jit(solution)/shard_map/ppermute | solution.py:574
  82.8 22.5 %collective-permute-start.14 = (bf16[2,512,128]{2,1,0:T(8,128)(2,1)S(1)}, bf16[2,512,128]{2,1,0:T(8,128)(2,1)S(1)}, u32[]{:S(2)}, u32[]{:S(2)}) collective-permute-start(bf16[2,512,128]{2,1,0:T(8,128)(2,1)S(1)} %get-tuple-element.98), channel_id=1, source_target_pairs={{0,4},{4,8},{8,12},{12,0},{1,5},{5,9},{9,13},{13,1},{2,6},{6,10},{... | collective-permute-start | bytes 786440 | tf_op jit(solution)/shard_map/ppermute | solution.py:580
  82.8 25.3 %collective-permute-start.15 = (bf16[2,512,128]{2,1,0:T(8,128)(2,1)S(1)}, bf16[2,512,128]{2,1,0:T(8,128)(2,1)S(1)}, u32[]{:S(2)}, u32[]{:S(2)}) collective-permute-start(bf16[2,512,128]{2,1,0:T(8,128)(2,1)S(1)} %get-tuple-element.99), channel_id=1, source_target_pairs={{0,8},{4,12},{8,0},{12,4},{1,9},{5,13},{9,1},{13,5},{2,10},{6,14},... | collective-permute-start | bytes 786440 | tf_op jit(solution)/shard_map/ppermute | solution.py:580
  84.3 23.8 %collective-permute-start.16 = (bf16[2,512,128]{2,1,0:T(8,128)(2,1)S(1)}, bf16[2,512,128]{2,1,0:T(8,128)(2,1)S(1)}, u32[]{:S(2)}, u32[]{:S(2)}) collective-permute-start(bf16[2,512,128]{2,1,0:T(8,128)(2,1)S(1)} %get-tuple-element.100), channel_id=1, source_target_pairs={{0,12},{4,0},{8,4},{12,8},{1,13},{5,1},{9,5},{13,9},{2,14},{6,2},{... | collective-permute-start | bytes 786440 | tf_op jit(solution)/shard_map/ppermute | solution.py:580
  103.1 11.5 %collective-permute-start.18 = (bf16[2,544,128]{2,1,0:T(8,128)(2,1)S(1)}, bf16[2,544,128]{2,1,0:T(8,128)(2,1)S(1)}, u32[]{:S(2)}, u32[]{:S(2)}) collective-permute-start(bf16[2,544,128]{2,1,0:T(8,128)(2,1)S(1)} %get-tuple-element.107), channel_id=1, source_target_pairs={{0,4},{4,8},{8,12},{12,0},{1,5},{5,9},{9,13},{13,1},{2,6},{6,10},{... | collective-permute-start | bytes 835592 | tf_op jit(solution)/shard_map/ppermute | solution.py:580
  103.7 23.8 %collective-permute-start.19 = (bf16[2,544,128]{2,1,0:T(8,128)(2,1)S(1)}, bf16[2,544,128]{2,1,0:T(8,128)(2,1)S(1)}, u32[]{:S(2)}, u32[]{:S(2)}) collective-permute-start(bf16[2,544,128]{2,1,0:T(8,128)(2,1)S(1)} %get-tuple-element.108), channel_id=1, source_target_pairs={{0,8},{4,12},{8,0},{12,4},{1,9},{5,13},{9,1},{13,5},{2,10},{6,14},... | collective-permute-start | bytes 835592 | tf_op jit(solution)/shard_map/ppermute | solution.py:580
  105.3 22.2 %collective-permute-start.20 = (bf16[2,544,128]{2,1,0:T(8,128)(2,1)S(1)}, bf16[2,544,128]{2,1,0:T(8,128)(2,1)S(1)}, u32[]{:S(2)}, u32[]{:S(2)}) collective-permute-start(bf16[2,544,128]{2,1,0:T(8,128)(2,1)S(1)} %get-tuple-element.109), channel_id=1, source_target_pairs={{0,12},{4,0},{8,4},{12,8},{1,13},{5,1},{9,5},{13,9},{2,14},{6,2},{... | collective-permute-start | bytes 835592 | tf_op jit(solution)/shard_map/ppermute | solution.py:580
  108.7 19.5 %collective-permute-start.17 = (bf16[4,512,128]{2,1,0:T(8,128)(2,1)S(1)}, bf16[4,512,128]{2,1,0:T(8,128)(2,1)S(1)}, u32[]{:S(2)}, u32[]{:S(2)}) collective-permute-start(bf16[4,512,128]{2,1,0:T(8,128)(2,1)S(1)} %swap_value.1), channel_id=1, source_target_pairs={{0,1},{1,0},{2,3},{3,2},{4,5},{5,4},{6,7},{7,6},{8,9},{9,8},{10,11... | collective-permute-start | bytes 1572872 | tf_op jit(solution)/shard_map/ppermute | solution.py:580
  128.1 2.6 %collective-permute-start.21 = (bf16[4,544,128]{2,1,0:T(8,128)(2,1)S(1)}, bf16[4,544,128]{2,1,0:T(8,128)(2,1)S(1)}, u32[]{:S(2)}, u32[]{:S(2)}) collective-permute-start(bf16[4,544,128]{2,1,0:T(8,128)(2,1)S(1)} %swap_query.1), channel_id=1, source_target_pairs={{0,1},{1,0},{2,3},{3,2},{4,5},{5,4},{6,7},{7,6},{8,9},{9,8},{10,11... | collective-permute-start | bytes 1671176 | tf_op jit(solution)/shard_map/ppermute | solution.py:580
  132.8 27.8 %collective-permute-start.23 = (bf16[1024,512]{1,0:T(8,128)(2,1)S(1)}, bf16[1024,512]{1,0:T(8,128)(2,1)S(1)}, u32[]{:S(2)}, u32[]{:S(2)}) collective-permute-start(bf16[1024,512]{1,0:T(8,128)(2,1)S(1)} %get-tuple-element.115), channel_id=1, source_target_pairs={{0,2},{2,0},{1,3},{3,1},{4,6},{6,4},{5,7},{7,5},{8,10},{10,8},{9,1... | collective-permute-start | bytes 3145736 | tf_op jit(solution)/shard_map/ppermute | solution.py:580
  134.3 2.4 %collective-permute-start.27 = (bf16[4,128,512]{2,1,0:T(8,128)(2,1)S(1)}, bf16[4,128,512]{2,1,0:T(8,128)(2,1)S(1)}, u32[]{:S(2)}, u32[]{:S(2)}) collective-permute-start(bf16[4,128,512]{2,1,0:T(8,128)(2,1)S(1)} %get-tuple-element.122), channel_id=1, source_target_pairs={{0,1},{1,0},{2,3},{3,2},{4,5},{5,4},{6,7},{7,6},{8,9},{9,8},{10,11... | collective-permute-start | bytes 1572872 | tf_op jit(solution)/shard_map/ppermute | solution.py:580
  136.3 9.1 %collective-permute-start.22 = (bf16[4,128,512]{2,1,0:T(8,128)(2,1)S(1)}, bf16[4,128,512]{2,1,0:T(8,128)(2,1)S(1)}, u32[]{:S(2)}, u32[]{:S(2)}) collective-permute-start(bf16[4,128,512]{2,1,0:T(8,128)(2,1)S(1)} %get-tuple-element.112), channel_id=1, source_target_pairs={{0,1},{1,0},{2,3},{3,2},{4,5},{5,4},{6,7},{7,6},{8,9},{9,8},{10,11... | collective-permute-start | bytes 1572872 | tf_op jit(solution)/shard_map/ppermute | solution.py:580
  137.3 9.4 %collective-permute-start.28 = (bf16[128,512]{1,0:T(8,128)(2,1)S(1)}, bf16[128,512]{1,0:T(8,128)(2,1)S(1)}, u32[]{:S(2)}, u32[]{:S(2)}) collective-permute-start(bf16[128,512]{1,0:T(8,128)(2,1)S(1)} %get-tuple-element.128), channel_id=1, source_target_pairs={{0,4},{4,8},{8,12},{12,0},{1,5},{5,9},{9,13},{13,1},{2,6},{6,10},{... | collective-permute-start | bytes 393224 | tf_op jit(solution)/shard_map/ppermute | solution.py:580
  142.9 9.7 %collective-permute-start.29 = (bf16[128,512]{1,0:T(8,128)(2,1)S(1)}, bf16[128,512]{1,0:T(8,128)(2,1)S(1)}, u32[]{:S(2)}, u32[]{:S(2)}) collective-permute-start(bf16[128,512]{1,0:T(8,128)(2,1)S(1)} %get-tuple-element.129), channel_id=1, source_target_pairs={{0,8},{4,12},{8,0},{12,4},{1,9},{5,13},{9,1},{13,5},{2,10},{6,14},... | collective-permute-start | bytes 393224 | tf_op jit(solution)/shard_map/ppermute | solution.py:580
  142.9 16.9 %collective-permute-start.30 = (bf16[128,512]{1,0:T(8,128)(2,1)S(1)}, bf16[128,512]{1,0:T(8,128)(2,1)S(1)}, u32[]{:S(2)}, u32[]{:S(2)}) collective-permute-start(bf16[128,512]{1,0:T(8,128)(2,1)S(1)} %get-tuple-element.130), channel_id=1, source_target_pairs={{0,12},{4,0},{8,4},{12,8},{1,13},{5,1},{9,5},{13,9},{2,14},{6,2},{... | collective-permute-start | bytes 393224 | tf_op jit(solution)/shard_map/ppermute | solution.py:580
  146.0 16.9 %collective-permute-start.24 = (bf16[128,512]{1,0:T(8,128)(2,1)S(1)}, bf16[128,512]{1,0:T(8,128)(2,1)S(1)}, u32[]{:S(2)}, u32[]{:S(2)}) collective-permute-start(bf16[128,512]{1,0:T(8,128)(2,1)S(1)} %get-tuple-element.118), channel_id=1, source_target_pairs={{0,4},{4,8},{8,12},{12,0},{1,5},{5,9},{9,13},{13,1},{2,6},{6,10},{... | collective-permute-start | bytes 393224 | tf_op jit(solution)/shard_map/ppermute | solution.py:580
  146.7 16.3 %collective-permute-start.25 = (bf16[128,512]{1,0:T(8,128)(2,1)S(1)}, bf16[128,512]{1,0:T(8,128)(2,1)S(1)}, u32[]{:S(2)}, u32[]{:S(2)}) collective-permute-start(bf16[128,512]{1,0:T(8,128)(2,1)S(1)} %get-tuple-element.119), channel_id=1, source_target_pairs={{0,8},{4,12},{8,0},{12,4},{1,9},{5,13},{9,1},{13,5},{2,10},{6,14},... | collective-permute-start | bytes 393224 | tf_op jit(solution)/shard_map/ppermute | solution.py:580
  152.5 10.5 %collective-permute-start.26 = (bf16[128,512]{1,0:T(8,128)(2,1)S(1)}, bf16[128,512]{1,0:T(8,128)(2,1)S(1)}, u32[]{:S(2)}, u32[]{:S(2)}) collective-permute-start(bf16[128,512]{1,0:T(8,128)(2,1)S(1)} %get-tuple-element.120), channel_id=1, source_target_pairs={{0,12},{4,0},{8,4},{12,8},{1,13},{5,1},{9,5},{13,9},{2,14},{6,2},{... | collective-permute-start | bytes 393224 | tf_op jit(solution)/shard_map/ppermute | solution.py:580

commit v20 on v19

--- a/solution.py
+++ b/solution.py
@@ -119,52 +119,71 @@
     ]
 
 
-def project_far_kernel(sizes, groups, rows, heads, assign_ref, tokens_hbm, weight_hbm, cotan_hbm, *refs):
-    out_refs, refs = refs[: sizes[1]], refs[sizes[1] :]
-    slot_ref, tokens_ref, weight_ref, cotan_ref, mixed_ref, sems = refs
-    toks = tokens_ref.shape[0]
-    fine = min(256, toks)
+def fold_halves(tile):
+    half = tile.shape[0] // 2
+    low = low_half((half, LANES))
+    up, down = tile[:half], tile[half:]
+    even = jnp.where(low, up, swap_halves(down)).astype(BF16)
+    return even, jnp.where(low, swap_halves(up), down).astype(BF16)
+
+
+def far_place(sizes, heads):
     me = (lax.axis_index("seq"), lax.axis_index("sub"))
     owner = owner_of(me, steps_of(sizes)[1], sizes) - me[1]
-    group, head = lax.div(owner, jnp.int32(heads)), lax.rem(owner, jnp.int32(heads))
+    head = lax.rem(owner, jnp.int32(heads))
     columns = pl.ds(pl.multiple_of(head * HD, LANES), sizes[1] * HD)
-    loads = [
-        load_rows(source, target, sems.at[kind], fine)
-        for kind, (source, target) in enumerate(
-            ((weight_hbm.at[:, columns], weight_ref), (tokens_hbm, tokens_ref), (cotan_hbm.at[:, columns], cotan_ref))
-        )
-    ]
-    for load in loads:
-        for copy in load:
-            copy.start()
+    return me[1], lax.div(owner, jnp.int32(heads)), columns
+
+
+def give_pieces(pieces, sub, out_refs):
+    for ahead, out_ref in enumerate(out_refs):
+        dest = lax.rem(sub + ahead, jnp.int32(len(pieces)))
+        chosen = pieces[0]
+        for other in range(1, len(pieces)):
+            chosen = jnp.where(dest == other, pieces[other], chosen)
+        out_ref[: chosen.shape[0], :] = chosen
+
+
+def cotan_far_kernel(sizes, groups, rows, heads, assign_ref, cotan_hbm, *refs):
+    out_refs, (slot_ref, cotan_ref, sems) = refs[: sizes[1]], refs[sizes[1] :]
+    toks = cotan_ref.shape[0]
+    sub, group, columns = far_place(sizes, heads)
+    load = load_rows(cotan_hbm.at[:, columns], cotan_ref, sems, min(256, toks))
+    for copy in load:
+        copy.start()
     slot, tallies = slots_of(assign_ref[...], groups, rows)
     slot_ref[...] = slot
     pick = ones_where(iota((rows, toks), 0) + group * rows == slot)
-    for copy in loads[0] + loads[2]:
+    for copy in load:
         copy.wait()
-    step = fine
-    for first in range(0, toks, step):
-        for copy in loads[1][first // fine : (first + step) // fine]:
-            copy.wait()
-        where = slice(first, first + step)
-        query, cotan = dot(tokens_ref[where, :], weight_ref[...]), cotan_ref[where, :].astype(F32)
-        for pair in range(sizes[1] // 2):
-            pair_columns = slice(pair * LANES, (pair + 1) * LANES)
-            even, odd = beside(query[:, pair_columns], cotan[:, pair_columns])
-            mixed_ref[where, 2 * pair * LANES : (2 * pair + 1) * LANES] = even
-            mixed_ref[where, (2 * pair + 1) * LANES : (2 * pair + 2) * LANES] = odd
-    part = min(256, rows)
-    for first in range(0, rows, part):
-        where = slice(first, first + part)
-        in_order = dot(pick[where, :], mixed_ref[...]).astype(BF16)
-        for ahead, out_ref in enumerate(out_refs):
-            sub = lax.rem(me[1] + ahead, jnp.int32(sizes[1]))
-            piece = in_order[:, :LANES]
-            for other in range(1, sizes[1]):
-                piece = jnp.where(sub == other, in_order[:, other * LANES : (other + 1) * LANES], piece)
-            out_ref[where, :] = piece
+    pieces = []
+    for first in range(0, sizes[1] * HD, LANES):
+        pieces += fold_halves(dot(pick, cotan_ref[:, first : first + LANES]))
+    give_pieces(pieces, sub, out_refs)
     for out_ref in out_refs:
-        out_ref[rows:, :] = tallies
+        out_ref[rows // 2 :, :] = tallies
+
+
+def query_far_kernel(sizes, groups, rows, heads, slot_ref, tokens_hbm, weight_hbm, *refs):
+    out_refs, (tokens_ref, weight_ref, query_ref, sems) = refs[: sizes[1]], refs[sizes[1] :]
+    toks = tokens_ref.shape[0]
+    fine = min(256, toks)
+    sub, group, columns = far_place(sizes, heads)
+    weight = load_rows(weight_hbm.at[:, columns], weight_ref, sems.at[0], fine)
+    tokens = load_rows(tokens_hbm, tokens_ref, sems.at[1], fine)
+    for copy in weight + tokens:
+        copy.start()
+    pick = ones_where(iota((rows, toks), 0) + group * rows == slot_ref[...])
+    for copy in weight:
+        copy.wait()
+    for index, copy in enumerate(tokens):
+        copy.wait()
+        where = slice(index * fine, (index + 1) * fine)
+        query_ref[where, :] = dot(tokens_ref[where, :], weight_ref[...]).astype(BF16)
+    pieces = []
+    for first in range(0, sizes[1] * HD, LANES):
+        pieces += fold_halves(dot(pick, query_ref[:, first : first + LANES]))
+    give_pieces(pieces, sub, out_refs)
 
 
 def project_query_kernel(sizes, groups, rows, me_ref, slot_ref, assign_ref, tokens_ref, weight_ref, cotan_ref, *rest):
@@ -314,16 +333,28 @@
 
 def value_grad_kernel(sizes, per_group, slot_rows, me_ref, *refs):
     owners = sizes[0] * sizes[1]
-    mixed_refs, out_refs, rest = refs[:owners], refs[owners : owners + sizes[0]], refs[owners + sizes[0] :]
+    near, came = owners - sizes[1], owners + sizes[1]
+    mixed_refs, far_refs = refs[:near], refs[near:came]
+    out_refs, rest = refs[came : came + sizes[0]], refs[came + sizes[0] :]
     dense_ref, counts_out_ref, counts_ref, place_ref, wide_ref, block_ref, home_ref = rest[:7]
     score_refs, probs_refs = rest[7:9], rest[9:11]
     half = out_refs[0].shape[1]
     rows = 2 * half
-    for ahead, mixed_ref in zip(steps_of(sizes), mixed_refs):
+    steps, subs = steps_of(sizes), sizes[1]
+    low = low_half((half, LANES))
+    for index, ahead in enumerate(steps):
         source = source_of(me_ref, ahead, sizes)
-        tail = mixed_ref[rows:, :].astype(F32).astype(jnp.int32)
-        counts_out_ref[pl.ds(source, 1), :] = tail[:1, :]
-        wide_ref[source, :rows, :] = mixed_ref[:rows, :].astype(F32)
+        if 1 <= index <= subs:
+            cotan = far_refs[index - 1][:half, :].astype(F32)
+            query = far_refs[index - 1 + subs][...].astype(F32)
+            tail = far_refs[index - 1][half:, :]
+            wide_ref[source, :half, :] = jnp.where(low, query, swap_halves(cotan))
+            wide_ref[source, half:rows, :] = jnp.where(low, swap_halves(query), cotan)
+        else:
+            mixed_ref = mixed_refs[index if index == 0 else index - subs]
+            tail = mixed_ref[rows:, :]
+            wide_ref[source, :rows, :] = mixed_ref[:rows, :].astype(F32)
+        counts_out_ref[pl.ds(source, 1), :] = tail.astype(F32).astype(jnp.int32)[:1, :]
         wide_ref[source, rows:, :] = jnp.zeros((slot_rows, LANES), F32)
     pltpu.sync_copy(counts_out_ref, counts_ref)
     blocks = gather_blocks(counts_ref, me_ref, place_ref, owners, per_group, slot_rows, wide_ref, block_ref)
@@ -561,18 +592,16 @@
     )(*inputs, *after)
 
 
+def send(part, ahead, sizes):
+    moves = [
+        (seq * sizes[1] + sub, (seq + ahead[0]) % sizes[0] * sizes[1] + (sub + ahead[1]) % sizes[1])
+        for seq, sub in steps_of(sizes)
+    ]
+    return part if ahead == (0, 0) else lax.ppermute(part, OWNERS, moves)
+
+
 def exchange(parts, sizes):
-    out = []
-    for ahead, part in zip(steps_of(sizes), parts):
-        moves = [
-            (
-                seq * sizes[1] + sub,
-                (seq + ahead[0]) % sizes[0] * sizes[1] + (sub + ahead[1]) % sizes[1],
-            )
-            for seq, sub in steps_of(sizes)
-        ]
-        out.append(part if ahead == (0, 0) else lax.ppermute(part, OWNERS, moves))
-    return out
+    return [send(part, ahead, sizes) for ahead, part in zip(steps_of(sizes), parts)]
 
 
 def shift(part, axis, ahead):
@@ -637,38 +666,55 @@
         return (shape(dims, BF16),) * count
 
     assign_row = assignment.reshape(1, toks)
-    *far_mixed, slot_row = call(
-        functools.partial(project_far_kernel, sizes, groups, rows, heads),
-        several(sizes[1], rows + COUNT_ROWS, LANES) + (shape((1, toks), jnp.int32),),
-        (assign_row, tokens_in, w_query, cotangent),
+    subs = sizes[1]
+    far_columns = subs * HD
+    loads = max(toks, width) // min(256, toks)
+    *far_cotan, slot_row = call(
+        functools.partial(cotan_far_kernel, sizes, groups, rows, heads),
+        several(subs, half + COUNT_ROWS, LANES) + (shape((1, toks), jnp.int32),),
+        (assign_row, cotangent),
         smem=(),
-        in_place=(1, 2, 3),
+        in_place=(1,),
+        scratch=[pltpu.VMEM((toks, far_columns), BF16), pltpu.SemaphoreType.DMA((loads,))],
+        flops=2 * rows * toks * far_columns,
+        vmem=60,
+        name="cotan_far",
+    )
+    far_query = call(
+        functools.partial(query_far_kernel, sizes, groups, rows, heads),
+        several(subs, half, LANES),
+        (slot_row, tokens_in, w_query),
+        smem=(),
+        in_place=(1, 2),
         scratch=[
             pltpu.VMEM((toks, width), BF16),
-            pltpu.VMEM((width, sizes[1] * HD), BF16),
-            pltpu.VMEM((toks, sizes[1] * HD), BF16),
-            pltpu.VMEM((toks, sizes[1] * LANES), BF16),
-            pltpu.SemaphoreType.DMA((3, max(toks, width) // min(256, toks))),
+            pltpu.VMEM((width, far_columns), BF16),
+            pltpu.VMEM((toks, far_columns), BF16),
+            pltpu.SemaphoreType.DMA((2, loads)),
         ],
-        flops=2 * toks * width * sizes[1] * HD + 2 * rows * toks * sizes[1] * LANES,
+        flops=2 * toks * width * far_columns + 2 * rows * toks * far_columns,
         vmem=60,
-        name="project_far",
-    )
+        name="query_far",
+    )
+    steps = steps_of(sizes)
+    far_cotan = [send(part, ahead, sizes) for ahead, part in zip(steps[1:], far_cotan)]
+    far_query = [send(part, ahead, sizes) for ahead, part in zip(steps[1:], far_query)]
     own_mixed, *near_mixed = call(
         functools.partial(project_query_kernel, sizes, groups, rows),
         several(owners - sizes[1], rows + COUNT_ROWS, LANES),
         (me, slot_row, assign_row, tokens_in, w_query, cotangent),
+        after=far_cotan,
         scratch=[pltpu.VMEM((toks, 2 * width_dev), BF16), pltpu.VMEM((owners, rows + COUNT_ROWS, LANES), BF16)],
         flops=2 * toks * width * width_dev + 4 * slots * toks * width_dev,
         name="project_query",
     )
-    send_mixed = [own_mixed, *far_mixed, *near_mixed]
-    got_mixed = exchange(send_mixed, sizes)
+    near_mixed = [send(part, ahead, sizes) for ahead, part in zip(steps[1 + subs :], near_mixed)]
+    got_mixed = [own_mixed, *far_query, *near_mixed]
     *send_value, turned, unsort = call(
         functools.partial(project_value_kernel, sizes, groups, rows),
         several(owners, half, LANES) + several(1, width, slots) + several(1, toks, slots),
         (me, slot_row, tokens_in, w_value),
-        after=near_mixed[:1],
+        after=[own_mixed],
         scratch=[pltpu.VMEM((toks, width_dev), BF16), pltpu.VMEM((owners, half, LANES), BF16)],
         flops=2 * toks * width * width_dev + 2 * slots * toks * width_dev,
         name="project_value",
@@ -689,7 +735,7 @@
         several(sizes[0], sizes[1], half, LANES)
         + several(1, held * BLOCK_ROWS, LANES)
         + (shape((owners, LANES), jnp.int32),),
-        (me, *got_mixed),
+        (me, own_mixed, *near_mixed, *far_cotan, *far_query),
         after=[unsort],
         scratch=[pltpu.SMEM((owners, LANES), jnp.int32), place, tall, dense_rows, tall]
         + [group_f32] * 2

time: 165 us -> 167 us (1.012)
  starting transfers between devices: 50.3 us -> 58.2 us
  waiting for transfers between devices: 49.5 us -> 41.7 us
  Pallas kernels: 61.2 us -> 63.8 us
    ppermute x14 -> x16, waiting for transfers between devices: 26 us -> 18.1 us  [send(): return part if ahead == (0, 0) else lax.ppermute(part, OWNERS, moves)]
    ppermute x14 -> x16, starting transfers between devices: 23.9 us -> 31.8 us  [send(): return part if ahead == (0, 0) else lax.ppermute(part, OWNERS, moves)]
    pallas_call x16 -> x17, Pallas kernels: 61.2 us -> 63.8 us  [call(): pl.pallas_call(body, out_shape=outs, in_specs=specs, out_specs=jax.tree.m...]
  transfers between devices with their start and end apart: 31 -> 33, of which waited for: 9 -> 10; matrix products, arithmetic and copies ran while one was open for 0% -> 0% of each run, Pallas kernels for 32% -> 35%
where the time goes in v20:
time: 167 us; the launch traced here: 166 us
  Pallas kernels  63.8 us (38%)
  starting transfers between devices  58.2 us (35%)
  waiting for transfers between devices  41.7 us (25%)
    pallas_call x17, Pallas kernels, call(): pl.pallas_call(body, out_shape=outs, in_specs=specs, out_specs=jax.tree.m...  63.8 us
    ppermute x16, starting transfers between devices, send(): return part if ahead == (0, 0) else lax.ppermute(part, OWNERS, moves)  31.8 us
    ppermute x17, starting transfers between devices, shift(): lax.ppermute(part, axis, [(i, (i + ahead) % size) for i in range(size)])  26.4 us
    ppermute x17, waiting for transfers between devices, shift(): lax.ppermute(part, axis, [(i, (i + ahead) % size) for i in range(size)])  23.6 us
    ppermute x16, waiting for transfers between devices, send(): return part if ahead == (0, 0) else lax.ppermute(part, OWNERS, moves)  18.1 us
  transfers between devices with their start and end apart: 33, of which 10 were waited for; matrix products, arithmetic and copies ran while one was open for 0% of the time, Pallas kernels for 35%

profile of v20, /device:TPU:0, one launch (start us, length us, event | category | flops | bytes accessed | tf_op | source)
XLA Modules:
  0.0 165.9 jit_solution(15182175514218874426)
XLA Ops:
  0.7 3.4 %cotan_far.1 = (bf16[528,128]{1,0:T(8,128)(2,1)}, bf16[528,128]{1,0:T(8,128)(2,1)}, s32[1,1024]{1,0:T(1,128)}) custom-call(s32[1,1024]{1,0:T(1,128)} %bitcast.5, bf16[1024,512]{1,0:T(8,128)(2,1)} %refs_5_.1), custom_call_target="tpu_custom_call" | custom-call | flops 268435456 | bytes 1327104 | tf_op jit(solution)/shard_map/cotan_far/pallas_call | solution.py:583
  4.1 4.1 %collective-permute-start = (bf16[528,128]{1,0:T(8,128)(2,1)}, bf16[528,128]{1,0:T(8,128)(2,1)S(1)}, u32[]{:S(2)}, u32[]{:S(2)}) collective-permute-start(bf16[528,128]{1,0:T(8,128)(2,1)} %get-tuple-element.71), channel_id=1, source_target_pairs={{0,8},{8,0},{9,1},{4,12},{5,13},{12,4},{13,5},{1,9},{2,10},{10,2},... | collective-permute-start | bytes 405512 | tf_op jit(solution)/shard_map/ppermute | solution.py:600
  8.2 4.4 %query_far.1 = (bf16[512,128]{1,0:T(8,128)(2,1)}, bf16[512,128]{1,0:T(8,128)(2,1)}) custom-call(s32[1,1024]{1,0:T(1,128)} %get-tuple-element.70.refs_1_.refs_0_, bf16[1024,1024]{1,0:T(8,128)(2,1)} %refs_1_.4, bf16[1024,512]{1,0:T(8,128)(2,1)} %refs_3_.5), custom_call_target="tpu_custom_call" | custom-call | flops 536870912 | bytes 3411968 | tf_op jit(solution)/shard_map/query_far/pallas_call | solution.py:583
  12.7 2.1 %collective-permute-start.7 = (bf16[512,128]{1,0:T(8,128)(2,1)}, bf16[512,128]{1,0:T(8,128)(2,1)S(1)}, u32[]{:S(2)}, u32[]{:S(2)}) collective-permute-start(bf16[512,128]{1,0:T(8,128)(2,1)} %get-tuple-element.81), channel_id=1, source_target_pairs={{0,8},{8,0},{9,1},{4,12},{5,13},{12,4},{13,5},{1,9},{2,10},{10,2},... | collective-permute-start | bytes 393224 | tf_op jit(solution)/shard_map/ppermute | solution.py:600
  14.8 0.6 collective-permute-start.8
  15.5 8.7 %collective-permute-done.refs_6_.refs_7_ = bf16[528,128]{1,0:T(8,128)(2,1)S(1)} collective-permute-done((bf16[528,128]{1,0:T(8,128)(2,1)}, bf16[528,128]{1,0:T(8,128)(2,1)S(1)}, u32[]{:S(2)}, u32[]{:S(2)}) %collective-permute-start) | collective-permute-done | bytes 135200 | tf_op jit(solution)/shard_map/ppermute | solution.py:600
  24.3 1.2 collective-permute-done.1.refs_7_.refs_8_
  25.5 1.2 copy-done.2
  26.7 4.8 %project_query.1 = (bf16[1040,128]{1,0:T(8,128)(2,1)S(1)}, bf16[1040,128]{1,0:T(8,128)(2,1)S(1)}, bf16[1040,128]{1,0:T(8,128)(2,1)S(1)}, bf16[1040,128]{1,0:T(8,...) custom-call(s32[4]{0:T(128)S(1)} %pad_add_fusion.refs_0_, s32[1,1024]{1,0:T(1,128)S(1)} %copy-done.5, ...), custom_call_target="tpu_custom_call" | custom-call | flops 3221225472 | bytes 5799952 | tf_op jit(solution)/shard_map/project_query/pallas_call | solution.py:583
  31.6 1.8 %collective-permute-start.2 = (bf16[1040,128]{1,0:T(8,128)(2,1)S(1)}, bf16[1040,128]{1,0:T(8,128)(2,1)S(1)}, u32[]{:S(2)}, u32[]{:S(2)}) collective-permute-start(bf16[1040,128]{1,0:T(8,128)(2,1)S(1)} %get-tuple-element.76), channel_id=1, source_target_pairs={{0,4},{8,12},{9,13},{4,8},{5,9},{12,0},{13,1},{1,5},{2,6},{10,14},... | collective-permute-start | bytes 798728 | tf_op jit(solution)/shard_map/ppermute | solution.py:600
  33.4 3.2 %collective-permute-start.4 = (bf16[1040,128]{1,0:T(8,128)(2,1)S(1)}, bf16[1040,128]{1,0:T(8,128)(2,1)S(1)}, u32[]{:S(2)}, u32[]{:S(2)}) collective-permute-start(bf16[1040,128]{1,0:T(8,128)(2,1)S(1)} %get-tuple-element.78), channel_id=1, source_target_pairs={{0,12},{8,4},{9,5},{4,0},{5,1},{12,8},{13,9},{1,13},{2,14},{10,6},... | collective-permute-start | bytes 798728 | tf_op jit(solution)/shard_map/ppermute | solution.py:600
  36.6 0.8 collective-permute-start.5
  37.4 1.0 collective-permute-start.6
  38.4 6.0 %project_value.1 = (bf16[512,128]{1,0:T(8,128)(2,1)S(1)}, bf16[512,128]{1,0:T(8,128)(2,1)S(1)}, bf16[512,128]{1,0:T(8,128)(2,1)S(1)}, bf16[512,128]{1,0:T(8,128)...) custom-call(s32[4]{0:T(128)S(1)} %pad_add_fusion.refs_0_, ...), custom_call_target="tpu_custom_call" | custom-call | flops 2147483648 | bytes 8392720 | tf_op jit(solution)/shard_map/project_value/pallas_call | solution.py:583
  44.5 4.5 %collective-permute-done.3.refs_3_ = bf16[1040,128]{1,0:T(8,128)(2,1)S(1)} collective-permute-done((bf16[1040,128]{1,0:T(8,128)(2,1)S(1)}, bf16[1040,128]{1,0:T(8,128)(2,1)S(1)}, u32[]{:S(2)}, u32[]{:S(2)}) %collective-permute-start.3) | collective-permute-done | bytes 266272 | tf_op jit(solution)/shard_map/ppermute | solution.py:600
  49.0 13.2 %collective-permute-start.14 = (bf16[512,128]{1,0:T(8,128)(2,1)S(1)}, bf16[512,128]{1,0:T(8,128)(2,1)S(1)}, u32[]{:S(2)}, u32[]{:S(2)}) collective-permute-start(bf16[512,128]{1,0:T(8,128)(2,1)S(1)} %get-tuple-element.98), channel_id=1, source_target_pairs={{0,13},{8,5},{9,4},{4,1},{5,0},{12,9},{13,8},{1,12},{2,15},{10,7},... | collective-permute-start | bytes 393224 | tf_op jit(solution)/shard_map/ppermute | solution.py:600
  62.4 2.0 %collective-permute-start.11 = (bf16[512,128]{1,0:T(8,128)(2,1)S(1)}, bf16[512,128]{1,0:T(8,128)(2,1)S(1)}, u32[]{:S(2)}, u32[]{:S(2)}) collective-permute-start(bf16[512,128]{1,0:T(8,128)(2,1)S(1)} %get-tuple-element.92), channel_id=1, source_target_pairs={{0,4},{8,12},{9,13},{4,8},{5,9},{12,0},{13,1},{1,5},{2,6},{10,14},... | collective-permute-start | bytes 393224 | tf_op jit(solution)/shard_map/ppermute | solution.py:600
  64.4 1.8 %collective-permute-start.10 = (bf16[512,128]{1,0:T(8,128)(2,1)S(1)}, bf16[512,128]{1,0:T(8,128)(2,1)S(1)}, u32[]{:S(2)}, u32[]{:S(2)}) collective-permute-start(bf16[512,128]{1,0:T(8,128)(2,1)S(1)} %get-tuple-element.90), channel_id=1, source_target_pairs={{0,9},{8,1},{9,0},{4,13},{5,12},{12,5},{13,4},{1,8},{2,11},{10,3},... | collective-permute-start | bytes 393224 | tf_op jit(solution)/shard_map/ppermute | solution.py:600
  66.2 0.8 collective-permute-start.9
  67.0 14.0 %value_grad.1 = (bf16[2,512,128]{2,1,0:T(8,128)(2,1)S(1)}, bf16[2,512,128]{2,1,0:T(8,128)(2,1)S(1)}, bf16[2,512,128]{2,1,0:T(8,128)(2,1)S(1)}, bf16[2,512,128]{2...) custom-call(s32[4]{0:T(128)S(1)} %pad_add_fusion.refs_0_, ...), custom_call_target="tpu_custom_call" | custom-call | flops 2147483648 | bytes 8163344 | tf_op jit(solution)/shard_map/value_grad/pallas_call | solution.py:583
  81.0 0.8 collective-permute-done.10.refs_5_
  81.7 2.8 %collective-permute-done.9.refs_4_ = bf16[512,128]{1,0:T(8,128)(2,1)S(1)} collective-permute-done((bf16[512,128]{1,0:T(8,128)(2,1)S(1)}, bf16[512,128]{1,0:T(8,128)(2,1)S(1)}, u32[]{:S(2)}, u32[]{:S(2)}) %collective-permute-start.9) | collective-permute-done | bytes 131104 | tf_op jit(solution)/shard_map/ppermute | solution.py:600
  84.6 3.2 %collective-permute-start.17 = (bf16[2,512,128]{2,1,0:T(8,128)(2,1)S(1)}, bf16[2,512,128]{2,1,0:T(8,128)(2,1)S(1)}, u32[]{:S(2)}, u32[]{:S(2)}) collective-permute-start(bf16[2,512,128]{2,1,0:T(8,128)(2,1)S(1)} %get-tuple-element.103), channel_id=1, source_target_pairs={{0,8},{4,12},{8,0},{12,4},{1,9},{5,13},{9,1},{13,5},{2,10},{6,14},... | collective-permute-start | bytes 786440 | tf_op jit(solution)/shard_map/ppermute | solution.py:609
  87.8 0.6 collective-permute-start.18
  88.4 16.6 %query_grad.1 = (bf16[2,544,128]{2,1,0:T(8,128)(2,1)S(1)}, bf16[2,544,128]{2,1,0:T(8,128)(2,1)S(1)}, bf16[2,544,128]{2,1,0:T(8,128)(2,1)S(1)}, bf16[2,544,128]{2,1,0:T(8,128)(2,1)S(1)}) custom-call(s32[4]{0:T(128)S(1)} %pad_add_fusion.refs_0_, s32[8,128]{1,0:T(8,128)S(1)} %get-tuple-element.105.refs_1_, bf16[19456,128]{1,0:T(8,128)(2,1)} %get-tuple-element.106.refs_2_, ...), custom_call_target="tpu_custom_call" | custom-call | flops 3221225472 | bytes 7147536 | tf_op jit(solution)/shard_map/query_grad/pallas_call | solution.py:583
  105.0 1.5 collective-permute-start.20
  106.5 0.7 collective-permute-start.21
  107.2 2.8 %collective-permute-start.22 = (bf16[2,544,128]{2,1,0:T(8,128)(2,1)S(1)}, bf16[2,544,128]{2,1,0:T(8,128)(2,1)S(1)}, u32[]{:S(2)}, u32[]{:S(2)}) collective-permute-start(bf16[2,544,128]{2,1,0:T(8,128)(2,1)S(1)} %get-tuple-element.113), channel_id=1, source_target_pairs={{0,12},{4,0},{8,4},{12,8},{1,13},{5,1},{9,5},{13,9},{2,14},{6,2},{... | collective-permute-start | bytes 835592 | tf_op jit(solution)/shard_map/ppermute | solution.py:609
  110.0 0.6 swap_value.1
  110.7 5.9 %collective-permute-done.20.refs_2_.refs_4_ = bf16[2,544,128]{2,1,0:T(8,128)(2,1)S(1)} collective-permute-done((bf16[2,544,128]{2,1,0:T(8,128)(2,1)S(1)}, bf16[2,544,128]{2,1,0:T(8,128)(2,1)S(1)}, u32[]{:S(2)}, u32[]{:S(2)}) %collective-permute-start.20) | collective-permute-done | bytes 278560 | tf_op jit(solution)/shard_map/ppermute | solution.py:609
  116.6 13.0 %collective-permute-done.21.refs_3_.refs_5_ = bf16[2,544,128]{2,1,0:T(8,128)(2,1)S(1)} collective-permute-done((bf16[2,544,128]{2,1,0:T(8,128)(2,1)S(1)}, bf16[2,544,128]{2,1,0:T(8,128)(2,1)S(1)}, u32[]{:S(2)}, u32[]{:S(2)}) %collective-permute-start.21) | collective-permute-done | bytes 278560 | tf_op jit(solution)/shard_map/ppermute | solution.py:609
  129.6 0.6 swap_query.1
  130.3 2.5 %value_home.1 = (bf16[1024,512]{1,0:T(8,128)(2,1)S(1)}, f32[1024,512]{1,0:T(8,128)S(1)}, bf16[4,128,512]{2,1,0:T(8,128)(2,1)S(1)}, bf16[4,128,512]{2,1,0:T(8,128)(2,1)S(1)}) custom-call(s32[4]{0:T(128)S(1)} %pad_add_fusion.refs_0_, bf16[1024,1024]{1,0:T(8,128)(2,1)S(1)} %get-tuple-element.75.refs_1_, bf16[1024,512]{1,0:T(8,128)(2,1)S(1)} %copy-done.3, ...), custom_call_target="tpu_custom_call" | custom-call | flops 1610612736 | bytes 8912912 | tf_op jit(solution)/shard_map/value_home/pallas_call | solution.py:583
  132.8 2.0 %query_home.1 = (bf16[1024,512]{1,0:T(8,128)(2,1)S(1)}, bf16[1024,512]{1,0:T(8,128)(2,1)S(1)}, f32[64,512]{1,0:T(8,128)}) custom-call(s32[4]{0:T(128)S(1)} %pad_add_fusion.refs_0_, bf16[1024,512]{1,0:T(8,128)(2,1)S(1)} %copy-done, f32[1024,512]{1,0:T(8,128)S(1)} %get-tuple-element.110.refs_2_, ...), custom_call_target="tpu_custom_call" | custom-call | flops 536870912 | bytes 7045136 | tf_op jit(solution)/shard_map/query_home/pallas_call | solution.py:583
  134.9 1.5 collective-permute-start.25
  136.6 1.8 %query_weight.1 = (bf16[4,128,512]{2,1,0:T(8,128)(2,1)S(1)}, bf16[4,128,512]{2,1,0:T(8,128)(2,1)S(1)}) custom-call(s32[4]{0:T(128)S(1)} %pad_add_fusion.refs_0_, bf16[1024,1024]{1,0:T(8,128)(2,1)S(1)} %get-tuple-element.75.refs_1_, bf16[1024,512]{1,0:T(8,128)(2,1)S(1)} %get-tuple-element.114.refs_2_.refs_1_), custom_call_target="tpu_custom_call" | custom-call | flops 1073741824 | bytes 4194320 | tf_op jit(solution)/shard_map/query_weight/pallas_call | solution.py:583
  138.7 0.7 value_subs.1
  139.4 5.6 %collective-permute-start.30 = (bf16[128,512]{1,0:T(8,128)(2,1)S(1)}, bf16[128,512]{1,0:T(8,128)(2,1)S(1)}, u32[]{:S(2)}, u32[]{:S(2)}) collective-permute-start(bf16[128,512]{1,0:T(8,128)(2,1)S(1)} %get-tuple-element.132), channel_id=1, source_target_pairs={{0,4},{4,8},{8,12},{12,0},{1,5},{5,9},{9,13},{13,1},{2,6},{6,10},{... | collective-permute-start | bytes 393224 | tf_op jit(solution)/shard_map/ppermute | solution.py:609
  145.0 2.4 %collective-permute-start.32 = (bf16[128,512]{1,0:T(8,128)(2,1)S(1)}, bf16[128,512]{1,0:T(8,128)(2,1)S(1)}, u32[]{:S(2)}, u32[]{:S(2)}) collective-permute-start(bf16[128,512]{1,0:T(8,128)(2,1)S(1)} %get-tuple-element.134), channel_id=1, source_target_pairs={{0,12},{4,0},{8,4},{12,8},{1,13},{5,1},{9,5},{13,9},{2,14},{6,2},{... | collective-permute-start | bytes 393224 | tf_op jit(solution)/shard_map/ppermute | solution.py:609
  147.4 0.7 query_subs.1
  148.2 0.7 collective-permute-done.30.refs_1_
  148.8 1.9 %collective-permute-start.27 = (bf16[128,512]{1,0:T(8,128)(2,1)S(1)}, bf16[128,512]{1,0:T(8,128)(2,1)S(1)}, u32[]{:S(2)}, u32[]{:S(2)}) collective-permute-start(bf16[128,512]{1,0:T(8,128)(2,1)S(1)} %get-tuple-element.123), channel_id=1, source_target_pairs={{0,8},{4,12},{8,0},{12,4},{1,9},{5,13},{9,1},{13,5},{2,10},{6,14},... | collective-permute-start | bytes 393224 | tf_op jit(solution)/shard_map/ppermute | solution.py:609
  150.7 3.9 %collective-permute-done.31.refs_2_ = bf16[128,512]{1,0:T(8,128)(2,1)S(1)} collective-permute-done((bf16[128,512]{1,0:T(8,128)(2,1)S(1)}, bf16[128,512]{1,0:T(8,128)(2,1)S(1)}, u32[]{:S(2)}, u32[]{:S(2)}) %collective-permute-start.31) | collective-permute-done | bytes 131104 | tf_op jit(solution)/shard_map/ppermute | solution.py:609
  154.6 5.4 %collective-permute-start.28 = (bf16[128,512]{1,0:T(8,128)(2,1)S(1)}, bf16[128,512]{1,0:T(8,128)(2,1)S(1)}, u32[]{:S(2)}, u32[]{:S(2)}) collective-permute-start(bf16[128,512]{1,0:T(8,128)(2,1)S(1)} %get-tuple-element.124), channel_id=1, source_target_pairs={{0,12},{4,0},{8,4},{12,8},{1,13},{5,1},{9,5},{13,9},{2,14},{6,2},{... | collective-permute-start | bytes 393224 | tf_op jit(solution)/shard_map/ppermute | solution.py:609
  160.1 1.8 %input_own.1.refs_2_.refs_4_ = bf16[1024,512]{1,0:T(8,128)(2,1)S(1)} custom-call(s32[4]{0:T(128)S(1)} %pad_add_fusion.refs_0_, bf16[1024,512]{1,0:T(8,128)(2,1)S(1)} %get-tuple-element.114.refs_2_.refs_1_, bf16[1024,512]{1,0:T(8,128)(2,1)S(1)} %get-tuple-element.118.refs_2_, bf16[1024,512]{1,0:T(8,128)(2,1)S(1)} %copy-done, bf16[1024,512]{1,0:T(8,128)(2,1)S(1)} %copy-done.3, ...), custom_call_target="tpu_custom_call" | custom-call | flops 1073741824 | bytes 5242896 | tf_op jit(solution)/shard_map/input_own/pallas_call | solution.py:583
  161.9 0.8 value_sum.1
  162.7 2.3 %input_sum.1 = (bf16[1024,512]{1,0:T(8,128)(2,1)}, bf16[128,512]{1,0:T(8,128)(2,1)S(1)}) custom-call(bf16[1024,1024]{1,0:T(8,128)(2,1)S(1)} %get-tuple-element.74.refs_11_.refs_0_, bf16[128,512]{1,0:T(8,128)(2,1)S(1)} %get-tuple-element.117.refs_5_.refs_1_, bf16[1024,512]{1,0:T(8,128)(2,1)S(1)} %input_own.1.refs_2_.refs_4_, ...), custom_call_target="tpu_custom_call" | custom-call | flops 1073741824 | bytes 5505024 | tf_op jit(solution)/shard_map/input_sum/pallas_call | solution.py:583
  165.1 0.8 query_sum.1
  (48 shorter events, 1.3 us)
Async XLA Ops:
  0.6 24.9 %copy-start = (bf16[1024,512]{1,0:T(8,128)(2,1)S(1)}, bf16[1024,512]{1,0:T(8,128)(2,1)}, u32[]{:S(2)}) copy-start(bf16[1024,512]{1,0:T(8,128)(2,1)} %refs_3_.5) | copy-start | bytes 3145732
  0.6 24.8 %copy-start.1 = (bf16[1024,1024]{1,0:T(8,128)(2,1)S(1)}, bf16[1024,1024]{1,0:T(8,128)(2,1)}, u32[]{:S(2)}) copy-start(bf16[1024,1024]{1,0:T(8,128)(2,1)} %refs_1_.4) | copy-start | bytes 6291460
  0.7 24.8 %copy-start.4 = (s32[1024,1]{0,1:T(1,128)S(1)}, s32[1024,1]{0,1:T(1,128)}, u32[]{:S(2)}) copy-start(s32[1024,1]{0,1:T(1,128)} %param.9) | copy-start | bytes 12292
  4.1 21.4 %copy-start.5 = (s32[1,1024]{1,0:T(1,128)S(1)}, s32[1,1024]{1,0:T(1,128)}, u32[]{:S(2)}) copy-start(s32[1,1024]{1,0:T(1,128)} %get-tuple-element.70.refs_1_.refs_0_) | copy-start | bytes 12292
  4.1 20.1 %collective-permute-start = (bf16[528,128]{1,0:T(8,128)(2,1)}, bf16[528,128]{1,0:T(8,128)(2,1)S(1)}, u32[]{:S(2)}, u32[]{:S(2)}) collective-permute-start(bf16[528,128]{1,0:T(8,128)(2,1)} %get-tuple-element.71), channel_id=1, source_target_pairs={{0,8},{8,0},{9,1},{4,12},{5,13},{12,4},{13,5},{1,9},{2,10},{10,2},... | collective-permute-start | bytes 405512 | tf_op jit(solution)/shard_map/ppermute | solution.py:600
  8.2 17.3 %collective-permute-start.1 = (bf16[528,128]{1,0:T(8,128)(2,1)}, bf16[528,128]{1,0:T(8,128)(2,1)S(1)}, u32[]{:S(2)}, u32[]{:S(2)}) collective-permute-start(bf16[528,128]{1,0:T(8,128)(2,1)} %get-tuple-element.72), channel_id=1, source_target_pairs={{0,9},{8,1},{9,0},{4,13},{5,12},{12,5},{13,4},{1,8},{2,11},{10,3},... | collective-permute-start | bytes 405512 | tf_op jit(solution)/shard_map/ppermute | solution.py:600
  12.7 23.9 %collective-permute-start.7 = (bf16[512,128]{1,0:T(8,128)(2,1)}, bf16[512,128]{1,0:T(8,128)(2,1)S(1)}, u32[]{:S(2)}, u32[]{:S(2)}) collective-permute-start(bf16[512,128]{1,0:T(8,128)(2,1)} %get-tuple-element.81), channel_id=1, source_target_pairs={{0,8},{8,0},{9,1},{4,12},{5,13},{12,4},{13,5},{1,9},{2,10},{10,2},... | collective-permute-start | bytes 393224 | tf_op jit(solution)/shard_map/ppermute | solution.py:600
  14.8 22.6 %collective-permute-start.8 = (bf16[512,128]{1,0:T(8,128)(2,1)}, bf16[512,128]{1,0:T(8,128)(2,1)}, u32[]{:S(2)}, u32[]{:S(2)}) collective-permute-start(bf16[512,128]{1,0:T(8,128)(2,1)} %get-tuple-element.82), channel_id=1, source_target_pairs={{0,9},{8,1},{9,0},{4,13},{5,12},{12,5},{13,4},{1,8},{2,11},{10,3},... | collective-permute-start | bytes 393224 | tf_op jit(solution)/shard_map/ppermute | solution.py:600
  25.5 1.2 copy-start.2
  26.7 11.7 %copy-start.3 = (bf16[1024,512]{1,0:T(8,128)(2,1)S(1)}, bf16[1024,512]{1,0:T(8,128)(2,1)}, u32[]{:S(2)}) copy-start(bf16[1024,512]{1,0:T(8,128)(2,1)} %refs_4_.3) | copy-start | bytes 3145732
  31.6 12.9 %collective-permute-start.2 = (bf16[1040,128]{1,0:T(8,128)(2,1)S(1)}, bf16[1040,128]{1,0:T(8,128)(2,1)S(1)}, u32[]{:S(2)}, u32[]{:S(2)}) collective-permute-start(bf16[1040,128]{1,0:T(8,128)(2,1)S(1)} %get-tuple-element.76), channel_id=1, source_target_pairs={{0,4},{8,12},{9,13},{4,8},{5,9},{12,0},{13,1},{1,5},{2,6},{10,14},... | collective-permute-start | bytes 798728 | tf_op jit(solution)/shard_map/ppermute | solution.py:600
  33.4 15.6 %collective-permute-start.3 = (bf16[1040,128]{1,0:T(8,128)(2,1)S(1)}, bf16[1040,128]{1,0:T(8,128)(2,1)S(1)}, u32[]{:S(2)}, u32[]{:S(2)}) collective-permute-start(bf16[1040,128]{1,0:T(8,128)(2,1)S(1)} %get-tuple-element.77), channel_id=1, source_target_pairs={{0,5},{8,13},{9,12},{4,9},{5,8},{12,1},{13,0},{1,4},{2,7},{10,15},... | collective-permute-start | bytes 798728 | tf_op jit(solution)/shard_map/ppermute | solution.py:600
  33.4 28.9 %collective-permute-start.4 = (bf16[1040,128]{1,0:T(8,128)(2,1)S(1)}, bf16[1040,128]{1,0:T(8,128)(2,1)S(1)}, u32[]{:S(2)}, u32[]{:S(2)}) collective-permute-start(bf16[1040,128]{1,0:T(8,128)(2,1)S(1)} %get-tuple-element.78), channel_id=1, source_target_pairs={{0,12},{8,4},{9,5},{4,0},{5,1},{12,8},{13,9},{1,13},{2,14},{10,6},... | collective-permute-start | bytes 798728 | tf_op jit(solution)/shard_map/ppermute | solution.py:600
  36.6 25.6 %collective-permute-start.5 = (bf16[1040,128]{1,0:T(8,128)(2,1)S(1)}, bf16[1040,128]{1,0:T(8,128)(2,1)S(1)}, u32[]{:S(2)}, u32[]{:S(2)}) collective-permute-start(bf16[1040,128]{1,0:T(8,128)(2,1)S(1)} %get-tuple-element.79), channel_id=1, source_target_pairs={{0,13},{8,5},{9,4},{4,1},{5,0},{12,9},{13,8},{1,12},{2,15},{10,7},... | collective-permute-start | bytes 798728 | tf_op jit(solution)/shard_map/ppermute | solution.py:600
  37.4 24.8 %collective-permute-start.6 = (bf16[1040,128]{1,0:T(8,128)(2,1)S(1)}, bf16[1040,128]{1,0:T(8,128)(2,1)S(1)}, u32[]{:S(2)}, u32[]{:S(2)}) collective-permute-start(bf16[1040,128]{1,0:T(8,128)(2,1)S(1)} %get-tuple-element.80), channel_id=1, source_target_pairs={{0,1},{8,9},{9,8},{4,5},{5,4},{12,13},{13,12},{1,0},{2,3},{10,11},... | collective-permute-start | bytes 798728 | tf_op jit(solution)/shard_map/ppermute | solution.py:600
  44.4 19.9 %collective-permute-start.15 = (bf16[512,128]{1,0:T(8,128)(2,1)S(1)}, bf16[512,128]{1,0:T(8,128)(2,1)S(1)}, u32[]{:S(2)}, u32[]{:S(2)}) collective-permute-start(bf16[512,128]{1,0:T(8,128)(2,1)S(1)} %get-tuple-element.100), channel_id=1, source_target_pairs={{0,1},{8,9},{9,8},{4,5},{5,4},{12,13},{13,12},{1,0},{2,3},{10,11},... | collective-permute-start | bytes 393224 | tf_op jit(solution)/shard_map/ppermute | solution.py:600
  49.0 17.2 %collective-permute-start.14 = (bf16[512,128]{1,0:T(8,128)(2,1)S(1)}, bf16[512,128]{1,0:T(8,128)(2,1)S(1)}, u32[]{:S(2)}, u32[]{:S(2)}) collective-permute-start(bf16[512,128]{1,0:T(8,128)(2,1)S(1)} %get-tuple-element.98), channel_id=1, source_target_pairs={{0,13},{8,5},{9,4},{4,1},{5,0},{12,9},{13,8},{1,12},{2,15},{10,7},... | collective-permute-start | bytes 393224 | tf_op jit(solution)/shard_map/ppermute | solution.py:600
  62.3 18.7 %collective-permute-start.13 = (bf16[512,128]{1,0:T(8,128)(2,1)S(1)}, bf16[512,128]{1,0:T(8,128)(2,1)S(1)}, u32[]{:S(2)}, u32[]{:S(2)}) collective-permute-start(bf16[512,128]{1,0:T(8,128)(2,1)S(1)} %get-tuple-element.96), channel_id=1, source_target_pairs={{0,12},{8,4},{9,5},{4,0},{5,1},{12,8},{13,9},{1,13},{2,14},{10,6},... | collective-permute-start | bytes 393224 | tf_op jit(solution)/shard_map/ppermute | solution.py:600
  62.3 18.6 %collective-permute-start.12 = (bf16[512,128]{1,0:T(8,128)(2,1)S(1)}, bf16[512,128]{1,0:T(8,128)(2,1)S(1)}, u32[]{:S(2)}, u32[]{:S(2)}) collective-permute-start(bf16[512,128]{1,0:T(8,128)(2,1)S(1)} %get-tuple-element.94), channel_id=1, source_target_pairs={{0,5},{8,13},{9,12},{4,9},{5,8},{12,1},{13,0},{1,4},{2,7},{10,15},... | collective-permute-start | bytes 393224 | tf_op jit(solution)/shard_map/ppermute | solution.py:600
  62.4 18.6 %collective-permute-start.11 = (bf16[512,128]{1,0:T(8,128)(2,1)S(1)}, bf16[512,128]{1,0:T(8,128)(2,1)S(1)}, u32[]{:S(2)}, u32[]{:S(2)}) collective-permute-start(bf16[512,128]{1,0:T(8,128)(2,1)S(1)} %get-tuple-element.92), channel_id=1, source_target_pairs={{0,4},{8,12},{9,13},{4,8},{5,9},{12,0},{13,1},{1,5},{2,6},{10,14},... | collective-permute-start | bytes 393224 | tf_op jit(solution)/shard_map/ppermute | solution.py:600
  64.4 17.4 %collective-permute-start.10 = (bf16[512,128]{1,0:T(8,128)(2,1)S(1)}, bf16[512,128]{1,0:T(8,128)(2,1)S(1)}, u32[]{:S(2)}, u32[]{:S(2)}) collective-permute-start(bf16[512,128]{1,0:T(8,128)(2,1)S(1)} %get-tuple-element.90), channel_id=1, source_target_pairs={{0,9},{8,1},{9,0},{4,13},{5,12},{12,5},{13,4},{1,8},{2,11},{10,3},... | collective-permute-start | bytes 393224 | tf_op jit(solution)/shard_map/ppermute | solution.py:600
  66.2 18.3 %collective-permute-start.9 = (bf16[512,128]{1,0:T(8,128)(2,1)S(1)}, bf16[512,128]{1,0:T(8,128)(2,1)S(1)}, u32[]{:S(2)}, u32[]{:S(2)}) collective-permute-start(bf16[512,128]{1,0:T(8,128)(2,1)S(1)} %get-tuple-element.88), channel_id=1, source_target_pairs={{0,8},{8,0},{9,1},{4,12},{5,13},{12,4},{13,5},{1,9},{2,10},{10,2},... | collective-permute-start | bytes 393224 | tf_op jit(solution)/shard_map/ppermute | solution.py:600
  84.6 22.6 %collective-permute-start.16 = (bf16[2,512,128]{2,1,0:T(8,128)(2,1)S(1)}, bf16[2,512,128]{2,1,0:T(8,128)(2,1)S(1)}, u32[]{:S(2)}, u32[]{:S(2)}) collective-permute-start(bf16[2,512,128]{2,1,0:T(8,128)(2,1)S(1)} %get-tuple-element.102), channel_id=1, source_target_pairs={{0,4},{4,8},{8,12},{12,0},{1,5},{5,9},{9,13},{13,1},{2,6},{6,10},{... | collective-permute-start | bytes 786440 | tf_op jit(solution)/shard_map/ppermute | solution.py:609
  84.6 25.5 %collective-permute-start.17 = (bf16[2,512,128]{2,1,0:T(8,128)(2,1)S(1)}, bf16[2,512,128]{2,1,0:T(8,128)(2,1)S(1)}, u32[]{:S(2)}, u32[]{:S(2)}) collective-permute-start(bf16[2,512,128]{2,1,0:T(8,128)(2,1)S(1)} %get-tuple-element.103), channel_id=1, source_target_pairs={{0,8},{4,12},{8,0},{12,4},{1,9},{5,13},{9,1},{13,5},{2,10},{6,14},... | collective-permute-start | bytes 786440 | tf_op jit(solution)/shard_map/ppermute | solution.py:609
  87.8 22.3 %collective-permute-start.18 = (bf16[2,512,128]{2,1,0:T(8,128)(2,1)S(1)}, bf16[2,512,128]{2,1,0:T(8,128)(2,1)S(1)}, u32[]{:S(2)}, u32[]{:S(2)}) collective-permute-start(bf16[2,512,128]{2,1,0:T(8,128)(2,1)S(1)} %get-tuple-element.104), channel_id=1, source_target_pairs={{0,12},{4,0},{8,4},{12,8},{1,13},{5,1},{9,5},{13,9},{2,14},{6,2},{... | collective-permute-start | bytes 786440 | tf_op jit(solution)/shard_map/ppermute | solution.py:609
  105.0 11.5 %collective-permute-start.20 = (bf16[2,544,128]{2,1,0:T(8,128)(2,1)S(1)}, bf16[2,544,128]{2,1,0:T(8,128)(2,1)S(1)}, u32[]{:S(2)}, u32[]{:S(2)}) collective-permute-start(bf16[2,544,128]{2,1,0:T(8,128)(2,1)S(1)} %get-tuple-element.111), channel_id=1, source_target_pairs={{0,4},{4,8},{8,12},{12,0},{1,5},{5,9},{9,13},{13,1},{2,6},{6,10},{... | collective-permute-start | bytes 835592 | tf_op jit(solution)/shard_map/ppermute | solution.py:609
  106.5 23.1 %collective-permute-start.21 = (bf16[2,544,128]{2,1,0:T(8,128)(2,1)S(1)}, bf16[2,544,128]{2,1,0:T(8,128)(2,1)S(1)}, u32[]{:S(2)}, u32[]{:S(2)}) collective-permute-start(bf16[2,544,128]{2,1,0:T(8,128)(2,1)S(1)} %get-tuple-element.112), channel_id=1, source_target_pairs={{0,8},{4,12},{8,0},{12,4},{1,9},{5,13},{9,1},{13,5},{2,10},{6,14},... | collective-permute-start | bytes 835592 | tf_op jit(solution)/shard_map/ppermute | solution.py:609
  107.2 22.4 %collective-permute-start.22 = (bf16[2,544,128]{2,1,0:T(8,128)(2,1)S(1)}, bf16[2,544,128]{2,1,0:T(8,128)(2,1)S(1)}, u32[]{:S(2)}, u32[]{:S(2)}) collective-permute-start(bf16[2,544,128]{2,1,0:T(8,128)(2,1)S(1)} %get-tuple-element.113), channel_id=1, source_target_pairs={{0,12},{4,0},{8,4},{12,8},{1,13},{5,1},{9,5},{13,9},{2,14},{6,2},{... | collective-permute-start | bytes 835592 | tf_op jit(solution)/shard_map/ppermute | solution.py:609
  110.6 19.6 %collective-permute-start.19 = (bf16[4,512,128]{2,1,0:T(8,128)(2,1)S(1)}, bf16[4,512,128]{2,1,0:T(8,128)(2,1)S(1)}, u32[]{:S(2)}, u32[]{:S(2)}) collective-permute-start(bf16[4,512,128]{2,1,0:T(8,128)(2,1)S(1)} %swap_value.1), channel_id=1, source_target_pairs={{0,1},{1,0},{2,3},{3,2},{4,5},{5,4},{6,7},{7,6},{8,9},{9,8},{10,11... | collective-permute-start | bytes 1572872 | tf_op jit(solution)/shard_map/ppermute | solution.py:609
  130.2 2.6 %collective-permute-start.23 = (bf16[4,544,128]{2,1,0:T(8,128)(2,1)S(1)}, bf16[4,544,128]{2,1,0:T(8,128)(2,1)S(1)}, u32[]{:S(2)}, u32[]{:S(2)}) collective-permute-start(bf16[4,544,128]{2,1,0:T(8,128)(2,1)S(1)} %swap_query.1), channel_id=1, source_target_pairs={{0,1},{1,0},{2,3},{3,2},{4,5},{5,4},{6,7},{7,6},{8,9},{9,8},{10,11... | collective-permute-start | bytes 1671176 | tf_op jit(solution)/shard_map/ppermute | solution.py:609
  134.9 27.8 %collective-permute-start.25 = (bf16[1024,512]{1,0:T(8,128)(2,1)S(1)}, bf16[1024,512]{1,0:T(8,128)(2,1)S(1)}, u32[]{:S(2)}, u32[]{:S(2)}) collective-permute-start(bf16[1024,512]{1,0:T(8,128)(2,1)S(1)} %get-tuple-element.119), channel_id=1, source_target_pairs={{0,2},{2,0},{1,3},{3,1},{4,6},{6,4},{5,7},{7,5},{8,10},{10,8},{9,1... | collective-permute-start | bytes 3145736 | tf_op jit(solution)/shard_map/ppermute | solution.py:609
  136.3 2.4 %collective-permute-start.29 = (bf16[4,128,512]{2,1,0:T(8,128)(2,1)S(1)}, bf16[4,128,512]{2,1,0:T(8,128)(2,1)S(1)}, u32[]{:S(2)}, u32[]{:S(2)}) collective-permute-start(bf16[4,128,512]{2,1,0:T(8,128)(2,1)S(1)} %get-tuple-element.126), channel_id=1, source_target_pairs={{0,1},{1,0},{2,3},{3,2},{4,5},{5,4},{6,7},{7,6},{8,9},{9,8},{10,11... | collective-permute-start | bytes 1572872 | tf_op jit(solution)/shard_map/ppermute | solution.py:609
  138.3 9.1 %collective-permute-start.24 = (bf16[4,128,512]{2,1,0:T(8,128)(2,1)S(1)}, bf16[4,128,512]{2,1,0:T(8,128)(2,1)S(1)}, u32[]{:S(2)}, u32[]{:S(2)}) collective-permute-start(bf16[4,128,512]{2,1,0:T(8,128)(2,1)S(1)} %get-tuple-element.116), channel_id=1, source_target_pairs={{0,1},{1,0},{2,3},{3,2},{4,5},{5,4},{6,7},{7,6},{8,9},{9,8},{10,11... | collective-permute-start | bytes 1572872 | tf_op jit(solution)/shard_map/ppermute | solution.py:609
  139.4 9.4 %collective-permute-start.30 = (bf16[128,512]{1,0:T(8,128)(2,1)S(1)}, bf16[128,512]{1,0:T(8,128)(2,1)S(1)}, u32[]{:S(2)}, u32[]{:S(2)}) collective-permute-start(bf16[128,512]{1,0:T(8,128)(2,1)S(1)} %get-tuple-element.132), channel_id=1, source_target_pairs={{0,4},{4,8},{8,12},{12,0},{1,5},{5,9},{9,13},{13,1},{2,6},{6,10},{... | collective-permute-start | bytes 393224 | tf_op jit(solution)/shard_map/ppermute | solution.py:609
  145.0 9.7 %collective-permute-start.31 = (bf16[128,512]{1,0:T(8,128)(2,1)S(1)}, bf16[128,512]{1,0:T(8,128)(2,1)S(1)}, u32[]{:S(2)}, u32[]{:S(2)}) collective-permute-start(bf16[128,512]{1,0:T(8,128)(2,1)S(1)} %get-tuple-element.133), channel_id=1, source_target_pairs={{0,8},{4,12},{8,0},{12,4},{1,9},{5,13},{9,1},{13,5},{2,10},{6,14},... | collective-permute-start | bytes 393224 | tf_op jit(solution)/shard_map/ppermute | solution.py:609
  145.0 16.9 %collective-permute-start.32 = (bf16[128,512]{1,0:T(8,128)(2,1)S(1)}, bf16[128,512]{1,0:T(8,128)(2,1)S(1)}, u32[]{:S(2)}, u32[]{:S(2)}) collective-permute-start(bf16[128,512]{1,0:T(8,128)(2,1)S(1)} %get-tuple-element.134), channel_id=1, source_target_pairs={{0,12},{4,0},{8,4},{12,8},{1,13},{5,1},{9,5},{13,9},{2,14},{6,2},{... | collective-permute-start | bytes 393224 | tf_op jit(solution)/shard_map/ppermute | solution.py:609
  148.1 16.9 %collective-permute-start.26 = (bf16[128,512]{1,0:T(8,128)(2,1)S(1)}, bf16[128,512]{1,0:T(8,128)(2,1)S(1)}, u32[]{:S(2)}, u32[]{:S(2)}) collective-permute-start(bf16[128,512]{1,0:T(8,128)(2,1)S(1)} %get-tuple-element.122), channel_id=1, source_target_pairs={{0,4},{4,8},{8,12},{12,0},{1,5},{5,9},{9,13},{13,1},{2,6},{6,10},{... | collective-permute-start | bytes 393224 | tf_op jit(solution)/shard_map/ppermute | solution.py:609
  148.8 16.3 %collective-permute-start.27 = (bf16[128,512]{1,0:T(8,128)(2,1)S(1)}, bf16[128,512]{1,0:T(8,128)(2,1)S(1)}, u32[]{:S(2)}, u32[]{:S(2)}) collective-permute-start(bf16[128,512]{1,0:T(8,128)(2,1)S(1)} %get-tuple-element.123), channel_id=1, source_target_pairs={{0,8},{4,12},{8,0},{12,4},{1,9},{5,13},{9,1},{13,5},{2,10},{6,14},... | collective-permute-start | bytes 393224 | tf_op jit(solution)/shard_map/ppermute | solution.py:609
  154.6 10.5 %collective-permute-start.28 = (bf16[128,512]{1,0:T(8,128)(2,1)S(1)}, bf16[128,512]{1,0:T(8,128)(2,1)S(1)}, u32[]{:S(2)}, u32[]{:S(2)}) collective-permute-start(bf16[128,512]{1,0:T(8,128)(2,1)S(1)} %get-tuple-element.124), channel_id=1, source_target_pairs={{0,12},{4,0},{8,4},{12,8},{1,13},{5,1},{9,5},{13,9},{2,14},{6,2},{... | collective-permute-start | bytes 393224 | tf_op jit(solution)/shard_map/ppermute | solution.py:609

commit v21 on v20

--- a/solution.py
+++ b/solution.py
@@ -698,12 +698,13 @@
     )
     steps = steps_of(sizes)
     far_cotan = [send(part, ahead, sizes) for ahead, part in zip(steps[1:], far_cotan)]
+    raw_query = far_query
     far_query = [send(part, ahead, sizes) for ahead, part in zip(steps[1:], far_query)]
     own_mixed, *near_mixed = call(
         functools.partial(project_query_kernel, sizes, groups, rows),
         several(owners - sizes[1], rows + COUNT_ROWS, LANES),
         (me, slot_row, assign_row, tokens_in, w_query, cotangent),
-        after=far_cotan,
+        after=raw_query[:1],
         scratch=[pltpu.VMEM((toks, 2 * width_dev), BF16), pltpu.VMEM((owners, rows + COUNT_ROWS, LANES), BF16)],
         flops=2 * toks * width * width_dev + 4 * slots * toks * width_dev,
         name="project_query",
@@ -714,7 +715,7 @@
         functools.partial(project_value_kernel, sizes, groups, rows),
         several(owners, half, LANES) + several(1, width, slots) + several(1, toks, slots),
         (me, slot_row, tokens_in, w_value),
-        after=[own_mixed],
+        after=[own_mixed, *far_cotan],
         scratch=[pltpu.VMEM((toks, width_dev), BF16), pltpu.VMEM((owners, half, LANES), BF16)],
         flops=2 * toks * width * width_dev + 2 * slots * toks * width_dev,
         name="project_value",

time: 167 us -> 165 us (0.988)
  starting transfers between devices: 58.2 us -> 56.1 us
    ppermute x16, starting transfers between devices: 31.8 us -> 27.8 us  [send(): return part if ahead == (0, 0) else lax.ppermute(part, OWNERS, moves)]
    ppermute x17, starting transfers between devices: 26.4 us -> 28.3 us  [shift(): lax.ppermute(part, axis, [(i, (i + ahead) % size) for i in range(size)])]
  transfers between devices with their start and end apart: 33 -> 33, of which waited for: 10 -> 9; matrix products, arithmetic and copies ran while one was open for 0% -> 0% of each run, Pallas kernels for 35% -> 34%
where the time goes in v21:
time: 165 us; the launch traced here: 164 us
  Pallas kernels  62.8 us (38%)
  starting transfers between devices  56.1 us (34%)
  waiting for transfers between devices  42.1 us (26%)
  local copies, waits for them, and re-layouts  2.15 us (1%)
    pallas_call x17, Pallas kernels, call(): pl.pallas_call(body, out_shape=outs, in_specs=specs, out_specs=jax.tree.m...  62.8 us
    ppermute x17, starting transfers between devices, shift(): lax.ppermute(part, axis, [(i, (i + ahead) % size) for i in range(size)])  28.3 us
    ppermute x16, starting transfers between devices, send(): return part if ahead == (0, 0) else lax.ppermute(part, OWNERS, moves)  27.8 us
    ppermute x17, waiting for transfers between devices, shift(): lax.ppermute(part, axis, [(i, (i + ahead) % size) for i in range(size)])  24.5 us
    ppermute x16, waiting for transfers between devices, send(): return part if ahead == (0, 0) else lax.ppermute(part, OWNERS, moves)  17.7 us
  transfers between devices with their start and end apart: 33, of which 9 were waited for; matrix products, arithmetic and copies ran while one was open for 0% of the time, Pallas kernels for 34%

profile of v21, /device:TPU:0, one launch (start us, length us, event | category | flops | bytes accessed | tf_op | source)
XLA Modules:
  0.0 164.1 jit_solution(8200704571515653311)
XLA Ops:
  0.7 3.4 %cotan_far.1 = (bf16[528,128]{1,0:T(8,128)(2,1)}, bf16[528,128]{1,0:T(8,128)(2,1)}, s32[1,1024]{1,0:T(1,128)}) custom-call(s32[1,1024]{1,0:T(1,128)} %bitcast.5, bf16[1024,512]{1,0:T(8,128)(2,1)} %refs_5_.1), custom_call_target="tpu_custom_call" | custom-call | flops 268435456 | bytes 1327104 | tf_op jit(solution)/shard_map/cotan_far/pallas_call | solution.py:583
  4.1 4.1 %collective-permute-start = (bf16[528,128]{1,0:T(8,128)(2,1)}, bf16[528,128]{1,0:T(8,128)(2,1)S(1)}, u32[]{:S(2)}, u32[]{:S(2)}) collective-permute-start(bf16[528,128]{1,0:T(8,128)(2,1)} %get-tuple-element.73), channel_id=1, source_target_pairs={{0,8},{8,0},{9,1},{4,12},{5,13},{12,4},{13,5},{1,9},{2,10},{10,2},... | collective-permute-start | bytes 405512 | tf_op jit(solution)/shard_map/ppermute | solution.py:600
  8.2 4.4 %query_far.1 = (bf16[512,128]{1,0:T(8,128)(2,1)}, bf16[512,128]{1,0:T(8,128)(2,1)}) custom-call(s32[1,1024]{1,0:T(1,128)} %get-tuple-element.70.refs_0_.refs_1_, bf16[1024,1024]{1,0:T(8,128)(2,1)} %refs_2_.4, bf16[1024,512]{1,0:T(8,128)(2,1)} %refs_3_.5), custom_call_target="tpu_custom_call" | custom-call | flops 536870912 | bytes 3411968 | tf_op jit(solution)/shard_map/query_far/pallas_call | solution.py:583
  12.7 2.7 %collective-permute-start.8 = (bf16[512,128]{1,0:T(8,128)(2,1)}, bf16[512,128]{1,0:T(8,128)(2,1)S(1)}, u32[]{:S(2)}, u32[]{:S(2)}) collective-permute-start(bf16[512,128]{1,0:T(8,128)(2,1)} %get-tuple-element.82), channel_id=1, source_target_pairs={{0,9},{8,1},{9,0},{4,13},{5,12},{12,5},{13,4},{1,8},{2,11},{10,3},... | collective-permute-start | bytes 393224 | tf_op jit(solution)/shard_map/ppermute | solution.py:600
  15.6 1.2 copy-done.2
  16.8 0.9 copy-done.6
  17.7 4.8 %project_query.1 = (bf16[1040,128]{1,0:T(8,128)(2,1)S(1)}, bf16[1040,128]{1,0:T(8,128)(2,1)S(1)}, bf16[1040,128]{1,0:T(8,128)(2,1)S(1)}, bf16[1040,128]{1,0:T(8,...) custom-call(s32[4]{0:T(128)S(1)} %pad_add_fusion.refs_0_, s32[1,1024]{1,0:T(1,128)S(1)} %copy-done.5, ...), custom_call_target="tpu_custom_call" | custom-call | flops 3221225472 | bytes 5799952 | tf_op jit(solution)/shard_map/project_query/pallas_call | solution.py:583
  22.5 1.9 %collective-permute-start.2 = (bf16[1040,128]{1,0:T(8,128)(2,1)S(1)}, bf16[1040,128]{1,0:T(8,128)(2,1)S(1)}, u32[]{:S(2)}, u32[]{:S(2)}) collective-permute-start(bf16[1040,128]{1,0:T(8,128)(2,1)S(1)} %get-tuple-element.77), channel_id=1, source_target_pairs={{0,4},{8,12},{9,13},{4,8},{5,9},{12,0},{13,1},{1,5},{2,6},{10,14},... | collective-permute-start | bytes 798728 | tf_op jit(solution)/shard_map/ppermute | solution.py:600
  24.4 9.6 %collective-permute-done.8.refs_10_ = bf16[512,128]{1,0:T(8,128)(2,1)S(1)} collective-permute-done((bf16[512,128]{1,0:T(8,128)(2,1)}, bf16[512,128]{1,0:T(8,128)(2,1)S(1)}, u32[]{:S(2)}, u32[]{:S(2)}) %collective-permute-start.8) | collective-permute-done | bytes 131104 | tf_op jit(solution)/shard_map/ppermute | solution.py:600
  34.0 3.7 %collective-permute-done.7.refs_9_ = bf16[512,128]{1,0:T(8,128)(2,1)} collective-permute-done((bf16[512,128]{1,0:T(8,128)(2,1)}, bf16[512,128]{1,0:T(8,128)(2,1)}, u32[]{:S(2)}, u32[]{:S(2)}) %collective-permute-start.7) | collective-permute-done | bytes 131104 | tf_op jit(solution)/shard_map/ppermute | solution.py:600
  37.7 1.2 collective-permute-start.4
  39.1 6.0 %project_value.1 = (bf16[512,128]{1,0:T(8,128)(2,1)S(1)}, bf16[512,128]{1,0:T(8,128)(2,1)S(1)}, bf16[512,128]{1,0:T(8,128)(2,1)S(1)}, bf16[512,128]{1,0:T(8,128)...) custom-call(s32[4]{0:T(128)S(1)} %pad_add_fusion.refs_0_, ...), custom_call_target="tpu_custom_call" | custom-call | flops 2147483648 | bytes 8392720 | tf_op jit(solution)/shard_map/project_value/pallas_call | solution.py:583
  45.1 0.5 collective-permute-start.15
  45.6 12.3 %collective-permute-start.14 = (bf16[512,128]{1,0:T(8,128)(2,1)S(1)}, bf16[512,128]{1,0:T(8,128)(2,1)S(1)}, u32[]{:S(2)}, u32[]{:S(2)}) collective-permute-start(bf16[512,128]{1,0:T(8,128)(2,1)S(1)} %get-tuple-element.98), channel_id=1, source_target_pairs={{0,13},{8,5},{9,4},{4,1},{5,0},{12,9},{13,8},{1,12},{2,15},{10,7},... | collective-permute-start | bytes 393224 | tf_op jit(solution)/shard_map/ppermute | solution.py:600
  57.9 0.7 collective-permute-start.13
  58.6 1.2 collective-permute-start.12
  59.8 0.3 collective-permute-start.11
  60.0 2.4 %collective-permute-start.10 = (bf16[512,128]{1,0:T(8,128)(2,1)S(1)}, bf16[512,128]{1,0:T(8,128)(2,1)S(1)}, u32[]{:S(2)}, u32[]{:S(2)}) collective-permute-start(bf16[512,128]{1,0:T(8,128)(2,1)S(1)} %get-tuple-element.90), channel_id=1, source_target_pairs={{0,9},{8,1},{9,0},{4,13},{5,12},{12,5},{13,4},{1,8},{2,11},{10,3},... | collective-permute-start | bytes 393224 | tf_op jit(solution)/shard_map/ppermute | solution.py:600
  62.4 0.4 collective-permute-start.9
  62.8 13.6 %value_grad.1 = (bf16[2,512,128]{2,1,0:T(8,128)(2,1)S(1)}, bf16[2,512,128]{2,1,0:T(8,128)(2,1)S(1)}, bf16[2,512,128]{2,1,0:T(8,128)(2,1)S(1)}, bf16[2,512,128]{2...) custom-call(s32[4]{0:T(128)S(1)} %pad_add_fusion.refs_0_, ...), custom_call_target="tpu_custom_call" | custom-call | flops 2147483648 | bytes 8163344 | tf_op jit(solution)/shard_map/value_grad/pallas_call | solution.py:583
  76.5 1.2 collective-permute-done.10.refs_5_
  77.7 3.1 %collective-permute-done.9.refs_4_ = bf16[512,128]{1,0:T(8,128)(2,1)S(1)} collective-permute-done((bf16[512,128]{1,0:T(8,128)(2,1)S(1)}, bf16[512,128]{1,0:T(8,128)(2,1)S(1)}, u32[]{:S(2)}, u32[]{:S(2)}) %collective-permute-start.9) | collective-permute-done | bytes 131104 | tf_op jit(solution)/shard_map/ppermute | solution.py:600
  80.8 1.9 %collective-permute-start.16 = (bf16[2,512,128]{2,1,0:T(8,128)(2,1)S(1)}, bf16[2,512,128]{2,1,0:T(8,128)(2,1)S(1)}, u32[]{:S(2)}, u32[]{:S(2)}) collective-permute-start(bf16[2,512,128]{2,1,0:T(8,128)(2,1)S(1)} %get-tuple-element.102), channel_id=1, source_target_pairs={{0,4},{4,8},{8,12},{12,0},{1,5},{5,9},{9,13},{13,1},{2,6},{6,10},{... | collective-permute-start | bytes 786440 | tf_op jit(solution)/shard_map/ppermute | solution.py:609
  82.7 3.4 %collective-permute-start.17 = (bf16[2,512,128]{2,1,0:T(8,128)(2,1)S(1)}, bf16[2,512,128]{2,1,0:T(8,128)(2,1)S(1)}, u32[]{:S(2)}, u32[]{:S(2)}) collective-permute-start(bf16[2,512,128]{2,1,0:T(8,128)(2,1)S(1)} %get-tuple-element.103), channel_id=1, source_target_pairs={{0,8},{4,12},{8,0},{12,4},{1,9},{5,13},{9,1},{13,5},{2,10},{6,14},... | collective-permute-start | bytes 786440 | tf_op jit(solution)/shard_map/ppermute | solution.py:609
  86.0 16.0 %query_grad.1 = (bf16[2,544,128]{2,1,0:T(8,128)(2,1)S(1)}, bf16[2,544,128]{2,1,0:T(8,128)(2,1)S(1)}, bf16[2,544,128]{2,1,0:T(8,128)(2,1)S(1)}, bf16[2,544,128]{2,1,0:T(8,128)(2,1)S(1)}) custom-call(s32[4]{0:T(128)S(1)} %pad_add_fusion.refs_0_, s32[8,128]{1,0:T(8,128)S(1)} %get-tuple-element.105.refs_1_, bf16[19456,128]{1,0:T(8,128)(2,1)} %get-tuple-element.106.refs_2_, ...), custom_call_target="tpu_custom_call" | custom-call | flops 3221225472 | bytes 7147536 | tf_op jit(solution)/shard_map/query_grad/pallas_call | solution.py:583
  102.0 2.1 %collective-permute-start.20 = (bf16[2,544,128]{2,1,0:T(8,128)(2,1)S(1)}, bf16[2,544,128]{2,1,0:T(8,128)(2,1)S(1)}, u32[]{:S(2)}, u32[]{:S(2)}) collective-permute-start(bf16[2,544,128]{2,1,0:T(8,128)(2,1)S(1)} %get-tuple-element.111), channel_id=1, source_target_pairs={{0,4},{4,8},{8,12},{12,0},{1,5},{5,9},{9,13},{13,1},{2,6},{6,10},{... | collective-permute-start | bytes 835592 | tf_op jit(solution)/shard_map/ppermute | solution.py:609
  104.1 2.4 %collective-permute-start.22 = (bf16[2,544,128]{2,1,0:T(8,128)(2,1)S(1)}, bf16[2,544,128]{2,1,0:T(8,128)(2,1)S(1)}, u32[]{:S(2)}, u32[]{:S(2)}) collective-permute-start(bf16[2,544,128]{2,1,0:T(8,128)(2,1)S(1)} %get-tuple-element.113), channel_id=1, source_target_pairs={{0,12},{4,0},{8,4},{12,8},{1,13},{5,1},{9,5},{13,9},{2,14},{6,2},{... | collective-permute-start | bytes 835592 | tf_op jit(solution)/shard_map/ppermute | solution.py:609
  106.5 0.6 swap_value.1
  107.2 6.3 %collective-permute-done.20.refs_2_.refs_4_ = bf16[2,544,128]{2,1,0:T(8,128)(2,1)S(1)} collective-permute-done((bf16[2,544,128]{2,1,0:T(8,128)(2,1)S(1)}, bf16[2,544,128]{2,1,0:T(8,128)(2,1)S(1)}, u32[]{:S(2)}, u32[]{:S(2)}) %collective-permute-start.20) | collective-permute-done | bytes 278560 | tf_op jit(solution)/shard_map/ppermute | solution.py:609
  113.5 13.4 %collective-permute-done.21.refs_3_.refs_5_ = bf16[2,544,128]{2,1,0:T(8,128)(2,1)S(1)} collective-permute-done((bf16[2,544,128]{2,1,0:T(8,128)(2,1)S(1)}, bf16[2,544,128]{2,1,0:T(8,128)(2,1)S(1)}, u32[]{:S(2)}, u32[]{:S(2)}) %collective-permute-start.21) | collective-permute-done | bytes 278560 | tf_op jit(solution)/shard_map/ppermute | solution.py:609
  126.9 0.6 swap_query.1
  127.6 2.5 %value_home.1 = (bf16[1024,512]{1,0:T(8,128)(2,1)S(1)}, f32[1024,512]{1,0:T(8,128)S(1)}, bf16[4,128,512]{2,1,0:T(8,128)(2,1)S(1)}, bf16[4,128,512]{2,1,0:T(8,128)(2,1)S(1)}) custom-call(s32[4]{0:T(128)S(1)} %pad_add_fusion.refs_0_, bf16[1024,1024]{1,0:T(8,128)(2,1)S(1)} %get-tuple-element.76.refs_1_, bf16[1024,512]{1,0:T(8,128)(2,1)S(1)} %copy-done.3, ...), custom_call_target="tpu_custom_call" | custom-call | flops 1610612736 | bytes 8912912 | tf_op jit(solution)/shard_map/value_home/pallas_call | solution.py:583
  130.1 2.1 %query_home.1 = (bf16[1024,512]{1,0:T(8,128)(2,1)S(1)}, bf16[1024,512]{1,0:T(8,128)(2,1)S(1)}, f32[64,512]{1,0:T(8,128)}) custom-call(s32[4]{0:T(128)S(1)} %pad_add_fusion.refs_0_, bf16[1024,512]{1,0:T(8,128)(2,1)S(1)} %copy-done, f32[1024,512]{1,0:T(8,128)S(1)} %get-tuple-element.110.refs_2_, ...), custom_call_target="tpu_custom_call" | custom-call | flops 536870912 | bytes 7045136 | tf_op jit(solution)/shard_map/query_home/pallas_call | solution.py:583
  132.1 1.5 collective-permute-start.25
  133.8 1.8 %query_weight.1 = (bf16[4,128,512]{2,1,0:T(8,128)(2,1)S(1)}, bf16[4,128,512]{2,1,0:T(8,128)(2,1)S(1)}) custom-call(s32[4]{0:T(128)S(1)} %pad_add_fusion.refs_0_, bf16[1024,1024]{1,0:T(8,128)(2,1)S(1)} %get-tuple-element.76.refs_1_, bf16[1024,512]{1,0:T(8,128)(2,1)S(1)} %get-tuple-element.114.refs_2_.refs_1_), custom_call_target="tpu_custom_call" | custom-call | flops 1073741824 | bytes 4194320 | tf_op jit(solution)/shard_map/query_weight/pallas_call | solution.py:583
  135.6 0.4 collective-permute-start.24
  136.0 0.7 value_subs.1
  136.7 6.5 %collective-permute-start.30 = (bf16[128,512]{1,0:T(8,128)(2,1)S(1)}, bf16[128,512]{1,0:T(8,128)(2,1)S(1)}, u32[]{:S(2)}, u32[]{:S(2)}) collective-permute-start(bf16[128,512]{1,0:T(8,128)(2,1)S(1)} %get-tuple-element.132), channel_id=1, source_target_pairs={{0,4},{4,8},{8,12},{12,0},{1,5},{5,9},{9,13},{13,1},{2,6},{6,10},{... | collective-permute-start | bytes 393224 | tf_op jit(solution)/shard_map/ppermute | solution.py:609
  143.2 2.4 %collective-permute-start.32 = (bf16[128,512]{1,0:T(8,128)(2,1)S(1)}, bf16[128,512]{1,0:T(8,128)(2,1)S(1)}, u32[]{:S(2)}, u32[]{:S(2)}) collective-permute-start(bf16[128,512]{1,0:T(8,128)(2,1)S(1)} %get-tuple-element.134), channel_id=1, source_target_pairs={{0,12},{4,0},{8,4},{12,8},{1,13},{5,1},{9,5},{13,9},{2,14},{6,2},{... | collective-permute-start | bytes 393224 | tf_op jit(solution)/shard_map/ppermute | solution.py:609
  145.6 0.7 query_subs.1
  146.4 0.7 collective-permute-done.30.refs_1_
  147.1 1.9 %collective-permute-start.27 = (bf16[128,512]{1,0:T(8,128)(2,1)S(1)}, bf16[128,512]{1,0:T(8,128)(2,1)S(1)}, u32[]{:S(2)}, u32[]{:S(2)}) collective-permute-start(bf16[128,512]{1,0:T(8,128)(2,1)S(1)} %get-tuple-element.123), channel_id=1, source_target_pairs={{0,8},{4,12},{8,0},{12,4},{1,9},{5,13},{9,1},{13,5},{2,10},{6,14},... | collective-permute-start | bytes 393224 | tf_op jit(solution)/shard_map/ppermute | solution.py:609
  148.9 3.9 %collective-permute-done.31.refs_2_ = bf16[128,512]{1,0:T(8,128)(2,1)S(1)} collective-permute-done((bf16[128,512]{1,0:T(8,128)(2,1)S(1)}, bf16[128,512]{1,0:T(8,128)(2,1)S(1)}, u32[]{:S(2)}, u32[]{:S(2)}) %collective-permute-start.31) | collective-permute-done | bytes 131104 | tf_op jit(solution)/shard_map/ppermute | solution.py:609
  152.9 5.4 %collective-permute-start.28 = (bf16[128,512]{1,0:T(8,128)(2,1)S(1)}, bf16[128,512]{1,0:T(8,128)(2,1)S(1)}, u32[]{:S(2)}, u32[]{:S(2)}) collective-permute-start(bf16[128,512]{1,0:T(8,128)(2,1)S(1)} %get-tuple-element.124), channel_id=1, source_target_pairs={{0,12},{4,0},{8,4},{12,8},{1,13},{5,1},{9,5},{13,9},{2,14},{6,2},{... | collective-permute-start | bytes 393224 | tf_op jit(solution)/shard_map/ppermute | solution.py:609
  158.3 1.8 %input_own.1.refs_2_.refs_4_ = bf16[1024,512]{1,0:T(8,128)(2,1)S(1)} custom-call(s32[4]{0:T(128)S(1)} %pad_add_fusion.refs_0_, bf16[1024,512]{1,0:T(8,128)(2,1)S(1)} %get-tuple-element.114.refs_2_.refs_1_, bf16[1024,512]{1,0:T(8,128)(2,1)S(1)} %get-tuple-element.118.refs_2_, bf16[1024,512]{1,0:T(8,128)(2,1)S(1)} %copy-done, bf16[1024,512]{1,0:T(8,128)(2,1)S(1)} %copy-done.3, ...), custom_call_target="tpu_custom_call" | custom-call | flops 1073741824 | bytes 5242896 | tf_op jit(solution)/shard_map/input_own/pallas_call | solution.py:583
  160.1 0.8 value_sum.1
  160.9 2.3 %input_sum.1 = (bf16[1024,512]{1,0:T(8,128)(2,1)}, bf16[128,512]{1,0:T(8,128)(2,1)S(1)}) custom-call(bf16[1024,1024]{1,0:T(8,128)(2,1)S(1)} %get-tuple-element.75.refs_11_.refs_0_, bf16[128,512]{1,0:T(8,128)(2,1)S(1)} %get-tuple-element.117.refs_5_.refs_1_, bf16[1024,512]{1,0:T(8,128)(2,1)S(1)} %input_own.1.refs_2_.refs_4_, ...), custom_call_target="tpu_custom_call" | custom-call | flops 1073741824 | bytes 5505024 | tf_op jit(solution)/shard_map/input_sum/pallas_call | solution.py:583
  163.4 0.8 query_sum.1
  (50 shorter events, 1.0 us)
Async XLA Ops:
  0.6 14.9 %copy-start = (bf16[1024,512]{1,0:T(8,128)(2,1)S(1)}, bf16[1024,512]{1,0:T(8,128)(2,1)}, u32[]{:S(2)}) copy-start(bf16[1024,512]{1,0:T(8,128)(2,1)} %refs_3_.5) | copy-start | bytes 3145732
  0.6 14.9 %copy-start.1 = (bf16[1024,1024]{1,0:T(8,128)(2,1)S(1)}, bf16[1024,1024]{1,0:T(8,128)(2,1)}, u32[]{:S(2)}) copy-start(bf16[1024,1024]{1,0:T(8,128)(2,1)} %refs_2_.4) | copy-start | bytes 6291460
  0.7 14.9 %copy-start.4 = (s32[1024,1]{0,1:T(1,128)S(1)}, s32[1024,1]{0,1:T(1,128)}, u32[]{:S(2)}) copy-start(s32[1024,1]{0,1:T(1,128)} %param.9) | copy-start | bytes 12292
  4.1 11.4 %copy-start.5 = (s32[1,1024]{1,0:T(1,128)S(1)}, s32[1,1024]{1,0:T(1,128)}, u32[]{:S(2)}) copy-start(s32[1,1024]{1,0:T(1,128)} %get-tuple-element.70.refs_0_.refs_1_) | copy-start | bytes 12292
  4.1 34.8 %collective-permute-start = (bf16[528,128]{1,0:T(8,128)(2,1)}, bf16[528,128]{1,0:T(8,128)(2,1)S(1)}, u32[]{:S(2)}, u32[]{:S(2)}) collective-permute-start(bf16[528,128]{1,0:T(8,128)(2,1)} %get-tuple-element.73), channel_id=1, source_target_pairs={{0,8},{8,0},{9,1},{4,12},{5,13},{12,4},{13,5},{1,9},{2,10},{10,2},... | collective-permute-start | bytes 405512 | tf_op jit(solution)/shard_map/ppermute | solution.py:600
  8.2 30.7 %collective-permute-start.1 = (bf16[528,128]{1,0:T(8,128)(2,1)}, bf16[528,128]{1,0:T(8,128)(2,1)S(1)}, u32[]{:S(2)}, u32[]{:S(2)}) collective-permute-start(bf16[528,128]{1,0:T(8,128)(2,1)} %get-tuple-element.74), channel_id=1, source_target_pairs={{0,9},{8,1},{9,0},{4,13},{5,12},{12,5},{13,4},{1,8},{2,11},{10,3},... | collective-permute-start | bytes 405512 | tf_op jit(solution)/shard_map/ppermute | solution.py:600
  12.7 21.3 %collective-permute-start.8 = (bf16[512,128]{1,0:T(8,128)(2,1)}, bf16[512,128]{1,0:T(8,128)(2,1)S(1)}, u32[]{:S(2)}, u32[]{:S(2)}) collective-permute-start(bf16[512,128]{1,0:T(8,128)(2,1)} %get-tuple-element.82), channel_id=1, source_target_pairs={{0,9},{8,1},{9,0},{4,13},{5,12},{12,5},{13,4},{1,8},{2,11},{10,3},... | collective-permute-start | bytes 393224 | tf_op jit(solution)/shard_map/ppermute | solution.py:600
  15.4 22.4 %collective-permute-start.7 = (bf16[512,128]{1,0:T(8,128)(2,1)}, bf16[512,128]{1,0:T(8,128)(2,1)}, u32[]{:S(2)}, u32[]{:S(2)}) collective-permute-start(bf16[512,128]{1,0:T(8,128)(2,1)} %get-tuple-element.71.refs_6_), channel_id=1, source_target_pairs={{0,8},{8,0},{9,1},{4,12},{5,13},{12,4},{13,5},{1,9},{2,10},{10,2},... | collective-permute-start | bytes 393224 | tf_op jit(solution)/shard_map/ppermute | solution.py:600
  15.5 1.2 copy-start.2
  16.8 0.9 copy-start.6
  17.7 21.4 %copy-start.3 = (bf16[1024,512]{1,0:T(8,128)(2,1)S(1)}, bf16[1024,512]{1,0:T(8,128)(2,1)}, u32[]{:S(2)}) copy-start(bf16[1024,512]{1,0:T(8,128)(2,1)} %refs_4_.3) | copy-start | bytes 3145732
  22.5 22.6 %collective-permute-start.2 = (bf16[1040,128]{1,0:T(8,128)(2,1)S(1)}, bf16[1040,128]{1,0:T(8,128)(2,1)S(1)}, u32[]{:S(2)}, u32[]{:S(2)}) collective-permute-start(bf16[1040,128]{1,0:T(8,128)(2,1)S(1)} %get-tuple-element.77), channel_id=1, source_target_pairs={{0,4},{8,12},{9,13},{4,8},{5,9},{12,0},{13,1},{1,5},{2,6},{10,14},... | collective-permute-start | bytes 798728 | tf_op jit(solution)/shard_map/ppermute | solution.py:600
  34.0 11.6 %collective-permute-start.3 = (bf16[1040,128]{1,0:T(8,128)(2,1)S(1)}, bf16[1040,128]{1,0:T(8,128)(2,1)S(1)}, u32[]{:S(2)}, u32[]{:S(2)}) collective-permute-start(bf16[1040,128]{1,0:T(8,128)(2,1)S(1)} %get-tuple-element.78), channel_id=1, source_target_pairs={{0,5},{8,13},{9,12},{4,9},{5,8},{12,1},{13,0},{1,4},{2,7},{10,15},... | collective-permute-start | bytes 798728 | tf_op jit(solution)/shard_map/ppermute | solution.py:600
  37.7 20.2 %collective-permute-start.4 = (bf16[1040,128]{1,0:T(8,128)(2,1)S(1)}, bf16[1040,128]{1,0:T(8,128)(2,1)S(1)}, u32[]{:S(2)}, u32[]{:S(2)}) collective-permute-start(bf16[1040,128]{1,0:T(8,128)(2,1)S(1)} %get-tuple-element.79), channel_id=1, source_target_pairs={{0,12},{8,4},{9,5},{4,0},{5,1},{12,8},{13,9},{1,13},{2,14},{10,6},... | collective-permute-start | bytes 798728 | tf_op jit(solution)/shard_map/ppermute | solution.py:600
  38.9 19.0 %collective-permute-start.5 = (bf16[1040,128]{1,0:T(8,128)(2,1)S(1)}, bf16[1040,128]{1,0:T(8,128)(2,1)S(1)}, u32[]{:S(2)}, u32[]{:S(2)}) collective-permute-start(bf16[1040,128]{1,0:T(8,128)(2,1)S(1)} %get-tuple-element.80), channel_id=1, source_target_pairs={{0,13},{8,5},{9,4},{4,1},{5,0},{12,9},{13,8},{1,12},{2,15},{10,7},... | collective-permute-start | bytes 798728 | tf_op jit(solution)/shard_map/ppermute | solution.py:600
  38.9 19.0 %collective-permute-start.6 = (bf16[1040,128]{1,0:T(8,128)(2,1)S(1)}, bf16[1040,128]{1,0:T(8,128)(2,1)S(1)}, u32[]{:S(2)}, u32[]{:S(2)}) collective-permute-start(bf16[1040,128]{1,0:T(8,128)(2,1)S(1)} %get-tuple-element.81), channel_id=1, source_target_pairs={{0,1},{8,9},{9,8},{4,5},{5,4},{12,13},{13,12},{1,0},{2,3},{10,11},... | collective-permute-start | bytes 798728 | tf_op jit(solution)/shard_map/ppermute | solution.py:600
  45.1 14.9 %collective-permute-start.15 = (bf16[512,128]{1,0:T(8,128)(2,1)S(1)}, bf16[512,128]{1,0:T(8,128)(2,1)S(1)}, u32[]{:S(2)}, u32[]{:S(2)}) collective-permute-start(bf16[512,128]{1,0:T(8,128)(2,1)S(1)} %get-tuple-element.100), channel_id=1, source_target_pairs={{0,1},{8,9},{9,8},{4,5},{5,4},{12,13},{13,12},{1,0},{2,3},{10,11},... | collective-permute-start | bytes 393224 | tf_op jit(solution)/shard_map/ppermute | solution.py:600
  45.6 16.8 %collective-permute-start.14 = (bf16[512,128]{1,0:T(8,128)(2,1)S(1)}, bf16[512,128]{1,0:T(8,128)(2,1)S(1)}, u32[]{:S(2)}, u32[]{:S(2)}) collective-permute-start(bf16[512,128]{1,0:T(8,128)(2,1)S(1)} %get-tuple-element.98), channel_id=1, source_target_pairs={{0,13},{8,5},{9,4},{4,1},{5,0},{12,9},{13,8},{1,12},{2,15},{10,7},... | collective-permute-start | bytes 393224 | tf_op jit(solution)/shard_map/ppermute | solution.py:600
  57.9 18.5 %collective-permute-start.13 = (bf16[512,128]{1,0:T(8,128)(2,1)S(1)}, bf16[512,128]{1,0:T(8,128)(2,1)S(1)}, u32[]{:S(2)}, u32[]{:S(2)}) collective-permute-start(bf16[512,128]{1,0:T(8,128)(2,1)S(1)} %get-tuple-element.96), channel_id=1, source_target_pairs={{0,12},{8,4},{9,5},{4,0},{5,1},{12,8},{13,9},{1,13},{2,14},{10,6},... | collective-permute-start | bytes 393224 | tf_op jit(solution)/shard_map/ppermute | solution.py:600
  58.6 17.9 %collective-permute-start.12 = (bf16[512,128]{1,0:T(8,128)(2,1)S(1)}, bf16[512,128]{1,0:T(8,128)(2,1)S(1)}, u32[]{:S(2)}, u32[]{:S(2)}) collective-permute-start(bf16[512,128]{1,0:T(8,128)(2,1)S(1)} %get-tuple-element.94), channel_id=1, source_target_pairs={{0,5},{8,13},{9,12},{4,9},{5,8},{12,1},{13,0},{1,4},{2,7},{10,15},... | collective-permute-start | bytes 393224 | tf_op jit(solution)/shard_map/ppermute | solution.py:600
  59.8 16.7 %collective-permute-start.11 = (bf16[512,128]{1,0:T(8,128)(2,1)S(1)}, bf16[512,128]{1,0:T(8,128)(2,1)S(1)}, u32[]{:S(2)}, u32[]{:S(2)}) collective-permute-start(bf16[512,128]{1,0:T(8,128)(2,1)S(1)} %get-tuple-element.92), channel_id=1, source_target_pairs={{0,4},{8,12},{9,13},{4,8},{5,9},{12,0},{13,1},{1,5},{2,6},{10,14},... | collective-permute-start | bytes 393224 | tf_op jit(solution)/shard_map/ppermute | solution.py:600
  60.0 17.7 %collective-permute-start.10 = (bf16[512,128]{1,0:T(8,128)(2,1)S(1)}, bf16[512,128]{1,0:T(8,128)(2,1)S(1)}, u32[]{:S(2)}, u32[]{:S(2)}) collective-permute-start(bf16[512,128]{1,0:T(8,128)(2,1)S(1)} %get-tuple-element.90), channel_id=1, source_target_pairs={{0,9},{8,1},{9,0},{4,13},{5,12},{12,5},{13,4},{1,8},{2,11},{10,3},... | collective-permute-start | bytes 393224 | tf_op jit(solution)/shard_map/ppermute | solution.py:600
  62.4 18.4 %collective-permute-start.9 = (bf16[512,128]{1,0:T(8,128)(2,1)S(1)}, bf16[512,128]{1,0:T(8,128)(2,1)S(1)}, u32[]{:S(2)}, u32[]{:S(2)}) collective-permute-start(bf16[512,128]{1,0:T(8,128)(2,1)S(1)} %get-tuple-element.88), channel_id=1, source_target_pairs={{0,8},{8,0},{9,1},{4,12},{5,13},{12,4},{13,5},{1,9},{2,10},{10,2},... | collective-permute-start | bytes 393224 | tf_op jit(solution)/shard_map/ppermute | solution.py:600
  80.8 23.3 %collective-permute-start.16 = (bf16[2,512,128]{2,1,0:T(8,128)(2,1)S(1)}, bf16[2,512,128]{2,1,0:T(8,128)(2,1)S(1)}, u32[]{:S(2)}, u32[]{:S(2)}) collective-permute-start(bf16[2,512,128]{2,1,0:T(8,128)(2,1)S(1)} %get-tuple-element.102), channel_id=1, source_target_pairs={{0,4},{4,8},{8,12},{12,0},{1,5},{5,9},{9,13},{13,1},{2,6},{6,10},{... | collective-permute-start | bytes 786440 | tf_op jit(solution)/shard_map/ppermute | solution.py:609
  82.7 23.9 %collective-permute-start.17 = (bf16[2,512,128]{2,1,0:T(8,128)(2,1)S(1)}, bf16[2,512,128]{2,1,0:T(8,128)(2,1)S(1)}, u32[]{:S(2)}, u32[]{:S(2)}) collective-permute-start(bf16[2,512,128]{2,1,0:T(8,128)(2,1)S(1)} %get-tuple-element.103), channel_id=1, source_target_pairs={{0,8},{4,12},{8,0},{12,4},{1,9},{5,13},{9,1},{13,5},{2,10},{6,14},... | collective-permute-start | bytes 786440 | tf_op jit(solution)/shard_map/ppermute | solution.py:609
  86.0 20.5 %collective-permute-start.18 = (bf16[2,512,128]{2,1,0:T(8,128)(2,1)S(1)}, bf16[2,512,128]{2,1,0:T(8,128)(2,1)S(1)}, u32[]{:S(2)}, u32[]{:S(2)}) collective-permute-start(bf16[2,512,128]{2,1,0:T(8,128)(2,1)S(1)} %get-tuple-element.104), channel_id=1, source_target_pairs={{0,12},{4,0},{8,4},{12,8},{1,13},{5,1},{9,5},{13,9},{2,14},{6,2},{... | collective-permute-start | bytes 786440 | tf_op jit(solution)/shard_map/ppermute | solution.py:609
  102.0 11.5 %collective-permute-start.20 = (bf16[2,544,128]{2,1,0:T(8,128)(2,1)S(1)}, bf16[2,544,128]{2,1,0:T(8,128)(2,1)S(1)}, u32[]{:S(2)}, u32[]{:S(2)}) collective-permute-start(bf16[2,544,128]{2,1,0:T(8,128)(2,1)S(1)} %get-tuple-element.111), channel_id=1, source_target_pairs={{0,4},{4,8},{8,12},{12,0},{1,5},{5,9},{9,13},{13,1},{2,6},{6,10},{... | collective-permute-start | bytes 835592 | tf_op jit(solution)/shard_map/ppermute | solution.py:609
  104.1 22.8 %collective-permute-start.21 = (bf16[2,544,128]{2,1,0:T(8,128)(2,1)S(1)}, bf16[2,544,128]{2,1,0:T(8,128)(2,1)S(1)}, u32[]{:S(2)}, u32[]{:S(2)}) collective-permute-start(bf16[2,544,128]{2,1,0:T(8,128)(2,1)S(1)} %get-tuple-element.112), channel_id=1, source_target_pairs={{0,8},{4,12},{8,0},{12,4},{1,9},{5,13},{9,1},{13,5},{2,10},{6,14},... | collective-permute-start | bytes 835592 | tf_op jit(solution)/shard_map/ppermute | solution.py:609
  104.1 22.8 %collective-permute-start.22 = (bf16[2,544,128]{2,1,0:T(8,128)(2,1)S(1)}, bf16[2,544,128]{2,1,0:T(8,128)(2,1)S(1)}, u32[]{:S(2)}, u32[]{:S(2)}) collective-permute-start(bf16[2,544,128]{2,1,0:T(8,128)(2,1)S(1)} %get-tuple-element.113), channel_id=1, source_target_pairs={{0,12},{4,0},{8,4},{12,8},{1,13},{5,1},{9,5},{13,9},{2,14},{6,2},{... | collective-permute-start | bytes 835592 | tf_op jit(solution)/shard_map/ppermute | solution.py:609
  107.1 20.4 %collective-permute-start.19 = (bf16[4,512,128]{2,1,0:T(8,128)(2,1)S(1)}, bf16[4,512,128]{2,1,0:T(8,128)(2,1)S(1)}, u32[]{:S(2)}, u32[]{:S(2)}) collective-permute-start(bf16[4,512,128]{2,1,0:T(8,128)(2,1)S(1)} %swap_value.1), channel_id=1, source_target_pairs={{0,1},{1,0},{2,3},{3,2},{4,5},{5,4},{6,7},{7,6},{8,9},{9,8},{10,11... | collective-permute-start | bytes 1572872 | tf_op jit(solution)/shard_map/ppermute | solution.py:609
  127.5 2.6 %collective-permute-start.23 = (bf16[4,544,128]{2,1,0:T(8,128)(2,1)S(1)}, bf16[4,544,128]{2,1,0:T(8,128)(2,1)S(1)}, u32[]{:S(2)}, u32[]{:S(2)}) collective-permute-start(bf16[4,544,128]{2,1,0:T(8,128)(2,1)S(1)} %swap_query.1), channel_id=1, source_target_pairs={{0,1},{1,0},{2,3},{3,2},{4,5},{5,4},{6,7},{7,6},{8,9},{9,8},{10,11... | collective-permute-start | bytes 1671176 | tf_op jit(solution)/shard_map/ppermute | solution.py:609
  132.1 28.8 %collective-permute-start.25 = (bf16[1024,512]{1,0:T(8,128)(2,1)S(1)}, bf16[1024,512]{1,0:T(8,128)(2,1)S(1)}, u32[]{:S(2)}, u32[]{:S(2)}) collective-permute-start(bf16[1024,512]{1,0:T(8,128)(2,1)S(1)} %get-tuple-element.119), channel_id=1, source_target_pairs={{0,2},{2,0},{1,3},{3,1},{4,6},{6,4},{5,7},{7,5},{8,10},{10,8},{9,1... | collective-permute-start | bytes 3145736 | tf_op jit(solution)/shard_map/ppermute | solution.py:609
  133.6 2.4 %collective-permute-start.29 = (bf16[4,128,512]{2,1,0:T(8,128)(2,1)S(1)}, bf16[4,128,512]{2,1,0:T(8,128)(2,1)S(1)}, u32[]{:S(2)}, u32[]{:S(2)}) collective-permute-start(bf16[4,128,512]{2,1,0:T(8,128)(2,1)S(1)} %get-tuple-element.126), channel_id=1, source_target_pairs={{0,1},{1,0},{2,3},{3,2},{4,5},{5,4},{6,7},{7,6},{8,9},{9,8},{10,11... | collective-permute-start | bytes 1572872 | tf_op jit(solution)/shard_map/ppermute | solution.py:609
  135.6 10.0 %collective-permute-start.24 = (bf16[4,128,512]{2,1,0:T(8,128)(2,1)S(1)}, bf16[4,128,512]{2,1,0:T(8,128)(2,1)S(1)}, u32[]{:S(2)}, u32[]{:S(2)}) collective-permute-start(bf16[4,128,512]{2,1,0:T(8,128)(2,1)S(1)} %get-tuple-element.116), channel_id=1, source_target_pairs={{0,1},{1,0},{2,3},{3,2},{4,5},{5,4},{6,7},{7,6},{8,9},{9,8},{10,11... | collective-permute-start | bytes 1572872 | tf_op jit(solution)/shard_map/ppermute | solution.py:609
  136.7 10.4 %collective-permute-start.30 = (bf16[128,512]{1,0:T(8,128)(2,1)S(1)}, bf16[128,512]{1,0:T(8,128)(2,1)S(1)}, u32[]{:S(2)}, u32[]{:S(2)}) collective-permute-start(bf16[128,512]{1,0:T(8,128)(2,1)S(1)} %get-tuple-element.132), channel_id=1, source_target_pairs={{0,4},{4,8},{8,12},{12,0},{1,5},{5,9},{9,13},{13,1},{2,6},{6,10},{... | collective-permute-start | bytes 393224 | tf_op jit(solution)/shard_map/ppermute | solution.py:609
  143.2 9.7 %collective-permute-start.31 = (bf16[128,512]{1,0:T(8,128)(2,1)S(1)}, bf16[128,512]{1,0:T(8,128)(2,1)S(1)}, u32[]{:S(2)}, u32[]{:S(2)}) collective-permute-start(bf16[128,512]{1,0:T(8,128)(2,1)S(1)} %get-tuple-element.133), channel_id=1, source_target_pairs={{0,8},{4,12},{8,0},{12,4},{1,9},{5,13},{9,1},{13,5},{2,10},{6,14},... | collective-permute-start | bytes 393224 | tf_op jit(solution)/shard_map/ppermute | solution.py:609
  143.2 16.9 %collective-permute-start.32 = (bf16[128,512]{1,0:T(8,128)(2,1)S(1)}, bf16[128,512]{1,0:T(8,128)(2,1)S(1)}, u32[]{:S(2)}, u32[]{:S(2)}) collective-permute-start(bf16[128,512]{1,0:T(8,128)(2,1)S(1)} %get-tuple-element.134), channel_id=1, source_target_pairs={{0,12},{4,0},{8,4},{12,8},{1,13},{5,1},{9,5},{13,9},{2,14},{6,2},{... | collective-permute-start | bytes 393224 | tf_op jit(solution)/shard_map/ppermute | solution.py:609
  146.3 16.9 %collective-permute-start.26 = (bf16[128,512]{1,0:T(8,128)(2,1)S(1)}, bf16[128,512]{1,0:T(8,128)(2,1)S(1)}, u32[]{:S(2)}, u32[]{:S(2)}) collective-permute-start(bf16[128,512]{1,0:T(8,128)(2,1)S(1)} %get-tuple-element.122), channel_id=1, source_target_pairs={{0,4},{4,8},{8,12},{12,0},{1,5},{5,9},{9,13},{13,1},{2,6},{6,10},{... | collective-permute-start | bytes 393224 | tf_op jit(solution)/shard_map/ppermute | solution.py:609
  147.1 16.3 %collective-permute-start.27 = (bf16[128,512]{1,0:T(8,128)(2,1)S(1)}, bf16[128,512]{1,0:T(8,128)(2,1)S(1)}, u32[]{:S(2)}, u32[]{:S(2)}) collective-permute-start(bf16[128,512]{1,0:T(8,128)(2,1)S(1)} %get-tuple-element.123), channel_id=1, source_target_pairs={{0,8},{4,12},{8,0},{12,4},{1,9},{5,13},{9,1},{13,5},{2,10},{6,14},... | collective-permute-start | bytes 393224 | tf_op jit(solution)/shard_map/ppermute | solution.py:609
  152.9 10.5 %collective-permute-start.28 = (bf16[128,512]{1,0:T(8,128)(2,1)S(1)}, bf16[128,512]{1,0:T(8,128)(2,1)S(1)}, u32[]{:S(2)}, u32[]{:S(2)}) collective-permute-start(bf16[128,512]{1,0:T(8,128)(2,1)S(1)} %get-tuple-element.124), channel_id=1, source_target_pairs={{0,12},{4,0},{8,4},{12,8},{1,13},{5,1},{9,5},{13,9},{2,14},{6,2},{... | collective-permute-start | bytes 393224 | tf_op jit(solution)/shard_map/ppermute | solution.py:609

commit v22 on v19

--- a/solution.py
+++ b/solution.py
@@ -496,7 +496,9 @@
     unfold(home_ref, centroid_ref, heads, half, home_ref.shape[1] - half, lambda x: x * factor)
 
 
-def query_weight_kernel(sizes, me_ref, turned_ref, rows_ref, *sub_refs):
+def query_weight_kernel(sizes, me_ref, turned_ref, rows_ref, *refs):
+    term_refs, sub_refs, seq_refs = refs[: sizes[1]], refs[sizes[1] : 2 * sizes[1]], refs[2 * sizes[1] :]
+    fold_subs_kernel(me_ref, *term_refs, *seq_refs)
     weight_partial(sizes, me_ref, turned_ref, rows_ref, sub_refs)
 
 
@@ -726,7 +728,7 @@
         name="value_home",
     )
     value_terms, value_weight = refs[: parts - 1], refs[parts - 1 :]
-    value_weight = fold_subs(me, value_weight, "value_subs")
+    value_weight = pass_round(value_weight, "sub")
     *partials, query_rows, centroid_grad = call(
         functools.partial(query_home_kernel, sizes, heads, (CLUSTERS / (toks * owners)) ** 0.5, parts),
         several(parts - 1, slots, columns)
@@ -738,15 +740,14 @@
         name="query_home",
     )
     arrived = [shift(partial, "head", k + 1) for k, partial in enumerate(partials)]
-    value_weight, _ = lax.optimization_barrier((value_weight, home_query))
-    value_weight = pass_round(value_weight, "seq")
-    query_weight = call(
+    refs = call(
         functools.partial(query_weight_kernel, sizes),
-        sub_shapes,
-        (me, turned, query_rows),
+        sub_shapes + several(sizes[0], piece, width_dev),
+        (me, turned, query_rows, *value_weight),
         flops=weight_flops,
         name="query_weight",
     )
+    query_weight, value_weight = refs[: sizes[1]], pass_round(refs[sizes[1] :], "seq")
     query_weight = fold_subs(me, query_weight, "query_subs")
     own = call(
         functools.partial(input_own_kernel, parts),

time: 165 us -> 165 us (level)
    pallas_call x16 -> x15, Pallas kernels: 61.2 us -> 59.6 us  [call(): pl.pallas_call(body, out_shape=outs, in_specs=specs, out_specs=jax.tree.m...]
  transfers between devices with their start and end apart: 31 -> 31, of which waited for: 9 -> 9; matrix products, arithmetic and copies ran while one was open for 0% -> 0% of each run, Pallas kernels for 32% -> 33%
where the time goes in v22:
time: 165 us; the launch traced here: 163 us
  Pallas kernels  59.6 us (36%)
  starting transfers between devices  50.5 us (31%)
  waiting for transfers between devices  50.5 us (31%)
  local copies, waits for them, and re-layouts  1.92 us (1%)
    pallas_call x15, Pallas kernels, call(): pl.pallas_call(body, out_shape=outs, in_specs=specs, out_specs=jax.tree.m...  59.6 us
    ppermute x17, starting transfers between devices, shift(): lax.ppermute(part, axis, [(i, (i + ahead) % size) for i in range(size)])  26.7 us
    ppermute x14, waiting for transfers between devices, exchange(): out.append(part if ahead == (0, 0) else lax.ppermute(part, OWNERS, moves))  26.4 us
    ppermute x17, waiting for transfers between devices, shift(): lax.ppermute(part, axis, [(i, (i + ahead) % size) for i in range(size)])  24.1 us
    ppermute x14, starting transfers between devices, exchange(): out.append(part if ahead == (0, 0) else lax.ppermute(part, OWNERS, moves))  23.9 us
  transfers between devices with their start and end apart: 31, of which 9 were waited for; matrix products, arithmetic and copies ran while one was open for 0% of the time, Pallas kernels for 33%

profile of v22, /device:TPU:0, one launch (start us, length us, event | category | flops | bytes accessed | tf_op | source)
XLA Modules:
  0.0 163.5 jit_solution(6805338913779149719)
XLA Ops:
  0.7 5.5 %project_far.1 = (bf16[1040,128]{1,0:T(8,128)(2,1)}, bf16[1040,128]{1,0:T(8,128)(2,1)}, s32[1,1024]{1,0:T(1,128)}) custom-call(s32[1,1024]{1,0:T(1,128)} %bitcast.5, bf16[1024,1024]{1,0:T(8,128)(2,1)} %refs_2_.4, bf16[1024,512]{1,0:T(8,128)(2,1)} %refs_3_.7, bf16[1024,512]{1,0:T(8,128)(2,1)} %refs_5_.1), custom_call_target="tpu_custom_call" | custom-call | flops 805306368 | bytes 4734976 | tf_op jit(solution)/shard_map/project_far/pallas_call | solution.py:554
  6.1 4.1 %collective-permute-start = (bf16[1040,128]{1,0:T(8,128)(2,1)}, bf16[1040,128]{1,0:T(8,128)(2,1)S(1)}, u32[]{:S(2)}, u32[]{:S(2)}) collective-permute-start(bf16[1040,128]{1,0:T(8,128)(2,1)} %get-tuple-element.69), channel_id=1, source_target_pairs={{0,8},{8,0},{9,1},{4,12},{5,13},{12,4},{13,5},{1,9},{2,10},{10,2},... | collective-permute-start | bytes 798728 | tf_op jit(solution)/shard_map/ppermute | solution.py:576
  10.3 0.1 pad_add_fusion.refs_0_
  10.4 1.2 copy-done.2
  11.6 0.7 copy-done.5
  12.3 4.8 %project_query.1 = (bf16[1040,128]{1,0:T(8,128)(2,1)S(1)}, bf16[1040,128]{1,0:T(8,128)(2,1)S(1)}, bf16[1040,128]{1,0:T(8,128)(2,1)S(1)}, bf16[1040,128]{1,0:T(8,...) custom-call(s32[4]{0:T(128)S(1)} %pad_add_fusion.refs_0_, s32[1,1024]{1,0:T(1,128)S(1)} %copy-done.5, ...), custom_call_target="tpu_custom_call" | custom-call | flops 3221225472 | bytes 5799952 | tf_op jit(solution)/shard_map/project_query/pallas_call | solution.py:554
  17.1 1.7 %collective-permute-start.3 = (bf16[1040,128]{1,0:T(8,128)(2,1)S(1)}, bf16[1040,128]{1,0:T(8,128)(2,1)S(1)}, u32[]{:S(2)}, u32[]{:S(2)}) collective-permute-start(bf16[1040,128]{1,0:T(8,128)(2,1)S(1)} %get-tuple-element.71), channel_id=1, source_target_pairs={{0,5},{8,13},{9,12},{4,9},{5,8},{12,1},{13,0},{1,4},{2,7},{10,15},... | collective-permute-start | bytes 798728 | tf_op jit(solution)/shard_map/ppermute | solution.py:576
  18.8 1.6 collective-permute-start.2
  20.3 2.2 %collective-permute-start.4 = (bf16[1040,128]{1,0:T(8,128)(2,1)S(1)}, bf16[1040,128]{1,0:T(8,128)(2,1)S(1)}, u32[]{:S(2)}, u32[]{:S(2)}) collective-permute-start(bf16[1040,128]{1,0:T(8,128)(2,1)S(1)} %get-tuple-element.72), channel_id=1, source_target_pairs={{0,12},{8,4},{9,5},{4,0},{5,1},{12,8},{13,9},{1,13},{2,14},{10,6},... | collective-permute-start | bytes 798728 | tf_op jit(solution)/shard_map/ppermute | solution.py:576
  22.6 18.0 %collective-permute-done.refs_2_ = bf16[1040,128]{1,0:T(8,128)(2,1)S(1)} collective-permute-done((bf16[1040,128]{1,0:T(8,128)(2,1)}, bf16[1040,128]{1,0:T(8,128)(2,1)S(1)}, u32[]{:S(2)}, u32[]{:S(2)}) %collective-permute-start) | collective-permute-done | bytes 266272 | tf_op jit(solution)/shard_map/ppermute | solution.py:576
  40.6 4.1 %collective-permute-done.1.refs_3_ = bf16[1040,128]{1,0:T(8,128)(2,1)} collective-permute-done((bf16[1040,128]{1,0:T(8,128)(2,1)}, bf16[1040,128]{1,0:T(8,128)(2,1)}, u32[]{:S(2)}, u32[]{:S(2)}) %collective-permute-start.1) | collective-permute-done | bytes 266272 | tf_op jit(solution)/shard_map/ppermute | solution.py:576
  44.8 1.4 collective-permute-start.6
  46.2 6.0 %project_value.1 = (bf16[512,128]{1,0:T(8,128)(2,1)S(1)}, bf16[512,128]{1,0:T(8,128)(2,1)S(1)}, bf16[512,128]{1,0:T(8,128)(2,1)S(1)}, bf16[512,128]{1,0:T(8,128)...) custom-call(s32[4]{0:T(128)S(1)} %pad_add_fusion.refs_0_, ...), custom_call_target="tpu_custom_call" | custom-call | flops 2147483648 | bytes 8392720 | tf_op jit(solution)/shard_map/project_value/pallas_call | solution.py:554
  52.2 0.1 collective-permute-start.13
  52.3 3.6 %collective-permute-start.12 = (bf16[512,128]{1,0:T(8,128)(2,1)S(1)}, bf16[512,128]{1,0:T(8,128)(2,1)S(1)}, u32[]{:S(2)}, u32[]{:S(2)}) collective-permute-start(bf16[512,128]{1,0:T(8,128)(2,1)S(1)} %get-tuple-element.90), channel_id=1, source_target_pairs={{0,13},{8,5},{9,4},{4,1},{5,0},{12,9},{13,8},{1,12},{2,15},{10,7},... | collective-permute-start | bytes 393224 | tf_op jit(solution)/shard_map/ppermute | solution.py:576
  55.9 4.7 %collective-permute-start.11 = (bf16[512,128]{1,0:T(8,128)(2,1)S(1)}, bf16[512,128]{1,0:T(8,128)(2,1)S(1)}, u32[]{:S(2)}, u32[]{:S(2)}) collective-permute-start(bf16[512,128]{1,0:T(8,128)(2,1)S(1)} %get-tuple-element.88), channel_id=1, source_target_pairs={{0,12},{8,4},{9,5},{4,0},{5,1},{12,8},{13,9},{1,13},{2,14},{10,6},... | collective-permute-start | bytes 393224 | tf_op jit(solution)/shard_map/ppermute | solution.py:576
  60.6 3.8 %collective-permute-start.8 = (bf16[512,128]{1,0:T(8,128)(2,1)S(1)}, bf16[512,128]{1,0:T(8,128)(2,1)S(1)}, u32[]{:S(2)}, u32[]{:S(2)}) collective-permute-start(bf16[512,128]{1,0:T(8,128)(2,1)S(1)} %get-tuple-element.82), channel_id=1, source_target_pairs={{0,9},{8,1},{9,0},{4,13},{5,12},{12,5},{13,4},{1,8},{2,11},{10,3},... | collective-permute-start | bytes 393224 | tf_op jit(solution)/shard_map/ppermute | solution.py:576
  64.5 0.6 collective-permute-start.7
  65.1 13.5 %value_grad.1 = (bf16[2,512,128]{2,1,0:T(8,128)(2,1)S(1)}, bf16[2,512,128]{2,1,0:T(8,128)(2,1)S(1)}, bf16[2,512,128]{2,1,0:T(8,128)(2,1)S(1)}, bf16[2,512,128]{2...) custom-call(s32[4]{0:T(128)S(1)} %pad_add_fusion.refs_0_, ...), custom_call_target="tpu_custom_call" | custom-call | flops 2147483648 | bytes 8163344 | tf_op jit(solution)/shard_map/value_grad/pallas_call | solution.py:554
  78.6 1.1 collective-permute-done.8.refs_5_
  79.6 3.2 %collective-permute-done.7.refs_4_ = bf16[512,128]{1,0:T(8,128)(2,1)S(1)} collective-permute-done((bf16[512,128]{1,0:T(8,128)(2,1)S(1)}, bf16[512,128]{1,0:T(8,128)(2,1)S(1)}, u32[]{:S(2)}, u32[]{:S(2)}) %collective-permute-start.7) | collective-permute-done | bytes 131104 | tf_op jit(solution)/shard_map/ppermute | solution.py:576
  82.8 1.5 collective-permute-start.15
  84.3 2.3 %collective-permute-start.16 = (bf16[2,512,128]{2,1,0:T(8,128)(2,1)S(1)}, bf16[2,512,128]{2,1,0:T(8,128)(2,1)S(1)}, u32[]{:S(2)}, u32[]{:S(2)}) collective-permute-start(bf16[2,512,128]{2,1,0:T(8,128)(2,1)S(1)} %get-tuple-element.96), channel_id=1, source_target_pairs={{0,12},{4,0},{8,4},{12,8},{1,13},{5,1},{9,5},{13,9},{2,14},{6,2},{... | collective-permute-start | bytes 786440 | tf_op jit(solution)/shard_map/ppermute | solution.py:582
  86.6 15.8 %query_grad.1 = (bf16[2,544,128]{2,1,0:T(8,128)(2,1)S(1)}, bf16[2,544,128]{2,1,0:T(8,128)(2,1)S(1)}, bf16[2,544,128]{2,1,0:T(8,128)(2,1)S(1)}, bf16[2,544,128]{2,1,0:T(8,128)(2,1)S(1)}) custom-call(s32[4]{0:T(128)S(1)} %pad_add_fusion.refs_0_, s32[8,128]{1,0:T(8,128)S(1)} %get-tuple-element.97.refs_1_, bf16[19456,128]{1,0:T(8,128)(2,1)} %get-tuple-element.98.refs_2_, ...), custom_call_target="tpu_custom_call" | custom-call | flops 3221225472 | bytes 7147536 | tf_op jit(solution)/shard_map/query_grad/pallas_call | solution.py:554
  102.4 0.6 collective-permute-start.18
  103.0 1.5 collective-permute-start.19
  104.6 2.8 %collective-permute-start.20 = (bf16[2,544,128]{2,1,0:T(8,128)(2,1)S(1)}, bf16[2,544,128]{2,1,0:T(8,128)(2,1)S(1)}, u32[]{:S(2)}, u32[]{:S(2)}) collective-permute-start(bf16[2,544,128]{2,1,0:T(8,128)(2,1)S(1)} %get-tuple-element.105), channel_id=1, source_target_pairs={{0,12},{4,0},{8,4},{12,8},{1,13},{5,1},{9,5},{13,9},{2,14},{6,2},{... | collective-permute-start | bytes 835592 | tf_op jit(solution)/shard_map/ppermute | solution.py:582
  107.4 0.6 swap_value.1
  108.1 5.9 %collective-permute-done.18.refs_2_.refs_4_ = bf16[2,544,128]{2,1,0:T(8,128)(2,1)S(1)} collective-permute-done((bf16[2,544,128]{2,1,0:T(8,128)(2,1)S(1)}, bf16[2,544,128]{2,1,0:T(8,128)(2,1)S(1)}, u32[]{:S(2)}, u32[]{:S(2)}) %collective-permute-start.18) | collective-permute-done | bytes 278560 | tf_op jit(solution)/shard_map/ppermute | solution.py:582
  114.0 13.5 %collective-permute-done.19.refs_3_.refs_5_ = bf16[2,544,128]{2,1,0:T(8,128)(2,1)S(1)} collective-permute-done((bf16[2,544,128]{2,1,0:T(8,128)(2,1)S(1)}, bf16[2,544,128]{2,1,0:T(8,128)(2,1)S(1)}, u32[]{:S(2)}, u32[]{:S(2)}) %collective-permute-start.19) | collective-permute-done | bytes 278560 | tf_op jit(solution)/shard_map/ppermute | solution.py:582
  127.5 0.6 swap_query.1
  128.2 2.5 %value_home.1 = (bf16[1024,512]{1,0:T(8,128)(2,1)S(1)}, f32[1024,512]{1,0:T(8,128)S(1)}, bf16[4,128,512]{2,1,0:T(8,128)(2,1)S(1)}, bf16[4,128,512]{2,1,0:T(8,128)(2,1)S(1)}) custom-call(s32[4]{0:T(128)S(1)} %pad_add_fusion.refs_0_, bf16[1024,1024]{1,0:T(8,128)(2,1)S(1)} %get-tuple-element.67.refs_1_, bf16[1024,512]{1,0:T(8,128)(2,1)S(1)} %copy-done.3, ...), custom_call_target="tpu_custom_call" | custom-call | flops 1610612736 | bytes 8912912 | tf_op jit(solution)/shard_map/value_home/pallas_call | solution.py:554
  130.7 0.5 collective-permute-start.22
  131.2 2.0 %query_home.1 = (bf16[1024,512]{1,0:T(8,128)(2,1)S(1)}, bf16[1024,512]{1,0:T(8,128)(2,1)S(1)}, f32[64,512]{1,0:T(8,128)}) custom-call(s32[4]{0:T(128)S(1)} %pad_add_fusion.refs_0_, bf16[1024,512]{1,0:T(8,128)(2,1)S(1)} %copy-done, f32[1024,512]{1,0:T(8,128)S(1)} %get-tuple-element.102.refs_2_, ...), custom_call_target="tpu_custom_call" | custom-call | flops 536870912 | bytes 7045136 | tf_op jit(solution)/shard_map/query_home/pallas_call | solution.py:554
  133.3 1.5 collective-permute-start.24
  134.8 2.0 %query_weight.1 = (bf16[4,128,512]{2,1,0:T(8,128)(2,1)S(1)}, bf16[4,128,512]{2,1,0:T(8,128)(2,1)S(1)}, bf16[128,512]{1,0:T(8,128)(2,1)S(1)}, bf16[128,512]{1,0:T...) custom-call(s32[4]{0:T(128)S(1)} %pad_add_fusion.refs_0_, ...), custom_call_target="tpu_custom_call" | custom-call | flops 1073741824 | bytes 5767184 | tf_op jit(solution)/shard_map/query_weight/pallas_call | solution.py:554
  136.8 5.6 %collective-permute-start.28 = (bf16[128,512]{1,0:T(8,128)(2,1)S(1)}, bf16[128,512]{1,0:T(8,128)(2,1)S(1)}, u32[]{:S(2)}, u32[]{:S(2)}) collective-permute-start(bf16[128,512]{1,0:T(8,128)(2,1)S(1)} %get-tuple-element.120), channel_id=1, source_target_pairs={{0,4},{4,8},{8,12},{12,0},{1,5},{5,9},{9,13},{13,1},{2,6},{6,10},{... | collective-permute-start | bytes 393224 | tf_op jit(solution)/shard_map/ppermute | solution.py:582
  142.4 2.5 %collective-permute-start.30 = (bf16[128,512]{1,0:T(8,128)(2,1)S(1)}, bf16[128,512]{1,0:T(8,128)(2,1)S(1)}, u32[]{:S(2)}, u32[]{:S(2)}) collective-permute-start(bf16[128,512]{1,0:T(8,128)(2,1)S(1)} %get-tuple-element.122), channel_id=1, source_target_pairs={{0,12},{4,0},{8,4},{12,8},{1,13},{5,1},{9,5},{13,9},{2,14},{6,2},{... | collective-permute-start | bytes 393224 | tf_op jit(solution)/shard_map/ppermute | solution.py:582
  144.8 0.7 query_subs.1
  145.6 0.6 collective-permute-done.28.refs_1_
  146.2 2.0 %collective-permute-start.26 = (bf16[128,512]{1,0:T(8,128)(2,1)S(1)}, bf16[128,512]{1,0:T(8,128)(2,1)S(1)}, u32[]{:S(2)}, u32[]{:S(2)}) collective-permute-start(bf16[128,512]{1,0:T(8,128)(2,1)S(1)} %get-tuple-element.117), channel_id=1, source_target_pairs={{0,8},{4,12},{8,0},{12,4},{1,9},{5,13},{9,1},{13,5},{2,10},{6,14},... | collective-permute-start | bytes 393224 | tf_op jit(solution)/shard_map/ppermute | solution.py:582
  148.2 3.8 %collective-permute-done.29.refs_2_ = bf16[128,512]{1,0:T(8,128)(2,1)S(1)} collective-permute-done((bf16[128,512]{1,0:T(8,128)(2,1)S(1)}, bf16[128,512]{1,0:T(8,128)(2,1)S(1)}, u32[]{:S(2)}, u32[]{:S(2)}) %collective-permute-start.29) | collective-permute-done | bytes 131104 | tf_op jit(solution)/shard_map/ppermute | solution.py:582
  152.0 5.5 %collective-permute-start.27 = (bf16[128,512]{1,0:T(8,128)(2,1)S(1)}, bf16[128,512]{1,0:T(8,128)(2,1)S(1)}, u32[]{:S(2)}, u32[]{:S(2)}) collective-permute-start(bf16[128,512]{1,0:T(8,128)(2,1)S(1)} %get-tuple-element.118), channel_id=1, source_target_pairs={{0,12},{4,0},{8,4},{12,8},{1,13},{5,1},{9,5},{13,9},{2,14},{6,2},{... | collective-permute-start | bytes 393224 | tf_op jit(solution)/shard_map/ppermute | solution.py:582
  157.5 1.8 %input_own.1.refs_2_.refs_4_ = bf16[1024,512]{1,0:T(8,128)(2,1)S(1)} custom-call(s32[4]{0:T(128)S(1)} %pad_add_fusion.refs_0_, bf16[1024,512]{1,0:T(8,128)(2,1)S(1)} %get-tuple-element.106.refs_2_.refs_1_, bf16[1024,512]{1,0:T(8,128)(2,1)S(1)} %get-tuple-element.112.refs_2_, bf16[1024,512]{1,0:T(8,128)(2,1)S(1)} %copy-done, bf16[1024,512]{1,0:T(8,128)(2,1)S(1)} %copy-done.3, ...), custom_call_target="tpu_custom_call" | custom-call | flops 1073741824 | bytes 5242896 | tf_op jit(solution)/shard_map/input_own/pallas_call | solution.py:554
  159.4 0.8 value_sum.1
  160.1 2.3 %input_sum.1 = (bf16[1024,512]{1,0:T(8,128)(2,1)}, bf16[128,512]{1,0:T(8,128)(2,1)S(1)}) custom-call(bf16[1024,1024]{1,0:T(8,128)(2,1)S(1)} %get-tuple-element.66.refs_9_.refs_0_, bf16[128,512]{1,0:T(8,128)(2,1)S(1)} %get-tuple-element.111.refs_5_.refs_1_, bf16[1024,512]{1,0:T(8,128)(2,1)S(1)} %input_own.1.refs_2_.refs_4_, ...), custom_call_target="tpu_custom_call" | custom-call | flops 1073741824 | bytes 5505024 | tf_op jit(solution)/shard_map/input_sum/pallas_call | solution.py:554
  162.4 0.2 collective-permute-done.26.refs_2_
  162.7 0.8 query_sum.1
  (42 shorter events, 0.4 us)
Async XLA Ops:
  0.6 9.7 %copy-start = (bf16[1024,512]{1,0:T(8,128)(2,1)S(1)}, bf16[1024,512]{1,0:T(8,128)(2,1)}, u32[]{:S(2)}) copy-start(bf16[1024,512]{1,0:T(8,128)(2,1)} %refs_3_.7) | copy-start | bytes 3145732
  0.6 9.7 %copy-start.1 = (bf16[1024,1024]{1,0:T(8,128)(2,1)S(1)}, bf16[1024,1024]{1,0:T(8,128)(2,1)}, u32[]{:S(2)}) copy-start(bf16[1024,1024]{1,0:T(8,128)(2,1)} %refs_2_.4) | copy-start | bytes 6291460
  0.7 9.7 %copy-start.4 = (s32[1024,1]{0,1:T(1,128)S(1)}, s32[1024,1]{0,1:T(1,128)}, u32[]{:S(2)}) copy-start(s32[1024,1]{0,1:T(1,128)} %param.9) | copy-start | bytes 12292
  6.1 34.5 %collective-permute-start = (bf16[1040,128]{1,0:T(8,128)(2,1)}, bf16[1040,128]{1,0:T(8,128)(2,1)S(1)}, u32[]{:S(2)}, u32[]{:S(2)}) collective-permute-start(bf16[1040,128]{1,0:T(8,128)(2,1)} %get-tuple-element.69), channel_id=1, source_target_pairs={{0,8},{8,0},{9,1},{4,12},{5,13},{12,4},{13,5},{1,9},{2,10},{10,2},... | collective-permute-start | bytes 798728 | tf_op jit(solution)/shard_map/ppermute | solution.py:576
  10.3 34.5 %collective-permute-start.1 = (bf16[1040,128]{1,0:T(8,128)(2,1)}, bf16[1040,128]{1,0:T(8,128)(2,1)}, u32[]{:S(2)}, u32[]{:S(2)}) collective-permute-start(bf16[1040,128]{1,0:T(8,128)(2,1)} %get-tuple-element.70), channel_id=1, source_target_pairs={{0,9},{8,1},{9,0},{4,13},{5,12},{12,5},{13,4},{1,8},{2,11},{10,3},... | collective-permute-start | bytes 798728 | tf_op jit(solution)/shard_map/ppermute | solution.py:576
  10.3 1.2 copy-start.2
  11.6 0.7 copy-start.5
  12.3 33.9 %copy-start.3 = (bf16[1024,512]{1,0:T(8,128)(2,1)S(1)}, bf16[1024,512]{1,0:T(8,128)(2,1)}, u32[]{:S(2)}) copy-start(bf16[1024,512]{1,0:T(8,128)(2,1)} %refs_4_.3) | copy-start | bytes 3145732
  17.1 35.1 %collective-permute-start.3 = (bf16[1040,128]{1,0:T(8,128)(2,1)S(1)}, bf16[1040,128]{1,0:T(8,128)(2,1)S(1)}, u32[]{:S(2)}, u32[]{:S(2)}) collective-permute-start(bf16[1040,128]{1,0:T(8,128)(2,1)S(1)} %get-tuple-element.71), channel_id=1, source_target_pairs={{0,5},{8,13},{9,12},{4,9},{5,8},{12,1},{13,0},{1,4},{2,7},{10,15},... | collective-permute-start | bytes 798728 | tf_op jit(solution)/shard_map/ppermute | solution.py:576
  18.8 33.5 %collective-permute-start.2 = (bf16[1040,128]{1,0:T(8,128)(2,1)S(1)}, bf16[1040,128]{1,0:T(8,128)(2,1)S(1)}, u32[]{:S(2)}, u32[]{:S(2)}) collective-permute-start(bf16[1040,128]{1,0:T(8,128)(2,1)S(1)} %get-tuple-element.65.refs_4_), channel_id=1, source_target_pairs={{0,4},{8,12},{9,13},{4,8},{5,9},{12,0},{13,1},{1,5},{2,6},{10,14},... | collective-permute-start | bytes 798728 | tf_op jit(solution)/shard_map/ppermute | solution.py:576
  20.3 35.6 %collective-permute-start.4 = (bf16[1040,128]{1,0:T(8,128)(2,1)S(1)}, bf16[1040,128]{1,0:T(8,128)(2,1)S(1)}, u32[]{:S(2)}, u32[]{:S(2)}) collective-permute-start(bf16[1040,128]{1,0:T(8,128)(2,1)S(1)} %get-tuple-element.72), channel_id=1, source_target_pairs={{0,12},{8,4},{9,5},{4,0},{5,1},{12,8},{13,9},{1,13},{2,14},{10,6},... | collective-permute-start | bytes 798728 | tf_op jit(solution)/shard_map/ppermute | solution.py:576
  40.6 15.3 %collective-permute-start.5 = (bf16[1040,128]{1,0:T(8,128)(2,1)S(1)}, bf16[1040,128]{1,0:T(8,128)(2,1)S(1)}, u32[]{:S(2)}, u32[]{:S(2)}) collective-permute-start(bf16[1040,128]{1,0:T(8,128)(2,1)S(1)} %get-tuple-element.73), channel_id=1, source_target_pairs={{0,13},{8,5},{9,4},{4,1},{5,0},{12,9},{13,8},{1,12},{2,15},{10,7},... | collective-permute-start | bytes 798728 | tf_op jit(solution)/shard_map/ppermute | solution.py:576
  44.8 11.2 %collective-permute-start.6 = (bf16[1040,128]{1,0:T(8,128)(2,1)S(1)}, bf16[1040,128]{1,0:T(8,128)(2,1)S(1)}, u32[]{:S(2)}, u32[]{:S(2)}) collective-permute-start(bf16[1040,128]{1,0:T(8,128)(2,1)S(1)} %get-tuple-element.74), channel_id=1, source_target_pairs={{0,1},{8,9},{9,8},{4,5},{5,4},{12,13},{13,12},{1,0},{2,3},{10,11},... | collective-permute-start | bytes 798728 | tf_op jit(solution)/shard_map/ppermute | solution.py:576
  52.2 8.4 %collective-permute-start.13 = (bf16[512,128]{1,0:T(8,128)(2,1)S(1)}, bf16[512,128]{1,0:T(8,128)(2,1)S(1)}, u32[]{:S(2)}, u32[]{:S(2)}) collective-permute-start(bf16[512,128]{1,0:T(8,128)(2,1)S(1)} %get-tuple-element.92), channel_id=1, source_target_pairs={{0,1},{8,9},{9,8},{4,5},{5,4},{12,13},{13,12},{1,0},{2,3},{10,11},... | collective-permute-start | bytes 393224 | tf_op jit(solution)/shard_map/ppermute | solution.py:576
  52.3 12.2 %collective-permute-start.12 = (bf16[512,128]{1,0:T(8,128)(2,1)S(1)}, bf16[512,128]{1,0:T(8,128)(2,1)S(1)}, u32[]{:S(2)}, u32[]{:S(2)}) collective-permute-start(bf16[512,128]{1,0:T(8,128)(2,1)S(1)} %get-tuple-element.90), channel_id=1, source_target_pairs={{0,13},{8,5},{9,4},{4,1},{5,0},{12,9},{13,8},{1,12},{2,15},{10,7},... | collective-permute-start | bytes 393224 | tf_op jit(solution)/shard_map/ppermute | solution.py:576
  55.9 22.7 %collective-permute-start.11 = (bf16[512,128]{1,0:T(8,128)(2,1)S(1)}, bf16[512,128]{1,0:T(8,128)(2,1)S(1)}, u32[]{:S(2)}, u32[]{:S(2)}) collective-permute-start(bf16[512,128]{1,0:T(8,128)(2,1)S(1)} %get-tuple-element.88), channel_id=1, source_target_pairs={{0,12},{8,4},{9,5},{4,0},{5,1},{12,8},{13,9},{1,13},{2,14},{10,6},... | collective-permute-start | bytes 393224 | tf_op jit(solution)/shard_map/ppermute | solution.py:576
  60.6 17.9 %collective-permute-start.10 = (bf16[512,128]{1,0:T(8,128)(2,1)S(1)}, bf16[512,128]{1,0:T(8,128)(2,1)S(1)}, u32[]{:S(2)}, u32[]{:S(2)}) collective-permute-start(bf16[512,128]{1,0:T(8,128)(2,1)S(1)} %get-tuple-element.86), channel_id=1, source_target_pairs={{0,5},{8,13},{9,12},{4,9},{5,8},{12,1},{13,0},{1,4},{2,7},{10,15},... | collective-permute-start | bytes 393224 | tf_op jit(solution)/shard_map/ppermute | solution.py:576
  60.6 17.9 %collective-permute-start.9 = (bf16[512,128]{1,0:T(8,128)(2,1)S(1)}, bf16[512,128]{1,0:T(8,128)(2,1)S(1)}, u32[]{:S(2)}, u32[]{:S(2)}) collective-permute-start(bf16[512,128]{1,0:T(8,128)(2,1)S(1)} %get-tuple-element.84), channel_id=1, source_target_pairs={{0,4},{8,12},{9,13},{4,8},{5,9},{12,0},{13,1},{1,5},{2,6},{10,14},... | collective-permute-start | bytes 393224 | tf_op jit(solution)/shard_map/ppermute | solution.py:576
  60.6 19.0 %collective-permute-start.8 = (bf16[512,128]{1,0:T(8,128)(2,1)S(1)}, bf16[512,128]{1,0:T(8,128)(2,1)S(1)}, u32[]{:S(2)}, u32[]{:S(2)}) collective-permute-start(bf16[512,128]{1,0:T(8,128)(2,1)S(1)} %get-tuple-element.82), channel_id=1, source_target_pairs={{0,9},{8,1},{9,0},{4,13},{5,12},{12,5},{13,4},{1,8},{2,11},{10,3},... | collective-permute-start | bytes 393224 | tf_op jit(solution)/shard_map/ppermute | solution.py:576
  64.5 18.4 %collective-permute-start.7 = (bf16[512,128]{1,0:T(8,128)(2,1)S(1)}, bf16[512,128]{1,0:T(8,128)(2,1)S(1)}, u32[]{:S(2)}, u32[]{:S(2)}) collective-permute-start(bf16[512,128]{1,0:T(8,128)(2,1)S(1)} %get-tuple-element.80), channel_id=1, source_target_pairs={{0,8},{8,0},{9,1},{4,12},{5,13},{12,4},{13,5},{1,9},{2,10},{10,2},... | collective-permute-start | bytes 393224 | tf_op jit(solution)/shard_map/ppermute | solution.py:576
  82.8 21.8 %collective-permute-start.14 = (bf16[2,512,128]{2,1,0:T(8,128)(2,1)S(1)}, bf16[2,512,128]{2,1,0:T(8,128)(2,1)S(1)}, u32[]{:S(2)}, u32[]{:S(2)}) collective-permute-start(bf16[2,512,128]{2,1,0:T(8,128)(2,1)S(1)} %get-tuple-element.94), channel_id=1, source_target_pairs={{0,4},{4,8},{8,12},{12,0},{1,5},{5,9},{9,13},{13,1},{2,6},{6,10},{... | collective-permute-start | bytes 786440 | tf_op jit(solution)/shard_map/ppermute | solution.py:582
  82.8 24.6 %collective-permute-start.15 = (bf16[2,512,128]{2,1,0:T(8,128)(2,1)S(1)}, bf16[2,512,128]{2,1,0:T(8,128)(2,1)S(1)}, u32[]{:S(2)}, u32[]{:S(2)}) collective-permute-start(bf16[2,512,128]{2,1,0:T(8,128)(2,1)S(1)} %get-tuple-element.95), channel_id=1, source_target_pairs={{0,8},{4,12},{8,0},{12,4},{1,9},{5,13},{9,1},{13,5},{2,10},{6,14},... | collective-permute-start | bytes 786440 | tf_op jit(solution)/shard_map/ppermute | solution.py:582
  84.3 23.1 %collective-permute-start.16 = (bf16[2,512,128]{2,1,0:T(8,128)(2,1)S(1)}, bf16[2,512,128]{2,1,0:T(8,128)(2,1)S(1)}, u32[]{:S(2)}, u32[]{:S(2)}) collective-permute-start(bf16[2,512,128]{2,1,0:T(8,128)(2,1)S(1)} %get-tuple-element.96), channel_id=1, source_target_pairs={{0,12},{4,0},{8,4},{12,8},{1,13},{5,1},{9,5},{13,9},{2,14},{6,2},{... | collective-permute-start | bytes 786440 | tf_op jit(solution)/shard_map/ppermute | solution.py:582
  102.4 11.5 %collective-permute-start.18 = (bf16[2,544,128]{2,1,0:T(8,128)(2,1)S(1)}, bf16[2,544,128]{2,1,0:T(8,128)(2,1)S(1)}, u32[]{:S(2)}, u32[]{:S(2)}) collective-permute-start(bf16[2,544,128]{2,1,0:T(8,128)(2,1)S(1)} %get-tuple-element.103), channel_id=1, source_target_pairs={{0,4},{4,8},{8,12},{12,0},{1,5},{5,9},{9,13},{13,1},{2,6},{6,10},{... | collective-permute-start | bytes 835592 | tf_op jit(solution)/shard_map/ppermute | solution.py:582
  103.0 24.5 %collective-permute-start.19 = (bf16[2,544,128]{2,1,0:T(8,128)(2,1)S(1)}, bf16[2,544,128]{2,1,0:T(8,128)(2,1)S(1)}, u32[]{:S(2)}, u32[]{:S(2)}) collective-permute-start(bf16[2,544,128]{2,1,0:T(8,128)(2,1)S(1)} %get-tuple-element.104), channel_id=1, source_target_pairs={{0,8},{4,12},{8,0},{12,4},{1,9},{5,13},{9,1},{13,5},{2,10},{6,14},... | collective-permute-start | bytes 835592 | tf_op jit(solution)/shard_map/ppermute | solution.py:582
  104.6 22.9 %collective-permute-start.20 = (bf16[2,544,128]{2,1,0:T(8,128)(2,1)S(1)}, bf16[2,544,128]{2,1,0:T(8,128)(2,1)S(1)}, u32[]{:S(2)}, u32[]{:S(2)}) collective-permute-start(bf16[2,544,128]{2,1,0:T(8,128)(2,1)S(1)} %get-tuple-element.105), channel_id=1, source_target_pairs={{0,12},{4,0},{8,4},{12,8},{1,13},{5,1},{9,5},{13,9},{2,14},{6,2},{... | collective-permute-start | bytes 835592 | tf_op jit(solution)/shard_map/ppermute | solution.py:582
  108.0 20.1 %collective-permute-start.17 = (bf16[4,512,128]{2,1,0:T(8,128)(2,1)S(1)}, bf16[4,512,128]{2,1,0:T(8,128)(2,1)S(1)}, u32[]{:S(2)}, u32[]{:S(2)}) collective-permute-start(bf16[4,512,128]{2,1,0:T(8,128)(2,1)S(1)} %swap_value.1), channel_id=1, source_target_pairs={{0,1},{1,0},{2,3},{3,2},{4,5},{5,4},{6,7},{7,6},{8,9},{9,8},{10,11... | collective-permute-start | bytes 1572872 | tf_op jit(solution)/shard_map/ppermute | solution.py:582
  128.1 3.1 %collective-permute-start.21 = (bf16[4,544,128]{2,1,0:T(8,128)(2,1)S(1)}, bf16[4,544,128]{2,1,0:T(8,128)(2,1)S(1)}, u32[]{:S(2)}, u32[]{:S(2)}) collective-permute-start(bf16[4,544,128]{2,1,0:T(8,128)(2,1)S(1)} %swap_query.1), channel_id=1, source_target_pairs={{0,1},{1,0},{2,3},{3,2},{4,5},{5,4},{6,7},{7,6},{8,9},{9,8},{10,11... | collective-permute-start | bytes 1671176 | tf_op jit(solution)/shard_map/ppermute | solution.py:582
  130.7 4.1 %collective-permute-start.22 = (bf16[4,128,512]{2,1,0:T(8,128)(2,1)S(1)}, bf16[4,128,512]{2,1,0:T(8,128)(2,1)S(1)}, u32[]{:S(2)}, u32[]{:S(2)}) collective-permute-start(bf16[4,128,512]{2,1,0:T(8,128)(2,1)S(1)} %get-tuple-element.108), channel_id=1, source_target_pairs={{0,1},{1,0},{2,3},{3,2},{4,5},{5,4},{6,7},{7,6},{8,9},{9,8},{10,11... | collective-permute-start | bytes 1572872 | tf_op jit(solution)/shard_map/ppermute | solution.py:582
  133.3 26.9 %collective-permute-start.24 = (bf16[1024,512]{1,0:T(8,128)(2,1)S(1)}, bf16[1024,512]{1,0:T(8,128)(2,1)S(1)}, u32[]{:S(2)}, u32[]{:S(2)}) collective-permute-start(bf16[1024,512]{1,0:T(8,128)(2,1)S(1)} %get-tuple-element.113), channel_id=1, source_target_pairs={{0,2},{2,0},{1,3},{3,1},{4,6},{6,4},{5,7},{7,5},{8,10},{10,8},{9,1... | collective-permute-start | bytes 3145736 | tf_op jit(solution)/shard_map/ppermute | solution.py:582
  136.7 8.1 %collective-permute-start.23 = (bf16[4,128,512]{2,1,0:T(8,128)(2,1)S(1)}, bf16[4,128,512]{2,1,0:T(8,128)(2,1)S(1)}, u32[]{:S(2)}, u32[]{:S(2)}) collective-permute-start(bf16[4,128,512]{2,1,0:T(8,128)(2,1)S(1)} %get-tuple-element.110), channel_id=1, source_target_pairs={{0,1},{1,0},{2,3},{3,2},{4,5},{5,4},{6,7},{7,6},{8,9},{9,8},{10,11... | collective-permute-start | bytes 1572872 | tf_op jit(solution)/shard_map/ppermute | solution.py:582
  136.8 9.4 %collective-permute-start.28 = (bf16[128,512]{1,0:T(8,128)(2,1)S(1)}, bf16[128,512]{1,0:T(8,128)(2,1)S(1)}, u32[]{:S(2)}, u32[]{:S(2)}) collective-permute-start(bf16[128,512]{1,0:T(8,128)(2,1)S(1)} %get-tuple-element.120), channel_id=1, source_target_pairs={{0,4},{4,8},{8,12},{12,0},{1,5},{5,9},{9,13},{13,1},{2,6},{6,10},{... | collective-permute-start | bytes 393224 | tf_op jit(solution)/shard_map/ppermute | solution.py:582
  142.4 9.6 %collective-permute-start.29 = (bf16[128,512]{1,0:T(8,128)(2,1)S(1)}, bf16[128,512]{1,0:T(8,128)(2,1)S(1)}, u32[]{:S(2)}, u32[]{:S(2)}) collective-permute-start(bf16[128,512]{1,0:T(8,128)(2,1)S(1)} %get-tuple-element.121), channel_id=1, source_target_pairs={{0,8},{4,12},{8,0},{12,4},{1,9},{5,13},{9,1},{13,5},{2,10},{6,14},... | collective-permute-start | bytes 393224 | tf_op jit(solution)/shard_map/ppermute | solution.py:582
  142.4 17.0 %collective-permute-start.30 = (bf16[128,512]{1,0:T(8,128)(2,1)S(1)}, bf16[128,512]{1,0:T(8,128)(2,1)S(1)}, u32[]{:S(2)}, u32[]{:S(2)}) collective-permute-start(bf16[128,512]{1,0:T(8,128)(2,1)S(1)} %get-tuple-element.122), channel_id=1, source_target_pairs={{0,12},{4,0},{8,4},{12,8},{1,13},{5,1},{9,5},{13,9},{2,14},{6,2},{... | collective-permute-start | bytes 393224 | tf_op jit(solution)/shard_map/ppermute | solution.py:582
  145.5 16.9 %collective-permute-start.25 = (bf16[128,512]{1,0:T(8,128)(2,1)S(1)}, bf16[128,512]{1,0:T(8,128)(2,1)S(1)}, u32[]{:S(2)}, u32[]{:S(2)}) collective-permute-start(bf16[128,512]{1,0:T(8,128)(2,1)S(1)} %get-tuple-element.116), channel_id=1, source_target_pairs={{0,4},{4,8},{8,12},{12,0},{1,5},{5,9},{9,13},{13,1},{2,6},{6,10},{... | collective-permute-start | bytes 393224 | tf_op jit(solution)/shard_map/ppermute | solution.py:582
  146.2 16.5 %collective-permute-start.26 = (bf16[128,512]{1,0:T(8,128)(2,1)S(1)}, bf16[128,512]{1,0:T(8,128)(2,1)S(1)}, u32[]{:S(2)}, u32[]{:S(2)}) collective-permute-start(bf16[128,512]{1,0:T(8,128)(2,1)S(1)} %get-tuple-element.117), channel_id=1, source_target_pairs={{0,8},{4,12},{8,0},{12,4},{1,9},{5,13},{9,1},{13,5},{2,10},{6,14},... | collective-permute-start | bytes 393224 | tf_op jit(solution)/shard_map/ppermute | solution.py:582
  152.0 10.7 %collective-permute-start.27 = (bf16[128,512]{1,0:T(8,128)(2,1)S(1)}, bf16[128,512]{1,0:T(8,128)(2,1)S(1)}, u32[]{:S(2)}, u32[]{:S(2)}) collective-permute-start(bf16[128,512]{1,0:T(8,128)(2,1)S(1)} %get-tuple-element.118), channel_id=1, source_target_pairs={{0,12},{4,0},{8,4},{12,8},{1,13},{5,1},{9,5},{13,9},{2,14},{6,2},{... | collective-permute-start | bytes 393224 | tf_op jit(solution)/shard_map/ppermute | solution.py:582

commit v23 on v22

--- a/solution.py
+++ b/solution.py
@@ -586,6 +586,11 @@
     return [parts[0]] + [shift(parts[ahead], axis, ahead) for ahead in range(1, len(parts))]
 
 
+def far_first(terms):
+    size = len(terms)
+    return [terms[0]] + [terms[k] for k in sorted(range(1, size), key=lambda k: -min(k, size - k))]
+
+
 def exchange_by_chip(me, parts, sizes, name, after=()):
     came = pass_round(parts, "seq")
     swapped = call(
@@ -747,7 +752,7 @@
         flops=weight_flops,
         name="query_weight",
     )
-    query_weight, value_weight = refs[: sizes[1]], pass_round(refs[sizes[1] :], "seq")
+    query_weight, value_weight = refs[: sizes[1]], far_first(pass_round(refs[sizes[1] :], "seq"))
     query_weight = fold_subs(me, query_weight, "query_subs")
     own = call(
         functools.partial(input_own_kernel, parts),
@@ -757,7 +762,7 @@
         flops=weight_flops * 2 // parts,
         name="input_own",
     )
-    query_weight = pass_round(query_weight, "seq")
+    query_weight = far_first(pass_round(query_weight, "seq"))
     grad_wv = add_up(value_weight, F32, "value_sum", [own])
     grad_input, own_weight = call(
         input_sum_kernel,

time: 165 us -> 166 us (level); the launches traced: 163 us -> 166 us
  transfers between devices with their start and end apart: 31 -> 31, of which waited for: 9 -> 9; matrix products, arithmetic and copies ran while one was open for 0% -> 0% of each run, Pallas kernels for 33% -> 32%
where the time goes in v23:
time: 166 us
  Pallas kernels  59.6 us (36%)
  waiting for transfers between devices  52.1 us (31%)
  starting transfers between devices  51.7 us (31%)
  local copies, waits for them, and re-layouts  1.92 us (1%)
    pallas_call x15, Pallas kernels, call(): pl.pallas_call(body, out_shape=outs, in_specs=specs, out_specs=jax.tree.m...  59.6 us
    ppermute x17, starting transfers between devices, shift(): lax.ppermute(part, axis, [(i, (i + ahead) % size) for i in range(size)])  27.8 us
    ppermute x14, waiting for transfers between devices, exchange(): out.append(part if ahead == (0, 0) else lax.ppermute(part, OWNERS, moves))  26.4 us
    ppermute x17, waiting for transfers between devices, shift(): lax.ppermute(part, axis, [(i, (i + ahead) % size) for i in range(size)])  25.7 us
    ppermute x14, starting transfers between devices, exchange(): out.append(part if ahead == (0, 0) else lax.ppermute(part, OWNERS, moves))  23.9 us
  transfers between devices with their start and end apart: 31, of which 9 were waited for; matrix products, arithmetic and copies ran while one was open for 0% of the time, Pallas kernels for 32%

profile of v23, /device:TPU:0, one launch (start us, length us, event | category | flops | bytes accessed | tf_op | source)
XLA Modules:
  0.0 166.2 jit_solution(2816016533886190447)
XLA Ops:
  0.7 5.5 %project_far.1 = (bf16[1040,128]{1,0:T(8,128)(2,1)}, bf16[1040,128]{1,0:T(8,128)(2,1)}, s32[1,1024]{1,0:T(1,128)}) custom-call(s32[1,1024]{1,0:T(1,128)} %bitcast.5, bf16[1024,1024]{1,0:T(8,128)(2,1)} %refs_2_.4, bf16[1024,512]{1,0:T(8,128)(2,1)} %refs_3_.7, bf16[1024,512]{1,0:T(8,128)(2,1)} %refs_5_.1), custom_call_target="tpu_custom_call" | custom-call | flops 805306368 | bytes 4734976 | tf_op jit(solution)/shard_map/project_far/pallas_call | solution.py:554
  6.1 4.1 %collective-permute-start = (bf16[1040,128]{1,0:T(8,128)(2,1)}, bf16[1040,128]{1,0:T(8,128)(2,1)S(1)}, u32[]{:S(2)}, u32[]{:S(2)}) collective-permute-start(bf16[1040,128]{1,0:T(8,128)(2,1)} %get-tuple-element.69), channel_id=1, source_target_pairs={{0,8},{8,0},{9,1},{4,12},{5,13},{12,4},{13,5},{1,9},{2,10},{10,2},... | collective-permute-start | bytes 798728 | tf_op jit(solution)/shard_map/ppermute | solution.py:576
  10.4 1.2 copy-done.2
  11.6 0.7 copy-done.5
  12.3 4.8 %project_query.1 = (bf16[1040,128]{1,0:T(8,128)(2,1)S(1)}, bf16[1040,128]{1,0:T(8,128)(2,1)S(1)}, bf16[1040,128]{1,0:T(8,128)(2,1)S(1)}, bf16[1040,128]{1,0:T(8,...) custom-call(s32[4]{0:T(128)S(1)} %pad_add_fusion.refs_0_, s32[1,1024]{1,0:T(1,128)S(1)} %copy-done.5, ...), custom_call_target="tpu_custom_call" | custom-call | flops 3221225472 | bytes 5799952 | tf_op jit(solution)/shard_map/project_query/pallas_call | solution.py:554
  17.1 1.7 %collective-permute-start.3 = (bf16[1040,128]{1,0:T(8,128)(2,1)S(1)}, bf16[1040,128]{1,0:T(8,128)(2,1)S(1)}, u32[]{:S(2)}, u32[]{:S(2)}) collective-permute-start(bf16[1040,128]{1,0:T(8,128)(2,1)S(1)} %get-tuple-element.71), channel_id=1, source_target_pairs={{0,5},{8,13},{9,12},{4,9},{5,8},{12,1},{13,0},{1,4},{2,7},{10,15},... | collective-permute-start | bytes 798728 | tf_op jit(solution)/shard_map/ppermute | solution.py:576
  18.8 1.6 collective-permute-start.2
  20.3 2.2 %collective-permute-start.4 = (bf16[1040,128]{1,0:T(8,128)(2,1)S(1)}, bf16[1040,128]{1,0:T(8,128)(2,1)S(1)}, u32[]{:S(2)}, u32[]{:S(2)}) collective-permute-start(bf16[1040,128]{1,0:T(8,128)(2,1)S(1)} %get-tuple-element.72), channel_id=1, source_target_pairs={{0,12},{8,4},{9,5},{4,0},{5,1},{12,8},{13,9},{1,13},{2,14},{10,6},... | collective-permute-start | bytes 798728 | tf_op jit(solution)/shard_map/ppermute | solution.py:576
  22.6 18.0 %collective-permute-done.refs_2_ = bf16[1040,128]{1,0:T(8,128)(2,1)S(1)} collective-permute-done((bf16[1040,128]{1,0:T(8,128)(2,1)}, bf16[1040,128]{1,0:T(8,128)(2,1)S(1)}, u32[]{:S(2)}, u32[]{:S(2)}) %collective-permute-start) | collective-permute-done | bytes 266272 | tf_op jit(solution)/shard_map/ppermute | solution.py:576
  40.6 4.1 %collective-permute-done.1.refs_3_ = bf16[1040,128]{1,0:T(8,128)(2,1)} collective-permute-done((bf16[1040,128]{1,0:T(8,128)(2,1)}, bf16[1040,128]{1,0:T(8,128)(2,1)}, u32[]{:S(2)}, u32[]{:S(2)}) %collective-permute-start.1) | collective-permute-done | bytes 266272 | tf_op jit(solution)/shard_map/ppermute | solution.py:576
  44.8 1.4 collective-permute-start.6
  46.2 6.0 %project_value.1 = (bf16[512,128]{1,0:T(8,128)(2,1)S(1)}, bf16[512,128]{1,0:T(8,128)(2,1)S(1)}, bf16[512,128]{1,0:T(8,128)(2,1)S(1)}, bf16[512,128]{1,0:T(8,128)...) custom-call(s32[4]{0:T(128)S(1)} %pad_add_fusion.refs_0_, ...), custom_call_target="tpu_custom_call" | custom-call | flops 2147483648 | bytes 8392720 | tf_op jit(solution)/shard_map/project_value/pallas_call | solution.py:554
  52.3 3.6 %collective-permute-start.12 = (bf16[512,128]{1,0:T(8,128)(2,1)S(1)}, bf16[512,128]{1,0:T(8,128)(2,1)S(1)}, u32[]{:S(2)}, u32[]{:S(2)}) collective-permute-start(bf16[512,128]{1,0:T(8,128)(2,1)S(1)} %get-tuple-element.90), channel_id=1, source_target_pairs={{0,13},{8,5},{9,4},{4,1},{5,0},{12,9},{13,8},{1,12},{2,15},{10,7},... | collective-permute-start | bytes 393224 | tf_op jit(solution)/shard_map/ppermute | solution.py:576
  55.9 4.7 %collective-permute-start.11 = (bf16[512,128]{1,0:T(8,128)(2,1)S(1)}, bf16[512,128]{1,0:T(8,128)(2,1)S(1)}, u32[]{:S(2)}, u32[]{:S(2)}) collective-permute-start(bf16[512,128]{1,0:T(8,128)(2,1)S(1)} %get-tuple-element.88), channel_id=1, source_target_pairs={{0,12},{8,4},{9,5},{4,0},{5,1},{12,8},{13,9},{1,13},{2,14},{10,6},... | collective-permute-start | bytes 393224 | tf_op jit(solution)/shard_map/ppermute | solution.py:576
  60.6 3.8 %collective-permute-start.8 = (bf16[512,128]{1,0:T(8,128)(2,1)S(1)}, bf16[512,128]{1,0:T(8,128)(2,1)S(1)}, u32[]{:S(2)}, u32[]{:S(2)}) collective-permute-start(bf16[512,128]{1,0:T(8,128)(2,1)S(1)} %get-tuple-element.82), channel_id=1, source_target_pairs={{0,9},{8,1},{9,0},{4,13},{5,12},{12,5},{13,4},{1,8},{2,11},{10,3},... | collective-permute-start | bytes 393224 | tf_op jit(solution)/shard_map/ppermute | solution.py:576
  64.5 0.6 collective-permute-start.7
  65.1 13.5 %value_grad.1 = (bf16[2,512,128]{2,1,0:T(8,128)(2,1)S(1)}, bf16[2,512,128]{2,1,0:T(8,128)(2,1)S(1)}, bf16[2,512,128]{2,1,0:T(8,128)(2,1)S(1)}, bf16[2,512,128]{2...) custom-call(s32[4]{0:T(128)S(1)} %pad_add_fusion.refs_0_, ...), custom_call_target="tpu_custom_call" | custom-call | flops 2147483648 | bytes 8163344 | tf_op jit(solution)/shard_map/value_grad/pallas_call | solution.py:554
  78.6 1.1 collective-permute-done.8.refs_5_
  79.6 3.2 %collective-permute-done.7.refs_4_ = bf16[512,128]{1,0:T(8,128)(2,1)S(1)} collective-permute-done((bf16[512,128]{1,0:T(8,128)(2,1)S(1)}, bf16[512,128]{1,0:T(8,128)(2,1)S(1)}, u32[]{:S(2)}, u32[]{:S(2)}) %collective-permute-start.7) | collective-permute-done | bytes 131104 | tf_op jit(solution)/shard_map/ppermute | solution.py:576
  82.8 1.5 collective-permute-start.15
  84.3 2.3 %collective-permute-start.16 = (bf16[2,512,128]{2,1,0:T(8,128)(2,1)S(1)}, bf16[2,512,128]{2,1,0:T(8,128)(2,1)S(1)}, u32[]{:S(2)}, u32[]{:S(2)}) collective-permute-start(bf16[2,512,128]{2,1,0:T(8,128)(2,1)S(1)} %get-tuple-element.96), channel_id=1, source_target_pairs={{0,12},{4,0},{8,4},{12,8},{1,13},{5,1},{9,5},{13,9},{2,14},{6,2},{... | collective-permute-start | bytes 786440 | tf_op jit(solution)/shard_map/ppermute | solution.py:582
  86.6 15.8 %query_grad.1 = (bf16[2,544,128]{2,1,0:T(8,128)(2,1)S(1)}, bf16[2,544,128]{2,1,0:T(8,128)(2,1)S(1)}, bf16[2,544,128]{2,1,0:T(8,128)(2,1)S(1)}, bf16[2,544,128]{2,1,0:T(8,128)(2,1)S(1)}) custom-call(s32[4]{0:T(128)S(1)} %pad_add_fusion.refs_0_, s32[8,128]{1,0:T(8,128)S(1)} %get-tuple-element.97.refs_1_, bf16[19456,128]{1,0:T(8,128)(2,1)} %get-tuple-element.98.refs_2_, ...), custom_call_target="tpu_custom_call" | custom-call | flops 3221225472 | bytes 7147536 | tf_op jit(solution)/shard_map/query_grad/pallas_call | solution.py:554
  102.4 0.6 collective-permute-start.18
  103.0 1.5 collective-permute-start.19
  104.6 2.8 %collective-permute-start.20 = (bf16[2,544,128]{2,1,0:T(8,128)(2,1)S(1)}, bf16[2,544,128]{2,1,0:T(8,128)(2,1)S(1)}, u32[]{:S(2)}, u32[]{:S(2)}) collective-permute-start(bf16[2,544,128]{2,1,0:T(8,128)(2,1)S(1)} %get-tuple-element.105), channel_id=1, source_target_pairs={{0,12},{4,0},{8,4},{12,8},{1,13},{5,1},{9,5},{13,9},{2,14},{6,2},{... | collective-permute-start | bytes 835592 | tf_op jit(solution)/shard_map/ppermute | solution.py:582
  107.4 0.6 swap_value.1
  108.1 5.9 %collective-permute-done.18.refs_2_.refs_4_ = bf16[2,544,128]{2,1,0:T(8,128)(2,1)S(1)} collective-permute-done((bf16[2,544,128]{2,1,0:T(8,128)(2,1)S(1)}, bf16[2,544,128]{2,1,0:T(8,128)(2,1)S(1)}, u32[]{:S(2)}, u32[]{:S(2)}) %collective-permute-start.18) | collective-permute-done | bytes 278560 | tf_op jit(solution)/shard_map/ppermute | solution.py:582
  114.0 13.5 %collective-permute-done.19.refs_3_.refs_5_ = bf16[2,544,128]{2,1,0:T(8,128)(2,1)S(1)} collective-permute-done((bf16[2,544,128]{2,1,0:T(8,128)(2,1)S(1)}, bf16[2,544,128]{2,1,0:T(8,128)(2,1)S(1)}, u32[]{:S(2)}, u32[]{:S(2)}) %collective-permute-start.19) | collective-permute-done | bytes 278560 | tf_op jit(solution)/shard_map/ppermute | solution.py:582
  127.5 0.6 swap_query.1
  128.2 2.5 %value_home.1 = (bf16[1024,512]{1,0:T(8,128)(2,1)S(1)}, f32[1024,512]{1,0:T(8,128)S(1)}, bf16[4,128,512]{2,1,0:T(8,128)(2,1)S(1)}, bf16[4,128,512]{2,1,0:T(8,128)(2,1)S(1)}) custom-call(s32[4]{0:T(128)S(1)} %pad_add_fusion.refs_0_, bf16[1024,1024]{1,0:T(8,128)(2,1)S(1)} %get-tuple-element.67.refs_1_, bf16[1024,512]{1,0:T(8,128)(2,1)S(1)} %copy-done.3, ...), custom_call_target="tpu_custom_call" | custom-call | flops 1610612736 | bytes 8912912 | tf_op jit(solution)/shard_map/value_home/pallas_call | solution.py:554
  130.7 0.5 collective-permute-start.22
  131.2 2.0 %query_home.1 = (bf16[1024,512]{1,0:T(8,128)(2,1)S(1)}, bf16[1024,512]{1,0:T(8,128)(2,1)S(1)}, f32[64,512]{1,0:T(8,128)}) custom-call(s32[4]{0:T(128)S(1)} %pad_add_fusion.refs_0_, bf16[1024,512]{1,0:T(8,128)(2,1)S(1)} %copy-done, f32[1024,512]{1,0:T(8,128)S(1)} %get-tuple-element.102.refs_2_, ...), custom_call_target="tpu_custom_call" | custom-call | flops 536870912 | bytes 7045136 | tf_op jit(solution)/shard_map/query_home/pallas_call | solution.py:554
  133.3 1.5 collective-permute-start.24
  134.8 2.0 %query_weight.1 = (bf16[4,128,512]{2,1,0:T(8,128)(2,1)S(1)}, bf16[4,128,512]{2,1,0:T(8,128)(2,1)S(1)}, bf16[128,512]{1,0:T(8,128)(2,1)S(1)}, bf16[128,512]{1,0:T...) custom-call(s32[4]{0:T(128)S(1)} %pad_add_fusion.refs_0_, ...), custom_call_target="tpu_custom_call" | custom-call | flops 1073741824 | bytes 5767184 | tf_op jit(solution)/shard_map/query_weight/pallas_call | solution.py:554
  136.8 4.5 %collective-permute-start.28 = (bf16[128,512]{1,0:T(8,128)(2,1)S(1)}, bf16[128,512]{1,0:T(8,128)(2,1)S(1)}, u32[]{:S(2)}, u32[]{:S(2)}) collective-permute-start(bf16[128,512]{1,0:T(8,128)(2,1)S(1)} %get-tuple-element.120), channel_id=1, source_target_pairs={{0,8},{4,12},{8,0},{12,4},{1,9},{5,13},{9,1},{13,5},{2,10},{6,14},... | collective-permute-start | bytes 393224 | tf_op jit(solution)/shard_map/ppermute | solution.py:582
  141.4 1.1 collective-permute-start.29
  142.5 2.7 %collective-permute-start.30 = (bf16[128,512]{1,0:T(8,128)(2,1)S(1)}, bf16[128,512]{1,0:T(8,128)(2,1)S(1)}, u32[]{:S(2)}, u32[]{:S(2)}) collective-permute-start(bf16[128,512]{1,0:T(8,128)(2,1)S(1)} %get-tuple-element.122), channel_id=1, source_target_pairs={{0,12},{4,0},{8,4},{12,8},{1,13},{5,1},{9,5},{13,9},{2,14},{6,2},{... | collective-permute-start | bytes 393224 | tf_op jit(solution)/shard_map/ppermute | solution.py:582
  145.2 0.7 query_subs.1
  145.9 0.2 collective-permute-start.25
  146.1 3.6 %collective-permute-start.26 = (bf16[128,512]{1,0:T(8,128)(2,1)S(1)}, bf16[128,512]{1,0:T(8,128)(2,1)S(1)}, u32[]{:S(2)}, u32[]{:S(2)}) collective-permute-start(bf16[128,512]{1,0:T(8,128)(2,1)S(1)} %get-tuple-element.117), channel_id=1, source_target_pairs={{0,4},{4,8},{8,12},{12,0},{1,5},{5,9},{9,13},{13,1},{2,6},{6,10},{... | collective-permute-start | bytes 393224 | tf_op jit(solution)/shard_map/ppermute | solution.py:582
  149.7 2.2 %collective-permute-done.29.refs_2_ = bf16[128,512]{1,0:T(8,128)(2,1)S(1)} collective-permute-done((bf16[128,512]{1,0:T(8,128)(2,1)S(1)}, bf16[128,512]{1,0:T(8,128)(2,1)S(1)}, u32[]{:S(2)}, u32[]{:S(2)}) %collective-permute-start.29) | collective-permute-done | bytes 131104 | tf_op jit(solution)/shard_map/ppermute | solution.py:582
  151.9 4.6 %collective-permute-start.27 = (bf16[128,512]{1,0:T(8,128)(2,1)S(1)}, bf16[128,512]{1,0:T(8,128)(2,1)S(1)}, u32[]{:S(2)}, u32[]{:S(2)}) collective-permute-start(bf16[128,512]{1,0:T(8,128)(2,1)S(1)} %get-tuple-element.118), channel_id=1, source_target_pairs={{0,12},{4,0},{8,4},{12,8},{1,13},{5,1},{9,5},{13,9},{2,14},{6,2},{... | collective-permute-start | bytes 393224 | tf_op jit(solution)/shard_map/ppermute | solution.py:582
  156.4 1.8 %input_own.1.refs_2_.refs_4_ = bf16[1024,512]{1,0:T(8,128)(2,1)S(1)} custom-call(s32[4]{0:T(128)S(1)} %pad_add_fusion.refs_0_, bf16[1024,512]{1,0:T(8,128)(2,1)S(1)} %get-tuple-element.106.refs_2_.refs_1_, bf16[1024,512]{1,0:T(8,128)(2,1)S(1)} %get-tuple-element.112.refs_2_, bf16[1024,512]{1,0:T(8,128)(2,1)S(1)} %copy-done, bf16[1024,512]{1,0:T(8,128)(2,1)S(1)} %copy-done.3, ...), custom_call_target="tpu_custom_call" | custom-call | flops 1073741824 | bytes 5242896 | tf_op jit(solution)/shard_map/input_own/pallas_call | solution.py:554
  158.3 0.8 value_sum.1
  159.1 2.3 %input_sum.1 = (bf16[1024,512]{1,0:T(8,128)(2,1)}, bf16[128,512]{1,0:T(8,128)(2,1)S(1)}) custom-call(bf16[1024,1024]{1,0:T(8,128)(2,1)S(1)} %get-tuple-element.66.refs_9_.refs_0_, bf16[128,512]{1,0:T(8,128)(2,1)S(1)} %get-tuple-element.111.refs_5_.refs_1_, bf16[1024,512]{1,0:T(8,128)(2,1)S(1)} %input_own.1.refs_2_.refs_4_, ...), custom_call_target="tpu_custom_call" | custom-call | flops 1073741824 | bytes 5505024 | tf_op jit(solution)/shard_map/input_sum/pallas_call | solution.py:554
  161.4 1.4 collective-permute-done.25.refs_1_
  162.7 2.7 %collective-permute-done.27.refs_3_ = bf16[128,512]{1,0:T(8,128)(2,1)S(1)} collective-permute-done((bf16[128,512]{1,0:T(8,128)(2,1)S(1)}, bf16[128,512]{1,0:T(8,128)(2,1)S(1)}, u32[]{:S(2)}, u32[]{:S(2)}) %collective-permute-start.27) | collective-permute-done | bytes 131104 | tf_op jit(solution)/shard_map/ppermute | solution.py:582
  165.4 0.8 query_sum.1
  (42 shorter events, 0.5 us)
Async XLA Ops:
  0.6 9.7 %copy-start = (bf16[1024,512]{1,0:T(8,128)(2,1)S(1)}, bf16[1024,512]{1,0:T(8,128)(2,1)}, u32[]{:S(2)}) copy-start(bf16[1024,512]{1,0:T(8,128)(2,1)} %refs_3_.7) | copy-start | bytes 3145732
  0.6 9.7 %copy-start.1 = (bf16[1024,1024]{1,0:T(8,128)(2,1)S(1)}, bf16[1024,1024]{1,0:T(8,128)(2,1)}, u32[]{:S(2)}) copy-start(bf16[1024,1024]{1,0:T(8,128)(2,1)} %refs_2_.4) | copy-start | bytes 6291460
  0.7 9.7 %copy-start.4 = (s32[1024,1]{0,1:T(1,128)S(1)}, s32[1024,1]{0,1:T(1,128)}, u32[]{:S(2)}) copy-start(s32[1024,1]{0,1:T(1,128)} %param.9) | copy-start | bytes 12292
  6.1 34.5 %collective-permute-start = (bf16[1040,128]{1,0:T(8,128)(2,1)}, bf16[1040,128]{1,0:T(8,128)(2,1)S(1)}, u32[]{:S(2)}, u32[]{:S(2)}) collective-permute-start(bf16[1040,128]{1,0:T(8,128)(2,1)} %get-tuple-element.69), channel_id=1, source_target_pairs={{0,8},{8,0},{9,1},{4,12},{5,13},{12,4},{13,5},{1,9},{2,10},{10,2},... | collective-permute-start | bytes 798728 | tf_op jit(solution)/shard_map/ppermute | solution.py:576
  10.3 34.5 %collective-permute-start.1 = (bf16[1040,128]{1,0:T(8,128)(2,1)}, bf16[1040,128]{1,0:T(8,128)(2,1)}, u32[]{:S(2)}, u32[]{:S(2)}) collective-permute-start(bf16[1040,128]{1,0:T(8,128)(2,1)} %get-tuple-element.70), channel_id=1, source_target_pairs={{0,9},{8,1},{9,0},{4,13},{5,12},{12,5},{13,4},{1,8},{2,11},{10,3},... | collective-permute-start | bytes 798728 | tf_op jit(solution)/shard_map/ppermute | solution.py:576
  10.3 1.2 copy-start.2
  11.6 0.7 copy-start.5
  12.3 33.9 %copy-start.3 = (bf16[1024,512]{1,0:T(8,128)(2,1)S(1)}, bf16[1024,512]{1,0:T(8,128)(2,1)}, u32[]{:S(2)}) copy-start(bf16[1024,512]{1,0:T(8,128)(2,1)} %refs_4_.3) | copy-start | bytes 3145732
  17.1 35.1 %collective-permute-start.3 = (bf16[1040,128]{1,0:T(8,128)(2,1)S(1)}, bf16[1040,128]{1,0:T(8,128)(2,1)S(1)}, u32[]{:S(2)}, u32[]{:S(2)}) collective-permute-start(bf16[1040,128]{1,0:T(8,128)(2,1)S(1)} %get-tuple-element.71), channel_id=1, source_target_pairs={{0,5},{8,13},{9,12},{4,9},{5,8},{12,1},{13,0},{1,4},{2,7},{10,15},... | collective-permute-start | bytes 798728 | tf_op jit(solution)/shard_map/ppermute | solution.py:576
  18.8 33.5 %collective-permute-start.2 = (bf16[1040,128]{1,0:T(8,128)(2,1)S(1)}, bf16[1040,128]{1,0:T(8,128)(2,1)S(1)}, u32[]{:S(2)}, u32[]{:S(2)}) collective-permute-start(bf16[1040,128]{1,0:T(8,128)(2,1)S(1)} %get-tuple-element.65.refs_4_), channel_id=1, source_target_pairs={{0,4},{8,12},{9,13},{4,8},{5,9},{12,0},{13,1},{1,5},{2,6},{10,14},... | collective-permute-start | bytes 798728 | tf_op jit(solution)/shard_map/ppermute | solution.py:576
  20.3 35.6 %collective-permute-start.4 = (bf16[1040,128]{1,0:T(8,128)(2,1)S(1)}, bf16[1040,128]{1,0:T(8,128)(2,1)S(1)}, u32[]{:S(2)}, u32[]{:S(2)}) collective-permute-start(bf16[1040,128]{1,0:T(8,128)(2,1)S(1)} %get-tuple-element.72), channel_id=1, source_target_pairs={{0,12},{8,4},{9,5},{4,0},{5,1},{12,8},{13,9},{1,13},{2,14},{10,6},... | collective-permute-start | bytes 798728 | tf_op jit(solution)/shard_map/ppermute | solution.py:576
  40.6 15.3 %collective-permute-start.5 = (bf16[1040,128]{1,0:T(8,128)(2,1)S(1)}, bf16[1040,128]{1,0:T(8,128)(2,1)S(1)}, u32[]{:S(2)}, u32[]{:S(2)}) collective-permute-start(bf16[1040,128]{1,0:T(8,128)(2,1)S(1)} %get-tuple-element.73), channel_id=1, source_target_pairs={{0,13},{8,5},{9,4},{4,1},{5,0},{12,9},{13,8},{1,12},{2,15},{10,7},... | collective-permute-start | bytes 798728 | tf_op jit(solution)/shard_map/ppermute | solution.py:576
  44.8 11.2 %collective-permute-start.6 = (bf16[1040,128]{1,0:T(8,128)(2,1)S(1)}, bf16[1040,128]{1,0:T(8,128)(2,1)S(1)}, u32[]{:S(2)}, u32[]{:S(2)}) collective-permute-start(bf16[1040,128]{1,0:T(8,128)(2,1)S(1)} %get-tuple-element.74), channel_id=1, source_target_pairs={{0,1},{8,9},{9,8},{4,5},{5,4},{12,13},{13,12},{1,0},{2,3},{10,11},... | collective-permute-start | bytes 798728 | tf_op jit(solution)/shard_map/ppermute | solution.py:576
  52.2 8.4 %collective-permute-start.13 = (bf16[512,128]{1,0:T(8,128)(2,1)S(1)}, bf16[512,128]{1,0:T(8,128)(2,1)S(1)}, u32[]{:S(2)}, u32[]{:S(2)}) collective-permute-start(bf16[512,128]{1,0:T(8,128)(2,1)S(1)} %get-tuple-element.92), channel_id=1, source_target_pairs={{0,1},{8,9},{9,8},{4,5},{5,4},{12,13},{13,12},{1,0},{2,3},{10,11},... | collective-permute-start | bytes 393224 | tf_op jit(solution)/shard_map/ppermute | solution.py:576
  52.3 12.2 %collective-permute-start.12 = (bf16[512,128]{1,0:T(8,128)(2,1)S(1)}, bf16[512,128]{1,0:T(8,128)(2,1)S(1)}, u32[]{:S(2)}, u32[]{:S(2)}) collective-permute-start(bf16[512,128]{1,0:T(8,128)(2,1)S(1)} %get-tuple-element.90), channel_id=1, source_target_pairs={{0,13},{8,5},{9,4},{4,1},{5,0},{12,9},{13,8},{1,12},{2,15},{10,7},... | collective-permute-start | bytes 393224 | tf_op jit(solution)/shard_map/ppermute | solution.py:576
  55.9 22.7 %collective-permute-start.11 = (bf16[512,128]{1,0:T(8,128)(2,1)S(1)}, bf16[512,128]{1,0:T(8,128)(2,1)S(1)}, u32[]{:S(2)}, u32[]{:S(2)}) collective-permute-start(bf16[512,128]{1,0:T(8,128)(2,1)S(1)} %get-tuple-element.88), channel_id=1, source_target_pairs={{0,12},{8,4},{9,5},{4,0},{5,1},{12,8},{13,9},{1,13},{2,14},{10,6},... | collective-permute-start | bytes 393224 | tf_op jit(solution)/shard_map/ppermute | solution.py:576
  60.6 17.9 %collective-permute-start.10 = (bf16[512,128]{1,0:T(8,128)(2,1)S(1)}, bf16[512,128]{1,0:T(8,128)(2,1)S(1)}, u32[]{:S(2)}, u32[]{:S(2)}) collective-permute-start(bf16[512,128]{1,0:T(8,128)(2,1)S(1)} %get-tuple-element.86), channel_id=1, source_target_pairs={{0,5},{8,13},{9,12},{4,9},{5,8},{12,1},{13,0},{1,4},{2,7},{10,15},... | collective-permute-start | bytes 393224 | tf_op jit(solution)/shard_map/ppermute | solution.py:576
  60.6 17.9 %collective-permute-start.9 = (bf16[512,128]{1,0:T(8,128)(2,1)S(1)}, bf16[512,128]{1,0:T(8,128)(2,1)S(1)}, u32[]{:S(2)}, u32[]{:S(2)}) collective-permute-start(bf16[512,128]{1,0:T(8,128)(2,1)S(1)} %get-tuple-element.84), channel_id=1, source_target_pairs={{0,4},{8,12},{9,13},{4,8},{5,9},{12,0},{13,1},{1,5},{2,6},{10,14},... | collective-permute-start | bytes 393224 | tf_op jit(solution)/shard_map/ppermute | solution.py:576
  60.6 19.0 %collective-permute-start.8 = (bf16[512,128]{1,0:T(8,128)(2,1)S(1)}, bf16[512,128]{1,0:T(8,128)(2,1)S(1)}, u32[]{:S(2)}, u32[]{:S(2)}) collective-permute-start(bf16[512,128]{1,0:T(8,128)(2,1)S(1)} %get-tuple-element.82), channel_id=1, source_target_pairs={{0,9},{8,1},{9,0},{4,13},{5,12},{12,5},{13,4},{1,8},{2,11},{10,3},... | collective-permute-start | bytes 393224 | tf_op jit(solution)/shard_map/ppermute | solution.py:576
  64.5 18.4 %collective-permute-start.7 = (bf16[512,128]{1,0:T(8,128)(2,1)S(1)}, bf16[512,128]{1,0:T(8,128)(2,1)S(1)}, u32[]{:S(2)}, u32[]{:S(2)}) collective-permute-start(bf16[512,128]{1,0:T(8,128)(2,1)S(1)} %get-tuple-element.80), channel_id=1, source_target_pairs={{0,8},{8,0},{9,1},{4,12},{5,13},{12,4},{13,5},{1,9},{2,10},{10,2},... | collective-permute-start | bytes 393224 | tf_op jit(solution)/shard_map/ppermute | solution.py:576
  82.8 21.8 %collective-permute-start.14 = (bf16[2,512,128]{2,1,0:T(8,128)(2,1)S(1)}, bf16[2,512,128]{2,1,0:T(8,128)(2,1)S(1)}, u32[]{:S(2)}, u32[]{:S(2)}) collective-permute-start(bf16[2,512,128]{2,1,0:T(8,128)(2,1)S(1)} %get-tuple-element.94), channel_id=1, source_target_pairs={{0,4},{4,8},{8,12},{12,0},{1,5},{5,9},{9,13},{13,1},{2,6},{6,10},{... | collective-permute-start | bytes 786440 | tf_op jit(solution)/shard_map/ppermute | solution.py:582
  82.8 24.6 %collective-permute-start.15 = (bf16[2,512,128]{2,1,0:T(8,128)(2,1)S(1)}, bf16[2,512,128]{2,1,0:T(8,128)(2,1)S(1)}, u32[]{:S(2)}, u32[]{:S(2)}) collective-permute-start(bf16[2,512,128]{2,1,0:T(8,128)(2,1)S(1)} %get-tuple-element.95), channel_id=1, source_target_pairs={{0,8},{4,12},{8,0},{12,4},{1,9},{5,13},{9,1},{13,5},{2,10},{6,14},... | collective-permute-start | bytes 786440 | tf_op jit(solution)/shard_map/ppermute | solution.py:582
  84.3 23.1 %collective-permute-start.16 = (bf16[2,512,128]{2,1,0:T(8,128)(2,1)S(1)}, bf16[2,512,128]{2,1,0:T(8,128)(2,1)S(1)}, u32[]{:S(2)}, u32[]{:S(2)}) collective-permute-start(bf16[2,512,128]{2,1,0:T(8,128)(2,1)S(1)} %get-tuple-element.96), channel_id=1, source_target_pairs={{0,12},{4,0},{8,4},{12,8},{1,13},{5,1},{9,5},{13,9},{2,14},{6,2},{... | collective-permute-start | bytes 786440 | tf_op jit(solution)/shard_map/ppermute | solution.py:582
  102.4 11.5 %collective-permute-start.18 = (bf16[2,544,128]{2,1,0:T(8,128)(2,1)S(1)}, bf16[2,544,128]{2,1,0:T(8,128)(2,1)S(1)}, u32[]{:S(2)}, u32[]{:S(2)}) collective-permute-start(bf16[2,544,128]{2,1,0:T(8,128)(2,1)S(1)} %get-tuple-element.103), channel_id=1, source_target_pairs={{0,4},{4,8},{8,12},{12,0},{1,5},{5,9},{9,13},{13,1},{2,6},{6,10},{... | collective-permute-start | bytes 835592 | tf_op jit(solution)/shard_map/ppermute | solution.py:582
  103.0 24.5 %collective-permute-start.19 = (bf16[2,544,128]{2,1,0:T(8,128)(2,1)S(1)}, bf16[2,544,128]{2,1,0:T(8,128)(2,1)S(1)}, u32[]{:S(2)}, u32[]{:S(2)}) collective-permute-start(bf16[2,544,128]{2,1,0:T(8,128)(2,1)S(1)} %get-tuple-element.104), channel_id=1, source_target_pairs={{0,8},{4,12},{8,0},{12,4},{1,9},{5,13},{9,1},{13,5},{2,10},{6,14},... | collective-permute-start | bytes 835592 | tf_op jit(solution)/shard_map/ppermute | solution.py:582
  104.6 22.9 %collective-permute-start.20 = (bf16[2,544,128]{2,1,0:T(8,128)(2,1)S(1)}, bf16[2,544,128]{2,1,0:T(8,128)(2,1)S(1)}, u32[]{:S(2)}, u32[]{:S(2)}) collective-permute-start(bf16[2,544,128]{2,1,0:T(8,128)(2,1)S(1)} %get-tuple-element.105), channel_id=1, source_target_pairs={{0,12},{4,0},{8,4},{12,8},{1,13},{5,1},{9,5},{13,9},{2,14},{6,2},{... | collective-permute-start | bytes 835592 | tf_op jit(solution)/shard_map/ppermute | solution.py:582
  108.0 20.1 %collective-permute-start.17 = (bf16[4,512,128]{2,1,0:T(8,128)(2,1)S(1)}, bf16[4,512,128]{2,1,0:T(8,128)(2,1)S(1)}, u32[]{:S(2)}, u32[]{:S(2)}) collective-permute-start(bf16[4,512,128]{2,1,0:T(8,128)(2,1)S(1)} %swap_value.1), channel_id=1, source_target_pairs={{0,1},{1,0},{2,3},{3,2},{4,5},{5,4},{6,7},{7,6},{8,9},{9,8},{10,11... | collective-permute-start | bytes 1572872 | tf_op jit(solution)/shard_map/ppermute | solution.py:582
  128.1 3.1 %collective-permute-start.21 = (bf16[4,544,128]{2,1,0:T(8,128)(2,1)S(1)}, bf16[4,544,128]{2,1,0:T(8,128)(2,1)S(1)}, u32[]{:S(2)}, u32[]{:S(2)}) collective-permute-start(bf16[4,544,128]{2,1,0:T(8,128)(2,1)S(1)} %swap_query.1), channel_id=1, source_target_pairs={{0,1},{1,0},{2,3},{3,2},{4,5},{5,4},{6,7},{7,6},{8,9},{9,8},{10,11... | collective-permute-start | bytes 1671176 | tf_op jit(solution)/shard_map/ppermute | solution.py:582
  130.7 4.1 %collective-permute-start.22 = (bf16[4,128,512]{2,1,0:T(8,128)(2,1)S(1)}, bf16[4,128,512]{2,1,0:T(8,128)(2,1)S(1)}, u32[]{:S(2)}, u32[]{:S(2)}) collective-permute-start(bf16[4,128,512]{2,1,0:T(8,128)(2,1)S(1)} %get-tuple-element.108), channel_id=1, source_target_pairs={{0,1},{1,0},{2,3},{3,2},{4,5},{5,4},{6,7},{7,6},{8,9},{9,8},{10,11... | collective-permute-start | bytes 1572872 | tf_op jit(solution)/shard_map/ppermute | solution.py:582
  133.3 25.8 %collective-permute-start.24 = (bf16[1024,512]{1,0:T(8,128)(2,1)S(1)}, bf16[1024,512]{1,0:T(8,128)(2,1)S(1)}, u32[]{:S(2)}, u32[]{:S(2)}) collective-permute-start(bf16[1024,512]{1,0:T(8,128)(2,1)S(1)} %get-tuple-element.113), channel_id=1, source_target_pairs={{0,2},{2,0},{1,3},{3,1},{4,6},{6,4},{5,7},{7,5},{8,10},{10,8},{9,1... | collective-permute-start | bytes 3145736 | tf_op jit(solution)/shard_map/ppermute | solution.py:582
  136.7 8.4 %collective-permute-start.23 = (bf16[4,128,512]{2,1,0:T(8,128)(2,1)S(1)}, bf16[4,128,512]{2,1,0:T(8,128)(2,1)S(1)}, u32[]{:S(2)}, u32[]{:S(2)}) collective-permute-start(bf16[4,128,512]{2,1,0:T(8,128)(2,1)S(1)} %get-tuple-element.110), channel_id=1, source_target_pairs={{0,1},{1,0},{2,3},{3,2},{4,5},{5,4},{6,7},{7,6},{8,9},{9,8},{10,11... | collective-permute-start | bytes 1572872 | tf_op jit(solution)/shard_map/ppermute | solution.py:582
  136.8 9.2 %collective-permute-start.28 = (bf16[128,512]{1,0:T(8,128)(2,1)S(1)}, bf16[128,512]{1,0:T(8,128)(2,1)S(1)}, u32[]{:S(2)}, u32[]{:S(2)}) collective-permute-start(bf16[128,512]{1,0:T(8,128)(2,1)S(1)} %get-tuple-element.120), channel_id=1, source_target_pairs={{0,8},{4,12},{8,0},{12,4},{1,9},{5,13},{9,1},{13,5},{2,10},{6,14},... | collective-permute-start | bytes 393224 | tf_op jit(solution)/shard_map/ppermute | solution.py:582
  141.4 10.5 %collective-permute-start.29 = (bf16[128,512]{1,0:T(8,128)(2,1)S(1)}, bf16[128,512]{1,0:T(8,128)(2,1)S(1)}, u32[]{:S(2)}, u32[]{:S(2)}) collective-permute-start(bf16[128,512]{1,0:T(8,128)(2,1)S(1)} %get-tuple-element.121), channel_id=1, source_target_pairs={{0,4},{4,8},{8,12},{12,0},{1,5},{5,9},{9,13},{13,1},{2,6},{6,10},{... | collective-permute-start | bytes 393224 | tf_op jit(solution)/shard_map/ppermute | solution.py:582
  142.5 15.8 %collective-permute-start.30 = (bf16[128,512]{1,0:T(8,128)(2,1)S(1)}, bf16[128,512]{1,0:T(8,128)(2,1)S(1)}, u32[]{:S(2)}, u32[]{:S(2)}) collective-permute-start(bf16[128,512]{1,0:T(8,128)(2,1)S(1)} %get-tuple-element.122), channel_id=1, source_target_pairs={{0,12},{4,0},{8,4},{12,8},{1,13},{5,1},{9,5},{13,9},{2,14},{6,2},{... | collective-permute-start | bytes 393224 | tf_op jit(solution)/shard_map/ppermute | solution.py:582
  145.9 16.9 %collective-permute-start.25 = (bf16[128,512]{1,0:T(8,128)(2,1)S(1)}, bf16[128,512]{1,0:T(8,128)(2,1)S(1)}, u32[]{:S(2)}, u32[]{:S(2)}) collective-permute-start(bf16[128,512]{1,0:T(8,128)(2,1)S(1)} %get-tuple-element.116), channel_id=1, source_target_pairs={{0,8},{4,12},{8,0},{12,4},{1,9},{5,13},{9,1},{13,5},{2,10},{6,14},... | collective-permute-start | bytes 393224 | tf_op jit(solution)/shard_map/ppermute | solution.py:582
  146.1 16.7 %collective-permute-start.26 = (bf16[128,512]{1,0:T(8,128)(2,1)S(1)}, bf16[128,512]{1,0:T(8,128)(2,1)S(1)}, u32[]{:S(2)}, u32[]{:S(2)}) collective-permute-start(bf16[128,512]{1,0:T(8,128)(2,1)S(1)} %get-tuple-element.117), channel_id=1, source_target_pairs={{0,4},{4,8},{8,12},{12,0},{1,5},{5,9},{9,13},{13,1},{2,6},{6,10},{... | collective-permute-start | bytes 393224 | tf_op jit(solution)/shard_map/ppermute | solution.py:582
  151.9 13.6 %collective-permute-start.27 = (bf16[128,512]{1,0:T(8,128)(2,1)S(1)}, bf16[128,512]{1,0:T(8,128)(2,1)S(1)}, u32[]{:S(2)}, u32[]{:S(2)}) collective-permute-start(bf16[128,512]{1,0:T(8,128)(2,1)S(1)} %get-tuple-element.118), channel_id=1, source_target_pairs={{0,12},{4,0},{8,4},{12,8},{1,13},{5,1},{9,5},{13,9},{2,14},{6,2},{... | collective-permute-start | bytes 393224 | tf_op jit(solution)/shard_map/ppermute | solution.py:582
